TPU v7x, 32 devices: a whole 2x2x4 slice. The times are simulated.
32 devices in a mesh: space: 8 (over y, x, core), snap: 4 (over z).
Axes of the slice: x: 2, y: 2, z: 4, core: 2. Of those that a mesh axis runs over, the one named last changes fastest.
Arguments:
- owned_x: bfloat16 [1024, 128, 512], P('space', None, 'snap'), may hold values from -600 to 600
- owned_y: bfloat16 [1024, 128, 512], P('space', None, 'snap'), may hold values from -6 to 6
- patch_dest: int32 [1024], P('space'), may hold values from -1 to 511, as said below
Outputs:
- q_basis: float32 [512, 128, 512], P('space', 'snap')
- r_factor: float32 [512, 512], replicated
- projection: float32 [512, 512], replicated
Inputs may be any that keep to these rules, and one draw needn't show every extreme that they name: `patch_dest`: every row block 0 to 511 is named by exactly one slot; -1 marks an empty slot. The 128 slots of one owner (one aligned block of 128 slots) name at most 16 row blocks of any one slab d * 64 to (d + 1) * 64 - 1, and some owner names exactly 16 of every slab.
All inputs are finite; a program needn't handle non-finite values.
Results may differ from a plain program's by a relative error of at most 0.0003.
Values may be sent and summed in bfloat16 or wider, within the bound.
No kernel may reach another device: no remote copies, remote signals or barrier semaphores. Data moves between devices by JAX's collectives and lax.ppermute only.
A program may use at most 128 MiB of HBM per device.

v0:
```python
import math

import jax
import jax.numpy as jnp
from jax import lax
from jax.sharding import PartitionSpec as P

PATCH = 128
BLK_DEV = 64


def slab_ranks(destination, per_slab):
    target = jnp.where(destination >= 0, destination // per_slab, -1)
    slot_count = destination.shape[-1]
    same_slab = target[..., :, None] == target[..., None, :]
    before = lax.broadcasted_iota(jnp.int32, (slot_count, slot_count), 1) < lax.broadcasted_iota(
        jnp.int32, (slot_count, slot_count), 0
    )
    order_rank = jnp.sum((same_slab & before).astype(jnp.int32), axis=-1)
    return (target, order_rank)


def send_table(destination, per_slab, slab_count, capacity):
    target, order_rank = slab_ranks(destination, per_slab)
    slot_count = destination.shape[0]
    where_to = jnp.where(target >= 0, target * capacity + order_rank, slab_count * capacity)
    start_table = jnp.full((slab_count * capacity,), slot_count, jnp.int32)
    return start_table.at[where_to].set(jnp.arange(slot_count, dtype=jnp.int32), mode="drop")


def arrival_index(all_lists, per_slab, capacity, my_slab):
    slot_count = all_lists.shape[1]
    target, order_rank = slab_ranks(all_lists, per_slab)
    wanted = my_slab * per_slab + jnp.arange(per_slab, dtype=jnp.int32)
    matches = all_lists.reshape(-1)[None, :] == wanted[:, None]
    located = jnp.argmax(matches, axis=1)
    source = located // slot_count
    return source * capacity + order_rank.reshape(-1)[located]


def pick_rows(payload, indices):
    return jnp.take(payload, indices, axis=0, mode="fill", fill_value=0)


def body(owned_x, owned_y, patch_dest):
    slab_count = lax.axis_size("space")
    slot_count = patch_dest.shape[0]
    capacity = slot_count // slab_count
    my_slab = lax.axis_index("space")
    all_lists = lax.all_gather(patch_dest, "space", axis=0, tiled=True)
    outgoing_table = send_table(patch_dest, BLK_DEV, slab_count, capacity)
    received_at = arrival_index(
        all_lists.reshape(slab_count, slot_count), BLK_DEV, capacity, my_slab
    )
    rows_total = slab_count * BLK_DEV * PATCH
    contract = (((0,), (0,)), ((), ()))
    block_x, block_y = (
        lax.all_to_all(owned_x, "snap", split_axis=1, concat_axis=2, tiled=True),
        lax.all_to_all(owned_y, "snap", split_axis=1, concat_axis=2, tiled=True),
    )
    width = block_x.shape[-1]
    used = patch_dest >= 0
    kept_x = jnp.where(used[:, None, None], block_x, jnp.zeros_like(block_x))
    local_cross = lax.dot_general(
        kept_x.reshape(-1, width),
        block_y.reshape(-1, width),
        contract,
        preferred_element_type=jnp.float32,
    )
    moved_x = lax.all_to_all(
        pick_rows(block_x, outgoing_table), "space", split_axis=0, concat_axis=0, tiled=True
    )
    slab_x = jnp.take(moved_x, received_at, axis=0)
    cell_rows = slab_x.reshape(-1, width)
    local_gram = lax.dot_general(cell_rows, cell_rows, contract, preferred_element_type=jnp.float32)
    gram_total, cross_total = lax.psum((local_gram, local_cross), ("space", "snap"))
    identity = jnp.eye(width, dtype=jnp.float32)
    lower = jnp.linalg.cholesky(gram_total / rows_total)
    inverse = lax.linalg.triangular_solve(lower, identity, left_side=True, lower=True)
    basis_rows = jnp.dot(cell_rows.astype(jnp.float32), inverse.T, precision=lax.Precision.HIGHEST)
    projection = jnp.dot(inverse, cross_total, precision=lax.Precision.HIGHEST) / math.sqrt(
        rows_total
    )
    return (basis_rows.reshape(slab_x.shape[0], slab_x.shape[1], width), lower.T, projection)


def solution(mesh):
    in_specs = (P("space", None, "snap"), P("space", None, "snap"), P("space"))
    out_specs = (P("space", "snap", None), P(), P())
    return jax.shard_map(body, mesh=mesh, in_specs=in_specs, out_specs=out_specs, check_vma=False)
```

profile of v0, /device:TPU:0, one launch (start us, length us, event | category | flops | bytes accessed | tf_op | source)
XLA Modules:
  0.0 593.5 jit_solution(731501483815323009)
XLA Ops:
  7.2 6.9 %copy.38 = bf16[128,128,128]{2,0,1:T(8,128)(2,1)} copy(bf16[128,128,128]{2,1,0:T(8,128)(2,1)} %param.3) | data formatting | bytes 8388608 | tf_op args[0]
  14.1 6.3 %all-to-all-start = ((bf16[128,128,128]{2,0,1:T(8,128)(2,1)}), bf16[128,128,128]{2,0,1:T(8,128)(2,1)}, u32[]{:S(2)}, u32[]{:S(2)}) async-start(bf16[128,128,128]{2,0,1:T(8,128)(2,1)} %copy.38), calls=%async_computation | async-start | bytes 8388608 | tf_op jit(solution)/shard_map/all_to_all | solution.py:58
  20.4 6.9 %copy.45 = bf16[128,128,128]{2,0,1:T(8,128)(2,1)} copy(bf16[128,128,128]{2,1,0:T(8,128)(2,1)} %param.4) | data formatting | bytes 8388608 | tf_op args[1]
  27.2 86.6 %all-to-all-done = bf16[128,128,128]{2,0,1:T(8,128)(2,1)} async-done(((bf16[128,128,128]{2,0,1:T(8,128)(2,1)}), bf16[128,128,128]{2,0,1:T(8,128)(2,1)}, u32[]{:S(2)}, u32[]{:S(2)}) %all-to-all-start) | async-done | bytes 4194336 | tf_op jit(solution)/shard_map/all_to_all | solution.py:58
  113.8 4.8 all-to-all-start.2
  118.9 1.0 scatter_custom_fusion
  119.9 6.4 %copy.40 = bf16[128,32,4,128]{0,3,2,1:T(8,128)(2,1)} copy(bf16[128,32,4,128]{3,0,1,2:T(8,128)(2,1)} %bitcast.6) | data formatting | bytes 8388608 | tf_op jit(solution)/shard_map/all_to_all | solution.py:58
  126.3 7.9 %copy.41 = bf16[128,32,512]{2,1,0:T(8,128)(2,1)} copy(bf16[128,32,512]{0,2,1:T(8,128)(2,1)} %bitcast.79) | data formatting | bytes 8388608 | tf_op jit(solution)/shard_map/all_to_all | solution.py:58
  134.3 5.0 gather_fusion.1
  139.3 4.6 broadcast_select_fusion.1
  143.9 67.4 %all-to-all-done.2 = bf16[128,128,128]{2,0,1:T(8,128)(2,1)} async-done(((bf16[128,128,128]{2,0,1:T(8,128)(2,1)}), bf16[128,128,128]{2,0,1:T(8,128)(2,1)}, u32[]{:S(2)}, u32[]{:S(2)}) %all-to-all-start.2) | async-done | bytes 4194336 | tf_op jit(solution)/shard_map/all_to_all | solution.py:59
  211.3 4.6 all-to-all-start.1
  216.0 52.0 %all-gather = s32[8,1,128]{2,1,0:T(1,128)S(1)} all-gather(s32[1,1,128]{2,1,0:T(1,128)S(1)} %bitcast.84), channel_id=1, replica_groups=mesh['space'=8,'snap'=4] {'space'}, dimensions={0}, use_global_device_ids=true | all-gather | bytes 4608 | tf_op jit(solution)/shard_map/all_gather | solution.py:50
  267.9 1.2 iota_reduce_fusion
  269.2 0.4 convert_reduce_fusion
  269.5 0.7 gather_fusion
  270.3 4.9 copy.39
  275.2 0.4 broadcast_select_fusion
  275.6 4.2 copy.44
  279.8 5.4 copy.46
  285.2 3.5 fusion
  288.8 2.9 gather_fusion.2
  291.7 2.7 convolution_bitcast_fusion
  294.5 1.2 fusion.18
  295.6 130.2 %all-reduce.4.cloned.1.call-done = (f32[512,512]{0,1:T(8,128)}, f32[512,512]{1,0:T(8,128)}) async-done(((f32[512,512]{0,1:T(8,128)}, f32[512,512]{1,0:T(8,128)}), (f32[512,512]{0,1:T(8,128)}, f32[512,512]{1,0:T(8,128)})) %all-reduce.4.cloned.1.call-update) | async-done | bytes 2097168 | tf_op jit(solution)/shard_map/psum | solution.py:76
  425.8 1.4 broadcast_multiply_fusion
  427.3 0.3 copy.43
  427.9 1.0 copy-done.2
  428.8 11.7 %cholesky.96 = f32[128,128]{1,0:T(8,128)S(1)} custom-call(f32[128,128]{1,0:T(8,128)S(1)} %cholesky.250), custom_call_target="Cholesky" | custom-call | tf_op jit(solution)/shard_map/jit(cholesky)/cholesky | solution.py:78
  440.6 9.8 %custom-call.30 = f32[1,128,128]{1,2,0:T(8,128)S(1)} custom-call(f32[1,128,128]{2,1,0:T(8,128)S(1)} %get-tuple-element.53), custom_call_target="InvertDiagBlocksLowerTriangular" | custom-call | tf_op jit(solution)/shard_map/jit(cholesky)/cholesky | solution.py:78
  450.5 1.3 constant_dynamic-update-slice_fusion.3
  451.9 1.3 convolution_subtract_fusion.3
  453.1 12.1 %cholesky.201 = f32[128,128]{1,0:T(8,128)S(1)} custom-call(f32[128,128]{1,0:T(8,128)S(1)} %cholesky.254), custom_call_target="Cholesky" | custom-call | tf_op jit(solution)/shard_map/jit(cholesky)/cholesky | solution.py:78
  465.3 9.8 %custom-call.31 = f32[1,128,128]{1,2,0:T(8,128)S(1)} custom-call(f32[1,128,128]{2,1,0:T(8,128)S(1)} %get-tuple-element.50), custom_call_target="InvertDiagBlocksLowerTriangular" | custom-call | tf_op jit(solution)/shard_map/jit(cholesky)/cholesky | solution.py:78
  475.1 0.3 convolution_dynamic-update-slice_fusion
  475.4 1.3 convolution_subtract_fusion.4
  476.7 11.7 %cholesky.222 = f32[128,128]{1,0:T(8,128)S(1)} custom-call(f32[128,128]{1,0:T(8,128)S(1)} %cholesky.259), custom_call_target="Cholesky" | custom-call | tf_op jit(solution)/shard_map/jit(cholesky)/cholesky | solution.py:78
  488.4 0.7 compare_reduce_fusion.1
  489.1 9.8 %custom-call.32 = f32[1,128,128]{1,2,0:T(8,128)S(1)} custom-call(f32[1,128,128]{2,1,0:T(8,128)S(1)} %get-tuple-element.47), custom_call_target="InvertDiagBlocksLowerTriangular" | custom-call | tf_op jit(solution)/shard_map/jit(cholesky)/cholesky | solution.py:78
  499.1 1.2 convolution_subtract_fusion.5
  500.3 11.9 %cholesky.239 = f32[128,128]{1,0:T(8,128)S(1)} custom-call(f32[128,128]{1,0:T(8,128)S(1)} %convolution_subtract_fusion.5), custom_call_target="Cholesky" | custom-call | tf_op jit(solution)/shard_map/jit(cholesky)/cholesky | solution.py:78
  512.2 0.7 compare_reduce_fusion
  512.9 0.6 compare_reduce_fusion.2
  516.1 1.2 fusion.9
  517.3 13.9 %while.1 = (s32[]{:T(128)}, f32[512,512]{1,0:T(8,128)}, s32[4,2]{0,1:T(2,128)S(1)}, f32[4,128,128]{2,1,0:T(8,128)}, s32[]{:T(128)}) while((s32[]{:T(128)}, f32[512,512]{1,0:T(8,128)}, s32[4,2]{0,1:T(2,128)S(1)}, f32[4,128,128]{2,1,0:T(8,128)}, s32[]{:T(128)}) %tuple.40), condition=%wide.while_cond, body=%wide.while_body.sunk | while | flops 2 | bytes 132705 | solution.py:79
  517.4 0.5 fusion.58
  517.9 2.9 bitcast_dynamic-update-slice_fusion.2
  520.9 0.5 fusion.58
  521.4 2.9 bitcast_dynamic-update-slice_fusion.2
  524.3 0.5 fusion.58
  524.9 2.9 bitcast_dynamic-update-slice_fusion.2
  527.8 0.5 fusion.58
  528.3 2.8 bitcast_dynamic-update-slice_fusion.2
  531.2 40.1 %custom-call.33 = f32[4,128,128]{1,2,0:T(8,128)S(1)} custom-call(f32[4,128,128]{2,1,0:T(8,128)} %get-tuple-element.12), custom_call_target="InvertDiagBlocksLowerTriangular" | custom-call | tf_op jit(solution)/shard_map/triangular_solve | solution.py:79
  571.3 0.3 fusion.20
  571.6 1.4 convolution_subtract_fusion.1
  573.0 0.4 fusion.32
  573.5 1.3 convolution_subtract_fusion
  574.8 0.4 fusion.30
  575.2 1.6 convolution_subtract_fusion.2
  576.8 0.4 fusion.29
  577.3 5.1 fusion.5
  582.4 2.8 convolution_multiply_fusion
  585.2 1.3 copy.47
  (49 shorter events, 1.5 us)
Async XLA Ops:
  14.1 99.7 %all-to-all-start = ((bf16[128,128,128]{2,0,1:T(8,128)(2,1)}), bf16[128,128,128]{2,0,1:T(8,128)(2,1)}, u32[]{:S(2)}, u32[]{:S(2)}) async-start(bf16[128,128,128]{2,0,1:T(8,128)(2,1)} %copy.38), calls=%async_computation | async-start | bytes 8388608 | tf_op jit(solution)/shard_map/all_to_all | solution.py:58
  27.2 91.4 %copy-start.6 = (s32[128]{0:T(128)S(1)}, s32[128]{0:T(128)}, u32[]{:S(2)}) copy-start(s32[128]{0:T(128)} %param.5) | copy-start | bytes 1540
  113.8 97.5 %all-to-all-start.2 = ((bf16[128,128,128]{2,0,1:T(8,128)(2,1)}), bf16[128,128,128]{2,0,1:T(8,128)(2,1)}, u32[]{:S(2)}, u32[]{:S(2)}) async-start(bf16[128,128,128]{2,0,1:T(8,128)(2,1)} %copy.45), calls=%async_computation.2 | async-start | bytes 8388608 | tf_op jit(solution)/shard_map/all_to_all | solution.py:59
  211.3 77.5 %all-to-all-start.1 = ((bf16[128,32,512]{2,1,0:T(8,128)(2,1)}), bf16[128,32,512]{2,1,0:T(8,128)(2,1)}, u32[]{:S(2)}, u32[]{:S(2)}) async-start(bf16[128,32,512]{2,1,0:T(8,128)(2,1)} %broadcast_select_fusion.1), calls=%async_computation.1 | async-start | bytes 8388608 | tf_op jit(solution)/shard_map/all_to_all | solution.py:70
  215.9 209.9 %all-reduce.4.cloned.1.call-start = ((), (), s32[]{:S(2)}) async-start(), calls=%async_computation.3 | async-start | bytes 4194304 | tf_op jit(solution)/shard_map/psum | solution.py:76
  291.6 2.7 copy-start.3
  425.8 1.8 copy-start
  427.8 1.0 copy-start.2
  450.5 121.1 %copy-start.1 = (f32[512,512]{1,0:T(8,128)S(1)}, f32[512,512]{1,0:T(8,128)}, u32[]{:S(2)}) copy-start(f32[512,512]{1,0:T(8,128)} %fusion.18) | copy-start | bytes 3145732
  571.3 6.0 %copy-start.4 = (bf16[64,32,512]{2,1,0:T(8,128)(2,1)S(1)}, bf16[64,32,512]{2,1,0:T(8,128)(2,1)}, u32[]{:S(2)}) copy-start(bf16[64,32,512]{2,1,0:T(8,128)(2,1)} %copy-done.3) | copy-start | bytes 6291460
  576.8 5.5 copy-start.5
Sparse Core Ops, SparseCore 0:
  294.5 131.3 all-reduce.3
where the time goes:
time: 601 us; the launch traced here: 594 us
  waiting for transfers between devices  284 us (47%)
  other arithmetic  130 us (22%)
  local copies, waits for them, and re-layouts  68.9 us (11%)
  blocking collectives  52 us (9%)
  matrix products  25.5 us (4%)
  between operations  17.2 us (3%)
  starting transfers between devices  15.8 us (3%)
    psum x1, waiting for transfers between devices, body(): lax.psum((local_gram, local_cross), ('space', 'snap'))  130 us
    all_to_all x1, waiting for transfers between devices, body(): lax.all_to_all(owned_x, 'snap', split_axis=1, concat_axis=2, tiled=True)  86.6 us
    another operation x14, other arithmetic, body(): lower = jnp.linalg.cholesky(gram_total / rows_total)  78.9 us
    all_to_all x1, waiting for transfers between devices, body(): lax.all_to_all(owned_y, 'snap', split_axis=1, concat_axis=2, tiled=True)  67.4 us
    all_gather x1, blocking collectives, body(): all_lists = lax.all_gather(patch_dest, 'space', axis=0, tiled=True)  52 us
    another operation x2, other arithmetic, body(): lax.linalg.triangular_solve(lower, identity, left_side=True, lower=True)  40.1 us
    all_to_all x3, local copies, waits for them, and re-layouts, body(): lax.all_to_all(owned_x, 'snap', split_axis=1, concat_axis=2, tiled=True)  19.3 us
    unnamed x17, local copies, waits for them, and re-layouts  16.1 us
  transfers between devices with their start and end apart: 4, of which 3 were waited for; matrix products, arithmetic and copies ran while one was open for 9% of the time, Pallas kernels for 0%

commit v1 on v0

v1 whole, which is shorter than its diff:
```python
import math

import jax
import jax.numpy as jnp
from jax import lax
from jax.experimental import pallas as pl
from jax.experimental.pallas import tpu as pltpu
from jax.sharding import PartitionSpec as P

TILE = 128
GROUP = 8
CELL_TILE = 16
HIGHEST = lax.Precision.HIGHEST
SMEM = pl.BlockSpec(memory_space=pltpu.SMEM)
VMEM = pl.BlockSpec(memory_space=pltpu.VMEM)
ANY = pl.BlockSpec(memory_space=pl.ANY)
ROWS_BY_ROWS = (((0,), (0,)), ((), ()))
LANES_BY_LANES = (((1,), (1,)), ((), ()))


def plan_kernel(slabs, capacity, per_slab, dest_ref, table_ref, meta_ref, count_ref):
    def clear(i, _):
        table_ref[i] = 0
        meta_ref[i // capacity, i % capacity] = -1
        return 0

    def clear_count(i, _):
        count_ref[i] = 0
        return 0

    def place(i, _):
        block = dest_ref[i]

        @pl.when(block >= 0)
        def _():
            slab = block // per_slab
            rank = count_ref[slab]
            count_ref[slab] = rank + 1
            table_ref[slab * capacity + rank] = i
            meta_ref[slab, rank] = block - slab * per_slab

        return 0

    lax.fori_loop(0, slabs, clear_count, 0)
    lax.fori_loop(0, slabs * capacity, clear, 0)
    lax.fori_loop(0, dest_ref.shape[0], place, 0)


def plan(dest, slabs, capacity, per_slab):
    return pl.pallas_call(
        lambda *refs: plan_kernel(slabs, capacity, per_slab, *refs),
        out_shape=(
            jax.ShapeDtypeStruct((slabs * capacity,), jnp.int32),
            jax.ShapeDtypeStruct((slabs, TILE), jnp.int32),
        ),
        in_specs=[SMEM],
        out_specs=(SMEM, SMEM),
        scratch_shapes=[pltpu.SMEM((slabs,), jnp.int32)],
        name="plan",
    )(dest)


def arrival_kernel(slabs, capacity, meta_ref, table_ref):
    def clear(i, _):
        table_ref[i] = 0
        return 0

    def place(i, _):
        block = meta_ref[i // capacity, i % capacity]

        @pl.when(block >= 0)
        def _():
            table_ref[block] = i

        return 0

    lax.fori_loop(0, table_ref.shape[0], clear, 0)
    lax.fori_loop(0, slabs * capacity, place, 0)


def arrival(meta, slabs, capacity, per_slab):
    return pl.pallas_call(
        lambda *refs: arrival_kernel(slabs, capacity, *refs),
        out_shape=jax.ShapeDtypeStruct((per_slab,), jnp.int32),
        in_specs=[SMEM],
        out_specs=SMEM,
        name="arrival",
    )(meta)


def pack_kernel(part, table_ref, owned_ref, out_ref, sem):
    def send(i, _):
        pltpu.make_async_copy(owned_ref.at[table_ref[i], :, part], out_ref.at[i], sem).start()
        return 0

    lax.fori_loop(0, out_ref.shape[0], send, 0)
    pltpu.make_async_copy(out_ref, out_ref, sem).wait()


def pack(owned, table, part):
    slots, shares, _, rows, width = owned.shape
    return pl.pallas_call(
        lambda *refs: pack_kernel(part, *refs),
        out_shape=jax.ShapeDtypeStruct((slots, shares, rows, width), owned.dtype),
        in_specs=[SMEM, ANY],
        out_specs=ANY,
        scratch_shapes=[pltpu.SemaphoreType.DMA],
        cost_estimate=pl.CostEstimate(
            flops=0, bytes_accessed=2 * slots * shares * rows * width * 2, transcendentals=0
        ),
        name="pack",
    )(table, owned)


def settle_kernel(table_ref, moved_ref, out_ref, sem):
    def send(i, _):
        pltpu.make_async_copy(moved_ref.at[table_ref[i]], out_ref.at[:, i], sem).start()
        return 0

    lax.fori_loop(0, out_ref.shape[1], send, 0)
    pltpu.make_async_copy(out_ref, out_ref, sem).wait()


def settle(moved, table):
    _, shares, rows, width = moved.shape
    blocks = table.shape[0]
    return pl.pallas_call(
        settle_kernel,
        out_shape=jax.ShapeDtypeStruct((shares, blocks, rows, width), moved.dtype),
        in_specs=[SMEM, ANY],
        out_specs=ANY,
        scratch_shapes=[pltpu.SemaphoreType.DMA],
        cost_estimate=pl.CostEstimate(
            flops=0, bytes_accessed=2 * shares * blocks * rows * width * 2, transcendentals=0
        ),
        name="settle",
    )(table, moved)


def whole_rows(ref):
    shares, blocks, rows, width = ref.shape
    parts = [ref[s].reshape(blocks * rows, width) for s in range(shares)]
    return jnp.concatenate(parts, axis=1)


def gram_kernel(parts, *refs):
    out_ref = refs[parts]
    shares = refs[0].shape[0]
    step = pl.program_id(0)

    @pl.when(step == 0)
    def _():
        out_ref[...] = jnp.zeros_like(out_ref)

    for part in range(parts):
        cells = whole_rows(refs[part])
        at = 0
        for a in range(shares):
            left = cells[:, a * TILE : (a + 1) * TILE]
            product = lax.dot_general(
                left, cells[:, a * TILE :], ROWS_BY_ROWS, preferred_element_type=jnp.float32
            )
            for b in range(a, shares):
                out_ref[at] += product[:, (b - a) * TILE : (b - a + 1) * TILE]
                at += 1


def gram_blocks(cells, steps=4):
    shares, blocks, rows, width = cells[0].shape
    pairs = shares * (shares + 1) // 2
    spec = pl.BlockSpec((shares, blocks // steps, rows, width), lambda i: (0, i, 0, 0))
    return pl.pallas_call(
        lambda *refs: gram_kernel(len(cells), *refs),
        grid=(steps,),
        out_shape=jax.ShapeDtypeStruct((pairs, TILE, TILE), jnp.float32),
        in_specs=[spec] * len(cells),
        out_specs=pl.BlockSpec((pairs, TILE, TILE), lambda i: (0, 0, 0)),
        name="gram_blocks",
    )(*cells)


def cross_kernel(parts, *refs):
    out_ref = refs[2 * parts]
    step = pl.program_id(0)

    @pl.when(step == 0)
    def _():
        out_ref[...] = jnp.zeros_like(out_ref)

    for part in range(parts):
        out_ref[...] += lax.dot_general(
            whole_rows(refs[part]),
            whole_rows(refs[parts + part]),
            ROWS_BY_ROWS,
            preferred_element_type=jnp.float32,
        )


def cross_sum(x_cells, y_cells, steps=4):
    shares, blocks, rows, width = x_cells[0].shape
    spec = pl.BlockSpec((shares, blocks // steps, rows, width), lambda i: (0, i, 0, 0))
    full = shares * width
    return pl.pallas_call(
        lambda *refs: cross_kernel(len(x_cells), *refs),
        grid=(steps,),
        out_shape=jax.ShapeDtypeStruct((full, full), jnp.float32),
        in_specs=[spec] * (2 * len(x_cells)),
        out_specs=pl.BlockSpec((full, full), lambda i: (0, 0)),
        name="cross_sum",
    )(*x_cells, *y_cells)


def three_terms(value):
    high = value.astype(jnp.bfloat16).astype(jnp.float32)
    rest = value - high
    middle = rest.astype(jnp.bfloat16).astype(jnp.float32)
    return high, middle, rest - middle


def lane_of(row, lane):
    return jnp.broadcast_to(row[:, lane : lane + 1], row.shape)


def row_of(ref, row):
    return jnp.broadcast_to(ref[row : row + 1, :], (GROUP, TILE))


def factor_tile(a_ref, w_ref, u_ref, v_ref):
    panels = TILE // GROUP
    a_rows = [row_of(a_ref, i) for i in range(GROUP)]
    w_rows = [row_of(w_ref, i) for i in range(GROUP)]
    for p in range(panels):
        base = p * GROUP
        small = {
            (i, k): lane_of(a_rows[i], base + k) for i in range(GROUP) for k in range(i, GROUP)
        }
        for j in range(GROUP):
            scale = lax.rsqrt(small[j, j])
            a_rows[j] = a_rows[j] * scale
            w_rows[j] = w_rows[j] * scale
            u_ref[base + j : base + j + 1, :] = a_rows[j][:1]
            v_ref[base + j : base + j + 1, :] = w_rows[j][:1]
            below = {k: small[j, k] * scale for k in range(j + 1, GROUP)}
            for k in range(j + 1, GROUP):
                for m in range(k, GROUP):
                    small[k, m] = small[k, m] - below[k] * below[m]
            for k in range(j + 1, GROUP):
                a_rows[k] = a_rows[k] - below[k] * a_rows[j]
                w_rows[k] = w_rows[k] - below[k] * w_rows[j]
        if p + 1 == panels:
            break
        after = base + GROUP
        next_a = [row_of(a_ref, after + i) for i in range(GROUP)]
        next_w = [row_of(w_ref, after + i) for i in range(GROUP)]
        for i in range(GROUP):
            for k in range(GROUP):
                factor = lane_of(a_rows[k], after + i)
                next_a[i] = next_a[i] - factor * a_rows[k]
                next_w[i] = next_w[i] - factor * w_rows[k]
        if p + 2 < panels:
            done = after + GROUP
            u = u_ref[base:after, :]
            v = v_ref[base:after, :]
            uh, um, ul = three_terms(u)
            vh, vm, vl = three_terms(v)
            left = jnp.concatenate([uh, uh, um, uh, ul, um], axis=0).astype(jnp.bfloat16)
            right_a = jnp.concatenate([uh, um, uh, ul, uh, um], axis=0)
            right_w = jnp.concatenate([vh, vm, vh, vl, vh, vm], axis=0)
            right = jnp.concatenate([right_a, right_w], axis=1).astype(jnp.bfloat16)
            update = lax.dot_general(
                left, right, ROWS_BY_ROWS, preferred_element_type=jnp.float32
            )
            a_ref[done:, :] = a_ref[done:, :] - update[done:, :TILE]
            w_ref[done:, :] = w_ref[done:, :] - update[done:, TILE:]
        a_rows, w_rows = next_a, next_w


def factor_kernel(tiles, rows_total, g_ref, r_ref, inv_ref, hi_ref, mid_ref, lo_ref, wide, a_ref, w_ref, u_ref, v_ref):
    row = lax.broadcasted_iota(jnp.int32, (TILE, TILE), 0)
    lane = lax.broadcasted_iota(jnp.int32, (TILE, TILE), 1)
    wide[...] = jnp.zeros_like(wide)
    at = 0
    for a in range(tiles):
        for b in range(a, tiles):
            wide[a, b] = g_ref[at] / rows_total
            at += 1

    def step(b, _):
        a_ref[...] = wide[b, b]
        w_ref[...] = jnp.where(row == lane, 1.0, 0.0)
        factor_tile(a_ref, w_ref, u_ref, v_ref)
        inverse = v_ref[...]
        wide[b, b] = jnp.where(row <= lane, u_ref[...], 0.0)
        wide[b, tiles + b] = inverse
        for j in range(1, tiles):
            wide[b, b + j] = lax.dot(
                inverse, wide[b, b + j], precision=HIGHEST, preferred_element_type=jnp.float32
            )

        def trail(r, _):
            left = wide[b, r]
            for j in range(1, tiles + 1):
                wide[r, b + j] = wide[r, b + j] - lax.dot_general(
                    left,
                    wide[b, b + j],
                    ROWS_BY_ROWS,
                    precision=HIGHEST,
                    preferred_element_type=jnp.float32,
                )
            return 0

        lax.fori_loop(b + 1, tiles, trail, 0)
        return 0

    lax.fori_loop(0, tiles, step, 0)
    zero = jnp.zeros((TILE, TILE), jnp.float32)
    for a in range(tiles):
        rows = slice(a * TILE, (a + 1) * TILE)
        for b in range(tiles):
            lanes = slice(b * TILE, (b + 1) * TILE)
            r_ref[rows, lanes] = wide[a, b] if b >= a else zero
            value = wide[a, tiles + b] if b <= a else zero
            inv_ref[rows, lanes] = value
            high, middle, low = three_terms(value)
            hi_ref[rows, lanes] = high.astype(jnp.bfloat16)
            mid_ref[rows, lanes] = middle.astype(jnp.bfloat16)
            lo_ref[rows, lanes] = low.astype(jnp.bfloat16)


def factor(blocks, tiles, rows_total):
    full = tiles * TILE
    tile = pltpu.VMEM((TILE, TILE), jnp.float32)
    return pl.pallas_call(
        lambda *refs: factor_kernel(tiles, rows_total, *refs),
        out_shape=(
            jax.ShapeDtypeStruct((full, full), jnp.float32),
            jax.ShapeDtypeStruct((full, full), jnp.float32),
            jax.ShapeDtypeStruct((full, full), jnp.bfloat16),
            jax.ShapeDtypeStruct((full, full), jnp.bfloat16),
            jax.ShapeDtypeStruct((full, full), jnp.bfloat16),
        ),
        in_specs=[VMEM],
        out_specs=(VMEM,) * 5,
        scratch_shapes=[
            pltpu.VMEM((tiles, 2 * tiles, TILE, TILE), jnp.float32),
            tile,
            tile,
            tile,
            tile,
        ],
        compiler_params=pltpu.CompilerParams(vmem_limit_bytes=32 * 1024 * 1024),
        cost_estimate=pl.CostEstimate(
            flops=40 * 10**9, bytes_accessed=8 * full * full, transcendentals=full
        ),
        name="factor",
    )(blocks)


def basis_kernel(parts, *refs):
    hi_ref, mid_ref, lo_ref, out_ref = refs[parts:]
    for part in range(parts):
        cells = whole_rows(refs[part])
        total = lax.dot_general(
            cells, lo_ref[...], LANES_BY_LANES, preferred_element_type=jnp.float32
        )
        total += lax.dot_general(
            cells, mid_ref[...], LANES_BY_LANES, preferred_element_type=jnp.float32
        )
        total += lax.dot_general(
            cells, hi_ref[...], LANES_BY_LANES, preferred_element_type=jnp.float32
        )
        blocks, rows = refs[part].shape[1:3]
        out_ref[:, part] = total.reshape(blocks, rows, total.shape[-1])


def basis(cells, terms, steps=8):
    shares, blocks, rows, width = cells[0].shape
    full = shares * width
    parts = len(cells)
    spec = pl.BlockSpec((shares, blocks // steps, rows, width), lambda i: (0, i, 0, 0))
    term = pl.BlockSpec((full, full), lambda i: (0, 0))
    return pl.pallas_call(
        lambda *refs: basis_kernel(parts, *refs),
        grid=(steps,),
        out_shape=jax.ShapeDtypeStruct((blocks, parts, rows, full), jnp.float32),
        in_specs=[spec] * parts + [term] * 3,
        out_specs=pl.BlockSpec((blocks // steps, parts, rows, full), lambda i: (i, 0, 0, 0)),
        compiler_params=pltpu.CompilerParams(vmem_limit_bytes=32 * 1024 * 1024),
        name="basis",
    )(*cells, *terms)


def sum_over_devices(value, slabs, shares):
    lanes = value.shape[-1]
    pieces = lax.all_to_all(value, "space", split_axis=0, concat_axis=0, tiled=True)
    piece = jnp.sum(pieces.reshape(slabs, -1, lanes), axis=0)
    piece = jnp.sum(lax.all_gather(piece, "snap", axis=0), axis=0)
    return lax.all_gather(piece, "space", axis=0, tiled=True)


def body(owned_x, owned_y, patch_dest):
    slabs = lax.axis_size("space")
    shares = lax.axis_size("snap")
    slots, patch, width = owned_x.shape
    capacity = slots // slabs
    per_slab = slots // 2
    parts = patch // shares // CELL_TILE
    rows_total = slabs * per_slab * patch
    full = shares * width

    table, meta = plan(patch_dest, slabs, capacity, per_slab)
    meta = lax.all_to_all(
        meta.reshape(slabs, 1, TILE), "space", split_axis=0, concat_axis=0, tiled=True
    ).reshape(slabs, TILE)
    arrived = arrival(meta, slabs, capacity, per_slab)

    def exchange(owned):
        owned = owned.reshape(slots, shares, parts, CELL_TILE, width)
        cells = []
        for part in range(parts):
            sent = pack(owned, table, part)
            moved = lax.all_to_all(sent, "space", split_axis=0, concat_axis=0, tiled=True)
            settled = settle(moved, arrived)
            cells.append(
                lax.all_to_all(settled, "snap", split_axis=0, concat_axis=0, tiled=True)
            )
        return cells

    x_cells = exchange(owned_x)
    y_cells = exchange(owned_y)

    tiles = full // TILE
    pairs = tiles * (tiles + 1) // 2
    local = gram_blocks(x_cells).reshape(pairs * TILE, TILE)
    total = sum_over_devices(local, slabs, shares).reshape(pairs, TILE, TILE)
    r_factor, inverse, *terms = factor(total, tiles, rows_total)
    q_basis = basis(x_cells, terms).reshape(per_slab, patch // shares, full)

    cross = sum_over_devices(cross_sum(x_cells, y_cells), slabs, shares)
    projection = jnp.dot(inverse, cross, precision=HIGHEST) / math.sqrt(rows_total)
    return q_basis, r_factor, projection


def solution(mesh):
    in_specs = (P("space", None, "snap"), P("space", None, "snap"), P("space"))
    out_specs = (P("space", "snap", None), P(), P())
    return jax.shard_map(body, mesh=mesh, in_specs=in_specs, out_specs=out_specs, check_vma=False)
```

time: 601 us -> 590 us (0.982); the launches traced: 594 us -> 589 us
  Pallas kernels: 0 us -> 449 us
  waiting for transfers between devices: 284 us -> 26.6 us
  other arithmetic: 130 us -> 0.82 us
  local copies, waits for them, and re-layouts: 68.9 us -> 3.65 us
  starting transfers between devices: 15.8 us -> 49.7 us
  matrix products: 25.5 us -> 4.04 us
  blocking collectives: 52 us -> 40.8 us
    pallas_call x0 -> x14, Pallas kernels: none -> 449 us  [the longest x4 261 us: pack(): pl.pallas_call(lambda *refs: pack_kernel(part, *refs), out_shape=jax.Shap...]
    psum x1 -> x0, waiting for transfers between devices: 130 us -> none  [body(): lax.psum((local_gram, local_cross), ('space', 'snap'))]
    all_to_all x3 -> x11, waiting for transfers between devices: 154 us -> 26.6 us  [the longest x4 20.4 us: exchange(): lax.all_to_all(settled, 'snap', split_axis=0, concat_axis=0, tiled=True)]
    another operation x17 -> x0, other arithmetic: 120 us -> none  [the longest x14 78.9 us: body(): lower = jnp.linalg.cholesky(gram_total / rows_total)]
    all_to_all x3 -> x11, starting transfers between devices: 15.8 us -> 49.7 us  [the longest x4 20.2 us: exchange(): lax.all_to_all(settled, 'snap', split_axis=0, concat_axis=0, tiled=True)]
    all_to_all x4 -> x0, local copies, waits for them, and re-layouts: 24.7 us -> none  [the longest x3 19.3 us: body(): lax.all_to_all(owned_x, 'snap', split_axis=1, concat_axis=2, tiled=True)]
    another operation x17 -> x0, local copies, waits for them, and re-layouts: 14 us -> none
    unnamed x17 -> x20, local copies, waits for them, and re-layouts: 16.1 us -> 3.65 us
  transfers between devices with their start and end apart: 4 -> 12, of which waited for: 3 -> 2; matrix products, arithmetic and copies ran while one was open for 9% -> 0% of each run, Pallas kernels for 0% -> 75%
where the time goes in v1:
time: 590 us; the launch traced here: 589 us
  Pallas kernels  449 us (76%)
  starting transfers between devices  49.7 us (8%)
  blocking collectives  40.8 us (7%)
  waiting for transfers between devices  26.6 us (5%)
  between operations  14.3 us (2%)
    pallas_call x4, Pallas kernels, pack(): pl.pallas_call(lambda *refs: pack_kernel(part, *refs), out_shape=jax.Shap...  261 us
    pallas_call x4, Pallas kernels, settle(): pl.pallas_call(settle_kernel, out_shape=jax.ShapeDtypeStruct((shares, blo...  134 us
    all_gather x2, blocking collectives, sum_over_devices(): piece = jnp.sum(lax.all_gather(piece, 'snap', axis=0), axis=0)  30.7 us
    pallas_call x1, Pallas kernels, factor(): pl.pallas_call(lambda *refs: factor_kernel(tiles, rows_total, *refs), out...  24.5 us
    all_to_all x4, waiting for transfers between devices, exchange(): lax.all_to_all(settled, 'snap', split_axis=0, concat_axis=0, tiled=True)  20.4 us
    all_to_all x4, starting transfers between devices, exchange(): lax.all_to_all(settled, 'snap', split_axis=0, concat_axis=0, tiled=True)  20.2 us
    all_to_all x4, starting transfers between devices, exchange(): lax.all_to_all(sent, 'space', split_axis=0, concat_axis=0, tiled=True)  16.9 us
  transfers between devices with their start and end apart: 12, of which 2 were waited for; matrix products, arithmetic and copies ran while one was open for 0% of the time, Pallas kernels for 75%

profile of v1, /device:TPU:0, one launch (start us, length us, event | category | flops | bytes accessed | tf_op | source)
XLA Modules:
  0.0 588.8 jit_solution(10029204625070207905)
XLA Ops:
  7.2 5.6 plan.1
  12.8 5.2 all-to-all-start
  18.0 65.3 %pack.7 = bf16[128,4,16,128]{3,2,1,0:T(8,128)(2,1)} custom-call(s32[128]{0:T(128)} %get-tuple-element.11.refs_0_, bf16[128,4,2,16,128]{4,3,2,1,0:T(8,128)(2,1)} %bitcast.15), custom_call_target="tpu_custom_call" | custom-call | bytes 4194304 | tf_op jit(solution)/shard_map/pack/pallas_call | solution.py:102
  83.3 0.0 all-to-all-done
  83.3 0.0 copy-start.9
  83.3 4.2 all-to-all-start.8
  87.5 65.3 %pack.6 = bf16[128,4,16,128]{3,2,1,0:T(8,128)(2,1)} custom-call(s32[128]{0:T(128)} %get-tuple-element.11.refs_0_, bf16[128,4,2,16,128]{4,3,2,1,0:T(8,128)(2,1)} %bitcast.16), custom_call_target="tpu_custom_call" | custom-call | bytes 4194304 | tf_op jit(solution)/shard_map/pack/pallas_call | solution.py:102
  152.8 0.0 copy-done.9
  152.8 0.0 all-to-all-done.8.moved_ref
  152.9 0.0 copy-start.5
  152.9 1.3 copy-done.5
  154.2 4.2 all-to-all-start.6
  158.4 65.3 %pack.5 = bf16[128,4,16,128]{3,2,1,0:T(8,128)(2,1)} custom-call(s32[128]{0:T(128)} %get-tuple-element.11.refs_0_, bf16[128,4,2,16,128]{4,3,2,1,0:T(8,128)(2,1)} %bitcast.17), custom_call_target="tpu_custom_call" | custom-call | bytes 4194304 | tf_op jit(solution)/shard_map/pack/pallas_call | solution.py:102
  223.7 0.0 all-to-all-done.6.moved_ref
  223.7 0.0 copy-start.4
  223.7 1.3 copy-done.4
  225.0 4.4 all-to-all-start.3
  229.4 65.3 %pack.4 = bf16[128,4,16,128]{3,2,1,0:T(8,128)(2,1)} custom-call(s32[128]{0:T(128)} %get-tuple-element.11.refs_0_, bf16[128,4,2,16,128]{4,3,2,1,0:T(8,128)(2,1)} %bitcast.18), custom_call_target="tpu_custom_call" | custom-call | bytes 4194304 | tf_op jit(solution)/shard_map/pack/pallas_call | solution.py:102
  294.7 0.0 all-to-all-done.3.moved_ref
  294.7 4.1 all-to-all-start.1
  298.9 3.9 arrival.1.table_ref
  302.8 33.5 %settle.7 = bf16[4,64,16,128]{3,2,1,0:T(8,128)(2,1)} custom-call(s32[64]{0:T(128)} %arrival.1.table_ref, bf16[128,4,16,128]{3,2,1,0:T(8,128)(2,1)} %copy-done.5), custom_call_target="tpu_custom_call" | custom-call | bytes 2097152 | tf_op jit(solution)/shard_map/settle/pallas_call | solution.py:127
  336.3 0.0 all-to-all-done.1.moved_ref
  336.3 0.0 copy-start.6
  336.4 4.9 all-to-all-start.9
  341.2 33.5 %settle.5 = bf16[4,64,16,128]{3,2,1,0:T(8,128)(2,1)} custom-call(s32[64]{0:T(128)} %arrival.1.table_ref, bf16[128,4,16,128]{3,2,1,0:T(8,128)(2,1)} %all-to-all-done.3.moved_ref), custom_call_target="tpu_custom_call" | custom-call | bytes 2097152 | tf_op jit(solution)/shard_map/settle/pallas_call | solution.py:127
  374.8 0.0 copy-done.6
  374.8 0.0 all-to-all-done.9.refs_3_
  374.8 0.0 copy-start.7
  374.8 1.0 copy-done.7
  375.8 5.1 all-to-all-start.4
  380.9 33.5 %settle.4 = bf16[4,64,16,128]{3,2,1,0:T(8,128)(2,1)} custom-call(s32[64]{0:T(128)} %arrival.1.table_ref, bf16[128,4,16,128]{3,2,1,0:T(8,128)(2,1)} %copy-done.6), custom_call_target="tpu_custom_call" | custom-call | bytes 2097152 | tf_op jit(solution)/shard_map/settle/pallas_call | solution.py:127
  414.4 0.0 all-to-all-done.4.refs_1_
  414.4 0.0 copy-start
  414.5 5.1 all-to-all-start.2
  419.6 33.5 %settle.6 = bf16[4,64,16,128]{3,2,1,0:T(8,128)(2,1)} custom-call(s32[64]{0:T(128)} %arrival.1.table_ref, bf16[128,4,16,128]{3,2,1,0:T(8,128)(2,1)} %copy-done.4), custom_call_target="tpu_custom_call" | custom-call | bytes 2097152 | tf_op jit(solution)/shard_map/settle/pallas_call | solution.py:127
  453.1 0.0 copy-done
  453.1 0.0 all-to-all-done.2.refs_0_
  453.1 0.0 copy-start.2
  453.1 5.1 all-to-all-start.7
  458.2 0.0 copy-done.2
  458.2 4.3 gram_blocks.1
  462.5 20.4 %all-to-all-done.7.refs_2_ = bf16[4,64,16,128]{3,2,1,0:T(8,128)(2,1)S(1)} async-done(((bf16[4,64,16,128]{3,2,1,0:T(8,128)(2,1)}), bf16[4,64,16,128]{3,2,1,0:T(8,128)(2,1)S(1)}, u32[]{:S(2)}, u32[]{:S(2)}) %all-to-all-start.7) | async-done | bytes 1048608 | tf_op jit(solution)/shard_map/all_to_all | solution.py:425
  483.0 0.0 copy-start.8
  483.0 3.8 all-to-all-start.5
  486.8 0.0 copy-done.8
  486.8 5.0 cross_sum.1
  491.8 6.1 %all-to-all-done.5 = f32[8,160,128]{2,1,0:T(8,128)S(1)} async-done(((f32[8,160,128]{2,1,0:T(8,128)}), f32[8,160,128]{2,1,0:T(8,128)S(1)}, u32[]{:S(2)}, u32[]{:S(2)}) %all-to-all-start.5) | async-done | bytes 655392 | tf_op jit(solution)/shard_map/all_to_all | solution.py:395
  498.0 3.6 all-to-all-start.10
  501.5 0.0 all-gather.4.cloned.1.call-start
  501.6 14.5 %all-gather = f32[640,128]{1,0:T(8,128)S(1)} all-gather(f32[160,128]{1,0:T(8,128)S(1)} %reduce_sum.36), channel_id=2, replica_groups=mesh['space'=8,'snap'=4] {'snap'}, dimensions={0}, use_global_device_ids=true | all-gather | bytes 409600 | tf_op jit(solution)/shard_map/all_gather | solution.py:397
  516.1 10.2 %all_gather.20 = f32[1280,128]{1,0:T(8,128)S(1)} all-gather(f32[160,128]{1,0:T(8,128)S(1)} %reduce_sum.37), channel_id=1, replica_groups=mesh['space'=8,'snap'=4] {'space'}, dimensions={0}, use_global_device_ids=true | all-gather | bytes 737280 | tf_op jit(solution)/shard_map/all_gather | solution.py:398
  526.3 0.0 all-to-all-done.10
  526.3 0.1 reduce_sum.38
  526.4 16.2 %all-gather.1 = f32[256,512]{1,0:T(8,128)S(1)} all-gather(f32[64,512]{1,0:T(8,128)S(1)} %reduce_sum.38), channel_id=3, replica_groups=mesh['space'=8,'snap'=4] {'snap'}, dimensions={0}, use_global_device_ids=true | all-gather | bytes 655360 | tf_op jit(solution)/shard_map/all_gather | solution.py:397
  542.6 0.7 reduce_sum.39
  543.2 0.0 all-gather.4.cloned.1.call-update
  543.3 0.0 copy-start.1
  543.3 0.0 copy-start.3
  543.3 24.5 %factor.1 = (f32[512,512]{1,0:T(8,128)}, f32[512,512]{1,0:T(8,128)S(1)}, bf16[512,512]{1,0:T(8,128)(2,1)S(1)}, bf16[512,512]{1,0:T(8,128)(2,1)S(1)}, bf16[512,512]{1,0:T(8,128)(2,1)S(1)}) custom-call(f32[10,128,128]{2,1,0:T(8,128)S(1)} %bitcast.14), custom_call_target="tpu_custom_call" | custom-call | flops 40000000000 | bytes 2097152 | tf_op jit(solution)/shard_map/factor/pallas_call | solution.py:333
  567.8 0.0 copy-done.1
  567.8 0.0 copy-done.3
  567.8 10.0 %basis.1 = f32[64,2,16,512]{3,2,1,0:T(8,128)} custom-call(bf16[4,64,16,128]{3,2,1,0:T(8,128)(2,1)S(1)} %copy-done.3, bf16[4,64,16,128]{3,2,1,0:T(8,128)(2,1)S(1)} %copy-done.1, bf16[512,512]{1,0:T(8,128)(2,1)S(1)} %get-tuple-element.12.refs_2_, bf16[512,512]{1,0:T(8,128)(2,1)S(1)} %get-tuple-element.13.refs_3_, bf16[512,512]{1,0:T(8,128)(2,1)S(1)} %get-tuple-element.14.refs_4_), custom_call_target="tpu_custom_call" | custom-call | tf_op jit(solution)/shard_map/basis/pallas_call | solution.py:382
  577.9 4.0 convolution_multiply_fusion
  (3 shorter events, 0.1 us)
Async XLA Ops:
  12.8 70.5 %all-to-all-start = ((s32[8,1,128]{2,1,0:T(1,128)}), s32[8,1,128]{2,1,0:T(1,128)S(1)}, u32[]{:S(2)}, u32[]{:S(2)}) async-start(s32[8,1,128]{2,1,0:T(1,128)} %bitcast.25), calls=%async_computation | async-start | bytes 8192 | tf_op jit(solution)/shard_map/all_to_all | solution.py:412
  83.3 69.5 %copy-start.9 = (s32[8,1,128]{2,1,0:T(1,128)}, s32[8,1,128]{2,1,0:T(1,128)S(1)}, u32[]{:S(2)}) copy-start(s32[8,1,128]{2,1,0:T(1,128)S(1)} %all-to-all-done) | copy-start | bytes 12292
  83.3 69.5 %all-to-all-start.8 = ((bf16[128,4,16,128]{3,2,1,0:T(8,128)(2,1)}), bf16[128,4,16,128]{3,2,1,0:T(8,128)(2,1)S(1)}, u32[]{:S(2)}, u32[]{:S(2)}) async-start(bf16[128,4,16,128]{3,2,1,0:T(8,128)(2,1)} %pack.7), calls=%async_computation.8 | async-start | bytes 4194304 | tf_op jit(solution)/shard_map/all_to_all | solution.py:422
  152.9 1.3 copy-start.5
  154.2 69.5 %all-to-all-start.6 = ((bf16[128,4,16,128]{3,2,1,0:T(8,128)(2,1)}), bf16[128,4,16,128]{3,2,1,0:T(8,128)(2,1)S(1)}, u32[]{:S(2)}, u32[]{:S(2)}) async-start(bf16[128,4,16,128]{3,2,1,0:T(8,128)(2,1)} %pack.6), calls=%async_computation.6 | async-start | bytes 4194304 | tf_op jit(solution)/shard_map/all_to_all | solution.py:422
  223.7 1.3 copy-start.4
  225.0 69.7 %all-to-all-start.3 = ((bf16[128,4,16,128]{3,2,1,0:T(8,128)(2,1)}), bf16[128,4,16,128]{3,2,1,0:T(8,128)(2,1)}, u32[]{:S(2)}, u32[]{:S(2)}) async-start(bf16[128,4,16,128]{3,2,1,0:T(8,128)(2,1)} %pack.5), calls=%async_computation.3 | async-start | bytes 4194304 | tf_op jit(solution)/shard_map/all_to_all | solution.py:422
  294.7 41.6 %all-to-all-start.1 = ((bf16[128,4,16,128]{3,2,1,0:T(8,128)(2,1)}), bf16[128,4,16,128]{3,2,1,0:T(8,128)(2,1)S(1)}, u32[]{:S(2)}, u32[]{:S(2)}) async-start(bf16[128,4,16,128]{3,2,1,0:T(8,128)(2,1)} %pack.4), calls=%async_computation.1 | async-start | bytes 4194304 | tf_op jit(solution)/shard_map/all_to_all | solution.py:422
  336.3 38.4 %copy-start.6 = (bf16[128,4,16,128]{3,2,1,0:T(8,128)(2,1)}, bf16[128,4,16,128]{3,2,1,0:T(8,128)(2,1)S(1)}, u32[]{:S(2)}) copy-start(bf16[128,4,16,128]{3,2,1,0:T(8,128)(2,1)S(1)} %all-to-all-done.1.moved_ref) | copy-start | bytes 6291460
  336.4 38.4 %all-to-all-start.9 = ((bf16[4,64,16,128]{3,2,1,0:T(8,128)(2,1)}), bf16[4,64,16,128]{3,2,1,0:T(8,128)(2,1)S(1)}, u32[]{:S(2)}, u32[]{:S(2)}) async-start(bf16[4,64,16,128]{3,2,1,0:T(8,128)(2,1)} %settle.7), calls=%async_computation.9 | async-start | bytes 2097152 | tf_op jit(solution)/shard_map/all_to_all | solution.py:425
  374.8 1.0 copy-start.7
  375.8 38.6 %all-to-all-start.4 = ((bf16[4,64,16,128]{3,2,1,0:T(8,128)(2,1)}), bf16[4,64,16,128]{3,2,1,0:T(8,128)(2,1)S(1)}, u32[]{:S(2)}, u32[]{:S(2)}) async-start(bf16[4,64,16,128]{3,2,1,0:T(8,128)(2,1)} %settle.5), calls=%async_computation.4 | async-start | bytes 2097152 | tf_op jit(solution)/shard_map/all_to_all | solution.py:425
  414.4 38.7 %copy-start = (bf16[4,64,16,128]{3,2,1,0:T(8,128)(2,1)}, bf16[4,64,16,128]{3,2,1,0:T(8,128)(2,1)S(1)}, u32[]{:S(2)}) copy-start(bf16[4,64,16,128]{3,2,1,0:T(8,128)(2,1)S(1)} %all-to-all-done.4.refs_1_) | copy-start | bytes 3145732
  414.5 38.7 %all-to-all-start.2 = ((bf16[4,64,16,128]{3,2,1,0:T(8,128)(2,1)}), bf16[4,64,16,128]{3,2,1,0:T(8,128)(2,1)S(1)}, u32[]{:S(2)}, u32[]{:S(2)}) async-start(bf16[4,64,16,128]{3,2,1,0:T(8,128)(2,1)} %settle.4), calls=%async_computation.2 | async-start | bytes 2097152 | tf_op jit(solution)/shard_map/all_to_all | solution.py:425
  453.1 5.1 copy-start.2
  453.1 29.8 %all-to-all-start.7 = ((bf16[4,64,16,128]{3,2,1,0:T(8,128)(2,1)}), bf16[4,64,16,128]{3,2,1,0:T(8,128)(2,1)S(1)}, u32[]{:S(2)}, u32[]{:S(2)}) async-start(bf16[4,64,16,128]{3,2,1,0:T(8,128)(2,1)} %settle.6), calls=%async_computation.7 | async-start | bytes 2097152 | tf_op jit(solution)/shard_map/all_to_all | solution.py:425
  483.0 3.8 copy-start.8
  483.0 15.0 %all-to-all-start.5 = ((f32[8,160,128]{2,1,0:T(8,128)}), f32[8,160,128]{2,1,0:T(8,128)S(1)}, u32[]{:S(2)}, u32[]{:S(2)}) async-start(f32[8,160,128]{2,1,0:T(8,128)} %bitcast.21), calls=%async_computation.5 | async-start | bytes 1310720 | tf_op jit(solution)/shard_map/all_to_all | solution.py:395
  498.0 28.4 %all-to-all-start.10 = ((f32[8,64,512]{2,1,0:T(8,128)}), f32[8,64,512]{2,1,0:T(8,128)S(1)}, u32[]{:S(2)}, u32[]{:S(2)}) async-start(f32[8,64,512]{2,1,0:T(8,128)} %bitcast.19), calls=%async_computation.10 | async-start | bytes 2097152 | tf_op jit(solution)/shard_map/all_to_all | solution.py:395
  501.5 76.4 %all-gather.4.cloned.1.call-start = ((), (), s32[]{:S(2)}) async-start(), calls=%async_computation.11 | async-start | bytes 1179648 | tf_op jit(solution)/shard_map/all_gather | solution.py:398
  543.3 24.6 %copy-start.1 = (bf16[4,64,16,128]{3,2,1,0:T(8,128)(2,1)S(1)}, bf16[4,64,16,128]{3,2,1,0:T(8,128)(2,1)}, u32[]{:S(2)}) copy-start(bf16[4,64,16,128]{3,2,1,0:T(8,128)(2,1)} %copy-done) | copy-start | bytes 3145732
  543.3 24.5 %copy-start.3 = (bf16[4,64,16,128]{3,2,1,0:T(8,128)(2,1)S(1)}, bf16[4,64,16,128]{3,2,1,0:T(8,128)(2,1)}, u32[]{:S(2)}) copy-start(bf16[4,64,16,128]{3,2,1,0:T(8,128)(2,1)} %copy-done.2) | copy-start | bytes 3145732
Sparse Core Ops, SparseCore 0:
  543.4 21.3 all-gather.3

commit v2 on v1

--- a/solution.py
+++ b/solution.py
@@ -10,6 +10,7 @@
 TILE = 128
 GROUP = 8
 CELL_TILE = 16
+VMEM_BYTES = 32 * 1024 * 1024
 HIGHEST = lax.Precision.HIGHEST
 SMEM = pl.BlockSpec(memory_space=pltpu.SMEM)
 VMEM = pl.BlockSpec(memory_space=pltpu.VMEM)
@@ -18,123 +19,72 @@
 LANES_BY_LANES = (((1,), (1,)), ((), ()))
 
 
-def plan_kernel(slabs, capacity, per_slab, dest_ref, table_ref, meta_ref, count_ref):
-    def clear(i, _):
-        table_ref[i] = 0
-        meta_ref[i // capacity, i % capacity] = -1
-        return 0
-
-    def clear_count(i, _):
-        count_ref[i] = 0
-        return 0
+def pack_kernel(slabs, capacity, per_slab, parts, dest_ref, owned_ref, *refs):
+    out_refs, meta_ref, count_ref = refs[:parts], refs[parts], refs[parts + 1]
+    for slab in range(slabs):
+        count_ref[slab] = 0
 
     def place(i, _):
         block = dest_ref[i]
 
         @pl.when(block >= 0)
         def _():
-            slab = block // per_slab
+            slab = lax.div(block, per_slab)
             rank = count_ref[slab]
             count_ref[slab] = rank + 1
-            table_ref[slab * capacity + rank] = i
             meta_ref[slab, rank] = block - slab * per_slab
+            at = slab * capacity + rank
+            for part in range(parts):
+                out_refs[part][at] = owned_ref[i, :, part]
 
         return 0
 
-    lax.fori_loop(0, slabs, clear_count, 0)
-    lax.fori_loop(0, slabs * capacity, clear, 0)
-    lax.fori_loop(0, dest_ref.shape[0], place, 0)
-
-
-def plan(dest, slabs, capacity, per_slab):
-    return pl.pallas_call(
-        lambda *refs: plan_kernel(slabs, capacity, per_slab, *refs),
-        out_shape=(
-            jax.ShapeDtypeStruct((slabs * capacity,), jnp.int32),
-            jax.ShapeDtypeStruct((slabs, TILE), jnp.int32),
-        ),
-        in_specs=[SMEM],
-        out_specs=(SMEM, SMEM),
+    lax.fori_loop(0, dest_ref.shape[0], place, 0, unroll=4)
+    for slab in range(slabs):
+        meta_ref[slab, capacity] = count_ref[slab]
+
+
+def pack(dest, owned, slabs, per_slab):
+    slots, shares, parts, rows, width = owned.shape
+    sent = jax.ShapeDtypeStruct((slots, shares, rows, width), owned.dtype)
+    outs = pl.pallas_call(
+        lambda *refs: pack_kernel(slabs, slots // slabs, per_slab, parts, *refs),
+        out_shape=(sent,) * parts + (jax.ShapeDtypeStruct((slabs, TILE), jnp.int32),),
+        in_specs=[SMEM, VMEM],
+        out_specs=(VMEM,) * parts + (SMEM,),
         scratch_shapes=[pltpu.SMEM((slabs,), jnp.int32)],
-        name="plan",
-    )(dest)
-
-
-def arrival_kernel(slabs, capacity, meta_ref, table_ref):
-    def clear(i, _):
-        table_ref[i] = 0
-        return 0
-
-    def place(i, _):
-        block = meta_ref[i // capacity, i % capacity]
-
-        @pl.when(block >= 0)
-        def _():
-            table_ref[block] = i
-
-        return 0
-
-    lax.fori_loop(0, table_ref.shape[0], clear, 0)
-    lax.fori_loop(0, slabs * capacity, place, 0)
-
-
-def arrival(meta, slabs, capacity, per_slab):
-    return pl.pallas_call(
-        lambda *refs: arrival_kernel(slabs, capacity, *refs),
-        out_shape=jax.ShapeDtypeStruct((per_slab,), jnp.int32),
-        in_specs=[SMEM],
-        out_specs=SMEM,
-        name="arrival",
-    )(meta)
-
-
-def pack_kernel(part, table_ref, owned_ref, out_ref, sem):
-    def send(i, _):
-        pltpu.make_async_copy(owned_ref.at[table_ref[i], :, part], out_ref.at[i], sem).start()
-        return 0
-
-    lax.fori_loop(0, out_ref.shape[0], send, 0)
-    pltpu.make_async_copy(out_ref, out_ref, sem).wait()
-
-
-def pack(owned, table, part):
-    slots, shares, _, rows, width = owned.shape
-    return pl.pallas_call(
-        lambda *refs: pack_kernel(part, *refs),
-        out_shape=jax.ShapeDtypeStruct((slots, shares, rows, width), owned.dtype),
-        in_specs=[SMEM, ANY],
-        out_specs=ANY,
-        scratch_shapes=[pltpu.SemaphoreType.DMA],
+        compiler_params=pltpu.CompilerParams(vmem_limit_bytes=VMEM_BYTES),
         cost_estimate=pl.CostEstimate(
-            flops=0, bytes_accessed=2 * slots * shares * rows * width * 2, transcendentals=0
+            flops=0, bytes_accessed=2 * owned.size * 2, transcendentals=0
         ),
         name="pack",
-    )(table, owned)
-
-
-def settle_kernel(table_ref, moved_ref, out_ref, sem):
-    def send(i, _):
-        pltpu.make_async_copy(moved_ref.at[table_ref[i]], out_ref.at[:, i], sem).start()
-        return 0
-
-    lax.fori_loop(0, out_ref.shape[1], send, 0)
-    pltpu.make_async_copy(out_ref, out_ref, sem).wait()
-
-
-def settle(moved, table):
-    _, shares, rows, width = moved.shape
-    blocks = table.shape[0]
-    return pl.pallas_call(
-        settle_kernel,
-        out_shape=jax.ShapeDtypeStruct((shares, blocks, rows, width), moved.dtype),
-        in_specs=[SMEM, ANY],
-        out_specs=ANY,
-        scratch_shapes=[pltpu.SemaphoreType.DMA],
+    )(dest, owned)
+    return outs[:parts], outs[parts]
+
+
+def settle_kernel(slabs, capacity, meta_ref, moved_ref, out_ref):
+    for source in range(slabs):
+
+        def place(rank, _):
+            out_ref[:, meta_ref[source, rank]] = moved_ref[source * capacity + rank]
+            return 0
+
+        lax.fori_loop(0, meta_ref[source, capacity], place, 0)
+
+
+def settle(meta, moved, slabs, per_slab):
+    slots, shares, rows, width = moved.shape
+    return pl.pallas_call(
+        lambda *refs: settle_kernel(slabs, slots // slabs, *refs),
+        out_shape=jax.ShapeDtypeStruct((shares, per_slab, rows, width), moved.dtype),
+        in_specs=[SMEM, VMEM],
+        out_specs=VMEM,
+        compiler_params=pltpu.CompilerParams(vmem_limit_bytes=VMEM_BYTES),
         cost_estimate=pl.CostEstimate(
-            flops=0, bytes_accessed=2 * shares * blocks * rows * width * 2, transcendentals=0
+            flops=0, bytes_accessed=2 * moved.size, transcendentals=0
         ),
         name="settle",
-    )(table, moved)
+    )(meta, moved)
 
 
 def whole_rows(ref):
@@ -348,7 +298,7 @@
             tile,
             tile,
         ],
-        compiler_params=pltpu.CompilerParams(vmem_limit_bytes=32 * 1024 * 1024),
+        compiler_params=pltpu.CompilerParams(vmem_limit_bytes=VMEM_BYTES),
         cost_estimate=pl.CostEstimate(
             flops=40 * 10**9, bytes_accessed=8 * full * full, transcendentals=full
         ),
@@ -385,7 +335,7 @@
         out_shape=jax.ShapeDtypeStruct((blocks, parts, rows, full), jnp.float32),
         in_specs=[spec] * parts + [term] * 3,
         out_specs=pl.BlockSpec((blocks // steps, parts, rows, full), lambda i: (i, 0, 0, 0)),
-        compiler_params=pltpu.CompilerParams(vmem_limit_bytes=32 * 1024 * 1024),
+        compiler_params=pltpu.CompilerParams(vmem_limit_bytes=VMEM_BYTES),
         name="basis",
     )(*cells, *terms)
 
@@ -394,7 +344,10 @@
     lanes = value.shape[-1]
     pieces = lax.all_to_all(value, "space", split_axis=0, concat_axis=0, tiled=True)
     piece = jnp.sum(pieces.reshape(slabs, -1, lanes), axis=0)
-    piece = jnp.sum(lax.all_gather(piece, "snap", axis=0), axis=0)
+    hop = 1
+    while hop < shares:
+        piece += lax.ppermute(piece, "snap", [(i, i ^ hop) for i in range(shares)])
+        hop *= 2
     return lax.all_gather(piece, "space", axis=0, tiled=True)
 
 
@@ -402,32 +355,29 @@
     slabs = lax.axis_size("space")
     shares = lax.axis_size("snap")
     slots, patch, width = owned_x.shape
-    capacity = slots // slabs
     per_slab = slots // 2
     parts = patch // shares // CELL_TILE
     rows_total = slabs * per_slab * patch
     full = shares * width
 
-    table, meta = plan(patch_dest, slabs, capacity, per_slab)
+    def parted(owned):
+        return owned.reshape(slots, shares, parts, CELL_TILE, width)
+
+    def exchange(sent, meta):
+        cells = []
+        for part in sent:
+            moved = lax.all_to_all(part, "space", split_axis=0, concat_axis=0, tiled=True)
+            settled = settle(meta, moved, slabs, per_slab)
+            cells.append(lax.all_to_all(settled, "snap", split_axis=0, concat_axis=0, tiled=True))
+        return cells
+
+    sent_x, meta = pack(patch_dest, parted(owned_x), slabs, per_slab)
     meta = lax.all_to_all(
         meta.reshape(slabs, 1, TILE), "space", split_axis=0, concat_axis=0, tiled=True
     ).reshape(slabs, TILE)
-    arrived = arrival(meta, slabs, capacity, per_slab)
-
-    def exchange(owned):
-        owned = owned.reshape(slots, shares, parts, CELL_TILE, width)
-        cells = []
-        for part in range(parts):
-            sent = pack(owned, table, part)
-            moved = lax.all_to_all(sent, "space", split_axis=0, concat_axis=0, tiled=True)
-            settled = settle(moved, arrived)
-            cells.append(
-                lax.all_to_all(settled, "snap", split_axis=0, concat_axis=0, tiled=True)
-            )
-        return cells
-
-    x_cells = exchange(owned_x)
-    y_cells = exchange(owned_y)
+    sent_y, _ = pack(patch_dest, parted(owned_y), slabs, per_slab)
+    x_cells = exchange(sent_x, meta)
+    y_cells = exchange(sent_y, meta)
 
     tiles = full // TILE
     pairs = tiles * (tiles + 1) // 2

time: 590 us -> 359 us (0.61)
  Pallas kernels: 449 us -> 57.3 us
  waiting for transfers between devices: 26.6 us -> 151 us
  blocking collectives: 40.8 us -> 78.9 us
  starting transfers between devices: 49.7 us -> 36.1 us
  local copies, waits for them, and re-layouts: 3.65 us -> 15.9 us
    pallas_call x10 -> x6, Pallas kernels: 405 us -> 13.5 us  [the longest x2 7.13 us: pack(): pl.pallas_call(lambda *refs: pack_kernel(slabs, slots // slabs, per_slab,...]
    all_to_all x0 -> x3, blocking collectives: none -> 69.8 us  [the longest x2 60.7 us: exchange(): lax.all_to_all(part, 'space', split_axis=0, concat_axis=0, tiled=True)]
    all_to_all x4, waiting for transfers between devices: 20.4 us -> 84.3 us  [exchange(): lax.all_to_all(settled, 'snap', split_axis=0, concat_axis=0, tiled=True)]
    all_to_all x5 -> x2, waiting for transfers between devices: 0.01 us -> 40.9 us  [exchange(): lax.all_to_all(part, 'space', split_axis=0, concat_axis=0, tiled=True)]
    all_gather x2 -> x0, blocking collectives: 30.7 us -> none  [sum_over_devices(): piece = jnp.sum(lax.all_gather(piece, 'snap', axis=0), axis=0)]
    all_to_all x2, waiting for transfers between devices: 6.15 us -> 21.3 us  [sum_over_devices(): lax.all_to_all(value, 'space', split_axis=0, concat_axis=0, tiled=True)]
    all_to_all x5 -> x2, starting transfers between devices: 22.1 us -> 7.34 us  [exchange(): lax.all_to_all(part, 'space', split_axis=0, concat_axis=0, tiled=True)]
    unnamed x20 -> x42, local copies, waits for them, and re-layouts: 3.65 us -> 15.9 us
  transfers between devices with their start and end apart: 12 -> 13, of which waited for: 2 -> 10; matrix products, arithmetic and copies ran while one was open for 0% -> 0% of each run, Pallas kernels for 75% -> 15%
where the time goes in v2:
time: 359 us; the launch traced here: 358 us
  waiting for transfers between devices  151 us (42%)
  blocking collectives  78.9 us (22%)
  Pallas kernels  57.3 us (16%)
  starting transfers between devices  36.1 us (10%)
  local copies, waits for them, and re-layouts  15.9 us (4%)
  between operations  14.3 us (4%)
  matrix products  4.04 us (1%)
    all_to_all x4, waiting for transfers between devices, exchange(): lax.all_to_all(settled, 'snap', split_axis=0, concat_axis=0, tiled=True)  84.3 us
    all_to_all x2, blocking collectives, exchange(): lax.all_to_all(part, 'space', split_axis=0, concat_axis=0, tiled=True)  60.7 us
    all_to_all x2, waiting for transfers between devices, exchange(): lax.all_to_all(part, 'space', split_axis=0, concat_axis=0, tiled=True)  40.9 us
    pallas_call x1, Pallas kernels, factor(): pl.pallas_call(lambda *refs: factor_kernel(tiles, rows_total, *refs), out...  24.5 us
    all_to_all x2, waiting for transfers between devices, sum_over_devices(): lax.all_to_all(value, 'space', split_axis=0, concat_axis=0, tiled=True)  21.3 us
    unnamed x42, local copies, waits for them, and re-layouts  15.9 us
    all_to_all x4, starting transfers between devices, exchange(): lax.all_to_all(settled, 'snap', split_axis=0, concat_axis=0, tiled=True)  15.6 us
    pallas_call x1, Pallas kernels, basis(): pl.pallas_call(lambda *refs: basis_kernel(parts, *refs), grid=(steps,), o...  10 us
  transfers between devices with their start and end apart: 13, of which 10 were waited for; matrix products, arithmetic and copies ran while one was open for 0% of the time, Pallas kernels for 15%

profile of v2, /device:TPU:0, one launch (start us, length us, event | category | flops | bytes accessed | tf_op | source)
XLA Modules:
  0.0 358.2 jit_solution(1159199471302670078)
XLA Ops:
  7.2 2.2 copy-done.10
  9.4 0.7 copy-done.17
  10.0 3.6 %pack.2 = (bf16[128,4,16,128]{3,2,1,0:T(8,128)(2,1)S(1)}, bf16[128,4,16,128]{3,2,1,0:T(8,128)(2,1)S(1)}, s32[8,128]{1,0:T(8,128)S(1)}) custom-call(s32[128]{0:T(128)S(1)} %copy-done.17, bf16[128,4,2,16,128]{4,3,2,1,0:T(8,128)(2,1)S(1)} %bitcast.12), custom_call_target="tpu_custom_call" | custom-call | bytes 8388608 | tf_op jit(solution)/shard_map/pack/pallas_call | solution.py:50
  13.6 0.0 copy-start.15
  13.6 9.1 %all_to_all.63 = s32[8,1,128]{2,1,0:T(1,128)S(1)} all-to-all(s32[8,1,128]{2,1,0:T(1,128)S(1)} %bitcast.19), channel_id=1, replica_groups=mesh['space'=8,'snap'=4] {'space'}, dimensions={0} | all-to-all | bytes 8192 | tf_op jit(solution)/shard_map/all_to_all | solution.py:375
  22.7 29.8 %all_to_all.64.refs_1_ = bf16[128,4,16,128]{3,2,1,0:T(8,128)(2,1)} all-to-all(bf16[128,4,16,128]{3,2,1,0:T(8,128)(2,1)S(1)} %get-tuple-element.15), channel_id=1, replica_groups=mesh['space'=8,'snap'=4] {'space'}, dimensions={0} | all-to-all | bytes 4194304 | tf_op jit(solution)/shard_map/all_to_all | solution.py:369
  52.4 0.0 copy-done.15
  52.4 3.7 %all-to-all-start.1 = ((bf16[128,4,16,128]{3,2,1,0:T(8,128)(2,1)}), bf16[128,4,16,128]{3,2,1,0:T(8,128)(2,1)S(1)}, u32[]{:S(2)}, u32[]{:S(2)}) async-start(bf16[128,4,16,128]{3,2,1,0:T(8,128)(2,1)} %copy-done.15), calls=%async_computation.1 | async-start | bytes 4194304 | tf_op jit(solution)/shard_map/all_to_all | solution.py:369
  56.2 0.0 copy-done.18
  56.2 0.0 copy-start.11
  56.2 2.2 copy-done.11
  58.4 3.5 pack.3
  61.9 0.0 copy-start.14
  61.9 1.4 copy-done.14
  63.3 1.4 copy-done.16
  64.7 18.0 %all-to-all-done.1.refs_1_ = bf16[128,4,16,128]{3,2,1,0:T(8,128)(2,1)S(1)} async-done(((bf16[128,4,16,128]{3,2,1,0:T(8,128)(2,1)}), bf16[128,4,16,128]{3,2,1,0:T(8,128)(2,1)S(1)}, u32[]{:S(2)}, u32[]{:S(2)}) %all-to-all-start.1) | async-done | bytes 2097184 | tf_op jit(solution)/shard_map/all_to_all | solution.py:369
  82.8 30.9 %all_to_all.65.refs_1_ = bf16[128,4,16,128]{3,2,1,0:T(8,128)(2,1)} all-to-all(bf16[128,4,16,128]{3,2,1,0:T(8,128)(2,1)} %copy-done.16), channel_id=1, replica_groups=mesh['space'=8,'snap'=4] {'space'}, dimensions={0} | all-to-all | bytes 4194304 | tf_op jit(solution)/shard_map/all_to_all | solution.py:369
  113.7 0.0 copy-done.6
  113.7 3.6 %all-to-all-start.8 = ((bf16[128,4,16,128]{3,2,1,0:T(8,128)(2,1)}), bf16[128,4,16,128]{3,2,1,0:T(8,128)(2,1)S(1)}, u32[]{:S(2)}, u32[]{:S(2)}) async-start(bf16[128,4,16,128]{3,2,1,0:T(8,128)(2,1)} %copy-done.14), calls=%async_computation.8 | async-start | bytes 4194304 | tf_op jit(solution)/shard_map/all_to_all | solution.py:369
  117.3 1.6 copy-done.9
  118.9 1.1 settle.5
  120.0 0.0 copy-start.12
  120.0 1.0 copy-done.12
  121.0 22.9 %all-to-all-done.8.refs_1_ = bf16[128,4,16,128]{3,2,1,0:T(8,128)(2,1)S(1)} async-done(((bf16[128,4,16,128]{3,2,1,0:T(8,128)(2,1)}), bf16[128,4,16,128]{3,2,1,0:T(8,128)(2,1)S(1)}, u32[]{:S(2)}, u32[]{:S(2)}) %all-to-all-start.8) | async-done | bytes 2097184 | tf_op jit(solution)/shard_map/all_to_all | solution.py:369
  143.9 1.4 copy-done.4
  145.2 5.0 %all-to-all-start.4 = ((bf16[4,64,16,128]{3,2,1,0:T(8,128)(2,1)}), bf16[4,64,16,128]{3,2,1,0:T(8,128)(2,1)S(1)}, u32[]{:S(2)}, u32[]{:S(2)}) async-start(bf16[4,64,16,128]{3,2,1,0:T(8,128)(2,1)} %copy-done.12), calls=%async_computation.4 | async-start | bytes 2097152 | tf_op jit(solution)/shard_map/all_to_all | solution.py:371
  150.2 1.1 settle.4
  151.4 0.0 copy-start.13
  151.4 1.0 copy-done.13
  152.3 20.8 %all-to-all-done.4.refs_1_ = bf16[4,64,16,128]{3,2,1,0:T(8,128)(2,1)S(1)} async-done(((bf16[4,64,16,128]{3,2,1,0:T(8,128)(2,1)}), bf16[4,64,16,128]{3,2,1,0:T(8,128)(2,1)S(1)}, u32[]{:S(2)}, u32[]{:S(2)}) %all-to-all-start.4) | async-done | bytes 1048608 | tf_op jit(solution)/shard_map/all_to_all | solution.py:371
  173.1 3.5 all-to-all-start.2
  176.6 1.6 copy-done.8
  178.2 2.1 settle.6
  180.3 21.1 %all-to-all-done.2.refs_0_ = bf16[4,64,16,128]{3,2,1,0:T(8,128)(2,1)S(1)} async-done(((bf16[4,64,16,128]{3,2,1,0:T(8,128)(2,1)}), bf16[4,64,16,128]{3,2,1,0:T(8,128)(2,1)S(1)}, u32[]{:S(2)}, u32[]{:S(2)}) %all-to-all-start.2) | async-done | bytes 1048608 | tf_op jit(solution)/shard_map/all_to_all | solution.py:371
  201.4 3.5 all-to-all-start.7
  204.9 1.6 copy-done.5
  206.5 2.1 settle.7
  208.6 21.5 %all-to-all-done.7.refs_2_ = bf16[4,64,16,128]{3,2,1,0:T(8,128)(2,1)S(1)} async-done(((bf16[4,64,16,128]{3,2,1,0:T(8,128)(2,1)}), bf16[4,64,16,128]{3,2,1,0:T(8,128)(2,1)S(1)}, u32[]{:S(2)}, u32[]{:S(2)}) %all-to-all-start.7) | async-done | bytes 1048608 | tf_op jit(solution)/shard_map/all_to_all | solution.py:371
  230.1 3.5 all-to-all-start.9
  233.6 4.3 %gram_blocks.1 = f32[10,128,128]{2,1,0:T(8,128)} custom-call(bf16[4,64,16,128]{3,2,1,0:T(8,128)(2,1)} %copy-done.2, bf16[4,64,16,128]{3,2,1,0:T(8,128)(2,1)} %copy-done), custom_call_target="tpu_custom_call" | custom-call | tf_op jit(solution)/shard_map/gram_blocks/pallas_call | solution.py:122
  237.9 20.9 %all-to-all-done.9.refs_3_ = bf16[4,64,16,128]{3,2,1,0:T(8,128)(2,1)S(1)} async-done(((bf16[4,64,16,128]{3,2,1,0:T(8,128)(2,1)}), bf16[4,64,16,128]{3,2,1,0:T(8,128)(2,1)S(1)}, u32[]{:S(2)}, u32[]{:S(2)}) %all-to-all-start.9) | async-done | bytes 1048608 | tf_op jit(solution)/shard_map/all_to_all | solution.py:371
  258.8 5.4 %all-to-all-start.5 = ((f32[8,160,128]{2,1,0:T(8,128)}), f32[8,160,128]{2,1,0:T(8,128)S(1)}, u32[]{:S(2)}, u32[]{:S(2)}) async-start(f32[8,160,128]{2,1,0:T(8,128)} %bitcast.22), calls=%async_computation.5 | async-start | bytes 1310720 | tf_op jit(solution)/shard_map/all_to_all | solution.py:345
  264.2 5.0 %cross_sum.1 = f32[512,512]{1,0:T(8,128)} custom-call(bf16[4,64,16,128]{3,2,1,0:T(8,128)(2,1)} %copy-done.2, bf16[4,64,16,128]{3,2,1,0:T(8,128)(2,1)} %copy-done, bf16[4,64,16,128]{3,2,1,0:T(8,128)(2,1)} %copy-done.19, bf16[4,64,16,128]{3,2,1,0:T(8,128)(2,1)} %copy-done.20), custom_call_target="tpu_custom_call" | custom-call | tf_op jit(solution)/shard_map/cross_sum/pallas_call | solution.py:153
  269.2 6.2 %all-to-all-done.5 = f32[8,160,128]{2,1,0:T(8,128)S(1)} async-done(((f32[8,160,128]{2,1,0:T(8,128)}), f32[8,160,128]{2,1,0:T(8,128)S(1)}, u32[]{:S(2)}, u32[]{:S(2)}) %all-to-all-start.5) | async-done | bytes 655392 | tf_op jit(solution)/shard_map/all_to_all | solution.py:345
  275.3 3.6 all-to-all-start.10
  278.9 0.0 all-gather.2.cloned.1.call-start
  279.0 0.1 collective-permute-start
  279.0 15.2 %all-to-all-done.10 = f32[8,64,512]{2,1,0:T(8,128)S(1)} async-done(((f32[8,64,512]{2,1,0:T(8,128)}), f32[8,64,512]{2,1,0:T(8,128)S(1)}, u32[]{:S(2)}, u32[]{:S(2)}) %all-to-all-start.10) | async-done | bytes 1048608 | tf_op jit(solution)/shard_map/all_to_all | solution.py:345
  294.2 0.1 reduce_sum.19
  294.3 0.1 collective-permute-start.2
  294.4 0.0 collective-permute-done
  294.4 2.1 collective-permute-start.1
  296.5 3.7 %collective-permute-done.1 = f32[160,128]{1,0:T(8,128)S(1)} collective-permute-done((f32[160,128]{1,0:T(8,128)S(1)}, f32[160,128]{1,0:T(8,128)S(1)}, u32[]{:S(2)}, u32[]{:S(2)}) %collective-permute-start.1) | collective-permute-done | bytes 81952 | tf_op jit(solution)/shard_map/ppermute | solution.py:349
  300.2 0.6 collective-permute-done.2
  300.8 2.0 collective-permute-start.3
  302.9 9.1 %all_gather.6 = f32[1280,128]{1,0:T(8,128)S(1)} all-gather(f32[160,128]{1,0:T(8,128)S(1)} %add.13), channel_id=1, replica_groups=mesh['space'=8,'snap'=4] {'space'}, dimensions={0}, use_global_device_ids=true | all-gather | bytes 737280 | tf_op jit(solution)/shard_map/all_gather | solution.py:351
  312.0 0.0 collective-permute-done.3
  312.0 0.7 add.15
  312.7 0.0 all-gather.2.cloned.1.call-update
  312.7 0.0 copy-start.1
  312.7 0.0 copy-start.3
  312.7 24.5 %factor.1 = (f32[512,512]{1,0:T(8,128)}, f32[512,512]{1,0:T(8,128)S(1)}, bf16[512,512]{1,0:T(8,128)(2,1)S(1)}, bf16[512,512]{1,0:T(8,128)(2,1)S(1)}, bf16[512,512]{1,0:T(8,128)(2,1)S(1)}) custom-call(f32[10,128,128]{2,1,0:T(8,128)S(1)} %bitcast.14), custom_call_target="tpu_custom_call" | custom-call | flops 40000000000 | bytes 2097152 | tf_op jit(solution)/shard_map/factor/pallas_call | solution.py:283
  337.3 10.0 %basis.1 = f32[64,2,16,512]{3,2,1,0:T(8,128)} custom-call(bf16[4,64,16,128]{3,2,1,0:T(8,128)(2,1)S(1)} %copy-done.3, bf16[4,64,16,128]{3,2,1,0:T(8,128)(2,1)S(1)} %copy-done.1, bf16[512,512]{1,0:T(8,128)(2,1)S(1)} %get-tuple-element.16.refs_2_, bf16[512,512]{1,0:T(8,128)(2,1)S(1)} %get-tuple-element.17.refs_3_, bf16[512,512]{1,0:T(8,128)(2,1)S(1)} %get-tuple-element.18.refs_4_), custom_call_target="tpu_custom_call" | custom-call | tf_op jit(solution)/shard_map/basis/pallas_call | solution.py:332
  347.3 4.0 %convolution_multiply_fusion = f32[512,512]{1,0:T(8,128)} fusion(f32[512,512]{1,0:T(8,128)S(1)} %get-tuple-element.20, f32[512,512]{1,0:T(8,128)} %all-gather.2.cloned.1.call-done), kind=kOutput, calls=%fused_computation | convolution fusion | flops 1610874880 | bytes 3145728 | tf_op jit(solution)/shard_map/dot_general | solution.py:390
  (26 shorter events, 0.1 us)
Async XLA Ops:
  7.2 2.2 copy-start.10
  9.4 0.7 copy-start.17
  13.6 38.8 %copy-start.15 = (bf16[128,4,16,128]{3,2,1,0:T(8,128)(2,1)}, bf16[128,4,16,128]{3,2,1,0:T(8,128)(2,1)S(1)}, u32[]{:S(2)}) copy-start(bf16[128,4,16,128]{3,2,1,0:T(8,128)(2,1)S(1)} %get-tuple-element.14) | copy-start | bytes 6291460
  52.4 3.7 %copy-start.18 = (s32[128]{0:T(128)S(1)}, s32[128]{0:T(128)}, u32[]{:S(2)}) copy-start(s32[128]{0:T(128)} %refs_0_.3) | copy-start | bytes 1540
  52.4 30.3 %all-to-all-start.1 = ((bf16[128,4,16,128]{3,2,1,0:T(8,128)(2,1)}), bf16[128,4,16,128]{3,2,1,0:T(8,128)(2,1)S(1)}, u32[]{:S(2)}, u32[]{:S(2)}) async-start(bf16[128,4,16,128]{3,2,1,0:T(8,128)(2,1)} %copy-done.15), calls=%async_computation.1 | async-start | bytes 4194304 | tf_op jit(solution)/shard_map/all_to_all | solution.py:369
  56.2 2.2 copy-start.11
  61.9 1.4 copy-start.14
  63.3 1.4 copy-start.16
  82.8 30.9 %copy-start.6 = (bf16[128,4,16,128]{3,2,1,0:T(8,128)(2,1)}, bf16[128,4,16,128]{3,2,1,0:T(8,128)(2,1)S(1)}, u32[]{:S(2)}) copy-start(bf16[128,4,16,128]{3,2,1,0:T(8,128)(2,1)S(1)} %all-to-all-done.1.refs_1_) | copy-start | bytes 6291460
  113.7 30.2 %all-to-all-start.8 = ((bf16[128,4,16,128]{3,2,1,0:T(8,128)(2,1)}), bf16[128,4,16,128]{3,2,1,0:T(8,128)(2,1)S(1)}, u32[]{:S(2)}, u32[]{:S(2)}) async-start(bf16[128,4,16,128]{3,2,1,0:T(8,128)(2,1)} %copy-done.14), calls=%async_computation.8 | async-start | bytes 4194304 | tf_op jit(solution)/shard_map/all_to_all | solution.py:369
  117.3 1.6 copy-start.9
  120.0 1.0 copy-start.12
  143.9 1.4 copy-start.4
  145.2 5.0 %copy-start.7 = (bf16[128,4,16,128]{3,2,1,0:T(8,128)(2,1)S(1)}, bf16[128,4,16,128]{3,2,1,0:T(8,128)(2,1)}, u32[]{:S(2)}) copy-start(bf16[128,4,16,128]{3,2,1,0:T(8,128)(2,1)} %copy-done.6) | copy-start | bytes 6291460
  145.2 27.9 %all-to-all-start.4 = ((bf16[4,64,16,128]{3,2,1,0:T(8,128)(2,1)}), bf16[4,64,16,128]{3,2,1,0:T(8,128)(2,1)S(1)}, u32[]{:S(2)}, u32[]{:S(2)}) async-start(bf16[4,64,16,128]{3,2,1,0:T(8,128)(2,1)} %copy-done.12), calls=%async_computation.4 | async-start | bytes 2097152 | tf_op jit(solution)/shard_map/all_to_all | solution.py:371
  151.4 1.0 copy-start.13
  173.1 7.2 %copy-start = (bf16[4,64,16,128]{3,2,1,0:T(8,128)(2,1)}, bf16[4,64,16,128]{3,2,1,0:T(8,128)(2,1)S(1)}, u32[]{:S(2)}) copy-start(bf16[4,64,16,128]{3,2,1,0:T(8,128)(2,1)S(1)} %all-to-all-done.4.refs_1_) | copy-start | bytes 3145732
  173.1 28.2 %all-to-all-start.2 = ((bf16[4,64,16,128]{3,2,1,0:T(8,128)(2,1)}), bf16[4,64,16,128]{3,2,1,0:T(8,128)(2,1)S(1)}, u32[]{:S(2)}, u32[]{:S(2)}) async-start(bf16[4,64,16,128]{3,2,1,0:T(8,128)(2,1)} %copy-done.13), calls=%async_computation.2 | async-start | bytes 2097152 | tf_op jit(solution)/shard_map/all_to_all | solution.py:371
  176.6 1.6 copy-start.8
  201.4 7.2 %copy-start.2 = (bf16[4,64,16,128]{3,2,1,0:T(8,128)(2,1)}, bf16[4,64,16,128]{3,2,1,0:T(8,128)(2,1)S(1)}, u32[]{:S(2)}) copy-start(bf16[4,64,16,128]{3,2,1,0:T(8,128)(2,1)S(1)} %all-to-all-done.2.refs_0_) | copy-start | bytes 3145732
  201.4 28.7 %all-to-all-start.7 = ((bf16[4,64,16,128]{3,2,1,0:T(8,128)(2,1)}), bf16[4,64,16,128]{3,2,1,0:T(8,128)(2,1)S(1)}, u32[]{:S(2)}, u32[]{:S(2)}) async-start(bf16[4,64,16,128]{3,2,1,0:T(8,128)(2,1)} %settle.6), calls=%async_computation.7 | async-start | bytes 2097152 | tf_op jit(solution)/shard_map/all_to_all | solution.py:371
  204.9 1.6 copy-start.5
  230.1 7.8 %copy-start.19 = (bf16[4,64,16,128]{3,2,1,0:T(8,128)(2,1)}, bf16[4,64,16,128]{3,2,1,0:T(8,128)(2,1)S(1)}, u32[]{:S(2)}) copy-start(bf16[4,64,16,128]{3,2,1,0:T(8,128)(2,1)S(1)} %all-to-all-done.7.refs_2_) | copy-start | bytes 3145732
  230.1 28.7 %all-to-all-start.9 = ((bf16[4,64,16,128]{3,2,1,0:T(8,128)(2,1)}), bf16[4,64,16,128]{3,2,1,0:T(8,128)(2,1)S(1)}, u32[]{:S(2)}, u32[]{:S(2)}) async-start(bf16[4,64,16,128]{3,2,1,0:T(8,128)(2,1)} %settle.7), calls=%async_computation.9 | async-start | bytes 2097152 | tf_op jit(solution)/shard_map/all_to_all | solution.py:371
  258.8 5.4 %copy-start.20 = (bf16[4,64,16,128]{3,2,1,0:T(8,128)(2,1)}, bf16[4,64,16,128]{3,2,1,0:T(8,128)(2,1)S(1)}, u32[]{:S(2)}) copy-start(bf16[4,64,16,128]{3,2,1,0:T(8,128)(2,1)S(1)} %all-to-all-done.9.refs_3_) | copy-start | bytes 3145732
  258.8 16.5 %all-to-all-start.5 = ((f32[8,160,128]{2,1,0:T(8,128)}), f32[8,160,128]{2,1,0:T(8,128)S(1)}, u32[]{:S(2)}, u32[]{:S(2)}) async-start(f32[8,160,128]{2,1,0:T(8,128)} %bitcast.22), calls=%async_computation.5 | async-start | bytes 1310720 | tf_op jit(solution)/shard_map/all_to_all | solution.py:345
  275.3 18.9 %all-to-all-start.10 = ((f32[8,64,512]{2,1,0:T(8,128)}), f32[8,64,512]{2,1,0:T(8,128)S(1)}, u32[]{:S(2)}, u32[]{:S(2)}) async-start(f32[8,64,512]{2,1,0:T(8,128)} %bitcast.20), calls=%async_computation.10 | async-start | bytes 2097152 | tf_op jit(solution)/shard_map/all_to_all | solution.py:345
  278.9 68.4 %all-gather.2.cloned.1.call-start = ((), (), s32[]{:S(2)}) async-start(), calls=%async_computation.11 | async-start | bytes 1179648 | tf_op jit(solution)/shard_map/all_gather | solution.py:351
  279.0 15.4 %collective-permute-start = (f32[160,128]{1,0:T(8,128)S(1)}, f32[160,128]{1,0:T(8,128)S(1)}, u32[]{:S(2)}, u32[]{:S(2)}) collective-permute-start(f32[160,128]{1,0:T(8,128)S(1)} %reduce_sum.18), channel_id=1, source_target_pairs={{0,1},{1,0},{2,3},{3,2},{4,5},{5,4},{6,7},{7,6},{8,9},{9,8},{10,11... | collective-permute-start | bytes 245768 | tf_op jit(solution)/shard_map/ppermute | solution.py:349
  294.3 6.5 %collective-permute-start.2 = (f32[64,512]{1,0:T(8,128)S(1)}, f32[64,512]{1,0:T(8,128)S(1)}, u32[]{:S(2)}, u32[]{:S(2)}) collective-permute-start(f32[64,512]{1,0:T(8,128)S(1)} %reduce_sum.19), channel_id=1, source_target_pairs={{0,1},{1,0},{2,3},{3,2},{4,5},{5,4},{6,7},{7,6},{8,9},{9,8},{10,11... | collective-permute-start | bytes 393224 | tf_op jit(solution)/shard_map/ppermute | solution.py:349
  294.4 5.8 %collective-permute-start.1 = (f32[160,128]{1,0:T(8,128)S(1)}, f32[160,128]{1,0:T(8,128)S(1)}, u32[]{:S(2)}, u32[]{:S(2)}) collective-permute-start(f32[160,128]{1,0:T(8,128)S(1)} %add.12), channel_id=1, source_target_pairs={{0,2},{1,3},{2,0},{3,1},{4,6},{5,7},{6,4},{7,5},{8,10},{9,11},{10,... | collective-permute-start | bytes 245768 | tf_op jit(solution)/shard_map/ppermute | solution.py:349
  300.8 11.2 %collective-permute-start.3 = (f32[64,512]{1,0:T(8,128)S(1)}, f32[64,512]{1,0:T(8,128)S(1)}, u32[]{:S(2)}, u32[]{:S(2)}) collective-permute-start(f32[64,512]{1,0:T(8,128)S(1)} %add.14), channel_id=1, source_target_pairs={{0,2},{1,3},{2,0},{3,1},{4,6},{5,7},{6,4},{7,5},{8,10},{9,11},{10,... | collective-permute-start | bytes 393224 | tf_op jit(solution)/shard_map/ppermute | solution.py:349
  312.7 24.6 %copy-start.1 = (bf16[4,64,16,128]{3,2,1,0:T(8,128)(2,1)S(1)}, bf16[4,64,16,128]{3,2,1,0:T(8,128)(2,1)}, u32[]{:S(2)}) copy-start(bf16[4,64,16,128]{3,2,1,0:T(8,128)(2,1)} %copy-done) | copy-start | bytes 3145732
  312.7 24.5 %copy-start.3 = (bf16[4,64,16,128]{3,2,1,0:T(8,128)(2,1)S(1)}, bf16[4,64,16,128]{3,2,1,0:T(8,128)(2,1)}, u32[]{:S(2)}) copy-start(bf16[4,64,16,128]{3,2,1,0:T(8,128)(2,1)} %copy-done.2) | copy-start | bytes 3145732
Sparse Core Ops, SparseCore 0:
  312.8 22.6 all-gather.1

commit v3 on v2

--- a/solution.py
+++ b/solution.py
@@ -20,7 +20,12 @@
 
 
 def pack_kernel(slabs, capacity, per_slab, parts, dest_ref, owned_ref, *refs):
-    out_refs, meta_ref, count_ref = refs[:parts], refs[parts], refs[parts + 1]
+    out_refs, (buf_ref, ids_ref, count_ref) = refs[:-3], refs[-3:]
+    shares = owned_ref.shape[1]
+    span = capacity * shares
+    me = lax.axis_index("space")
+    lane = lax.broadcasted_iota(jnp.int32, (1, TILE), 1)
+    ids_ref[...] = jnp.full_like(ids_ref, -1)
     for slab in range(slabs):
         count_ref[slab] = 0
 
@@ -32,132 +37,209 @@
             slab = lax.div(block, per_slab)
             rank = count_ref[slab]
             count_ref[slab] = rank + 1
-            meta_ref[slab, rank] = block - slab * per_slab
-            at = slab * capacity + rank
+            here = pl.ds(slab, 1)
+            ids_ref[here, :] = jnp.where(lane == rank, block - slab * per_slab, ids_ref[here, :])
+            at = slab * span + rank * shares
             for part in range(parts):
-                out_refs[part][at] = owned_ref[i, :, part]
+                buf_ref[part, pl.ds(at, shares)] = owned_ref[i, :, part]
 
         return 0
 
     lax.fori_loop(0, dest_ref.shape[0], place, 0, unroll=4)
-    for slab in range(slabs):
-        meta_ref[slab, capacity] = count_ref[slab]
-
-
-def pack(dest, owned, slabs, per_slab):
+    for part in range(parts):
+        for m in range(slabs):
+            out_ref = out_refs[part * slabs + m]
+            slab = me ^ m
+            out_ref[:span] = buf_ref[part, pl.ds(slab * span, span)]
+            if out_ref.shape[0] > span:
+                ids = ids_ref[pl.ds(slab, 1), :].astype(jnp.float32)
+                out_ref[span] = jnp.broadcast_to(ids, out_ref.shape[1:]).astype(out_ref.dtype)
+
+
+def pack(dest, owned, slabs, per_slab, after=None):
     slots, shares, parts, rows, width = owned.shape
-    sent = jax.ShapeDtypeStruct((slots, shares, rows, width), owned.dtype)
+    capacity = slots // slabs
+    span = capacity * shares
+    first = 0 if after is None else 1
+    sent = []
+    for part in range(parts):
+        extra = 1 if after is None and part == 0 else 0
+        sent += [jax.ShapeDtypeStruct((span + extra, rows, width), owned.dtype)] * slabs
     outs = pl.pallas_call(
-        lambda *refs: pack_kernel(slabs, slots // slabs, per_slab, parts, *refs),
-        out_shape=(sent,) * parts + (jax.ShapeDtypeStruct((slabs, TILE), jnp.int32),),
-        in_specs=[SMEM, VMEM],
-        out_specs=(VMEM,) * parts + (SMEM,),
-        scratch_shapes=[pltpu.SMEM((slabs,), jnp.int32)],
+        lambda *refs: pack_kernel(slabs, capacity, per_slab, parts, *refs[first:]),
+        out_shape=tuple(sent),
+        in_specs=[SMEM] * first + [SMEM, VMEM],
+        out_specs=(VMEM,) * len(sent),
+        scratch_shapes=[
+            pltpu.VMEM((parts, slots * shares, rows, width), owned.dtype),
+            pltpu.VMEM((slabs, TILE), jnp.int32),
+            pltpu.SMEM((slabs,), jnp.int32),
+        ],
         compiler_params=pltpu.CompilerParams(vmem_limit_bytes=VMEM_BYTES),
         cost_estimate=pl.CostEstimate(
             flops=0, bytes_accessed=2 * owned.size * 2, transcendentals=0
         ),
         name="pack",
-    )(dest, owned)
-    return outs[:parts], outs[parts]
-
-
-def settle_kernel(slabs, capacity, meta_ref, moved_ref, out_ref):
-    for source in range(slabs):
+    )(*([] if after is None else [after]), dest, owned)
+    return [outs[part * slabs : (part + 1) * slabs] for part in range(parts)]
+
+
+def settle_kernel(slabs, capacity, first, *refs):
+    if first:
+        moved_refs, out_refs, (ids_ref, meta_ref) = refs[:slabs], refs[slabs:-2], refs[-2:]
+        meta_ref, ids_ref = ids_ref, meta_ref
+        span = moved_refs[0].shape[0] - 1
+        for m in range(slabs):
+            tile = moved_refs[m][span].astype(jnp.float32)
+            ids_ref[m : m + 1, :] = tile[:1].astype(jnp.int32)
+        pltpu.sync_copy(ids_ref, meta_ref)
+    else:
+        meta_ref, moved_refs, out_refs = refs[0], refs[1 : 1 + slabs], refs[1 + slabs :]
+    shares = len(out_refs)
+    mine = lax.axis_index("snap")
+    for m in range(slabs):
 
         def place(rank, _):
-            out_ref[:, meta_ref[source, rank]] = moved_ref[source * capacity + rank]
+            block = meta_ref[m, rank]
+
+            @pl.when(block >= 0)
+            def _():
+                for r in range(shares):
+                    out_refs[r][block] = moved_refs[m][rank * shares + (mine ^ r)]
+
             return 0
 
-        lax.fori_loop(0, meta_ref[source, capacity], place, 0)
-
-
-def settle(meta, moved, slabs, per_slab):
-    slots, shares, rows, width = moved.shape
-    return pl.pallas_call(
-        lambda *refs: settle_kernel(slabs, slots // slabs, *refs),
-        out_shape=jax.ShapeDtypeStruct((shares, per_slab, rows, width), moved.dtype),
-        in_specs=[SMEM, VMEM],
-        out_specs=VMEM,
-        compiler_params=pltpu.CompilerParams(vmem_limit_bytes=VMEM_BYTES),
-        cost_estimate=pl.CostEstimate(
-            flops=0, bytes_accessed=2 * moved.size, transcendentals=0
+        lax.fori_loop(0, capacity, place, 0, unroll=4)
+
+
+def settle(meta, moved, capacity, per_slab, shares):
+    first = meta is None
+    slabs = len(moved)
+    rows, width = moved[0].shape[1:]
+    pieces = (jax.ShapeDtypeStruct((per_slab, rows, width), moved[0].dtype),) * shares
+    ids = jax.ShapeDtypeStruct((slabs, TILE), jnp.int32)
+    outs = pl.pallas_call(
+        lambda *refs: settle_kernel(slabs, capacity, first, *refs),
+        out_shape=pieces + ((ids,) if first else ()),
+        in_specs=([] if first else [SMEM]) + [VMEM] * slabs,
+        out_specs=(VMEM,) * shares + ((SMEM,) if first else ()),
+        scratch_shapes=[pltpu.VMEM((slabs, TILE), jnp.int32)] if first else [],
+        compiler_params=pltpu.CompilerParams(vmem_limit_bytes=VMEM_BYTES),
+        cost_estimate=pl.CostEstimate(
+            flops=0, bytes_accessed=2 * slabs * moved[0].size, transcendentals=0
         ),
         name="settle",
-    )(meta, moved)
-
-
-def whole_rows(ref):
-    shares, blocks, rows, width = ref.shape
-    parts = [ref[s].reshape(blocks * rows, width) for s in range(shares)]
-    return jnp.concatenate(parts, axis=1)
-
-
-def gram_kernel(parts, *refs):
-    out_ref = refs[parts]
-    shares = refs[0].shape[0]
+    )(*([] if first else [meta]), *moved)
+    return outs[:shares], (outs[shares] if first else meta)
+
+
+def whole_rows(refs):
+    blocks, rows, width = refs[0].shape
+    return jnp.concatenate([ref[...].reshape(blocks * rows, width) for ref in refs], axis=1)
+
+
+def tile_of(row, lane, tiles):
+    return row * tiles - lax.div(row * (row - 1), 2) + lane - row
+
+
+def gram_kernel(parts, shares, *refs):
+    out_ref, acc_ref = refs[-2:]
     step = pl.program_id(0)
 
     @pl.when(step == 0)
     def _():
-        out_ref[...] = jnp.zeros_like(out_ref)
+        acc_ref[...] = jnp.zeros_like(acc_ref)
 
     for part in range(parts):
-        cells = whole_rows(refs[part])
-        at = 0
+        cells = whole_rows(refs[part * shares : (part + 1) * shares])
+        acc_ref[...] += lax.dot_general(
+            cells, cells, ROWS_BY_ROWS, preferred_element_type=jnp.float32
+        )
+
+    @pl.when(step == pl.num_programs(0) - 1)
+    def _():
+        mine = lax.axis_index("snap")
         for a in range(shares):
-            left = cells[:, a * TILE : (a + 1) * TILE]
-            product = lax.dot_general(
-                left, cells[:, a * TILE :], ROWS_BY_ROWS, preferred_element_type=jnp.float32
-            )
-            for b in range(a, shares):
-                out_ref[at] += product[:, (b - a) * TILE : (b - a + 1) * TILE]
-                at += 1
+            for b in range(shares):
+                row, lane = mine ^ a, mine ^ b
+
+                @pl.when(row <= lane)
+                def _():
+                    out_ref[tile_of(row, lane, shares)] = acc_ref[
+                        a * TILE : (a + 1) * TILE, b * TILE : (b + 1) * TILE
+                    ]
 
 
 def gram_blocks(cells, steps=4):
-    shares, blocks, rows, width = cells[0].shape
+    shares = len(cells[0])
+    blocks, rows, width = cells[0][0].shape
     pairs = shares * (shares + 1) // 2
-    spec = pl.BlockSpec((shares, blocks // steps, rows, width), lambda i: (0, i, 0, 0))
+    full = shares * width
+    spec = pl.BlockSpec((blocks // steps, rows, width), lambda i: (i, 0, 0))
     return pl.pallas_call(
-        lambda *refs: gram_kernel(len(cells), *refs),
+        lambda *refs: gram_kernel(len(cells), shares, *refs),
         grid=(steps,),
         out_shape=jax.ShapeDtypeStruct((pairs, TILE, TILE), jnp.float32),
-        in_specs=[spec] * len(cells),
+        in_specs=[spec] * (len(cells) * shares),
         out_specs=pl.BlockSpec((pairs, TILE, TILE), lambda i: (0, 0, 0)),
+        scratch_shapes=[pltpu.VMEM((full, full), jnp.float32)],
+        compiler_params=pltpu.CompilerParams(vmem_limit_bytes=VMEM_BYTES),
+        cost_estimate=pl.CostEstimate(
+            flops=2 * len(cells) * blocks * rows * full * full,
+            bytes_accessed=2 * len(cells) * blocks * rows * full,
+            transcendentals=0,
+        ),
         name="gram_blocks",
-    )(*cells)
-
-
-def cross_kernel(parts, *refs):
-    out_ref = refs[2 * parts]
+    )(*[piece for part in cells for piece in part])
+
+
+def cross_kernel(parts, shares, *refs):
+    out_ref, acc_ref = refs[-2:]
     step = pl.program_id(0)
 
     @pl.when(step == 0)
     def _():
-        out_ref[...] = jnp.zeros_like(out_ref)
+        acc_ref[...] = jnp.zeros_like(acc_ref)
 
     for part in range(parts):
-        out_ref[...] += lax.dot_general(
-            whole_rows(refs[part]),
-            whole_rows(refs[parts + part]),
-            ROWS_BY_ROWS,
-            preferred_element_type=jnp.float32,
+        x_refs = refs[part * shares : (part + 1) * shares]
+        y_refs = refs[(parts + part) * shares : (parts + part + 1) * shares]
+        acc_ref[...] += lax.dot_general(
+            whole_rows(x_refs), whole_rows(y_refs), ROWS_BY_ROWS, preferred_element_type=jnp.float32
         )
 
+    @pl.when(step == pl.num_programs(0) - 1)
+    def _():
+        mine = lax.axis_index("snap")
+        for a in range(shares):
+            rows = pl.ds(pl.multiple_of((mine ^ a) * TILE, TILE), TILE)
+            for b in range(shares):
+                lanes = pl.ds(pl.multiple_of((mine ^ b) * TILE, TILE), TILE)
+                out_ref[rows, lanes] = acc_ref[
+                    a * TILE : (a + 1) * TILE, b * TILE : (b + 1) * TILE
+                ]
+
 
 def cross_sum(x_cells, y_cells, steps=4):
-    shares, blocks, rows, width = x_cells[0].shape
-    spec = pl.BlockSpec((shares, blocks // steps, rows, width), lambda i: (0, i, 0, 0))
+    parts, shares = len(x_cells), len(x_cells[0])
+    blocks, rows, width = x_cells[0][0].shape
+    spec = pl.BlockSpec((blocks // steps, rows, width), lambda i: (i, 0, 0))
     full = shares * width
     return pl.pallas_call(
-        lambda *refs: cross_kernel(len(x_cells), *refs),
+        lambda *refs: cross_kernel(parts, shares, *refs),
         grid=(steps,),
         out_shape=jax.ShapeDtypeStruct((full, full), jnp.float32),
-        in_specs=[spec] * (2 * len(x_cells)),
+        in_specs=[spec] * (2 * parts * shares),
         out_specs=pl.BlockSpec((full, full), lambda i: (0, 0)),
+        scratch_shapes=[pltpu.VMEM((full, full), jnp.float32)],
+        compiler_params=pltpu.CompilerParams(vmem_limit_bytes=VMEM_BYTES),
+        cost_estimate=pl.CostEstimate(
+            flops=2 * parts * blocks * rows * full * full,
+            bytes_accessed=4 * parts * blocks * rows * full,
+            transcendentals=0,
+        ),
         name="cross_sum",
-    )(*x_cells, *y_cells)
+    )(*[piece for part in list(x_cells) + list(y_cells) for piece in part])
 
 
 def three_terms(value):
@@ -264,6 +346,7 @@
 
     lax.fori_loop(0, tiles, step, 0)
     zero = jnp.zeros((TILE, TILE), jnp.float32)
+    mine = lax.axis_index("snap")
     for a in range(tiles):
         rows = slice(a * TILE, (a + 1) * TILE)
         for b in range(tiles):
@@ -272,6 +355,7 @@
             value = wide[a, tiles + b] if b <= a else zero
             inv_ref[rows, lanes] = value
             high, middle, low = three_terms(value)
+            lanes = pl.ds(pl.multiple_of((mine ^ b) * TILE, TILE), TILE)
             hi_ref[rows, lanes] = high.astype(jnp.bfloat16)
             mid_ref[rows, lanes] = middle.astype(jnp.bfloat16)
             lo_ref[rows, lanes] = low.astype(jnp.bfloat16)
@@ -306,10 +390,10 @@
     )(blocks)
 
 
-def basis_kernel(parts, *refs):
-    hi_ref, mid_ref, lo_ref, out_ref = refs[parts:]
+def basis_kernel(parts, shares, *refs):
+    hi_ref, mid_ref, lo_ref, out_ref = refs[parts * shares :]
     for part in range(parts):
-        cells = whole_rows(refs[part])
+        cells = whole_rows(refs[part * shares : (part + 1) * shares])
         total = lax.dot_general(
             cells, lo_ref[...], LANES_BY_LANES, preferred_element_type=jnp.float32
         )
@@ -319,25 +403,34 @@
         total += lax.dot_general(
             cells, hi_ref[...], LANES_BY_LANES, preferred_element_type=jnp.float32
         )
-        blocks, rows = refs[part].shape[1:3]
-        out_ref[:, part] = total.reshape(blocks, rows, total.shape[-1])
+        blocks, _, rows, full = out_ref.shape
+        out_ref[:, part] = total.reshape(blocks, rows, full)
 
 
 def basis(cells, terms, steps=8):
-    shares, blocks, rows, width = cells[0].shape
+    parts, shares = len(cells), len(cells[0])
+    blocks, rows, width = cells[0][0].shape
     full = shares * width
-    parts = len(cells)
-    spec = pl.BlockSpec((shares, blocks // steps, rows, width), lambda i: (0, i, 0, 0))
+    spec = pl.BlockSpec((blocks // steps, rows, width), lambda i: (i, 0, 0))
     term = pl.BlockSpec((full, full), lambda i: (0, 0))
     return pl.pallas_call(
-        lambda *refs: basis_kernel(parts, *refs),
+        lambda *refs: basis_kernel(parts, shares, *refs),
         grid=(steps,),
         out_shape=jax.ShapeDtypeStruct((blocks, parts, rows, full), jnp.float32),
-        in_specs=[spec] * parts + [term] * 3,
+        in_specs=[spec] * (parts * shares) + [term] * 3,
         out_specs=pl.BlockSpec((blocks // steps, parts, rows, full), lambda i: (i, 0, 0, 0)),
         compiler_params=pltpu.CompilerParams(vmem_limit_bytes=VMEM_BYTES),
+        cost_estimate=pl.CostEstimate(
+            flops=6 * parts * blocks * rows * full * full,
+            bytes_accessed=6 * parts * blocks * rows * full,
+            transcendentals=0,
+        ),
         name="basis",
-    )(*cells, *terms)
+    )(*[piece for part in cells for piece in part], *terms)
+
+
+def swap(value, axis, mask):
+    return lax.ppermute(value, axis, [(i, i ^ mask) for i in range(lax.axis_size(axis))])
 
 
 def sum_over_devices(value, slabs, shares):
@@ -346,7 +439,7 @@
     piece = jnp.sum(pieces.reshape(slabs, -1, lanes), axis=0)
     hop = 1
     while hop < shares:
-        piece += lax.ppermute(piece, "snap", [(i, i ^ hop) for i in range(shares)])
+        piece += swap(piece, "snap", hop)
         hop *= 2
     return lax.all_gather(piece, "space", axis=0, tiled=True)
 
@@ -366,18 +459,15 @@
     def exchange(sent, meta):
         cells = []
         for part in sent:
-            moved = lax.all_to_all(part, "space", split_axis=0, concat_axis=0, tiled=True)
-            settled = settle(meta, moved, slabs, per_slab)
-            cells.append(lax.all_to_all(settled, "snap", split_axis=0, concat_axis=0, tiled=True))
-        return cells
-
-    sent_x, meta = pack(patch_dest, parted(owned_x), slabs, per_slab)
-    meta = lax.all_to_all(
-        meta.reshape(slabs, 1, TILE), "space", split_axis=0, concat_axis=0, tiled=True
-    ).reshape(slabs, TILE)
-    sent_y, _ = pack(patch_dest, parted(owned_y), slabs, per_slab)
-    x_cells = exchange(sent_x, meta)
-    y_cells = exchange(sent_y, meta)
+            moved = [part[0]] + [swap(part[m], "space", m) for m in range(1, slabs)]
+            pieces, meta = settle(meta, moved, slots // slabs, per_slab, shares)
+            cells.append([pieces[0]] + [swap(pieces[r], "snap", r) for r in range(1, shares)])
+        return cells, meta
+
+    sent_x = pack(patch_dest, parted(owned_x), slabs, per_slab)
+    x_cells, meta = exchange(sent_x, None)
+    sent_y = pack(patch_dest, parted(owned_y), slabs, per_slab, meta)
+    y_cells, _ = exchange(sent_y, meta)
 
     tiles = full // TILE
     pairs = tiles * (tiles + 1) // 2

time: 359 us -> 288 us (0.80)
  blocking collectives: 78.9 us -> 9.05 us
  starting transfers between devices: 36.1 us -> 87 us
  waiting for transfers between devices: 151 us -> 107 us
  local copies, waits for them, and re-layouts: 15.9 us -> 4.84 us
    all_to_all x6 -> x0, waiting for transfers between devices: 125 us -> none  [the longest x4 84.3 us: exchange(): lax.all_to_all(settled, 'snap', split_axis=0, concat_axis=0, tiled=True)]
    ppermute x4 -> x44, waiting for transfers between devices: 4.34 us -> 99.3 us  [swap(): lax.ppermute(value, axis, [(i, i ^ mask) for i in range(lax.axis_size(axi...]
    ppermute x4 -> x44, starting transfers between devices: 4.23 us -> 78.9 us  [swap(): lax.ppermute(value, axis, [(i, i ^ mask) for i in range(lax.axis_size(axi...]
    all_to_all x3 -> x0, blocking collectives: 69.8 us -> none  [the longest x2 60.7 us: exchange(): lax.all_to_all(part, 'space', split_axis=0, concat_axis=0, tiled=True)]
    all_to_all x6 -> x0, starting transfers between devices: 22.9 us -> none  [the longest x4 15.6 us: exchange(): lax.all_to_all(settled, 'snap', split_axis=0, concat_axis=0, tiled=True)]
    all_to_all x2, waiting for transfers between devices: 21.3 us -> 8.07 us  [sum_over_devices(): lax.all_to_all(value, 'space', split_axis=0, concat_axis=0, tiled=True)]
    unnamed x42 -> x20, local copies, waits for them, and re-layouts: 15.9 us -> 4.84 us
  transfers between devices with their start and end apart: 13 -> 47, of which waited for: 10 -> 16; matrix products, arithmetic and copies ran while one was open for 0% -> 0% of each run, Pallas kernels for 15% -> 19%
where the time goes in v3:
time: 288 us
  waiting for transfers between devices  107 us (37%)
  starting transfers between devices  87 us (30%)
  Pallas kernels  59.2 us (21%)
  between operations  14.2 us (5%)
  blocking collectives  9.05 us (3%)
  local copies, waits for them, and re-layouts  4.84 us (2%)
  matrix products  4.04 us (1%)
    ppermute x44, waiting for transfers between devices, swap(): lax.ppermute(value, axis, [(i, i ^ mask) for i in range(lax.axis_size(axi...  99.3 us
    ppermute x44, starting transfers between devices, swap(): lax.ppermute(value, axis, [(i, i ^ mask) for i in range(lax.axis_size(axi...  78.9 us
    pallas_call x1, Pallas kernels, factor(): pl.pallas_call(lambda *refs: factor_kernel(tiles, rows_total, *refs), out...  24.7 us
    pallas_call x4, Pallas kernels, settle(): pl.pallas_call(lambda *refs: settle_kernel(slabs, capacity, first, *refs)...  11.3 us
    pallas_call x1, Pallas kernels, basis(): pl.pallas_call(lambda *refs: basis_kernel(parts, shares, *refs), grid=(st...  9.89 us
    all_gather x1, blocking collectives, sum_over_devices(): return lax.all_gather(piece, 'space', axis=0, tiled=True)  9.05 us
    all_to_all x2, starting transfers between devices, sum_over_devices(): lax.all_to_all(value, 'space', split_axis=0, concat_axis=0, tiled=True)  8.09 us
    all_to_all x2, waiting for transfers between devices, sum_over_devices(): lax.all_to_all(value, 'space', split_axis=0, concat_axis=0, tiled=True)  8.07 us
  transfers between devices with their start and end apart: 47, of which 16 were waited for; matrix products, arithmetic and copies ran while one was open for 0% of the time, Pallas kernels for 19%

profile of v3, /device:TPU:0, one launch (start us, length us, event | category | flops | bytes accessed | tf_op | source)
XLA Modules:
  0.0 287.6 jit_solution(1393342918435050348)
XLA Ops:
  7.2 2.3 copy-done.1
  9.5 0.8 copy-done.6
  10.3 3.1 %pack.2 = (bf16[65,16,128]{2,1,0:T(8,128)(2,1)S(1)}, bf16[65,16,128]{2,1,0:T(8,128)(2,1)S(1)}, bf16[65,16,128]{2,1,0:T(8,128)(2,1)S(1)}, bf16[65,16,128]{2,1,0:T...) custom-call(s32[128]{0:T(128)S(1)} %copy-done.6, ...), custom_call_target="tpu_custom_call" | custom-call | bytes 8388608 | tf_op jit(solution)/shard_map/pack/pallas_call | solution.py:68
  13.9 2.6 collective-permute-start.1
  16.6 1.1 collective-permute-start.3
  18.1 2.5 collective-permute-start.5
  20.6 3.2 %collective-permute-done.1.refs_2_ = bf16[65,16,128]{2,1,0:T(8,128)(2,1)S(1)} collective-permute-done((bf16[65,16,128]{2,1,0:T(8,128)(2,1)S(1)}, bf16[65,16,128]{2,1,0:T(8,128)(2,1)S(1)}, u32[]{:S(2)}, u32[]{:S(2)}) %collective-permute-start.1) | collective-permute-done | bytes 266272 | tf_op jit(solution)/shard_map/ppermute | solution.py:433
  24.3 4.6 %collective-permute-done.2.refs_3_ = bf16[65,16,128]{2,1,0:T(8,128)(2,1)S(1)} collective-permute-done((bf16[65,16,128]{2,1,0:T(8,128)(2,1)S(1)}, bf16[65,16,128]{2,1,0:T(8,128)(2,1)S(1)}, u32[]{:S(2)}, u32[]{:S(2)}) %collective-permute-start.2) | collective-permute-done | bytes 266272 | tf_op jit(solution)/shard_map/ppermute | solution.py:433
  29.6 1.9 collective-permute-start.11
  31.5 9.7 %collective-permute-done.4.refs_5_ = bf16[65,16,128]{2,1,0:T(8,128)(2,1)S(1)} collective-permute-done((bf16[65,16,128]{2,1,0:T(8,128)(2,1)S(1)}, bf16[65,16,128]{2,1,0:T(8,128)(2,1)S(1)}, u32[]{:S(2)}, u32[]{:S(2)}) %collective-permute-start.4) | collective-permute-done | bytes 266272 | tf_op jit(solution)/shard_map/ppermute | solution.py:433
  41.2 2.6 collective-permute-start.12
  43.8 1.1 collective-permute-start.13
  45.0 3.0 %settle.4 = (bf16[64,16,128]{2,1,0:T(8,128)(2,1)S(1)}, bf16[64,16,128]{2,1,0:T(8,128)(2,1)S(1)}, bf16[64,16,128]{2,1,0:T(8,128)(2,1)S(1)}, bf16[64,16,128]{2,1,0:T(8,128)(2,1)S(1)}, s32[8,128]{1,0:T(8,128)S(1)}) custom-call(bf16[65,16,128]{2,1,0:T(8,128)(2,1)S(1)} %get-tuple-element.57.refs_0_, bf16[65,16,128]{2,1,0:T(8,128)(2,1)S(1)} %collective-permute-done.refs_1_, ...), custom_call_target="tpu_custom_call" | custom-call | bytes 2129920 | tf_op jit(solution)/shard_map/settle/pallas_call | solution.py:121
  48.0 4.1 %pack.3 = (bf16[64,16,128]{2,1,0:T(8,128)(2,1)S(1)}, bf16[64,16,128]{2,1,0:T(8,128)(2,1)S(1)}, bf16[64,16,128]{2,1,0:T(8,128)(2,1)S(1)}, bf16[64,16,128]{2,1,0:T...) custom-call(s32[8,128]{1,0:T(8,128)S(1)} %get-tuple-element.69.refs_, ...), custom_call_target="tpu_custom_call" | custom-call | bytes 8388608 | tf_op jit(solution)/shard_map/pack/pallas_call | solution.py:68
  52.5 2.8 collective-permute-start.16
  55.7 12.0 %collective-permute-done.14.refs_6_ = bf16[64,16,128]{2,1,0:T(8,128)(2,1)S(1)} collective-permute-done((bf16[64,16,128]{2,1,0:T(8,128)(2,1)S(1)}, bf16[64,16,128]{2,1,0:T(8,128)(2,1)S(1)}, u32[]{:S(2)}, u32[]{:S(2)}) %collective-permute-start.14) | collective-permute-done | bytes 262176 | tf_op jit(solution)/shard_map/ppermute | solution.py:433
  67.7 1.3 collective-permute-start.34
  69.0 1.1 collective-permute-start.35
  70.2 2.1 collective-permute-start.37
  72.3 2.3 settle.5
  74.7 1.2 collective-permute-start.38
  75.8 1.8 collective-permute-done.34.refs_4_
  77.6 0.7 collective-permute-start.22
  78.3 12.6 %collective-permute-start.23 = (bf16[64,16,128]{2,1,0:T(8,128)(2,1)S(1)}, bf16[64,16,128]{2,1,0:T(8,128)(2,1)S(1)}, u32[]{:S(2)}, u32[]{:S(2)}) collective-permute-start(bf16[64,16,128]{2,1,0:T(8,128)(2,1)S(1)} %get-tuple-element.89), channel_id=1, source_target_pairs={{0,8},{4,12},{8,0},{12,4},{16,24},{20,28},{24,16},{28,20},{1,9},{5... | collective-permute-start | bytes 786440 | tf_op jit(solution)/shard_map/ppermute | solution.py:433
  90.9 2.0 collective-permute-done.36.refs_6_
  92.9 1.7 collective-permute-start.24
  94.6 1.6 collective-permute-start.17
  96.2 2.6 collective-permute-start.18
  99.0 0.7 collective-permute-start.7
  99.7 0.7 collective-permute-done.24.refs_4_
  100.4 0.7 copy-done.4
  101.1 2.8 collective-permute-start.8
  103.9 4.7 %collective-permute-done.17.refs_5_ = bf16[64,16,128]{2,1,0:T(8,128)(2,1)S(1)} collective-permute-done((bf16[64,16,128]{2,1,0:T(8,128)(2,1)S(1)}, bf16[64,16,128]{2,1,0:T(8,128)(2,1)S(1)}, u32[]{:S(2)}, u32[]{:S(2)}) %collective-permute-start.17) | collective-permute-done | bytes 262176 | tf_op jit(solution)/shard_map/ppermute | solution.py:433
  108.5 4.1 %collective-permute-start.9 = (bf16[64,16,128]{2,1,0:T(8,128)(2,1)S(1)}, bf16[64,16,128]{2,1,0:T(8,128)(2,1)S(1)}, u32[]{:S(2)}, u32[]{:S(2)}) collective-permute-start(bf16[64,16,128]{2,1,0:T(8,128)(2,1)S(1)} %get-tuple-element.68), channel_id=1, source_target_pairs={{0,3},{1,2},{2,1},{3,0},{4,7},{5,6},{6,5},{7,4},{8,11},{9,10},{10,... | collective-permute-start | bytes 786440 | tf_op jit(solution)/shard_map/ppermute | solution.py:433
  112.7 3.1 %settle.7 = (bf16[64,16,128]{2,1,0:T(8,128)(2,1)S(1)}, bf16[64,16,128]{2,1,0:T(8,128)(2,1)}, bf16[64,16,128]{2,1,0:T(8,128)(2,1)S(1)}, bf16[64,16,128]{2,1,0:T(8,128)(2,1)S(1)}) custom-call(s32[8,128]{1,0:T(8,128)S(1)} %get-tuple-element.69.refs_0_, bf16[64,16,128]{2,1,0:T(8,128)(2,1)S(1)} %get-tuple-element.99.refs_1_, ...), custom_call_target="tpu_custom_call" | custom-call | bytes 2097152 | tf_op jit(solution)/shard_map/settle/pallas_call | solution.py:121
  115.7 1.9 collective-permute-done.18.refs_6_
  117.6 1.7 collective-permute-start.25
  119.9 1.9 collective-permute-start.27
  121.8 18.3 %collective-permute-done.8.refs_2_ = bf16[64,16,128]{2,1,0:T(8,128)(2,1)S(1)} collective-permute-done((bf16[64,16,128]{2,1,0:T(8,128)(2,1)S(1)}, bf16[64,16,128]{2,1,0:T(8,128)(2,1)S(1)}, u32[]{:S(2)}, u32[]{:S(2)}) %collective-permute-start.8) | collective-permute-done | bytes 262176 | tf_op jit(solution)/shard_map/ppermute | solution.py:433
  140.1 4.5 %collective-permute-start.39 = (bf16[64,16,128]{2,1,0:T(8,128)(2,1)}, bf16[64,16,128]{2,1,0:T(8,128)(2,1)S(1)}, u32[]{:S(2)}, u32[]{:S(2)}) collective-permute-start(bf16[64,16,128]{2,1,0:T(8,128)(2,1)} %get-tuple-element.108), channel_id=1, source_target_pairs={{0,1},{1,0},{2,3},{3,2},{4,5},{5,4},{6,7},{7,6},{8,9},{9,8},{10,11... | collective-permute-start | bytes 786440 | tf_op jit(solution)/shard_map/ppermute | solution.py:433
  144.7 2.9 %gram_blocks.1 = f32[10,128,128]{2,1,0:T(8,128)} custom-call(bf16[64,16,128]{2,1,0:T(8,128)(2,1)S(1)} %get-tuple-element.65.refs_0_, bf16[64,16,128]{2,1,0:T(8,128)(2,1)S(1)} %collective-permute-done.7.refs_1_, bf16[64,16,128]{2,1,0:T(8,128)(2,1)S(1)} %collective-permute-done.8.refs_2_, bf16[64,16,128]{2,1,0:T(8,128)(2,1)S(1)} %collective-permute-done.9.refs_3_, ...), custom_call_target="tpu_custom_call" | custom-call | flops 1073741824 | bytes 2097152 | tf_op jit(solution)/shard_map/gram_blocks/pallas_call | solution.py:179
  147.6 4.2 %all-to-all-start = ((f32[8,160,128]{2,1,0:T(8,128)}), f32[8,160,128]{2,1,0:T(8,128)}, u32[]{:S(2)}, u32[]{:S(2)}) async-start(f32[8,160,128]{2,1,0:T(8,128)} %bitcast.1), calls=%async_computation | async-start | bytes 1310720 | tf_op jit(solution)/shard_map/all_to_all | solution.py:438
  151.8 1.1 collective-permute-start.40
  152.9 1.5 collective-permute-start.41
  154.5 0.9 copy-done.5
  155.4 2.9 %settle.6 = (bf16[64,16,128]{2,1,0:T(8,128)(2,1)S(1)}, bf16[64,16,128]{2,1,0:T(8,128)(2,1)S(1)}, bf16[64,16,128]{2,1,0:T(8,128)(2,1)S(1)}, bf16[64,16,128]{2,1,0:T(8,128)(2,1)S(1)}) custom-call(s32[8,128]{1,0:T(8,128)S(1)} %get-tuple-element.69.refs_0_, bf16[64,16,128]{2,1,0:T(8,128)(2,1)S(1)} %get-tuple-element.87.refs_1_, ...), custom_call_target="tpu_custom_call" | custom-call | bytes 2097152 | tf_op jit(solution)/shard_map/settle/pallas_call | solution.py:121
  158.4 2.2 collective-permute-start.29
  160.5 0.8 collective-permute-start.30
  161.3 1.7 collective-permute-start.31
  163.0 10.0 %collective-permute-done.40.refs_14_ = bf16[64,16,128]{2,1,0:T(8,128)(2,1)S(1)} collective-permute-done((bf16[64,16,128]{2,1,0:T(8,128)(2,1)}, bf16[64,16,128]{2,1,0:T(8,128)(2,1)S(1)}, u32[]{:S(2)}, u32[]{:S(2)}) %collective-permute-start.40) | collective-permute-done | bytes 262176 | tf_op jit(solution)/shard_map/ppermute | solution.py:433
  173.0 5.0 %collective-permute-done.29.refs_9_ = bf16[64,16,128]{2,1,0:T(8,128)(2,1)S(1)} collective-permute-done((bf16[64,16,128]{2,1,0:T(8,128)(2,1)S(1)}, bf16[64,16,128]{2,1,0:T(8,128)(2,1)S(1)}, u32[]{:S(2)}, u32[]{:S(2)}) %collective-permute-start.29) | collective-permute-done | bytes 262176 | tf_op jit(solution)/shard_map/ppermute | solution.py:433
  178.1 17.1 %collective-permute-done.30.refs_10_ = bf16[64,16,128]{2,1,0:T(8,128)(2,1)S(1)} collective-permute-done((bf16[64,16,128]{2,1,0:T(8,128)(2,1)S(1)}, bf16[64,16,128]{2,1,0:T(8,128)(2,1)S(1)}, u32[]{:S(2)}, u32[]{:S(2)}) %collective-permute-start.30) | collective-permute-done | bytes 262176 | tf_op jit(solution)/shard_map/ppermute | solution.py:433
  195.2 3.1 %cross_sum.1 = f32[512,512]{1,0:T(8,128)} custom-call(bf16[64,16,128]{2,1,0:T(8,128)(2,1)S(1)} %get-tuple-element.65.refs_0_, bf16[64,16,128]{2,1,0:T(8,128)(2,1)S(1)} %collective-permute-done.7.refs_1_, bf16[64,16,128]{2,1,0:T(8,128)(2,1)S(1)} %collective-permute-done.8.refs_2_, bf16[64,16,128]{2,1,0:T(8,128)(2,1)S(1)} %collective-permute-done.9.refs_3_, ...), custom_call_target="tpu_custom_call" | custom-call | flops 1073741824 | bytes 4194304 | tf_op jit(solution)/shard_map/cross_sum/pallas_call | solution.py:228
  198.3 3.9 %all-to-all-start.1 = ((f32[8,64,512]{2,1,0:T(8,128)}), f32[8,64,512]{2,1,0:T(8,128)S(1)}, u32[]{:S(2)}, u32[]{:S(2)}) async-start(f32[8,64,512]{2,1,0:T(8,128)} %bitcast.5), calls=%async_computation.1 | async-start | bytes 2097152 | tf_op jit(solution)/shard_map/all_to_all | solution.py:438
  202.2 1.1 reduce_sum.18
  203.4 6.2 %collective-permute-start.20 = (f32[160,128]{1,0:T(8,128)S(1)}, f32[160,128]{1,0:T(8,128)S(1)}, u32[]{:S(2)}, u32[]{:S(2)}) collective-permute-start(f32[160,128]{1,0:T(8,128)S(1)} %reduce_sum.18), channel_id=1, source_target_pairs={{0,1},{1,0},{2,3},{3,2},{4,5},{5,4},{6,7},{7,6},{8,9},{9,8},{10,11... | collective-permute-start | bytes 245768 | tf_op jit(solution)/shard_map/ppermute | solution.py:433
  209.5 8.1 %all-to-all-done.1 = f32[8,64,512]{2,1,0:T(8,128)S(1)} async-done(((f32[8,64,512]{2,1,0:T(8,128)}), f32[8,64,512]{2,1,0:T(8,128)S(1)}, u32[]{:S(2)}, u32[]{:S(2)}) %all-to-all-start.1) | async-done | bytes 1048608 | tf_op jit(solution)/shard_map/all_to_all | solution.py:438
  217.7 6.2 %collective-permute-start.42 = (f32[64,512]{1,0:T(8,128)S(1)}, f32[64,512]{1,0:T(8,128)S(1)}, u32[]{:S(2)}, u32[]{:S(2)}) collective-permute-start(f32[64,512]{1,0:T(8,128)S(1)} %reduce_sum.19), channel_id=1, source_target_pairs={{0,1},{1,0},{2,3},{3,2},{4,5},{5,4},{6,7},{7,6},{8,9},{9,8},{10,11... | collective-permute-start | bytes 393224 | tf_op jit(solution)/shard_map/ppermute | solution.py:433
  223.9 0.7 collective-permute-start.21
  224.6 7.7 %collective-permute-done.21 = f32[160,128]{1,0:T(8,128)S(1)} collective-permute-done((f32[160,128]{1,0:T(8,128)S(1)}, f32[160,128]{1,0:T(8,128)S(1)}, u32[]{:S(2)}, u32[]{:S(2)}) %collective-permute-start.21) | collective-permute-done | bytes 81952 | tf_op jit(solution)/shard_map/ppermute | solution.py:433
  232.4 9.1 %all_gather.6 = f32[1280,128]{1,0:T(8,128)S(1)} all-gather(f32[160,128]{1,0:T(8,128)S(1)} %add.13), channel_id=1, replica_groups=mesh['space'=8,'snap'=4] {'space'}, dimensions={0}, use_global_device_ids=true | all-gather | bytes 737280 | tf_op jit(solution)/shard_map/all_gather | solution.py:444
  242.2 24.7 %factor.1 = (f32[512,512]{1,0:T(8,128)}, f32[512,512]{1,0:T(8,128)S(1)}, bf16[512,512]{1,0:T(8,128)(2,1)S(1)}, bf16[512,512]{1,0:T(8,128)(2,1)S(1)}, bf16[512,512]{1,0:T(8,128)(2,1)S(1)}) custom-call(f32[10,128,128]{2,1,0:T(8,128)S(1)} %bitcast.10), custom_call_target="tpu_custom_call" | custom-call | flops 40000000000 | bytes 2097152 | tf_op jit(solution)/shard_map/factor/pallas_call | solution.py:367
  266.9 9.9 %basis.1 = f32[64,2,16,512]{3,2,1,0:T(8,128)} custom-call(bf16[64,16,128]{2,1,0:T(8,128)(2,1)S(1)} %get-tuple-element.65.refs_0_, bf16[64,16,128]{2,1,0:T(8,128)(2,1)S(1)} %collective-permute-done.7.refs_1_, bf16[64,16,128]{2,1,0:T(8,128)(2,1)S(1)} %collective-permute-done.8.refs_2_, bf16[64,16,128]{2,1,0:T(8,128)(2,1)S(1)} %copy-done.3, ...), custom_call_target="tpu_custom_call" | custom-call | flops 3221225472 | bytes 6291456 | tf_op jit(solution)/shard_map/basis/pallas_call | solution.py:416
  276.8 4.0 %convolution_multiply_fusion = f32[512,512]{1,0:T(8,128)} fusion(f32[512,512]{1,0:T(8,128)S(1)} %get-tuple-element.86, f32[512,512]{1,0:T(8,128)} %all-gather.2.cloned.1.call-done), kind=kOutput, calls=%fused_computation | convolution fusion | flops 1610874880 | bytes 3145728 | tf_op jit(solution)/shard_map/dot_general | solution.py:480
  (69 shorter events, 4.8 us)
Async XLA Ops:
  7.2 40.8 %copy-start = (bf16[128,128,128]{2,1,0:T(8,128)(2,1)S(1)}, bf16[128,128,128]{2,1,0:T(8,128)(2,1)}, u32[]{:S(2)}) copy-start(bf16[128,128,128]{2,1,0:T(8,128)(2,1)} %param.4) | copy-start | bytes 12582916
  7.2 2.3 copy-start.1
  9.5 0.8 copy-start.6
  10.3 37.7 %copy-start.7 = (s32[128]{0:T(128)S(1)}, s32[128]{0:T(128)}, u32[]{:S(2)}) copy-start(s32[128]{0:T(128)} %refs_1_.1) | copy-start | bytes 1540
  13.5 4.6 %collective-permute-start = (bf16[65,16,128]{2,1,0:T(8,128)(2,1)S(1)}, bf16[65,16,128]{2,1,0:T(8,128)(2,1)S(1)}, u32[]{:S(2)}, u32[]{:S(2)}) collective-permute-start(bf16[65,16,128]{2,1,0:T(8,128)(2,1)S(1)} %get-tuple-element.58), channel_id=1, source_target_pairs={{0,4},{4,0},{8,12},{12,8},{16,20},{20,16},{24,28},{28,24},{1,5},{5... | collective-permute-start | bytes 798728 | tf_op jit(solution)/shard_map/ppermute | solution.py:433
  13.9 9.8 %collective-permute-start.1 = (bf16[65,16,128]{2,1,0:T(8,128)(2,1)S(1)}, bf16[65,16,128]{2,1,0:T(8,128)(2,1)S(1)}, u32[]{:S(2)}, u32[]{:S(2)}) collective-permute-start(bf16[65,16,128]{2,1,0:T(8,128)(2,1)S(1)} %get-tuple-element.59), channel_id=1, source_target_pairs={{0,8},{4,12},{8,0},{12,4},{16,24},{20,28},{24,16},{28,20},{1,9},{5... | collective-permute-start | bytes 798728 | tf_op jit(solution)/shard_map/ppermute | solution.py:433
  16.5 12.4 %collective-permute-start.2 = (bf16[65,16,128]{2,1,0:T(8,128)(2,1)S(1)}, bf16[65,16,128]{2,1,0:T(8,128)(2,1)S(1)}, u32[]{:S(2)}, u32[]{:S(2)}) collective-permute-start(bf16[65,16,128]{2,1,0:T(8,128)(2,1)S(1)} %get-tuple-element.60), channel_id=1, source_target_pairs={{0,12},{4,8},{8,4},{12,0},{16,28},{20,24},{24,20},{28,16},{1,13},{... | collective-permute-start | bytes 798728 | tf_op jit(solution)/shard_map/ppermute | solution.py:433
  16.6 13.0 %collective-permute-start.3 = (bf16[65,16,128]{2,1,0:T(8,128)(2,1)S(1)}, bf16[65,16,128]{2,1,0:T(8,128)(2,1)S(1)}, u32[]{:S(2)}, u32[]{:S(2)}) collective-permute-start(bf16[65,16,128]{2,1,0:T(8,128)(2,1)S(1)} %get-tuple-element.61), channel_id=1, source_target_pairs={{0,16},{4,20},{8,24},{12,28},{16,0},{20,4},{24,8},{28,12},{1,17},{... | collective-permute-start | bytes 798728 | tf_op jit(solution)/shard_map/ppermute | solution.py:433
  17.7 23.5 %collective-permute-start.4 = (bf16[65,16,128]{2,1,0:T(8,128)(2,1)S(1)}, bf16[65,16,128]{2,1,0:T(8,128)(2,1)S(1)}, u32[]{:S(2)}, u32[]{:S(2)}) collective-permute-start(bf16[65,16,128]{2,1,0:T(8,128)(2,1)S(1)} %get-tuple-element.62), channel_id=1, source_target_pairs={{0,20},{4,16},{8,28},{12,24},{16,4},{20,0},{24,12},{28,8},{1,21},{... | collective-permute-start | bytes 798728 | tf_op jit(solution)/shard_map/ppermute | solution.py:433
  18.1 25.7 %collective-permute-start.5 = (bf16[65,16,128]{2,1,0:T(8,128)(2,1)S(1)}, bf16[65,16,128]{2,1,0:T(8,128)(2,1)S(1)}, u32[]{:S(2)}, u32[]{:S(2)}) collective-permute-start(bf16[65,16,128]{2,1,0:T(8,128)(2,1)S(1)} %get-tuple-element.63), channel_id=1, source_target_pairs={{0,24},{4,28},{8,16},{12,20},{16,8},{20,12},{24,0},{28,4},{1,25},{... | collective-permute-start | bytes 798728 | tf_op jit(solution)/shard_map/ppermute | solution.py:433
  23.8 21.2 %collective-permute-start.6 = (bf16[65,16,128]{2,1,0:T(8,128)(2,1)S(1)}, bf16[65,16,128]{2,1,0:T(8,128)(2,1)S(1)}, u32[]{:S(2)}, u32[]{:S(2)}) collective-permute-start(bf16[65,16,128]{2,1,0:T(8,128)(2,1)S(1)} %get-tuple-element.64), channel_id=1, source_target_pairs={{0,28},{4,24},{8,20},{12,16},{16,12},{20,8},{24,4},{28,0},{1,29},{... | collective-permute-start | bytes 798728 | tf_op jit(solution)/shard_map/ppermute | solution.py:433
  28.9 23.2 %collective-permute-start.10 = (bf16[64,16,128]{2,1,0:T(8,128)(2,1)S(1)}, bf16[64,16,128]{2,1,0:T(8,128)(2,1)S(1)}, u32[]{:S(2)}, u32[]{:S(2)}) collective-permute-start(bf16[64,16,128]{2,1,0:T(8,128)(2,1)S(1)} %get-tuple-element.71), channel_id=1, source_target_pairs={{0,4},{4,0},{8,12},{12,8},{16,20},{20,16},{24,28},{28,24},{1,5},{5... | collective-permute-start | bytes 786440 | tf_op jit(solution)/shard_map/ppermute | solution.py:433
  29.6 22.9 %collective-permute-start.11 = (bf16[64,16,128]{2,1,0:T(8,128)(2,1)S(1)}, bf16[64,16,128]{2,1,0:T(8,128)(2,1)S(1)}, u32[]{:S(2)}, u32[]{:S(2)}) collective-permute-start(bf16[64,16,128]{2,1,0:T(8,128)(2,1)S(1)} %get-tuple-element.72), channel_id=1, source_target_pairs={{0,8},{4,12},{8,0},{12,4},{16,24},{20,28},{24,16},{28,20},{1,9},{5... | collective-permute-start | bytes 786440 | tf_op jit(solution)/shard_map/ppermute | solution.py:433
  41.2 14.0 %collective-permute-start.12 = (bf16[64,16,128]{2,1,0:T(8,128)(2,1)S(1)}, bf16[64,16,128]{2,1,0:T(8,128)(2,1)S(1)}, u32[]{:S(2)}, u32[]{:S(2)}) collective-permute-start(bf16[64,16,128]{2,1,0:T(8,128)(2,1)S(1)} %get-tuple-element.73), channel_id=1, source_target_pairs={{0,12},{4,8},{8,4},{12,0},{16,28},{20,24},{24,20},{28,16},{1,13},{... | collective-permute-start | bytes 786440 | tf_op jit(solution)/shard_map/ppermute | solution.py:433
  43.8 11.4 %collective-permute-start.13 = (bf16[64,16,128]{2,1,0:T(8,128)(2,1)S(1)}, bf16[64,16,128]{2,1,0:T(8,128)(2,1)S(1)}, u32[]{:S(2)}, u32[]{:S(2)}) collective-permute-start(bf16[64,16,128]{2,1,0:T(8,128)(2,1)S(1)} %get-tuple-element.74), channel_id=1, source_target_pairs={{0,16},{4,20},{8,24},{12,28},{16,0},{20,4},{24,8},{28,12},{1,17},{... | collective-permute-start | bytes 786440 | tf_op jit(solution)/shard_map/ppermute | solution.py:433
  44.9 22.7 %collective-permute-start.14 = (bf16[64,16,128]{2,1,0:T(8,128)(2,1)S(1)}, bf16[64,16,128]{2,1,0:T(8,128)(2,1)S(1)}, u32[]{:S(2)}, u32[]{:S(2)}) collective-permute-start(bf16[64,16,128]{2,1,0:T(8,128)(2,1)S(1)} %get-tuple-element.75), channel_id=1, source_target_pairs={{0,20},{4,16},{8,28},{12,24},{16,4},{20,0},{24,12},{28,8},{1,21},{... | collective-permute-start | bytes 786440 | tf_op jit(solution)/shard_map/ppermute | solution.py:433
  52.1 16.9 %collective-permute-start.15 = (bf16[64,16,128]{2,1,0:T(8,128)(2,1)S(1)}, bf16[64,16,128]{2,1,0:T(8,128)(2,1)S(1)}, u32[]{:S(2)}, u32[]{:S(2)}) collective-permute-start(bf16[64,16,128]{2,1,0:T(8,128)(2,1)S(1)} %get-tuple-element.76), channel_id=1, source_target_pairs={{0,24},{4,28},{8,16},{12,20},{16,8},{20,12},{24,0},{28,4},{1,25},{... | collective-permute-start | bytes 786440 | tf_op jit(solution)/shard_map/ppermute | solution.py:433
  52.5 17.6 %collective-permute-start.16 = (bf16[64,16,128]{2,1,0:T(8,128)(2,1)S(1)}, bf16[64,16,128]{2,1,0:T(8,128)(2,1)S(1)}, u32[]{:S(2)}, u32[]{:S(2)}) collective-permute-start(bf16[64,16,128]{2,1,0:T(8,128)(2,1)S(1)} %get-tuple-element.77), channel_id=1, source_target_pairs={{0,28},{4,24},{8,20},{12,16},{16,12},{20,8},{24,4},{28,0},{1,29},{... | collective-permute-start | bytes 786440 | tf_op jit(solution)/shard_map/ppermute | solution.py:433
  55.2 14.9 %collective-permute-start.32 = (bf16[64,16,128]{2,1,0:T(8,128)(2,1)S(1)}, bf16[64,16,128]{2,1,0:T(8,128)(2,1)S(1)}, u32[]{:S(2)}, u32[]{:S(2)}) collective-permute-start(bf16[64,16,128]{2,1,0:T(8,128)(2,1)S(1)} %get-tuple-element.100), channel_id=1, source_target_pairs={{0,4},{4,0},{8,12},{12,8},{16,20},{20,16},{24,28},{28,24},{1,5},{5... | collective-permute-start | bytes 786440 | tf_op jit(solution)/shard_map/ppermute | solution.py:433
  55.2 19.4 %collective-permute-start.33 = (bf16[64,16,128]{2,1,0:T(8,128)(2,1)S(1)}, bf16[64,16,128]{2,1,0:T(8,128)(2,1)S(1)}, u32[]{:S(2)}, u32[]{:S(2)}) collective-permute-start(bf16[64,16,128]{2,1,0:T(8,128)(2,1)S(1)} %get-tuple-element.101), channel_id=1, source_target_pairs={{0,8},{4,12},{8,0},{12,4},{16,24},{20,28},{24,16},{28,20},{1,9},{5... | collective-permute-start | bytes 786440 | tf_op jit(solution)/shard_map/ppermute | solution.py:433
  67.7 9.9 %collective-permute-start.34 = (bf16[64,16,128]{2,1,0:T(8,128)(2,1)S(1)}, bf16[64,16,128]{2,1,0:T(8,128)(2,1)S(1)}, u32[]{:S(2)}, u32[]{:S(2)}) collective-permute-start(bf16[64,16,128]{2,1,0:T(8,128)(2,1)S(1)} %get-tuple-element.102), channel_id=1, source_target_pairs={{0,12},{4,8},{8,4},{12,0},{16,28},{20,24},{24,20},{28,16},{1,13},{... | collective-permute-start | bytes 786440 | tf_op jit(solution)/shard_map/ppermute | solution.py:433
  69.0 9.3 %collective-permute-start.35 = (bf16[64,16,128]{2,1,0:T(8,128)(2,1)S(1)}, bf16[64,16,128]{2,1,0:T(8,128)(2,1)S(1)}, u32[]{:S(2)}, u32[]{:S(2)}) collective-permute-start(bf16[64,16,128]{2,1,0:T(8,128)(2,1)S(1)} %get-tuple-element.103), channel_id=1, source_target_pairs={{0,16},{4,20},{8,24},{12,28},{16,0},{20,4},{24,8},{28,12},{1,17},{... | collective-permute-start | bytes 786440 | tf_op jit(solution)/shard_map/ppermute | solution.py:433
  70.1 22.7 %collective-permute-start.36 = (bf16[64,16,128]{2,1,0:T(8,128)(2,1)S(1)}, bf16[64,16,128]{2,1,0:T(8,128)(2,1)S(1)}, u32[]{:S(2)}, u32[]{:S(2)}) collective-permute-start(bf16[64,16,128]{2,1,0:T(8,128)(2,1)S(1)} %get-tuple-element.104), channel_id=1, source_target_pairs={{0,20},{4,16},{8,28},{12,24},{16,4},{20,0},{24,12},{28,8},{1,21},{... | collective-permute-start | bytes 786440 | tf_op jit(solution)/shard_map/ppermute | solution.py:433
  70.2 24.4 %collective-permute-start.37 = (bf16[64,16,128]{2,1,0:T(8,128)(2,1)S(1)}, bf16[64,16,128]{2,1,0:T(8,128)(2,1)S(1)}, u32[]{:S(2)}, u32[]{:S(2)}) collective-permute-start(bf16[64,16,128]{2,1,0:T(8,128)(2,1)S(1)} %get-tuple-element.105), channel_id=1, source_target_pairs={{0,24},{4,28},{8,16},{12,20},{16,8},{20,12},{24,0},{28,4},{1,25},{... | collective-permute-start | bytes 786440 | tf_op jit(solution)/shard_map/ppermute | solution.py:433
  74.7 21.5 %collective-permute-start.38 = (bf16[64,16,128]{2,1,0:T(8,128)(2,1)S(1)}, bf16[64,16,128]{2,1,0:T(8,128)(2,1)S(1)}, u32[]{:S(2)}, u32[]{:S(2)}) collective-permute-start(bf16[64,16,128]{2,1,0:T(8,128)(2,1)S(1)} %get-tuple-element.106), channel_id=1, source_target_pairs={{0,28},{4,24},{8,20},{12,16},{16,12},{20,8},{24,4},{28,0},{1,29},{... | collective-permute-start | bytes 786440 | tf_op jit(solution)/shard_map/ppermute | solution.py:433
  77.6 21.2 %collective-permute-start.22 = (bf16[64,16,128]{2,1,0:T(8,128)(2,1)S(1)}, bf16[64,16,128]{2,1,0:T(8,128)(2,1)S(1)}, u32[]{:S(2)}, u32[]{:S(2)}) collective-permute-start(bf16[64,16,128]{2,1,0:T(8,128)(2,1)S(1)} %get-tuple-element.88), channel_id=1, source_target_pairs={{0,4},{4,0},{8,12},{12,8},{16,20},{20,16},{24,28},{28,24},{1,5},{5... | collective-permute-start | bytes 786440 | tf_op jit(solution)/shard_map/ppermute | solution.py:433
  78.3 20.7 %collective-permute-start.23 = (bf16[64,16,128]{2,1,0:T(8,128)(2,1)S(1)}, bf16[64,16,128]{2,1,0:T(8,128)(2,1)S(1)}, u32[]{:S(2)}, u32[]{:S(2)}) collective-permute-start(bf16[64,16,128]{2,1,0:T(8,128)(2,1)S(1)} %get-tuple-element.89), channel_id=1, source_target_pairs={{0,8},{4,12},{8,0},{12,4},{16,24},{20,28},{24,16},{28,20},{1,9},{5... | collective-permute-start | bytes 786440 | tf_op jit(solution)/shard_map/ppermute | solution.py:433
  92.9 7.6 %collective-permute-start.24 = (bf16[64,16,128]{2,1,0:T(8,128)(2,1)S(1)}, bf16[64,16,128]{2,1,0:T(8,128)(2,1)S(1)}, u32[]{:S(2)}, u32[]{:S(2)}) collective-permute-start(bf16[64,16,128]{2,1,0:T(8,128)(2,1)S(1)} %get-tuple-element.90), channel_id=1, source_target_pairs={{0,12},{4,8},{8,4},{12,0},{16,28},{20,24},{24,20},{28,16},{1,13},{... | collective-permute-start | bytes 786440 | tf_op jit(solution)/shard_map/ppermute | solution.py:433
  94.6 14.0 %collective-permute-start.17 = (bf16[64,16,128]{2,1,0:T(8,128)(2,1)S(1)}, bf16[64,16,128]{2,1,0:T(8,128)(2,1)S(1)}, u32[]{:S(2)}, u32[]{:S(2)}) collective-permute-start(bf16[64,16,128]{2,1,0:T(8,128)(2,1)S(1)} %get-tuple-element.79), channel_id=1, source_target_pairs={{0,1},{1,0},{2,3},{3,2},{4,5},{5,4},{6,7},{7,6},{8,9},{9,8},{10,11... | collective-permute-start | bytes 786440 | tf_op jit(solution)/shard_map/ppermute | solution.py:433
  96.2 21.4 %collective-permute-start.18 = (bf16[64,16,128]{2,1,0:T(8,128)(2,1)S(1)}, bf16[64,16,128]{2,1,0:T(8,128)(2,1)S(1)}, u32[]{:S(2)}, u32[]{:S(2)}) collective-permute-start(bf16[64,16,128]{2,1,0:T(8,128)(2,1)S(1)} %get-tuple-element.80), channel_id=1, source_target_pairs={{0,2},{1,3},{2,0},{3,1},{4,6},{5,7},{6,4},{7,5},{8,10},{9,11},{10,... | collective-permute-start | bytes 786440 | tf_op jit(solution)/shard_map/ppermute | solution.py:433
  98.8 20.5 %collective-permute-start.19 = (bf16[64,16,128]{2,1,0:T(8,128)(2,1)S(1)}, bf16[64,16,128]{2,1,0:T(8,128)(2,1)S(1)}, u32[]{:S(2)}, u32[]{:S(2)}) collective-permute-start(bf16[64,16,128]{2,1,0:T(8,128)(2,1)S(1)} %get-tuple-element.81), channel_id=1, source_target_pairs={{0,3},{1,2},{2,1},{3,0},{4,7},{5,6},{6,5},{7,4},{8,11},{9,10},{10,... | collective-permute-start | bytes 786440 | tf_op jit(solution)/shard_map/ppermute | solution.py:433
  99.0 20.9 %collective-permute-start.7 = (bf16[64,16,128]{2,1,0:T(8,128)(2,1)S(1)}, bf16[64,16,128]{2,1,0:T(8,128)(2,1)S(1)}, u32[]{:S(2)}, u32[]{:S(2)}) collective-permute-start(bf16[64,16,128]{2,1,0:T(8,128)(2,1)S(1)} %get-tuple-element.66), channel_id=1, source_target_pairs={{0,1},{1,0},{2,3},{3,2},{4,5},{5,4},{6,7},{7,6},{8,9},{9,8},{10,11... | collective-permute-start | bytes 786440 | tf_op jit(solution)/shard_map/ppermute | solution.py:433
  100.4 0.7 copy-start.4
  101.1 39.0 %collective-permute-start.8 = (bf16[64,16,128]{2,1,0:T(8,128)(2,1)S(1)}, bf16[64,16,128]{2,1,0:T(8,128)(2,1)S(1)}, u32[]{:S(2)}, u32[]{:S(2)}) collective-permute-start(bf16[64,16,128]{2,1,0:T(8,128)(2,1)S(1)} %get-tuple-element.67), channel_id=1, source_target_pairs={{0,2},{1,3},{2,0},{3,1},{4,6},{5,7},{6,4},{7,5},{8,10},{9,11},{10,... | collective-permute-start | bytes 786440 | tf_op jit(solution)/shard_map/ppermute | solution.py:433
  108.5 31.5 %collective-permute-start.9 = (bf16[64,16,128]{2,1,0:T(8,128)(2,1)S(1)}, bf16[64,16,128]{2,1,0:T(8,128)(2,1)S(1)}, u32[]{:S(2)}, u32[]{:S(2)}) collective-permute-start(bf16[64,16,128]{2,1,0:T(8,128)(2,1)S(1)} %get-tuple-element.68), channel_id=1, source_target_pairs={{0,3},{1,2},{2,1},{3,0},{4,7},{5,6},{6,5},{7,4},{8,11},{9,10},{10,... | collective-permute-start | bytes 786440 | tf_op jit(solution)/shard_map/ppermute | solution.py:433
  115.7 24.3 %copy-start.8 = (bf16[64,16,128]{2,1,0:T(8,128)(2,1)}, bf16[64,16,128]{2,1,0:T(8,128)(2,1)S(1)}, u32[]{:S(2)}) copy-start(bf16[64,16,128]{2,1,0:T(8,128)(2,1)S(1)} %get-tuple-element.110) | copy-start | bytes 786436
  115.7 24.4 %copy-start.9 = (bf16[64,16,128]{2,1,0:T(8,128)(2,1)}, bf16[64,16,128]{2,1,0:T(8,128)(2,1)S(1)}, u32[]{:S(2)}) copy-start(bf16[64,16,128]{2,1,0:T(8,128)(2,1)S(1)} %get-tuple-element.109) | copy-start | bytes 786436
  117.6 34.2 %collective-permute-start.25 = (bf16[64,16,128]{2,1,0:T(8,128)(2,1)}, bf16[64,16,128]{2,1,0:T(8,128)(2,1)}, u32[]{:S(2)}, u32[]{:S(2)}) collective-permute-start(bf16[64,16,128]{2,1,0:T(8,128)(2,1)} %get-tuple-element.91), channel_id=1, source_target_pairs={{0,16},{4,20},{8,24},{12,28},{16,0},{20,4},{24,8},{28,12},{1,17},{... | collective-permute-start | bytes 786440 | tf_op jit(solution)/shard_map/ppermute | solution.py:433
  119.3 33.6 %collective-permute-start.26 = (bf16[64,16,128]{2,1,0:T(8,128)(2,1)}, bf16[64,16,128]{2,1,0:T(8,128)(2,1)}, u32[]{:S(2)}, u32[]{:S(2)}) collective-permute-start(bf16[64,16,128]{2,1,0:T(8,128)(2,1)} %get-tuple-element.92), channel_id=1, source_target_pairs={{0,20},{4,16},{8,28},{12,24},{16,4},{20,0},{24,12},{28,8},{1,21},{... | collective-permute-start | bytes 786440 | tf_op jit(solution)/shard_map/ppermute | solution.py:433
  119.9 34.6 %collective-permute-start.27 = (bf16[64,16,128]{2,1,0:T(8,128)(2,1)}, bf16[64,16,128]{2,1,0:T(8,128)(2,1)}, u32[]{:S(2)}, u32[]{:S(2)}) collective-permute-start(bf16[64,16,128]{2,1,0:T(8,128)(2,1)} %get-tuple-element.93), channel_id=1, source_target_pairs={{0,24},{4,28},{8,16},{12,20},{16,8},{20,12},{24,0},{28,4},{1,25},{... | collective-permute-start | bytes 786440 | tf_op jit(solution)/shard_map/ppermute | solution.py:433
  140.1 14.4 %collective-permute-start.28 = (bf16[64,16,128]{2,1,0:T(8,128)(2,1)}, bf16[64,16,128]{2,1,0:T(8,128)(2,1)}, u32[]{:S(2)}, u32[]{:S(2)}) collective-permute-start(bf16[64,16,128]{2,1,0:T(8,128)(2,1)} %get-tuple-element.94), channel_id=1, source_target_pairs={{0,28},{4,24},{8,20},{12,16},{16,12},{20,8},{24,4},{28,0},{1,29},{... | collective-permute-start | bytes 786440 | tf_op jit(solution)/shard_map/ppermute | solution.py:433
  140.1 58.2 %copy-start.2 = (bf16[64,16,128]{2,1,0:T(8,128)(2,1)}, bf16[64,16,128]{2,1,0:T(8,128)(2,1)S(1)}, u32[]{:S(2)}) copy-start(bf16[64,16,128]{2,1,0:T(8,128)(2,1)S(1)} %collective-permute-done.9.refs_3_) | copy-start | bytes 786436
  140.1 21.2 %collective-permute-start.39 = (bf16[64,16,128]{2,1,0:T(8,128)(2,1)}, bf16[64,16,128]{2,1,0:T(8,128)(2,1)S(1)}, u32[]{:S(2)}, u32[]{:S(2)}) collective-permute-start(bf16[64,16,128]{2,1,0:T(8,128)(2,1)} %get-tuple-element.108), channel_id=1, source_target_pairs={{0,1},{1,0},{2,3},{3,2},{4,5},{5,4},{6,7},{7,6},{8,9},{9,8},{10,11... | collective-permute-start | bytes 786440 | tf_op jit(solution)/shard_map/ppermute | solution.py:433
  147.6 50.7 %all-to-all-start = ((f32[8,160,128]{2,1,0:T(8,128)}), f32[8,160,128]{2,1,0:T(8,128)}, u32[]{:S(2)}, u32[]{:S(2)}) async-start(f32[8,160,128]{2,1,0:T(8,128)} %bitcast.1), calls=%async_computation | async-start | bytes 1310720 | tf_op jit(solution)/shard_map/all_to_all | solution.py:438
  151.8 21.2 %collective-permute-start.40 = (bf16[64,16,128]{2,1,0:T(8,128)(2,1)}, bf16[64,16,128]{2,1,0:T(8,128)(2,1)S(1)}, u32[]{:S(2)}, u32[]{:S(2)}) collective-permute-start(bf16[64,16,128]{2,1,0:T(8,128)(2,1)} %copy-done.9), channel_id=1, source_target_pairs={{0,2},{1,3},{2,0},{3,1},{4,6},{5,7},{6,4},{7,5},{8,10},{9,11},{10,... | collective-permute-start | bytes 786440 | tf_op jit(solution)/shard_map/ppermute | solution.py:433
  152.9 20.1 %collective-permute-start.41 = (bf16[64,16,128]{2,1,0:T(8,128)(2,1)}, bf16[64,16,128]{2,1,0:T(8,128)(2,1)S(1)}, u32[]{:S(2)}, u32[]{:S(2)}) collective-permute-start(bf16[64,16,128]{2,1,0:T(8,128)(2,1)} %copy-done.8), channel_id=1, source_target_pairs={{0,3},{1,2},{2,1},{3,0},{4,7},{5,6},{6,5},{7,4},{8,11},{9,10},{10,... | collective-permute-start | bytes 786440 | tf_op jit(solution)/shard_map/ppermute | solution.py:433
  154.5 1.0 copy-start.5
  158.4 19.7 %collective-permute-start.29 = (bf16[64,16,128]{2,1,0:T(8,128)(2,1)S(1)}, bf16[64,16,128]{2,1,0:T(8,128)(2,1)S(1)}, u32[]{:S(2)}, u32[]{:S(2)}) collective-permute-start(bf16[64,16,128]{2,1,0:T(8,128)(2,1)S(1)} %get-tuple-element.96), channel_id=1, source_target_pairs={{0,1},{1,0},{2,3},{3,2},{4,5},{5,4},{6,7},{7,6},{8,9},{9,8},{10,11... | collective-permute-start | bytes 786440 | tf_op jit(solution)/shard_map/ppermute | solution.py:433
  160.5 34.7 %collective-permute-start.30 = (bf16[64,16,128]{2,1,0:T(8,128)(2,1)S(1)}, bf16[64,16,128]{2,1,0:T(8,128)(2,1)S(1)}, u32[]{:S(2)}, u32[]{:S(2)}) collective-permute-start(bf16[64,16,128]{2,1,0:T(8,128)(2,1)S(1)} %get-tuple-element.97), channel_id=1, source_target_pairs={{0,2},{1,3},{2,0},{3,1},{4,6},{5,7},{6,4},{7,5},{8,10},{9,11},{10,... | collective-permute-start | bytes 786440 | tf_op jit(solution)/shard_map/ppermute | solution.py:433
  161.3 33.9 %collective-permute-start.31 = (bf16[64,16,128]{2,1,0:T(8,128)(2,1)S(1)}, bf16[64,16,128]{2,1,0:T(8,128)(2,1)S(1)}, u32[]{:S(2)}, u32[]{:S(2)}) collective-permute-start(bf16[64,16,128]{2,1,0:T(8,128)(2,1)S(1)} %get-tuple-element.98), channel_id=1, source_target_pairs={{0,3},{1,2},{2,1},{3,0},{4,7},{5,6},{6,5},{7,4},{8,11},{9,10},{10,... | collective-permute-start | bytes 786440 | tf_op jit(solution)/shard_map/ppermute | solution.py:433
  198.3 19.3 %all-to-all-start.1 = ((f32[8,64,512]{2,1,0:T(8,128)}), f32[8,64,512]{2,1,0:T(8,128)S(1)}, u32[]{:S(2)}, u32[]{:S(2)}) async-start(f32[8,64,512]{2,1,0:T(8,128)} %bitcast.5), calls=%async_computation.1 | async-start | bytes 2097152 | tf_op jit(solution)/shard_map/all_to_all | solution.py:438
  202.2 74.6 %all-gather.2.cloned.1.call-start = ((), (), s32[]{:S(2)}) async-start(), calls=%async_computation.2 | async-start | bytes 1179648 | tf_op jit(solution)/shard_map/all_gather | solution.py:444
  203.4 20.5 %collective-permute-start.20 = (f32[160,128]{1,0:T(8,128)S(1)}, f32[160,128]{1,0:T(8,128)S(1)}, u32[]{:S(2)}, u32[]{:S(2)}) collective-permute-start(f32[160,128]{1,0:T(8,128)S(1)} %reduce_sum.18), channel_id=1, source_target_pairs={{0,1},{1,0},{2,3},{3,2},{4,5},{5,4},{6,7},{7,6},{8,9},{9,8},{10,11... | collective-permute-start | bytes 245768 | tf_op jit(solution)/shard_map/ppermute | solution.py:433
  217.7 14.6 %collective-permute-start.42 = (f32[64,512]{1,0:T(8,128)S(1)}, f32[64,512]{1,0:T(8,128)S(1)}, u32[]{:S(2)}, u32[]{:S(2)}) collective-permute-start(f32[64,512]{1,0:T(8,128)S(1)} %reduce_sum.19), channel_id=1, source_target_pairs={{0,1},{1,0},{2,3},{3,2},{4,5},{5,4},{6,7},{7,6},{8,9},{9,8},{10,11... | collective-permute-start | bytes 393224 | tf_op jit(solution)/shard_map/ppermute | solution.py:433
  223.9 8.4 %collective-permute-start.21 = (f32[160,128]{1,0:T(8,128)S(1)}, f32[160,128]{1,0:T(8,128)S(1)}, u32[]{:S(2)}, u32[]{:S(2)}) collective-permute-start(f32[160,128]{1,0:T(8,128)S(1)} %add.12), channel_id=1, source_target_pairs={{0,2},{1,3},{2,0},{3,1},{4,6},{5,7},{6,4},{7,5},{8,10},{9,11},{10,... | collective-permute-start | bytes 245768 | tf_op jit(solution)/shard_map/ppermute | solution.py:433
  232.4 9.1 %collective-permute-start.43 = (f32[64,512]{1,0:T(8,128)S(1)}, f32[64,512]{1,0:T(8,128)S(1)}, u32[]{:S(2)}, u32[]{:S(2)}) collective-permute-start(f32[64,512]{1,0:T(8,128)S(1)} %add.14), channel_id=1, source_target_pairs={{0,2},{1,3},{2,0},{3,1},{4,6},{5,7},{6,4},{7,5},{8,10},{9,11},{10,... | collective-permute-start | bytes 393224 | tf_op jit(solution)/shard_map/ppermute | solution.py:433
  242.2 24.7 %copy-start.3 = (bf16[64,16,128]{2,1,0:T(8,128)(2,1)S(1)}, bf16[64,16,128]{2,1,0:T(8,128)(2,1)}, u32[]{:S(2)}) copy-start(bf16[64,16,128]{2,1,0:T(8,128)(2,1)} %copy-done.2) | copy-start | bytes 786436
Sparse Core Ops, SparseCore 0:
  242.3 23.6 all-gather.1

commit v4 on v3

--- a/solution.py
+++ b/solution.py
@@ -20,10 +20,9 @@
 
 
 def pack_kernel(slabs, capacity, per_slab, parts, dest_ref, owned_ref, *refs):
-    out_refs, (buf_ref, ids_ref, count_ref) = refs[:-3], refs[-3:]
+    out_refs, (ids_ref, count_ref) = refs[:parts], refs[parts:]
     shares = owned_ref.shape[1]
-    span = capacity * shares
-    me = lax.axis_index("space")
+    used = capacity * shares
     lane = lax.broadcasted_iota(jnp.int32, (1, TILE), 1)
     ids_ref[...] = jnp.full_like(ids_ref, -1)
     for slab in range(slabs):
@@ -39,39 +38,35 @@
             count_ref[slab] = rank + 1
             here = pl.ds(slab, 1)
             ids_ref[here, :] = jnp.where(lane == rank, block - slab * per_slab, ids_ref[here, :])
-            at = slab * span + rank * shares
             for part in range(parts):
-                buf_ref[part, pl.ds(at, shares)] = owned_ref[i, :, part]
+                at = slab * (out_refs[part].shape[0] // slabs) + rank * shares
+                out_refs[part][pl.ds(at, shares)] = owned_ref[i, :, part]
 
         return 0
 
     lax.fori_loop(0, dest_ref.shape[0], place, 0, unroll=4)
     for part in range(parts):
-        for m in range(slabs):
-            out_ref = out_refs[part * slabs + m]
-            slab = me ^ m
-            out_ref[:span] = buf_ref[part, pl.ds(slab * span, span)]
-            if out_ref.shape[0] > span:
-                ids = ids_ref[pl.ds(slab, 1), :].astype(jnp.float32)
-                out_ref[span] = jnp.broadcast_to(ids, out_ref.shape[1:]).astype(out_ref.dtype)
-
-
-def pack(dest, owned, slabs, per_slab, after=None):
+        span = out_refs[part].shape[0] // slabs
+        if span > used:
+            for slab in range(slabs):
+                ids = ids_ref[slab : slab + 1, :].astype(jnp.float32)
+                tile = jnp.broadcast_to(ids, out_refs[part].shape[1:])
+                out_refs[part][slab * span + used] = tile.astype(out_refs[part].dtype)
+
+
+def pack(dest, owned, slabs, per_slab, with_ids, after=()):
     slots, shares, parts, rows, width = owned.shape
     capacity = slots // slabs
-    span = capacity * shares
-    first = 0 if after is None else 1
     sent = []
     for part in range(parts):
-        extra = 1 if after is None and part == 0 else 0
-        sent += [jax.ShapeDtypeStruct((span + extra, rows, width), owned.dtype)] * slabs
-    outs = pl.pallas_call(
-        lambda *refs: pack_kernel(slabs, capacity, per_slab, parts, *refs[first:]),
+        extra = slabs if with_ids and part == 0 else 0
+        sent.append(jax.ShapeDtypeStruct((slots * shares + extra, rows, width), owned.dtype))
+    return pl.pallas_call(
+        lambda *refs: pack_kernel(slabs, capacity, per_slab, parts, *refs[len(after) :]),
         out_shape=tuple(sent),
-        in_specs=[SMEM] * first + [SMEM, VMEM],
+        in_specs=[ANY] * len(after) + [SMEM, VMEM],
         out_specs=(VMEM,) * len(sent),
         scratch_shapes=[
-            pltpu.VMEM((parts, slots * shares, rows, width), owned.dtype),
             pltpu.VMEM((slabs, TILE), jnp.int32),
             pltpu.SMEM((slabs,), jnp.int32),
         ],
@@ -80,56 +75,52 @@
             flops=0, bytes_accessed=2 * owned.size * 2, transcendentals=0
         ),
         name="pack",
-    )(*([] if after is None else [after]), dest, owned)
-    return [outs[part * slabs : (part + 1) * slabs] for part in range(parts)]
+    )(*after, dest, owned)
 
 
 def settle_kernel(slabs, capacity, first, *refs):
     if first:
-        moved_refs, out_refs, (ids_ref, meta_ref) = refs[:slabs], refs[slabs:-2], refs[-2:]
-        meta_ref, ids_ref = ids_ref, meta_ref
-        span = moved_refs[0].shape[0] - 1
-        for m in range(slabs):
-            tile = moved_refs[m][span].astype(jnp.float32)
-            ids_ref[m : m + 1, :] = tile[:1].astype(jnp.int32)
+        moved_ref, out_refs, meta_ref, ids_ref = refs[0], refs[1:-2], refs[-2], refs[-1]
+        span = moved_ref.shape[0] // slabs
+        for source in range(slabs):
+            tile = moved_ref[source * span + span - 1].astype(jnp.float32)
+            ids_ref[source : source + 1, :] = tile[:1].astype(jnp.int32)
         pltpu.sync_copy(ids_ref, meta_ref)
     else:
-        meta_ref, moved_refs, out_refs = refs[0], refs[1 : 1 + slabs], refs[1 + slabs :]
+        meta_ref, moved_ref, out_refs = refs[0], refs[1], refs[2:]
+        span = moved_ref.shape[0] // slabs
     shares = len(out_refs)
     mine = lax.axis_index("snap")
-    for m in range(slabs):
+    for source in range(slabs):
 
         def place(rank, _):
-            block = meta_ref[m, rank]
+            block = meta_ref[source, rank]
 
             @pl.when(block >= 0)
             def _():
                 for r in range(shares):
-                    out_refs[r][block] = moved_refs[m][rank * shares + (mine ^ r)]
+                    out_refs[r][block] = moved_ref[source * span + rank * shares + (mine ^ r)]
 
             return 0
 
         lax.fori_loop(0, capacity, place, 0, unroll=4)
 
 
-def settle(meta, moved, capacity, per_slab, shares):
+def settle(meta, moved, slabs, capacity, per_slab, shares, after=()):
     first = meta is None
-    slabs = len(moved)
-    rows, width = moved[0].shape[1:]
-    pieces = (jax.ShapeDtypeStruct((per_slab, rows, width), moved[0].dtype),) * shares
+    rows, width = moved.shape[1:]
+    pieces = (jax.ShapeDtypeStruct((per_slab, rows, width), moved.dtype),) * shares
     ids = jax.ShapeDtypeStruct((slabs, TILE), jnp.int32)
     outs = pl.pallas_call(
-        lambda *refs: settle_kernel(slabs, capacity, first, *refs),
+        lambda *refs: settle_kernel(slabs, capacity, first, *refs[len(after) :]),
         out_shape=pieces + ((ids,) if first else ()),
-        in_specs=([] if first else [SMEM]) + [VMEM] * slabs,
+        in_specs=[ANY] * len(after) + ([] if first else [SMEM]) + [VMEM],
         out_specs=(VMEM,) * shares + ((SMEM,) if first else ()),
         scratch_shapes=[pltpu.VMEM((slabs, TILE), jnp.int32)] if first else [],
         compiler_params=pltpu.CompilerParams(vmem_limit_bytes=VMEM_BYTES),
-        cost_estimate=pl.CostEstimate(
-            flops=0, bytes_accessed=2 * slabs * moved[0].size, transcendentals=0
-        ),
+        cost_estimate=pl.CostEstimate(flops=0, bytes_accessed=2 * moved.size, transcendentals=0),
         name="settle",
-    )(*([] if first else [meta]), *moved)
+    )(*after, *([] if first else [meta]), moved)
     return outs[:shares], (outs[shares] if first else meta)
 
 
@@ -220,16 +211,16 @@
                 ]
 
 
-def cross_sum(x_cells, y_cells, steps=4):
+def cross_sum(x_cells, y_cells, after, steps=4):
     parts, shares = len(x_cells), len(x_cells[0])
     blocks, rows, width = x_cells[0][0].shape
     spec = pl.BlockSpec((blocks // steps, rows, width), lambda i: (i, 0, 0))
     full = shares * width
     return pl.pallas_call(
-        lambda *refs: cross_kernel(parts, shares, *refs),
+        lambda *refs: cross_kernel(parts, shares, *refs[len(after) :]),
         grid=(steps,),
         out_shape=jax.ShapeDtypeStruct((full, full), jnp.float32),
-        in_specs=[spec] * (2 * parts * shares),
+        in_specs=[ANY] * len(after) + [spec] * (2 * parts * shares),
         out_specs=pl.BlockSpec((full, full), lambda i: (0, 0)),
         scratch_shapes=[pltpu.VMEM((full, full), jnp.float32)],
         compiler_params=pltpu.CompilerParams(vmem_limit_bytes=VMEM_BYTES),
@@ -239,7 +230,7 @@
             transcendentals=0,
         ),
         name="cross_sum",
-    )(*[piece for part in list(x_cells) + list(y_cells) for piece in part])
+    )(*after, *[piece for part in list(x_cells) + list(y_cells) for piece in part])
 
 
 def three_terms(value):
@@ -361,11 +352,11 @@
             lo_ref[rows, lanes] = low.astype(jnp.bfloat16)
 
 
-def factor(blocks, tiles, rows_total):
+def factor(blocks, tiles, rows_total, after):
     full = tiles * TILE
     tile = pltpu.VMEM((TILE, TILE), jnp.float32)
     return pl.pallas_call(
-        lambda *refs: factor_kernel(tiles, rows_total, *refs),
+        lambda *refs: factor_kernel(tiles, rows_total, *refs[len(after) :]),
         out_shape=(
             jax.ShapeDtypeStruct((full, full), jnp.float32),
             jax.ShapeDtypeStruct((full, full), jnp.float32),
@@ -373,7 +364,7 @@
             jax.ShapeDtypeStruct((full, full), jnp.bfloat16),
             jax.ShapeDtypeStruct((full, full), jnp.bfloat16),
         ),
-        in_specs=[VMEM],
+        in_specs=[ANY] * len(after) + [VMEM],
         out_specs=(VMEM,) * 5,
         scratch_shapes=[
             pltpu.VMEM((tiles, 2 * tiles, TILE, TILE), jnp.float32),
@@ -387,7 +378,7 @@
             flops=40 * 10**9, bytes_accessed=8 * full * full, transcendentals=full
         ),
         name="factor",
-    )(blocks)
+    )(*after, blocks)
 
 
 def basis_kernel(parts, shares, *refs):
@@ -433,10 +424,11 @@
     return lax.ppermute(value, axis, [(i, i ^ mask) for i in range(lax.axis_size(axis))])
 
 
-def sum_over_devices(value, slabs, shares):
-    lanes = value.shape[-1]
-    pieces = lax.all_to_all(value, "space", split_axis=0, concat_axis=0, tiled=True)
-    piece = jnp.sum(pieces.reshape(slabs, -1, lanes), axis=0)
+def slab_sum(value, slabs):
+    return lax.psum_scatter(value, "space", scatter_dimension=0, tiled=True)
+
+
+def share_sum(piece, shares):
     hop = 1
     while hop < shares:
         piece += swap(piece, "snap", hop)
@@ -452,31 +444,44 @@
     parts = patch // shares // CELL_TILE
     rows_total = slabs * per_slab * patch
     full = shares * width
+    tiles = full // TILE
+    pairs = tiles * (tiles + 1) // 2
 
     def parted(owned):
         return owned.reshape(slots, shares, parts, CELL_TILE, width)
 
-    def exchange(sent, meta):
-        cells = []
-        for part in sent:
-            moved = [part[0]] + [swap(part[m], "space", m) for m in range(1, slabs)]
-            pieces, meta = settle(meta, moved, slots // slabs, per_slab, shares)
-            cells.append([pieces[0]] + [swap(pieces[r], "snap", r) for r in range(1, shares)])
-        return cells, meta
-
-    sent_x = pack(patch_dest, parted(owned_x), slabs, per_slab)
-    x_cells, meta = exchange(sent_x, None)
-    sent_y = pack(patch_dest, parted(owned_y), slabs, per_slab, meta)
-    y_cells, _ = exchange(sent_y, meta)
-
-    tiles = full // TILE
-    pairs = tiles * (tiles + 1) // 2
-    local = gram_blocks(x_cells).reshape(pairs * TILE, TILE)
-    total = sum_over_devices(local, slabs, shares).reshape(pairs, TILE, TILE)
-    r_factor, inverse, *terms = factor(total, tiles, rows_total)
+    def to_slabs(part):
+        return lax.all_to_all(part, "space", split_axis=0, concat_axis=0, tiled=True)
+
+    def to_rows(pieces):
+        return [pieces[0]] + [swap(pieces[r], "snap", r) for r in range(1, shares)]
+
+    def place(meta, moved, after=()):
+        return settle(meta, moved, slabs, slots // slabs, per_slab, shares, after)
+
+    sent_x = pack(patch_dest, parted(owned_x), slabs, per_slab, True)
+    moved_x = [to_slabs(part) for part in sent_x]
+    pieces, meta = place(None, moved_x[0])
+    x_cells = [to_rows(pieces)]
+    sent_y = pack(patch_dest, parted(owned_y), slabs, per_slab, False, [meta])
+    for moved in moved_x[1:]:
+        pieces, _ = place(meta, moved, x_cells[-1][1:] + [sent_y[0]])
+        x_cells.append(to_rows(pieces))
+    gram_piece = slab_sum(gram_blocks(x_cells).reshape(pairs * TILE, TILE), slabs)
+
+    y_cells, after = [], x_cells[-1][1:]
+    for part in sent_y:
+        pieces, _ = place(meta, to_slabs(part), after)
+        y_cells.append(to_rows(pieces))
+        after = y_cells[-1][1:] + [gram_piece]
+
+    gram = share_sum(gram_piece, shares)
+    r_factor, inverse, *terms = factor(
+        gram.reshape(pairs, TILE, TILE), tiles, rows_total, [y_cells[-1][0]]
+    )
     q_basis = basis(x_cells, terms).reshape(per_slab, patch // shares, full)
 
-    cross = sum_over_devices(cross_sum(x_cells, y_cells), slabs, shares)
+    cross = share_sum(slab_sum(cross_sum(x_cells, y_cells, [gram]), slabs), shares)
     projection = jnp.dot(inverse, cross, precision=HIGHEST) / math.sqrt(rows_total)
     return q_basis, r_factor, projection
 

time: 288 us -> 351 us (1.22)
  blocking collectives: 9.05 us -> 71.1 us
  starting transfers between devices: 87 us -> 38.5 us
  waiting for transfers between devices: 107 us -> 147 us
  local copies, waits for them, and re-layouts: 4.84 us -> 15.4 us
    all_to_all x0 -> x2, blocking collectives: none -> 61.1 us  [to_slabs(): lax.all_to_all(part, 'space', split_axis=0, concat_axis=0, tiled=True)]
    reduce_scatter x0 -> x2, waiting for transfers between devices: none -> 60.6 us  [slab_sum(): return lax.psum_scatter(value, 'space', scatter_dimension=0, tiled=True)]
    ppermute x44 -> x16, starting transfers between devices: 78.9 us -> 30.2 us  [swap(): lax.ppermute(value, axis, [(i, i ^ mask) for i in range(lax.axis_size(axi...]
    ppermute x44 -> x16, waiting for transfers between devices: 99.3 us -> 69.9 us  [swap(): lax.ppermute(value, axis, [(i, i ^ mask) for i in range(lax.axis_size(axi...]
    unnamed x20 -> x64, local copies, waits for them, and re-layouts: 4.84 us -> 15.4 us
    all_to_all x2, waiting for transfers between devices: 8.07 us -> 16.6 us  [to_slabs(): lax.all_to_all(part, 'space', split_axis=0, concat_axis=0, tiled=True)]
  transfers between devices with their start and end apart: 47 -> 21, of which waited for: 16 -> 10; matrix products, arithmetic and copies ran while one was open for 0% -> 0% of each run, Pallas kernels for 19% -> 15%
where the time goes in v4:
time: 351 us; the launch traced here: 350 us
  waiting for transfers between devices  147 us (42%)
  blocking collectives  71.1 us (20%)
  Pallas kernels  58.3 us (17%)
  starting transfers between devices  38.5 us (11%)
  local copies, waits for them, and re-layouts  15.4 us (4%)
  between operations  14.1 us (4%)
  matrix products  4.04 us (1%)
    ppermute x16, waiting for transfers between devices, swap(): lax.ppermute(value, axis, [(i, i ^ mask) for i in range(lax.axis_size(axi...  69.9 us
    all_to_all x2, blocking collectives, to_slabs(): lax.all_to_all(part, 'space', split_axis=0, concat_axis=0, tiled=True)  61.1 us
    reduce_scatter x2, waiting for transfers between devices, slab_sum(): return lax.psum_scatter(value, 'space', scatter_dimension=0, tiled=True)  60.6 us
    ppermute x16, starting transfers between devices, swap(): lax.ppermute(value, axis, [(i, i ^ mask) for i in range(lax.axis_size(axi...  30.2 us
    pallas_call x1, Pallas kernels, factor(): pl.pallas_call(lambda *refs: factor_kernel(tiles, rows_total, *refs[len(a...  24.7 us
    all_to_all x2, waiting for transfers between devices, to_slabs(): lax.all_to_all(part, 'space', split_axis=0, concat_axis=0, tiled=True)  16.6 us
    unnamed x64, local copies, waits for them, and re-layouts  15.4 us
    pallas_call x4, Pallas kernels, settle(): pl.pallas_call(lambda *refs: settle_kernel(slabs, capacity, first, *refs[...  12 us
  transfers between devices with their start and end apart: 21, of which 10 were waited for; matrix products, arithmetic and copies ran while one was open for 0% of the time, Pallas kernels for 15%

profile of v4, /device:TPU:0, one launch (start us, length us, event | category | flops | bytes accessed | tf_op | source)
XLA Modules:
  0.0 350.3 jit_solution(8895113211528612474)
XLA Ops:
  7.2 2.2 copy-done.4
  9.4 0.7 copy-done.30
  10.0 2.6 pack.2
  12.7 31.3 %all_to_all.20.refs_0_ = bf16[520,16,128]{2,1,0:T(8,128)(2,1)S(1)} all-to-all(bf16[520,16,128]{2,1,0:T(8,128)(2,1)S(1)} %get-tuple-element.29), channel_id=1, replica_groups=mesh['space'=8,'snap'=4] {'space'}, dimensions={0} | all-to-all | bytes 4259840 | tf_op jit(solution)/shard_map/all_to_all | solution.py:454
  43.9 4.4 %all-to-all-start.1 = ((bf16[512,16,128]{2,1,0:T(8,128)(2,1)}), bf16[512,16,128]{2,1,0:T(8,128)(2,1)}, u32[]{:S(2)}, u32[]{:S(2)}) async-start(bf16[512,16,128]{2,1,0:T(8,128)(2,1)} %copy-done.6), calls=%async_computation.1 | async-start | bytes 4194304 | tf_op jit(solution)/shard_map/all_to_all | solution.py:454
  48.3 3.1 settle.4
  51.4 0.7 copy-done.19
  52.2 2.2 copy-done.3
  54.3 2.6 pack.3
  57.0 1.3 copy-done.5
  58.3 16.6 %all-to-all-done.1.refs_5_ = bf16[512,16,128]{2,1,0:T(8,128)(2,1)} async-done(((bf16[512,16,128]{2,1,0:T(8,128)(2,1)}), bf16[512,16,128]{2,1,0:T(8,128)(2,1)}, u32[]{:S(2)}, u32[]{:S(2)}) %all-to-all-start.1) | async-done | bytes 2097184 | tf_op jit(solution)/shard_map/all_to_all | solution.py:454
  75.0 29.8 %all_to_all.21.refs_4_ = bf16[512,16,128]{2,1,0:T(8,128)(2,1)} all-to-all(bf16[512,16,128]{2,1,0:T(8,128)(2,1)S(1)} %get-tuple-element.35.refs_3_), channel_id=1, replica_groups=mesh['space'=8,'snap'=4] {'space'}, dimensions={0} | all-to-all | bytes 4194304 | tf_op jit(solution)/shard_map/all_to_all | solution.py:454
  104.7 3.6 %all-to-all-start.3 = ((bf16[512,16,128]{2,1,0:T(8,128)(2,1)}), bf16[512,16,128]{2,1,0:T(8,128)(2,1)S(1)}, u32[]{:S(2)}, u32[]{:S(2)}) async-start(bf16[512,16,128]{2,1,0:T(8,128)(2,1)} %copy-done.5), calls=%async_computation.4 | async-start | bytes 4194304 | tf_op jit(solution)/shard_map/all_to_all | solution.py:454
  108.3 0.0 reduce-scatter.3.cloned.1.call-start
  108.4 1.6 collective-permute-start
  110.0 2.6 collective-permute-start.1
  112.6 0.2 collective-permute-start.2
  112.8 9.4 %collective-permute-done.refs_0_.refs_1_.refs_2_ = bf16[64,16,128]{2,1,0:T(8,128)(2,1)S(1)} collective-permute-done((bf16[64,16,128]{2,1,0:T(8,128)(2,1)}, bf16[64,16,128]{2,1,0:T(8,128)(2,1)S(1)}, u32[]{:S(2)}, u32[]{:S(2)}) %collective-permute-start) | collective-permute-done | bytes 262176 | tf_op jit(solution)/shard_map/ppermute | solution.py:424
  122.3 9.3 %collective-permute-done.1.refs_1_.refs_2_.refs_3_ = bf16[64,16,128]{2,1,0:T(8,128)(2,1)S(1)} collective-permute-done((bf16[64,16,128]{2,1,0:T(8,128)(2,1)}, bf16[64,16,128]{2,1,0:T(8,128)(2,1)S(1)}, u32[]{:S(2)}, u32[]{:S(2)}) %collective-permute-start.1) | collective-permute-done | bytes 262176 | tf_op jit(solution)/shard_map/ppermute | solution.py:424
  131.6 1.6 copy-done.2
  133.2 3.4 settle.5
  136.6 0.0 copy-start.23
  136.6 5.3 %collective-permute-start.3 = (bf16[64,16,128]{2,1,0:T(8,128)(2,1)S(1)}, bf16[64,16,128]{2,1,0:T(8,128)(2,1)S(1)}, u32[]{:S(2)}, u32[]{:S(2)}) collective-permute-start(bf16[64,16,128]{2,1,0:T(8,128)(2,1)S(1)} %get-tuple-element.38), channel_id=1, source_target_pairs={{0,1},{1,0},{2,3},{3,2},{4,5},{5,4},{6,7},{7,6},{8,9},{9,8},{10,11... | collective-permute-start | bytes 786440 | tf_op jit(solution)/shard_map/ppermute | solution.py:424
  141.9 1.1 collective-permute-start.4
  143.0 1.4 collective-permute-start.5
  144.4 7.7 %collective-permute-done.3.refs_0_.refs_5_.refs_6_ = bf16[64,16,128]{2,1,0:T(8,128)(2,1)S(1)} collective-permute-done((bf16[64,16,128]{2,1,0:T(8,128)(2,1)S(1)}, bf16[64,16,128]{2,1,0:T(8,128)(2,1)S(1)}, u32[]{:S(2)}, u32[]{:S(2)}) %collective-permute-start.3) | collective-permute-done | bytes 262176 | tf_op jit(solution)/shard_map/ppermute | solution.py:424
  152.0 11.2 %collective-permute-done.4.refs_1_.refs_6_.refs_7_ = bf16[64,16,128]{2,1,0:T(8,128)(2,1)S(1)} collective-permute-done((bf16[64,16,128]{2,1,0:T(8,128)(2,1)S(1)}, bf16[64,16,128]{2,1,0:T(8,128)(2,1)S(1)}, u32[]{:S(2)}, u32[]{:S(2)}) %collective-permute-start.4) | collective-permute-done | bytes 262176 | tf_op jit(solution)/shard_map/ppermute | solution.py:424
  163.3 2.1 gram_blocks.1
  165.4 0.7 copy-done.13
  166.1 0.8 copy-done.17
  167.0 0.0 reduce-scatter.3.cloned.1.call-update
  167.0 0.0 reduce-scatter.5.cloned.1.call-start
  167.1 1.6 copy-done
  168.7 0.9 copy-done.14
  169.6 3.2 settle.6
  172.8 0.7 copy-done.28
  173.5 4.1 %collective-permute-start.6 = (bf16[64,16,128]{2,1,0:T(8,128)(2,1)}, bf16[64,16,128]{2,1,0:T(8,128)(2,1)S(1)}, u32[]{:S(2)}, u32[]{:S(2)}) collective-permute-start(bf16[64,16,128]{2,1,0:T(8,128)(2,1)} %get-tuple-element.41), channel_id=1, source_target_pairs={{0,1},{1,0},{2,3},{3,2},{4,5},{5,4},{6,7},{7,6},{8,9},{9,8},{10,11... | collective-permute-start | bytes 786440 | tf_op jit(solution)/shard_map/ppermute | solution.py:424
  177.6 1.0 collective-permute-start.7
  178.6 1.5 collective-permute-start.8
  180.1 24.4 %reduce-scatter.3.cloned.1.call-done.refs_3_ = f32[160,128]{1,0:T(8,128)} async-done(((f32[1280,128]{1,0:T(8,128)}), f32[160,128]{1,0:T(8,128)}) %reduce-scatter.3.cloned.1.call-update) | async-done | bytes 81936 | tf_op jit(solution)/shard_map/reduce_scatter | solution.py:428
  204.5 1.5 collective-permute-start.9
  206.0 0.9 copy-done.18
  207.0 2.3 settle.7
  209.3 0.6 collective-permute-start.11
  209.9 2.4 collective-permute-start.12
  212.3 1.4 collective-permute-start.13
  213.8 1.6 collective-permute-start.10
  215.4 22.9 %collective-permute-done.10 = f32[160,128]{1,0:T(8,128)S(1)} collective-permute-done((f32[160,128]{1,0:T(8,128)S(1)}, f32[160,128]{1,0:T(8,128)S(1)}, u32[]{:S(2)}, u32[]{:S(2)}) %collective-permute-start.10) | collective-permute-done | bytes 81952 | tf_op jit(solution)/shard_map/ppermute | solution.py:424
  238.3 10.1 %all_gather.6.refs_0_ = f32[1280,128]{1,0:T(8,128)S(1)} all-gather(f32[160,128]{1,0:T(8,128)S(1)} %add.17), channel_id=1, replica_groups=mesh['space'=8,'snap'=4] {'space'}, dimensions={0}, use_global_device_ids=true | all-gather | bytes 737280 | tf_op jit(solution)/shard_map/all_gather | solution.py:436
  248.5 4.3 %cross_sum.1 = f32[512,512]{1,0:T(8,128)} custom-call(f32[1280,128]{1,0:T(8,128)S(1)} %all_gather.6.refs_0_, bf16[64,16,128]{2,1,0:T(8,128)(2,1)S(1)} %copy-done.21, bf16[64,16,128]{2,1,0:T(8,128)(2,1)S(1)} %collective-permute-done.refs_0_.refs_1_.refs_2_, bf16[64,16,128]{2,1,0:T(8,128)(2,1)S(1)} %collective-permute-done.1.refs_1_.refs_2_.refs_3_, ...), custom_call_target="tpu_custom_call" | custom-call | flops 1073741824 | bytes 4194304 | tf_op jit(solution)/shard_map/cross_sum/pallas_call | solution.py:219
  252.8 0.0 reduce-scatter.5.cloned.1.call-update
  252.8 0.2 all-gather.2.cloned.1.call-start
  253.0 36.2 %reduce-scatter.5.cloned.1.call-done = f32[64,512]{1,0:T(8,128)} async-done(((f32[512,512]{1,0:T(8,128)}), f32[64,512]{1,0:T(8,128)}) %reduce-scatter.5.cloned.1.call-update) | async-done | bytes 131088 | tf_op jit(solution)/shard_map/reduce_scatter | solution.py:428
  289.2 1.5 collective-permute-start.14
  290.7 3.8 %collective-permute-done.14 = f32[64,512]{1,0:T(8,128)S(1)} collective-permute-done((f32[64,512]{1,0:T(8,128)}, f32[64,512]{1,0:T(8,128)S(1)}, u32[]{:S(2)}, u32[]{:S(2)}) %collective-permute-start.14) | collective-permute-done | bytes 131104 | tf_op jit(solution)/shard_map/ppermute | solution.py:424
  294.5 0.9 add.18
  295.5 2.5 collective-permute-start.15
  297.9 5.5 %collective-permute-done.15 = f32[64,512]{1,0:T(8,128)S(1)} collective-permute-done((f32[64,512]{1,0:T(8,128)S(1)}, f32[64,512]{1,0:T(8,128)S(1)}, u32[]{:S(2)}, u32[]{:S(2)}) %collective-permute-start.15) | collective-permute-done | bytes 131104 | tf_op jit(solution)/shard_map/ppermute | solution.py:424
  303.5 0.7 add.19
  304.1 0.0 all-gather.2.cloned.1.call-update
  304.2 0.9 copy-done.27
  305.1 24.7 %factor.1 = (f32[512,512]{1,0:T(8,128)}, f32[512,512]{1,0:T(8,128)S(1)}, bf16[512,512]{1,0:T(8,128)(2,1)S(1)}, bf16[512,512]{1,0:T(8,128)(2,1)S(1)}, bf16[512,512]{1,0:T(8,128)(2,1)S(1)}) custom-call(bf16[64,16,128]{2,1,0:T(8,128)(2,1)S(1)} %copy-done.27, f32[10,128,128]{2,1,0:T(8,128)S(1)} %bitcast.9), custom_call_target="tpu_custom_call" | custom-call | flops 40000000000 | bytes 2097152 | tf_op jit(solution)/shard_map/factor/pallas_call | solution.py:358
  329.8 9.9 %basis.1 = f32[64,2,16,512]{3,2,1,0:T(8,128)} custom-call(bf16[64,16,128]{2,1,0:T(8,128)(2,1)S(1)} %copy-done.22, bf16[64,16,128]{2,1,0:T(8,128)(2,1)S(1)} %collective-permute-done.refs_0_.refs_1_.refs_2_, bf16[64,16,128]{2,1,0:T(8,128)(2,1)S(1)} %collective-permute-done.1.refs_1_.refs_2_.refs_3_, ...), custom_call_target="tpu_custom_call" | custom-call | flops 3221225472 | bytes 6291456 | tf_op jit(solution)/shard_map/basis/pallas_call | solution.py:407
  339.7 4.0 %convolution_multiply_fusion = f32[512,512]{1,0:T(8,128)} fusion(f32[512,512]{1,0:T(8,128)S(1)} %get-tuple-element.50, f32[512,512]{1,0:T(8,128)} %all-gather.2.cloned.1.call-done), kind=kOutput, calls=%fused_computation | convolution fusion | flops 1610874880 | bytes 3145728 | tf_op jit(solution)/shard_map/dot_general | solution.py:485
  (63 shorter events, 0.2 us)
Async XLA Ops:
  7.2 2.2 copy-start.4
  9.4 0.7 copy-start.30
  12.6 31.3 %copy-start.6 = (bf16[512,16,128]{2,1,0:T(8,128)(2,1)}, bf16[512,16,128]{2,1,0:T(8,128)(2,1)S(1)}, u32[]{:S(2)}) copy-start(bf16[512,16,128]{2,1,0:T(8,128)(2,1)S(1)} %get-tuple-element.36) | copy-start | bytes 6291460
  43.9 31.0 %all-to-all-start.1 = ((bf16[512,16,128]{2,1,0:T(8,128)(2,1)}), bf16[512,16,128]{2,1,0:T(8,128)(2,1)}, u32[]{:S(2)}, u32[]{:S(2)}) async-start(bf16[512,16,128]{2,1,0:T(8,128)(2,1)} %copy-done.6), calls=%async_computation.1 | async-start | bytes 4194304 | tf_op jit(solution)/shard_map/all_to_all | solution.py:454
  48.3 3.9 %copy-start.31 = (s32[128]{0:T(128)S(1)}, s32[128]{0:T(128)}, u32[]{:S(2)}) copy-start(s32[128]{0:T(128)} %refs_1_.1) | copy-start | bytes 1540
  51.4 0.7 copy-start.19
  52.2 2.2 copy-start.3
  57.0 1.4 copy-start.5
  58.3 46.4 %copy-start.1 = (bf16[512,16,128]{2,1,0:T(8,128)(2,1)}, bf16[512,16,128]{2,1,0:T(8,128)(2,1)S(1)}, u32[]{:S(2)}) copy-start(bf16[512,16,128]{2,1,0:T(8,128)(2,1)S(1)} %get-tuple-element.35.refs_3_) | copy-start | bytes 6291460
  104.7 101.2 %all-to-all-start.3 = ((bf16[512,16,128]{2,1,0:T(8,128)(2,1)}), bf16[512,16,128]{2,1,0:T(8,128)(2,1)S(1)}, u32[]{:S(2)}, u32[]{:S(2)}) async-start(bf16[512,16,128]{2,1,0:T(8,128)(2,1)} %copy-done.5), calls=%async_computation.4 | async-start | bytes 4194304 | tf_op jit(solution)/shard_map/all_to_all | solution.py:454
  108.3 96.1 %reduce-scatter.3.cloned.1.call-start = ((), (), s32[]{:S(2)}) async-start(), calls=%async_computation.6 | async-start | bytes 737280 | tf_op jit(solution)/shard_map/reduce_scatter | solution.py:428
  108.4 13.9 %collective-permute-start = (bf16[64,16,128]{2,1,0:T(8,128)(2,1)}, bf16[64,16,128]{2,1,0:T(8,128)(2,1)S(1)}, u32[]{:S(2)}, u32[]{:S(2)}) collective-permute-start(bf16[64,16,128]{2,1,0:T(8,128)(2,1)} %get-tuple-element.31), channel_id=1, source_target_pairs={{0,1},{1,0},{2,3},{3,2},{4,5},{5,4},{6,7},{7,6},{8,9},{9,8},{10,11... | collective-permute-start | bytes 786440 | tf_op jit(solution)/shard_map/ppermute | solution.py:424
  110.0 21.6 %collective-permute-start.1 = (bf16[64,16,128]{2,1,0:T(8,128)(2,1)}, bf16[64,16,128]{2,1,0:T(8,128)(2,1)S(1)}, u32[]{:S(2)}, u32[]{:S(2)}) collective-permute-start(bf16[64,16,128]{2,1,0:T(8,128)(2,1)} %get-tuple-element.32), channel_id=1, source_target_pairs={{0,2},{1,3},{2,0},{3,1},{4,6},{5,7},{6,4},{7,5},{8,10},{9,11},{10,... | collective-permute-start | bytes 786440 | tf_op jit(solution)/shard_map/ppermute | solution.py:424
  112.6 19.0 %collective-permute-start.2 = (bf16[64,16,128]{2,1,0:T(8,128)(2,1)S(1)}, bf16[64,16,128]{2,1,0:T(8,128)(2,1)S(1)}, u32[]{:S(2)}, u32[]{:S(2)}) collective-permute-start(bf16[64,16,128]{2,1,0:T(8,128)(2,1)S(1)} %get-tuple-element.33), channel_id=1, source_target_pairs={{0,3},{1,2},{2,1},{3,0},{4,7},{5,6},{6,5},{7,4},{8,11},{9,10},{10,... | collective-permute-start | bytes 786440 | tf_op jit(solution)/shard_map/ppermute | solution.py:424
  131.6 1.6 copy-start.2
  133.2 30.1 %copy-start.20 = (bf16[64,16,128]{2,1,0:T(8,128)(2,1)S(1)}, bf16[64,16,128]{2,1,0:T(8,128)(2,1)}, u32[]{:S(2)}) copy-start(bf16[64,16,128]{2,1,0:T(8,128)(2,1)} %copy-done.19) | copy-start | bytes 786436
  136.6 28.8 %copy-start.23 = (bf16[64,16,128]{2,1,0:T(8,128)(2,1)}, bf16[64,16,128]{2,1,0:T(8,128)(2,1)S(1)}, u32[]{:S(2)}) copy-start(bf16[64,16,128]{2,1,0:T(8,128)(2,1)S(1)} %get-tuple-element.37.refs_4_.refs_5_) | copy-start | bytes 786436
  136.6 15.4 %collective-permute-start.3 = (bf16[64,16,128]{2,1,0:T(8,128)(2,1)S(1)}, bf16[64,16,128]{2,1,0:T(8,128)(2,1)S(1)}, u32[]{:S(2)}, u32[]{:S(2)}) collective-permute-start(bf16[64,16,128]{2,1,0:T(8,128)(2,1)S(1)} %get-tuple-element.38), channel_id=1, source_target_pairs={{0,1},{1,0},{2,3},{3,2},{4,5},{5,4},{6,7},{7,6},{8,9},{9,8},{10,11... | collective-permute-start | bytes 786440 | tf_op jit(solution)/shard_map/ppermute | solution.py:424
  141.9 21.4 %collective-permute-start.4 = (bf16[64,16,128]{2,1,0:T(8,128)(2,1)S(1)}, bf16[64,16,128]{2,1,0:T(8,128)(2,1)S(1)}, u32[]{:S(2)}, u32[]{:S(2)}) collective-permute-start(bf16[64,16,128]{2,1,0:T(8,128)(2,1)S(1)} %get-tuple-element.39), channel_id=1, source_target_pairs={{0,2},{1,3},{2,0},{3,1},{4,6},{5,7},{6,4},{7,5},{8,10},{9,11},{10,... | collective-permute-start | bytes 786440 | tf_op jit(solution)/shard_map/ppermute | solution.py:424
  143.0 20.3 %collective-permute-start.5 = (bf16[64,16,128]{2,1,0:T(8,128)(2,1)S(1)}, bf16[64,16,128]{2,1,0:T(8,128)(2,1)S(1)}, u32[]{:S(2)}, u32[]{:S(2)}) collective-permute-start(bf16[64,16,128]{2,1,0:T(8,128)(2,1)S(1)} %get-tuple-element.40), channel_id=1, source_target_pairs={{0,3},{1,2},{2,1},{3,0},{4,7},{5,6},{6,5},{7,4},{8,11},{9,10},{10,... | collective-permute-start | bytes 786440 | tf_op jit(solution)/shard_map/ppermute | solution.py:424
  152.0 15.0 %copy-start.7 = (bf16[64,16,128]{2,1,0:T(8,128)(2,1)}, bf16[64,16,128]{2,1,0:T(8,128)(2,1)S(1)}, u32[]{:S(2)}) copy-start(bf16[64,16,128]{2,1,0:T(8,128)(2,1)S(1)} %collective-permute-done.3.refs_0_.refs_5_.refs_6_) | copy-start | bytes 786436
  163.3 3.8 %copy-start.10 = (bf16[64,16,128]{2,1,0:T(8,128)(2,1)}, bf16[64,16,128]{2,1,0:T(8,128)(2,1)S(1)}, u32[]{:S(2)}) copy-start(bf16[64,16,128]{2,1,0:T(8,128)(2,1)S(1)} %collective-permute-done.4.refs_1_.refs_6_.refs_7_) | copy-start | bytes 786436
  165.4 0.7 copy-start.13
  166.1 0.8 copy-start.17
  167.0 122.2 %reduce-scatter.5.cloned.1.call-start = ((), (), s32[]{:S(2)}) async-start(), calls=%async_computation.7 | async-start | bytes 1179648 | tf_op jit(solution)/shard_map/reduce_scatter | solution.py:428
  167.1 1.6 copy-start
  168.7 0.9 copy-start.14
  172.8 0.7 copy-start.28
  173.5 32.5 %collective-permute-start.6 = (bf16[64,16,128]{2,1,0:T(8,128)(2,1)}, bf16[64,16,128]{2,1,0:T(8,128)(2,1)S(1)}, u32[]{:S(2)}, u32[]{:S(2)}) collective-permute-start(bf16[64,16,128]{2,1,0:T(8,128)(2,1)} %get-tuple-element.41), channel_id=1, source_target_pairs={{0,1},{1,0},{2,3},{3,2},{4,5},{5,4},{6,7},{7,6},{8,9},{9,8},{10,11... | collective-permute-start | bytes 786440 | tf_op jit(solution)/shard_map/ppermute | solution.py:424
  177.6 28.4 %collective-permute-start.7 = (bf16[64,16,128]{2,1,0:T(8,128)(2,1)}, bf16[64,16,128]{2,1,0:T(8,128)(2,1)S(1)}, u32[]{:S(2)}, u32[]{:S(2)}) collective-permute-start(bf16[64,16,128]{2,1,0:T(8,128)(2,1)} %get-tuple-element.42), channel_id=1, source_target_pairs={{0,2},{1,3},{2,0},{3,1},{4,6},{5,7},{6,4},{7,5},{8,10},{9,11},{10,... | collective-permute-start | bytes 786440 | tf_op jit(solution)/shard_map/ppermute | solution.py:424
  178.6 27.4 %collective-permute-start.8 = (bf16[64,16,128]{2,1,0:T(8,128)(2,1)}, bf16[64,16,128]{2,1,0:T(8,128)(2,1)}, u32[]{:S(2)}, u32[]{:S(2)}) collective-permute-start(bf16[64,16,128]{2,1,0:T(8,128)(2,1)} %get-tuple-element.43), channel_id=1, source_target_pairs={{0,3},{1,2},{2,1},{3,0},{4,7},{5,6},{6,5},{7,4},{8,11},{9,10},{10,... | collective-permute-start | bytes 786440 | tf_op jit(solution)/shard_map/ppermute | solution.py:424
  204.5 9.3 %collective-permute-start.9 = (f32[160,128]{1,0:T(8,128)}, f32[160,128]{1,0:T(8,128)S(1)}, u32[]{:S(2)}, u32[]{:S(2)}) collective-permute-start(f32[160,128]{1,0:T(8,128)} %reduce-scatter.3.cloned.1.call-done.refs_3_), channel_id=1, source_target_pairs={{0,1},{1,0},{2,3},{3,2},{4,5},{5,4},{6,7},{7,6},{8,9},{9,8},{10,11... | collective-permute-start | bytes 245768 | tf_op jit(solution)/shard_map/ppermute | solution.py:424
  206.0 42.4 %copy-start.8 = (bf16[64,16,128]{2,1,0:T(8,128)(2,1)S(1)}, bf16[64,16,128]{2,1,0:T(8,128)(2,1)}, u32[]{:S(2)}) copy-start(bf16[64,16,128]{2,1,0:T(8,128)(2,1)} %copy-done.7) | copy-start | bytes 786436
  206.0 42.5 %copy-start.11 = (bf16[64,16,128]{2,1,0:T(8,128)(2,1)S(1)}, bf16[64,16,128]{2,1,0:T(8,128)(2,1)}, u32[]{:S(2)}) copy-start(bf16[64,16,128]{2,1,0:T(8,128)(2,1)} %copy-done.10) | copy-start | bytes 786436
  206.0 42.5 %copy-start.15 = (bf16[64,16,128]{2,1,0:T(8,128)(2,1)S(1)}, bf16[64,16,128]{2,1,0:T(8,128)(2,1)}, u32[]{:S(2)}) copy-start(bf16[64,16,128]{2,1,0:T(8,128)(2,1)} %copy-done.13) | copy-start | bytes 786436
  206.0 1.0 copy-start.18
  207.0 41.5 %copy-start.21 = (bf16[64,16,128]{2,1,0:T(8,128)(2,1)S(1)}, bf16[64,16,128]{2,1,0:T(8,128)(2,1)}, u32[]{:S(2)}) copy-start(bf16[64,16,128]{2,1,0:T(8,128)(2,1)} %copy-done.19) | copy-start | bytes 786436
  207.0 41.5 %copy-start.24 = (bf16[64,16,128]{2,1,0:T(8,128)(2,1)S(1)}, bf16[64,16,128]{2,1,0:T(8,128)(2,1)}, u32[]{:S(2)}) copy-start(bf16[64,16,128]{2,1,0:T(8,128)(2,1)} %copy-done.23) | copy-start | bytes 786436
  207.0 41.5 %copy-start.29 = (bf16[64,16,128]{2,1,0:T(8,128)(2,1)S(1)}, bf16[64,16,128]{2,1,0:T(8,128)(2,1)}, u32[]{:S(2)}) copy-start(bf16[64,16,128]{2,1,0:T(8,128)(2,1)} %copy-done.28) | copy-start | bytes 786436
  209.3 39.1 %copy-start.26 = (bf16[64,16,128]{2,1,0:T(8,128)(2,1)}, bf16[64,16,128]{2,1,0:T(8,128)(2,1)S(1)}, u32[]{:S(2)}) copy-start(bf16[64,16,128]{2,1,0:T(8,128)(2,1)S(1)} %get-tuple-element.45.refs_0_.refs_13_) | copy-start | bytes 786436
  209.3 39.1 %collective-permute-start.11 = (bf16[64,16,128]{2,1,0:T(8,128)(2,1)S(1)}, bf16[64,16,128]{2,1,0:T(8,128)(2,1)S(1)}, u32[]{:S(2)}, u32[]{:S(2)}) collective-permute-start(bf16[64,16,128]{2,1,0:T(8,128)(2,1)S(1)} %get-tuple-element.52), channel_id=1, source_target_pairs={{0,1},{1,0},{2,3},{3,2},{4,5},{5,4},{6,7},{7,6},{8,9},{9,8},{10,11... | collective-permute-start | bytes 786440 | tf_op jit(solution)/shard_map/ppermute | solution.py:424
  209.9 38.5 %collective-permute-start.12 = (bf16[64,16,128]{2,1,0:T(8,128)(2,1)S(1)}, bf16[64,16,128]{2,1,0:T(8,128)(2,1)S(1)}, u32[]{:S(2)}, u32[]{:S(2)}) collective-permute-start(bf16[64,16,128]{2,1,0:T(8,128)(2,1)S(1)} %get-tuple-element.53), channel_id=1, source_target_pairs={{0,2},{1,3},{2,0},{3,1},{4,6},{5,7},{6,4},{7,5},{8,10},{9,11},{10,... | collective-permute-start | bytes 786440 | tf_op jit(solution)/shard_map/ppermute | solution.py:424
  212.3 36.1 %collective-permute-start.13 = (bf16[64,16,128]{2,1,0:T(8,128)(2,1)S(1)}, bf16[64,16,128]{2,1,0:T(8,128)(2,1)S(1)}, u32[]{:S(2)}, u32[]{:S(2)}) collective-permute-start(bf16[64,16,128]{2,1,0:T(8,128)(2,1)S(1)} %get-tuple-element.54), channel_id=1, source_target_pairs={{0,3},{1,2},{2,1},{3,0},{4,7},{5,6},{6,5},{7,4},{8,11},{9,10},{10,... | collective-permute-start | bytes 786440 | tf_op jit(solution)/shard_map/ppermute | solution.py:424
  213.8 24.5 %collective-permute-start.10 = (f32[160,128]{1,0:T(8,128)S(1)}, f32[160,128]{1,0:T(8,128)S(1)}, u32[]{:S(2)}, u32[]{:S(2)}) collective-permute-start(f32[160,128]{1,0:T(8,128)S(1)} %add.16), channel_id=1, source_target_pairs={{0,2},{1,3},{2,0},{3,1},{4,6},{5,7},{6,4},{7,5},{8,10},{9,11},{10,... | collective-permute-start | bytes 245768 | tf_op jit(solution)/shard_map/ppermute | solution.py:424
  252.8 86.9 %all-gather.2.cloned.1.call-start = ((), (), s32[]{:S(2)}) async-start(), calls=%async_computation.8 | async-start | bytes 1179648 | tf_op jit(solution)/shard_map/all_gather | solution.py:436
  289.2 5.3 %collective-permute-start.14 = (f32[64,512]{1,0:T(8,128)}, f32[64,512]{1,0:T(8,128)S(1)}, u32[]{:S(2)}, u32[]{:S(2)}) collective-permute-start(f32[64,512]{1,0:T(8,128)} %reduce-scatter.5.cloned.1.call-done), channel_id=1, source_target_pairs={{0,1},{1,0},{2,3},{3,2},{4,5},{5,4},{6,7},{7,6},{8,9},{9,8},{10,11... | collective-permute-start | bytes 393224 | tf_op jit(solution)/shard_map/ppermute | solution.py:424
  295.5 8.0 %collective-permute-start.15 = (f32[64,512]{1,0:T(8,128)S(1)}, f32[64,512]{1,0:T(8,128)S(1)}, u32[]{:S(2)}, u32[]{:S(2)}) collective-permute-start(f32[64,512]{1,0:T(8,128)S(1)} %add.18), channel_id=1, source_target_pairs={{0,2},{1,3},{2,0},{3,1},{4,6},{5,7},{6,4},{7,5},{8,10},{9,11},{10,... | collective-permute-start | bytes 393224 | tf_op jit(solution)/shard_map/ppermute | solution.py:424
  304.2 1.0 copy-start.27
  305.1 24.7 %copy-start.9 = (bf16[64,16,128]{2,1,0:T(8,128)(2,1)S(1)}, bf16[64,16,128]{2,1,0:T(8,128)(2,1)}, u32[]{:S(2)}) copy-start(bf16[64,16,128]{2,1,0:T(8,128)(2,1)} %copy-done.7) | copy-start | bytes 786436
  305.1 24.7 %copy-start.12 = (bf16[64,16,128]{2,1,0:T(8,128)(2,1)S(1)}, bf16[64,16,128]{2,1,0:T(8,128)(2,1)}, u32[]{:S(2)}) copy-start(bf16[64,16,128]{2,1,0:T(8,128)(2,1)} %copy-done.10) | copy-start | bytes 786436
  305.1 24.7 %copy-start.16 = (bf16[64,16,128]{2,1,0:T(8,128)(2,1)S(1)}, bf16[64,16,128]{2,1,0:T(8,128)(2,1)}, u32[]{:S(2)}) copy-start(bf16[64,16,128]{2,1,0:T(8,128)(2,1)} %copy-done.13) | copy-start | bytes 786436
  305.1 24.7 %copy-start.22 = (bf16[64,16,128]{2,1,0:T(8,128)(2,1)S(1)}, bf16[64,16,128]{2,1,0:T(8,128)(2,1)}, u32[]{:S(2)}) copy-start(bf16[64,16,128]{2,1,0:T(8,128)(2,1)} %copy-done.19) | copy-start | bytes 786436
  305.1 24.7 %copy-start.25 = (bf16[64,16,128]{2,1,0:T(8,128)(2,1)S(1)}, bf16[64,16,128]{2,1,0:T(8,128)(2,1)}, u32[]{:S(2)}) copy-start(bf16[64,16,128]{2,1,0:T(8,128)(2,1)} %copy-done.23) | copy-start | bytes 786436
Sparse Core Ops, SparseCore 0:
  167.1 37.3 reduce-scatter.2
  252.9 36.2 reduce-scatter.4
  304.3 23.6 all-gather.1

commit v5 on v4

--- a/solution.py
+++ b/solution.py
@@ -9,6 +9,7 @@
 
 TILE = 128
 GROUP = 8
+CORES = 2
 CELL_TILE = 16
 VMEM_BYTES = 32 * 1024 * 1024
 HIGHEST = lax.Precision.HIGHEST
@@ -20,9 +21,11 @@
 
 
 def pack_kernel(slabs, capacity, per_slab, parts, dest_ref, owned_ref, *refs):
-    out_refs, (ids_ref, count_ref) = refs[:parts], refs[parts:]
+    out_refs, (ids_ref, count_ref) = refs[: 2 * parts], refs[2 * parts :]
+    chips = slabs // CORES
     shares = owned_ref.shape[1]
     used = capacity * shares
+    me = lax.axis_index("space")
     lane = lax.broadcasted_iota(jnp.int32, (1, TILE), 1)
     ids_ref[...] = jnp.full_like(ids_ref, -1)
     for slab in range(slabs):
@@ -38,30 +41,39 @@
             count_ref[slab] = rank + 1
             here = pl.ds(slab, 1)
             ids_ref[here, :] = jnp.where(lane == rank, block - slab * per_slab, ids_ref[here, :])
-            for part in range(parts):
-                at = slab * (out_refs[part].shape[0] // slabs) + rank * shares
-                out_refs[part][pl.ds(at, shares)] = owned_ref[i, :, part]
+            away = slab ^ me
+            chip = lax.shift_right_logical(away, 1)
+            for core in range(CORES):
+
+                @pl.when((away & 1) == core)
+                def _():
+                    for part in range(parts):
+                        out_ref = out_refs[part * CORES + core]
+                        at = chip * (out_ref.shape[0] // chips) + rank * shares
+                        out_ref[pl.ds(at, shares)] = owned_ref[i, :, part]
 
         return 0
 
-    lax.fori_loop(0, dest_ref.shape[0], place, 0, unroll=4)
-    for part in range(parts):
-        span = out_refs[part].shape[0] // slabs
-        if span > used:
-            for slab in range(slabs):
-                ids = ids_ref[slab : slab + 1, :].astype(jnp.float32)
-                tile = jnp.broadcast_to(ids, out_refs[part].shape[1:])
-                out_refs[part][slab * span + used] = tile.astype(out_refs[part].dtype)
+    lax.fori_loop(0, dest_ref.shape[0], place, 0, unroll=2)
+    for away in range(slabs):
+        for part in range(parts):
+            out_ref = out_refs[part * CORES + away % CORES]
+            span = out_ref.shape[0] // chips
+            if span > used:
+                ids = ids_ref[pl.ds(me ^ away, 1), :].astype(jnp.float32)
+                tile = jnp.broadcast_to(ids, out_ref.shape[1:]).astype(out_ref.dtype)
+                out_ref[away // CORES * span + used] = tile
 
 
 def pack(dest, owned, slabs, per_slab, with_ids, after=()):
     slots, shares, parts, rows, width = owned.shape
+    chips = slabs // CORES
     capacity = slots // slabs
     sent = []
     for part in range(parts):
-        extra = slabs if with_ids and part == 0 else 0
-        sent.append(jax.ShapeDtypeStruct((slots * shares + extra, rows, width), owned.dtype))
-    return pl.pallas_call(
+        span = capacity * shares + (1 if with_ids and part == 0 else 0)
+        sent += [jax.ShapeDtypeStruct((chips * span, rows, width), owned.dtype)] * CORES
+    outs = pl.pallas_call(
         lambda *refs: pack_kernel(slabs, capacity, per_slab, parts, *refs[len(after) :]),
         out_shape=tuple(sent),
         in_specs=[ANY] * len(after) + [SMEM, VMEM],
@@ -76,51 +88,79 @@
         ),
         name="pack",
     )(*after, dest, owned)
-
-
-def settle_kernel(slabs, capacity, first, *refs):
+    return [outs[part * CORES : (part + 1) * CORES] for part in range(parts)]
+
+
+def merge_kernel(same_ref, other_ref, *out_refs):
+    span = same_ref.shape[0] // len(out_refs)
+    for chip, out_ref in enumerate(out_refs):
+        out_ref[:span] = same_ref[chip * span : (chip + 1) * span]
+        out_ref[span:] = other_ref[chip * span : (chip + 1) * span]
+
+
+def merge(same, other, chips):
+    tiles, rows, width = same.shape
+    out = jax.ShapeDtypeStruct((CORES * tiles // chips, rows, width), same.dtype)
+    return pl.pallas_call(
+        merge_kernel,
+        out_shape=(out,) * chips,
+        in_specs=[VMEM, VMEM],
+        out_specs=(VMEM,) * chips,
+        compiler_params=pltpu.CompilerParams(vmem_limit_bytes=VMEM_BYTES),
+        cost_estimate=pl.CostEstimate(flops=0, bytes_accessed=8 * same.size, transcendentals=0),
+        name="merge",
+    )(same, other)
+
+
+def settle_kernel(chips, capacity, first, *refs):
     if first:
-        moved_ref, out_refs, meta_ref, ids_ref = refs[0], refs[1:-2], refs[-2], refs[-1]
-        span = moved_ref.shape[0] // slabs
-        for source in range(slabs):
-            tile = moved_ref[source * span + span - 1].astype(jnp.float32)
+        moved_refs, out_refs, meta_ref, ids_ref = refs[:chips], refs[chips:-2], refs[-2], refs[-1]
+        span = moved_refs[0].shape[0] // CORES
+        for source in range(chips * CORES):
+            at = source % CORES * span + span - 1
+            tile = moved_refs[source // CORES][at].astype(jnp.float32)
             ids_ref[source : source + 1, :] = tile[:1].astype(jnp.int32)
         pltpu.sync_copy(ids_ref, meta_ref)
     else:
-        meta_ref, moved_ref, out_refs = refs[0], refs[1], refs[2:]
-        span = moved_ref.shape[0] // slabs
+        meta_ref, moved_refs, out_refs = refs[0], refs[1 : 1 + chips], refs[1 + chips :]
+        span = moved_refs[0].shape[0] // CORES
     shares = len(out_refs)
     mine = lax.axis_index("snap")
-    for source in range(slabs):
+    for source in range(chips * CORES):
+        moved_ref = moved_refs[source // CORES]
 
         def place(rank, _):
             block = meta_ref[source, rank]
 
             @pl.when(block >= 0)
             def _():
+                at = source % CORES * span + rank * shares
                 for r in range(shares):
-                    out_refs[r][block] = moved_ref[source * span + rank * shares + (mine ^ r)]
+                    out_refs[r][block] = moved_ref[at + (mine ^ r)]
 
             return 0
 
         lax.fori_loop(0, capacity, place, 0, unroll=4)
 
 
-def settle(meta, moved, slabs, capacity, per_slab, shares, after=()):
+def settle(meta, moved, capacity, per_slab, shares, after=()):
     first = meta is None
-    rows, width = moved.shape[1:]
-    pieces = (jax.ShapeDtypeStruct((per_slab, rows, width), moved.dtype),) * shares
-    ids = jax.ShapeDtypeStruct((slabs, TILE), jnp.int32)
+    chips = len(moved)
+    rows, width = moved[0].shape[1:]
+    pieces = (jax.ShapeDtypeStruct((per_slab, rows, width), moved[0].dtype),) * shares
+    ids = jax.ShapeDtypeStruct((chips * CORES, TILE), jnp.int32)
     outs = pl.pallas_call(
-        lambda *refs: settle_kernel(slabs, capacity, first, *refs[len(after) :]),
+        lambda *refs: settle_kernel(chips, capacity, first, *refs[len(after) :]),
         out_shape=pieces + ((ids,) if first else ()),
-        in_specs=[ANY] * len(after) + ([] if first else [SMEM]) + [VMEM],
+        in_specs=[ANY] * len(after) + ([] if first else [SMEM]) + [VMEM] * chips,
         out_specs=(VMEM,) * shares + ((SMEM,) if first else ()),
-        scratch_shapes=[pltpu.VMEM((slabs, TILE), jnp.int32)] if first else [],
-        compiler_params=pltpu.CompilerParams(vmem_limit_bytes=VMEM_BYTES),
-        cost_estimate=pl.CostEstimate(flops=0, bytes_accessed=2 * moved.size, transcendentals=0),
+        scratch_shapes=[pltpu.VMEM((chips * CORES, TILE), jnp.int32)] if first else [],
+        compiler_params=pltpu.CompilerParams(vmem_limit_bytes=VMEM_BYTES),
+        cost_estimate=pl.CostEstimate(
+            flops=0, bytes_accessed=2 * chips * moved[0].size, transcendentals=0
+        ),
         name="settle",
-    )(*after, *([] if first else [meta]), moved)
+    )(*after, *([] if first else [meta]), *moved)
     return outs[:shares], (outs[shares] if first else meta)
 
 
@@ -298,44 +338,46 @@
         a_rows, w_rows = next_a, next_w
 
 
-def factor_kernel(tiles, rows_total, g_ref, r_ref, inv_ref, hi_ref, mid_ref, lo_ref, wide, a_ref, w_ref, u_ref, v_ref):
+def factor_step(tiles, b, wide, a_ref, w_ref, u_ref, v_ref):
     row = lax.broadcasted_iota(jnp.int32, (TILE, TILE), 0)
     lane = lax.broadcasted_iota(jnp.int32, (TILE, TILE), 1)
-    wide[...] = jnp.zeros_like(wide)
+    a_ref[...] = wide[b, b]
+    w_ref[...] = jnp.where(row == lane, 1.0, 0.0)
+    factor_tile(a_ref, w_ref, u_ref, v_ref)
+    inverse = v_ref[...]
+    wide[b, b] = jnp.where(row <= lane, u_ref[...], 0.0)
+    wide[b, tiles + b] = inverse
+    for j in range(1, tiles):
+        wide[b, b + j] = lax.dot(
+            inverse, wide[b, b + j], precision=HIGHEST, preferred_element_type=jnp.float32
+        )
+    for r in range(b + 1, tiles):
+        for c in list(range(r, tiles)) + list(range(tiles, tiles + b + 1)):
+            update = lax.dot_general(
+                wide[b, r],
+                wide[b, c],
+                ROWS_BY_ROWS,
+                precision=HIGHEST,
+                preferred_element_type=jnp.float32,
+            )
+            wide[r, c] = -update if c == tiles + b else wide[r, c] - update
+
+
+def first_kernel(tiles, rows_total, g_ref, wide, *scratch):
     at = 0
     for a in range(tiles):
         for b in range(a, tiles):
             wide[a, b] = g_ref[at] / rows_total
             at += 1
-
-    def step(b, _):
-        a_ref[...] = wide[b, b]
-        w_ref[...] = jnp.where(row == lane, 1.0, 0.0)
-        factor_tile(a_ref, w_ref, u_ref, v_ref)
-        inverse = v_ref[...]
-        wide[b, b] = jnp.where(row <= lane, u_ref[...], 0.0)
-        wide[b, tiles + b] = inverse
-        for j in range(1, tiles):
-            wide[b, b + j] = lax.dot(
-                inverse, wide[b, b + j], precision=HIGHEST, preferred_element_type=jnp.float32
-            )
-
-        def trail(r, _):
-            left = wide[b, r]
-            for j in range(1, tiles + 1):
-                wide[r, b + j] = wide[r, b + j] - lax.dot_general(
-                    left,
-                    wide[b, b + j],
-                    ROWS_BY_ROWS,
-                    precision=HIGHEST,
-                    preferred_element_type=jnp.float32,
-                )
-            return 0
-
-        lax.fori_loop(b + 1, tiles, trail, 0)
-        return 0
-
-    lax.fori_loop(0, tiles, step, 0)
+    factor_step(tiles, 0, wide, *scratch)
+
+
+def next_kernel(tiles, b, _, wide, *scratch):
+    factor_step(tiles, b, wide, *scratch)
+
+
+def last_kernel(tiles, wide, r_ref, inv_ref, hi_ref, mid_ref, lo_ref, *scratch):
+    factor_step(tiles, tiles - 1, wide, *scratch)
     zero = jnp.zeros((TILE, TILE), jnp.float32)
     mine = lax.axis_index("snap")
     for a in range(tiles):
@@ -352,33 +394,39 @@
             lo_ref[rows, lanes] = low.astype(jnp.bfloat16)
 
 
-def factor(blocks, tiles, rows_total, after):
-    full = tiles * TILE
-    tile = pltpu.VMEM((TILE, TILE), jnp.float32)
+def factor_call(kernel, out_shape, value, after, aliases, tiles):
+    many = isinstance(out_shape, tuple)
     return pl.pallas_call(
-        lambda *refs: factor_kernel(tiles, rows_total, *refs[len(after) :]),
-        out_shape=(
-            jax.ShapeDtypeStruct((full, full), jnp.float32),
-            jax.ShapeDtypeStruct((full, full), jnp.float32),
-            jax.ShapeDtypeStruct((full, full), jnp.bfloat16),
-            jax.ShapeDtypeStruct((full, full), jnp.bfloat16),
-            jax.ShapeDtypeStruct((full, full), jnp.bfloat16),
-        ),
+        lambda *refs: kernel(*refs[len(after) :]),
+        out_shape=out_shape,
         in_specs=[ANY] * len(after) + [VMEM],
-        out_specs=(VMEM,) * 5,
-        scratch_shapes=[
-            pltpu.VMEM((tiles, 2 * tiles, TILE, TILE), jnp.float32),
-            tile,
-            tile,
-            tile,
-            tile,
-        ],
+        out_specs=(VMEM,) * len(out_shape) if many else VMEM,
+        scratch_shapes=[pltpu.VMEM((TILE, TILE), jnp.float32)] * 4,
+        input_output_aliases={len(after): 0} if aliases else {},
         compiler_params=pltpu.CompilerParams(vmem_limit_bytes=VMEM_BYTES),
         cost_estimate=pl.CostEstimate(
-            flops=40 * 10**9, bytes_accessed=8 * full * full, transcendentals=full
+            flops=7 * 10**9, bytes_accessed=value.size * 4, transcendentals=TILE
         ),
         name="factor",
-    )(*after, blocks)
+    )(*after, value)
+
+
+def factor_steps(blocks, tiles, rows_total, after):
+    state = jax.ShapeDtypeStruct((tiles, 2 * tiles, TILE, TILE), jnp.float32)
+    full = jax.ShapeDtypeStruct((tiles * TILE, tiles * TILE), jnp.float32)
+    term = jax.ShapeDtypeStruct(full.shape, jnp.bfloat16)
+    value = factor_call(
+        lambda *refs: first_kernel(tiles, rows_total, *refs), state, blocks, after, False, tiles
+    )
+    for b in range(1, tiles - 1):
+        after = yield value
+        value = factor_call(
+            lambda *refs: next_kernel(tiles, b, *refs), state, value, after, True, tiles
+        )
+    after = yield value
+    yield factor_call(
+        lambda *refs: last_kernel(tiles, *refs), (full, full, term, term, term), value, after, False, tiles
+    )
 
 
 def basis_kernel(parts, shares, *refs):
@@ -425,7 +473,8 @@
 
 
 def slab_sum(value, slabs):
-    return lax.psum_scatter(value, "space", scatter_dimension=0, tiled=True)
+    pieces = lax.all_to_all(value, "space", split_axis=0, concat_axis=0, tiled=True)
+    return jnp.sum(pieces.reshape(slabs, -1, value.shape[-1]), axis=0)
 
 
 def share_sum(piece, shares):
@@ -450,38 +499,49 @@
     def parted(owned):
         return owned.reshape(slots, shares, parts, CELL_TILE, width)
 
-    def to_slabs(part):
-        return lax.all_to_all(part, "space", split_axis=0, concat_axis=0, tiled=True)
+    def merged(part):
+        return merge(part[0], swap(part[1], "space", 1), slabs // CORES)
+
+    def to_chips(joined):
+        return [joined[0]] + [swap(joined[m], "space", CORES * m) for m in range(1, len(joined))]
 
     def to_rows(pieces):
         return [pieces[0]] + [swap(pieces[r], "snap", r) for r in range(1, shares)]
 
     def place(meta, moved, after=()):
-        return settle(meta, moved, slabs, slots // slabs, per_slab, shares, after)
+        return settle(meta, moved, slots // slabs, per_slab, shares, after)
 
     sent_x = pack(patch_dest, parted(owned_x), slabs, per_slab, True)
-    moved_x = [to_slabs(part) for part in sent_x]
+    moved_x = [to_chips(merged(part)) for part in sent_x]
     pieces, meta = place(None, moved_x[0])
     x_cells = [to_rows(pieces)]
-    sent_y = pack(patch_dest, parted(owned_y), slabs, per_slab, False, [meta])
+    sent_y = pack(patch_dest, parted(owned_y), slabs, per_slab, False, x_cells[0][1:2])
+    joined_y = [merged(part) for part in sent_y]
     for moved in moved_x[1:]:
-        pieces, _ = place(meta, moved, x_cells[-1][1:] + [sent_y[0]])
+        pieces, _ = place(meta, moved, x_cells[-1][1:] + [joined_y[0][0]])
         x_cells.append(to_rows(pieces))
     gram_piece = slab_sum(gram_blocks(x_cells).reshape(pairs * TILE, TILE), slabs)
 
     y_cells, after = [], x_cells[-1][1:]
-    for part in sent_y:
-        pieces, _ = place(meta, to_slabs(part), after)
+    for joined in joined_y:
+        pieces, _ = place(meta, to_chips(joined), after)
         y_cells.append(to_rows(pieces))
         after = y_cells[-1][1:] + [gram_piece]
 
     gram = share_sum(gram_piece, shares)
-    r_factor, inverse, *terms = factor(
+    steps = factor_steps(
         gram.reshape(pairs, TILE, TILE), tiles, rows_total, [y_cells[-1][0]]
     )
+    state = next(steps)
+    cross_local = cross_sum(x_cells, y_cells, [state])
+    state = steps.send([cross_local])
+    cross_piece = slab_sum(cross_local, slabs)
+    for _ in range(tiles - 2):
+        state = steps.send([cross_piece])
+    cross = share_sum(cross_piece, shares)
+    r_factor, inverse, *terms = state
     q_basis = basis(x_cells, terms).reshape(per_slab, patch // shares, full)
 
-    cross = share_sum(slab_sum(cross_sum(x_cells, y_cells, [gram]), slabs), shares)
     projection = jnp.dot(inverse, cross, precision=HIGHEST) / math.sqrt(rows_total)
     return q_basis, r_factor, projection
 

time: 351 us -> 300 us (0.85)
  blocking collectives: 71.1 us -> 30.5 us
  starting transfers between devices: 38.5 us -> 64.3 us
  waiting for transfers between devices: 147 us -> 122 us
  local copies, waits for them, and re-layouts: 15.4 us -> 6.27 us
    reduce_scatter x2 -> x0, waiting for transfers between devices: 60.6 us -> none  [slab_sum(): return lax.psum_scatter(value, 'space', scatter_dimension=0, tiled=True)]
    ppermute x16 -> x32, waiting for transfers between devices: 69.9 us -> 119 us  [swap(): lax.ppermute(value, axis, [(i, i ^ mask) for i in range(lax.axis_size(axi...]
    all_to_all x2 -> x1, blocking collectives: 61.1 us -> 19.6 us  [slab_sum(): lax.all_to_all(value, 'space', split_axis=0, concat_axis=0, tiled=True)]
    ppermute x16 -> x32, starting transfers between devices: 30.2 us -> 59.9 us  [swap(): lax.ppermute(value, axis, [(i, i ^ mask) for i in range(lax.axis_size(axi...]
    all_to_all x2 -> x1, waiting for transfers between devices: 16.6 us -> 2.79 us  [slab_sum(): lax.all_to_all(value, 'space', split_axis=0, concat_axis=0, tiled=True)]
    unnamed x64 -> x66, local copies, waits for them, and re-layouts: 15.4 us -> 6.27 us
    all_to_all x2 -> x1, starting transfers between devices: 7.96 us -> 4.34 us  [slab_sum(): lax.all_to_all(value, 'space', split_axis=0, concat_axis=0, tiled=True)]
    pallas_call x5 -> x12, Pallas kernels: 36.7 us -> 33.8 us  [the longest x4 19.8 us: factor_call(): pl.pallas_call(lambda *refs: kernel(*refs[len(after):]), out_shape=out_sh...]
  transfers between devices with their start and end apart: 21 -> 34, of which waited for: 10 -> 17; matrix products, arithmetic and copies ran while one was open for 0% -> 0% of each run, Pallas kernels for 15% -> 17%
where the time goes in v5:
time: 300 us
  waiting for transfers between devices  122 us (41%)
  starting transfers between devices  64.3 us (21%)
  Pallas kernels  55.5 us (18%)
  blocking collectives  30.5 us (10%)
  between operations  14.5 us (5%)
  local copies, waits for them, and re-layouts  6.27 us (2%)
  matrix products  4.04 us (1%)
  other arithmetic  3.16 us (1%)
    ppermute x32, waiting for transfers between devices, swap(): lax.ppermute(value, axis, [(i, i ^ mask) for i in range(lax.axis_size(axi...  119 us
    ppermute x32, starting transfers between devices, swap(): lax.ppermute(value, axis, [(i, i ^ mask) for i in range(lax.axis_size(axi...  59.9 us
    pallas_call x4, Pallas kernels, factor_call(): pl.pallas_call(lambda *refs: kernel(*refs[len(after):]), out_shape=out_sh...  19.8 us
    all_to_all x1, blocking collectives, slab_sum(): lax.all_to_all(value, 'space', split_axis=0, concat_axis=0, tiled=True)  19.6 us
    pallas_call x4, Pallas kernels, settle(): pl.pallas_call(lambda *refs: settle_kernel(chips, capacity, first, *refs[...  11.6 us
    all_gather x1, blocking collectives, share_sum(): return lax.all_gather(piece, 'space', axis=0, tiled=True)  10.9 us
    pallas_call x1, Pallas kernels, basis(): pl.pallas_call(lambda *refs: basis_kernel(parts, shares, *refs), grid=(st...  9.91 us
    pallas_call x2, Pallas kernels, pack(): pl.pallas_call(lambda *refs: pack_kernel(slabs, capacity, per_slab, parts...  7.43 us
  transfers between devices with their start and end apart: 34, of which 17 were waited for; matrix products, arithmetic and copies ran while one was open for 0% of the time, Pallas kernels for 17%

profile of v5, /device:TPU:0, one launch (start us, length us, event | category | flops | bytes accessed | tf_op | source)
XLA Modules:
  0.0 300.4 jit_solution(946998525630893003)
XLA Ops:
  7.2 2.2 copy-done.1
  10.0 3.3 %pack.2 = (bf16[260,16,128]{2,1,0:T(8,128)(2,1)S(1)}, bf16[260,16,128]{2,1,0:T(8,128)(2,1)S(1)}, bf16[256,16,128]{2,1,0:T(8,128)(2,1)S(1)}, bf16[256,16,128]{2,1,0:T(8,128)(2,1)S(1)}) custom-call(s32[128]{0:T(128)S(1)} %copy-done.29, bf16[128,4,2,16,128]{4,3,2,1,0:T(8,128)(2,1)S(1)} %bitcast.10), custom_call_target="tpu_custom_call" | custom-call | bytes 8388608 | tf_op jit(solution)/shard_map/pack/pallas_call | solution.py:76
  13.4 2.7 collective-permute-done.other_ref
  16.2 1.8 collective-permute-start.1
  18.0 2.2 collective-permute-start.2
  20.6 10.6 %collective-permute-done.1.refs_1_ = bf16[130,16,128]{2,1,0:T(8,128)(2,1)S(1)} collective-permute-done((bf16[130,16,128]{2,1,0:T(8,128)(2,1)S(1)}, bf16[130,16,128]{2,1,0:T(8,128)(2,1)S(1)}, u32[]{:S(2)}, u32[]{:S(2)}) %collective-permute-start.1) | collective-permute-done | bytes 532512 | tf_op jit(solution)/shard_map/ppermute | solution.py:472
  31.2 12.0 %collective-permute-done.2.refs_2_ = bf16[130,16,128]{2,1,0:T(8,128)(2,1)S(1)} collective-permute-done((bf16[130,16,128]{2,1,0:T(8,128)(2,1)S(1)}, bf16[130,16,128]{2,1,0:T(8,128)(2,1)S(1)}, u32[]{:S(2)}, u32[]{:S(2)}) %collective-permute-start.2) | collective-permute-done | bytes 532512 | tf_op jit(solution)/shard_map/ppermute | solution.py:472
  43.2 1.1 collective-permute-done.3.refs_3_
  44.3 3.0 settle.4
  47.3 1.6 collective-permute-start.4
  49.0 6.2 %collective-permute-done.4.refs_0_.refs_1_.refs_2_ = bf16[64,16,128]{2,1,0:T(8,128)(2,1)S(1)} collective-permute-done((bf16[64,16,128]{2,1,0:T(8,128)(2,1)S(1)}, bf16[64,16,128]{2,1,0:T(8,128)(2,1)S(1)}, u32[]{:S(2)}, u32[]{:S(2)}) %collective-permute-start.4) | collective-permute-done | bytes 262176 | tf_op jit(solution)/shard_map/ppermute | solution.py:472
  55.2 4.2 %pack.3 = (bf16[256,16,128]{2,1,0:T(8,128)(2,1)S(1)}, bf16[256,16,128]{2,1,0:T(8,128)(2,1)S(1)}, bf16[256,16,128]{2,1,0:T(8,128)(2,1)S(1)}, bf16[256,16,128]{2,1,0:T(8,128)(2,1)}) custom-call(bf16[64,16,128]{2,1,0:T(8,128)(2,1)S(1)} %collective-permute-done.4.refs_0_.refs_1_.refs_2_, s32[128]{0:T(128)S(1)} %copy-done.30, ...), custom_call_target="tpu_custom_call" | custom-call | bytes 8388608 | tf_op jit(solution)/shard_map/pack/pallas_call | solution.py:76
  60.1 1.0 collective-permute-start.10
  61.1 2.1 collective-permute-start.11
  63.3 11.0 %collective-permute-done.9.refs_6_ = bf16[128,16,128]{2,1,0:T(8,128)(2,1)S(1)} collective-permute-done((bf16[128,16,128]{2,1,0:T(8,128)(2,1)S(1)}, bf16[128,16,128]{2,1,0:T(8,128)(2,1)S(1)}, u32[]{:S(2)}, u32[]{:S(2)}) %collective-permute-start.9) | collective-permute-done | bytes 524320 | tf_op jit(solution)/shard_map/ppermute | solution.py:472
  74.3 2.6 collective-permute-start.5
  76.9 1.3 collective-permute-start.6
  78.2 0.9 merge.5
  79.1 6.4 %collective-permute-done.11.refs_8_ = bf16[128,16,128]{2,1,0:T(8,128)(2,1)S(1)} collective-permute-done((bf16[128,16,128]{2,1,0:T(8,128)(2,1)S(1)}, bf16[128,16,128]{2,1,0:T(8,128)(2,1)S(1)}, u32[]{:S(2)}, u32[]{:S(2)}) %collective-permute-start.11) | collective-permute-done | bytes 524320 | tf_op jit(solution)/shard_map/ppermute | solution.py:472
  85.5 9.6 %collective-permute-done.5.refs_1_.refs_2_.refs_3_ = bf16[64,16,128]{2,1,0:T(8,128)(2,1)S(1)} collective-permute-done((bf16[64,16,128]{2,1,0:T(8,128)(2,1)S(1)}, bf16[64,16,128]{2,1,0:T(8,128)(2,1)S(1)}, u32[]{:S(2)}, u32[]{:S(2)}) %collective-permute-start.5) | collective-permute-done | bytes 262176 | tf_op jit(solution)/shard_map/ppermute | solution.py:472
  95.1 2.3 settle.5
  97.5 5.2 %collective-permute-start.12 = (bf16[64,16,128]{2,1,0:T(8,128)(2,1)S(1)}, bf16[64,16,128]{2,1,0:T(8,128)(2,1)S(1)}, u32[]{:S(2)}, u32[]{:S(2)}) collective-permute-start(bf16[64,16,128]{2,1,0:T(8,128)(2,1)S(1)} %get-tuple-element.70), channel_id=1, source_target_pairs={{0,1},{1,0},{2,3},{3,2},{4,5},{5,4},{6,7},{7,6},{8,9},{9,8},{10,11... | collective-permute-start | bytes 786440 | tf_op jit(solution)/shard_map/ppermute | solution.py:472
  102.7 2.0 collective-permute-start.13
  104.7 1.4 collective-permute-start.14
  106.5 8.0 %collective-permute-done.12.refs_0_.refs_5_.refs_6_ = bf16[64,16,128]{2,1,0:T(8,128)(2,1)S(1)} collective-permute-done((bf16[64,16,128]{2,1,0:T(8,128)(2,1)S(1)}, bf16[64,16,128]{2,1,0:T(8,128)(2,1)S(1)}, u32[]{:S(2)}, u32[]{:S(2)}) %collective-permute-start.12) | collective-permute-done | bytes 262176 | tf_op jit(solution)/shard_map/ppermute | solution.py:472
  114.6 9.5 %collective-permute-done.13.refs_1_.refs_6_.refs_7_ = bf16[64,16,128]{2,1,0:T(8,128)(2,1)S(1)} collective-permute-done((bf16[64,16,128]{2,1,0:T(8,128)(2,1)S(1)}, bf16[64,16,128]{2,1,0:T(8,128)(2,1)S(1)}, u32[]{:S(2)}, u32[]{:S(2)}) %collective-permute-start.13) | collective-permute-done | bytes 262176 | tf_op jit(solution)/shard_map/ppermute | solution.py:472
  124.0 2.1 gram_blocks.1
  127.0 0.8 copy-done.20
  127.8 4.3 %all-to-all-start = ((f32[8,160,128]{2,1,0:T(8,128)}), f32[8,160,128]{2,1,0:T(8,128)}, u32[]{:S(2)}, u32[]{:S(2)}) async-start(f32[8,160,128]{2,1,0:T(8,128)} %bitcast.11), calls=%async_computation | async-start | bytes 1310720 | tf_op jit(solution)/shard_map/all_to_all | solution.py:476
  132.2 1.9 collective-permute-start.16
  134.1 1.4 collective-permute-start.17
  135.5 1.2 merge.7
  136.8 0.8 copy-done.21
  137.9 1.8 collective-permute-start.23
  139.7 1.4 collective-permute-start.24
  141.1 2.8 all-to-all-done
  143.9 1.1 reduce_sum.18.refs_3_
  145.0 20.3 %collective-permute-done.16.refs_6_ = bf16[128,16,128]{2,1,0:T(8,128)(2,1)} collective-permute-done((bf16[128,16,128]{2,1,0:T(8,128)(2,1)}, bf16[128,16,128]{2,1,0:T(8,128)(2,1)}, u32[]{:S(2)}, u32[]{:S(2)}) %collective-permute-start.16) | collective-permute-done | bytes 524320 | tf_op jit(solution)/shard_map/ppermute | solution.py:472
  165.3 4.9 %collective-permute-start.25 = (f32[160,128]{1,0:T(8,128)S(1)}, f32[160,128]{1,0:T(8,128)S(1)}, u32[]{:S(2)}, u32[]{:S(2)}) collective-permute-start(f32[160,128]{1,0:T(8,128)S(1)} %reduce_sum.18.refs_3_), channel_id=1, source_target_pairs={{0,1},{1,0},{2,3},{3,2},{4,5},{5,4},{6,7},{7,6},{8,9},{9,8},{10,11... | collective-permute-start | bytes 245768 | tf_op jit(solution)/shard_map/ppermute | solution.py:472
  170.3 0.9 copy-done.17
  171.3 3.2 %settle.6 = (bf16[64,16,128]{2,1,0:T(8,128)(2,1)S(1)}, bf16[64,16,128]{2,1,0:T(8,128)(2,1)S(1)}, bf16[64,16,128]{2,1,0:T(8,128)(2,1)S(1)}, bf16[64,16,128]{2,1,0:T(8,128)(2,1)S(1)}) custom-call(bf16[64,16,128]{2,1,0:T(8,128)(2,1)S(1)} %copy-done.9, bf16[64,16,128]{2,1,0:T(8,128)(2,1)S(1)} %copy-done.13, bf16[64,16,128]{2,1,0:T(8,128)(2,1)S(1)} %copy-done.17, ...), custom_call_target="tpu_custom_call" | custom-call | bytes 2097152 | tf_op jit(solution)/shard_map/settle/pallas_call | solution.py:152
  174.5 3.9 %collective-permute-start.19 = (bf16[64,16,128]{2,1,0:T(8,128)(2,1)S(1)}, bf16[64,16,128]{2,1,0:T(8,128)(2,1)S(1)}, u32[]{:S(2)}, u32[]{:S(2)}) collective-permute-start(bf16[64,16,128]{2,1,0:T(8,128)(2,1)S(1)} %get-tuple-element.77), channel_id=1, source_target_pairs={{0,2},{1,3},{2,0},{3,1},{4,6},{5,7},{6,4},{7,5},{8,10},{9,11},{10,... | collective-permute-start | bytes 786440 | tf_op jit(solution)/shard_map/ppermute | solution.py:472
  178.9 8.4 %collective-permute-done.23.refs_7_ = bf16[128,16,128]{2,1,0:T(8,128)(2,1)} collective-permute-done((bf16[128,16,128]{2,1,0:T(8,128)(2,1)}, bf16[128,16,128]{2,1,0:T(8,128)(2,1)}, u32[]{:S(2)}, u32[]{:S(2)}) %collective-permute-start.23) | collective-permute-done | bytes 524320 | tf_op jit(solution)/shard_map/ppermute | solution.py:472
  187.3 6.9 %collective-permute-start.26 = (f32[160,128]{1,0:T(8,128)S(1)}, f32[160,128]{1,0:T(8,128)S(1)}, u32[]{:S(2)}, u32[]{:S(2)}) collective-permute-start(f32[160,128]{1,0:T(8,128)S(1)} %add.12), channel_id=1, source_target_pairs={{0,2},{1,3},{2,0},{3,1},{4,6},{5,7},{6,4},{7,5},{8,10},{9,11},{10,... | collective-permute-start | bytes 245768 | tf_op jit(solution)/shard_map/ppermute | solution.py:472
  194.2 4.4 %collective-permute-done.19.refs_1_.refs_11_ = bf16[64,16,128]{2,1,0:T(8,128)(2,1)S(1)} collective-permute-done((bf16[64,16,128]{2,1,0:T(8,128)(2,1)S(1)}, bf16[64,16,128]{2,1,0:T(8,128)(2,1)S(1)}, u32[]{:S(2)}, u32[]{:S(2)}) %collective-permute-start.19) | collective-permute-done | bytes 262176 | tf_op jit(solution)/shard_map/ppermute | solution.py:472
  198.7 3.1 %settle.7 = (bf16[64,16,128]{2,1,0:T(8,128)(2,1)S(1)}, bf16[64,16,128]{2,1,0:T(8,128)(2,1)S(1)}, bf16[64,16,128]{2,1,0:T(8,128)(2,1)S(1)}, bf16[64,16,128]{2,1,0:T(8,128)(2,1)S(1)}) custom-call(bf16[64,16,128]{2,1,0:T(8,128)(2,1)S(1)} %collective-permute-done.18.refs_0_.refs_10_, bf16[64,16,128]{2,1,0:T(8,128)(2,1)S(1)} %collective-permute-done.19.refs_1_.refs_11_, ...), custom_call_target="tpu_custom_call" | custom-call | bytes 2097152 | tf_op jit(solution)/shard_map/settle/pallas_call | solution.py:152
  201.8 5.0 %collective-permute-start.27 = (bf16[64,16,128]{2,1,0:T(8,128)(2,1)S(1)}, bf16[64,16,128]{2,1,0:T(8,128)(2,1)S(1)}, u32[]{:S(2)}, u32[]{:S(2)}) collective-permute-start(bf16[64,16,128]{2,1,0:T(8,128)(2,1)S(1)} %get-tuple-element.87), channel_id=1, source_target_pairs={{0,1},{1,0},{2,3},{3,2},{4,5},{5,4},{6,7},{7,6},{8,9},{9,8},{10,11... | collective-permute-start | bytes 786440 | tf_op jit(solution)/shard_map/ppermute | solution.py:472
  206.8 1.1 collective-permute-start.28
  207.9 1.4 collective-permute-start.29
  209.3 10.9 %all_gather.6 = f32[1280,128]{1,0:T(8,128)S(1)} all-gather(f32[160,128]{1,0:T(8,128)S(1)} %add.13), channel_id=1, replica_groups=mesh['space'=8,'snap'=4] {'space'}, dimensions={0}, use_global_device_ids=true | all-gather | bytes 737280 | tf_op jit(solution)/shard_map/all_gather | solution.py:485
  220.2 5.0 %factor.4.refs_0_.refs_1_ = f32[4,8,128,128]{3,2,1,0:T(8,128)S(1)} custom-call(bf16[64,16,128]{2,1,0:T(8,128)(2,1)S(1)} %get-tuple-element.85.refs_0_.refs_13_, f32[10,128,128]{2,1,0:T(8,128)S(1)} %bitcast.12), custom_call_target="tpu_custom_call" | custom-call | flops 7000000000 | bytes 655360 | tf_op jit(solution)/shard_map/factor/pallas_call | solution.py:399
  225.2 1.7 collective-permute-done.28.refs_15_
  226.9 2.2 cross_sum.1.refs_0_
  229.1 19.6 %all_to_all.18 = f32[8,64,512]{2,1,0:T(8,128)} all-to-all(f32[8,64,512]{2,1,0:T(8,128)S(1)} %bitcast.8), channel_id=1, replica_groups=mesh['space'=8,'snap'=4] {'space'}, dimensions={0} | all-to-all | bytes 2097152 | tf_op jit(solution)/shard_map/all_to_all | solution.py:476
  248.7 1.3 reduce_sum.19.refs_0_
  250.0 3.4 %collective-permute-start.30 = (f32[64,512]{1,0:T(8,128)S(1)}, f32[64,512]{1,0:T(8,128)S(1)}, u32[]{:S(2)}, u32[]{:S(2)}) collective-permute-start(f32[64,512]{1,0:T(8,128)S(1)} %reduce_sum.19.refs_0_), channel_id=1, source_target_pairs={{0,1},{1,0},{2,3},{3,2},{4,5},{5,4},{6,7},{7,6},{8,9},{9,8},{10,11... | collective-permute-start | bytes 393224 | tf_op jit(solution)/shard_map/ppermute | solution.py:472
  253.4 2.9 collective-permute-done.30
  256.4 3.1 %collective-permute-start.31 = (f32[64,512]{1,0:T(8,128)S(1)}, f32[64,512]{1,0:T(8,128)S(1)}, u32[]{:S(2)}, u32[]{:S(2)}) collective-permute-start(f32[64,512]{1,0:T(8,128)S(1)} %add.14), channel_id=1, source_target_pairs={{0,2},{1,3},{2,0},{3,1},{4,6},{5,7},{6,4},{7,5},{8,10},{9,11},{10,... | collective-permute-start | bytes 393224 | tf_op jit(solution)/shard_map/ppermute | solution.py:472
  259.5 4.5 %collective-permute-done.31 = f32[64,512]{1,0:T(8,128)S(1)} collective-permute-done((f32[64,512]{1,0:T(8,128)S(1)}, f32[64,512]{1,0:T(8,128)S(1)}, u32[]{:S(2)}, u32[]{:S(2)}) %collective-permute-start.31) | collective-permute-done | bytes 131104 | tf_op jit(solution)/shard_map/ppermute | solution.py:472
  264.7 4.8 %factor.5.refs_1_ = f32[4,8,128,128]{3,2,1,0:T(8,128)S(1)} custom-call(f32[512,512]{1,0:T(8,128)S(1)} %cross_sum.1.refs_0_, f32[4,8,128,128]{3,2,1,0:T(8,128)S(1)} %factor.4.refs_0_.refs_1_), custom_call_target="tpu_custom_call", output_to_operand_aliasing={{}: (1, {})} | custom-call | flops 7000000000 | bytes 2097152 | tf_op jit(solution)/shard_map/factor/pallas_call | solution.py:399
  269.5 4.6 %factor.6.refs_1_ = f32[4,8,128,128]{3,2,1,0:T(8,128)S(1)} custom-call(f32[64,512]{1,0:T(8,128)S(1)} %reduce_sum.19.refs_0_, f32[4,8,128,128]{3,2,1,0:T(8,128)S(1)} %factor.5.refs_1_), custom_call_target="tpu_custom_call", output_to_operand_aliasing={{}: (1, {})} | custom-call | flops 7000000000 | bytes 2097152 | tf_op jit(solution)/shard_map/factor/pallas_call | solution.py:399
  274.1 5.4 %factor.7 = (f32[512,512]{1,0:T(8,128)}, f32[512,512]{1,0:T(8,128)S(1)}, bf16[512,512]{1,0:T(8,128)(2,1)S(1)}, bf16[512,512]{1,0:T(8,128)(2,1)S(1)}, bf16[512,512]{1,0:T(8,128)(2,1)S(1)}) custom-call(f32[64,512]{1,0:T(8,128)S(1)} %reduce_sum.19.refs_0_, f32[4,8,128,128]{3,2,1,0:T(8,128)S(1)} %factor.6.refs_1_), custom_call_target="tpu_custom_call" | custom-call | flops 7000000000 | bytes 2097152 | tf_op jit(solution)/shard_map/factor/pallas_call | solution.py:399
  279.6 9.9 %basis.1 = f32[64,2,16,512]{3,2,1,0:T(8,128)} custom-call(bf16[64,16,128]{2,1,0:T(8,128)(2,1)S(1)} %copy-done.25, bf16[64,16,128]{2,1,0:T(8,128)(2,1)S(1)} %collective-permute-done.4.refs_0_.refs_1_.refs_2_, bf16[64,16,128]{2,1,0:T(8,128)(2,1)S(1)} %copy-done.4, bf16[64,16,128]{2,1,0:T(8,128)(2,1)S(1)} %copy-done.7, bf16[64,16,128]{2,1,0:T(8,128)(2,1)S(1)} %copy-done.28, ...), custom_call_target="tpu_custom_call" | custom-call | flops 3221225472 | bytes 6291456 | tf_op jit(solution)/shard_map/basis/pallas_call | solution.py:455
  289.5 4.0 %convolution_multiply_fusion = f32[512,512]{1,0:T(8,128)} fusion(f32[512,512]{1,0:T(8,128)S(1)} %get-tuple-element.94, f32[512,512]{1,0:T(8,128)} %all-gather.2.cloned.1.call-done), kind=kOutput, calls=%fused_computation | convolution fusion | flops 1610874880 | bytes 3145728 | tf_op jit(solution)/shard_map/dot_general | solution.py:545
  (97 shorter events, 4.9 us)
Async XLA Ops:
  7.2 2.2 copy-start.1
  13.3 2.7 collective-permute-start
  16.0 39.1 %copy-start = (bf16[128,128,128]{2,1,0:T(8,128)(2,1)S(1)}, bf16[128,128,128]{2,1,0:T(8,128)(2,1)}, u32[]{:S(2)}) copy-start(bf16[128,128,128]{2,1,0:T(8,128)(2,1)} %param.4) | copy-start | bytes 12582916
  16.0 39.1 %copy-start.30 = (s32[128]{0:T(128)S(1)}, s32[128]{0:T(128)}, u32[]{:S(2)}) copy-start(s32[128]{0:T(128)} %refs_1_.1) | copy-start | bytes 1540
  16.2 15.0 %collective-permute-start.1 = (bf16[130,16,128]{2,1,0:T(8,128)(2,1)S(1)}, bf16[130,16,128]{2,1,0:T(8,128)(2,1)S(1)}, u32[]{:S(2)}, u32[]{:S(2)}) collective-permute-start(bf16[130,16,128]{2,1,0:T(8,128)(2,1)S(1)} %get-tuple-element.52), channel_id=1, source_target_pairs={{0,8},{4,12},{8,0},{12,4},{16,24},{20,28},{24,16},{28,20},{1,9},{5... | collective-permute-start | bytes 1597448 | tf_op jit(solution)/shard_map/ppermute | solution.py:472
  18.0 25.3 %collective-permute-start.2 = (bf16[130,16,128]{2,1,0:T(8,128)(2,1)S(1)}, bf16[130,16,128]{2,1,0:T(8,128)(2,1)S(1)}, u32[]{:S(2)}, u32[]{:S(2)}) collective-permute-start(bf16[130,16,128]{2,1,0:T(8,128)(2,1)S(1)} %get-tuple-element.53), channel_id=1, source_target_pairs={{0,16},{4,20},{8,24},{12,28},{16,0},{20,4},{24,8},{28,12},{1,17},{... | collective-permute-start | bytes 1597448 | tf_op jit(solution)/shard_map/ppermute | solution.py:472
  20.2 24.1 %collective-permute-start.3 = (bf16[130,16,128]{2,1,0:T(8,128)(2,1)S(1)}, bf16[130,16,128]{2,1,0:T(8,128)(2,1)S(1)}, u32[]{:S(2)}, u32[]{:S(2)}) collective-permute-start(bf16[130,16,128]{2,1,0:T(8,128)(2,1)S(1)} %get-tuple-element.54), channel_id=1, source_target_pairs={{0,24},{4,28},{8,16},{12,20},{16,8},{20,12},{24,0},{28,4},{1,25},{... | collective-permute-start | bytes 1597448 | tf_op jit(solution)/shard_map/ppermute | solution.py:472
  20.6 38.8 %collective-permute-start.8 = (bf16[256,16,128]{2,1,0:T(8,128)(2,1)S(1)}, bf16[256,16,128]{2,1,0:T(8,128)(2,1)S(1)}, u32[]{:S(2)}, u32[]{:S(2)}) collective-permute-start(bf16[256,16,128]{2,1,0:T(8,128)(2,1)S(1)} %get-tuple-element.64), channel_id=1, source_target_pairs={{0,4},{4,0},{8,12},{12,8},{16,20},{20,16},{24,28},{28,24},{1,5},{5... | collective-permute-start | bytes 3145736 | tf_op jit(solution)/shard_map/ppermute | solution.py:472
  47.3 76.7 %copy-start.23 = (bf16[64,16,128]{2,1,0:T(8,128)(2,1)}, bf16[64,16,128]{2,1,0:T(8,128)(2,1)S(1)}, u32[]{:S(2)}) copy-start(bf16[64,16,128]{2,1,0:T(8,128)(2,1)S(1)} %get-tuple-element.55.refs_0_.refs_1_) | copy-start | bytes 786436
  47.3 7.8 %collective-permute-start.4 = (bf16[64,16,128]{2,1,0:T(8,128)(2,1)S(1)}, bf16[64,16,128]{2,1,0:T(8,128)(2,1)S(1)}, u32[]{:S(2)}, u32[]{:S(2)}) collective-permute-start(bf16[64,16,128]{2,1,0:T(8,128)(2,1)S(1)} %get-tuple-element.56), channel_id=1, source_target_pairs={{0,1},{1,0},{2,3},{3,2},{4,5},{5,4},{6,7},{7,6},{8,9},{9,8},{10,11... | collective-permute-start | bytes 786440 | tf_op jit(solution)/shard_map/ppermute | solution.py:472
  59.3 17.5 %collective-permute-start.7 = (bf16[256,16,128]{2,1,0:T(8,128)(2,1)S(1)}, bf16[256,16,128]{2,1,0:T(8,128)(2,1)S(1)}, u32[]{:S(2)}, u32[]{:S(2)}) collective-permute-start(bf16[256,16,128]{2,1,0:T(8,128)(2,1)S(1)} %get-tuple-element.60), channel_id=1, source_target_pairs={{0,4},{4,0},{8,12},{12,8},{16,20},{20,16},{24,28},{28,24},{1,5},{5... | collective-permute-start | bytes 3145736 | tf_op jit(solution)/shard_map/ppermute | solution.py:472
  59.5 14.8 %collective-permute-start.9 = (bf16[128,16,128]{2,1,0:T(8,128)(2,1)S(1)}, bf16[128,16,128]{2,1,0:T(8,128)(2,1)S(1)}, u32[]{:S(2)}, u32[]{:S(2)}) collective-permute-start(bf16[128,16,128]{2,1,0:T(8,128)(2,1)S(1)} %get-tuple-element.66), channel_id=1, source_target_pairs={{0,8},{4,12},{8,0},{12,4},{16,24},{20,28},{24,16},{28,20},{1,9},{5... | collective-permute-start | bytes 1572872 | tf_op jit(solution)/shard_map/ppermute | solution.py:472
  59.6 76.0 %collective-permute-start.21 = (bf16[256,16,128]{2,1,0:T(8,128)(2,1)}, bf16[256,16,128]{2,1,0:T(8,128)(2,1)S(1)}, u32[]{:S(2)}, u32[]{:S(2)}) collective-permute-start(bf16[256,16,128]{2,1,0:T(8,128)(2,1)} %get-tuple-element.80), channel_id=1, source_target_pairs={{0,4},{4,0},{8,12},{12,8},{16,20},{20,16},{24,28},{28,24},{1,5},{5... | collective-permute-start | bytes 3145736 | tf_op jit(solution)/shard_map/ppermute | solution.py:472
  60.1 19.0 %collective-permute-start.10 = (bf16[128,16,128]{2,1,0:T(8,128)(2,1)S(1)}, bf16[128,16,128]{2,1,0:T(8,128)(2,1)S(1)}, u32[]{:S(2)}, u32[]{:S(2)}) collective-permute-start(bf16[128,16,128]{2,1,0:T(8,128)(2,1)S(1)} %get-tuple-element.67), channel_id=1, source_target_pairs={{0,16},{4,20},{8,24},{12,28},{16,0},{20,4},{24,8},{28,12},{1,17},{... | collective-permute-start | bytes 1572872 | tf_op jit(solution)/shard_map/ppermute | solution.py:472
  61.1 24.4 %collective-permute-start.11 = (bf16[128,16,128]{2,1,0:T(8,128)(2,1)S(1)}, bf16[128,16,128]{2,1,0:T(8,128)(2,1)S(1)}, u32[]{:S(2)}, u32[]{:S(2)}) collective-permute-start(bf16[128,16,128]{2,1,0:T(8,128)(2,1)S(1)} %get-tuple-element.68), channel_id=1, source_target_pairs={{0,24},{4,28},{8,16},{12,20},{16,8},{20,12},{24,0},{28,4},{1,25},{... | collective-permute-start | bytes 1572872 | tf_op jit(solution)/shard_map/ppermute | solution.py:472
  74.3 20.9 %collective-permute-start.5 = (bf16[64,16,128]{2,1,0:T(8,128)(2,1)S(1)}, bf16[64,16,128]{2,1,0:T(8,128)(2,1)S(1)}, u32[]{:S(2)}, u32[]{:S(2)}) collective-permute-start(bf16[64,16,128]{2,1,0:T(8,128)(2,1)S(1)} %get-tuple-element.57), channel_id=1, source_target_pairs={{0,2},{1,3},{2,0},{3,1},{4,6},{5,7},{6,4},{7,5},{8,10},{9,11},{10,... | collective-permute-start | bytes 786440 | tf_op jit(solution)/shard_map/ppermute | solution.py:472
  76.9 18.3 %collective-permute-start.6 = (bf16[64,16,128]{2,1,0:T(8,128)(2,1)S(1)}, bf16[64,16,128]{2,1,0:T(8,128)(2,1)S(1)}, u32[]{:S(2)}, u32[]{:S(2)}) collective-permute-start(bf16[64,16,128]{2,1,0:T(8,128)(2,1)S(1)} %get-tuple-element.58), channel_id=1, source_target_pairs={{0,3},{1,2},{2,1},{3,0},{4,7},{5,6},{6,5},{7,4},{8,11},{9,10},{10,... | collective-permute-start | bytes 786440 | tf_op jit(solution)/shard_map/ppermute | solution.py:472
  79.1 47.0 %copy-start.31 = (bf16[128,16,128]{2,1,0:T(8,128)(2,1)}, bf16[128,16,128]{2,1,0:T(8,128)(2,1)S(1)}, u32[]{:S(2)}) copy-start(bf16[128,16,128]{2,1,0:T(8,128)(2,1)S(1)} %get-tuple-element.75) | copy-start | bytes 1572868
  79.1 47.0 %copy-start.32 = (bf16[128,16,128]{2,1,0:T(8,128)(2,1)}, bf16[128,16,128]{2,1,0:T(8,128)(2,1)S(1)}, u32[]{:S(2)}) copy-start(bf16[128,16,128]{2,1,0:T(8,128)(2,1)S(1)} %get-tuple-element.74) | copy-start | bytes 1572868
  95.1 31.1 %copy-start.2 = (bf16[64,16,128]{2,1,0:T(8,128)(2,1)}, bf16[64,16,128]{2,1,0:T(8,128)(2,1)S(1)}, u32[]{:S(2)}) copy-start(bf16[64,16,128]{2,1,0:T(8,128)(2,1)S(1)} %collective-permute-done.5.refs_1_.refs_2_.refs_3_) | copy-start | bytes 786436
  95.1 31.1 %copy-start.5 = (bf16[64,16,128]{2,1,0:T(8,128)(2,1)}, bf16[64,16,128]{2,1,0:T(8,128)(2,1)S(1)}, u32[]{:S(2)}) copy-start(bf16[64,16,128]{2,1,0:T(8,128)(2,1)S(1)} %collective-permute-done.6.refs_2_.refs_3_.refs_4_) | copy-start | bytes 786436
  97.5 28.7 %copy-start.26 = (bf16[64,16,128]{2,1,0:T(8,128)(2,1)}, bf16[64,16,128]{2,1,0:T(8,128)(2,1)S(1)}, u32[]{:S(2)}) copy-start(bf16[64,16,128]{2,1,0:T(8,128)(2,1)S(1)} %get-tuple-element.69.refs_4_.refs_5_) | copy-start | bytes 786436
  97.5 17.1 %collective-permute-start.12 = (bf16[64,16,128]{2,1,0:T(8,128)(2,1)S(1)}, bf16[64,16,128]{2,1,0:T(8,128)(2,1)S(1)}, u32[]{:S(2)}, u32[]{:S(2)}) collective-permute-start(bf16[64,16,128]{2,1,0:T(8,128)(2,1)S(1)} %get-tuple-element.70), channel_id=1, source_target_pairs={{0,1},{1,0},{2,3},{3,2},{4,5},{5,4},{6,7},{7,6},{8,9},{9,8},{10,11... | collective-permute-start | bytes 786440 | tf_op jit(solution)/shard_map/ppermute | solution.py:472
  102.7 21.3 %collective-permute-start.13 = (bf16[64,16,128]{2,1,0:T(8,128)(2,1)S(1)}, bf16[64,16,128]{2,1,0:T(8,128)(2,1)S(1)}, u32[]{:S(2)}, u32[]{:S(2)}) collective-permute-start(bf16[64,16,128]{2,1,0:T(8,128)(2,1)S(1)} %get-tuple-element.71), channel_id=1, source_target_pairs={{0,2},{1,3},{2,0},{3,1},{4,6},{5,7},{6,4},{7,5},{8,10},{9,11},{10,... | collective-permute-start | bytes 786440 | tf_op jit(solution)/shard_map/ppermute | solution.py:472
  104.7 19.4 %collective-permute-start.14 = (bf16[64,16,128]{2,1,0:T(8,128)(2,1)S(1)}, bf16[64,16,128]{2,1,0:T(8,128)(2,1)S(1)}, u32[]{:S(2)}, u32[]{:S(2)}) collective-permute-start(bf16[64,16,128]{2,1,0:T(8,128)(2,1)S(1)} %get-tuple-element.72), channel_id=1, source_target_pairs={{0,3},{1,2},{2,1},{3,0},{4,7},{5,6},{6,5},{7,4},{8,11},{9,10},{10,... | collective-permute-start | bytes 786440 | tf_op jit(solution)/shard_map/ppermute | solution.py:472
  106.1 33.6 %collective-permute-start.15 = (bf16[128,16,128]{2,1,0:T(8,128)(2,1)}, bf16[128,16,128]{2,1,0:T(8,128)(2,1)}, u32[]{:S(2)}, u32[]{:S(2)}) collective-permute-start(bf16[128,16,128]{2,1,0:T(8,128)(2,1)} %get-tuple-element.73), channel_id=1, source_target_pairs={{0,8},{4,12},{8,0},{12,4},{16,24},{20,28},{24,16},{28,20},{1,9},{5... | collective-permute-start | bytes 1572872 | tf_op jit(solution)/shard_map/ppermute | solution.py:472
  124.0 2.2 copy-start.12
  124.0 2.2 copy-start.16
  127.0 0.8 copy-start.20
  127.8 42.5 %copy-start.9 = (bf16[64,16,128]{2,1,0:T(8,128)(2,1)S(1)}, bf16[64,16,128]{2,1,0:T(8,128)(2,1)}, u32[]{:S(2)}) copy-start(bf16[64,16,128]{2,1,0:T(8,128)(2,1)} %copy-done.8) | copy-start | bytes 786436
  127.8 42.5 %copy-start.13 = (bf16[64,16,128]{2,1,0:T(8,128)(2,1)S(1)}, bf16[64,16,128]{2,1,0:T(8,128)(2,1)}, u32[]{:S(2)}) copy-start(bf16[64,16,128]{2,1,0:T(8,128)(2,1)} %copy-done.12) | copy-start | bytes 786436
  127.8 16.1 %all-to-all-start = ((f32[8,160,128]{2,1,0:T(8,128)}), f32[8,160,128]{2,1,0:T(8,128)}, u32[]{:S(2)}, u32[]{:S(2)}) async-start(f32[8,160,128]{2,1,0:T(8,128)} %bitcast.11), calls=%async_computation | async-start | bytes 1310720 | tf_op jit(solution)/shard_map/all_to_all | solution.py:476
  132.2 157.3 %all-gather.2.cloned.1.call-start = ((), (), s32[]{:S(2)}) async-start(), calls=%async_computation.2 | async-start | bytes 1179648 | tf_op jit(solution)/shard_map/all_gather | solution.py:485
  132.2 33.1 %collective-permute-start.16 = (bf16[128,16,128]{2,1,0:T(8,128)(2,1)}, bf16[128,16,128]{2,1,0:T(8,128)(2,1)}, u32[]{:S(2)}, u32[]{:S(2)}) collective-permute-start(bf16[128,16,128]{2,1,0:T(8,128)(2,1)} %copy-done.32), channel_id=1, source_target_pairs={{0,16},{4,20},{8,24},{12,28},{16,0},{20,4},{24,8},{28,12},{1,17},{... | collective-permute-start | bytes 1572872 | tf_op jit(solution)/shard_map/ppermute | solution.py:472
  134.1 36.2 %collective-permute-start.17 = (bf16[128,16,128]{2,1,0:T(8,128)(2,1)}, bf16[128,16,128]{2,1,0:T(8,128)(2,1)}, u32[]{:S(2)}, u32[]{:S(2)}) collective-permute-start(bf16[128,16,128]{2,1,0:T(8,128)(2,1)} %copy-done.31), channel_id=1, source_target_pairs={{0,24},{4,28},{8,16},{12,20},{16,8},{20,12},{24,0},{28,4},{1,25},{... | collective-permute-start | bytes 1572872 | tf_op jit(solution)/shard_map/ppermute | solution.py:472
  137.6 36.9 %collective-permute-start.22 = (bf16[128,16,128]{2,1,0:T(8,128)(2,1)}, bf16[128,16,128]{2,1,0:T(8,128)(2,1)}, u32[]{:S(2)}, u32[]{:S(2)}) collective-permute-start(bf16[128,16,128]{2,1,0:T(8,128)(2,1)} %get-tuple-element.82), channel_id=1, source_target_pairs={{0,8},{4,12},{8,0},{12,4},{16,24},{20,28},{24,16},{28,20},{1,9},{5... | collective-permute-start | bytes 1572872 | tf_op jit(solution)/shard_map/ppermute | solution.py:472
  137.9 49.5 %collective-permute-start.23 = (bf16[128,16,128]{2,1,0:T(8,128)(2,1)}, bf16[128,16,128]{2,1,0:T(8,128)(2,1)}, u32[]{:S(2)}, u32[]{:S(2)}) collective-permute-start(bf16[128,16,128]{2,1,0:T(8,128)(2,1)} %get-tuple-element.83), channel_id=1, source_target_pairs={{0,16},{4,20},{8,24},{12,28},{16,0},{20,4},{24,8},{28,12},{1,17},{... | collective-permute-start | bytes 1572872 | tf_op jit(solution)/shard_map/ppermute | solution.py:472
  139.7 54.6 %collective-permute-start.24 = (bf16[128,16,128]{2,1,0:T(8,128)(2,1)}, bf16[128,16,128]{2,1,0:T(8,128)(2,1)}, u32[]{:S(2)}, u32[]{:S(2)}) collective-permute-start(bf16[128,16,128]{2,1,0:T(8,128)(2,1)} %get-tuple-element.84), channel_id=1, source_target_pairs={{0,24},{4,28},{8,16},{12,20},{16,8},{20,12},{24,0},{28,4},{1,25},{... | collective-permute-start | bytes 1572872 | tf_op jit(solution)/shard_map/ppermute | solution.py:472
  165.3 13.1 %collective-permute-start.25 = (f32[160,128]{1,0:T(8,128)S(1)}, f32[160,128]{1,0:T(8,128)S(1)}, u32[]{:S(2)}, u32[]{:S(2)}) collective-permute-start(f32[160,128]{1,0:T(8,128)S(1)} %reduce_sum.18.refs_3_), channel_id=1, source_target_pairs={{0,1},{1,0},{2,3},{3,2},{4,5},{5,4},{6,7},{7,6},{8,9},{9,8},{10,11... | collective-permute-start | bytes 245768 | tf_op jit(solution)/shard_map/ppermute | solution.py:472
  170.3 1.0 copy-start.17
  171.3 27.4 %copy-start.22 = (bf16[128,16,128]{2,1,0:T(8,128)(2,1)S(1)}, bf16[128,16,128]{2,1,0:T(8,128)(2,1)}, u32[]{:S(2)}) copy-start(bf16[128,16,128]{2,1,0:T(8,128)(2,1)} %copy-done.21) | copy-start | bytes 1572868
  174.4 19.8 %collective-permute-start.18 = (bf16[64,16,128]{2,1,0:T(8,128)(2,1)S(1)}, bf16[64,16,128]{2,1,0:T(8,128)(2,1)S(1)}, u32[]{:S(2)}, u32[]{:S(2)}) collective-permute-start(bf16[64,16,128]{2,1,0:T(8,128)(2,1)S(1)} %get-tuple-element.76), channel_id=1, source_target_pairs={{0,1},{1,0},{2,3},{3,2},{4,5},{5,4},{6,7},{7,6},{8,9},{9,8},{10,11... | collective-permute-start | bytes 786440 | tf_op jit(solution)/shard_map/ppermute | solution.py:472
  174.5 24.1 %collective-permute-start.19 = (bf16[64,16,128]{2,1,0:T(8,128)(2,1)S(1)}, bf16[64,16,128]{2,1,0:T(8,128)(2,1)S(1)}, u32[]{:S(2)}, u32[]{:S(2)}) collective-permute-start(bf16[64,16,128]{2,1,0:T(8,128)(2,1)S(1)} %get-tuple-element.77), channel_id=1, source_target_pairs={{0,2},{1,3},{2,0},{3,1},{4,6},{5,7},{6,4},{7,5},{8,10},{9,11},{10,... | collective-permute-start | bytes 786440 | tf_op jit(solution)/shard_map/ppermute | solution.py:472
  178.5 20.2 %collective-permute-start.20 = (bf16[64,16,128]{2,1,0:T(8,128)(2,1)S(1)}, bf16[64,16,128]{2,1,0:T(8,128)(2,1)S(1)}, u32[]{:S(2)}, u32[]{:S(2)}) collective-permute-start(bf16[64,16,128]{2,1,0:T(8,128)(2,1)S(1)} %get-tuple-element.78), channel_id=1, source_target_pairs={{0,3},{1,2},{2,1},{3,0},{4,7},{5,6},{6,5},{7,4},{8,11},{9,10},{10,... | collective-permute-start | bytes 786440 | tf_op jit(solution)/shard_map/ppermute | solution.py:472
  187.3 21.9 %collective-permute-start.26 = (f32[160,128]{1,0:T(8,128)S(1)}, f32[160,128]{1,0:T(8,128)S(1)}, u32[]{:S(2)}, u32[]{:S(2)}) collective-permute-start(f32[160,128]{1,0:T(8,128)S(1)} %add.12), channel_id=1, source_target_pairs={{0,2},{1,3},{2,0},{3,1},{4,6},{5,7},{6,4},{7,5},{8,10},{9,11},{10,... | collective-permute-start | bytes 245768 | tf_op jit(solution)/shard_map/ppermute | solution.py:472
  201.8 23.4 %collective-permute-start.27 = (bf16[64,16,128]{2,1,0:T(8,128)(2,1)S(1)}, bf16[64,16,128]{2,1,0:T(8,128)(2,1)S(1)}, u32[]{:S(2)}, u32[]{:S(2)}) collective-permute-start(bf16[64,16,128]{2,1,0:T(8,128)(2,1)S(1)} %get-tuple-element.87), channel_id=1, source_target_pairs={{0,1},{1,0},{2,3},{3,2},{4,5},{5,4},{6,7},{7,6},{8,9},{9,8},{10,11... | collective-permute-start | bytes 786440 | tf_op jit(solution)/shard_map/ppermute | solution.py:472
  206.8 20.1 %collective-permute-start.28 = (bf16[64,16,128]{2,1,0:T(8,128)(2,1)S(1)}, bf16[64,16,128]{2,1,0:T(8,128)(2,1)S(1)}, u32[]{:S(2)}, u32[]{:S(2)}) collective-permute-start(bf16[64,16,128]{2,1,0:T(8,128)(2,1)S(1)} %get-tuple-element.88), channel_id=1, source_target_pairs={{0,2},{1,3},{2,0},{3,1},{4,6},{5,7},{6,4},{7,5},{8,10},{9,11},{10,... | collective-permute-start | bytes 786440 | tf_op jit(solution)/shard_map/ppermute | solution.py:472
  207.9 19.0 %collective-permute-start.29 = (bf16[64,16,128]{2,1,0:T(8,128)(2,1)S(1)}, bf16[64,16,128]{2,1,0:T(8,128)(2,1)S(1)}, u32[]{:S(2)}, u32[]{:S(2)}) collective-permute-start(bf16[64,16,128]{2,1,0:T(8,128)(2,1)S(1)} %get-tuple-element.89), channel_id=1, source_target_pairs={{0,3},{1,2},{2,1},{3,0},{4,7},{5,6},{6,5},{7,4},{8,11},{9,10},{10,... | collective-permute-start | bytes 786440 | tf_op jit(solution)/shard_map/ppermute | solution.py:472
  220.2 6.7 %copy-start.3 = (bf16[64,16,128]{2,1,0:T(8,128)(2,1)S(1)}, bf16[64,16,128]{2,1,0:T(8,128)(2,1)}, u32[]{:S(2)}) copy-start(bf16[64,16,128]{2,1,0:T(8,128)(2,1)} %copy-done.2) | copy-start | bytes 786436
  220.2 6.7 %copy-start.6 = (bf16[64,16,128]{2,1,0:T(8,128)(2,1)S(1)}, bf16[64,16,128]{2,1,0:T(8,128)(2,1)}, u32[]{:S(2)}) copy-start(bf16[64,16,128]{2,1,0:T(8,128)(2,1)} %copy-done.5) | copy-start | bytes 786436
  220.2 6.7 %copy-start.10 = (bf16[64,16,128]{2,1,0:T(8,128)(2,1)S(1)}, bf16[64,16,128]{2,1,0:T(8,128)(2,1)}, u32[]{:S(2)}) copy-start(bf16[64,16,128]{2,1,0:T(8,128)(2,1)} %copy-done.8) | copy-start | bytes 786436
  220.2 6.7 %copy-start.14 = (bf16[64,16,128]{2,1,0:T(8,128)(2,1)S(1)}, bf16[64,16,128]{2,1,0:T(8,128)(2,1)}, u32[]{:S(2)}) copy-start(bf16[64,16,128]{2,1,0:T(8,128)(2,1)} %copy-done.12) | copy-start | bytes 786436
  220.2 6.7 %copy-start.18 = (bf16[64,16,128]{2,1,0:T(8,128)(2,1)S(1)}, bf16[64,16,128]{2,1,0:T(8,128)(2,1)}, u32[]{:S(2)}) copy-start(bf16[64,16,128]{2,1,0:T(8,128)(2,1)} %copy-done.16) | copy-start | bytes 786436
  220.2 6.7 %copy-start.24 = (bf16[64,16,128]{2,1,0:T(8,128)(2,1)S(1)}, bf16[64,16,128]{2,1,0:T(8,128)(2,1)}, u32[]{:S(2)}) copy-start(bf16[64,16,128]{2,1,0:T(8,128)(2,1)} %copy-done.23) | copy-start | bytes 786436
  220.2 6.7 %copy-start.27 = (bf16[64,16,128]{2,1,0:T(8,128)(2,1)S(1)}, bf16[64,16,128]{2,1,0:T(8,128)(2,1)}, u32[]{:S(2)}) copy-start(bf16[64,16,128]{2,1,0:T(8,128)(2,1)} %copy-done.26) | copy-start | bytes 786436
  250.0 6.4 %collective-permute-start.30 = (f32[64,512]{1,0:T(8,128)S(1)}, f32[64,512]{1,0:T(8,128)S(1)}, u32[]{:S(2)}, u32[]{:S(2)}) collective-permute-start(f32[64,512]{1,0:T(8,128)S(1)} %reduce_sum.19.refs_0_), channel_id=1, source_target_pairs={{0,1},{1,0},{2,3},{3,2},{4,5},{5,4},{6,7},{7,6},{8,9},{9,8},{10,11... | collective-permute-start | bytes 393224 | tf_op jit(solution)/shard_map/ppermute | solution.py:472
  256.4 7.6 %collective-permute-start.31 = (f32[64,512]{1,0:T(8,128)S(1)}, f32[64,512]{1,0:T(8,128)S(1)}, u32[]{:S(2)}, u32[]{:S(2)}) collective-permute-start(f32[64,512]{1,0:T(8,128)S(1)} %add.14), channel_id=1, source_target_pairs={{0,2},{1,3},{2,0},{3,1},{4,6},{5,7},{6,4},{7,5},{8,10},{9,11},{10,... | collective-permute-start | bytes 393224 | tf_op jit(solution)/shard_map/ppermute | solution.py:472
  274.1 5.5 %copy-start.4 = (bf16[64,16,128]{2,1,0:T(8,128)(2,1)S(1)}, bf16[64,16,128]{2,1,0:T(8,128)(2,1)}, u32[]{:S(2)}) copy-start(bf16[64,16,128]{2,1,0:T(8,128)(2,1)} %copy-done.2) | copy-start | bytes 786436
  274.1 5.5 %copy-start.7 = (bf16[64,16,128]{2,1,0:T(8,128)(2,1)S(1)}, bf16[64,16,128]{2,1,0:T(8,128)(2,1)}, u32[]{:S(2)}) copy-start(bf16[64,16,128]{2,1,0:T(8,128)(2,1)} %copy-done.5) | copy-start | bytes 786436
  274.1 5.5 %copy-start.11 = (bf16[64,16,128]{2,1,0:T(8,128)(2,1)S(1)}, bf16[64,16,128]{2,1,0:T(8,128)(2,1)}, u32[]{:S(2)}) copy-start(bf16[64,16,128]{2,1,0:T(8,128)(2,1)} %copy-done.8) | copy-start | bytes 786436
  274.1 5.5 %copy-start.15 = (bf16[64,16,128]{2,1,0:T(8,128)(2,1)S(1)}, bf16[64,16,128]{2,1,0:T(8,128)(2,1)}, u32[]{:S(2)}) copy-start(bf16[64,16,128]{2,1,0:T(8,128)(2,1)} %copy-done.12) | copy-start | bytes 786436
  274.1 5.5 %copy-start.19 = (bf16[64,16,128]{2,1,0:T(8,128)(2,1)S(1)}, bf16[64,16,128]{2,1,0:T(8,128)(2,1)}, u32[]{:S(2)}) copy-start(bf16[64,16,128]{2,1,0:T(8,128)(2,1)} %copy-done.16) | copy-start | bytes 786436
  274.1 5.5 %copy-start.25 = (bf16[64,16,128]{2,1,0:T(8,128)(2,1)S(1)}, bf16[64,16,128]{2,1,0:T(8,128)(2,1)}, u32[]{:S(2)}) copy-start(bf16[64,16,128]{2,1,0:T(8,128)(2,1)} %copy-done.23) | copy-start | bytes 786436
  274.1 5.5 %copy-start.28 = (bf16[64,16,128]{2,1,0:T(8,128)(2,1)S(1)}, bf16[64,16,128]{2,1,0:T(8,128)(2,1)}, u32[]{:S(2)}) copy-start(bf16[64,16,128]{2,1,0:T(8,128)(2,1)} %copy-done.26) | copy-start | bytes 786436
  (3 other events, 2.2 us)
Sparse Core Ops, SparseCore 0:
  264.8 23.3 all-gather.1

commit v6 on v5

--- a/solution.py
+++ b/solution.py
@@ -18,6 +18,14 @@
 ANY = pl.BlockSpec(memory_space=pl.ANY)
 ROWS_BY_ROWS = (((0,), (0,)), ((), ()))
 LANES_BY_LANES = (((1,), (1,)), ((), ()))
+
+
+def cost(flops, bytes_accessed, transcendentals):
+    return pl.CostEstimate(
+        flops=flops,
+        bytes_accessed=bytes_accessed,
+        transcendentals=transcendentals,
+    )
 
 
 def pack_kernel(slabs, capacity, per_slab, parts, dest_ref, owned_ref, *refs):
@@ -83,7 +91,7 @@
             pltpu.SMEM((slabs,), jnp.int32),
         ],
         compiler_params=pltpu.CompilerParams(vmem_limit_bytes=VMEM_BYTES),
-        cost_estimate=pl.CostEstimate(
+        cost_estimate=cost(
             flops=0, bytes_accessed=2 * owned.size * 2, transcendentals=0
         ),
         name="pack",
@@ -107,7 +115,7 @@
         in_specs=[VMEM, VMEM],
         out_specs=(VMEM,) * chips,
         compiler_params=pltpu.CompilerParams(vmem_limit_bytes=VMEM_BYTES),
-        cost_estimate=pl.CostEstimate(flops=0, bytes_accessed=8 * same.size, transcendentals=0),
+        cost_estimate=cost(flops=0, bytes_accessed=8 * same.size, transcendentals=0),
         name="merge",
     )(same, other)
 
@@ -156,7 +164,7 @@
         out_specs=(VMEM,) * shares + ((SMEM,) if first else ()),
         scratch_shapes=[pltpu.VMEM((chips * CORES, TILE), jnp.int32)] if first else [],
         compiler_params=pltpu.CompilerParams(vmem_limit_bytes=VMEM_BYTES),
-        cost_estimate=pl.CostEstimate(
+        cost_estimate=cost(
             flops=0, bytes_accessed=2 * chips * moved[0].size, transcendentals=0
         ),
         name="settle",
@@ -201,27 +209,27 @@
                     ]
 
 
-def gram_blocks(cells, steps=4):
+def gram_blocks(cells, after, steps=4):
     shares = len(cells[0])
     blocks, rows, width = cells[0][0].shape
     pairs = shares * (shares + 1) // 2
     full = shares * width
     spec = pl.BlockSpec((blocks // steps, rows, width), lambda i: (i, 0, 0))
     return pl.pallas_call(
-        lambda *refs: gram_kernel(len(cells), shares, *refs),
+        lambda *refs: gram_kernel(len(cells), shares, *refs[len(after) :]),
         grid=(steps,),
         out_shape=jax.ShapeDtypeStruct((pairs, TILE, TILE), jnp.float32),
-        in_specs=[spec] * (len(cells) * shares),
+        in_specs=[ANY] * len(after) + [spec] * (len(cells) * shares),
         out_specs=pl.BlockSpec((pairs, TILE, TILE), lambda i: (0, 0, 0)),
         scratch_shapes=[pltpu.VMEM((full, full), jnp.float32)],
         compiler_params=pltpu.CompilerParams(vmem_limit_bytes=VMEM_BYTES),
-        cost_estimate=pl.CostEstimate(
+        cost_estimate=cost(
             flops=2 * len(cells) * blocks * rows * full * full,
             bytes_accessed=2 * len(cells) * blocks * rows * full,
             transcendentals=0,
         ),
         name="gram_blocks",
-    )(*[piece for part in cells for piece in part])
+    )(*after, *[piece for part in cells for piece in part])
 
 
 def cross_kernel(parts, shares, *refs):
@@ -264,7 +272,7 @@
         out_specs=pl.BlockSpec((full, full), lambda i: (0, 0)),
         scratch_shapes=[pltpu.VMEM((full, full), jnp.float32)],
         compiler_params=pltpu.CompilerParams(vmem_limit_bytes=VMEM_BYTES),
-        cost_estimate=pl.CostEstimate(
+        cost_estimate=cost(
             flops=2 * parts * blocks * rows * full * full,
             bytes_accessed=4 * parts * blocks * rows * full,
             transcendentals=0,
@@ -404,7 +412,7 @@
         scratch_shapes=[pltpu.VMEM((TILE, TILE), jnp.float32)] * 4,
         input_output_aliases={len(after): 0} if aliases else {},
         compiler_params=pltpu.CompilerParams(vmem_limit_bytes=VMEM_BYTES),
-        cost_estimate=pl.CostEstimate(
+        cost_estimate=cost(
             flops=7 * 10**9, bytes_accessed=value.size * 4, transcendentals=TILE
         ),
         name="factor",
@@ -429,60 +437,82 @@
     )
 
 
-def basis_kernel(parts, shares, *refs):
-    hi_ref, mid_ref, lo_ref, out_ref = refs[parts * shares :]
-    for part in range(parts):
-        cells = whole_rows(refs[part * shares : (part + 1) * shares])
-        total = lax.dot_general(
-            cells, lo_ref[...], LANES_BY_LANES, preferred_element_type=jnp.float32
-        )
-        total += lax.dot_general(
-            cells, mid_ref[...], LANES_BY_LANES, preferred_element_type=jnp.float32
-        )
-        total += lax.dot_general(
-            cells, hi_ref[...], LANES_BY_LANES, preferred_element_type=jnp.float32
-        )
-        blocks, _, rows, full = out_ref.shape
-        out_ref[:, part] = total.reshape(blocks, rows, full)
-
-
-def basis(cells, terms, steps=8):
-    parts, shares = len(cells), len(cells[0])
-    blocks, rows, width = cells[0][0].shape
+def basis_kernel(*refs):
+    hi_ref, mid_ref, lo_ref, out_ref = refs[-4:]
+    cells = whole_rows(refs[:-4])
+    total = lax.dot_general(
+        cells, lo_ref[...], LANES_BY_LANES, preferred_element_type=jnp.float32
+    )
+    total += lax.dot_general(
+        cells, mid_ref[...], LANES_BY_LANES, preferred_element_type=jnp.float32
+    )
+    total += lax.dot_general(
+        cells, hi_ref[...], LANES_BY_LANES, preferred_element_type=jnp.float32
+    )
+    out_ref[:, 0] = total.reshape(out_ref.shape[0], *out_ref.shape[2:])
+
+
+def basis(cells, terms, part, parts, filled, after, steps=4):
+    shares = len(cells)
+    blocks, rows, width = cells[0].shape
     full = shares * width
     spec = pl.BlockSpec((blocks // steps, rows, width), lambda i: (i, 0, 0))
     term = pl.BlockSpec((full, full), lambda i: (0, 0))
-    return pl.pallas_call(
-        lambda *refs: basis_kernel(parts, shares, *refs),
+    unread = ([] if filled is None else [filled]) + list(after)
+    return pl.pallas_call(
+        lambda *refs: basis_kernel(*refs[len(unread) :]),
         grid=(steps,),
         out_shape=jax.ShapeDtypeStruct((blocks, parts, rows, full), jnp.float32),
-        in_specs=[spec] * (parts * shares) + [term] * 3,
-        out_specs=pl.BlockSpec((blocks // steps, parts, rows, full), lambda i: (i, 0, 0, 0)),
-        compiler_params=pltpu.CompilerParams(vmem_limit_bytes=VMEM_BYTES),
-        cost_estimate=pl.CostEstimate(
-            flops=6 * parts * blocks * rows * full * full,
-            bytes_accessed=6 * parts * blocks * rows * full,
+        in_specs=[ANY] * len(unread) + [spec] * shares + [term] * 3,
+        out_specs=pl.BlockSpec((blocks // steps, 1, rows, full), lambda i: (i, part, 0, 0)),
+        input_output_aliases={} if filled is None else {0: 0},
+        compiler_params=pltpu.CompilerParams(vmem_limit_bytes=VMEM_BYTES),
+        cost_estimate=cost(
+            flops=6 * blocks * rows * full * full,
+            bytes_accessed=6 * blocks * rows * full,
             transcendentals=0,
         ),
         name="basis",
-    )(*[piece for part in cells for piece in part], *terms)
+    )(*unread, *cells, *terms)
+
+
+def sum_kernel(count, value_ref, out_ref):
+    rows = out_ref.shape[0]
+    total = value_ref[:rows]
+    for i in range(1, count):
+        total += value_ref[i * rows : (i + 1) * rows]
+    out_ref[...] = total
+
+
+def sum_pieces(value, count, after):
+    rows, lanes = value.shape
+    return pl.pallas_call(
+        lambda *refs: sum_kernel(count, *refs[len(after) :]),
+        out_shape=jax.ShapeDtypeStruct((rows // count, lanes), value.dtype),
+        in_specs=[ANY] * len(after) + [VMEM],
+        out_specs=VMEM,
+        cost_estimate=cost(flops=value.size, bytes_accessed=4 * value.size, transcendentals=0),
+        name="sum_pieces",
+    )(*after, value)
+
+
+def add_kernel(one_ref, two_ref, out_ref):
+    out_ref[...] = one_ref[...] + two_ref[...]
+
+
+def add(one, two, after):
+    return pl.pallas_call(
+        lambda *refs: add_kernel(*refs[len(after) :]),
+        out_shape=jax.ShapeDtypeStruct(one.shape, one.dtype),
+        in_specs=[ANY] * len(after) + [VMEM, VMEM],
+        out_specs=VMEM,
+        cost_estimate=cost(flops=one.size, bytes_accessed=12 * one.size, transcendentals=0),
+        name="add",
+    )(*after, one, two)
 
 
 def swap(value, axis, mask):
     return lax.ppermute(value, axis, [(i, i ^ mask) for i in range(lax.axis_size(axis))])
-
-
-def slab_sum(value, slabs):
-    pieces = lax.all_to_all(value, "space", split_axis=0, concat_axis=0, tiled=True)
-    return jnp.sum(pieces.reshape(slabs, -1, value.shape[-1]), axis=0)
-
-
-def share_sum(piece, shares):
-    hop = 1
-    while hop < shares:
-        piece += swap(piece, "snap", hop)
-        hop *= 2
-    return lax.all_gather(piece, "space", axis=0, tiled=True)
 
 
 def body(owned_x, owned_y, patch_dest):
@@ -508,42 +538,59 @@
     def to_rows(pieces):
         return [pieces[0]] + [swap(pieces[r], "snap", r) for r in range(1, shares)]
 
-    def place(meta, moved, after=()):
+    def place(meta, moved, after):
         return settle(meta, moved, slots // slabs, per_slab, shares, after)
 
+    def to_pieces(value):
+        return lax.all_to_all(value, "space", split_axis=0, concat_axis=0, tiled=True)
+
+    def hops():
+        hop = 1
+        while hop < shares:
+            yield hop
+            hop *= 2
+
     sent_x = pack(patch_dest, parted(owned_x), slabs, per_slab, True)
-    moved_x = [to_chips(merged(part)) for part in sent_x]
-    pieces, meta = place(None, moved_x[0])
+    joined_x = [merged(part) for part in sent_x]
+    moved_x = [to_chips(joined) for joined in joined_x]
+    sent_y = pack(patch_dest, parted(owned_y), slabs, per_slab, False)
+    joined_y = [merged(part) for part in sent_y]
+    moved_y = [to_chips(joined) for joined in joined_y]
+
+    pieces, meta = place(None, moved_x[0], [joined[0] for joined in joined_x[1:]] + [sent_y[0][0]])
     x_cells = [to_rows(pieces)]
-    sent_y = pack(patch_dest, parted(owned_y), slabs, per_slab, False, x_cells[0][1:2])
-    joined_y = [merged(part) for part in sent_y]
     for moved in moved_x[1:]:
-        pieces, _ = place(meta, moved, x_cells[-1][1:] + [joined_y[0][0]])
+        pieces, _ = place(meta, moved, x_cells[-1][1:] + moved_y[0][1:2])
         x_cells.append(to_rows(pieces))
-    gram_piece = slab_sum(gram_blocks(x_cells).reshape(pairs * TILE, TILE), slabs)
-
-    y_cells, after = [], x_cells[-1][1:]
-    for joined in joined_y:
-        pieces, _ = place(meta, to_chips(joined), after)
+    gram_local = gram_blocks(x_cells, [joined[0] for joined in joined_y[1:]])
+    gram = to_pieces(gram_local.reshape(pairs * TILE, TILE))
+    pieces, _ = place(meta, moved_y[0], x_cells[-1][1:])
+    y_cells = [to_rows(pieces)]
+    gram = sum_pieces(gram, slabs, pieces[:1])
+    for hop in hops():
+        gram = add(gram, swap(gram, "snap", hop), y_cells[0][1:2] if hop == 1 else y_cells[0][2:] + moved_y[1][1:])
+    gram = lax.all_gather(gram, "space", axis=0, tiled=True)
+    for moved in moved_y[1:]:
+        pieces, _ = place(meta, moved, y_cells[-1][1:])
         y_cells.append(to_rows(pieces))
-        after = y_cells[-1][1:] + [gram_piece]
-
-    gram = share_sum(gram_piece, shares)
-    steps = factor_steps(
-        gram.reshape(pairs, TILE, TILE), tiles, rows_total, [y_cells[-1][0]]
-    )
+
+    steps = factor_steps(gram.reshape(pairs, TILE, TILE), tiles, rows_total, pieces[:1])
     state = next(steps)
+    for _ in range(tiles - 2):
+        state = steps.send([])
     cross_local = cross_sum(x_cells, y_cells, [state])
-    state = steps.send([cross_local])
-    cross_piece = slab_sum(cross_local, slabs)
-    for _ in range(tiles - 2):
-        state = steps.send([cross_piece])
-    cross = share_sum(cross_piece, shares)
-    r_factor, inverse, *terms = state
-    q_basis = basis(x_cells, terms).reshape(per_slab, patch // shares, full)
-
+    cross = to_pieces(cross_local)
+    r_factor, inverse, *terms = steps.send([cross_local])
+
+    q_basis = basis(x_cells[0], terms, 0, parts, None, [])
+    cross = sum_pieces(cross, slabs, [q_basis])
+    for part in range(1, parts):
+        q_basis = basis(x_cells[part], terms, part, parts, q_basis, [cross])
+    for hop in hops():
+        cross = add(cross, swap(cross, "snap", hop), [q_basis] if hop == 1 else [])
+    cross = lax.all_gather(cross, "space", axis=0, tiled=True)
     projection = jnp.dot(inverse, cross, precision=HIGHEST) / math.sqrt(rows_total)
-    return q_basis, r_factor, projection
+    return q_basis.reshape(per_slab, patch // shares, full), r_factor, projection
 
 
 def solution(mesh):

time: 300 us -> 288 us (0.960)
  blocking collectives: 30.5 us -> 10.3 us
  waiting for transfers between devices: 122 us -> 110 us
  Pallas kernels: 55.5 us -> 66.2 us
  local copies, waits for them, and re-layouts: 6.27 us -> 12.5 us
  starting transfers between devices: 64.3 us -> 69.1 us
  other arithmetic: 3.16 us -> 0 us
    ppermute x32, waiting for transfers between devices: 119 us -> 82 us  [swap(): lax.ppermute(value, axis, [(i, i ^ mask) for i in range(lax.axis_size(axi...]
    all_gather x1, waiting for transfers between devices: 0.01 us -> 23.6 us  [body(): cross = lax.all_gather(cross, 'space', axis=0, tiled=True)]
    all_to_all x1 -> x0, blocking collectives: 19.6 us -> none  [slab_sum(): lax.all_to_all(value, 'space', split_axis=0, concat_axis=0, tiled=True)]
    pallas_call x2 -> x9, Pallas kernels: 12.1 us -> 19.8 us  [the longest x2 6.82 us: basis(): pl.pallas_call(lambda *refs: basis_kernel(*refs[len(unread):]), grid=(ste...]
    unnamed x66 -> x72, local copies, waits for them, and re-layouts: 6.27 us -> 12.5 us
    all_to_all x1 -> x2, starting transfers between devices: 4.34 us -> 8.46 us  [to_pieces(): lax.all_to_all(value, 'space', split_axis=0, concat_axis=0, tiled=True)]
  transfers between devices with their start and end apart: 34 -> 35, of which waited for: 17 -> 15; matrix products, arithmetic and copies ran while one was open for 0% -> 0% of each run, Pallas kernels for 17% -> 18%
where the time goes in v6:
time: 288 us; the launch traced here: 286 us
  waiting for transfers between devices  110 us (38%)
  starting transfers between devices  69.1 us (24%)
  Pallas kernels  66.2 us (23%)
  between operations  14.4 us (5%)
  local copies, waits for them, and re-layouts  12.5 us (4%)
  blocking collectives  10.3 us (4%)
  matrix products  4.04 us (1%)
    ppermute x32, waiting for transfers between devices, swap(): lax.ppermute(value, axis, [(i, i ^ mask) for i in range(lax.axis_size(axi...  82 us
    ppermute x32, starting transfers between devices, swap(): lax.ppermute(value, axis, [(i, i ^ mask) for i in range(lax.axis_size(axi...  60.6 us
    all_gather x1, waiting for transfers between devices, body(): cross = lax.all_gather(cross, 'space', axis=0, tiled=True)  23.6 us
    pallas_call x4, Pallas kernels, factor_call(): pl.pallas_call(lambda *refs: kernel(*refs[len(after):]), out_shape=out_sh...  19.7 us
    pallas_call x4, Pallas kernels, settle(): pl.pallas_call(lambda *refs: settle_kernel(chips, capacity, first, *refs[...  12.7 us
    unnamed x72, local copies, waits for them, and re-layouts  12.5 us
    all_gather x1, blocking collectives, body(): gram = lax.all_gather(gram, 'space', axis=0, tiled=True)  10.3 us
    all_to_all x2, starting transfers between devices, to_pieces(): lax.all_to_all(value, 'space', split_axis=0, concat_axis=0, tiled=True)  8.46 us
  transfers between devices with their start and end apart: 35, of which 15 were waited for; matrix products, arithmetic and copies ran while one was open for 0% of the time, Pallas kernels for 18%

profile of v6, /device:TPU:0, one launch (start us, length us, event | category | flops | bytes accessed | tf_op | source)
XLA Modules:
  0.0 286.3 jit_solution(3427352778265246128)
XLA Ops:
  7.2 2.2 copy-done
  10.0 3.4 %pack.2 = (bf16[260,16,128]{2,1,0:T(8,128)(2,1)S(1)}, bf16[260,16,128]{2,1,0:T(8,128)(2,1)S(1)}, bf16[256,16,128]{2,1,0:T(8,128)(2,1)S(1)}, bf16[256,16,128]{2,1,0:T(8,128)(2,1)S(1)}) custom-call(s32[128]{0:T(128)S(1)} %copy-done.27, bf16[128,4,2,16,128]{4,3,2,1,0:T(8,128)(2,1)S(1)} %bitcast.10), custom_call_target="tpu_custom_call" | custom-call | bytes 8388608 | tf_op jit(solution)/shard_map/pack/pallas_call | solution.py:84
  13.6 3.3 %pack.3 = (bf16[256,16,128]{2,1,0:T(8,128)(2,1)S(1)}, bf16[256,16,128]{2,1,0:T(8,128)(2,1)S(1)}, bf16[256,16,128]{2,1,0:T(8,128)(2,1)S(1)}, bf16[256,16,128]{2,1,0:T(8,128)(2,1)S(1)}) custom-call(s32[128]{0:T(128)S(1)} %copy-done.28, bf16[128,4,2,16,128]{4,3,2,1,0:T(8,128)(2,1)S(1)} %bitcast.11), custom_call_target="tpu_custom_call" | custom-call | bytes 8388608 | tf_op jit(solution)/shard_map/pack/pallas_call | solution.py:84
  17.6 2.4 collective-permute-start.2
  23.1 1.5 collective-permute-start.9
  24.8 8.1 %collective-permute-done.2.refs_3_ = bf16[130,16,128]{2,1,0:T(8,128)(2,1)S(1)} collective-permute-done((bf16[130,16,128]{2,1,0:T(8,128)(2,1)S(1)}, bf16[130,16,128]{2,1,0:T(8,128)(2,1)S(1)}, u32[]{:S(2)}, u32[]{:S(2)}) %collective-permute-start.2) | collective-permute-done | bytes 532512 | tf_op jit(solution)/shard_map/ppermute | solution.py:515
  32.9 2.1 collective-permute-start.10
  34.9 9.1 %collective-permute-done.3.refs_4_ = bf16[130,16,128]{2,1,0:T(8,128)(2,1)S(1)} collective-permute-done((bf16[130,16,128]{2,1,0:T(8,128)(2,1)S(1)}, bf16[130,16,128]{2,1,0:T(8,128)(2,1)S(1)}, u32[]{:S(2)}, u32[]{:S(2)}) %collective-permute-start.3) | collective-permute-done | bytes 532512 | tf_op jit(solution)/shard_map/ppermute | solution.py:515
  44.0 2.5 collective-permute-start.11
  46.5 1.1 collective-permute-start.12
  47.6 3.0 %settle.4 = (bf16[64,16,128]{2,1,0:T(8,128)(2,1)S(1)}, bf16[64,16,128]{2,1,0:T(8,128)(2,1)S(1)}, bf16[64,16,128]{2,1,0:T(8,128)(2,1)S(1)}, bf16[64,16,128]{2,1,0:T(8,128)(2,1)S(1)}, s32[8,128]{1,0:T(8,128)S(1)}) custom-call(bf16[128,16,128]{2,1,0:T(8,128)(2,1)S(1)} %get-tuple-element.51.refs_0_.refs_5_, ...), custom_call_target="tpu_custom_call" | custom-call | bytes 2129920 | tf_op jit(solution)/shard_map/settle/pallas_call | solution.py:160
  50.6 5.0 %collective-permute-done.9.refs_3_.refs_5_ = bf16[128,16,128]{2,1,0:T(8,128)(2,1)S(1)} collective-permute-done((bf16[128,16,128]{2,1,0:T(8,128)(2,1)S(1)}, bf16[128,16,128]{2,1,0:T(8,128)(2,1)S(1)}, u32[]{:S(2)}, u32[]{:S(2)}) %collective-permute-start.9) | collective-permute-done | bytes 524320 | tf_op jit(solution)/shard_map/ppermute | solution.py:515
  55.6 2.8 collective-permute-start.5
  58.4 8.4 %collective-permute-done.10.refs_6_ = bf16[128,16,128]{2,1,0:T(8,128)(2,1)S(1)} collective-permute-done((bf16[128,16,128]{2,1,0:T(8,128)(2,1)S(1)}, bf16[128,16,128]{2,1,0:T(8,128)(2,1)S(1)}, u32[]{:S(2)}, u32[]{:S(2)}) %collective-permute-start.10) | collective-permute-done | bytes 524320 | tf_op jit(solution)/shard_map/ppermute | solution.py:515
  66.8 3.8 %collective-permute-start.6 = (bf16[64,16,128]{2,1,0:T(8,128)(2,1)S(1)}, bf16[64,16,128]{2,1,0:T(8,128)(2,1)S(1)}, u32[]{:S(2)}, u32[]{:S(2)}) collective-permute-start(bf16[64,16,128]{2,1,0:T(8,128)(2,1)S(1)} %get-tuple-element.61), channel_id=1, source_target_pairs={{0,2},{1,3},{2,0},{3,1},{4,6},{5,7},{6,4},{7,5},{8,10},{9,11},{10,... | collective-permute-start | bytes 786440 | tf_op jit(solution)/shard_map/ppermute | solution.py:515
  70.6 1.3 collective-permute-start.7
  72.0 7.6 %collective-permute-done.12.refs_8_ = bf16[128,16,128]{2,1,0:T(8,128)(2,1)S(1)} collective-permute-done((bf16[128,16,128]{2,1,0:T(8,128)(2,1)S(1)}, bf16[128,16,128]{2,1,0:T(8,128)(2,1)S(1)}, u32[]{:S(2)}, u32[]{:S(2)}) %collective-permute-start.12) | collective-permute-done | bytes 524320 | tf_op jit(solution)/shard_map/ppermute | solution.py:515
  79.6 8.4 %collective-permute-done.6.refs_1_.refs_3_.refs_2_ = bf16[64,16,128]{2,1,0:T(8,128)(2,1)S(1)} collective-permute-done((bf16[64,16,128]{2,1,0:T(8,128)(2,1)S(1)}, bf16[64,16,128]{2,1,0:T(8,128)(2,1)S(1)}, u32[]{:S(2)}, u32[]{:S(2)}) %collective-permute-start.6) | collective-permute-done | bytes 262176 | tf_op jit(solution)/shard_map/ppermute | solution.py:515
  87.9 2.3 settle.5
  90.3 5.2 %collective-permute-start.13 = (bf16[64,16,128]{2,1,0:T(8,128)(2,1)S(1)}, bf16[64,16,128]{2,1,0:T(8,128)(2,1)S(1)}, u32[]{:S(2)}, u32[]{:S(2)}) collective-permute-start(bf16[64,16,128]{2,1,0:T(8,128)(2,1)S(1)} %get-tuple-element.69), channel_id=1, source_target_pairs={{0,1},{1,0},{2,3},{3,2},{4,5},{5,4},{6,7},{7,6},{8,9},{9,8},{10,11... | collective-permute-start | bytes 786440 | tf_op jit(solution)/shard_map/ppermute | solution.py:515
  95.5 2.0 collective-permute-start.14
  97.5 1.4 collective-permute-start.15
  98.8 2.2 collective-permute-start.16
  101.5 1.1 merge.7
  102.6 4.7 %collective-permute-done.13.refs_0_.refs_6_.refs_3_ = bf16[64,16,128]{2,1,0:T(8,128)(2,1)S(1)} collective-permute-done((bf16[64,16,128]{2,1,0:T(8,128)(2,1)S(1)}, bf16[64,16,128]{2,1,0:T(8,128)(2,1)S(1)}, u32[]{:S(2)}, u32[]{:S(2)}) %collective-permute-start.13) | collective-permute-done | bytes 262176 | tf_op jit(solution)/shard_map/ppermute | solution.py:515
  107.3 9.5 %collective-permute-done.14.refs_1_.refs_7_.refs_4_ = bf16[64,16,128]{2,1,0:T(8,128)(2,1)S(1)} collective-permute-done((bf16[64,16,128]{2,1,0:T(8,128)(2,1)S(1)}, bf16[64,16,128]{2,1,0:T(8,128)(2,1)S(1)}, u32[]{:S(2)}, u32[]{:S(2)}) %collective-permute-start.14) | collective-permute-done | bytes 262176 | tf_op jit(solution)/shard_map/ppermute | solution.py:515
  116.8 2.9 %gram_blocks.1 = f32[10,128,128]{2,1,0:T(8,128)} custom-call(bf16[128,16,128]{2,1,0:T(8,128)(2,1)S(1)} %get-tuple-element.80.refs_4_.refs_0_, bf16[64,16,128]{2,1,0:T(8,128)(2,1)S(1)} %get-tuple-element.59.refs_1_.refs_0_, bf16[64,16,128]{2,1,0:T(8,128)(2,1)S(1)} %collective-permute-done.5.refs_0_.refs_2_.refs_1_, ...), custom_call_target="tpu_custom_call" | custom-call | flops 1073741824 | bytes 2097152 | tf_op jit(solution)/shard_map/gram_blocks/pallas_call | solution.py:218
  119.8 4.2 %all-to-all-start = ((f32[8,160,128]{2,1,0:T(8,128)}), f32[8,160,128]{2,1,0:T(8,128)}, u32[]{:S(2)}, u32[]{:S(2)}) async-start(f32[8,160,128]{2,1,0:T(8,128)} %bitcast.2), calls=%async_computation | async-start | bytes 1310720 | tf_op jit(solution)/shard_map/all_to_all | solution.py:545
  124.0 1.9 collective-permute-start.22
  125.9 3.6 %settle.6 = (bf16[64,16,128]{2,1,0:T(8,128)(2,1)S(1)}, bf16[64,16,128]{2,1,0:T(8,128)(2,1)}, bf16[64,16,128]{2,1,0:T(8,128)(2,1)S(1)}, bf16[64,16,128]{2,1,0:T(8,128)(2,1)S(1)}) custom-call(bf16[64,16,128]{2,1,0:T(8,128)(2,1)S(1)} %collective-permute-done.13.refs_0_.refs_6_.refs_3_, bf16[64,16,128]{2,1,0:T(8,128)(2,1)S(1)} %collective-permute-done.14.refs_1_.refs_7_.refs_4_, ...), custom_call_target="tpu_custom_call" | custom-call | bytes 2097152 | tf_op jit(solution)/shard_map/settle/pallas_call | solution.py:160
  131.7 5.0 %collective-permute-start.18 = (bf16[64,16,128]{2,1,0:T(8,128)(2,1)}, bf16[64,16,128]{2,1,0:T(8,128)(2,1)S(1)}, u32[]{:S(2)}, u32[]{:S(2)}) collective-permute-start(bf16[64,16,128]{2,1,0:T(8,128)(2,1)} %get-tuple-element.75), channel_id=1, source_target_pairs={{0,1},{1,0},{2,3},{3,2},{4,5},{5,4},{6,7},{7,6},{8,9},{9,8},{10,11... | collective-permute-start | bytes 786440 | tf_op jit(solution)/shard_map/ppermute | solution.py:515
  136.6 1.5 collective-permute-start.23
  138.4 1.8 sum_pieces.2.refs_1_
  140.1 2.2 collective-permute-start.25
  142.3 1.6 collective-permute-done.18.refs_0_.refs_10_
  144.0 3.8 %collective-permute-start.19 = (bf16[64,16,128]{2,1,0:T(8,128)(2,1)}, bf16[64,16,128]{2,1,0:T(8,128)(2,1)S(1)}, u32[]{:S(2)}, u32[]{:S(2)}) collective-permute-start(bf16[64,16,128]{2,1,0:T(8,128)(2,1)} %copy-done.31), channel_id=1, source_target_pairs={{0,2},{1,3},{2,0},{3,1},{4,6},{5,7},{6,4},{7,5},{8,10},{9,11},{10,... | collective-permute-start | bytes 786440 | tf_op jit(solution)/shard_map/ppermute | solution.py:515
  147.7 1.1 collective-permute-start.20
  148.9 1.6 add.4.refs_5_
  150.5 2.3 collective-permute-start.26
  152.7 8.8 %collective-permute-done.23.refs_6_.refs_3_ = bf16[128,16,128]{2,1,0:T(8,128)(2,1)S(1)} collective-permute-done((bf16[128,16,128]{2,1,0:T(8,128)(2,1)}, bf16[128,16,128]{2,1,0:T(8,128)(2,1)S(1)}, u32[]{:S(2)}, u32[]{:S(2)}) %collective-permute-start.23) | collective-permute-done | bytes 524320 | tf_op jit(solution)/shard_map/ppermute | solution.py:515
  161.5 5.2 %collective-permute-done.19.refs_1_.refs_0_.refs_11_ = bf16[64,16,128]{2,1,0:T(8,128)(2,1)S(1)} collective-permute-done((bf16[64,16,128]{2,1,0:T(8,128)(2,1)}, bf16[64,16,128]{2,1,0:T(8,128)(2,1)S(1)}, u32[]{:S(2)}, u32[]{:S(2)}) %collective-permute-start.19) | collective-permute-done | bytes 262176 | tf_op jit(solution)/shard_map/ppermute | solution.py:515
  168.8 3.8 %settle.7 = (bf16[64,16,128]{2,1,0:T(8,128)(2,1)S(1)}, bf16[64,16,128]{2,1,0:T(8,128)(2,1)}, bf16[64,16,128]{2,1,0:T(8,128)(2,1)}, bf16[64,16,128]{2,1,0:T(8,128)(2,1)}) custom-call(bf16[64,16,128]{2,1,0:T(8,128)(2,1)S(1)} %copy-done.7, bf16[64,16,128]{2,1,0:T(8,128)(2,1)S(1)} %collective-permute-done.19.refs_1_.refs_0_.refs_11_, ...), custom_call_target="tpu_custom_call" | custom-call | bytes 2097152 | tf_op jit(solution)/shard_map/settle/pallas_call | solution.py:160
  172.6 5.8 %collective-permute-start.27 = (bf16[64,16,128]{2,1,0:T(8,128)(2,1)}, bf16[64,16,128]{2,1,0:T(8,128)(2,1)}, u32[]{:S(2)}, u32[]{:S(2)}) collective-permute-start(bf16[64,16,128]{2,1,0:T(8,128)(2,1)} %get-tuple-element.87), channel_id=1, source_target_pairs={{0,1},{1,0},{2,3},{3,2},{4,5},{5,4},{6,7},{7,6},{8,9},{9,8},{10,11... | collective-permute-start | bytes 786440 | tf_op jit(solution)/shard_map/ppermute | solution.py:515
  178.3 1.2 collective-permute-start.28
  179.6 1.4 collective-permute-start.29
  181.7 1.6 add.5
  183.2 10.3 %all_gather.6 = f32[1280,128]{1,0:T(8,128)S(1)} all-gather(f32[160,128]{1,0:T(8,128)} %add.5), channel_id=1, replica_groups=mesh['space'=8,'snap'=4] {'space'}, dimensions={0}, use_global_device_ids=true | all-gather | bytes 737280 | tf_op jit(solution)/shard_map/all_gather | solution.py:572
  193.5 4.9 %factor.4.refs_0_ = f32[4,8,128,128]{3,2,1,0:T(8,128)S(1)} custom-call(bf16[64,16,128]{2,1,0:T(8,128)(2,1)S(1)} %get-tuple-element.84.refs_0_.refs_13_, f32[10,128,128]{2,1,0:T(8,128)S(1)} %bitcast.12), custom_call_target="tpu_custom_call" | custom-call | flops 7000000000 | bytes 655360 | tf_op jit(solution)/shard_map/factor/pallas_call | solution.py:407
  198.5 4.8 %factor.5.refs_0_ = f32[4,8,128,128]{3,2,1,0:T(8,128)S(1)} custom-call(f32[4,8,128,128]{3,2,1,0:T(8,128)S(1)} %factor.4.refs_0_), custom_call_target="tpu_custom_call", output_to_operand_aliasing={{}: (0, {})} | custom-call | flops 7000000000 | bytes 2097152 | tf_op jit(solution)/shard_map/factor/pallas_call | solution.py:407
  203.4 4.6 %factor.6.refs_0_.refs_1_ = f32[4,8,128,128]{3,2,1,0:T(8,128)S(1)} custom-call(f32[4,8,128,128]{3,2,1,0:T(8,128)S(1)} %factor.5.refs_0_), custom_call_target="tpu_custom_call", output_to_operand_aliasing={{}: (0, {})} | custom-call | flops 7000000000 | bytes 2097152 | tf_op jit(solution)/shard_map/factor/pallas_call | solution.py:407
  208.3 4.7 %cross_sum.1.refs_0_ = f32[512,512]{1,0:T(8,128)} custom-call(f32[4,8,128,128]{3,2,1,0:T(8,128)S(1)} %factor.6.refs_0_.refs_1_, bf16[64,16,128]{2,1,0:T(8,128)(2,1)S(1)} %copy-done.21, bf16[64,16,128]{2,1,0:T(8,128)(2,1)S(1)} %collective-permute-done.5.refs_0_.refs_2_.refs_1_, bf16[64,16,128]{2,1,0:T(8,128)(2,1)S(1)} %collective-permute-done.6.refs_1_.refs_3_.refs_2_, ...), custom_call_target="tpu_custom_call" | custom-call | flops 1073741824 | bytes 4194304 | tf_op jit(solution)/shard_map/cross_sum/pallas_call | solution.py:267
  213.0 4.2 %all-to-all-start.1 = ((f32[8,64,512]{2,1,0:T(8,128)}), f32[8,64,512]{2,1,0:T(8,128)}, u32[]{:S(2)}, u32[]{:S(2)}) async-start(f32[8,64,512]{2,1,0:T(8,128)} %bitcast.5), calls=%async_computation.1 | async-start | bytes 2097152 | tf_op jit(solution)/shard_map/all_to_all | solution.py:545
  217.3 1.6 copy-done.10
  218.8 5.4 %factor.7 = (f32[512,512]{1,0:T(8,128)}, f32[512,512]{1,0:T(8,128)S(1)}, bf16[512,512]{1,0:T(8,128)(2,1)S(1)}, bf16[512,512]{1,0:T(8,128)(2,1)S(1)}, bf16[512,512]{1,0:T(8,128)(2,1)S(1)}) custom-call(f32[512,512]{1,0:T(8,128)} %cross_sum.1.refs_0_, f32[4,8,128,128]{3,2,1,0:T(8,128)S(1)} %copy-done.10), custom_call_target="tpu_custom_call" | custom-call | flops 7000000000 | bytes 2097152 | tf_op jit(solution)/shard_map/factor/pallas_call | solution.py:407
  225.2 3.4 %basis.2.refs_0_ = f32[64,2,16,512]{3,2,1,0:T(8,128)} custom-call(bf16[64,16,128]{2,1,0:T(8,128)(2,1)S(1)} %copy-done.22, bf16[64,16,128]{2,1,0:T(8,128)(2,1)S(1)} %collective-permute-done.5.refs_0_.refs_2_.refs_1_, bf16[64,16,128]{2,1,0:T(8,128)(2,1)S(1)} %collective-permute-done.6.refs_1_.refs_3_.refs_2_, ...), custom_call_target="tpu_custom_call" | custom-call | flops 1610612736 | bytes 3145728 | tf_op jit(solution)/shard_map/basis/pallas_call | solution.py:462
  228.6 4.0 %all-to-all-done.1 = f32[8,64,512]{2,1,0:T(8,128)} async-done(((f32[8,64,512]{2,1,0:T(8,128)}), f32[8,64,512]{2,1,0:T(8,128)}, u32[]{:S(2)}, u32[]{:S(2)}) %all-to-all-start.1) | async-done | bytes 1048608 | tf_op jit(solution)/shard_map/all_to_all | solution.py:545
  232.6 1.9 sum_pieces.3.refs_1_
  236.3 3.4 %basis.3.refs_0_ = f32[64,2,16,512]{3,2,1,0:T(8,128)} custom-call(f32[64,2,16,512]{3,2,1,0:T(8,128)} %basis.2.refs_0_, f32[64,512]{1,0:T(8,128)S(1)} %copy-done.13, bf16[64,16,128]{2,1,0:T(8,128)(2,1)S(1)} %copy-done.17, bf16[64,16,128]{2,1,0:T(8,128)(2,1)S(1)} %collective-permute-done.13.refs_0_.refs_6_.refs_3_, ...), custom_call_target="tpu_custom_call", output_to_operand_aliasing={{}: (0, {})} | custom-call | flops 1610612736 | bytes 3145728 | tf_op jit(solution)/shard_map/basis/pallas_call | solution.py:462
  240.4 1.6 add.6.refs_0_
  242.0 2.1 collective-permute-start.31
  244.1 5.4 %collective-permute-done.31.refs_1_ = f32[64,512]{1,0:T(8,128)S(1)} collective-permute-done((f32[64,512]{1,0:T(8,128)}, f32[64,512]{1,0:T(8,128)S(1)}, u32[]{:S(2)}, u32[]{:S(2)}) %collective-permute-start.31) | collective-permute-done | bytes 131104 | tf_op jit(solution)/shard_map/ppermute | solution.py:515
  250.1 1.6 add.7
  251.8 23.6 %all-gather.2.cloned.1.call-done = f32[512,512]{1,0:T(8,128)} async-done(((f32[64,512]{1,0:T(8,128)}), f32[512,512]{1,0:T(8,128)}) %all-gather.2.cloned.1.call-update) | async-done | bytes 1048592 | tf_op jit(solution)/shard_map/all_gather | solution.py:591
  275.4 4.0 %convolution_multiply_fusion = f32[512,512]{1,0:T(8,128)} fusion(f32[512,512]{1,0:T(8,128)S(1)} %copy-done.15, f32[512,512]{1,0:T(8,128)} %all-gather.2.cloned.1.call-done), kind=kOutput, calls=%fused_computation | convolution fusion | flops 1610874880 | bytes 3145728 | tf_op jit(solution)/shard_map/dot_general | solution.py:592
  (105 shorter events, 14.7 us)
Async XLA Ops:
  7.2 2.2 copy-start
  10.0 3.5 %copy-start.1 = (bf16[128,128,128]{2,1,0:T(8,128)(2,1)S(1)}, bf16[128,128,128]{2,1,0:T(8,128)(2,1)}, u32[]{:S(2)}) copy-start(bf16[128,128,128]{2,1,0:T(8,128)(2,1)} %param.4) | copy-start | bytes 12582916
  10.0 3.5 %copy-start.28 = (s32[128]{0:T(128)S(1)}, s32[128]{0:T(128)}, u32[]{:S(2)}) copy-start(s32[128]{0:T(128)} %refs_0_.3) | copy-start | bytes 1540
  13.5 4.0 %collective-permute-start.1 = (bf16[260,16,128]{2,1,0:T(8,128)(2,1)S(1)}, bf16[260,16,128]{2,1,0:T(8,128)(2,1)S(1)}, u32[]{:S(2)}, u32[]{:S(2)}) collective-permute-start(bf16[260,16,128]{2,1,0:T(8,128)(2,1)S(1)} %get-tuple-element.54), channel_id=1, source_target_pairs={{0,4},{4,0},{8,12},{12,8},{16,20},{20,16},{24,28},{28,24},{1,5},{5... | collective-permute-start | bytes 3194888 | tf_op jit(solution)/shard_map/ppermute | solution.py:515
  16.9 5.1 %collective-permute-start.8 = (bf16[256,16,128]{2,1,0:T(8,128)(2,1)S(1)}, bf16[256,16,128]{2,1,0:T(8,128)(2,1)S(1)}, u32[]{:S(2)}, u32[]{:S(2)}) collective-permute-start(bf16[256,16,128]{2,1,0:T(8,128)(2,1)S(1)} %get-tuple-element.63), channel_id=1, source_target_pairs={{0,4},{4,0},{8,12},{12,8},{16,20},{20,16},{24,28},{28,24},{1,5},{5... | collective-permute-start | bytes 3145736 | tf_op jit(solution)/shard_map/ppermute | solution.py:515
  17.0 6.1 %collective-permute-start = (bf16[256,16,128]{2,1,0:T(8,128)(2,1)S(1)}, bf16[256,16,128]{2,1,0:T(8,128)(2,1)S(1)}, u32[]{:S(2)}, u32[]{:S(2)}) collective-permute-start(bf16[256,16,128]{2,1,0:T(8,128)(2,1)S(1)} %get-tuple-element.50), channel_id=1, source_target_pairs={{0,4},{4,0},{8,12},{12,8},{16,20},{20,16},{24,28},{28,24},{1,5},{5... | collective-permute-start | bytes 3145736 | tf_op jit(solution)/shard_map/ppermute | solution.py:515
  17.6 15.2 %collective-permute-start.2 = (bf16[130,16,128]{2,1,0:T(8,128)(2,1)S(1)}, bf16[130,16,128]{2,1,0:T(8,128)(2,1)S(1)}, u32[]{:S(2)}, u32[]{:S(2)}) collective-permute-start(bf16[130,16,128]{2,1,0:T(8,128)(2,1)S(1)} %get-tuple-element.56), channel_id=1, source_target_pairs={{0,8},{4,12},{8,0},{12,4},{16,24},{20,28},{24,16},{28,20},{1,9},{5... | collective-permute-start | bytes 1597448 | tf_op jit(solution)/shard_map/ppermute | solution.py:515
  20.0 24.0 %collective-permute-start.3 = (bf16[130,16,128]{2,1,0:T(8,128)(2,1)S(1)}, bf16[130,16,128]{2,1,0:T(8,128)(2,1)S(1)}, u32[]{:S(2)}, u32[]{:S(2)}) collective-permute-start(bf16[130,16,128]{2,1,0:T(8,128)(2,1)S(1)} %get-tuple-element.57), channel_id=1, source_target_pairs={{0,16},{4,20},{8,24},{12,28},{16,0},{20,4},{24,8},{28,12},{1,17},{... | collective-permute-start | bytes 1597448 | tf_op jit(solution)/shard_map/ppermute | solution.py:515
  21.1 25.4 %collective-permute-start.4 = (bf16[130,16,128]{2,1,0:T(8,128)(2,1)S(1)}, bf16[130,16,128]{2,1,0:T(8,128)(2,1)S(1)}, u32[]{:S(2)}, u32[]{:S(2)}) collective-permute-start(bf16[130,16,128]{2,1,0:T(8,128)(2,1)S(1)} %get-tuple-element.58), channel_id=1, source_target_pairs={{0,24},{4,28},{8,16},{12,20},{16,8},{20,12},{24,0},{28,4},{1,25},{... | collective-permute-start | bytes 1597448 | tf_op jit(solution)/shard_map/ppermute | solution.py:515
  22.0 79.0 %collective-permute-start.21 = (bf16[256,16,128]{2,1,0:T(8,128)(2,1)S(1)}, bf16[256,16,128]{2,1,0:T(8,128)(2,1)S(1)}, u32[]{:S(2)}, u32[]{:S(2)}) collective-permute-start(bf16[256,16,128]{2,1,0:T(8,128)(2,1)S(1)} %get-tuple-element.79), channel_id=1, source_target_pairs={{0,4},{4,0},{8,12},{12,8},{16,20},{20,16},{24,28},{28,24},{1,5},{5... | collective-permute-start | bytes 3145736 | tf_op jit(solution)/shard_map/ppermute | solution.py:515
  23.1 32.4 %collective-permute-start.9 = (bf16[128,16,128]{2,1,0:T(8,128)(2,1)S(1)}, bf16[128,16,128]{2,1,0:T(8,128)(2,1)S(1)}, u32[]{:S(2)}, u32[]{:S(2)}) collective-permute-start(bf16[128,16,128]{2,1,0:T(8,128)(2,1)S(1)} %get-tuple-element.64), channel_id=1, source_target_pairs={{0,8},{4,12},{8,0},{12,4},{16,24},{20,28},{24,16},{28,20},{1,9},{5... | collective-permute-start | bytes 1572872 | tf_op jit(solution)/shard_map/ppermute | solution.py:515
  32.9 33.9 %collective-permute-start.10 = (bf16[128,16,128]{2,1,0:T(8,128)(2,1)S(1)}, bf16[128,16,128]{2,1,0:T(8,128)(2,1)S(1)}, u32[]{:S(2)}, u32[]{:S(2)}) collective-permute-start(bf16[128,16,128]{2,1,0:T(8,128)(2,1)S(1)} %get-tuple-element.66), channel_id=1, source_target_pairs={{0,8},{4,12},{8,0},{12,4},{16,24},{20,28},{24,16},{28,20},{1,9},{5... | collective-permute-start | bytes 1572872 | tf_op jit(solution)/shard_map/ppermute | solution.py:515
  44.0 26.6 %collective-permute-start.11 = (bf16[128,16,128]{2,1,0:T(8,128)(2,1)S(1)}, bf16[128,16,128]{2,1,0:T(8,128)(2,1)S(1)}, u32[]{:S(2)}, u32[]{:S(2)}) collective-permute-start(bf16[128,16,128]{2,1,0:T(8,128)(2,1)S(1)} %get-tuple-element.67), channel_id=1, source_target_pairs={{0,16},{4,20},{8,24},{12,28},{16,0},{20,4},{24,8},{28,12},{1,17},{... | collective-permute-start | bytes 1572872 | tf_op jit(solution)/shard_map/ppermute | solution.py:515
  46.5 33.1 %collective-permute-start.12 = (bf16[128,16,128]{2,1,0:T(8,128)(2,1)S(1)}, bf16[128,16,128]{2,1,0:T(8,128)(2,1)S(1)}, u32[]{:S(2)}, u32[]{:S(2)}) collective-permute-start(bf16[128,16,128]{2,1,0:T(8,128)(2,1)S(1)} %get-tuple-element.68), channel_id=1, source_target_pairs={{0,24},{4,28},{8,16},{12,20},{16,8},{20,12},{24,0},{28,4},{1,25},{... | collective-permute-start | bytes 1572872 | tf_op jit(solution)/shard_map/ppermute | solution.py:515
  50.6 66.2 %copy-start.20 = (bf16[64,16,128]{2,1,0:T(8,128)(2,1)}, bf16[64,16,128]{2,1,0:T(8,128)(2,1)S(1)}, u32[]{:S(2)}) copy-start(bf16[64,16,128]{2,1,0:T(8,128)(2,1)S(1)} %get-tuple-element.59.refs_1_.refs_0_) | copy-start | bytes 786436
  55.6 24.0 %collective-permute-start.5 = (bf16[64,16,128]{2,1,0:T(8,128)(2,1)S(1)}, bf16[64,16,128]{2,1,0:T(8,128)(2,1)S(1)}, u32[]{:S(2)}, u32[]{:S(2)}) collective-permute-start(bf16[64,16,128]{2,1,0:T(8,128)(2,1)S(1)} %get-tuple-element.60), channel_id=1, source_target_pairs={{0,1},{1,0},{2,3},{3,2},{4,5},{5,4},{6,7},{7,6},{8,9},{9,8},{10,11... | collective-permute-start | bytes 786440 | tf_op jit(solution)/shard_map/ppermute | solution.py:515
  66.8 21.1 %collective-permute-start.6 = (bf16[64,16,128]{2,1,0:T(8,128)(2,1)S(1)}, bf16[64,16,128]{2,1,0:T(8,128)(2,1)S(1)}, u32[]{:S(2)}, u32[]{:S(2)}) collective-permute-start(bf16[64,16,128]{2,1,0:T(8,128)(2,1)S(1)} %get-tuple-element.61), channel_id=1, source_target_pairs={{0,2},{1,3},{2,0},{3,1},{4,6},{5,7},{6,4},{7,5},{8,10},{9,11},{10,... | collective-permute-start | bytes 786440 | tf_op jit(solution)/shard_map/ppermute | solution.py:515
  70.6 17.3 %collective-permute-start.7 = (bf16[64,16,128]{2,1,0:T(8,128)(2,1)S(1)}, bf16[64,16,128]{2,1,0:T(8,128)(2,1)S(1)}, u32[]{:S(2)}, u32[]{:S(2)}) collective-permute-start(bf16[64,16,128]{2,1,0:T(8,128)(2,1)S(1)} %get-tuple-element.62), channel_id=1, source_target_pairs={{0,3},{1,2},{2,1},{3,0},{4,7},{5,6},{6,5},{7,4},{8,11},{9,10},{10,... | collective-permute-start | bytes 786440 | tf_op jit(solution)/shard_map/ppermute | solution.py:515
  90.3 29.5 %copy-start.16 = (bf16[64,16,128]{2,1,0:T(8,128)(2,1)}, bf16[64,16,128]{2,1,0:T(8,128)(2,1)S(1)}, u32[]{:S(2)}) copy-start(bf16[64,16,128]{2,1,0:T(8,128)(2,1)S(1)} %get-tuple-element.86.refs_5_.refs_2_) | copy-start | bytes 786436
  90.3 17.1 %collective-permute-start.13 = (bf16[64,16,128]{2,1,0:T(8,128)(2,1)S(1)}, bf16[64,16,128]{2,1,0:T(8,128)(2,1)S(1)}, u32[]{:S(2)}, u32[]{:S(2)}) collective-permute-start(bf16[64,16,128]{2,1,0:T(8,128)(2,1)S(1)} %get-tuple-element.69), channel_id=1, source_target_pairs={{0,1},{1,0},{2,3},{3,2},{4,5},{5,4},{6,7},{7,6},{8,9},{9,8},{10,11... | collective-permute-start | bytes 786440 | tf_op jit(solution)/shard_map/ppermute | solution.py:515
  95.5 21.3 %collective-permute-start.14 = (bf16[64,16,128]{2,1,0:T(8,128)(2,1)S(1)}, bf16[64,16,128]{2,1,0:T(8,128)(2,1)S(1)}, u32[]{:S(2)}, u32[]{:S(2)}) collective-permute-start(bf16[64,16,128]{2,1,0:T(8,128)(2,1)S(1)} %get-tuple-element.70), channel_id=1, source_target_pairs={{0,2},{1,3},{2,0},{3,1},{4,6},{5,7},{6,4},{7,5},{8,10},{9,11},{10,... | collective-permute-start | bytes 786440 | tf_op jit(solution)/shard_map/ppermute | solution.py:515
  97.5 19.3 %collective-permute-start.15 = (bf16[64,16,128]{2,1,0:T(8,128)(2,1)S(1)}, bf16[64,16,128]{2,1,0:T(8,128)(2,1)S(1)}, u32[]{:S(2)}, u32[]{:S(2)}) collective-permute-start(bf16[64,16,128]{2,1,0:T(8,128)(2,1)S(1)} %get-tuple-element.71), channel_id=1, source_target_pairs={{0,3},{1,2},{2,1},{3,0},{4,7},{5,6},{6,5},{7,4},{8,11},{9,10},{10,... | collective-permute-start | bytes 786440 | tf_op jit(solution)/shard_map/ppermute | solution.py:515
  98.8 27.0 %collective-permute-start.16 = (bf16[128,16,128]{2,1,0:T(8,128)(2,1)}, bf16[128,16,128]{2,1,0:T(8,128)(2,1)}, u32[]{:S(2)}, u32[]{:S(2)}) collective-permute-start(bf16[128,16,128]{2,1,0:T(8,128)(2,1)} %get-tuple-element.73), channel_id=1, source_target_pairs={{0,16},{4,20},{8,24},{12,28},{16,0},{20,4},{24,8},{28,12},{1,17},{... | collective-permute-start | bytes 1572872 | tf_op jit(solution)/shard_map/ppermute | solution.py:515
  101.0 24.9 %collective-permute-start.17 = (bf16[128,16,128]{2,1,0:T(8,128)(2,1)}, bf16[128,16,128]{2,1,0:T(8,128)(2,1)}, u32[]{:S(2)}, u32[]{:S(2)}) collective-permute-start(bf16[128,16,128]{2,1,0:T(8,128)(2,1)} %get-tuple-element.74), channel_id=1, source_target_pairs={{0,24},{4,28},{8,16},{12,20},{16,8},{20,12},{24,0},{28,4},{1,25},{... | collective-permute-start | bytes 1572872 | tf_op jit(solution)/shard_map/ppermute | solution.py:515
  102.6 17.2 %copy-start.23 = (bf16[128,16,128]{2,1,0:T(8,128)(2,1)}, bf16[128,16,128]{2,1,0:T(8,128)(2,1)S(1)}, u32[]{:S(2)}) copy-start(bf16[128,16,128]{2,1,0:T(8,128)(2,1)S(1)} %get-tuple-element.80.refs_4_.refs_0_) | copy-start | bytes 1572868
  102.6 17.2 %copy-start.29 = (bf16[128,16,128]{2,1,0:T(8,128)(2,1)}, bf16[128,16,128]{2,1,0:T(8,128)(2,1)S(1)}, u32[]{:S(2)}) copy-start(bf16[128,16,128]{2,1,0:T(8,128)(2,1)S(1)} %get-tuple-element.81) | copy-start | bytes 1572868
  119.8 18.6 %all-to-all-start = ((f32[8,160,128]{2,1,0:T(8,128)}), f32[8,160,128]{2,1,0:T(8,128)}, u32[]{:S(2)}, u32[]{:S(2)}) async-start(f32[8,160,128]{2,1,0:T(8,128)} %bitcast.2), calls=%async_computation | async-start | bytes 1310720 | tf_op jit(solution)/shard_map/all_to_all | solution.py:545
  124.0 26.5 %collective-permute-start.22 = (bf16[128,16,128]{2,1,0:T(8,128)(2,1)}, bf16[128,16,128]{2,1,0:T(8,128)(2,1)S(1)}, u32[]{:S(2)}, u32[]{:S(2)}) collective-permute-start(bf16[128,16,128]{2,1,0:T(8,128)(2,1)} %copy-done.29), channel_id=1, source_target_pairs={{0,8},{4,12},{8,0},{12,4},{16,24},{20,28},{24,16},{28,20},{1,9},{5... | collective-permute-start | bytes 1572872 | tf_op jit(solution)/shard_map/ppermute | solution.py:515
  131.7 12.3 %collective-permute-start.18 = (bf16[64,16,128]{2,1,0:T(8,128)(2,1)}, bf16[64,16,128]{2,1,0:T(8,128)(2,1)S(1)}, u32[]{:S(2)}, u32[]{:S(2)}) collective-permute-start(bf16[64,16,128]{2,1,0:T(8,128)(2,1)} %get-tuple-element.75), channel_id=1, source_target_pairs={{0,1},{1,0},{2,3},{3,2},{4,5},{5,4},{6,7},{7,6},{8,9},{9,8},{10,11... | collective-permute-start | bytes 786440 | tf_op jit(solution)/shard_map/ppermute | solution.py:515
  136.6 24.9 %collective-permute-start.23 = (bf16[128,16,128]{2,1,0:T(8,128)(2,1)}, bf16[128,16,128]{2,1,0:T(8,128)(2,1)S(1)}, u32[]{:S(2)}, u32[]{:S(2)}) collective-permute-start(bf16[128,16,128]{2,1,0:T(8,128)(2,1)} %get-tuple-element.82), channel_id=1, source_target_pairs={{0,16},{4,20},{8,24},{12,28},{16,0},{20,4},{24,8},{28,12},{1,17},{... | collective-permute-start | bytes 1572872 | tf_op jit(solution)/shard_map/ppermute | solution.py:515
  138.1 23.4 %collective-permute-start.24 = (bf16[128,16,128]{2,1,0:T(8,128)(2,1)}, bf16[128,16,128]{2,1,0:T(8,128)(2,1)}, u32[]{:S(2)}, u32[]{:S(2)}) collective-permute-start(bf16[128,16,128]{2,1,0:T(8,128)(2,1)} %get-tuple-element.83), channel_id=1, source_target_pairs={{0,24},{4,28},{8,16},{12,20},{16,8},{20,12},{24,0},{28,4},{1,25},{... | collective-permute-start | bytes 1572872 | tf_op jit(solution)/shard_map/ppermute | solution.py:515
  140.1 7.6 %collective-permute-start.25 = (f32[160,128]{1,0:T(8,128)}, f32[160,128]{1,0:T(8,128)S(1)}, u32[]{:S(2)}, u32[]{:S(2)}) collective-permute-start(f32[160,128]{1,0:T(8,128)} %sum_pieces.2.refs_1_), channel_id=1, source_target_pairs={{0,1},{1,0},{2,3},{3,2},{4,5},{5,4},{6,7},{7,6},{8,9},{9,8},{10,11... | collective-permute-start | bytes 245768 | tf_op jit(solution)/shard_map/ppermute | solution.py:515
  144.0 4.9 %copy-start.6 = (bf16[64,16,128]{2,1,0:T(8,128)(2,1)}, bf16[64,16,128]{2,1,0:T(8,128)(2,1)S(1)}, u32[]{:S(2)}) copy-start(bf16[64,16,128]{2,1,0:T(8,128)(2,1)S(1)} %collective-permute-done.18.refs_0_.refs_10_) | copy-start | bytes 786436
  144.0 22.7 %collective-permute-start.19 = (bf16[64,16,128]{2,1,0:T(8,128)(2,1)}, bf16[64,16,128]{2,1,0:T(8,128)(2,1)S(1)}, u32[]{:S(2)}, u32[]{:S(2)}) collective-permute-start(bf16[64,16,128]{2,1,0:T(8,128)(2,1)} %copy-done.31), channel_id=1, source_target_pairs={{0,2},{1,3},{2,0},{3,1},{4,6},{5,7},{6,4},{7,5},{8,10},{9,11},{10,... | collective-permute-start | bytes 786440 | tf_op jit(solution)/shard_map/ppermute | solution.py:515
  147.7 1.1 copy-start.35
  147.7 19.0 %collective-permute-start.20 = (bf16[64,16,128]{2,1,0:T(8,128)(2,1)}, bf16[64,16,128]{2,1,0:T(8,128)(2,1)S(1)}, u32[]{:S(2)}, u32[]{:S(2)}) collective-permute-start(bf16[64,16,128]{2,1,0:T(8,128)(2,1)} %copy-done.30), channel_id=1, source_target_pairs={{0,3},{1,2},{2,1},{3,0},{4,7},{5,6},{6,5},{7,4},{8,11},{9,10},{10,... | collective-permute-start | bytes 786440 | tf_op jit(solution)/shard_map/ppermute | solution.py:515
  150.5 30.6 %copy-start.11 = (bf16[128,16,128]{2,1,0:T(8,128)(2,1)}, bf16[128,16,128]{2,1,0:T(8,128)(2,1)S(1)}, u32[]{:S(2)}) copy-start(bf16[128,16,128]{2,1,0:T(8,128)(2,1)S(1)} %collective-permute-done.22.refs_5_.refs_2_) | copy-start | bytes 1572868
  150.5 30.6 %collective-permute-start.26 = (f32[160,128]{1,0:T(8,128)}, f32[160,128]{1,0:T(8,128)S(1)}, u32[]{:S(2)}, u32[]{:S(2)}) collective-permute-start(f32[160,128]{1,0:T(8,128)} %add.4.refs_5_), channel_id=1, source_target_pairs={{0,2},{1,3},{2,0},{3,1},{4,6},{5,7},{6,4},{7,5},{8,10},{9,11},{10,... | collective-permute-start | bytes 245768 | tf_op jit(solution)/shard_map/ppermute | solution.py:515
  161.5 19.5 %copy-start.12 = (bf16[128,16,128]{2,1,0:T(8,128)(2,1)}, bf16[128,16,128]{2,1,0:T(8,128)(2,1)S(1)}, u32[]{:S(2)}) copy-start(bf16[128,16,128]{2,1,0:T(8,128)(2,1)S(1)} %collective-permute-done.23.refs_6_.refs_3_) | copy-start | bytes 1572868
  166.7 14.3 %copy-start.2 = (bf16[64,16,128]{2,1,0:T(8,128)(2,1)}, bf16[64,16,128]{2,1,0:T(8,128)(2,1)S(1)}, u32[]{:S(2)}) copy-start(bf16[64,16,128]{2,1,0:T(8,128)(2,1)S(1)} %collective-permute-done.19.refs_1_.refs_0_.refs_11_) | copy-start | bytes 786436
  166.7 1.0 copy-start.7
  167.8 1.0 copy-start.24
  168.8 12.2 %copy-start.4 = (bf16[64,16,128]{2,1,0:T(8,128)(2,1)}, bf16[64,16,128]{2,1,0:T(8,128)(2,1)S(1)}, u32[]{:S(2)}) copy-start(bf16[64,16,128]{2,1,0:T(8,128)(2,1)S(1)} %collective-permute-done.20.refs_2_.refs_1_.refs_12_) | copy-start | bytes 786436
  172.6 25.9 %copy-start.25 = (bf16[64,16,128]{2,1,0:T(8,128)(2,1)}, bf16[64,16,128]{2,1,0:T(8,128)(2,1)S(1)}, u32[]{:S(2)}) copy-start(bf16[64,16,128]{2,1,0:T(8,128)(2,1)S(1)} %get-tuple-element.84.refs_0_.refs_13_) | copy-start | bytes 786436
  172.6 35.4 %collective-permute-start.27 = (bf16[64,16,128]{2,1,0:T(8,128)(2,1)}, bf16[64,16,128]{2,1,0:T(8,128)(2,1)}, u32[]{:S(2)}, u32[]{:S(2)}) collective-permute-start(bf16[64,16,128]{2,1,0:T(8,128)(2,1)} %get-tuple-element.87), channel_id=1, source_target_pairs={{0,1},{1,0},{2,3},{3,2},{4,5},{5,4},{6,7},{7,6},{8,9},{9,8},{10,11... | collective-permute-start | bytes 786440 | tf_op jit(solution)/shard_map/ppermute | solution.py:515
  178.3 29.9 %collective-permute-start.28 = (bf16[64,16,128]{2,1,0:T(8,128)(2,1)}, bf16[64,16,128]{2,1,0:T(8,128)(2,1)}, u32[]{:S(2)}, u32[]{:S(2)}) collective-permute-start(bf16[64,16,128]{2,1,0:T(8,128)(2,1)} %get-tuple-element.88), channel_id=1, source_target_pairs={{0,2},{1,3},{2,0},{3,1},{4,6},{5,7},{6,4},{7,5},{8,10},{9,11},{10,... | collective-permute-start | bytes 786440 | tf_op jit(solution)/shard_map/ppermute | solution.py:515
  179.6 28.6 %collective-permute-start.29 = (bf16[64,16,128]{2,1,0:T(8,128)(2,1)}, bf16[64,16,128]{2,1,0:T(8,128)(2,1)}, u32[]{:S(2)}, u32[]{:S(2)}) collective-permute-start(bf16[64,16,128]{2,1,0:T(8,128)(2,1)} %get-tuple-element.89), channel_id=1, source_target_pairs={{0,3},{1,2},{2,1},{3,0},{4,7},{5,6},{6,5},{7,4},{8,11},{9,10},{10,... | collective-permute-start | bytes 786440 | tf_op jit(solution)/shard_map/ppermute | solution.py:515
  203.3 4.9 %copy-start.3 = (bf16[64,16,128]{2,1,0:T(8,128)(2,1)S(1)}, bf16[64,16,128]{2,1,0:T(8,128)(2,1)}, u32[]{:S(2)}) copy-start(bf16[64,16,128]{2,1,0:T(8,128)(2,1)} %copy-done.2) | copy-start | bytes 786436
  203.3 4.9 %copy-start.5 = (bf16[64,16,128]{2,1,0:T(8,128)(2,1)S(1)}, bf16[64,16,128]{2,1,0:T(8,128)(2,1)}, u32[]{:S(2)}) copy-start(bf16[64,16,128]{2,1,0:T(8,128)(2,1)} %copy-done.4) | copy-start | bytes 786436
  203.3 4.9 %copy-start.8 = (bf16[64,16,128]{2,1,0:T(8,128)(2,1)S(1)}, bf16[64,16,128]{2,1,0:T(8,128)(2,1)}, u32[]{:S(2)}) copy-start(bf16[64,16,128]{2,1,0:T(8,128)(2,1)} %copy-done.6) | copy-start | bytes 786436
  203.3 4.9 %copy-start.17 = (bf16[64,16,128]{2,1,0:T(8,128)(2,1)S(1)}, bf16[64,16,128]{2,1,0:T(8,128)(2,1)}, u32[]{:S(2)}) copy-start(bf16[64,16,128]{2,1,0:T(8,128)(2,1)} %copy-done.16) | copy-start | bytes 786436
  203.3 4.9 %copy-start.19 = (bf16[64,16,128]{2,1,0:T(8,128)(2,1)S(1)}, bf16[64,16,128]{2,1,0:T(8,128)(2,1)}, u32[]{:S(2)}) copy-start(bf16[64,16,128]{2,1,0:T(8,128)(2,1)} %copy-done.18) | copy-start | bytes 786436
  203.3 4.9 %copy-start.21 = (bf16[64,16,128]{2,1,0:T(8,128)(2,1)S(1)}, bf16[64,16,128]{2,1,0:T(8,128)(2,1)}, u32[]{:S(2)}) copy-start(bf16[64,16,128]{2,1,0:T(8,128)(2,1)} %copy-done.20) | copy-start | bytes 786436
  203.4 4.9 %copy-start.26 = (bf16[64,16,128]{2,1,0:T(8,128)(2,1)S(1)}, bf16[64,16,128]{2,1,0:T(8,128)(2,1)}, u32[]{:S(2)}) copy-start(bf16[64,16,128]{2,1,0:T(8,128)(2,1)} %copy-done.25) | copy-start | bytes 786436
  207.9 5.0 %copy-start.9 = (f32[4,8,128,128]{3,2,1,0:T(8,128)}, f32[4,8,128,128]{3,2,1,0:T(8,128)S(1)}, u32[]{:S(2)}) copy-start(f32[4,8,128,128]{3,2,1,0:T(8,128)S(1)} %factor.6.refs_0_.refs_1_) | copy-start | bytes 6291460
  213.0 19.7 %all-to-all-start.1 = ((f32[8,64,512]{2,1,0:T(8,128)}), f32[8,64,512]{2,1,0:T(8,128)}, u32[]{:S(2)}, u32[]{:S(2)}) async-start(f32[8,64,512]{2,1,0:T(8,128)} %bitcast.5), calls=%async_computation.1 | async-start | bytes 2097152 | tf_op jit(solution)/shard_map/all_to_all | solution.py:545
  217.2 58.2 %all-gather.2.cloned.1.call-start = ((), (), s32[]{:S(2)}) async-start(), calls=%async_computation.2 | async-start | bytes 1179648 | tf_op jit(solution)/shard_map/all_gather | solution.py:591
  217.2 1.6 copy-start.10
  218.8 6.4 %copy-start.22 = (bf16[64,16,128]{2,1,0:T(8,128)(2,1)S(1)}, bf16[64,16,128]{2,1,0:T(8,128)(2,1)}, u32[]{:S(2)}) copy-start(bf16[64,16,128]{2,1,0:T(8,128)(2,1)} %copy-done.20) | copy-start | bytes 786436
  224.2 1.0 copy-start.14
  234.5 5.2 %collective-permute-start.30 = (f32[64,512]{1,0:T(8,128)}, f32[64,512]{1,0:T(8,128)S(1)}, u32[]{:S(2)}, u32[]{:S(2)}) collective-permute-start(f32[64,512]{1,0:T(8,128)} %sum_pieces.3.refs_1_), channel_id=1, source_target_pairs={{0,1},{1,0},{2,3},{3,2},{4,5},{5,4},{6,7},{7,6},{8,9},{9,8},{10,11... | collective-permute-start | bytes 393224 | tf_op jit(solution)/shard_map/ppermute | solution.py:515
  235.3 0.9 copy-start.13
  239.7 35.7 %copy-start.15 = (f32[512,512]{1,0:T(8,128)S(1)}, f32[512,512]{1,0:T(8,128)}, u32[]{:S(2)}) copy-start(f32[512,512]{1,0:T(8,128)} %copy-done.14) | copy-start | bytes 3145732
  242.0 7.5 %collective-permute-start.31 = (f32[64,512]{1,0:T(8,128)}, f32[64,512]{1,0:T(8,128)S(1)}, u32[]{:S(2)}, u32[]{:S(2)}) collective-permute-start(f32[64,512]{1,0:T(8,128)} %add.6.refs_0_), channel_id=1, source_target_pairs={{0,2},{1,3},{2,0},{3,1},{4,6},{5,7},{6,4},{7,5},{8,10},{9,11},{10,... | collective-permute-start | bytes 393224 | tf_op jit(solution)/shard_map/ppermute | solution.py:515
  (7 other events, 4.7 us)
Sparse Core Ops, SparseCore 0:
  251.9 23.4 all-gather.1

commit v7 on v6

--- a/solution.py
+++ b/solution.py
@@ -120,7 +120,7 @@
     )(same, other)
 
 
-def settle_kernel(chips, capacity, first, *refs):
+def settle_kernel(chips, capacity, first, joint, *refs):
     if first:
         moved_refs, out_refs, meta_ref, ids_ref = refs[:chips], refs[chips:-2], refs[-2], refs[-1]
         span = moved_refs[0].shape[0] // CORES
@@ -132,7 +132,7 @@
     else:
         meta_ref, moved_refs, out_refs = refs[0], refs[1 : 1 + chips], refs[1 + chips :]
         span = moved_refs[0].shape[0] // CORES
-    shares = len(out_refs)
+    shares = out_refs[0].shape[0] if joint else len(out_refs)
     mine = lax.axis_index("snap")
     for source in range(chips * CORES):
         moved_ref = moved_refs[source // CORES]
@@ -143,25 +143,31 @@
             @pl.when(block >= 0)
             def _():
                 at = source % CORES * span + rank * shares
-                for r in range(shares):
-                    out_refs[r][block] = moved_ref[at + (mine ^ r)]
+                if joint:
+                    out_refs[0][:, block] = moved_ref[pl.ds(at, shares)]
+                else:
+                    for r in range(shares):
+                        out_refs[r][block] = moved_ref[at + (mine ^ r)]
 
             return 0
 
         lax.fori_loop(0, capacity, place, 0, unroll=4)
 
 
-def settle(meta, moved, capacity, per_slab, shares, after=()):
+def settle(meta, moved, capacity, per_slab, shares, joint, after=()):
     first = meta is None
     chips = len(moved)
     rows, width = moved[0].shape[1:]
-    pieces = (jax.ShapeDtypeStruct((per_slab, rows, width), moved[0].dtype),) * shares
+    if joint:
+        pieces = (jax.ShapeDtypeStruct((shares, per_slab, rows, width), moved[0].dtype),)
+    else:
+        pieces = (jax.ShapeDtypeStruct((per_slab, rows, width), moved[0].dtype),) * shares
     ids = jax.ShapeDtypeStruct((chips * CORES, TILE), jnp.int32)
     outs = pl.pallas_call(
-        lambda *refs: settle_kernel(chips, capacity, first, *refs[len(after) :]),
+        lambda *refs: settle_kernel(chips, capacity, first, joint, *refs[len(after) :]),
         out_shape=pieces + ((ids,) if first else ()),
         in_specs=[ANY] * len(after) + ([] if first else [SMEM]) + [VMEM] * chips,
-        out_specs=(VMEM,) * shares + ((SMEM,) if first else ()),
+        out_specs=(VMEM,) * len(pieces) + ((SMEM,) if first else ()),
         scratch_shapes=[pltpu.VMEM((chips * CORES, TILE), jnp.int32)] if first else [],
         compiler_params=pltpu.CompilerParams(vmem_limit_bytes=VMEM_BYTES),
         cost_estimate=cost(
@@ -169,7 +175,7 @@
         ),
         name="settle",
     )(*after, *([] if first else [meta]), *moved)
-    return outs[:shares], (outs[shares] if first else meta)
+    return outs[: len(pieces)], (outs[-1] if first else meta)
 
 
 def whole_rows(refs):
@@ -177,51 +183,44 @@
     return jnp.concatenate([ref[...].reshape(blocks * rows, width) for ref in refs], axis=1)
 
 
-def tile_of(row, lane, tiles):
-    return row * tiles - lax.div(row * (row - 1), 2) + lane - row
-
-
-def gram_kernel(parts, shares, *refs):
-    out_ref, acc_ref = refs[-2:]
-    step = pl.program_id(0)
-
-    @pl.when(step == 0)
+def joint_rows(ref):
+    return whole_rows([ref.at[share] for share in range(ref.shape[0])])
+
+
+def gram_kernel(parts, *refs):
+    out_ref = refs[-1]
+    shares = refs[0].shape[0]
+
+    @pl.when(pl.program_id(0) == 0)
     def _():
-        acc_ref[...] = jnp.zeros_like(acc_ref)
+        out_ref[...] = jnp.zeros_like(out_ref)
 
     for part in range(parts):
-        cells = whole_rows(refs[part * shares : (part + 1) * shares])
-        acc_ref[...] += lax.dot_general(
-            cells, cells, ROWS_BY_ROWS, preferred_element_type=jnp.float32
-        )
-
-    @pl.when(step == pl.num_programs(0) - 1)
-    def _():
-        mine = lax.axis_index("snap")
+        cells = joint_rows(refs[part])
+        at = 0
         for a in range(shares):
-            for b in range(shares):
-                row, lane = mine ^ a, mine ^ b
-
-                @pl.when(row <= lane)
-                def _():
-                    out_ref[tile_of(row, lane, shares)] = acc_ref[
-                        a * TILE : (a + 1) * TILE, b * TILE : (b + 1) * TILE
-                    ]
+            product = lax.dot_general(
+                cells[:, a * TILE : (a + 1) * TILE],
+                cells[:, a * TILE :],
+                ROWS_BY_ROWS,
+                preferred_element_type=jnp.float32,
+            )
+            for b in range(a, shares):
+                out_ref[at] += product[:, (b - a) * TILE : (b - a + 1) * TILE]
+                at += 1
 
 
 def gram_blocks(cells, after, steps=4):
-    shares = len(cells[0])
-    blocks, rows, width = cells[0][0].shape
+    shares, blocks, rows, width = cells[0].shape
     pairs = shares * (shares + 1) // 2
     full = shares * width
-    spec = pl.BlockSpec((blocks // steps, rows, width), lambda i: (i, 0, 0))
-    return pl.pallas_call(
-        lambda *refs: gram_kernel(len(cells), shares, *refs[len(after) :]),
+    spec = pl.BlockSpec((shares, blocks // steps, rows, width), lambda i: (0, i, 0, 0))
+    return pl.pallas_call(
+        lambda *refs: gram_kernel(len(cells), *refs[len(after) :]),
         grid=(steps,),
         out_shape=jax.ShapeDtypeStruct((pairs, TILE, TILE), jnp.float32),
-        in_specs=[ANY] * len(after) + [spec] * (len(cells) * shares),
+        in_specs=[ANY] * len(after) + [spec] * len(cells),
         out_specs=pl.BlockSpec((pairs, TILE, TILE), lambda i: (0, 0, 0)),
-        scratch_shapes=[pltpu.VMEM((full, full), jnp.float32)],
         compiler_params=pltpu.CompilerParams(vmem_limit_bytes=VMEM_BYTES),
         cost_estimate=cost(
             flops=2 * len(cells) * blocks * rows * full * full,
@@ -229,7 +228,7 @@
             transcendentals=0,
         ),
         name="gram_blocks",
-    )(*after, *[piece for part in cells for piece in part])
+    )(*after, *cells)
 
 
 def cross_kernel(parts, shares, *refs):
@@ -241,34 +240,33 @@
         acc_ref[...] = jnp.zeros_like(acc_ref)
 
     for part in range(parts):
-        x_refs = refs[part * shares : (part + 1) * shares]
-        y_refs = refs[(parts + part) * shares : (parts + part + 1) * shares]
+        y_refs = refs[parts + part * shares : parts + (part + 1) * shares]
         acc_ref[...] += lax.dot_general(
-            whole_rows(x_refs), whole_rows(y_refs), ROWS_BY_ROWS, preferred_element_type=jnp.float32
+            joint_rows(refs[part]),
+            whole_rows(y_refs),
+            ROWS_BY_ROWS,
+            preferred_element_type=jnp.float32,
         )
 
     @pl.when(step == pl.num_programs(0) - 1)
     def _():
         mine = lax.axis_index("snap")
-        for a in range(shares):
-            rows = pl.ds(pl.multiple_of((mine ^ a) * TILE, TILE), TILE)
-            for b in range(shares):
-                lanes = pl.ds(pl.multiple_of((mine ^ b) * TILE, TILE), TILE)
-                out_ref[rows, lanes] = acc_ref[
-                    a * TILE : (a + 1) * TILE, b * TILE : (b + 1) * TILE
-                ]
+        for b in range(shares):
+            lanes = pl.ds(pl.multiple_of((mine ^ b) * TILE, TILE), TILE)
+            out_ref[:, lanes] = acc_ref[:, b * TILE : (b + 1) * TILE]
 
 
 def cross_sum(x_cells, y_cells, after, steps=4):
-    parts, shares = len(x_cells), len(x_cells[0])
-    blocks, rows, width = x_cells[0][0].shape
+    parts = len(x_cells)
+    shares, blocks, rows, width = x_cells[0].shape
     spec = pl.BlockSpec((blocks // steps, rows, width), lambda i: (i, 0, 0))
+    joint = pl.BlockSpec((shares, blocks // steps, rows, width), lambda i: (0, i, 0, 0))
     full = shares * width
     return pl.pallas_call(
         lambda *refs: cross_kernel(parts, shares, *refs[len(after) :]),
         grid=(steps,),
         out_shape=jax.ShapeDtypeStruct((full, full), jnp.float32),
-        in_specs=[ANY] * len(after) + [spec] * (2 * parts * shares),
+        in_specs=[ANY] * len(after) + [joint] * parts + [spec] * (parts * shares),
         out_specs=pl.BlockSpec((full, full), lambda i: (0, 0)),
         scratch_shapes=[pltpu.VMEM((full, full), jnp.float32)],
         compiler_params=pltpu.CompilerParams(vmem_limit_bytes=VMEM_BYTES),
@@ -278,7 +276,7 @@
             transcendentals=0,
         ),
         name="cross_sum",
-    )(*after, *[piece for part in list(x_cells) + list(y_cells) for piece in part])
+    )(*after, *x_cells, *[piece for part in y_cells for piece in part])
 
 
 def three_terms(value):
@@ -387,7 +385,6 @@
 def last_kernel(tiles, wide, r_ref, inv_ref, hi_ref, mid_ref, lo_ref, *scratch):
     factor_step(tiles, tiles - 1, wide, *scratch)
     zero = jnp.zeros((TILE, TILE), jnp.float32)
-    mine = lax.axis_index("snap")
     for a in range(tiles):
         rows = slice(a * TILE, (a + 1) * TILE)
         for b in range(tiles):
@@ -396,7 +393,6 @@
             value = wide[a, tiles + b] if b <= a else zero
             inv_ref[rows, lanes] = value
             high, middle, low = three_terms(value)
-            lanes = pl.ds(pl.multiple_of((mine ^ b) * TILE, TILE), TILE)
             hi_ref[rows, lanes] = high.astype(jnp.bfloat16)
             mid_ref[rows, lanes] = middle.astype(jnp.bfloat16)
             lo_ref[rows, lanes] = low.astype(jnp.bfloat16)
@@ -439,7 +435,7 @@
 
 def basis_kernel(*refs):
     hi_ref, mid_ref, lo_ref, out_ref = refs[-4:]
-    cells = whole_rows(refs[:-4])
+    cells = joint_rows(refs[0])
     total = lax.dot_general(
         cells, lo_ref[...], LANES_BY_LANES, preferred_element_type=jnp.float32
     )
@@ -453,17 +449,16 @@
 
 
 def basis(cells, terms, part, parts, filled, after, steps=4):
-    shares = len(cells)
-    blocks, rows, width = cells[0].shape
+    shares, blocks, rows, width = cells.shape
     full = shares * width
-    spec = pl.BlockSpec((blocks // steps, rows, width), lambda i: (i, 0, 0))
+    spec = pl.BlockSpec((shares, blocks // steps, rows, width), lambda i: (0, i, 0, 0))
     term = pl.BlockSpec((full, full), lambda i: (0, 0))
     unread = ([] if filled is None else [filled]) + list(after)
     return pl.pallas_call(
         lambda *refs: basis_kernel(*refs[len(unread) :]),
         grid=(steps,),
         out_shape=jax.ShapeDtypeStruct((blocks, parts, rows, full), jnp.float32),
-        in_specs=[ANY] * len(unread) + [spec] * shares + [term] * 3,
+        in_specs=[ANY] * len(unread) + [spec] + [term] * 3,
         out_specs=pl.BlockSpec((blocks // steps, 1, rows, full), lambda i: (i, part, 0, 0)),
         input_output_aliases={} if filled is None else {0: 0},
         compiler_params=pltpu.CompilerParams(vmem_limit_bytes=VMEM_BYTES),
@@ -473,7 +468,7 @@
             transcendentals=0,
         ),
         name="basis",
-    )(*unread, *cells, *terms)
+    )(*unread, cells, *terms)
 
 
 def sum_kernel(count, value_ref, out_ref):
@@ -509,6 +504,53 @@
         cost_estimate=cost(flops=one.size, bytes_accessed=12 * one.size, transcendentals=0),
         name="add",
     )(*after, one, two)
+
+
+def join_kernel(*refs):
+    rows = refs[0].shape[0]
+    for i, ref in enumerate(refs[:-1]):
+        refs[-1][i * rows : (i + 1) * rows] = ref[...]
+
+
+def join(values):
+    rows, lanes = values[0].shape
+    return pl.pallas_call(
+        join_kernel,
+        out_shape=jax.ShapeDtypeStruct((len(values) * rows, lanes), values[0].dtype),
+        in_specs=[VMEM] * len(values),
+        out_specs=VMEM,
+        name="join",
+    )(*values)
+
+
+def projection_kernel(slabs, divisor, inverse_ref, same_ref, other_ref, out_ref, cross_ref):
+    me = lax.axis_index("space")
+    rows = cross_ref.shape[0] // slabs
+    for away in range(slabs):
+        at = pl.ds(pl.multiple_of((me ^ away) * rows, rows), rows)
+        chip = slice(away // CORES * rows, (away // CORES + 1) * rows)
+        cross_ref[at, :] = (other_ref if away % CORES else same_ref)[chip]
+    out_ref[...] = (
+        lax.dot(
+            inverse_ref[...],
+            cross_ref[...],
+            precision=HIGHEST,
+            preferred_element_type=jnp.float32,
+        )
+        / divisor
+    )
+
+
+def project(inverse, same, other, slabs, divisor):
+    return pl.pallas_call(
+        lambda *refs: projection_kernel(slabs, divisor, *refs),
+        out_shape=jax.ShapeDtypeStruct(inverse.shape, jnp.float32),
+        in_specs=[VMEM] * 3,
+        out_specs=VMEM,
+        scratch_shapes=[pltpu.VMEM(inverse.shape, jnp.float32)],
+        compiler_params=pltpu.CompilerParams(vmem_limit_bytes=VMEM_BYTES),
+        name="project",
+    )(inverse, same, other)
 
 
 def swap(value, axis, mask):
@@ -538,8 +580,8 @@
     def to_rows(pieces):
         return [pieces[0]] + [swap(pieces[r], "snap", r) for r in range(1, shares)]
 
-    def place(meta, moved, after):
-        return settle(meta, moved, slots // slabs, per_slab, shares, after)
+    def place(meta, moved, joint, after):
+        return settle(meta, moved, slots // slabs, per_slab, shares, joint, after)
 
     def to_pieces(value):
         return lax.all_to_all(value, "space", split_axis=0, concat_axis=0, tiled=True)
@@ -557,21 +599,25 @@
     joined_y = [merged(part) for part in sent_y]
     moved_y = [to_chips(joined) for joined in joined_y]
 
-    pieces, meta = place(None, moved_x[0], [joined[0] for joined in joined_x[1:]] + [sent_y[0][0]])
-    x_cells = [to_rows(pieces)]
+    def to_joint_rows(pieces):
+        return lax.all_to_all(pieces[0], "snap", split_axis=0, concat_axis=0, tiled=True)
+
+    after = [joined[0] for joined in joined_x[1:]] + [sent_y[0][0]]
+    pieces, meta = place(None, moved_x[0], True, after)
+    x_cells = [to_joint_rows(pieces)]
     for moved in moved_x[1:]:
-        pieces, _ = place(meta, moved, x_cells[-1][1:] + moved_y[0][1:2])
-        x_cells.append(to_rows(pieces))
+        pieces, _ = place(meta, moved, True, joined_y[0][:1])
+        x_cells.append(to_joint_rows(pieces))
     gram_local = gram_blocks(x_cells, [joined[0] for joined in joined_y[1:]])
     gram = to_pieces(gram_local.reshape(pairs * TILE, TILE))
-    pieces, _ = place(meta, moved_y[0], x_cells[-1][1:])
+    pieces, _ = place(meta, moved_y[0], False, [])
     y_cells = [to_rows(pieces)]
     gram = sum_pieces(gram, slabs, pieces[:1])
     for hop in hops():
-        gram = add(gram, swap(gram, "snap", hop), y_cells[0][1:2] if hop == 1 else y_cells[0][2:] + moved_y[1][1:])
+        gram = add(gram, swap(gram, "snap", hop), [])
     gram = lax.all_gather(gram, "space", axis=0, tiled=True)
     for moved in moved_y[1:]:
-        pieces, _ = place(meta, moved, y_cells[-1][1:])
+        pieces, _ = place(meta, moved, False, y_cells[-1][1:])
         y_cells.append(to_rows(pieces))
 
     steps = factor_steps(gram.reshape(pairs, TILE, TILE), tiles, rows_total, pieces[:1])
@@ -588,8 +634,8 @@
         q_basis = basis(x_cells[part], terms, part, parts, q_basis, [cross])
     for hop in hops():
         cross = add(cross, swap(cross, "snap", hop), [q_basis] if hop == 1 else [])
-    cross = lax.all_gather(cross, "space", axis=0, tiled=True)
-    projection = jnp.dot(inverse, cross, precision=HIGHEST) / math.sqrt(rows_total)
+    same = join([cross] + [swap(cross, "space", m) for m in range(CORES, slabs, CORES)])
+    projection = project(inverse, same, swap(same, "space", 1), slabs, math.sqrt(rows_total))
     return q_basis.reshape(per_slab, patch // shares, full), r_factor, projection
 
 

time: 288 us -> 284 us (0.986)
  starting transfers between devices: 69.1 us -> 51.8 us
  waiting for transfers between devices: 110 us -> 125 us
  between operations: 14.4 us -> 1.15 us
  local copies, waits for them, and re-layouts: 12.5 us -> 24.2 us
  matrix products: 4.04 us -> 0 us
    ppermute x32 -> x30, starting transfers between devices: 60.6 us -> 33.3 us  [swap(): lax.ppermute(value, axis, [(i, i ^ mask) for i in range(lax.axis_size(axi...]
    all_gather x1 -> x0, waiting for transfers between devices: 23.6 us -> none  [body(): cross = lax.all_gather(cross, 'space', axis=0, tiled=True)]
    ppermute x32 -> x30, waiting for transfers between devices: 82 us -> 103 us  [swap(): lax.ppermute(value, axis, [(i, i ^ mask) for i in range(lax.axis_size(axi...]
    all_to_all x0 -> x2, waiting for transfers between devices: none -> 19.4 us  [to_joint_rows(): lax.all_to_all(pieces[0], 'snap', split_axis=0, concat_axis=0, tiled=True)]
    unnamed x72 -> x86, local copies, waits for them, and re-layouts: 12.5 us -> 24.2 us
    all_to_all x0 -> x2, starting transfers between devices: none -> 9.96 us  [to_joint_rows(): lax.all_to_all(pieces[0], 'snap', split_axis=0, concat_axis=0, tiled=True)]
    pallas_call x5 -> x7, Pallas kernels: 15.7 us -> 20 us  [the longest x4 12.5 us: settle(): pl.pallas_call(lambda *refs: settle_kernel(chips, capacity, first, joint,...]
    dot_general x1 -> x0, matrix products: 4.04 us -> none  [body(): jnp.dot(inverse, cross, precision=HIGHEST) / math.sqrt(rows_total)]
  transfers between devices with their start and end apart: 35 -> 34, of which waited for: 15 -> 18; matrix products, arithmetic and copies ran while one was open for 0% -> 0% of each run, Pallas kernels for 18% -> 17%
where the time goes in v7:
time: 284 us; the launch traced here: 283 us
  waiting for transfers between devices  125 us (44%)
  Pallas kernels  69 us (24%)
  starting transfers between devices  51.8 us (18%)
  local copies, waits for them, and re-layouts  24.2 us (9%)
  blocking collectives  11 us (4%)
    ppermute x30, waiting for transfers between devices, swap(): lax.ppermute(value, axis, [(i, i ^ mask) for i in range(lax.axis_size(axi...  103 us
    ppermute x30, starting transfers between devices, swap(): lax.ppermute(value, axis, [(i, i ^ mask) for i in range(lax.axis_size(axi...  33.3 us
    unnamed x86, local copies, waits for them, and re-layouts  24.2 us
    pallas_call x4, Pallas kernels, factor_call(): pl.pallas_call(lambda *refs: kernel(*refs[len(after):]), out_shape=out_sh...  19.7 us
    all_to_all x2, waiting for transfers between devices, to_joint_rows(): lax.all_to_all(pieces[0], 'snap', split_axis=0, concat_axis=0, tiled=True)  19.4 us
    pallas_call x4, Pallas kernels, settle(): pl.pallas_call(lambda *refs: settle_kernel(chips, capacity, first, joint,...  12.5 us
    all_gather x1, blocking collectives, body(): gram = lax.all_gather(gram, 'space', axis=0, tiled=True)  11 us
    all_to_all x2, starting transfers between devices, to_joint_rows(): lax.all_to_all(pieces[0], 'snap', split_axis=0, concat_axis=0, tiled=True)  9.96 us
  transfers between devices with their start and end apart: 34, of which 18 were waited for; matrix products, arithmetic and copies ran while one was open for 0% of the time, Pallas kernels for 17%

profile of v7, /device:TPU:0, one launch (start us, length us, event | category | flops | bytes accessed | tf_op | source)
XLA Modules:
  0.0 282.6 jit_solution(15799422167657614370)
XLA Ops:
  0.6 2.2 copy-done
  3.5 3.0 %pack.2 = (bf16[260,16,128]{2,1,0:T(8,128)(2,1)S(1)}, bf16[260,16,128]{2,1,0:T(8,128)(2,1)S(1)}, bf16[256,16,128]{2,1,0:T(8,128)(2,1)S(1)}, bf16[256,16,128]{2,1,0:T(8,128)(2,1)S(1)}) custom-call(s32[128]{0:T(128)S(1)} %copy-done.23, bf16[128,4,2,16,128]{4,3,2,1,0:T(8,128)(2,1)S(1)} %bitcast.8), custom_call_target="tpu_custom_call" | custom-call | bytes 8388608 | tf_op jit(solution)/shard_map/pack/pallas_call | solution.py:84
  7.1 2.2 collective-permute-done.1.other_ref
  9.4 2.7 collective-permute-start.2
  12.1 2.5 collective-permute-start.3
  14.6 2.9 %pack.3 = (bf16[256,16,128]{2,1,0:T(8,128)(2,1)S(1)}, bf16[256,16,128]{2,1,0:T(8,128)(2,1)S(1)}, bf16[256,16,128]{2,1,0:T(8,128)(2,1)S(1)}, bf16[256,16,128]{2,1,0:T(8,128)(2,1)S(1)}) custom-call(s32[128]{0:T(128)S(1)} %copy-done.24, bf16[128,4,2,16,128]{4,3,2,1,0:T(8,128)(2,1)S(1)} %bitcast.9), custom_call_target="tpu_custom_call" | custom-call | bytes 8388608 | tf_op jit(solution)/shard_map/pack/pallas_call | solution.py:84
  19.5 1.3 merge.4
  20.7 4.3 %collective-permute-done.2.refs_3_ = bf16[130,16,128]{2,1,0:T(8,128)(2,1)S(1)} collective-permute-done((bf16[130,16,128]{2,1,0:T(8,128)(2,1)S(1)}, bf16[130,16,128]{2,1,0:T(8,128)(2,1)S(1)}, u32[]{:S(2)}, u32[]{:S(2)}) %collective-permute-start.2) | collective-permute-done | bytes 532512 | tf_op jit(solution)/shard_map/ppermute | solution.py:557
  25.0 13.1 %collective-permute-done.3.refs_4_ = bf16[130,16,128]{2,1,0:T(8,128)(2,1)S(1)} collective-permute-done((bf16[130,16,128]{2,1,0:T(8,128)(2,1)S(1)}, bf16[130,16,128]{2,1,0:T(8,128)(2,1)S(1)}, u32[]{:S(2)}, u32[]{:S(2)}) %collective-permute-start.3) | collective-permute-done | bytes 532512 | tf_op jit(solution)/shard_map/ppermute | solution.py:557
  38.1 2.7 settle.4
  41.8 4.9 %all-to-all-start = ((bf16[4,64,16,128]{3,2,1,0:T(8,128)(2,1)}), bf16[4,64,16,128]{3,2,1,0:T(8,128)(2,1)S(1)}, u32[]{:S(2)}, u32[]{:S(2)}) async-start(bf16[4,64,16,128]{3,2,1,0:T(8,128)(2,1)} %copy-done.14), calls=%async_computation | async-start | bytes 2097152 | tf_op jit(solution)/shard_map/all_to_all | solution.py:603
  46.7 1.5 collective-permute-start.16
  48.8 1.4 collective-permute-start.18
  52.8 8.9 %collective-permute-done.16.refs_3_ = bf16[128,16,128]{2,1,0:T(8,128)(2,1)S(1)} collective-permute-done((bf16[128,16,128]{2,1,0:T(8,128)(2,1)}, bf16[128,16,128]{2,1,0:T(8,128)(2,1)S(1)}, u32[]{:S(2)}, u32[]{:S(2)}) %collective-permute-start.16) | collective-permute-done | bytes 524320 | tf_op jit(solution)/shard_map/ppermute | solution.py:557
  61.6 10.3 %collective-permute-done.17.refs_4_ = bf16[128,16,128]{2,1,0:T(8,128)(2,1)S(1)} collective-permute-done((bf16[128,16,128]{2,1,0:T(8,128)(2,1)}, bf16[128,16,128]{2,1,0:T(8,128)(2,1)S(1)}, u32[]{:S(2)}, u32[]{:S(2)}) %collective-permute-start.17) | collective-permute-done | bytes 524320 | tf_op jit(solution)/shard_map/ppermute | solution.py:557
  72.0 1.7 collective-permute-done.18.refs_5_
  73.7 3.0 %settle.7 = bf16[4,64,16,128]{3,2,1,0:T(8,128)(2,1)} custom-call(bf16[128,16,128]{2,1,0:T(8,128)(2,1)S(1)} %get-tuple-element.55.refs_1_.refs_0_, s32[8,128]{1,0:T(8,128)S(1)} %get-tuple-element.53.refs_0_.refs_3_.refs_1_, bf16[128,16,128]{2,1,0:T(8,128)(2,1)S(1)} %get-tuple-element.44.refs_0_.refs_2_, ...), custom_call_target="tpu_custom_call" | custom-call | bytes 2097152 | tf_op jit(solution)/shard_map/settle/pallas_call | solution.py:166
  76.7 5.1 %all-to-all-start.1 = ((bf16[4,64,16,128]{3,2,1,0:T(8,128)(2,1)}), bf16[4,64,16,128]{3,2,1,0:T(8,128)(2,1)S(1)}, u32[]{:S(2)}, u32[]{:S(2)}) async-start(bf16[4,64,16,128]{3,2,1,0:T(8,128)(2,1)} %settle.7), calls=%async_computation.1 | async-start | bytes 2097152 | tf_op jit(solution)/shard_map/all_to_all | solution.py:603
  82.4 2.3 collective-permute-done.12.other_ref
  88.0 19.4 %all-to-all-done.1.refs_2_ = bf16[4,64,16,128]{3,2,1,0:T(8,128)(2,1)S(1)} async-done(((bf16[4,64,16,128]{3,2,1,0:T(8,128)(2,1)}), bf16[4,64,16,128]{3,2,1,0:T(8,128)(2,1)S(1)}, u32[]{:S(2)}, u32[]{:S(2)}) %all-to-all-start.1) | async-done | bytes 1048608 | tf_op jit(solution)/shard_map/all_to_all | solution.py:603
  107.4 1.0 copy-done.18
  108.5 2.7 gram_blocks.1
  111.2 4.3 %all-to-all-start.2 = ((f32[8,160,128]{2,1,0:T(8,128)}), f32[8,160,128]{2,1,0:T(8,128)}, u32[]{:S(2)}, u32[]{:S(2)}) async-start(f32[8,160,128]{2,1,0:T(8,128)} %bitcast.2), calls=%async_computation.2 | async-start | bytes 1310720 | tf_op jit(solution)/shard_map/all_to_all | solution.py:587
  115.5 1.9 collective-permute-start.7
  117.4 1.4 collective-permute-start.8
  119.1 1.9 collective-permute-start.14
  120.9 1.4 collective-permute-start.15
  122.4 26.2 %collective-permute-done.7.refs_3_ = bf16[128,16,128]{2,1,0:T(8,128)(2,1)S(1)} collective-permute-done((bf16[128,16,128]{2,1,0:T(8,128)(2,1)}, bf16[128,16,128]{2,1,0:T(8,128)(2,1)S(1)}, u32[]{:S(2)}, u32[]{:S(2)}) %collective-permute-start.7) | collective-permute-done | bytes 524320 | tf_op jit(solution)/shard_map/ppermute | solution.py:557
  148.6 2.8 settle.5
  153.5 1.9 sum_pieces.2.refs_0_
  155.4 2.0 collective-permute-start.9
  157.4 7.5 %collective-permute-done.19.refs_1_ = f32[160,128]{1,0:T(8,128)S(1)} collective-permute-done((f32[160,128]{1,0:T(8,128)}, f32[160,128]{1,0:T(8,128)S(1)}, u32[]{:S(2)}, u32[]{:S(2)}) %collective-permute-start.19) | collective-permute-done | bytes 81952 | tf_op jit(solution)/shard_map/ppermute | solution.py:557
  164.9 1.8 collective-permute-start.11
  166.6 1.6 add.4.refs_0_
  168.2 2.5 collective-permute-done.14.refs_6_
  170.7 10.0 %collective-permute-done.10.refs_1_.refs_5_ = bf16[64,16,128]{2,1,0:T(8,128)(2,1)S(1)} collective-permute-done((bf16[64,16,128]{2,1,0:T(8,128)(2,1)}, bf16[64,16,128]{2,1,0:T(8,128)(2,1)S(1)}, u32[]{:S(2)}, u32[]{:S(2)}) %collective-permute-start.10) | collective-permute-done | bytes 262176 | tf_op jit(solution)/shard_map/ppermute | solution.py:557
  180.7 3.9 %settle.6 = (bf16[64,16,128]{2,1,0:T(8,128)(2,1)S(1)}, bf16[64,16,128]{2,1,0:T(8,128)(2,1)}, bf16[64,16,128]{2,1,0:T(8,128)(2,1)}, bf16[64,16,128]{2,1,0:T(8,128)(2,1)}) custom-call(bf16[64,16,128]{2,1,0:T(8,128)(2,1)S(1)} %collective-permute-done.9.refs_0_.refs_4_, bf16[64,16,128]{2,1,0:T(8,128)(2,1)S(1)} %collective-permute-done.10.refs_1_.refs_5_, ...), custom_call_target="tpu_custom_call" | custom-call | bytes 2097152 | tf_op jit(solution)/shard_map/settle/pallas_call | solution.py:166
  185.4 4.8 %collective-permute-start.21 = (bf16[64,16,128]{2,1,0:T(8,128)(2,1)}, bf16[64,16,128]{2,1,0:T(8,128)(2,1)S(1)}, u32[]{:S(2)}, u32[]{:S(2)}) collective-permute-start(bf16[64,16,128]{2,1,0:T(8,128)(2,1)} %get-tuple-element.73), channel_id=1, source_target_pairs={{0,1},{1,0},{2,3},{3,2},{4,5},{5,4},{6,7},{7,6},{8,9},{9,8},{10,11... | collective-permute-start | bytes 786440 | tf_op jit(solution)/shard_map/ppermute | solution.py:557
  190.2 2.4 collective-permute-start.23
  193.2 1.6 add.5
  194.7 11.0 %all_gather.3 = f32[1280,128]{1,0:T(8,128)S(1)} all-gather(f32[160,128]{1,0:T(8,128)} %add.5), channel_id=1, replica_groups=mesh['space'=8,'snap'=4] {'space'}, dimensions={0}, use_global_device_ids=true | all-gather | bytes 737280 | tf_op jit(solution)/shard_map/all_gather | solution.py:618
  206.6 4.9 %factor.4.refs_0_ = f32[4,8,128,128]{3,2,1,0:T(8,128)S(1)} custom-call(bf16[64,16,128]{2,1,0:T(8,128)(2,1)S(1)} %copy-done.21, f32[10,128,128]{2,1,0:T(8,128)S(1)} %bitcast.10), custom_call_target="tpu_custom_call" | custom-call | flops 7000000000 | bytes 655360 | tf_op jit(solution)/shard_map/factor/pallas_call | solution.py:403
  211.6 4.8 %factor.5.refs_0_ = f32[4,8,128,128]{3,2,1,0:T(8,128)S(1)} custom-call(f32[4,8,128,128]{3,2,1,0:T(8,128)S(1)} %factor.4.refs_0_), custom_call_target="tpu_custom_call", output_to_operand_aliasing={{}: (0, {})} | custom-call | flops 7000000000 | bytes 2097152 | tf_op jit(solution)/shard_map/factor/pallas_call | solution.py:403
  216.4 4.6 %factor.6.refs_0_.refs_1_ = f32[4,8,128,128]{3,2,1,0:T(8,128)S(1)} custom-call(f32[4,8,128,128]{3,2,1,0:T(8,128)S(1)} %factor.5.refs_0_), custom_call_target="tpu_custom_call", output_to_operand_aliasing={{}: (0, {})} | custom-call | flops 7000000000 | bytes 2097152 | tf_op jit(solution)/shard_map/factor/pallas_call | solution.py:403
  221.3 4.5 %cross_sum.1.refs_0_ = f32[512,512]{1,0:T(8,128)} custom-call(f32[4,8,128,128]{3,2,1,0:T(8,128)S(1)} %factor.6.refs_0_.refs_1_, bf16[4,64,16,128]{3,2,1,0:T(8,128)(2,1)S(1)} %all-to-all-done.refs_1_.refs_0_, bf16[4,64,16,128]{3,2,1,0:T(8,128)(2,1)S(1)} %all-to-all-done.1.refs_2_, bf16[64,16,128]{2,1,0:T(8,128)(2,1)S(1)} %copy-done.16, ...), custom_call_target="tpu_custom_call" | custom-call | flops 1073741824 | bytes 4194304 | tf_op jit(solution)/shard_map/cross_sum/pallas_call | solution.py:265
  225.8 4.2 %all-to-all-start.3 = ((f32[8,64,512]{2,1,0:T(8,128)}), f32[8,64,512]{2,1,0:T(8,128)}, u32[]{:S(2)}, u32[]{:S(2)}) async-start(f32[8,64,512]{2,1,0:T(8,128)} %bitcast.5), calls=%async_computation.3 | async-start | bytes 2097152 | tf_op jit(solution)/shard_map/all_to_all | solution.py:587
  230.1 1.6 copy-done.3
  231.7 5.4 %factor.7 = (f32[512,512]{1,0:T(8,128)}, f32[512,512]{1,0:T(8,128)S(1)}, bf16[512,512]{1,0:T(8,128)(2,1)S(1)}, bf16[512,512]{1,0:T(8,128)(2,1)S(1)}, bf16[512,512]{1,0:T(8,128)(2,1)S(1)}) custom-call(f32[512,512]{1,0:T(8,128)} %cross_sum.1.refs_0_, f32[4,8,128,128]{3,2,1,0:T(8,128)S(1)} %copy-done.3), custom_call_target="tpu_custom_call" | custom-call | flops 7000000000 | bytes 2097152 | tf_op jit(solution)/shard_map/factor/pallas_call | solution.py:403
  238.0 3.5 %basis.2.refs_0_ = f32[64,2,16,512]{3,2,1,0:T(8,128)} custom-call(bf16[4,64,16,128]{3,2,1,0:T(8,128)(2,1)S(1)} %all-to-all-done.refs_1_.refs_0_, bf16[512,512]{1,0:T(8,128)(2,1)S(1)} %get-tuple-element.76.refs_1_.refs_3_, bf16[512,512]{1,0:T(8,128)(2,1)S(1)} %get-tuple-element.77.refs_2_.refs_4_, bf16[512,512]{1,0:T(8,128)(2,1)S(1)} %get-tuple-element.78.refs_3_.refs_5_), custom_call_target="tpu_custom_call" | custom-call | flops 1610612736 | bytes 3145728 | tf_op jit(solution)/shard_map/basis/pallas_call | solution.py:457
  242.3 3.2 %all-to-all-done.3 = f32[8,64,512]{2,1,0:T(8,128)} async-done(((f32[8,64,512]{2,1,0:T(8,128)}), f32[8,64,512]{2,1,0:T(8,128)}, u32[]{:S(2)}, u32[]{:S(2)}) %all-to-all-start.3) | async-done | bytes 1048608 | tf_op jit(solution)/shard_map/all_to_all | solution.py:587
  245.5 2.0 sum_pieces.3.refs_1_
  247.5 1.1 collective-permute-start.24
  249.5 3.5 %basis.3.refs_0_ = f32[64,2,16,512]{3,2,1,0:T(8,128)} custom-call(f32[64,2,16,512]{3,2,1,0:T(8,128)} %basis.2.refs_0_, f32[64,512]{1,0:T(8,128)S(1)} %copy-done.9, bf16[4,64,16,128]{3,2,1,0:T(8,128)(2,1)S(1)} %all-to-all-done.1.refs_2_, bf16[512,512]{1,0:T(8,128)(2,1)S(1)} %get-tuple-element.76.refs_1_.refs_3_, ...), custom_call_target="tpu_custom_call", output_to_operand_aliasing={{}: (0, {})} | custom-call | flops 1610612736 | bytes 3145728 | tf_op jit(solution)/shard_map/basis/pallas_call | solution.py:457
  253.7 1.6 add.6.refs_0_
  256.2 6.6 %collective-permute-done.25.refs_1_ = f32[64,512]{1,0:T(8,128)S(1)} collective-permute-done((f32[64,512]{1,0:T(8,128)}, f32[64,512]{1,0:T(8,128)S(1)}, u32[]{:S(2)}, u32[]{:S(2)}) %collective-permute-start.25) | collective-permute-done | bytes 131104 | tf_op jit(solution)/shard_map/ppermute | solution.py:557
  263.5 1.6 add.7.refs_0_
  265.1 1.9 collective-permute-start.28
  267.0 1.7 collective-permute-start.27
  268.7 3.4 %collective-permute-done.28.refs_3_ = f32[64,512]{1,0:T(8,128)S(1)} collective-permute-done((f32[64,512]{1,0:T(8,128)}, f32[64,512]{1,0:T(8,128)S(1)}, u32[]{:S(2)}, u32[]{:S(2)}) %collective-permute-start.28) | collective-permute-done | bytes 131104 | tf_op jit(solution)/shard_map/ppermute | solution.py:557
  272.1 1.3 collective-permute-done.27.refs_2_
  274.7 1.9 join.1.refs_1_
  276.6 2.1 collective-permute-done.29.refs_2_
  278.7 1.0 copy-done.4
  279.8 2.9 %project.1 = f32[512,512]{1,0:T(8,128)} custom-call(f32[512,512]{1,0:T(8,128)S(1)} %copy-done.11, f32[256,512]{1,0:T(8,128)S(1)} %copy-done.4, f32[256,512]{1,0:T(8,128)S(1)} %collective-permute-done.29.refs_2_), custom_call_target="tpu_custom_call" | custom-call | tf_op jit(solution)/shard_map/project/pallas_call | solution.py:545
  (117 shorter events, 22.3 us)
Async XLA Ops:
  0.6 2.2 copy-start
  3.5 11.1 %copy-start.1 = (bf16[128,128,128]{2,1,0:T(8,128)(2,1)S(1)}, bf16[128,128,128]{2,1,0:T(8,128)(2,1)}, u32[]{:S(2)}) copy-start(bf16[128,128,128]{2,1,0:T(8,128)(2,1)} %param.4) | copy-start | bytes 12582916
  6.5 8.1 %copy-start.24 = (s32[128]{0:T(128)S(1)}, s32[128]{0:T(128)}, u32[]{:S(2)}) copy-start(s32[128]{0:T(128)} %refs_0_.3) | copy-start | bytes 1540
  6.5 2.7 collective-permute-start.1
  6.6 11.9 %collective-permute-start = (bf16[256,16,128]{2,1,0:T(8,128)(2,1)S(1)}, bf16[256,16,128]{2,1,0:T(8,128)(2,1)S(1)}, u32[]{:S(2)}, u32[]{:S(2)}) collective-permute-start(bf16[256,16,128]{2,1,0:T(8,128)(2,1)S(1)} %get-tuple-element.43), channel_id=1, source_target_pairs={{0,4},{4,0},{8,12},{12,8},{16,20},{20,16},{24,28},{28,24},{1,5},{5... | collective-permute-start | bytes 3145736 | tf_op jit(solution)/shard_map/ppermute | solution.py:557
  9.4 15.6 %collective-permute-start.2 = (bf16[130,16,128]{2,1,0:T(8,128)(2,1)S(1)}, bf16[130,16,128]{2,1,0:T(8,128)(2,1)S(1)}, u32[]{:S(2)}, u32[]{:S(2)}) collective-permute-start(bf16[130,16,128]{2,1,0:T(8,128)(2,1)S(1)} %get-tuple-element.49), channel_id=1, source_target_pairs={{0,8},{4,12},{8,0},{12,4},{16,24},{20,28},{24,16},{28,20},{1,9},{5... | collective-permute-start | bytes 1597448 | tf_op jit(solution)/shard_map/ppermute | solution.py:557
  12.1 26.0 %collective-permute-start.3 = (bf16[130,16,128]{2,1,0:T(8,128)(2,1)S(1)}, bf16[130,16,128]{2,1,0:T(8,128)(2,1)S(1)}, u32[]{:S(2)}, u32[]{:S(2)}) collective-permute-start(bf16[130,16,128]{2,1,0:T(8,128)(2,1)S(1)} %get-tuple-element.50), channel_id=1, source_target_pairs={{0,16},{4,20},{8,24},{12,28},{16,0},{20,4},{24,8},{28,12},{1,17},{... | collective-permute-start | bytes 1597448 | tf_op jit(solution)/shard_map/ppermute | solution.py:557
  14.6 23.5 %collective-permute-start.4 = (bf16[130,16,128]{2,1,0:T(8,128)(2,1)S(1)}, bf16[130,16,128]{2,1,0:T(8,128)(2,1)S(1)}, u32[]{:S(2)}, u32[]{:S(2)}) collective-permute-start(bf16[130,16,128]{2,1,0:T(8,128)(2,1)S(1)} %get-tuple-element.51), channel_id=1, source_target_pairs={{0,24},{4,28},{8,16},{12,20},{16,8},{20,12},{24,0},{28,4},{1,25},{... | collective-permute-start | bytes 1597448 | tf_op jit(solution)/shard_map/ppermute | solution.py:557
  17.5 1.0 copy-start.12
  18.5 1.0 copy-start.25
  18.5 19.6 %copy-start.26 = (bf16[256,16,128]{2,1,0:T(8,128)(2,1)}, bf16[256,16,128]{2,1,0:T(8,128)(2,1)S(1)}, u32[]{:S(2)}) copy-start(bf16[256,16,128]{2,1,0:T(8,128)(2,1)S(1)} %get-tuple-element.54) | copy-start | bytes 3145732
  40.9 1.0 copy-start.14
  41.8 34.9 %all-to-all-start = ((bf16[4,64,16,128]{3,2,1,0:T(8,128)(2,1)}), bf16[4,64,16,128]{3,2,1,0:T(8,128)(2,1)S(1)}, u32[]{:S(2)}, u32[]{:S(2)}) async-start(bf16[4,64,16,128]{3,2,1,0:T(8,128)(2,1)} %copy-done.14), calls=%async_computation | async-start | bytes 2097152 | tf_op jit(solution)/shard_map/all_to_all | solution.py:603
  46.7 3.5 %collective-permute-start.5 = (bf16[256,16,128]{2,1,0:T(8,128)(2,1)}, bf16[256,16,128]{2,1,0:T(8,128)(2,1)S(1)}, u32[]{:S(2)}, u32[]{:S(2)}) collective-permute-start(bf16[256,16,128]{2,1,0:T(8,128)(2,1)} %copy-done.26), channel_id=1, source_target_pairs={{0,4},{4,0},{8,12},{12,8},{16,20},{20,16},{24,28},{28,24},{1,5},{5... | collective-permute-start | bytes 3145736 | tf_op jit(solution)/shard_map/ppermute | solution.py:557
  46.7 14.9 %collective-permute-start.16 = (bf16[128,16,128]{2,1,0:T(8,128)(2,1)}, bf16[128,16,128]{2,1,0:T(8,128)(2,1)S(1)}, u32[]{:S(2)}, u32[]{:S(2)}) collective-permute-start(bf16[128,16,128]{2,1,0:T(8,128)(2,1)} %get-tuple-element.70), channel_id=1, source_target_pairs={{0,8},{4,12},{8,0},{12,4},{16,24},{20,28},{24,16},{28,20},{1,9},{5... | collective-permute-start | bytes 1572872 | tf_op jit(solution)/shard_map/ppermute | solution.py:557
  48.2 23.8 %collective-permute-start.17 = (bf16[128,16,128]{2,1,0:T(8,128)(2,1)}, bf16[128,16,128]{2,1,0:T(8,128)(2,1)S(1)}, u32[]{:S(2)}, u32[]{:S(2)}) collective-permute-start(bf16[128,16,128]{2,1,0:T(8,128)(2,1)} %get-tuple-element.71), channel_id=1, source_target_pairs={{0,16},{4,20},{8,24},{12,28},{16,0},{20,4},{24,8},{28,12},{1,17},{... | collective-permute-start | bytes 1572872 | tf_op jit(solution)/shard_map/ppermute | solution.py:557
  48.8 24.9 %collective-permute-start.18 = (bf16[128,16,128]{2,1,0:T(8,128)(2,1)}, bf16[128,16,128]{2,1,0:T(8,128)(2,1)S(1)}, u32[]{:S(2)}, u32[]{:S(2)}) collective-permute-start(bf16[128,16,128]{2,1,0:T(8,128)(2,1)} %get-tuple-element.72), channel_id=1, source_target_pairs={{0,24},{4,28},{8,16},{12,20},{16,8},{20,12},{24,0},{28,4},{1,25},{... | collective-permute-start | bytes 1572872 | tf_op jit(solution)/shard_map/ppermute | solution.py:557
  50.3 0.8 copy-start.28
  51.2 0.8 copy-start.30
  52.0 0.8 copy-start.31
  52.8 23.9 %copy-start.5 = (bf16[128,16,128]{2,1,0:T(8,128)(2,1)}, bf16[128,16,128]{2,1,0:T(8,128)(2,1)S(1)}, u32[]{:S(2)}) copy-start(bf16[128,16,128]{2,1,0:T(8,128)(2,1)S(1)} %get-tuple-element.55.refs_1_.refs_0_) | copy-start | bytes 1572868
  73.7 11.0 %copy-start.13 = (bf16[256,16,128]{2,1,0:T(8,128)(2,1)S(1)}, bf16[256,16,128]{2,1,0:T(8,128)(2,1)}, u32[]{:S(2)}) copy-start(bf16[256,16,128]{2,1,0:T(8,128)(2,1)} %copy-done.12) | copy-start | bytes 3145732
  76.7 30.7 %all-to-all-start.1 = ((bf16[4,64,16,128]{3,2,1,0:T(8,128)(2,1)}), bf16[4,64,16,128]{3,2,1,0:T(8,128)(2,1)S(1)}, u32[]{:S(2)}, u32[]{:S(2)}) async-start(bf16[4,64,16,128]{3,2,1,0:T(8,128)(2,1)} %settle.7), calls=%async_computation.1 | async-start | bytes 2097152 | tf_op jit(solution)/shard_map/all_to_all | solution.py:603
  81.8 2.9 %collective-permute-start.12 = (bf16[256,16,128]{2,1,0:T(8,128)(2,1)}, bf16[256,16,128]{2,1,0:T(8,128)(2,1)S(1)}, u32[]{:S(2)}, u32[]{:S(2)}) collective-permute-start(bf16[256,16,128]{2,1,0:T(8,128)(2,1)} %copy-done.25), channel_id=1, source_target_pairs={{0,4},{4,0},{8,12},{12,8},{16,20},{20,16},{24,28},{28,24},{1,5},{5... | collective-permute-start | bytes 3145736 | tf_op jit(solution)/shard_map/ppermute | solution.py:557
  81.8 39.1 %collective-permute-start.6 = (bf16[128,16,128]{2,1,0:T(8,128)(2,1)}, bf16[128,16,128]{2,1,0:T(8,128)(2,1)}, u32[]{:S(2)}, u32[]{:S(2)}) collective-permute-start(bf16[128,16,128]{2,1,0:T(8,128)(2,1)} %copy-done.31), channel_id=1, source_target_pairs={{0,8},{4,12},{8,0},{12,4},{16,24},{20,28},{24,16},{28,20},{1,9},{5... | collective-permute-start | bytes 1572872 | tf_op jit(solution)/shard_map/ppermute | solution.py:557
  87.2 0.8 copy-start.32
  107.4 1.0 copy-start.18
  108.5 40.1 %copy-start.6 = (bf16[128,16,128]{2,1,0:T(8,128)(2,1)S(1)}, bf16[128,16,128]{2,1,0:T(8,128)(2,1)}, u32[]{:S(2)}) copy-start(bf16[128,16,128]{2,1,0:T(8,128)(2,1)} %copy-done.5) | copy-start | bytes 1572868
  111.2 69.6 %copy-start.19 = (bf16[128,16,128]{2,1,0:T(8,128)(2,1)S(1)}, bf16[128,16,128]{2,1,0:T(8,128)(2,1)}, u32[]{:S(2)}) copy-start(bf16[128,16,128]{2,1,0:T(8,128)(2,1)} %copy-done.17) | copy-start | bytes 1572868
  111.2 42.3 %all-to-all-start.2 = ((f32[8,160,128]{2,1,0:T(8,128)}), f32[8,160,128]{2,1,0:T(8,128)}, u32[]{:S(2)}, u32[]{:S(2)}) async-start(f32[8,160,128]{2,1,0:T(8,128)} %bitcast.2), calls=%async_computation.2 | async-start | bytes 1310720 | tf_op jit(solution)/shard_map/all_to_all | solution.py:587
  115.5 33.1 %collective-permute-start.7 = (bf16[128,16,128]{2,1,0:T(8,128)(2,1)}, bf16[128,16,128]{2,1,0:T(8,128)(2,1)S(1)}, u32[]{:S(2)}, u32[]{:S(2)}) collective-permute-start(bf16[128,16,128]{2,1,0:T(8,128)(2,1)} %copy-done.30), channel_id=1, source_target_pairs={{0,16},{4,20},{8,24},{12,28},{16,0},{20,4},{24,8},{28,12},{1,17},{... | collective-permute-start | bytes 1572872 | tf_op jit(solution)/shard_map/ppermute | solution.py:557
  117.4 31.2 %collective-permute-start.8 = (bf16[128,16,128]{2,1,0:T(8,128)(2,1)}, bf16[128,16,128]{2,1,0:T(8,128)(2,1)S(1)}, u32[]{:S(2)}, u32[]{:S(2)}) collective-permute-start(bf16[128,16,128]{2,1,0:T(8,128)(2,1)} %copy-done.28), channel_id=1, source_target_pairs={{0,24},{4,28},{8,16},{12,20},{16,8},{20,12},{24,0},{28,4},{1,25},{... | collective-permute-start | bytes 1572872 | tf_op jit(solution)/shard_map/ppermute | solution.py:557
  118.9 38.5 %collective-permute-start.13 = (bf16[128,16,128]{2,1,0:T(8,128)(2,1)}, bf16[128,16,128]{2,1,0:T(8,128)(2,1)}, u32[]{:S(2)}, u32[]{:S(2)}) collective-permute-start(bf16[128,16,128]{2,1,0:T(8,128)(2,1)} %copy-done.32), channel_id=1, source_target_pairs={{0,8},{4,12},{8,0},{12,4},{16,24},{20,28},{24,16},{28,20},{1,9},{5... | collective-permute-start | bytes 1572872 | tf_op jit(solution)/shard_map/ppermute | solution.py:557
  119.1 51.6 %collective-permute-start.14 = (bf16[128,16,128]{2,1,0:T(8,128)(2,1)}, bf16[128,16,128]{2,1,0:T(8,128)(2,1)}, u32[]{:S(2)}, u32[]{:S(2)}) collective-permute-start(bf16[128,16,128]{2,1,0:T(8,128)(2,1)} %copy-done.29), channel_id=1, source_target_pairs={{0,16},{4,20},{8,24},{12,28},{16,0},{20,4},{24,8},{28,12},{1,17},{... | collective-permute-start | bytes 1572872 | tf_op jit(solution)/shard_map/ppermute | solution.py:557
  120.9 49.8 %collective-permute-start.15 = (bf16[128,16,128]{2,1,0:T(8,128)(2,1)}, bf16[128,16,128]{2,1,0:T(8,128)(2,1)}, u32[]{:S(2)}, u32[]{:S(2)}) collective-permute-start(bf16[128,16,128]{2,1,0:T(8,128)(2,1)} %copy-done.27), channel_id=1, source_target_pairs={{0,24},{4,28},{8,16},{12,20},{16,8},{20,12},{24,0},{28,4},{1,25},{... | collective-permute-start | bytes 1572872 | tf_op jit(solution)/shard_map/ppermute | solution.py:557
  153.5 11.4 %copy-start.33 = (bf16[64,16,128]{2,1,0:T(8,128)(2,1)}, bf16[64,16,128]{2,1,0:T(8,128)(2,1)S(1)}, u32[]{:S(2)}) copy-start(bf16[64,16,128]{2,1,0:T(8,128)(2,1)S(1)} %get-tuple-element.61) | copy-start | bytes 786436
  155.4 9.5 %collective-permute-start.19 = (f32[160,128]{1,0:T(8,128)}, f32[160,128]{1,0:T(8,128)S(1)}, u32[]{:S(2)}, u32[]{:S(2)}) collective-permute-start(f32[160,128]{1,0:T(8,128)} %sum_pieces.2.refs_0_), channel_id=1, source_target_pairs={{0,1},{1,0},{2,3},{3,2},{4,5},{5,4},{6,7},{7,6},{8,9},{9,8},{10,11... | collective-permute-start | bytes 245768 | tf_op jit(solution)/shard_map/ppermute | solution.py:557
  155.4 15.3 %collective-permute-start.9 = (bf16[64,16,128]{2,1,0:T(8,128)(2,1)}, bf16[64,16,128]{2,1,0:T(8,128)(2,1)S(1)}, u32[]{:S(2)}, u32[]{:S(2)}) collective-permute-start(bf16[64,16,128]{2,1,0:T(8,128)(2,1)} %copy-done.35), channel_id=1, source_target_pairs={{0,1},{1,0},{2,3},{3,2},{4,5},{5,4},{6,7},{7,6},{8,9},{9,8},{10,11... | collective-permute-start | bytes 786440 | tf_op jit(solution)/shard_map/ppermute | solution.py:557
  157.4 23.3 %collective-permute-start.10 = (bf16[64,16,128]{2,1,0:T(8,128)(2,1)}, bf16[64,16,128]{2,1,0:T(8,128)(2,1)S(1)}, u32[]{:S(2)}, u32[]{:S(2)}) collective-permute-start(bf16[64,16,128]{2,1,0:T(8,128)(2,1)} %copy-done.34), channel_id=1, source_target_pairs={{0,2},{1,3},{2,0},{3,1},{4,6},{5,7},{6,4},{7,5},{8,10},{9,11},{10,... | collective-permute-start | bytes 786440 | tf_op jit(solution)/shard_map/ppermute | solution.py:557
  164.9 1.8 copy-start.42
  164.9 15.9 %collective-permute-start.11 = (bf16[64,16,128]{2,1,0:T(8,128)(2,1)}, bf16[64,16,128]{2,1,0:T(8,128)(2,1)S(1)}, u32[]{:S(2)}, u32[]{:S(2)}) collective-permute-start(bf16[64,16,128]{2,1,0:T(8,128)(2,1)} %copy-done.33), channel_id=1, source_target_pairs={{0,3},{1,2},{2,1},{3,0},{4,7},{5,6},{6,5},{7,4},{8,11},{9,10},{10,... | collective-permute-start | bytes 786440 | tf_op jit(solution)/shard_map/ppermute | solution.py:557
  170.7 21.8 %collective-permute-start.20 = (f32[160,128]{1,0:T(8,128)}, f32[160,128]{1,0:T(8,128)S(1)}, u32[]{:S(2)}, u32[]{:S(2)}) collective-permute-start(f32[160,128]{1,0:T(8,128)} %add.4.refs_0_), channel_id=1, source_target_pairs={{0,2},{1,3},{2,0},{3,1},{4,6},{5,7},{6,4},{7,5},{8,10},{9,11},{10,... | collective-permute-start | bytes 245768 | tf_op jit(solution)/shard_map/ppermute | solution.py:557
  185.4 35.6 %collective-permute-start.21 = (bf16[64,16,128]{2,1,0:T(8,128)(2,1)}, bf16[64,16,128]{2,1,0:T(8,128)(2,1)S(1)}, u32[]{:S(2)}, u32[]{:S(2)}) collective-permute-start(bf16[64,16,128]{2,1,0:T(8,128)(2,1)} %get-tuple-element.73), channel_id=1, source_target_pairs={{0,1},{1,0},{2,3},{3,2},{4,5},{5,4},{6,7},{7,6},{8,9},{9,8},{10,11... | collective-permute-start | bytes 786440 | tf_op jit(solution)/shard_map/ppermute | solution.py:557
  190.2 30.9 %collective-permute-start.22 = (bf16[64,16,128]{2,1,0:T(8,128)(2,1)}, bf16[64,16,128]{2,1,0:T(8,128)(2,1)S(1)}, u32[]{:S(2)}, u32[]{:S(2)}) collective-permute-start(bf16[64,16,128]{2,1,0:T(8,128)(2,1)} %get-tuple-element.74), channel_id=1, source_target_pairs={{0,2},{1,3},{2,0},{3,1},{4,6},{5,7},{6,4},{7,5},{8,10},{9,11},{10,... | collective-permute-start | bytes 786440 | tf_op jit(solution)/shard_map/ppermute | solution.py:557
  190.2 30.9 %collective-permute-start.23 = (bf16[64,16,128]{2,1,0:T(8,128)(2,1)}, bf16[64,16,128]{2,1,0:T(8,128)(2,1)}, u32[]{:S(2)}, u32[]{:S(2)}) collective-permute-start(bf16[64,16,128]{2,1,0:T(8,128)(2,1)} %get-tuple-element.75), channel_id=1, source_target_pairs={{0,3},{1,2},{2,1},{3,0},{4,7},{5,6},{6,5},{7,4},{8,11},{9,10},{10,... | collective-permute-start | bytes 786440 | tf_op jit(solution)/shard_map/ppermute | solution.py:557
  205.7 0.9 copy-start.21
  216.4 4.6 %copy-start.16 = (bf16[64,16,128]{2,1,0:T(8,128)(2,1)S(1)}, bf16[64,16,128]{2,1,0:T(8,128)(2,1)}, u32[]{:S(2)}) copy-start(bf16[64,16,128]{2,1,0:T(8,128)(2,1)} %copy-done.15) | copy-start | bytes 786436
  216.4 4.6 %copy-start.22 = (bf16[64,16,128]{2,1,0:T(8,128)(2,1)S(1)}, bf16[64,16,128]{2,1,0:T(8,128)(2,1)}, u32[]{:S(2)}) copy-start(bf16[64,16,128]{2,1,0:T(8,128)(2,1)} %copy-done.20) | copy-start | bytes 786436
  221.0 4.8 %copy-start.2 = (f32[4,8,128,128]{3,2,1,0:T(8,128)}, f32[4,8,128,128]{3,2,1,0:T(8,128)S(1)}, u32[]{:S(2)}) copy-start(f32[4,8,128,128]{3,2,1,0:T(8,128)S(1)} %factor.6.refs_0_.refs_1_) | copy-start | bytes 6291460
  225.8 19.7 %all-to-all-start.3 = ((f32[8,64,512]{2,1,0:T(8,128)}), f32[8,64,512]{2,1,0:T(8,128)}, u32[]{:S(2)}, u32[]{:S(2)}) async-start(f32[8,64,512]{2,1,0:T(8,128)} %bitcast.5), calls=%async_computation.3 | async-start | bytes 2097152 | tf_op jit(solution)/shard_map/all_to_all | solution.py:587
  230.1 1.6 copy-start.3
  237.1 1.0 copy-start.10
  241.5 0.8 copy-start.7
  245.5 3.1 %copy-start.8 = (bf16[512,512]{1,0:T(8,128)(2,1)S(1)}, bf16[512,512]{1,0:T(8,128)(2,1)}, u32[]{:S(2)}) copy-start(bf16[512,512]{1,0:T(8,128)(2,1)} %copy-done.7) | copy-start | bytes 1572868
  247.5 5.5 %collective-permute-start.24 = (f32[64,512]{1,0:T(8,128)}, f32[64,512]{1,0:T(8,128)S(1)}, u32[]{:S(2)}, u32[]{:S(2)}) collective-permute-start(f32[64,512]{1,0:T(8,128)} %sum_pieces.3.refs_1_), channel_id=1, source_target_pairs={{0,1},{1,0},{2,3},{3,2},{4,5},{5,4},{6,7},{7,6},{8,9},{9,8},{10,11... | collective-permute-start | bytes 393224 | tf_op jit(solution)/shard_map/ppermute | solution.py:557
  248.6 0.9 copy-start.9
  253.0 25.7 %copy-start.11 = (f32[512,512]{1,0:T(8,128)S(1)}, f32[512,512]{1,0:T(8,128)}, u32[]{:S(2)}) copy-start(f32[512,512]{1,0:T(8,128)} %copy-done.10) | copy-start | bytes 3145732
  255.3 7.5 %collective-permute-start.25 = (f32[64,512]{1,0:T(8,128)}, f32[64,512]{1,0:T(8,128)S(1)}, u32[]{:S(2)}, u32[]{:S(2)}) collective-permute-start(f32[64,512]{1,0:T(8,128)} %add.6.refs_0_), channel_id=1, source_target_pairs={{0,2},{1,3},{2,0},{3,1},{4,6},{5,7},{6,4},{7,5},{8,10},{9,11},{10,... | collective-permute-start | bytes 393224 | tf_op jit(solution)/shard_map/ppermute | solution.py:557
  265.1 7.0 %collective-permute-start.28 = (f32[64,512]{1,0:T(8,128)}, f32[64,512]{1,0:T(8,128)S(1)}, u32[]{:S(2)}, u32[]{:S(2)}) collective-permute-start(f32[64,512]{1,0:T(8,128)} %add.7.refs_0_), channel_id=1, source_target_pairs={{0,24},{4,28},{8,16},{12,20},{16,8},{20,12},{24,0},{28,4},{1,25},{... | collective-permute-start | bytes 393224 | tf_op jit(solution)/shard_map/ppermute | solution.py:557
  267.0 6.4 %collective-permute-start.27 = (f32[64,512]{1,0:T(8,128)}, f32[64,512]{1,0:T(8,128)S(1)}, u32[]{:S(2)}, u32[]{:S(2)}) collective-permute-start(f32[64,512]{1,0:T(8,128)} %add.7.refs_0_), channel_id=1, source_target_pairs={{0,16},{4,20},{8,24},{12,28},{16,0},{20,4},{24,8},{28,12},{1,17},{... | collective-permute-start | bytes 393224 | tf_op jit(solution)/shard_map/ppermute | solution.py:557
  268.7 5.2 %collective-permute-start.26 = (f32[64,512]{1,0:T(8,128)}, f32[64,512]{1,0:T(8,128)S(1)}, u32[]{:S(2)}, u32[]{:S(2)}) collective-permute-start(f32[64,512]{1,0:T(8,128)} %add.7.refs_0_), channel_id=1, source_target_pairs={{0,8},{4,12},{8,0},{12,4},{16,24},{20,28},{24,16},{28,20},{1,9},{5... | collective-permute-start | bytes 393224 | tf_op jit(solution)/shard_map/ppermute | solution.py:557
  272.1 1.8 copy-start.38
  276.6 2.1 collective-permute-start.29
  278.7 1.0 copy-start.4
  (13 other events, 9.1 us)

commit v8 on v7

--- a/solution.py
+++ b/solution.py
@@ -28,11 +28,12 @@
     )
 
 
-def pack_kernel(slabs, capacity, per_slab, parts, dest_ref, owned_ref, *refs):
-    out_refs, (ids_ref, count_ref) = refs[: 2 * parts], refs[2 * parts :]
+def pack_kernel(slabs, capacity, per_slab, dest_ref, owned_ref, *refs):
+    out_refs, (ids_ref, count_ref) = refs[:CORES], refs[CORES:]
     chips = slabs // CORES
-    shares = owned_ref.shape[1]
-    used = capacity * shares
+    tiles = owned_ref.shape[1]
+    used = capacity * tiles
+    span = out_refs[0].shape[0] // chips
     me = lax.axis_index("space")
     lane = lax.broadcasted_iota(jnp.int32, (1, TILE), 1)
     ids_ref[...] = jnp.full_like(ids_ref, -1)
@@ -50,53 +51,43 @@
             here = pl.ds(slab, 1)
             ids_ref[here, :] = jnp.where(lane == rank, block - slab * per_slab, ids_ref[here, :])
             away = slab ^ me
-            chip = lax.shift_right_logical(away, 1)
+            at = pl.ds(lax.shift_right_logical(away, 1) * span + rank * tiles, tiles)
             for core in range(CORES):
 
                 @pl.when((away & 1) == core)
                 def _():
-                    for part in range(parts):
-                        out_ref = out_refs[part * CORES + core]
-                        at = chip * (out_ref.shape[0] // chips) + rank * shares
-                        out_ref[pl.ds(at, shares)] = owned_ref[i, :, part]
+                    out_refs[core][at] = owned_ref[i]
 
         return 0
 
     lax.fori_loop(0, dest_ref.shape[0], place, 0, unroll=2)
-    for away in range(slabs):
-        for part in range(parts):
-            out_ref = out_refs[part * CORES + away % CORES]
-            span = out_ref.shape[0] // chips
-            if span > used:
-                ids = ids_ref[pl.ds(me ^ away, 1), :].astype(jnp.float32)
-                tile = jnp.broadcast_to(ids, out_ref.shape[1:]).astype(out_ref.dtype)
-                out_ref[away // CORES * span + used] = tile
-
-
-def pack(dest, owned, slabs, per_slab, with_ids, after=()):
-    slots, shares, parts, rows, width = owned.shape
+    if span > used:
+        for away in range(slabs):
+            out_ref = out_refs[away % CORES]
+            ids = ids_ref[pl.ds(me ^ away, 1), :].astype(jnp.float32)
+            tile = jnp.broadcast_to(ids, out_ref.shape[1:]).astype(out_ref.dtype)
+            out_ref[away // CORES * span + used] = tile
+
+
+def pack(dest, owned, slabs, per_slab, with_ids):
+    slots, tiles, rows, width = owned.shape
     chips = slabs // CORES
     capacity = slots // slabs
-    sent = []
-    for part in range(parts):
-        span = capacity * shares + (1 if with_ids and part == 0 else 0)
-        sent += [jax.ShapeDtypeStruct((chips * span, rows, width), owned.dtype)] * CORES
-    outs = pl.pallas_call(
-        lambda *refs: pack_kernel(slabs, capacity, per_slab, parts, *refs[len(after) :]),
-        out_shape=tuple(sent),
-        in_specs=[ANY] * len(after) + [SMEM, VMEM],
-        out_specs=(VMEM,) * len(sent),
+    span = capacity * tiles + (1 if with_ids else 0)
+    sent = jax.ShapeDtypeStruct((chips * span, rows, width), owned.dtype)
+    return pl.pallas_call(
+        lambda *refs: pack_kernel(slabs, capacity, per_slab, *refs),
+        out_shape=(sent,) * CORES,
+        in_specs=[SMEM, VMEM],
+        out_specs=(VMEM,) * CORES,
         scratch_shapes=[
             pltpu.VMEM((slabs, TILE), jnp.int32),
             pltpu.SMEM((slabs,), jnp.int32),
         ],
         compiler_params=pltpu.CompilerParams(vmem_limit_bytes=VMEM_BYTES),
-        cost_estimate=cost(
-            flops=0, bytes_accessed=2 * owned.size * 2, transcendentals=0
-        ),
+        cost_estimate=cost(flops=0, bytes_accessed=2 * owned.size * 2, transcendentals=0),
         name="pack",
-    )(*after, dest, owned)
-    return [outs[part * CORES : (part + 1) * CORES] for part in range(parts)]
+    )(dest, owned)
 
 
 def merge_kernel(same_ref, other_ref, *out_refs):
@@ -106,33 +97,37 @@
         out_ref[span:] = other_ref[chip * span : (chip + 1) * span]
 
 
-def merge(same, other, chips):
+def merge(same, other, chips, after):
     tiles, rows, width = same.shape
     out = jax.ShapeDtypeStruct((CORES * tiles // chips, rows, width), same.dtype)
     return pl.pallas_call(
-        merge_kernel,
+        lambda *refs: merge_kernel(*refs[len(after) :]),
         out_shape=(out,) * chips,
-        in_specs=[VMEM, VMEM],
+        in_specs=[ANY] * len(after) + [VMEM, VMEM],
         out_specs=(VMEM,) * chips,
         compiler_params=pltpu.CompilerParams(vmem_limit_bytes=VMEM_BYTES),
         cost_estimate=cost(flops=0, bytes_accessed=8 * same.size, transcendentals=0),
         name="merge",
-    )(same, other)
-
-
-def settle_kernel(chips, capacity, first, joint, *refs):
+    )(*after, same, other)
+
+
+def settle_kernel(chips, capacity, parts, part, *refs):
+    first = part is None
     if first:
-        moved_refs, out_refs, meta_ref, ids_ref = refs[:chips], refs[chips:-2], refs[-2], refs[-1]
+        moved_refs, (out_ref, meta_ref, ids_ref) = refs[:chips], refs[chips:]
         span = moved_refs[0].shape[0] // CORES
         for source in range(chips * CORES):
             at = source % CORES * span + span - 1
             tile = moved_refs[source // CORES][at].astype(jnp.float32)
             ids_ref[source : source + 1, :] = tile[:1].astype(jnp.int32)
         pltpu.sync_copy(ids_ref, meta_ref)
+        shares = out_ref.shape[0]
     else:
         meta_ref, moved_refs, out_refs = refs[0], refs[1 : 1 + chips], refs[1 + chips :]
         span = moved_refs[0].shape[0] // CORES
-    shares = out_refs[0].shape[0] if joint else len(out_refs)
+        shares = len(out_refs)
+    tiles = shares * parts
+    rows = moved_refs[0].shape[1]
     mine = lax.axis_index("snap")
     for source in range(chips * CORES):
         moved_ref = moved_refs[source // CORES]
@@ -142,32 +137,37 @@
 
             @pl.when(block >= 0)
             def _():
-                at = source % CORES * span + rank * shares
-                if joint:
-                    out_refs[0][:, block] = moved_ref[pl.ds(at, shares)]
-                else:
-                    for r in range(shares):
-                        out_refs[r][block] = moved_ref[at + (mine ^ r)]
+                at = source % CORES * span + rank * tiles
+                for share in range(shares):
+                    if first:
+                        for k in range(parts):
+                            cells = slice(k * rows, (k + 1) * rows)
+                            out_ref[share, block, cells] = moved_ref[at + share * parts + k]
+                    else:
+                        cells = moved_ref[at + (mine ^ share) * parts + part]
+                        out_refs[share][block] = cells
 
             return 0
 
         lax.fori_loop(0, capacity, place, 0, unroll=4)
 
 
-def settle(meta, moved, capacity, per_slab, shares, joint, after=()):
-    first = meta is None
+def settle(meta, moved, capacity, per_slab, shares, parts, part, after):
+    first = part is None
     chips = len(moved)
     rows, width = moved[0].shape[1:]
-    if joint:
-        pieces = (jax.ShapeDtypeStruct((shares, per_slab, rows, width), moved[0].dtype),)
+    if first:
+        pieces = (
+            jax.ShapeDtypeStruct((shares, per_slab, parts * rows, width), moved[0].dtype),
+            jax.ShapeDtypeStruct((chips * CORES, TILE), jnp.int32),
+        )
     else:
         pieces = (jax.ShapeDtypeStruct((per_slab, rows, width), moved[0].dtype),) * shares
-    ids = jax.ShapeDtypeStruct((chips * CORES, TILE), jnp.int32)
-    outs = pl.pallas_call(
-        lambda *refs: settle_kernel(chips, capacity, first, joint, *refs[len(after) :]),
-        out_shape=pieces + ((ids,) if first else ()),
+    return pl.pallas_call(
+        lambda *refs: settle_kernel(chips, capacity, parts, part, *refs[len(after) :]),
+        out_shape=pieces,
         in_specs=[ANY] * len(after) + ([] if first else [SMEM]) + [VMEM] * chips,
-        out_specs=(VMEM,) * len(pieces) + ((SMEM,) if first else ()),
+        out_specs=(VMEM, SMEM) if first else (VMEM,) * shares,
         scratch_shapes=[pltpu.VMEM((chips * CORES, TILE), jnp.int32)] if first else [],
         compiler_params=pltpu.CompilerParams(vmem_limit_bytes=VMEM_BYTES),
         cost_estimate=cost(
@@ -175,7 +175,6 @@
         ),
         name="settle",
     )(*after, *([] if first else [meta]), *moved)
-    return outs[: len(pieces)], (outs[-1] if first else meta)
 
 
 def whole_rows(refs):
@@ -187,63 +186,62 @@
     return whole_rows([ref.at[share] for share in range(ref.shape[0])])
 
 
-def gram_kernel(parts, *refs):
-    out_ref = refs[-1]
-    shares = refs[0].shape[0]
+def gram_kernel(x_ref, out_ref):
+    shares = x_ref.shape[0]
 
     @pl.when(pl.program_id(0) == 0)
     def _():
         out_ref[...] = jnp.zeros_like(out_ref)
 
-    for part in range(parts):
-        cells = joint_rows(refs[part])
-        at = 0
-        for a in range(shares):
-            product = lax.dot_general(
-                cells[:, a * TILE : (a + 1) * TILE],
-                cells[:, a * TILE :],
-                ROWS_BY_ROWS,
-                preferred_element_type=jnp.float32,
-            )
-            for b in range(a, shares):
-                out_ref[at] += product[:, (b - a) * TILE : (b - a + 1) * TILE]
-                at += 1
+    cells = joint_rows(x_ref)
+    at = 0
+    for a in range(shares):
+        product = lax.dot_general(
+            cells[:, a * TILE : (a + 1) * TILE],
+            cells[:, a * TILE :],
+            ROWS_BY_ROWS,
+            preferred_element_type=jnp.float32,
+        )
+        for b in range(a, shares):
+            out_ref[at] += product[:, (b - a) * TILE : (b - a + 1) * TILE]
+            at += 1
 
 
 def gram_blocks(cells, after, steps=4):
-    shares, blocks, rows, width = cells[0].shape
+    shares, blocks, rows, width = cells.shape
     pairs = shares * (shares + 1) // 2
     full = shares * width
     spec = pl.BlockSpec((shares, blocks // steps, rows, width), lambda i: (0, i, 0, 0))
     return pl.pallas_call(
-        lambda *refs: gram_kernel(len(cells), *refs[len(after) :]),
+        lambda *refs: gram_kernel(*refs[len(after) :]),
         grid=(steps,),
         out_shape=jax.ShapeDtypeStruct((pairs, TILE, TILE), jnp.float32),
-        in_specs=[ANY] * len(after) + [spec] * len(cells),
+        in_specs=[ANY] * len(after) + [spec],
         out_specs=pl.BlockSpec((pairs, TILE, TILE), lambda i: (0, 0, 0)),
         compiler_params=pltpu.CompilerParams(vmem_limit_bytes=VMEM_BYTES),
         cost_estimate=cost(
-            flops=2 * len(cells) * blocks * rows * full * full,
-            bytes_accessed=2 * len(cells) * blocks * rows * full,
+            flops=2 * blocks * rows * full * full,
+            bytes_accessed=2 * blocks * rows * full,
             transcendentals=0,
         ),
         name="gram_blocks",
-    )(*after, *cells)
+    )(*after, cells)
 
 
 def cross_kernel(parts, shares, *refs):
-    out_ref, acc_ref = refs[-2:]
+    x_ref, (out_ref, acc_ref) = refs[0], refs[-2:]
     step = pl.program_id(0)
 
     @pl.when(step == 0)
     def _():
         acc_ref[...] = jnp.zeros_like(acc_ref)
 
+    rows = x_ref.shape[2] // parts
     for part in range(parts):
-        y_refs = refs[parts + part * shares : parts + (part + 1) * shares]
+        cells = slice(part * rows, (part + 1) * rows)
         acc_ref[...] += lax.dot_general(
-            joint_rows(refs[part]),
-            whole_rows(y_refs),
+            whole_rows([x_ref.at[share, :, cells] for share in range(shares)]),
+            whole_rows(refs[1 + part * shares : 1 + (part + 1) * shares]),
             ROWS_BY_ROWS,
             preferred_element_type=jnp.float32,
         )
@@ -257,26 +255,26 @@
 
 
 def cross_sum(x_cells, y_cells, after, steps=4):
-    parts = len(x_cells)
-    shares, blocks, rows, width = x_cells[0].shape
-    spec = pl.BlockSpec((blocks // steps, rows, width), lambda i: (i, 0, 0))
-    joint = pl.BlockSpec((shares, blocks // steps, rows, width), lambda i: (0, i, 0, 0))
+    parts = len(y_cells)
+    shares, blocks, cells, width = x_cells.shape
+    spec = pl.BlockSpec((blocks // steps, cells // parts, width), lambda i: (i, 0, 0))
+    joint = pl.BlockSpec((shares, blocks // steps, cells, width), lambda i: (0, i, 0, 0))
     full = shares * width
     return pl.pallas_call(
         lambda *refs: cross_kernel(parts, shares, *refs[len(after) :]),
         grid=(steps,),
         out_shape=jax.ShapeDtypeStruct((full, full), jnp.float32),
-        in_specs=[ANY] * len(after) + [joint] * parts + [spec] * (parts * shares),
+        in_specs=[ANY] * len(after) + [joint] + [spec] * (parts * shares),
         out_specs=pl.BlockSpec((full, full), lambda i: (0, 0)),
         scratch_shapes=[pltpu.VMEM((full, full), jnp.float32)],
         compiler_params=pltpu.CompilerParams(vmem_limit_bytes=VMEM_BYTES),
         cost_estimate=cost(
-            flops=2 * parts * blocks * rows * full * full,
-            bytes_accessed=4 * parts * blocks * rows * full,
+            flops=2 * blocks * cells * full * full,
+            bytes_accessed=4 * blocks * cells * full,
             transcendentals=0,
         ),
         name="cross_sum",
-    )(*after, *x_cells, *[piece for part in y_cells for piece in part])
+    )(*after, x_cells, *[piece for part in y_cells for piece in part])
 
 
 def three_terms(value):
@@ -445,26 +443,28 @@
     total += lax.dot_general(
         cells, hi_ref[...], LANES_BY_LANES, preferred_element_type=jnp.float32
     )
-    out_ref[:, 0] = total.reshape(out_ref.shape[0], *out_ref.shape[2:])
-
-
-def basis(cells, terms, part, parts, filled, after, steps=4):
+    out_ref[...] = total.reshape(out_ref.shape)
+
+
+def basis(cells, terms, call, calls, filled, after, steps=4):
     shares, blocks, rows, width = cells.shape
     full = shares * width
-    spec = pl.BlockSpec((shares, blocks // steps, rows, width), lambda i: (0, i, 0, 0))
+    size = blocks // calls // steps
+    first = call * steps
+    spec = pl.BlockSpec((shares, size, rows, width), lambda i: (0, first + i, 0, 0))
     term = pl.BlockSpec((full, full), lambda i: (0, 0))
     unread = ([] if filled is None else [filled]) + list(after)
     return pl.pallas_call(
         lambda *refs: basis_kernel(*refs[len(unread) :]),
         grid=(steps,),
-        out_shape=jax.ShapeDtypeStruct((blocks, parts, rows, full), jnp.float32),
+        out_shape=jax.ShapeDtypeStruct((blocks, rows, full), jnp.float32),
         in_specs=[ANY] * len(unread) + [spec] + [term] * 3,
-        out_specs=pl.BlockSpec((blocks // steps, 1, rows, full), lambda i: (i, part, 0, 0)),
+        out_specs=pl.BlockSpec((size, rows, full), lambda i: (first + i, 0, 0)),
         input_output_aliases={} if filled is None else {0: 0},
         compiler_params=pltpu.CompilerParams(vmem_limit_bytes=VMEM_BYTES),
         cost_estimate=cost(
-            flops=6 * blocks * rows * full * full,
-            bytes_accessed=6 * blocks * rows * full,
+            flops=6 * blocks * rows * full * full // calls,
+            bytes_accessed=6 * blocks * rows * full // calls,
             transcendentals=0,
         ),
         name="basis",
@@ -568,11 +568,12 @@
     tiles = full // TILE
     pairs = tiles * (tiles + 1) // 2
 
-    def parted(owned):
-        return owned.reshape(slots, shares, parts, CELL_TILE, width)
-
-    def merged(part):
-        return merge(part[0], swap(part[1], "space", 1), slabs // CORES)
+    def packed(owned, with_ids):
+        tiles = owned.reshape(slots, patch // CELL_TILE, CELL_TILE, width)
+        return pack(patch_dest, tiles, slabs, per_slab, with_ids)
+
+    def merged(sent, after):
+        return merge(sent[0], swap(sent[1], "space", 1), slabs // CORES, after)
 
     def to_chips(joined):
         return [joined[0]] + [swap(joined[m], "space", CORES * m) for m in range(1, len(joined))]
@@ -580,8 +581,8 @@
     def to_rows(pieces):
         return [pieces[0]] + [swap(pieces[r], "snap", r) for r in range(1, shares)]
 
-    def place(meta, moved, joint, after):
-        return settle(meta, moved, slots // slabs, per_slab, shares, joint, after)
+    def place(meta, moved, part, after):
+        return settle(meta, moved, slots // slabs, per_slab, shares, parts, part, after)
 
     def to_pieces(value):
         return lax.all_to_all(value, "space", split_axis=0, concat_axis=0, tiled=True)
@@ -592,32 +593,21 @@
             yield hop
             hop *= 2
 
-    sent_x = pack(patch_dest, parted(owned_x), slabs, per_slab, True)
-    joined_x = [merged(part) for part in sent_x]
-    moved_x = [to_chips(joined) for joined in joined_x]
-    sent_y = pack(patch_dest, parted(owned_y), slabs, per_slab, False)
-    joined_y = [merged(part) for part in sent_y]
-    moved_y = [to_chips(joined) for joined in joined_y]
-
-    def to_joint_rows(pieces):
-        return lax.all_to_all(pieces[0], "snap", split_axis=0, concat_axis=0, tiled=True)
-
-    after = [joined[0] for joined in joined_x[1:]] + [sent_y[0][0]]
-    pieces, meta = place(None, moved_x[0], True, after)
-    x_cells = [to_joint_rows(pieces)]
-    for moved in moved_x[1:]:
-        pieces, _ = place(meta, moved, True, joined_y[0][:1])
-        x_cells.append(to_joint_rows(pieces))
-    gram_local = gram_blocks(x_cells, [joined[0] for joined in joined_y[1:]])
+    moved_x = to_chips(merged(packed(owned_x, True), []))
+    moved_y = to_chips(merged(packed(owned_y, False), moved_x[1:3]))
+    pieces, meta = place(None, moved_x, None, [])
+    x_cells = lax.all_to_all(pieces, "snap", split_axis=0, concat_axis=0, tiled=True)
+
+    gram_local = gram_blocks(x_cells, moved_y[1:2])
     gram = to_pieces(gram_local.reshape(pairs * TILE, TILE))
-    pieces, _ = place(meta, moved_y[0], False, [])
+    pieces = place(meta, moved_y, 0, [gram_local])
     y_cells = [to_rows(pieces)]
     gram = sum_pieces(gram, slabs, pieces[:1])
     for hop in hops():
-        gram = add(gram, swap(gram, "snap", hop), [])
+        gram = add(gram, swap(gram, "snap", hop), y_cells[0][hop : hop + 1])
     gram = lax.all_gather(gram, "space", axis=0, tiled=True)
-    for moved in moved_y[1:]:
-        pieces, _ = place(meta, moved, False, y_cells[-1][1:])
+    for part in range(1, parts):
+        pieces = place(meta, moved_y, part, y_cells[-1][1:3])
         y_cells.append(to_rows(pieces))
 
     steps = factor_steps(gram.reshape(pairs, TILE, TILE), tiles, rows_total, pieces[:1])
@@ -628,15 +618,14 @@
     cross = to_pieces(cross_local)
     r_factor, inverse, *terms = steps.send([cross_local])
 
-    q_basis = basis(x_cells[0], terms, 0, parts, None, [])
+    q_basis = basis(x_cells, terms, 0, 2, None, [])
     cross = sum_pieces(cross, slabs, [q_basis])
-    for part in range(1, parts):
-        q_basis = basis(x_cells[part], terms, part, parts, q_basis, [cross])
+    q_basis = basis(x_cells, terms, 1, 2, q_basis, [cross])
     for hop in hops():
         cross = add(cross, swap(cross, "snap", hop), [q_basis] if hop == 1 else [])
     same = join([cross] + [swap(cross, "space", m) for m in range(CORES, slabs, CORES)])
     projection = project(inverse, same, swap(same, "space", 1), slabs, math.sqrt(rows_total))
-    return q_basis.reshape(per_slab, patch // shares, full), r_factor, projection
+    return q_basis, r_factor, projection
 
 
 def solution(mesh):

time: 284 us -> 258 us (0.908)
  waiting for transfers between devices: 125 us -> 107 us
  starting transfers between devices: 51.8 us -> 40.4 us
  local copies, waits for them, and re-layouts: 24.2 us -> 29.5 us
    ppermute x30 -> x22, waiting for transfers between devices: 103 us -> 90.3 us  [swap(): lax.ppermute(value, axis, [(i, i ^ mask) for i in range(lax.axis_size(axi...]
    ppermute x30 -> x22, starting transfers between devices: 33.3 us -> 27 us  [swap(): lax.ppermute(value, axis, [(i, i ^ mask) for i in range(lax.axis_size(axi...]
    all_to_all x2 -> x1, waiting for transfers between devices: 19.4 us -> 13.2 us  [body(): lax.all_to_all(pieces, 'snap', split_axis=0, concat_axis=0, tiled=True)]
    unnamed x86 -> x82, local copies, waits for them, and re-layouts: 24.2 us -> 29.5 us
    all_to_all x2 -> x1, starting transfers between devices: 9.96 us -> 4.87 us  [body(): lax.all_to_all(pieces, 'snap', split_axis=0, concat_axis=0, tiled=True)]
    pallas_call x11 -> x8, Pallas kernels: 22.8 us -> 21.7 us  [the longest x3 11.2 us: settle(): pl.pallas_call(lambda *refs: settle_kernel(chips, capacity, parts, part,...]
  transfers between devices with their start and end apart: 34 -> 25, of which waited for: 18 -> 14; matrix products, arithmetic and copies ran while one was open for 0% -> 0% of each run, Pallas kernels for 17% -> 20%
where the time goes in v8:
time: 258 us; the launch traced here: 257 us
  waiting for transfers between devices  107 us (41%)
  Pallas kernels  67.8 us (26%)
  starting transfers between devices  40.4 us (16%)
  local copies, waits for them, and re-layouts  29.5 us (11%)
  blocking collectives  10.8 us (4%)
    ppermute x22, waiting for transfers between devices, swap(): lax.ppermute(value, axis, [(i, i ^ mask) for i in range(lax.axis_size(axi...  90.3 us
    unnamed x82, local copies, waits for them, and re-layouts  29.5 us
    ppermute x22, starting transfers between devices, swap(): lax.ppermute(value, axis, [(i, i ^ mask) for i in range(lax.axis_size(axi...  27 us
    pallas_call x4, Pallas kernels, factor_call(): pl.pallas_call(lambda *refs: kernel(*refs[len(after):]), out_shape=out_sh...  19.7 us
    all_to_all x1, waiting for transfers between devices, body(): lax.all_to_all(pieces, 'snap', split_axis=0, concat_axis=0, tiled=True)  13.2 us
    pallas_call x3, Pallas kernels, settle(): pl.pallas_call(lambda *refs: settle_kernel(chips, capacity, parts, part,...  11.2 us
    all_gather x1, blocking collectives, body(): gram = lax.all_gather(gram, 'space', axis=0, tiled=True)  10.8 us
    all_to_all x2, starting transfers between devices, to_pieces(): lax.all_to_all(value, 'space', split_axis=0, concat_axis=0, tiled=True)  8.44 us
  transfers between devices with their start and end apart: 25, of which 14 were waited for; matrix products, arithmetic and copies ran while one was open for 0% of the time, Pallas kernels for 20%

profile of v8, /device:TPU:0, one launch (start us, length us, event | category | flops | bytes accessed | tf_op | source)
XLA Modules:
  0.0 257.1 jit_solution(17728815546903098791)
XLA Ops:
  0.6 2.2 copy-done.2
  3.5 2.0 pack.2
  5.5 1.0 collective-permute-start
  6.6 3.8 %collective-permute-done.refs_1_ = bf16[516,16,128]{2,1,0:T(8,128)(2,1)S(1)} collective-permute-done((bf16[516,16,128]{2,1,0:T(8,128)(2,1)S(1)}, bf16[516,16,128]{2,1,0:T(8,128)(2,1)S(1)}, u32[]{:S(2)}, u32[]{:S(2)}) %collective-permute-start) | collective-permute-done | bytes 2113568 | tf_op jit(solution)/shard_map/ppermute | solution.py:557
  10.7 4.0 %collective-permute-start.1 = (bf16[258,16,128]{2,1,0:T(8,128)(2,1)S(1)}, bf16[258,16,128]{2,1,0:T(8,128)(2,1)S(1)}, u32[]{:S(2)}, u32[]{:S(2)}) collective-permute-start(bf16[258,16,128]{2,1,0:T(8,128)(2,1)S(1)} %get-tuple-element.33), channel_id=1, source_target_pairs={{0,8},{4,12},{8,0},{12,4},{16,24},{20,28},{24,16},{28,20},{1,9},{5... | collective-permute-start | bytes 3170312 | tf_op jit(solution)/shard_map/ppermute | solution.py:557
  15.2 1.0 collective-permute-start.3
  16.2 3.4 %pack.3 = (bf16[512,16,128]{2,1,0:T(8,128)(2,1)S(1)}, bf16[512,16,128]{2,1,0:T(8,128)(2,1)}) custom-call(s32[128]{0:T(128)S(1)} %copy-done.32, bf16[128,8,16,128]{3,2,1,0:T(8,128)(2,1)S(1)} %bitcast.8), custom_call_target="tpu_custom_call" | custom-call | bytes 8388608 | tf_op jit(solution)/shard_map/pack/pallas_call | solution.py:78
  19.6 1.3 copy-done.15
  21.0 17.8 %collective-permute-done.1.refs_1_.refs_0_ = bf16[258,16,128]{2,1,0:T(8,128)(2,1)S(1)} collective-permute-done((bf16[258,16,128]{2,1,0:T(8,128)(2,1)S(1)}, bf16[258,16,128]{2,1,0:T(8,128)(2,1)S(1)}, u32[]{:S(2)}, u32[]{:S(2)}) %collective-permute-start.1) | collective-permute-done | bytes 1056800 | tf_op jit(solution)/shard_map/ppermute | solution.py:557
  38.8 23.6 %collective-permute-done.2.refs_2_.refs_1_ = bf16[258,16,128]{2,1,0:T(8,128)(2,1)S(1)} collective-permute-done((bf16[258,16,128]{2,1,0:T(8,128)(2,1)S(1)}, bf16[258,16,128]{2,1,0:T(8,128)(2,1)S(1)}, u32[]{:S(2)}, u32[]{:S(2)}) %collective-permute-start.2) | collective-permute-done | bytes 1056800 | tf_op jit(solution)/shard_map/ppermute | solution.py:557
  62.4 2.8 %settle.3 = (bf16[4,64,32,128]{3,2,1,0:T(8,128)(2,1)S(1)}, s32[8,128]{1,0:T(8,128)S(1)}) custom-call(bf16[258,16,128]{2,1,0:T(8,128)(2,1)S(1)} %get-tuple-element.32.refs_0_, bf16[258,16,128]{2,1,0:T(8,128)(2,1)S(1)} %collective-permute-done.1.refs_1_.refs_0_, bf16[258,16,128]{2,1,0:T(8,128)(2,1)S(1)} %collective-permute-done.2.refs_2_.refs_1_, ...), custom_call_target="tpu_custom_call" | custom-call | bytes 4227072 | tf_op jit(solution)/shard_map/settle/pallas_call | solution.py:166
  65.2 1.3 copy-done.19
  66.5 4.9 %all-to-all-start = ((bf16[4,64,32,128]{3,2,1,0:T(8,128)(2,1)}), bf16[4,64,32,128]{3,2,1,0:T(8,128)(2,1)S(1)}, u32[]{:S(2)}, u32[]{:S(2)}) async-start(bf16[4,64,32,128]{3,2,1,0:T(8,128)(2,1)} %copy-done.19), calls=%async_computation | async-start | bytes 4194304 | tf_op jit(solution)/shard_map/all_to_all | solution.py:599
  71.4 1.2 copy-done.1
  72.6 1.6 copy-done.16
  74.2 3.0 %merge.3 = (bf16[256,16,128]{2,1,0:T(8,128)(2,1)S(1)}, bf16[256,16,128]{2,1,0:T(8,128)(2,1)S(1)}, bf16[256,16,128]{2,1,0:T(8,128)(2,1)}, bf16[256,16,128]{2,1,0:T(8,128)(2,1)}) custom-call(bf16[258,16,128]{2,1,0:T(8,128)(2,1)S(1)} %collective-permute-done.1.refs_1_.refs_0_, bf16[258,16,128]{2,1,0:T(8,128)(2,1)S(1)} %copy-done.1, ...), custom_call_target="tpu_custom_call" | custom-call | bytes 8388608 | tf_op jit(solution)/shard_map/merge/pallas_call | solution.py:103
  78.6 1.4 collective-permute-start.6
  79.9 1.8 collective-permute-start.7
  81.7 22.6 %collective-permute-done.5.refs_0_.refs_3_.refs_4_ = bf16[256,16,128]{2,1,0:T(8,128)(2,1)S(1)} collective-permute-done((bf16[256,16,128]{2,1,0:T(8,128)(2,1)S(1)}, bf16[256,16,128]{2,1,0:T(8,128)(2,1)S(1)}, u32[]{:S(2)}, u32[]{:S(2)}) %collective-permute-start.5) | collective-permute-done | bytes 1048608 | tf_op jit(solution)/shard_map/ppermute | solution.py:557
  105.3 13.2 %all-to-all-done.refs_1_.refs_0_.refs_2_ = bf16[4,64,32,128]{3,2,1,0:T(8,128)(2,1)S(1)} async-done(((bf16[4,64,32,128]{3,2,1,0:T(8,128)(2,1)}), bf16[4,64,32,128]{3,2,1,0:T(8,128)(2,1)S(1)}, u32[]{:S(2)}, u32[]{:S(2)}) %all-to-all-start) | async-done | bytes 2097184 | tf_op jit(solution)/shard_map/all_to_all | solution.py:599
  118.6 1.2 copy-done.7
  119.8 1.9 gram_blocks.1.refs_0_
  122.5 4.2 %all-to-all-start.1 = ((f32[8,160,128]{2,1,0:T(8,128)}), f32[8,160,128]{2,1,0:T(8,128)}, u32[]{:S(2)}, u32[]{:S(2)}) async-start(f32[8,160,128]{2,1,0:T(8,128)} %bitcast.9), calls=%async_computation.1 | async-start | bytes 1310720 | tf_op jit(solution)/shard_map/all_to_all | solution.py:588
  126.7 1.2 copy-done.8
  128.0 1.1 copy-done.11
  129.1 4.1 %settle.4 = (bf16[64,16,128]{2,1,0:T(8,128)(2,1)S(1)}, bf16[64,16,128]{2,1,0:T(8,128)(2,1)}, bf16[64,16,128]{2,1,0:T(8,128)(2,1)}, bf16[64,16,128]{2,1,0:T(8,128)(2,1)S(1)}) custom-call(f32[10,128,128]{2,1,0:T(8,128)S(1)} %copy-done.11, s32[8,128]{1,0:T(8,128)S(1)} %get-tuple-element.40.refs_1_.refs_2_, bf16[256,16,128]{2,1,0:T(8,128)(2,1)S(1)} %copy-done.5, ...), custom_call_target="tpu_custom_call" | custom-call | bytes 4194304 | tf_op jit(solution)/shard_map/settle/pallas_call | solution.py:166
  134.7 2.4 collective-permute-start.9
  137.9 1.8 sum_pieces.2.refs_1_
  139.6 9.7 %collective-permute-done.8.refs_0_.refs_3_ = bf16[64,16,128]{2,1,0:T(8,128)(2,1)S(1)} collective-permute-done((bf16[64,16,128]{2,1,0:T(8,128)(2,1)}, bf16[64,16,128]{2,1,0:T(8,128)(2,1)S(1)}, u32[]{:S(2)}, u32[]{:S(2)}) %collective-permute-start.8) | collective-permute-done | bytes 262176 | tf_op jit(solution)/shard_map/ppermute | solution.py:557
  149.3 1.5 collective-permute-done.10.refs_2_
  151.4 1.6 add.4.refs_1_
  153.3 2.4 collective-permute-start.12
  155.7 1.2 copy-done.9
  157.8 4.2 %settle.5 = (bf16[64,16,128]{2,1,0:T(8,128)(2,1)S(1)}, bf16[64,16,128]{2,1,0:T(8,128)(2,1)}, bf16[64,16,128]{2,1,0:T(8,128)(2,1)}, bf16[64,16,128]{2,1,0:T(8,128)(2,1)}) custom-call(bf16[64,16,128]{2,1,0:T(8,128)(2,1)S(1)} %copy-done.13, bf16[64,16,128]{2,1,0:T(8,128)(2,1)} %collective-permute-done.9.refs_1_.refs_0_.refs_4_, ...), custom_call_target="tpu_custom_call" | custom-call | bytes 4194304 | tf_op jit(solution)/shard_map/settle/pallas_call | solution.py:166
  163.6 1.2 collective-permute-start.14
  164.8 2.4 collective-permute-start.15
  167.8 1.6 add.5
  169.4 10.8 %all_gather.3 = f32[1280,128]{1,0:T(8,128)S(1)} all-gather(f32[160,128]{1,0:T(8,128)} %add.5), channel_id=1, replica_groups=mesh['space'=8,'snap'=4] {'space'}, dimensions={0}, use_global_device_ids=true | all-gather | bytes 737280 | tf_op jit(solution)/shard_map/all_gather | solution.py:608
  181.1 4.9 %factor.4.refs_0_ = f32[4,8,128,128]{3,2,1,0:T(8,128)S(1)} custom-call(bf16[64,16,128]{2,1,0:T(8,128)(2,1)S(1)} %copy-done.29, f32[10,128,128]{2,1,0:T(8,128)S(1)} %bitcast.10), custom_call_target="tpu_custom_call" | custom-call | flops 7000000000 | bytes 655360 | tf_op jit(solution)/shard_map/factor/pallas_call | solution.py:401
  186.1 4.8 %factor.5.refs_0_ = f32[4,8,128,128]{3,2,1,0:T(8,128)S(1)} custom-call(f32[4,8,128,128]{3,2,1,0:T(8,128)S(1)} %factor.4.refs_0_), custom_call_target="tpu_custom_call", output_to_operand_aliasing={{}: (0, {})} | custom-call | flops 7000000000 | bytes 2097152 | tf_op jit(solution)/shard_map/factor/pallas_call | solution.py:401
  190.9 4.6 %factor.6.refs_0_.refs_1_ = f32[4,8,128,128]{3,2,1,0:T(8,128)S(1)} custom-call(f32[4,8,128,128]{3,2,1,0:T(8,128)S(1)} %factor.5.refs_0_), custom_call_target="tpu_custom_call", output_to_operand_aliasing={{}: (0, {})} | custom-call | flops 7000000000 | bytes 2097152 | tf_op jit(solution)/shard_map/factor/pallas_call | solution.py:401
  195.8 4.5 %cross_sum.1.refs_0_ = f32[512,512]{1,0:T(8,128)} custom-call(f32[4,8,128,128]{3,2,1,0:T(8,128)S(1)} %factor.6.refs_0_.refs_1_, bf16[4,64,32,128]{3,2,1,0:T(8,128)(2,1)S(1)} %all-to-all-done.refs_1_.refs_0_.refs_2_, bf16[64,16,128]{2,1,0:T(8,128)(2,1)S(1)} %copy-done.27, bf16[64,16,128]{2,1,0:T(8,128)(2,1)S(1)} %copy-done.14, ...), custom_call_target="tpu_custom_call" | custom-call | flops 1073741824 | bytes 4194304 | tf_op jit(solution)/shard_map/cross_sum/pallas_call | solution.py:263
  200.3 4.2 %all-to-all-start.2 = ((f32[8,64,512]{2,1,0:T(8,128)}), f32[8,64,512]{2,1,0:T(8,128)}, u32[]{:S(2)}, u32[]{:S(2)}) async-start(f32[8,64,512]{2,1,0:T(8,128)} %bitcast.5), calls=%async_computation.2 | async-start | bytes 2097152 | tf_op jit(solution)/shard_map/all_to_all | solution.py:588
  204.6 1.6 copy-done.18
  206.2 5.4 %factor.7 = (f32[512,512]{1,0:T(8,128)}, f32[512,512]{1,0:T(8,128)S(1)}, bf16[512,512]{1,0:T(8,128)(2,1)S(1)}, bf16[512,512]{1,0:T(8,128)(2,1)S(1)}, bf16[512,512]{1,0:T(8,128)(2,1)S(1)}) custom-call(f32[512,512]{1,0:T(8,128)} %cross_sum.1.refs_0_, f32[4,8,128,128]{3,2,1,0:T(8,128)S(1)} %copy-done.18), custom_call_target="tpu_custom_call" | custom-call | flops 7000000000 | bytes 2097152 | tf_op jit(solution)/shard_map/factor/pallas_call | solution.py:401
  211.6 1.0 copy-done.24
  212.6 3.5 %basis.2.refs_0_ = f32[64,32,512]{2,1,0:T(8,128)} custom-call(bf16[4,64,32,128]{3,2,1,0:T(8,128)(2,1)S(1)} %all-to-all-done.refs_1_.refs_0_.refs_2_, bf16[512,512]{1,0:T(8,128)(2,1)S(1)} %get-tuple-element.52.refs_1_.refs_3_, bf16[512,512]{1,0:T(8,128)(2,1)S(1)} %get-tuple-element.53.refs_2_.refs_4_, bf16[512,512]{1,0:T(8,128)(2,1)S(1)} %get-tuple-element.54.refs_3_.refs_5_), custom_call_target="tpu_custom_call" | custom-call | flops 1610612736 | bytes 3145728 | tf_op jit(solution)/shard_map/basis/pallas_call | solution.py:457
  216.9 3.1 %all-to-all-done.2 = f32[8,64,512]{2,1,0:T(8,128)} async-done(((f32[8,64,512]{2,1,0:T(8,128)}), f32[8,64,512]{2,1,0:T(8,128)}, u32[]{:S(2)}, u32[]{:S(2)}) %all-to-all-start.2) | async-done | bytes 1048608 | tf_op jit(solution)/shard_map/all_to_all | solution.py:588
  220.0 1.9 sum_pieces.3.refs_1_
  221.9 1.0 copy-done.22
  223.9 3.5 %basis.3.refs_0_ = f32[64,32,512]{2,1,0:T(8,128)} custom-call(f32[64,32,512]{2,1,0:T(8,128)} %basis.2.refs_0_, f32[64,512]{1,0:T(8,128)S(1)} %copy-done.23, bf16[4,64,32,128]{3,2,1,0:T(8,128)(2,1)S(1)} %all-to-all-done.refs_1_.refs_0_.refs_2_, bf16[512,512]{1,0:T(8,128)(2,1)S(1)} %get-tuple-element.52.refs_1_.refs_3_, ...), custom_call_target="tpu_custom_call", output_to_operand_aliasing={{}: (0, {})} | custom-call | flops 1610612736 | bytes 3145728 | tf_op jit(solution)/shard_map/basis/pallas_call | solution.py:457
  228.0 1.6 add.6.refs_0_
  229.6 2.0 collective-permute-start.17
  231.6 4.1 %collective-permute-done.17.refs_1_ = f32[64,512]{1,0:T(8,128)S(1)} collective-permute-done((f32[64,512]{1,0:T(8,128)}, f32[64,512]{1,0:T(8,128)S(1)}, u32[]{:S(2)}, u32[]{:S(2)}) %collective-permute-start.17) | collective-permute-done | bytes 131104 | tf_op jit(solution)/shard_map/ppermute | solution.py:557
  236.4 1.6 add.7.refs_0_
  238.0 3.6 %collective-permute-start.20 = (f32[64,512]{1,0:T(8,128)}, f32[64,512]{1,0:T(8,128)S(1)}, u32[]{:S(2)}, u32[]{:S(2)}) collective-permute-start(f32[64,512]{1,0:T(8,128)} %add.7.refs_0_), channel_id=1, source_target_pairs={{0,24},{4,28},{8,16},{12,20},{16,8},{20,12},{24,0},{28,4},{1,25},{... | collective-permute-start | bytes 393224 | tf_op jit(solution)/shard_map/ppermute | solution.py:557
  241.6 1.7 collective-permute-start.19
  243.3 2.0 collective-permute-done.20.refs_3_
  245.3 1.9 collective-permute-done.19.refs_2_
  247.2 1.2 collective-permute-done.18.refs_1_
  249.1 1.9 join.1.refs_1_
  251.0 2.1 collective-permute-done.21.refs_2_
  253.1 1.0 copy-done.20
  254.2 2.9 %project.1 = f32[512,512]{1,0:T(8,128)} custom-call(f32[512,512]{1,0:T(8,128)S(1)} %copy-done.25, f32[256,512]{1,0:T(8,128)S(1)} %copy-done.20, f32[256,512]{1,0:T(8,128)S(1)} %collective-permute-done.21.refs_2_), custom_call_target="tpu_custom_call" | custom-call | tf_op jit(solution)/shard_map/project/pallas_call | solution.py:545
  (92 shorter events, 15.8 us)
Async XLA Ops:
  0.6 2.2 copy-start.2
  2.8 0.7 copy-start.31
  5.5 4.9 %collective-permute-start = (bf16[516,16,128]{2,1,0:T(8,128)(2,1)S(1)}, bf16[516,16,128]{2,1,0:T(8,128)(2,1)S(1)}, u32[]{:S(2)}, u32[]{:S(2)}) collective-permute-start(bf16[516,16,128]{2,1,0:T(8,128)(2,1)S(1)} %get-tuple-element.31), channel_id=1, source_target_pairs={{0,4},{4,0},{8,12},{12,8},{16,20},{20,16},{24,28},{28,24},{1,5},{5... | collective-permute-start | bytes 6340616 | tf_op jit(solution)/shard_map/ppermute | solution.py:557
  10.4 5.8 %copy-start.3 = (bf16[128,128,128]{2,1,0:T(8,128)(2,1)S(1)}, bf16[128,128,128]{2,1,0:T(8,128)(2,1)}, u32[]{:S(2)}) copy-start(bf16[128,128,128]{2,1,0:T(8,128)(2,1)} %param.4) | copy-start | bytes 12582916
  10.4 5.8 %copy-start.32 = (s32[128]{0:T(128)S(1)}, s32[128]{0:T(128)}, u32[]{:S(2)}) copy-start(s32[128]{0:T(128)} %refs_0_.3) | copy-start | bytes 1540
  10.7 28.1 %collective-permute-start.1 = (bf16[258,16,128]{2,1,0:T(8,128)(2,1)S(1)}, bf16[258,16,128]{2,1,0:T(8,128)(2,1)S(1)}, u32[]{:S(2)}, u32[]{:S(2)}) collective-permute-start(bf16[258,16,128]{2,1,0:T(8,128)(2,1)S(1)} %get-tuple-element.33), channel_id=1, source_target_pairs={{0,8},{4,12},{8,0},{12,4},{16,24},{20,28},{24,16},{28,20},{1,9},{5... | collective-permute-start | bytes 3170312 | tf_op jit(solution)/shard_map/ppermute | solution.py:557
  14.7 47.7 %collective-permute-start.2 = (bf16[258,16,128]{2,1,0:T(8,128)(2,1)S(1)}, bf16[258,16,128]{2,1,0:T(8,128)(2,1)S(1)}, u32[]{:S(2)}, u32[]{:S(2)}) collective-permute-start(bf16[258,16,128]{2,1,0:T(8,128)(2,1)S(1)} %get-tuple-element.34), channel_id=1, source_target_pairs={{0,16},{4,20},{8,24},{12,28},{16,0},{20,4},{24,8},{28,12},{1,17},{... | collective-permute-start | bytes 3170312 | tf_op jit(solution)/shard_map/ppermute | solution.py:557
  15.2 47.2 %collective-permute-start.3 = (bf16[258,16,128]{2,1,0:T(8,128)(2,1)S(1)}, bf16[258,16,128]{2,1,0:T(8,128)(2,1)S(1)}, u32[]{:S(2)}, u32[]{:S(2)}) collective-permute-start(bf16[258,16,128]{2,1,0:T(8,128)(2,1)S(1)} %get-tuple-element.35), channel_id=1, source_target_pairs={{0,24},{4,28},{8,16},{12,20},{16,8},{20,12},{24,0},{28,4},{1,25},{... | collective-permute-start | bytes 3170312 | tf_op jit(solution)/shard_map/ppermute | solution.py:557
  19.6 1.3 copy-start.15
  20.9 50.5 %collective-permute-start.4 = (bf16[512,16,128]{2,1,0:T(8,128)(2,1)}, bf16[512,16,128]{2,1,0:T(8,128)(2,1)}, u32[]{:S(2)}, u32[]{:S(2)}) collective-permute-start(bf16[512,16,128]{2,1,0:T(8,128)(2,1)} %get-tuple-element.38), channel_id=1, source_target_pairs={{0,4},{4,0},{8,12},{12,8},{16,20},{20,16},{24,28},{28,24},{1,5},{5... | collective-permute-start | bytes 6291464 | tf_op jit(solution)/shard_map/ppermute | solution.py:557
  62.4 2.8 %copy-start = (bf16[258,16,128]{2,1,0:T(8,128)(2,1)}, bf16[258,16,128]{2,1,0:T(8,128)(2,1)S(1)}, u32[]{:S(2)}) copy-start(bf16[258,16,128]{2,1,0:T(8,128)(2,1)S(1)} %collective-permute-done.2.refs_2_.refs_1_) | copy-start | bytes 3170308
  65.2 1.3 copy-start.19
  66.5 52.0 %all-to-all-start = ((bf16[4,64,32,128]{3,2,1,0:T(8,128)(2,1)}), bf16[4,64,32,128]{3,2,1,0:T(8,128)(2,1)S(1)}, u32[]{:S(2)}, u32[]{:S(2)}) async-start(bf16[4,64,32,128]{3,2,1,0:T(8,128)(2,1)} %copy-done.19), calls=%async_computation | async-start | bytes 4194304 | tf_op jit(solution)/shard_map/all_to_all | solution.py:599
  71.4 1.2 copy-start.1
  72.6 1.6 copy-start.16
  77.2 1.0 copy-start.4
  78.2 26.1 %collective-permute-start.5 = (bf16[256,16,128]{2,1,0:T(8,128)(2,1)S(1)}, bf16[256,16,128]{2,1,0:T(8,128)(2,1)S(1)}, u32[]{:S(2)}, u32[]{:S(2)}) collective-permute-start(bf16[256,16,128]{2,1,0:T(8,128)(2,1)S(1)} %get-tuple-element.39), channel_id=1, source_target_pairs={{0,8},{4,12},{8,0},{12,4},{16,24},{20,28},{24,16},{28,20},{1,9},{5... | collective-permute-start | bytes 3145736 | tf_op jit(solution)/shard_map/ppermute | solution.py:557
  78.6 48.1 %collective-permute-start.6 = (bf16[256,16,128]{2,1,0:T(8,128)(2,1)}, bf16[256,16,128]{2,1,0:T(8,128)(2,1)}, u32[]{:S(2)}, u32[]{:S(2)}) collective-permute-start(bf16[256,16,128]{2,1,0:T(8,128)(2,1)} %get-tuple-element.42), channel_id=1, source_target_pairs={{0,16},{4,20},{8,24},{12,28},{16,0},{20,4},{24,8},{28,12},{1,17},{... | collective-permute-start | bytes 3145736 | tf_op jit(solution)/shard_map/ppermute | solution.py:557
  79.9 46.8 %copy-start.5 = (bf16[256,16,128]{2,1,0:T(8,128)(2,1)S(1)}, bf16[256,16,128]{2,1,0:T(8,128)(2,1)}, u32[]{:S(2)}) copy-start(bf16[256,16,128]{2,1,0:T(8,128)(2,1)} %copy-done.4) | copy-start | bytes 3145732
  79.9 46.8 %collective-permute-start.7 = (bf16[256,16,128]{2,1,0:T(8,128)(2,1)}, bf16[256,16,128]{2,1,0:T(8,128)(2,1)}, u32[]{:S(2)}, u32[]{:S(2)}) collective-permute-start(bf16[256,16,128]{2,1,0:T(8,128)(2,1)} %get-tuple-element.43), channel_id=1, source_target_pairs={{0,24},{4,28},{8,16},{12,20},{16,8},{20,12},{24,0},{28,4},{1,25},{... | collective-permute-start | bytes 3145736 | tf_op jit(solution)/shard_map/ppermute | solution.py:557
  104.3 1.0 copy-start.6
  118.5 1.2 copy-start.7
  121.7 0.8 copy-start.10
  122.5 15.4 %all-to-all-start.1 = ((f32[8,160,128]{2,1,0:T(8,128)}), f32[8,160,128]{2,1,0:T(8,128)}, u32[]{:S(2)}, u32[]{:S(2)}) async-start(f32[8,160,128]{2,1,0:T(8,128)} %bitcast.9), calls=%async_computation.1 | async-start | bytes 1310720 | tf_op jit(solution)/shard_map/all_to_all | solution.py:588
  126.7 1.2 copy-start.8
  128.0 1.1 copy-start.11
  133.2 0.7 copy-start.26
  133.9 0.7 copy-start.33
  134.6 14.7 %collective-permute-start.8 = (bf16[64,16,128]{2,1,0:T(8,128)(2,1)}, bf16[64,16,128]{2,1,0:T(8,128)(2,1)S(1)}, u32[]{:S(2)}, u32[]{:S(2)}) collective-permute-start(bf16[64,16,128]{2,1,0:T(8,128)(2,1)} %get-tuple-element.44), channel_id=1, source_target_pairs={{0,1},{1,0},{2,3},{3,2},{4,5},{5,4},{6,7},{7,6},{8,9},{9,8},{10,11... | collective-permute-start | bytes 786440 | tf_op jit(solution)/shard_map/ppermute | solution.py:557
  134.7 20.9 %collective-permute-start.9 = (bf16[64,16,128]{2,1,0:T(8,128)(2,1)}, bf16[64,16,128]{2,1,0:T(8,128)(2,1)}, u32[]{:S(2)}, u32[]{:S(2)}) collective-permute-start(bf16[64,16,128]{2,1,0:T(8,128)(2,1)} %get-tuple-element.45), channel_id=1, source_target_pairs={{0,2},{1,3},{2,0},{3,1},{4,6},{5,7},{6,4},{7,5},{8,10},{9,11},{10,... | collective-permute-start | bytes 786440 | tf_op jit(solution)/shard_map/ppermute | solution.py:557
  139.6 11.2 %collective-permute-start.10 = (f32[160,128]{1,0:T(8,128)}, f32[160,128]{1,0:T(8,128)S(1)}, u32[]{:S(2)}, u32[]{:S(2)}) collective-permute-start(f32[160,128]{1,0:T(8,128)} %sum_pieces.2.refs_1_), channel_id=1, source_target_pairs={{0,1},{1,0},{2,3},{3,2},{4,5},{5,4},{6,7},{7,6},{8,9},{9,8},{10,11... | collective-permute-start | bytes 245768 | tf_op jit(solution)/shard_map/ppermute | solution.py:557
  149.3 1.5 copy-start.12
  153.0 14.2 %collective-permute-start.11 = (f32[160,128]{1,0:T(8,128)}, f32[160,128]{1,0:T(8,128)S(1)}, u32[]{:S(2)}, u32[]{:S(2)}) collective-permute-start(f32[160,128]{1,0:T(8,128)} %add.4.refs_1_), channel_id=1, source_target_pairs={{0,2},{1,3},{2,0},{3,1},{4,6},{5,7},{6,4},{7,5},{8,10},{9,11},{10,... | collective-permute-start | bytes 245768 | tf_op jit(solution)/shard_map/ppermute | solution.py:557
  153.3 42.2 %collective-permute-start.12 = (bf16[64,16,128]{2,1,0:T(8,128)(2,1)}, bf16[64,16,128]{2,1,0:T(8,128)(2,1)S(1)}, u32[]{:S(2)}, u32[]{:S(2)}) collective-permute-start(bf16[64,16,128]{2,1,0:T(8,128)(2,1)} %copy-done.33), channel_id=1, source_target_pairs={{0,3},{1,2},{2,1},{3,0},{4,7},{5,6},{6,5},{7,4},{8,11},{9,10},{10,... | collective-permute-start | bytes 786440 | tf_op jit(solution)/shard_map/ppermute | solution.py:557
  155.7 1.2 copy-start.9
  156.9 0.9 copy-start.13
  162.1 0.7 copy-start.28
  162.8 32.7 %collective-permute-start.13 = (bf16[64,16,128]{2,1,0:T(8,128)(2,1)}, bf16[64,16,128]{2,1,0:T(8,128)(2,1)S(1)}, u32[]{:S(2)}, u32[]{:S(2)}) collective-permute-start(bf16[64,16,128]{2,1,0:T(8,128)(2,1)} %get-tuple-element.49), channel_id=1, source_target_pairs={{0,1},{1,0},{2,3},{3,2},{4,5},{5,4},{6,7},{7,6},{8,9},{9,8},{10,11... | collective-permute-start | bytes 786440 | tf_op jit(solution)/shard_map/ppermute | solution.py:557
  163.6 31.9 %collective-permute-start.14 = (bf16[64,16,128]{2,1,0:T(8,128)(2,1)}, bf16[64,16,128]{2,1,0:T(8,128)(2,1)S(1)}, u32[]{:S(2)}, u32[]{:S(2)}) collective-permute-start(bf16[64,16,128]{2,1,0:T(8,128)(2,1)} %get-tuple-element.50), channel_id=1, source_target_pairs={{0,2},{1,3},{2,0},{3,1},{4,6},{5,7},{6,4},{7,5},{8,10},{9,11},{10,... | collective-permute-start | bytes 786440 | tf_op jit(solution)/shard_map/ppermute | solution.py:557
  164.8 30.7 %collective-permute-start.15 = (bf16[64,16,128]{2,1,0:T(8,128)(2,1)}, bf16[64,16,128]{2,1,0:T(8,128)(2,1)S(1)}, u32[]{:S(2)}, u32[]{:S(2)}) collective-permute-start(bf16[64,16,128]{2,1,0:T(8,128)(2,1)} %get-tuple-element.51), channel_id=1, source_target_pairs={{0,3},{1,2},{2,1},{3,0},{4,7},{5,6},{6,5},{7,4},{8,11},{9,10},{10,... | collective-permute-start | bytes 786440 | tf_op jit(solution)/shard_map/ppermute | solution.py:557
  180.2 0.9 copy-start.29
  190.9 4.9 %copy-start.14 = (bf16[64,16,128]{2,1,0:T(8,128)(2,1)S(1)}, bf16[64,16,128]{2,1,0:T(8,128)(2,1)}, u32[]{:S(2)}) copy-start(bf16[64,16,128]{2,1,0:T(8,128)(2,1)} %copy-done.12) | copy-start | bytes 786436
  190.9 4.9 %copy-start.27 = (bf16[64,16,128]{2,1,0:T(8,128)(2,1)S(1)}, bf16[64,16,128]{2,1,0:T(8,128)(2,1)}, u32[]{:S(2)}) copy-start(bf16[64,16,128]{2,1,0:T(8,128)(2,1)} %copy-done.26) | copy-start | bytes 786436
  190.9 4.9 %copy-start.30 = (bf16[64,16,128]{2,1,0:T(8,128)(2,1)S(1)}, bf16[64,16,128]{2,1,0:T(8,128)(2,1)}, u32[]{:S(2)}) copy-start(bf16[64,16,128]{2,1,0:T(8,128)(2,1)} %copy-done.28) | copy-start | bytes 786436
  195.5 4.8 %copy-start.17 = (f32[4,8,128,128]{3,2,1,0:T(8,128)}, f32[4,8,128,128]{3,2,1,0:T(8,128)S(1)}, u32[]{:S(2)}) copy-start(f32[4,8,128,128]{3,2,1,0:T(8,128)S(1)} %factor.6.refs_0_.refs_1_) | copy-start | bytes 6291460
  200.3 19.7 %all-to-all-start.2 = ((f32[8,64,512]{2,1,0:T(8,128)}), f32[8,64,512]{2,1,0:T(8,128)}, u32[]{:S(2)}, u32[]{:S(2)}) async-start(f32[8,64,512]{2,1,0:T(8,128)} %bitcast.5), calls=%async_computation.2 | async-start | bytes 2097152 | tf_op jit(solution)/shard_map/all_to_all | solution.py:588
  204.6 1.6 copy-start.18
  211.6 1.0 copy-start.24
  216.0 0.8 copy-start.21
  221.9 5.4 %collective-permute-start.16 = (f32[64,512]{1,0:T(8,128)}, f32[64,512]{1,0:T(8,128)S(1)}, u32[]{:S(2)}, u32[]{:S(2)}) collective-permute-start(f32[64,512]{1,0:T(8,128)} %sum_pieces.3.refs_1_), channel_id=1, source_target_pairs={{0,1},{1,0},{2,3},{3,2},{4,5},{5,4},{6,7},{7,6},{8,9},{9,8},{10,11... | collective-permute-start | bytes 393224 | tf_op jit(solution)/shard_map/ppermute | solution.py:557
  221.9 1.0 copy-start.22
  223.0 0.9 copy-start.23
  227.4 25.8 %copy-start.25 = (f32[512,512]{1,0:T(8,128)S(1)}, f32[512,512]{1,0:T(8,128)}, u32[]{:S(2)}) copy-start(f32[512,512]{1,0:T(8,128)} %copy-done.24) | copy-start | bytes 3145732
  227.4 0.6 copy-start.34
  229.6 6.1 %collective-permute-start.17 = (f32[64,512]{1,0:T(8,128)}, f32[64,512]{1,0:T(8,128)S(1)}, u32[]{:S(2)}, u32[]{:S(2)}) collective-permute-start(f32[64,512]{1,0:T(8,128)} %add.6.refs_0_), channel_id=1, source_target_pairs={{0,2},{1,3},{2,0},{3,1},{4,6},{5,7},{6,4},{7,5},{8,10},{9,11},{10,... | collective-permute-start | bytes 393224 | tf_op jit(solution)/shard_map/ppermute | solution.py:557
  235.7 0.7 copy-start.35
  238.0 7.3 %collective-permute-start.20 = (f32[64,512]{1,0:T(8,128)}, f32[64,512]{1,0:T(8,128)S(1)}, u32[]{:S(2)}, u32[]{:S(2)}) collective-permute-start(f32[64,512]{1,0:T(8,128)} %add.7.refs_0_), channel_id=1, source_target_pairs={{0,24},{4,28},{8,16},{12,20},{16,8},{20,12},{24,0},{28,4},{1,25},{... | collective-permute-start | bytes 393224 | tf_op jit(solution)/shard_map/ppermute | solution.py:557
  241.6 5.7 %collective-permute-start.19 = (f32[64,512]{1,0:T(8,128)}, f32[64,512]{1,0:T(8,128)S(1)}, u32[]{:S(2)}, u32[]{:S(2)}) collective-permute-start(f32[64,512]{1,0:T(8,128)} %add.7.refs_0_), channel_id=1, source_target_pairs={{0,16},{4,20},{8,24},{12,28},{16,0},{20,4},{24,8},{28,12},{1,17},{... | collective-permute-start | bytes 393224 | tf_op jit(solution)/shard_map/ppermute | solution.py:557
  243.3 5.2 %collective-permute-start.18 = (f32[64,512]{1,0:T(8,128)}, f32[64,512]{1,0:T(8,128)S(1)}, u32[]{:S(2)}, u32[]{:S(2)}) collective-permute-start(f32[64,512]{1,0:T(8,128)} %add.7.refs_0_), channel_id=1, source_target_pairs={{0,8},{4,12},{8,0},{12,4},{16,24},{20,28},{24,16},{28,20},{1,9},{5... | collective-permute-start | bytes 393224 | tf_op jit(solution)/shard_map/ppermute | solution.py:557
  245.3 3.1 %copy-start.36 = (f32[64,512]{1,0:T(8,128)}, f32[64,512]{1,0:T(8,128)S(1)}, u32[]{:S(2)}) copy-start(f32[64,512]{1,0:T(8,128)S(1)} %collective-permute-done.20.refs_3_) | copy-start | bytes 393220
  247.2 1.2 copy-start.37
  248.4 0.6 copy-start.38
  251.0 2.1 collective-permute-start.21
  253.1 1.0 copy-start.20
  (2 other events, 1.3 us)

commit v9 on v6

v9 whole, which is shorter than its diff:
```python
import math

import jax
import jax.numpy as jnp
from jax import lax
from jax.experimental import pallas as pl
from jax.experimental.pallas import tpu as pltpu
from jax.sharding import PartitionSpec as P

TILE = 128
GROUP = 8
CORES = 2
VMEM_BYTES = 32 * 1024 * 1024
HIGHEST = lax.Precision.HIGHEST
SMEM = pl.BlockSpec(memory_space=pltpu.SMEM)
VMEM = pl.BlockSpec(memory_space=pltpu.VMEM)
ANY = pl.BlockSpec(memory_space=pl.ANY)
LIGHT = pl.CostEstimate(flops=1, bytes_accessed=1, transcendentals=0)
ROWS_BY_ROWS = (((0,), (0,)), ((), ()))
LANES_BY_LANES = (((1,), (1,)), ((), ()))


def pack_kernel(slabs, capacity, per_slab, shares_of, dest_ref, owned_ref, *refs):
    out_refs, (ids_ref, count_ref) = refs[:-2], refs[-2:]
    chips = slabs // CORES
    me = lax.axis_index("space")
    mine = lax.axis_index("snap")
    lane = lax.broadcasted_iota(jnp.int32, (1, TILE), 1)
    ids_ref[...] = jnp.full_like(ids_ref, -1)
    for slab in range(slabs):
        count_ref[slab] = 0

    def place(i, _):
        block = dest_ref[i]

        @pl.when(block >= 0)
        def _():
            slab = lax.div(block, per_slab)
            rank = count_ref[slab]
            count_ref[slab] = rank + 1
            here = pl.ds(slab, 1)
            ids_ref[here, :] = jnp.where(lane == rank, block - slab * per_slab, ids_ref[here, :])
            away = slab ^ me
            chip = lax.shift_right_logical(away, 1)
            for core in range(CORES):

                @pl.when((away & 1) == core)
                def _():
                    for group, shares in enumerate(shares_of):
                        out_ref = out_refs[group * CORES + core]
                        at = chip * (out_ref.shape[0] // chips) + rank * len(shares)
                        for k, share in enumerate(shares):
                            out_ref[at + k] = owned_ref[i, mine ^ share]

        return 0

    lax.fori_loop(0, dest_ref.shape[0], place, 0, unroll=2)
    for group, shares in enumerate(shares_of):
        used = capacity * len(shares)
        for away in range(slabs):
            out_ref = out_refs[group * CORES + away % CORES]
            span = out_ref.shape[0] // chips
            if span > used:
                ids = ids_ref[pl.ds(me ^ away, 1), :].astype(jnp.float32)
                tile = jnp.broadcast_to(ids, out_ref.shape[1:]).astype(out_ref.dtype)
                out_ref[away // CORES * span + used] = tile


def pack(dest, owned, slabs, per_slab, shares_of, with_ids, after):
    slots, _, rows, width = owned.shape
    chips = slabs // CORES
    capacity = slots // slabs
    sent = []
    for group, shares in enumerate(shares_of):
        span = capacity * len(shares) + (1 if with_ids and group == 0 else 0)
        sent += [jax.ShapeDtypeStruct((chips * span, rows, width), owned.dtype)] * CORES
    outs = pl.pallas_call(
        lambda *refs: pack_kernel(slabs, capacity, per_slab, shares_of, *refs[len(after) :]),
        out_shape=tuple(sent),
        in_specs=[ANY] * len(after) + [SMEM, VMEM],
        out_specs=(VMEM,) * len(sent),
        scratch_shapes=[
            pltpu.VMEM((slabs, TILE), jnp.int32),
            pltpu.SMEM((slabs,), jnp.int32),
        ],
        compiler_params=pltpu.CompilerParams(vmem_limit_bytes=VMEM_BYTES),
        cost_estimate=LIGHT,
        name="pack",
    )(*after, dest, owned)
    return [outs[at : at + CORES] for at in range(0, len(outs), CORES)]


def merge_kernel(same_ref, other_ref, *out_refs):
    span = same_ref.shape[0] // len(out_refs)
    for chip, out_ref in enumerate(out_refs):
        out_ref[:span] = same_ref[chip * span : (chip + 1) * span]
        out_ref[span:] = other_ref[chip * span : (chip + 1) * span]


def pick_kernel(picked, same_ref, other_ref, *out_refs):
    for chip, out_ref in enumerate(out_refs):
        for owner, ref in enumerate((same_ref, other_ref)):
            out_ref[owner] = ref[chip, :, picked]


def merge(same, other, chips, after, picked=None, of=1):
    tiles, rows, width = same.shape
    if picked is None:
        kernel = merge_kernel
        shape = (CORES * tiles // chips, rows, width)
    else:
        kernel = lambda *refs: pick_kernel(picked, *refs)
        ranks = tiles // chips // of
        shape = (CORES, ranks, picked.stop - picked.start, rows, width)
        same, other = (value.reshape(chips, ranks, of, rows, width) for value in (same, other))
    outs = pl.pallas_call(
        lambda *refs: kernel(*refs[len(after) :]),
        out_shape=(jax.ShapeDtypeStruct(shape, same.dtype),) * chips,
        in_specs=[ANY] * len(after) + [VMEM, VMEM],
        out_specs=(VMEM,) * chips,
        compiler_params=pltpu.CompilerParams(vmem_limit_bytes=VMEM_BYTES),
        cost_estimate=LIGHT,
        name="merge",
    )(*after, same, other)
    return [out.reshape(-1, rows, width) for out in outs]


def settle_kernel(chips, capacity, with_ids, far, *refs):
    if with_ids:
        moved_refs, out_refs, meta_ref, ids_ref = refs[:chips], refs[chips:-2], refs[-2], refs[-1]
        span = moved_refs[0].shape[0] // CORES
        for source in range(chips * CORES):
            at = source % CORES * span + span - 1
            tile = moved_refs[source // CORES][at].astype(jnp.float32)
            ids_ref[source : source + 1, :] = tile[:1].astype(jnp.int32)
        pltpu.sync_copy(ids_ref, meta_ref)
    else:
        meta_ref, moved_refs, out_refs = refs[0], refs[1 : 1 + chips], refs[1 + chips :]
        span = moved_refs[0].shape[0] // CORES
    mine = lax.axis_index("snap")
    count = len(far) or len(out_refs)
    for source in range(chips * CORES):
        moved_ref = moved_refs[source // CORES]

        def place(rank, _):
            block = meta_ref[source, rank]

            @pl.when(block >= 0)
            def _():
                at = source % CORES * span + rank * count
                for k in range(count):
                    if far:
                        out_refs[0][mine ^ far[k], block] = moved_ref[at + k]
                    else:
                        out_refs[k][block] = moved_ref[at + k]

            return 0

        lax.fori_loop(0, capacity, place, 0, unroll=4)


def settle(meta, moved, capacity, per_slab, shares, far, after):
    with_ids = meta is None
    chips = len(moved)
    rows, width = moved[0].shape[1:]
    if far:
        pieces = (jax.ShapeDtypeStruct((shares, per_slab, rows, width), moved[0].dtype),)
    else:
        pieces = (jax.ShapeDtypeStruct((per_slab, rows, width), moved[0].dtype),) * (shares // 2)
    ids = jax.ShapeDtypeStruct((chips * CORES, TILE), jnp.int32)
    outs = pl.pallas_call(
        lambda *refs: settle_kernel(chips, capacity, with_ids, far, *refs[len(after) :]),
        out_shape=pieces + ((ids,) if with_ids else ()),
        in_specs=[ANY] * len(after) + ([] if with_ids else [SMEM]) + [VMEM] * chips,
        out_specs=(VMEM,) * len(pieces) + ((SMEM,) if with_ids else ()),
        scratch_shapes=[pltpu.VMEM((chips * CORES, TILE), jnp.int32)] if with_ids else [],
        compiler_params=pltpu.CompilerParams(vmem_limit_bytes=VMEM_BYTES),
        cost_estimate=LIGHT,
        name="settle",
    )(*after, *([] if with_ids else [meta]), *moved)
    return list(outs[: len(pieces)]), (outs[-1] if with_ids else meta)


def by_distance(refs):
    near = len(refs) - 1
    mine = lax.axis_index("snap")
    return list(refs[:near]) + [refs[near].at[mine ^ share] for share in range(near, 2 * near)]


def cell_specs(shares, size, rows, width, first):
    near = pl.BlockSpec((size, rows, width), lambda i: (first + i, 0, 0))
    far = pl.BlockSpec((shares, size, rows, width), lambda i: (0, first + i, 0, 0))
    return [near] * (shares // 2) + [far]


def whole_rows(refs):
    blocks, rows, width = refs[0].shape
    return jnp.concatenate([ref[...].reshape(blocks * rows, width) for ref in refs], axis=1)


def tile_of(row, lane, tiles):
    return row * tiles - lax.div(row * (row - 1), 2) + lane - row


def gram_kernel(shares, *refs):
    out_ref, acc_ref = refs[-2:]
    step = pl.program_id(0)

    @pl.when(step == 0)
    def _():
        acc_ref[...] = jnp.zeros_like(acc_ref)

    cells = whole_rows(by_distance(refs[:-2]))
    acc_ref[...] += lax.dot_general(
        cells, cells, ROWS_BY_ROWS, preferred_element_type=jnp.float32
    )

    @pl.when(step == pl.num_programs(0) - 1)
    def _():
        mine = lax.axis_index("snap")
        for a in range(shares):
            for b in range(shares):
                row, lane = mine ^ a, mine ^ b

                @pl.when(row <= lane)
                def _():
                    out_ref[tile_of(row, lane, shares)] = acc_ref[
                        a * TILE : (a + 1) * TILE, b * TILE : (b + 1) * TILE
                    ]


def gram_blocks(cells, after, steps=4):
    shares, blocks, rows, width = cells[-1].shape
    pairs = shares * (shares + 1) // 2
    full = shares * width
    return pl.pallas_call(
        lambda *refs: gram_kernel(shares, *refs[len(after) :]),
        grid=(steps,),
        out_shape=jax.ShapeDtypeStruct((pairs, TILE, TILE), jnp.float32),
        in_specs=[ANY] * len(after) + cell_specs(shares, blocks // steps, rows, width, 0),
        out_specs=pl.BlockSpec((pairs, TILE, TILE), lambda i: (0, 0, 0)),
        scratch_shapes=[pltpu.VMEM((full, full), jnp.float32)],
        compiler_params=pltpu.CompilerParams(vmem_limit_bytes=VMEM_BYTES),
        cost_estimate=LIGHT,
        name="gram_blocks",
    )(*after, *cells)


def cross_kernel(shares, *refs):
    out_ref, acc_ref = refs[-2:]
    step = pl.program_id(0)

    @pl.when(step == 0)
    def _():
        acc_ref[...] = jnp.zeros_like(acc_ref)

    count = len(refs) // 2 - 1
    acc_ref[...] += lax.dot_general(
        whole_rows(by_distance(refs[:count])),
        whole_rows(by_distance(refs[count : 2 * count])),
        ROWS_BY_ROWS,
        preferred_element_type=jnp.float32,
    )

    @pl.when(step == pl.num_programs(0) - 1)
    def _():
        mine = lax.axis_index("snap")
        for a in range(shares):
            rows = pl.ds(pl.multiple_of((mine ^ a) * TILE, TILE), TILE)
            for b in range(shares):
                lanes = pl.ds(pl.multiple_of((mine ^ b) * TILE, TILE), TILE)
                out_ref[rows, lanes] = acc_ref[
                    a * TILE : (a + 1) * TILE, b * TILE : (b + 1) * TILE
                ]


def cross_sum(x_cells, y_cells, after, steps=4):
    shares, blocks, rows, width = x_cells[-1].shape
    full = shares * width
    specs = cell_specs(shares, blocks // steps, rows, width, 0)
    return pl.pallas_call(
        lambda *refs: cross_kernel(shares, *refs[len(after) :]),
        grid=(steps,),
        out_shape=jax.ShapeDtypeStruct((full, full), jnp.float32),
        in_specs=[ANY] * len(after) + specs * 2,
        out_specs=pl.BlockSpec((full, full), lambda i: (0, 0)),
        scratch_shapes=[pltpu.VMEM((full, full), jnp.float32)],
        compiler_params=pltpu.CompilerParams(vmem_limit_bytes=VMEM_BYTES),
        cost_estimate=LIGHT,
        name="cross_sum",
    )(*after, *x_cells, *y_cells)


def three_terms(value):
    high = value.astype(jnp.bfloat16).astype(jnp.float32)
    rest = value - high
    middle = rest.astype(jnp.bfloat16).astype(jnp.float32)
    return high, middle, rest - middle


def lane_of(row, lane):
    return jnp.broadcast_to(row[:, lane : lane + 1], row.shape)


def row_of(ref, row):
    return jnp.broadcast_to(ref[row : row + 1, :], (GROUP, TILE))


def factor_tile(a_ref, w_ref, u_ref, v_ref):
    panels = TILE // GROUP
    a_rows = [row_of(a_ref, i) for i in range(GROUP)]
    w_rows = [row_of(w_ref, i) for i in range(GROUP)]
    for p in range(panels):
        base = p * GROUP
        small = {
            (i, k): lane_of(a_rows[i], base + k) for i in range(GROUP) for k in range(i, GROUP)
        }
        for j in range(GROUP):
            scale = lax.rsqrt(small[j, j])
            a_rows[j] = a_rows[j] * scale
            w_rows[j] = w_rows[j] * scale
            u_ref[base + j : base + j + 1, :] = a_rows[j][:1]
            v_ref[base + j : base + j + 1, :] = w_rows[j][:1]
            below = {k: small[j, k] * scale for k in range(j + 1, GROUP)}
            for k in range(j + 1, GROUP):
                for m in range(k, GROUP):
                    small[k, m] = small[k, m] - below[k] * below[m]
            for k in range(j + 1, GROUP):
                a_rows[k] = a_rows[k] - below[k] * a_rows[j]
                w_rows[k] = w_rows[k] - below[k] * w_rows[j]
        if p + 1 == panels:
            break
        after = base + GROUP
        next_a = [row_of(a_ref, after + i) for i in range(GROUP)]
        next_w = [row_of(w_ref, after + i) for i in range(GROUP)]
        for i in range(GROUP):
            for k in range(GROUP):
                factor = lane_of(a_rows[k], after + i)
                next_a[i] = next_a[i] - factor * a_rows[k]
                next_w[i] = next_w[i] - factor * w_rows[k]
        if p + 2 < panels:
            done = after + GROUP
            u = u_ref[base:after, :]
            v = v_ref[base:after, :]
            uh, um, ul = three_terms(u)
            vh, vm, vl = three_terms(v)
            left = jnp.concatenate([uh, uh, um, uh, ul, um], axis=0).astype(jnp.bfloat16)
            right_a = jnp.concatenate([uh, um, uh, ul, uh, um], axis=0)
            right_w = jnp.concatenate([vh, vm, vh, vl, vh, vm], axis=0)
            right = jnp.concatenate([right_a, right_w], axis=1).astype(jnp.bfloat16)
            update = lax.dot_general(
                left, right, ROWS_BY_ROWS, preferred_element_type=jnp.float32
            )
            a_ref[done:, :] = a_ref[done:, :] - update[done:, :TILE]
            w_ref[done:, :] = w_ref[done:, :] - update[done:, TILE:]
        a_rows, w_rows = next_a, next_w


def factor_step(tiles, b, wide, a_ref, w_ref, u_ref, v_ref):
    row = lax.broadcasted_iota(jnp.int32, (TILE, TILE), 0)
    lane = lax.broadcasted_iota(jnp.int32, (TILE, TILE), 1)
    a_ref[...] = wide[b, b]
    w_ref[...] = jnp.where(row == lane, 1.0, 0.0)
    factor_tile(a_ref, w_ref, u_ref, v_ref)
    inverse = v_ref[...]
    wide[b, b] = jnp.where(row <= lane, u_ref[...], 0.0)
    wide[b, tiles + b] = inverse
    for j in range(1, tiles):
        wide[b, b + j] = lax.dot(
            inverse, wide[b, b + j], precision=HIGHEST, preferred_element_type=jnp.float32
        )
    for r in range(b + 1, tiles):
        for c in list(range(r, tiles)) + list(range(tiles, tiles + b + 1)):
            update = lax.dot_general(
                wide[b, r],
                wide[b, c],
                ROWS_BY_ROWS,
                precision=HIGHEST,
                preferred_element_type=jnp.float32,
            )
            wide[r, c] = -update if c == tiles + b else wide[r, c] - update


def first_kernel(tiles, rows_total, g_ref, wide, *scratch):
    at = 0
    for a in range(tiles):
        for b in range(a, tiles):
            wide[a, b] = g_ref[at] / rows_total
            at += 1
    factor_step(tiles, 0, wide, *scratch)


def next_kernel(tiles, b, _, wide, *scratch):
    factor_step(tiles, b, wide, *scratch)


def last_kernel(tiles, wide, r_ref, inv_ref, hi_ref, mid_ref, lo_ref, *scratch):
    factor_step(tiles, tiles - 1, wide, *scratch)
    zero = jnp.zeros((TILE, TILE), jnp.float32)
    mine = lax.axis_index("snap")
    for a in range(tiles):
        rows = slice(a * TILE, (a + 1) * TILE)
        for b in range(tiles):
            lanes = slice(b * TILE, (b + 1) * TILE)
            r_ref[rows, lanes] = wide[a, b] if b >= a else zero
            value = wide[a, tiles + b] if b <= a else zero
            inv_ref[rows, lanes] = value
            high, middle, low = three_terms(value)
            lanes = pl.ds(pl.multiple_of((mine ^ b) * TILE, TILE), TILE)
            hi_ref[rows, lanes] = high.astype(jnp.bfloat16)
            mid_ref[rows, lanes] = middle.astype(jnp.bfloat16)
            lo_ref[rows, lanes] = low.astype(jnp.bfloat16)


def factor_call(kernel, out_shape, value, after, aliases, tiles):
    many = isinstance(out_shape, tuple)
    return pl.pallas_call(
        lambda *refs: kernel(*refs[len(after) :]),
        out_shape=out_shape,
        in_specs=[ANY] * len(after) + [VMEM],
        out_specs=(VMEM,) * len(out_shape) if many else VMEM,
        scratch_shapes=[pltpu.VMEM((TILE, TILE), jnp.float32)] * 4,
        input_output_aliases={len(after): 0} if aliases else {},
        compiler_params=pltpu.CompilerParams(vmem_limit_bytes=VMEM_BYTES),
        cost_estimate=LIGHT,
        name="factor",
    )(*after, value)


def factor_steps(blocks, tiles, rows_total, after):
    state = jax.ShapeDtypeStruct((tiles, 2 * tiles, TILE, TILE), jnp.float32)
    full = jax.ShapeDtypeStruct((tiles * TILE, tiles * TILE), jnp.float32)
    term = jax.ShapeDtypeStruct(full.shape, jnp.bfloat16)
    value = factor_call(
        lambda *refs: first_kernel(tiles, rows_total, *refs), state, blocks, after, False, tiles
    )
    for b in range(1, tiles - 1):
        after = yield value
        value = factor_call(
            lambda *refs: next_kernel(tiles, b, *refs), state, value, after, True, tiles
        )
    after = yield value
    yield factor_call(
        lambda *refs: last_kernel(tiles, *refs), (full, full, term, term, term), value, after, False, tiles
    )


def basis_kernel(*refs):
    hi_ref, mid_ref, lo_ref, out_ref = refs[-4:]
    cells = whole_rows(by_distance(refs[:-4]))
    total = lax.dot_general(
        cells, lo_ref[...], LANES_BY_LANES, preferred_element_type=jnp.float32
    )
    total += lax.dot_general(
        cells, mid_ref[...], LANES_BY_LANES, preferred_element_type=jnp.float32
    )
    total += lax.dot_general(
        cells, hi_ref[...], LANES_BY_LANES, preferred_element_type=jnp.float32
    )
    out_ref[...] = total.reshape(out_ref.shape)


def basis(cells, terms, call, calls, filled, after, steps=4):
    shares, blocks, rows, width = cells[-1].shape
    full = shares * width
    size = blocks // calls // steps
    first = call * steps
    term = pl.BlockSpec((full, full), lambda i: (0, 0))
    unread = ([] if filled is None else [filled]) + list(after)
    return pl.pallas_call(
        lambda *refs: basis_kernel(*refs[len(unread) :]),
        grid=(steps,),
        out_shape=jax.ShapeDtypeStruct((blocks, rows, full), jnp.float32),
        in_specs=[ANY] * len(unread) + cell_specs(shares, size, rows, width, first) + [term] * 3,
        out_specs=pl.BlockSpec((size, rows, full), lambda i: (first + i, 0, 0)),
        input_output_aliases={} if filled is None else {0: 0},
        compiler_params=pltpu.CompilerParams(vmem_limit_bytes=VMEM_BYTES),
        cost_estimate=LIGHT,
        name="basis",
    )(*unread, *cells, *terms)


def sum_kernel(count, copies, value_ref, out_ref):
    rows = value_ref.shape[0] // count
    total = value_ref[:rows]
    for i in range(1, count):
        total += value_ref[i * rows : (i + 1) * rows]
    for i in range(copies):
        out_ref[i * rows : (i + 1) * rows] = total


def sum_pieces(value, count, after, copies=1):
    rows, lanes = value.shape
    return pl.pallas_call(
        lambda *refs: sum_kernel(count, copies, *refs[len(after) :]),
        out_shape=jax.ShapeDtypeStruct((rows // count * copies, lanes), value.dtype),
        in_specs=[ANY] * len(after) + [VMEM],
        out_specs=VMEM,
        cost_estimate=LIGHT,
        name="sum_pieces",
    )(*after, value)


def add_kernel(one_ref, two_ref, out_ref):
    out_ref[...] = one_ref[...] + two_ref[...]


def add(one, two, after):
    return pl.pallas_call(
        lambda *refs: add_kernel(*refs[len(after) :]),
        out_shape=jax.ShapeDtypeStruct(one.shape, one.dtype),
        in_specs=[ANY] * len(after) + [VMEM, VMEM],
        out_specs=VMEM,
        cost_estimate=LIGHT,
        name="add",
    )(*after, one, two)


def join_kernel(*refs):
    rows = refs[0].shape[0]
    for i, ref in enumerate(refs[:-1]):
        refs[-1][i * rows : (i + 1) * rows] = ref[...]


def join(values):
    rows, lanes = values[0].shape
    return pl.pallas_call(
        join_kernel,
        out_shape=jax.ShapeDtypeStruct((len(values) * rows, lanes), values[0].dtype),
        in_specs=[VMEM] * len(values),
        out_specs=VMEM,
        name="join",
    )(*values)


def projection_kernel(slabs, divisor, inverse_ref, same_ref, other_ref, out_ref, cross_ref):
    me = lax.axis_index("space")
    rows = cross_ref.shape[0] // slabs
    for away in range(slabs):
        at = pl.ds(pl.multiple_of((me ^ away) * rows, rows), rows)
        chip = slice(away // CORES * rows, (away // CORES + 1) * rows)
        cross_ref[at, :] = (other_ref if away % CORES else same_ref)[chip]
    out_ref[...] = (
        lax.dot(
            inverse_ref[...],
            cross_ref[...],
            precision=HIGHEST,
            preferred_element_type=jnp.float32,
        )
        / divisor
    )


def project(inverse, same, other, slabs, divisor):
    return pl.pallas_call(
        lambda *refs: projection_kernel(slabs, divisor, *refs),
        out_shape=jax.ShapeDtypeStruct(inverse.shape, jnp.float32),
        in_specs=[VMEM] * 3,
        out_specs=VMEM,
        scratch_shapes=[pltpu.VMEM(inverse.shape, jnp.float32)],
        compiler_params=pltpu.CompilerParams(vmem_limit_bytes=VMEM_BYTES),
        name="project",
    )(inverse, same, other)


def swap(value, axis, mask):
    return lax.ppermute(value, axis, [(i, i ^ mask) for i in range(lax.axis_size(axis))])


def body(owned_x, owned_y, patch_dest):
    slabs = lax.axis_size("space")
    shares = lax.axis_size("snap")
    slots, patch, width = owned_x.shape
    per_slab = slots // 2
    rows_total = slabs * per_slab * patch
    full = shares * width
    tiles = full // TILE
    pairs = tiles * (tiles + 1) // 2
    half = shares // 2
    shares_of = (tuple(range(half, shares)), tuple(range(half)))

    def packed(owned, groups, with_ids, after):
        cells = owned.reshape(slots, shares, patch // shares, width)
        return pack(patch_dest, cells, slabs, per_slab, groups, with_ids, after)

    def merged(sent, after):
        return merge(sent[0], swap(sent[1], "space", 1), slabs // CORES, after)

    def to_chips(joined):
        return [joined[0]] + [swap(joined[m], "space", CORES * m) for m in range(1, len(joined))]

    def to_pieces(value, axis="space"):
        return lax.all_to_all(value, axis, split_axis=0, concat_axis=0, tiled=True)

    def place_far(meta, moved, after):
        pieces, meta = settle(
            meta, moved, slots // slabs, per_slab, shares, shares_of[0], after
        )
        return pieces[0], to_pieces(pieces[0], "snap"), meta

    def place_near(meta, moved, after):
        pieces, _ = settle(meta, moved, slots // slabs, per_slab, shares, (), after)
        return [
            swap(piece, "snap", share) if share else piece
            for share, piece in zip(shares_of[1], pieces)
        ]

    def hops():
        hop = 1
        while hop < shares:
            yield hop
            hop *= 2

    chips = slabs // CORES
    sent_x = packed(owned_x, shares_of, True, [])
    ((same_y, other_y),) = packed(owned_y, (shares_of[0] + shares_of[1],), False, [])
    other_y = swap(other_y, "space", 1)
    joined_near = merged(sent_x[1], [])
    far = to_chips(merged(sent_x[0], []))
    settled, x_far, meta = place_far(None, far, [other_y, joined_near[0]])
    near = to_chips(joined_near)
    y_far = to_chips(merge(same_y, other_y, chips, near[1:3], slice(0, half), shares))
    y_near = to_chips(merge(same_y, other_y, chips, y_far[1:3], slice(half, shares), shares))
    x_cells = place_near(meta, near, []) + [x_far]

    gram_local = gram_blocks(x_cells, y_far[1:3])
    gram = to_pieces(gram_local.reshape(pairs * TILE, TILE))
    gram = sum_pieces(gram, slabs, [])
    settled, y_cells, _ = place_far(meta, y_far, [gram])
    for hop in hops():
        gram = add(gram, swap(gram, "snap", hop), [settled] if hop == 1 else y_near[1:3])
    y_cells = place_near(meta, y_near, [gram]) + [y_cells]
    gram = lax.all_gather(gram, "space", axis=0, tiled=True)

    steps = factor_steps(gram.reshape(pairs, TILE, TILE), tiles, rows_total, y_cells[:1])
    state = next(steps)
    for _ in range(tiles - 2):
        state = steps.send([])
    cross_local = cross_sum(x_cells, y_cells, [state])
    cross = to_pieces(cross_local)
    r_factor, inverse, *terms = steps.send([cross_local])

    q_basis = basis(x_cells, terms, 0, 2, None, [])
    cross = sum_pieces(cross, slabs, [q_basis])
    q_basis = basis(x_cells, terms, 1, 2, q_basis, [cross])
    for hop in hops():
        cross = add(cross, swap(cross, "snap", hop), [q_basis] if hop == 1 else [])
    same = join([cross] + [swap(cross, "space", m) for m in range(CORES, slabs, CORES)])
    projection = project(inverse, same, swap(same, "space", 1), slabs, math.sqrt(rows_total))
    return q_basis, r_factor, projection


def solution(mesh):
    in_specs = (P("space", None, "snap"), P("space", None, "snap"), P("space"))
    out_specs = (P("space", "snap", None), P(), P())
    return jax.shard_map(body, mesh=mesh, in_specs=in_specs, out_specs=out_specs, check_vma=False)
```

time: 288 us -> 306 us (1.062)
  local copies, waits for them, and re-layouts: 12.5 us -> 46.1 us
  waiting for transfers between devices: 110 us -> 130 us
  starting transfers between devices: 69.1 us -> 52.5 us
  between operations: 14.4 us -> 0.98 us
  matrix products: 4.04 us -> 0 us
    ppermute x32 -> x25, waiting for transfers between devices: 82 us -> 119 us  [swap(): lax.ppermute(value, axis, [(i, i ^ mask) for i in range(lax.axis_size(axi...]
    unnamed x72 -> x116, local copies, waits for them, and re-layouts: 12.5 us -> 46.1 us
    ppermute x32 -> x25, starting transfers between devices: 60.6 us -> 34.4 us  [swap(): lax.ppermute(value, axis, [(i, i ^ mask) for i in range(lax.axis_size(axi...]
    all_gather x1 -> x0, waiting for transfers between devices: 23.6 us -> none  [body(): cross = lax.all_gather(cross, 'space', axis=0, tiled=True)]
    all_to_all x2 -> x4, starting transfers between devices: 8.46 us -> 18.1 us  [to_pieces(): return lax.all_to_all(value, axis, split_axis=0, concat_axis=0, tiled=True)]
    all_to_all x2 -> x4, waiting for transfers between devices: 3.98 us -> 10.4 us  [to_pieces(): return lax.all_to_all(value, axis, split_axis=0, concat_axis=0, tiled=True)]
    dot_general x1 -> x0, matrix products: 4.04 us -> none  [body(): jnp.dot(inverse, cross, precision=HIGHEST) / math.sqrt(rows_total)]
    pallas_call x14 -> x16, Pallas kernels: 33.3 us -> 32.5 us  [the longest x4 10.4 us: settle(): pl.pallas_call(lambda *refs: settle_kernel(chips, capacity, with_ids, far...]
  transfers between devices with their start and end apart: 35 -> 29, of which waited for: 15 -> 17; matrix products, arithmetic and copies ran while one was open for 0% -> 0% of each run, Pallas kernels for 18% -> 13%
where the time goes in v9:
time: 306 us; the launch traced here: 304 us
  waiting for transfers between devices  130 us (42%)
  Pallas kernels  65.6 us (21%)
  starting transfers between devices  52.5 us (17%)
  local copies, waits for them, and re-layouts  46.1 us (15%)
  blocking collectives  9.36 us (3%)
    ppermute x25, waiting for transfers between devices, swap(): lax.ppermute(value, axis, [(i, i ^ mask) for i in range(lax.axis_size(axi...  119 us
    unnamed x116, local copies, waits for them, and re-layouts  46.1 us
    ppermute x25, starting transfers between devices, swap(): lax.ppermute(value, axis, [(i, i ^ mask) for i in range(lax.axis_size(axi...  34.4 us
    pallas_call x4, Pallas kernels, factor_call(): pl.pallas_call(lambda *refs: kernel(*refs[len(after):]), out_shape=out_sh...  19.7 us
    all_to_all x4, starting transfers between devices, to_pieces(): return lax.all_to_all(value, axis, split_axis=0, concat_axis=0, tiled=True)  18.1 us
    all_to_all x4, waiting for transfers between devices, to_pieces(): return lax.all_to_all(value, axis, split_axis=0, concat_axis=0, tiled=True)  10.4 us
    pallas_call x4, Pallas kernels, settle(): pl.pallas_call(lambda *refs: settle_kernel(chips, capacity, with_ids, far...  10.4 us
    all_gather x1, blocking collectives, body(): gram = lax.all_gather(gram, 'space', axis=0, tiled=True)  9.36 us
  transfers between devices with their start and end apart: 29, of which 17 were waited for; matrix products, arithmetic and copies ran while one was open for 0% of the time, Pallas kernels for 13%

profile of v9, /device:TPU:0, one launch (start us, length us, event | category | flops | bytes accessed | tf_op | source)
XLA Modules:
  0.0 304.2 jit_solution(1968198232569752885)
XLA Ops:
  0.6 2.2 copy-done.18
  3.5 2.5 pack.2
  6.0 1.3 copy-done.7
  7.3 1.8 collective-permute-start
  9.1 2.5 pack.3
  11.6 1.5 collective-permute-start.2
  13.1 2.3 collective-permute-done.2.refs_1_
  15.5 2.7 collective-permute-start.3
  19.3 1.4 collective-permute-start.5
  20.9 10.4 %collective-permute-done.3.refs_3_ = bf16[66,32,128]{2,1,0:T(8,128)(2,1)S(1)} collective-permute-done((bf16[66,32,128]{2,1,0:T(8,128)(2,1)S(1)}, bf16[66,32,128]{2,1,0:T(8,128)(2,1)S(1)}, u32[]{:S(2)}, u32[]{:S(2)}) %collective-permute-start.3) | collective-permute-done | bytes 540704 | tf_op jit(solution)/shard_map/ppermute | solution.py:567
  31.3 11.7 %collective-permute-done.4.refs_4_ = bf16[66,32,128]{2,1,0:T(8,128)(2,1)S(1)} collective-permute-done((bf16[66,32,128]{2,1,0:T(8,128)(2,1)S(1)}, bf16[66,32,128]{2,1,0:T(8,128)(2,1)S(1)}, u32[]{:S(2)}, u32[]{:S(2)}) %collective-permute-start.4) | collective-permute-done | bytes 540704 | tf_op jit(solution)/shard_map/ppermute | solution.py:567
  43.0 1.8 collective-permute-done.5.refs_5_
  44.8 2.8 settle.4
  49.0 5.0 %all-to-all-start = ((bf16[4,64,32,128]{3,2,1,0:T(8,128)(2,1)}), bf16[4,64,32,128]{3,2,1,0:T(8,128)(2,1)S(1)}, u32[]{:S(2)}, u32[]{:S(2)}) async-start(bf16[4,64,32,128]{3,2,1,0:T(8,128)(2,1)} %copy-done.29), calls=%async_computation | async-start | bytes 4194304 | tf_op jit(solution)/shard_map/all_to_all | solution.py:593
  54.6 1.7 collective-permute-start.7
  57.5 11.6 %collective-permute-done.6.refs_2_.refs_0_ = bf16[64,32,128]{2,1,0:T(8,128)(2,1)S(1)} collective-permute-done((bf16[64,32,128]{2,1,0:T(8,128)(2,1)}, bf16[64,32,128]{2,1,0:T(8,128)(2,1)S(1)}, u32[]{:S(2)}, u32[]{:S(2)}) %collective-permute-start.6) | collective-permute-done | bytes 524320 | tf_op jit(solution)/shard_map/ppermute | solution.py:567
  69.1 9.8 %collective-permute-done.7.refs_3_.refs_1_ = bf16[64,32,128]{2,1,0:T(8,128)(2,1)S(1)} collective-permute-done((bf16[64,32,128]{2,1,0:T(8,128)(2,1)}, bf16[64,32,128]{2,1,0:T(8,128)(2,1)S(1)}, u32[]{:S(2)}, u32[]{:S(2)}) %collective-permute-start.7) | collective-permute-done | bytes 524320 | tf_op jit(solution)/shard_map/ppermute | solution.py:567
  78.9 2.1 settle.5
  80.9 1.8 collective-permute-start.9
  82.7 1.6 copy-done.8
  86.1 1.4 collective-permute-start.11
  88.2 15.1 %collective-permute-done.9.refs_3_.refs_2_.refs_1_ = bf16[64,32,128]{2,1,0:T(8,128)(2,1)S(1)} collective-permute-done((bf16[64,32,128]{2,1,0:T(8,128)(2,1)S(1)}, bf16[64,32,128]{2,1,0:T(8,128)(2,1)S(1)}, u32[]{:S(2)}, u32[]{:S(2)}) %collective-permute-start.9) | collective-permute-done | bytes 524320 | tf_op jit(solution)/shard_map/ppermute | solution.py:567
  107.1 2.3 gram_blocks.1
  110.2 4.2 %all-to-all-start.1 = ((f32[8,160,128]{2,1,0:T(8,128)}), f32[8,160,128]{2,1,0:T(8,128)}, u32[]{:S(2)}, u32[]{:S(2)}) async-start(f32[8,160,128]{2,1,0:T(8,128)} %bitcast.23), calls=%async_computation.1 | async-start | bytes 1310720 | tf_op jit(solution)/shard_map/all_to_all | solution.py:593
  114.4 2.8 collective-permute-start.14
  117.2 8.8 %all-to-all-done.1 = f32[8,160,128]{2,1,0:T(8,128)} async-done(((f32[8,160,128]{2,1,0:T(8,128)}), f32[8,160,128]{2,1,0:T(8,128)}, u32[]{:S(2)}, u32[]{:S(2)}) %all-to-all-start.1) | async-done | bytes 655392 | tf_op jit(solution)/shard_map/all_to_all | solution.py:593
  126.0 1.7 sum_pieces.2.refs_0_.refs_1_
  127.7 9.0 %collective-permute-done.14.refs_5_ = bf16[64,32,128]{2,1,0:T(8,128)(2,1)} collective-permute-done((bf16[64,32,128]{2,1,0:T(8,128)(2,1)}, bf16[64,32,128]{2,1,0:T(8,128)(2,1)}, u32[]{:S(2)}, u32[]{:S(2)}) %collective-permute-start.14) | collective-permute-done | bytes 524320 | tf_op jit(solution)/shard_map/ppermute | solution.py:567
  140.8 2.6 settle.6.refs_0_
  144.7 4.7 %all-to-all-start.2 = ((bf16[4,64,32,128]{3,2,1,0:T(8,128)(2,1)}), bf16[4,64,32,128]{3,2,1,0:T(8,128)(2,1)}, u32[]{:S(2)}, u32[]{:S(2)}) async-start(bf16[4,64,32,128]{3,2,1,0:T(8,128)(2,1)} %copy-done.6), calls=%async_computation.2 | async-start | bytes 4194304 | tf_op jit(solution)/shard_map/all_to_all | solution.py:593
  149.4 1.6 copy-done.5
  151.0 1.6 copy-done.9
  157.7 2.6 collective-permute-start.17
  160.2 2.0 collective-permute-start.15
  162.2 22.6 %collective-permute-done.15.refs_2_ = f32[160,128]{1,0:T(8,128)S(1)} collective-permute-done((f32[160,128]{1,0:T(8,128)S(1)}, f32[160,128]{1,0:T(8,128)S(1)}, u32[]{:S(2)}, u32[]{:S(2)}) %collective-permute-start.15) | collective-permute-done | bytes 81952 | tf_op jit(solution)/shard_map/ppermute | solution.py:567
  185.5 1.6 add.4.refs_2_
  187.1 4.6 %collective-permute-start.16 = (f32[160,128]{1,0:T(8,128)}, f32[160,128]{1,0:T(8,128)S(1)}, u32[]{:S(2)}, u32[]{:S(2)}) collective-permute-start(f32[160,128]{1,0:T(8,128)} %add.4.refs_2_), channel_id=1, source_target_pairs={{0,2},{1,3},{2,0},{3,1},{4,6},{5,7},{6,4},{7,5},{8,10},{9,11},{10,... | collective-permute-start | bytes 245768 | tf_op jit(solution)/shard_map/ppermute | solution.py:567
  191.7 9.2 %collective-permute-done.16.refs_3_ = f32[160,128]{1,0:T(8,128)S(1)} collective-permute-done((f32[160,128]{1,0:T(8,128)}, f32[160,128]{1,0:T(8,128)S(1)}, u32[]{:S(2)}, u32[]{:S(2)}) %collective-permute-start.16) | collective-permute-done | bytes 81952 | tf_op jit(solution)/shard_map/ppermute | solution.py:567
  201.6 1.6 add.5.refs_0_
  205.1 2.9 settle.7
  208.0 9.4 %all_gather.3 = f32[1280,128]{1,0:T(8,128)S(1)} all-gather(f32[160,128]{1,0:T(8,128)S(1)} %copy-done.36), channel_id=1, replica_groups=mesh['space'=8,'snap'=4] {'space'}, dimensions={0}, use_global_device_ids=true | all-gather | bytes 737280 | tf_op jit(solution)/shard_map/all_gather | solution.py:633
  217.4 4.9 %factor.4.refs_0_ = f32[4,8,128,128]{3,2,1,0:T(8,128)S(1)} custom-call(bf16[64,32,128]{2,1,0:T(8,128)(2,1)S(1)} %get-tuple-element.62.refs_0_.refs_4_, f32[10,128,128]{2,1,0:T(8,128)S(1)} %bitcast.24), custom_call_target="tpu_custom_call" | custom-call | flops 1 | bytes 1 | tf_op jit(solution)/shard_map/factor/pallas_call | solution.py:417
  222.3 4.8 %factor.5.refs_0_ = f32[4,8,128,128]{3,2,1,0:T(8,128)S(1)} custom-call(f32[4,8,128,128]{3,2,1,0:T(8,128)S(1)} %factor.4.refs_0_), custom_call_target="tpu_custom_call", output_to_operand_aliasing={{}: (0, {})} | custom-call | flops 1 | bytes 1 | tf_op jit(solution)/shard_map/factor/pallas_call | solution.py:417
  227.1 4.6 %factor.6.refs_0_.refs_1_ = f32[4,8,128,128]{3,2,1,0:T(8,128)S(1)} custom-call(f32[4,8,128,128]{3,2,1,0:T(8,128)S(1)} %factor.5.refs_0_), custom_call_target="tpu_custom_call", output_to_operand_aliasing={{}: (0, {})} | custom-call | flops 1 | bytes 1 | tf_op jit(solution)/shard_map/factor/pallas_call | solution.py:417
  231.7 1.3 copy-done
  233.9 1.6 copy-done.1
  237.5 4.8 %cross_sum.1.refs_0_ = f32[512,512]{1,0:T(8,128)} custom-call(f32[4,8,128,128]{3,2,1,0:T(8,128)S(1)} %copy-done.1, bf16[64,32,128]{2,1,0:T(8,128)(2,1)S(1)} %get-tuple-element.50.refs_2_.refs_1_.refs_0_, bf16[64,32,128]{2,1,0:T(8,128)(2,1)S(1)} %collective-permute-done.9.refs_3_.refs_2_.refs_1_, ...), custom_call_target="tpu_custom_call" | custom-call | flops 1 | bytes 1 | tf_op jit(solution)/shard_map/cross_sum/pallas_call | solution.py:281
  242.4 4.3 %all-to-all-start.3 = ((f32[8,64,512]{2,1,0:T(8,128)}), f32[8,64,512]{2,1,0:T(8,128)}, u32[]{:S(2)}, u32[]{:S(2)}) async-start(f32[8,64,512]{2,1,0:T(8,128)} %bitcast.15), calls=%async_computation.3 | async-start | bytes 2097152 | tf_op jit(solution)/shard_map/all_to_all | solution.py:593
  246.6 1.6 copy-done.2
  248.2 5.4 %factor.7 = (f32[512,512]{1,0:T(8,128)}, f32[512,512]{1,0:T(8,128)S(1)}, bf16[512,512]{1,0:T(8,128)(2,1)S(1)}, bf16[512,512]{1,0:T(8,128)(2,1)S(1)}, bf16[512,512]{1,0:T(8,128)(2,1)S(1)}) custom-call(f32[512,512]{1,0:T(8,128)} %cross_sum.1.refs_0_, f32[4,8,128,128]{3,2,1,0:T(8,128)S(1)} %copy-done.2), custom_call_target="tpu_custom_call" | custom-call | flops 1 | bytes 1 | tf_op jit(solution)/shard_map/factor/pallas_call | solution.py:417
  254.6 3.5 %basis.2.refs_0_ = f32[64,32,512]{2,1,0:T(8,128)} custom-call(bf16[64,32,128]{2,1,0:T(8,128)(2,1)S(1)} %get-tuple-element.50.refs_2_.refs_1_.refs_0_, bf16[64,32,128]{2,1,0:T(8,128)(2,1)S(1)} %collective-permute-done.9.refs_3_.refs_2_.refs_1_, bf16[4,64,32,128]{3,2,1,0:T(8,128)(2,1)S(1)} %all-to-all-done.refs_4_.refs_3_.refs_2_, ...), custom_call_target="tpu_custom_call" | custom-call | flops 1 | bytes 1 | tf_op jit(solution)/shard_map/basis/pallas_call | solution.py:470
  260.5 1.6 all-to-all-done.3
  262.0 1.9 sum_pieces.3.refs_1_
  264.0 2.0 collective-permute-start.19
  270.0 3.5 %basis.3.refs_0_ = f32[64,32,512]{2,1,0:T(8,128)} custom-call(f32[64,32,512]{2,1,0:T(8,128)} %basis.2.refs_0_, f32[64,512]{1,0:T(8,128)S(1)} %copy-done.33, bf16[64,32,128]{2,1,0:T(8,128)(2,1)S(1)} %get-tuple-element.50.refs_2_.refs_1_.refs_0_, ...), custom_call_target="tpu_custom_call", output_to_operand_aliasing={{}: (0, {})} | custom-call | flops 1 | bytes 1 | tf_op jit(solution)/shard_map/basis/pallas_call | solution.py:470
  274.1 1.6 add.6.refs_0_
  275.8 7.6 %collective-permute-done.20.refs_1_ = f32[64,512]{1,0:T(8,128)S(1)} collective-permute-done((f32[64,512]{1,0:T(8,128)}, f32[64,512]{1,0:T(8,128)S(1)}, u32[]{:S(2)}, u32[]{:S(2)}) %collective-permute-start.20) | collective-permute-done | bytes 131104 | tf_op jit(solution)/shard_map/ppermute | solution.py:567
  284.0 1.6 add.7.refs_0_
  285.6 2.6 collective-permute-start.23
  289.1 3.4 %collective-permute-done.23.refs_3_ = f32[64,512]{1,0:T(8,128)S(1)} collective-permute-done((f32[64,512]{1,0:T(8,128)}, f32[64,512]{1,0:T(8,128)S(1)}, u32[]{:S(2)}, u32[]{:S(2)}) %collective-permute-start.23) | collective-permute-done | bytes 131104 | tf_op jit(solution)/shard_map/ppermute | solution.py:567
  292.5 2.5 collective-permute-done.22.refs_2_
  296.2 1.9 join.1.refs_1_
  298.2 2.1 collective-permute-done.24.refs_2_
  301.3 2.9 project.1
  (137 shorter events, 40.7 us)
Async XLA Ops:
  0.6 2.2 copy-start.18
  3.5 5.6 %copy-start.19 = (bf16[128,128,128]{2,1,0:T(8,128)(2,1)S(1)}, bf16[128,128,128]{2,1,0:T(8,128)(2,1)}, u32[]{:S(2)}) copy-start(bf16[128,128,128]{2,1,0:T(8,128)(2,1)} %param.3) | copy-start | bytes 12582916
  5.9 1.3 copy-start.7
  7.3 37.5 %collective-permute-start = (bf16[256,32,128]{2,1,0:T(8,128)(2,1)S(1)}, bf16[256,32,128]{2,1,0:T(8,128)(2,1)S(1)}, u32[]{:S(2)}, u32[]{:S(2)}) collective-permute-start(bf16[256,32,128]{2,1,0:T(8,128)(2,1)S(1)} %get-tuple-element.36), channel_id=1, source_target_pairs={{0,4},{4,0},{8,12},{12,8},{16,20},{20,16},{24,28},{28,24},{1,5},{5... | collective-permute-start | bytes 6291464 | tf_op jit(solution)/shard_map/ppermute | solution.py:567
  11.6 3.8 %collective-permute-start.2 = (bf16[132,32,128]{2,1,0:T(8,128)(2,1)S(1)}, bf16[132,32,128]{2,1,0:T(8,128)(2,1)S(1)}, u32[]{:S(2)}, u32[]{:S(2)}) collective-permute-start(bf16[132,32,128]{2,1,0:T(8,128)(2,1)S(1)} %get-tuple-element.41), channel_id=1, source_target_pairs={{0,4},{4,0},{8,12},{12,8},{16,20},{20,16},{24,28},{28,24},{1,5},{5... | collective-permute-start | bytes 3244040 | tf_op jit(solution)/shard_map/ppermute | solution.py:567
  13.1 7.6 %collective-permute-start.1 = (bf16[128,32,128]{2,1,0:T(8,128)(2,1)S(1)}, bf16[128,32,128]{2,1,0:T(8,128)(2,1)S(1)}, u32[]{:S(2)}, u32[]{:S(2)}) collective-permute-start(bf16[128,32,128]{2,1,0:T(8,128)(2,1)S(1)} %get-tuple-element.38), channel_id=1, source_target_pairs={{0,4},{4,0},{8,12},{12,8},{16,20},{20,16},{24,28},{28,24},{1,5},{5... | collective-permute-start | bytes 3145736 | tf_op jit(solution)/shard_map/ppermute | solution.py:567
  15.5 15.7 %collective-permute-start.3 = (bf16[66,32,128]{2,1,0:T(8,128)(2,1)S(1)}, bf16[66,32,128]{2,1,0:T(8,128)(2,1)S(1)}, u32[]{:S(2)}, u32[]{:S(2)}) collective-permute-start(bf16[66,32,128]{2,1,0:T(8,128)(2,1)S(1)} %get-tuple-element.43), channel_id=1, source_target_pairs={{0,8},{4,12},{8,0},{12,4},{16,24},{20,28},{24,16},{28,20},{1,9},{5... | collective-permute-start | bytes 1622024 | tf_op jit(solution)/shard_map/ppermute | solution.py:567
  18.2 24.7 %collective-permute-start.4 = (bf16[66,32,128]{2,1,0:T(8,128)(2,1)S(1)}, bf16[66,32,128]{2,1,0:T(8,128)(2,1)S(1)}, u32[]{:S(2)}, u32[]{:S(2)}) collective-permute-start(bf16[66,32,128]{2,1,0:T(8,128)(2,1)S(1)} %get-tuple-element.44), channel_id=1, source_target_pairs={{0,16},{4,20},{8,24},{12,28},{16,0},{20,4},{24,8},{28,12},{1,17},{... | collective-permute-start | bytes 1622024 | tf_op jit(solution)/shard_map/ppermute | solution.py:567
  19.3 25.5 %collective-permute-start.5 = (bf16[66,32,128]{2,1,0:T(8,128)(2,1)S(1)}, bf16[66,32,128]{2,1,0:T(8,128)(2,1)S(1)}, u32[]{:S(2)}, u32[]{:S(2)}) collective-permute-start(bf16[66,32,128]{2,1,0:T(8,128)(2,1)S(1)} %get-tuple-element.45), channel_id=1, source_target_pairs={{0,24},{4,28},{8,16},{12,20},{16,8},{20,12},{24,0},{28,4},{1,25},{... | collective-permute-start | bytes 1622024 | tf_op jit(solution)/shard_map/ppermute | solution.py:567
  20.8 26.8 %copy-start.30 = (bf16[64,32,128]{2,1,0:T(8,128)(2,1)}, bf16[64,32,128]{2,1,0:T(8,128)(2,1)S(1)}, u32[]{:S(2)}) copy-start(bf16[64,32,128]{2,1,0:T(8,128)(2,1)S(1)} %get-tuple-element.39.refs_1_) | copy-start | bytes 1572868
  20.9 26.8 %copy-start.46 = (bf16[64,32,128]{2,1,0:T(8,128)(2,1)}, bf16[64,32,128]{2,1,0:T(8,128)(2,1)S(1)}, u32[]{:S(2)}) copy-start(bf16[64,32,128]{2,1,0:T(8,128)(2,1)S(1)} %get-tuple-element.49) | copy-start | bytes 1572868
  20.9 26.8 %copy-start.48 = (bf16[64,32,128]{2,1,0:T(8,128)(2,1)}, bf16[64,32,128]{2,1,0:T(8,128)(2,1)S(1)}, u32[]{:S(2)}) copy-start(bf16[64,32,128]{2,1,0:T(8,128)(2,1)S(1)} %get-tuple-element.48) | copy-start | bytes 1572868
  20.9 26.8 %copy-start.49 = (bf16[64,32,128]{2,1,0:T(8,128)(2,1)}, bf16[64,32,128]{2,1,0:T(8,128)(2,1)S(1)}, u32[]{:S(2)}) copy-start(bf16[64,32,128]{2,1,0:T(8,128)(2,1)S(1)} %get-tuple-element.47) | copy-start | bytes 1572868
  44.8 2.9 copy-start.3
  47.7 1.3 copy-start.29
  49.0 7.3 %copy-start.47 = (bf16[64,32,128]{2,1,0:T(8,128)(2,1)S(1)}, bf16[64,32,128]{2,1,0:T(8,128)(2,1)}, u32[]{:S(2)}) copy-start(bf16[64,32,128]{2,1,0:T(8,128)(2,1)} %copy-done.46) | copy-start | bytes 1572868
  49.0 29.9 %copy-start.31 = (bf16[64,32,128]{2,1,0:T(8,128)(2,1)S(1)}, bf16[64,32,128]{2,1,0:T(8,128)(2,1)}, u32[]{:S(2)}) copy-start(bf16[64,32,128]{2,1,0:T(8,128)(2,1)} %copy-done.30) | copy-start | bytes 1572868
  49.0 56.0 %all-to-all-start = ((bf16[4,64,32,128]{3,2,1,0:T(8,128)(2,1)}), bf16[4,64,32,128]{3,2,1,0:T(8,128)(2,1)S(1)}, u32[]{:S(2)}, u32[]{:S(2)}) async-start(bf16[4,64,32,128]{3,2,1,0:T(8,128)(2,1)} %copy-done.29), calls=%async_computation | async-start | bytes 4194304 | tf_op jit(solution)/shard_map/all_to_all | solution.py:593
  54.0 28.7 %copy-start.4 = (bf16[256,32,128]{2,1,0:T(8,128)(2,1)S(1)}, bf16[256,32,128]{2,1,0:T(8,128)(2,1)}, u32[]{:S(2)}) copy-start(bf16[256,32,128]{2,1,0:T(8,128)(2,1)} %copy-done.3) | copy-start | bytes 6291460
  54.0 15.1 %collective-permute-start.6 = (bf16[64,32,128]{2,1,0:T(8,128)(2,1)}, bf16[64,32,128]{2,1,0:T(8,128)(2,1)S(1)}, u32[]{:S(2)}, u32[]{:S(2)}) collective-permute-start(bf16[64,32,128]{2,1,0:T(8,128)(2,1)} %copy-done.49), channel_id=1, source_target_pairs={{0,8},{4,12},{8,0},{12,4},{16,24},{20,28},{24,16},{28,20},{1,9},{5... | collective-permute-start | bytes 1572872 | tf_op jit(solution)/shard_map/ppermute | solution.py:567
  54.6 24.3 %collective-permute-start.7 = (bf16[64,32,128]{2,1,0:T(8,128)(2,1)}, bf16[64,32,128]{2,1,0:T(8,128)(2,1)S(1)}, u32[]{:S(2)}, u32[]{:S(2)}) collective-permute-start(bf16[64,32,128]{2,1,0:T(8,128)(2,1)} %copy-done.48), channel_id=1, source_target_pairs={{0,16},{4,20},{8,24},{12,28},{16,0},{20,4},{24,8},{28,12},{1,17},{... | collective-permute-start | bytes 1572872 | tf_op jit(solution)/shard_map/ppermute | solution.py:567
  56.3 22.5 %collective-permute-start.8 = (bf16[64,32,128]{2,1,0:T(8,128)(2,1)S(1)}, bf16[64,32,128]{2,1,0:T(8,128)(2,1)S(1)}, u32[]{:S(2)}, u32[]{:S(2)}) collective-permute-start(bf16[64,32,128]{2,1,0:T(8,128)(2,1)S(1)} %copy-done.47), channel_id=1, source_target_pairs={{0,24},{4,28},{8,16},{12,20},{16,8},{20,12},{24,0},{28,4},{1,25},{... | collective-permute-start | bytes 1572872 | tf_op jit(solution)/shard_map/ppermute | solution.py:567
  80.9 22.4 %collective-permute-start.9 = (bf16[64,32,128]{2,1,0:T(8,128)(2,1)S(1)}, bf16[64,32,128]{2,1,0:T(8,128)(2,1)S(1)}, u32[]{:S(2)}, u32[]{:S(2)}) collective-permute-start(bf16[64,32,128]{2,1,0:T(8,128)(2,1)S(1)} %get-tuple-element.51), channel_id=1, source_target_pairs={{0,1},{1,0},{2,3},{3,2},{4,5},{5,4},{6,7},{7,6},{8,9},{9,8},{10,11... | collective-permute-start | bytes 1572872 | tf_op jit(solution)/shard_map/ppermute | solution.py:567
  82.7 1.6 copy-start.8
  86.1 17.2 %collective-permute-start.11 = (bf16[64,32,128]{2,1,0:T(8,128)(2,1)S(1)}, bf16[64,32,128]{2,1,0:T(8,128)(2,1)S(1)}, u32[]{:S(2)}, u32[]{:S(2)}) collective-permute-start(bf16[64,32,128]{2,1,0:T(8,128)(2,1)S(1)} %bitcast.29), channel_id=1, source_target_pairs={{0,16},{4,20},{8,24},{12,28},{16,0},{20,4},{24,8},{28,12},{1,17},{... | collective-permute-start | bytes 1572872 | tf_op jit(solution)/shard_map/ppermute | solution.py:567
  87.5 16.6 %collective-permute-start.10 = (bf16[64,32,128]{2,1,0:T(8,128)(2,1)S(1)}, bf16[64,32,128]{2,1,0:T(8,128)(2,1)S(1)}, u32[]{:S(2)}, u32[]{:S(2)}) collective-permute-start(bf16[64,32,128]{2,1,0:T(8,128)(2,1)S(1)} %bitcast.28), channel_id=1, source_target_pairs={{0,8},{4,12},{8,0},{12,4},{16,24},{20,28},{24,16},{28,20},{1,9},{5... | collective-permute-start | bytes 1572872 | tf_op jit(solution)/shard_map/ppermute | solution.py:567
  105.0 1.0 copy-start.11
  110.2 15.8 %all-to-all-start.1 = ((f32[8,160,128]{2,1,0:T(8,128)}), f32[8,160,128]{2,1,0:T(8,128)}, u32[]{:S(2)}, u32[]{:S(2)}) async-start(f32[8,160,128]{2,1,0:T(8,128)} %bitcast.23), calls=%async_computation.1 | async-start | bytes 1310720 | tf_op jit(solution)/shard_map/all_to_all | solution.py:593
  114.4 22.4 %collective-permute-start.14 = (bf16[64,32,128]{2,1,0:T(8,128)(2,1)}, bf16[64,32,128]{2,1,0:T(8,128)(2,1)}, u32[]{:S(2)}, u32[]{:S(2)}) collective-permute-start(bf16[64,32,128]{2,1,0:T(8,128)(2,1)} %bitcast.27), channel_id=1, source_target_pairs={{0,24},{4,28},{8,16},{12,20},{16,8},{20,12},{24,0},{28,4},{1,25},{... | collective-permute-start | bytes 1572872 | tf_op jit(solution)/shard_map/ppermute | solution.py:567
  136.8 1.0 copy-start.12
  137.8 1.0 copy-start.16
  139.7 1.0 copy-start.40
  143.4 1.3 copy-start.6
  144.7 89.1 %all-to-all-start.2 = ((bf16[4,64,32,128]{3,2,1,0:T(8,128)(2,1)}), bf16[4,64,32,128]{3,2,1,0:T(8,128)(2,1)}, u32[]{:S(2)}, u32[]{:S(2)}) async-start(bf16[4,64,32,128]{3,2,1,0:T(8,128)(2,1)} %copy-done.6), calls=%async_computation.2 | async-start | bytes 4194304 | tf_op jit(solution)/shard_map/all_to_all | solution.py:593
  149.4 1.6 copy-start.5
  151.0 1.6 copy-start.9
  152.6 1.0 copy-start.13
  153.6 1.0 copy-start.17
  154.7 5.5 %copy-start.38 = (f32[160,128]{1,0:T(8,128)S(1)}, f32[160,128]{1,0:T(8,128)}, u32[]{:S(2)}) copy-start(f32[160,128]{1,0:T(8,128)} %sum_pieces.2.refs_0_.refs_1_) | copy-start | bytes 245764
  156.7 35.0 %collective-permute-start.13 = (bf16[64,32,128]{2,1,0:T(8,128)(2,1)}, bf16[64,32,128]{2,1,0:T(8,128)(2,1)}, u32[]{:S(2)}, u32[]{:S(2)}) collective-permute-start(bf16[64,32,128]{2,1,0:T(8,128)(2,1)} %bitcast.7), channel_id=1, source_target_pairs={{0,16},{4,20},{8,24},{12,28},{16,0},{20,4},{24,8},{28,12},{1,17},{... | collective-permute-start | bytes 1572872 | tf_op jit(solution)/shard_map/ppermute | solution.py:567
  157.3 34.4 %collective-permute-start.12 = (bf16[64,32,128]{2,1,0:T(8,128)(2,1)}, bf16[64,32,128]{2,1,0:T(8,128)(2,1)}, u32[]{:S(2)}, u32[]{:S(2)}) collective-permute-start(bf16[64,32,128]{2,1,0:T(8,128)(2,1)} %bitcast.6), channel_id=1, source_target_pairs={{0,8},{4,12},{8,0},{12,4},{16,24},{20,28},{24,16},{28,20},{1,9},{5... | collective-permute-start | bytes 1572872 | tf_op jit(solution)/shard_map/ppermute | solution.py:567
  157.7 45.5 %collective-permute-start.17 = (bf16[64,32,128]{2,1,0:T(8,128)(2,1)}, bf16[64,32,128]{2,1,0:T(8,128)(2,1)}, u32[]{:S(2)}, u32[]{:S(2)}) collective-permute-start(bf16[64,32,128]{2,1,0:T(8,128)(2,1)} %bitcast.13), channel_id=1, source_target_pairs={{0,24},{4,28},{8,16},{12,20},{16,8},{20,12},{24,0},{28,4},{1,25},{... | collective-permute-start | bytes 1572872 | tf_op jit(solution)/shard_map/ppermute | solution.py:567
  160.2 24.7 %collective-permute-start.15 = (f32[160,128]{1,0:T(8,128)S(1)}, f32[160,128]{1,0:T(8,128)S(1)}, u32[]{:S(2)}, u32[]{:S(2)}) collective-permute-start(f32[160,128]{1,0:T(8,128)S(1)} %copy-done.38), channel_id=1, source_target_pairs={{0,1},{1,0},{2,3},{3,2},{4,5},{5,4},{6,7},{7,6},{8,9},{9,8},{10,11... | collective-permute-start | bytes 245768 | tf_op jit(solution)/shard_map/ppermute | solution.py:567
  187.1 13.8 %collective-permute-start.16 = (f32[160,128]{1,0:T(8,128)}, f32[160,128]{1,0:T(8,128)S(1)}, u32[]{:S(2)}, u32[]{:S(2)}) collective-permute-start(f32[160,128]{1,0:T(8,128)} %add.4.refs_2_), channel_id=1, source_target_pairs={{0,2},{1,3},{2,0},{3,1},{4,6},{5,7},{6,4},{7,5},{8,10},{9,11},{10,... | collective-permute-start | bytes 245768 | tf_op jit(solution)/shard_map/ppermute | solution.py:567
  204.0 1.0 copy-start.44
  207.9 19.2 %copy-start.21 = (bf16[64,32,128]{2,1,0:T(8,128)(2,1)}, bf16[64,32,128]{2,1,0:T(8,128)(2,1)S(1)}, u32[]{:S(2)}) copy-start(bf16[64,32,128]{2,1,0:T(8,128)(2,1)S(1)} %get-tuple-element.62.refs_0_.refs_4_) | copy-start | bytes 1572868
  207.9 25.1 %collective-permute-start.18 = (bf16[64,32,128]{2,1,0:T(8,128)(2,1)S(1)}, bf16[64,32,128]{2,1,0:T(8,128)(2,1)S(1)}, u32[]{:S(2)}, u32[]{:S(2)}) collective-permute-start(bf16[64,32,128]{2,1,0:T(8,128)(2,1)S(1)} %get-tuple-element.63), channel_id=1, source_target_pairs={{0,1},{1,0},{2,3},{3,2},{4,5},{5,4},{6,7},{7,6},{8,9},{9,8},{10,11... | collective-permute-start | bytes 1572872 | tf_op jit(solution)/shard_map/ppermute | solution.py:567
  231.7 1.3 copy-start
  233.9 1.6 copy-start.1
  235.4 1.0 copy-start.22
  236.5 1.0 copy-start.42
  242.4 19.7 %all-to-all-start.3 = ((f32[8,64,512]{2,1,0:T(8,128)}), f32[8,64,512]{2,1,0:T(8,128)}, u32[]{:S(2)}, u32[]{:S(2)}) async-start(f32[8,64,512]{2,1,0:T(8,128)} %bitcast.15), calls=%async_computation.3 | async-start | bytes 2097152 | tf_op jit(solution)/shard_map/all_to_all | solution.py:593
  246.6 1.6 copy-start.2
  264.0 9.5 %collective-permute-start.19 = (f32[64,512]{1,0:T(8,128)}, f32[64,512]{1,0:T(8,128)S(1)}, u32[]{:S(2)}, u32[]{:S(2)}) collective-permute-start(f32[64,512]{1,0:T(8,128)} %sum_pieces.3.refs_1_), channel_id=1, source_target_pairs={{0,1},{1,0},{2,3},{3,2},{4,5},{5,4},{6,7},{7,6},{8,9},{9,8},{10,11... | collective-permute-start | bytes 393224 | tf_op jit(solution)/shard_map/ppermute | solution.py:567
  266.0 1.0 copy-start.24
  268.0 1.0 copy-start.28
  273.5 26.8 %copy-start.35 = (f32[512,512]{1,0:T(8,128)S(1)}, f32[512,512]{1,0:T(8,128)}, u32[]{:S(2)}) copy-start(f32[512,512]{1,0:T(8,128)} %copy-done.34) | copy-start | bytes 3145732
  275.8 7.6 %collective-permute-start.20 = (f32[64,512]{1,0:T(8,128)}, f32[64,512]{1,0:T(8,128)S(1)}, u32[]{:S(2)}, u32[]{:S(2)}) collective-permute-start(f32[64,512]{1,0:T(8,128)} %add.6.refs_0_), channel_id=1, source_target_pairs={{0,2},{1,3},{2,0},{3,1},{4,6},{5,7},{6,4},{7,5},{8,10},{9,11},{10,... | collective-permute-start | bytes 393224 | tf_op jit(solution)/shard_map/ppermute | solution.py:567
  285.6 6.8 %collective-permute-start.23 = (f32[64,512]{1,0:T(8,128)}, f32[64,512]{1,0:T(8,128)S(1)}, u32[]{:S(2)}, u32[]{:S(2)}) collective-permute-start(f32[64,512]{1,0:T(8,128)} %add.7.refs_0_), channel_id=1, source_target_pairs={{0,24},{4,28},{8,16},{12,20},{16,8},{20,12},{24,0},{28,4},{1,25},{... | collective-permute-start | bytes 393224 | tf_op jit(solution)/shard_map/ppermute | solution.py:567
  288.2 6.7 %collective-permute-start.22 = (f32[64,512]{1,0:T(8,128)}, f32[64,512]{1,0:T(8,128)S(1)}, u32[]{:S(2)}, u32[]{:S(2)}) collective-permute-start(f32[64,512]{1,0:T(8,128)} %add.7.refs_0_), channel_id=1, source_target_pairs={{0,16},{4,20},{8,24},{12,28},{16,0},{20,4},{24,8},{28,12},{1,17},{... | collective-permute-start | bytes 393224 | tf_op jit(solution)/shard_map/ppermute | solution.py:567
  288.9 6.3 %collective-permute-start.21 = (f32[64,512]{1,0:T(8,128)}, f32[64,512]{1,0:T(8,128)S(1)}, u32[]{:S(2)}, u32[]{:S(2)}) collective-permute-start(f32[64,512]{1,0:T(8,128)} %add.7.refs_0_), channel_id=1, source_target_pairs={{0,8},{4,12},{8,0},{12,4},{16,24},{20,28},{24,16},{28,20},{1,9},{5... | collective-permute-start | bytes 393224 | tf_op jit(solution)/shard_map/ppermute | solution.py:567
  292.5 2.7 copy-start.53
  298.2 2.1 collective-permute-start.24
  300.3 1.0 copy-start.32
  (23 other events, 18.4 us)

commit v10 on v9

--- a/solution.py
+++ b/solution.py
@@ -125,7 +125,7 @@
     return [out.reshape(-1, rows, width) for out in outs]
 
 
-def settle_kernel(chips, capacity, with_ids, far, *refs):
+def settle_kernel(chips, capacity, with_ids, far, cuts, *refs):
     if with_ids:
         moved_refs, out_refs, meta_ref, ids_ref = refs[:chips], refs[chips:-2], refs[-2], refs[-1]
         span = moved_refs[0].shape[0] // CORES
@@ -138,7 +138,7 @@
         meta_ref, moved_refs, out_refs = refs[0], refs[1 : 1 + chips], refs[1 + chips :]
         span = moved_refs[0].shape[0] // CORES
     mine = lax.axis_index("snap")
-    count = len(far) or len(out_refs)
+    count = len(far) or len(out_refs) // cuts
     for source in range(chips * CORES):
         moved_ref = moved_refs[source // CORES]
 
@@ -148,28 +148,32 @@
             @pl.when(block >= 0)
             def _():
                 at = source % CORES * span + rank * count
-                for k in range(count):
-                    if far:
+                if far:
+                    for k in range(count):
                         out_refs[0][mine ^ far[k], block] = moved_ref[at + k]
-                    else:
-                        out_refs[k][block] = moved_ref[at + k]
+                else:
+                    for k, out_ref in enumerate(out_refs):
+                        rows = out_ref.shape[1]
+                        cells = slice(k % cuts * rows, (k % cuts + 1) * rows)
+                        out_ref[block] = moved_ref[at + k // cuts, cells]
 
             return 0
 
         lax.fori_loop(0, capacity, place, 0, unroll=4)
 
 
-def settle(meta, moved, capacity, per_slab, shares, far, after):
+def settle(meta, moved, capacity, per_slab, shares, far, cuts, after):
     with_ids = meta is None
     chips = len(moved)
     rows, width = moved[0].shape[1:]
     if far:
         pieces = (jax.ShapeDtypeStruct((shares, per_slab, rows, width), moved[0].dtype),)
     else:
-        pieces = (jax.ShapeDtypeStruct((per_slab, rows, width), moved[0].dtype),) * (shares // 2)
+        piece = jax.ShapeDtypeStruct((per_slab, rows // cuts, width), moved[0].dtype)
+        pieces = (piece,) * (shares // 2 * cuts)
     ids = jax.ShapeDtypeStruct((chips * CORES, TILE), jnp.int32)
     outs = pl.pallas_call(
-        lambda *refs: settle_kernel(chips, capacity, with_ids, far, *refs[len(after) :]),
+        lambda *refs: settle_kernel(chips, capacity, with_ids, far, cuts, *refs[len(after) :]),
         out_shape=pieces + ((ids,) if with_ids else ()),
         in_specs=[ANY] * len(after) + ([] if with_ids else [SMEM]) + [VMEM] * chips,
         out_specs=(VMEM,) * len(pieces) + ((SMEM,) if with_ids else ()),
@@ -254,10 +258,16 @@
     def _():
         acc_ref[...] = jnp.zeros_like(acc_ref)
 
-    count = len(refs) // 2 - 1
+    count = shares // 2 + 1
+    rows = refs[0].shape[1]
+    y_refs, y_shares = refs[count:-2], []
+    while y_refs:
+        cuts = rows // y_refs[0].shape[1]
+        y_shares.append(jnp.concatenate([ref[...] for ref in y_refs[:cuts]], axis=1))
+        y_refs = y_refs[cuts:]
     acc_ref[...] += lax.dot_general(
         whole_rows(by_distance(refs[:count])),
-        whole_rows(by_distance(refs[count : 2 * count])),
+        whole_rows(y_shares),
         ROWS_BY_ROWS,
         preferred_element_type=jnp.float32,
     )
@@ -278,11 +288,13 @@
     shares, blocks, rows, width = x_cells[-1].shape
     full = shares * width
     specs = cell_specs(shares, blocks // steps, rows, width, 0)
+    for piece in y_cells:
+        specs.append(pl.BlockSpec((blocks // steps, piece.shape[1], width), lambda i: (i, 0, 0)))
     return pl.pallas_call(
         lambda *refs: cross_kernel(shares, *refs[len(after) :]),
         grid=(steps,),
         out_shape=jax.ShapeDtypeStruct((full, full), jnp.float32),
-        in_specs=[ANY] * len(after) + specs * 2,
+        in_specs=[ANY] * len(after) + specs,
         out_specs=pl.BlockSpec((full, full), lambda i: (0, 0)),
         scratch_shapes=[pltpu.VMEM((full, full), jnp.float32)],
         compiler_params=pltpu.CompilerParams(vmem_limit_bytes=VMEM_BYTES),
@@ -522,15 +534,16 @@
         refs[-1][i * rows : (i + 1) * rows] = ref[...]
 
 
-def join(values):
+def join(values, after):
     rows, lanes = values[0].shape
     return pl.pallas_call(
-        join_kernel,
+        lambda *refs: join_kernel(*refs[len(after) :]),
         out_shape=jax.ShapeDtypeStruct((len(values) * rows, lanes), values[0].dtype),
-        in_specs=[VMEM] * len(values),
+        in_specs=[ANY] * len(after) + [VMEM] * len(values),
         out_specs=VMEM,
+        cost_estimate=LIGHT,
         name="join",
-    )(*values)
+    )(*after, *values)
 
 
 def projection_kernel(slabs, divisor, inverse_ref, same_ref, other_ref, out_ref, cross_ref):
@@ -594,15 +607,15 @@
 
     def place_far(meta, moved, after):
         pieces, meta = settle(
-            meta, moved, slots // slabs, per_slab, shares, shares_of[0], after
+            meta, moved, slots // slabs, per_slab, shares, shares_of[0], 1, after
         )
-        return pieces[0], to_pieces(pieces[0], "snap"), meta
-
-    def place_near(meta, moved, after):
-        pieces, _ = settle(meta, moved, slots // slabs, per_slab, shares, (), after)
-        return [
-            swap(piece, "snap", share) if share else piece
-            for share, piece in zip(shares_of[1], pieces)
+        return to_pieces(pieces[0], "snap"), meta
+
+    def place(meta, moved, group, cuts, after):
+        pieces, _ = settle(meta, moved, slots // slabs, per_slab, shares, (), cuts, after)
+        return pieces, [
+            swap(piece, "snap", shares_of[group][k // cuts]) if shares_of[group][k // cuts] else piece
+            for k, piece in enumerate(pieces)
         ]
 
     def hops():
@@ -617,35 +630,38 @@
     other_y = swap(other_y, "space", 1)
     joined_near = merged(sent_x[1], [])
     far = to_chips(merged(sent_x[0], []))
-    settled, x_far, meta = place_far(None, far, [other_y, joined_near[0]])
+    x_far, meta = place_far(None, far, [other_y, joined_near[0]])
     near = to_chips(joined_near)
     y_far = to_chips(merge(same_y, other_y, chips, near[1:3], slice(0, half), shares))
     y_near = to_chips(merge(same_y, other_y, chips, y_far[1:3], slice(half, shares), shares))
-    x_cells = place_near(meta, near, []) + [x_far]
-
-    gram_local = gram_blocks(x_cells, y_far[1:3])
+    _, x_near = place(meta, near, 1, 1, [])
+    x_cells = x_near + [x_far]
+
+    gram_local = gram_blocks(x_cells, y_far[1:2])
     gram = to_pieces(gram_local.reshape(pairs * TILE, TILE))
-    gram = sum_pieces(gram, slabs, [])
-    settled, y_cells, _ = place_far(meta, y_far, [gram])
-    for hop in hops():
-        gram = add(gram, swap(gram, "snap", hop), [settled] if hop == 1 else y_near[1:3])
-    y_cells = place_near(meta, y_near, [gram]) + [y_cells]
+    settled, y_far = place(meta, y_far, 0, 2, [gram_local])
+    gram = sum_pieces(gram, slabs, settled[:1], shares)
+    gram = sum_pieces(to_pieces(gram, "snap"), shares, [y_far[0], y_far[2]] + y_near[1:3])
+    settled, y_near = place(meta, y_near, 1, 1, [gram])
+    y_cells = y_near + y_far
     gram = lax.all_gather(gram, "space", axis=0, tiled=True)
 
-    steps = factor_steps(gram.reshape(pairs, TILE, TILE), tiles, rows_total, y_cells[:1])
+    steps = factor_steps(gram.reshape(pairs, TILE, TILE), tiles, rows_total, settled[:1])
     state = next(steps)
-    for _ in range(tiles - 2):
+    for _ in range(tiles - 3):
         state = steps.send([])
     cross_local = cross_sum(x_cells, y_cells, [state])
-    cross = to_pieces(cross_local)
-    r_factor, inverse, *terms = steps.send([cross_local])
-
-    q_basis = basis(x_cells, terms, 0, 2, None, [])
-    cross = sum_pieces(cross, slabs, [q_basis])
+    state = steps.send([cross_local])
+    cross = sum_pieces(to_pieces(cross_local), slabs, [state])
+    r_factor, inverse, *terms = steps.send([cross])
+    tied = [r_factor]
+    for hop in hops():
+        cross = add(cross, swap(cross, "snap", hop), tied)
+        if hop == 1:
+            q_basis = basis(x_cells, terms, 0, 2, None, [cross])
+            tied = [q_basis]
     q_basis = basis(x_cells, terms, 1, 2, q_basis, [cross])
-    for hop in hops():
-        cross = add(cross, swap(cross, "snap", hop), [q_basis] if hop == 1 else [])
-    same = join([cross] + [swap(cross, "space", m) for m in range(CORES, slabs, CORES)])
+    same = join([cross] + [swap(cross, "space", m) for m in range(CORES, slabs, CORES)], [q_basis])
     projection = project(inverse, same, swap(same, "space", 1), slabs, math.sqrt(rows_total))
     return q_basis, r_factor, projection
 

time: 306 us -> 300 us (0.980)
  local copies, waits for them, and re-layouts: 46.1 us -> 40.1 us
    unnamed x116 -> x122, local copies, waits for them, and re-layouts: 46.1 us -> 40.1 us
    ppermute x25 -> x27, waiting for transfers between devices: 119 us -> 123 us  [swap(): lax.ppermute(value, axis, [(i, i ^ mask) for i in range(lax.axis_size(axi...]
    pallas_call x4 -> x2, Pallas kernels: 6.41 us -> 3.28 us  [add(): pl.pallas_call(lambda *refs: add_kernel(*refs[len(after):]), out_shape=ja...]
    ppermute x25 -> x27, starting transfers between devices: 34.4 us -> 33 us  [swap(): lax.ppermute(value, axis, [(i, i ^ mask) for i in range(lax.axis_size(axi...]
  transfers between devices with their start and end apart: 29 -> 31, of which waited for: 17 -> 12; matrix products, arithmetic and copies ran while one was open for 0% -> 0% of each run, Pallas kernels for 13% -> 13%
where the time goes in v10:
time: 300 us; the launch traced here: 299 us
  waiting for transfers between devices  132 us (44%)
  Pallas kernels  63.9 us (21%)
  starting transfers between devices  51.3 us (17%)
  local copies, waits for them, and re-layouts  40.1 us (13%)
  blocking collectives  10.5 us (4%)
    ppermute x27, waiting for transfers between devices, swap(): lax.ppermute(value, axis, [(i, i ^ mask) for i in range(lax.axis_size(axi...  123 us
    unnamed x122, local copies, waits for them, and re-layouts  40.1 us
    ppermute x27, starting transfers between devices, swap(): lax.ppermute(value, axis, [(i, i ^ mask) for i in range(lax.axis_size(axi...  33 us
    pallas_call x4, Pallas kernels, factor_call(): pl.pallas_call(lambda *refs: kernel(*refs[len(after):]), out_shape=out_sh...  19.7 us
    all_to_all x4, starting transfers between devices, to_pieces(): return lax.all_to_all(value, axis, split_axis=0, concat_axis=0, tiled=True)  18.3 us
    all_gather x1, blocking collectives, body(): gram = lax.all_gather(gram, 'space', axis=0, tiled=True)  10.5 us
    pallas_call x4, Pallas kernels, settle(): pl.pallas_call(lambda *refs: settle_kernel(chips, capacity, with_ids, far...  10.3 us
    all_to_all x4, waiting for transfers between devices, to_pieces(): return lax.all_to_all(value, axis, split_axis=0, concat_axis=0, tiled=True)  9.31 us
  transfers between devices with their start and end apart: 31, of which 12 were waited for; matrix products, arithmetic and copies ran while one was open for 0% of the time, Pallas kernels for 13%

profile of v10, /device:TPU:0, one launch (start us, length us, event | category | flops | bytes accessed | tf_op | source)
XLA Modules:
  0.0 298.7 jit_solution(6477069300302494384)
XLA Ops:
  0.6 2.2 copy-done.17
  3.5 3.0 %pack.3 = (bf16[256,32,128]{2,1,0:T(8,128)(2,1)S(1)}, bf16[256,32,128]{2,1,0:T(8,128)(2,1)S(1)}) custom-call(s32[128]{0:T(128)S(1)} %copy-done.49, bf16[128,4,32,128]{3,2,1,0:T(8,128)(2,1)S(1)} %bitcast.24), custom_call_target="tpu_custom_call" | custom-call | flops 1 | bytes 1 | tf_op jit(solution)/shard_map/pack/pallas_call | solution.py:77
  6.5 1.3 copy-done.9
  7.8 1.6 collective-permute-start.3
  9.4 3.1 %pack.2 = (bf16[132,32,128]{2,1,0:T(8,128)(2,1)S(1)}, bf16[132,32,128]{2,1,0:T(8,128)(2,1)S(1)}, bf16[128,32,128]{2,1,0:T(8,128)(2,1)S(1)}, bf16[128,32,128]{2,1,0:T(8,128)(2,1)S(1)}) custom-call(s32[128]{0:T(128)S(1)} %copy-done.49, bf16[128,4,32,128]{3,2,1,0:T(8,128)(2,1)S(1)} %bitcast.25), custom_call_target="tpu_custom_call" | custom-call | flops 1 | bytes 1 | tf_op jit(solution)/shard_map/pack/pallas_call | solution.py:77
  12.5 1.2 collective-permute-start.5
  13.8 2.3 collective-permute-done.5.refs_1_
  16.2 1.3 collective-permute-start.6
  20.0 11.4 %collective-permute-done.6.refs_3_ = bf16[66,32,128]{2,1,0:T(8,128)(2,1)S(1)} collective-permute-done((bf16[66,32,128]{2,1,0:T(8,128)(2,1)S(1)}, bf16[66,32,128]{2,1,0:T(8,128)(2,1)S(1)}, u32[]{:S(2)}, u32[]{:S(2)}) %collective-permute-start.6) | collective-permute-done | bytes 540704 | tf_op jit(solution)/shard_map/ppermute | solution.py:580
  31.4 11.7 %collective-permute-done.7.refs_4_ = bf16[66,32,128]{2,1,0:T(8,128)(2,1)S(1)} collective-permute-done((bf16[66,32,128]{2,1,0:T(8,128)(2,1)S(1)}, bf16[66,32,128]{2,1,0:T(8,128)(2,1)S(1)}, u32[]{:S(2)}, u32[]{:S(2)}) %collective-permute-start.7) | collective-permute-done | bytes 540704 | tf_op jit(solution)/shard_map/ppermute | solution.py:580
  43.1 2.8 settle.4
  46.0 1.3 copy-done.28
  47.4 5.2 %all-to-all-start = ((bf16[4,64,32,128]{3,2,1,0:T(8,128)(2,1)}), bf16[4,64,32,128]{3,2,1,0:T(8,128)(2,1)S(1)}, u32[]{:S(2)}, u32[]{:S(2)}) async-start(bf16[4,64,32,128]{3,2,1,0:T(8,128)(2,1)} %copy-done.28), calls=%async_computation | async-start | bytes 4194304 | tf_op jit(solution)/shard_map/all_to_all | solution.py:606
  52.6 1.7 collective-permute-start.1
  54.5 1.5 collective-permute-start.9
  56.1 11.6 %collective-permute-done.1.refs_0_.refs_2_ = bf16[64,32,128]{2,1,0:T(8,128)(2,1)S(1)} collective-permute-done((bf16[64,32,128]{2,1,0:T(8,128)(2,1)}, bf16[64,32,128]{2,1,0:T(8,128)(2,1)S(1)}, u32[]{:S(2)}, u32[]{:S(2)}) %collective-permute-start.1) | collective-permute-done | bytes 524320 | tf_op jit(solution)/shard_map/ppermute | solution.py:580
  67.6 8.5 %collective-permute-done.2.refs_1_.refs_3_ = bf16[64,32,128]{2,1,0:T(8,128)(2,1)S(1)} collective-permute-done((bf16[64,32,128]{2,1,0:T(8,128)(2,1)}, bf16[64,32,128]{2,1,0:T(8,128)(2,1)S(1)}, u32[]{:S(2)}, u32[]{:S(2)}) %collective-permute-start.2) | collective-permute-done | bytes 524320 | tf_op jit(solution)/shard_map/ppermute | solution.py:580
  76.2 1.7 collective-permute-done.9.refs_4_
  77.9 2.1 settle.5
  80.0 1.8 collective-permute-start.10
  81.8 1.6 copy-done.10
  86.5 15.9 %collective-permute-done.10.refs_2_.refs_3_ = bf16[64,32,128]{2,1,0:T(8,128)(2,1)S(1)} collective-permute-done((bf16[64,32,128]{2,1,0:T(8,128)(2,1)S(1)}, bf16[64,32,128]{2,1,0:T(8,128)(2,1)S(1)}, u32[]{:S(2)}, u32[]{:S(2)}) %collective-permute-start.10) | collective-permute-done | bytes 524320 | tf_op jit(solution)/shard_map/ppermute | solution.py:580
  103.2 1.4 copy-done.15
  104.6 2.3 gram_blocks.1.refs_0_
  107.8 4.2 %all-to-all-start.1 = ((f32[8,160,128]{2,1,0:T(8,128)}), f32[8,160,128]{2,1,0:T(8,128)}, u32[]{:S(2)}, u32[]{:S(2)}) async-start(f32[8,160,128]{2,1,0:T(8,128)} %bitcast.23), calls=%async_computation.1 | async-start | bytes 1310720 | tf_op jit(solution)/shard_map/all_to_all | solution.py:606
  112.0 1.9 collective-permute-start.11
  113.9 1.4 collective-permute-start.12
  115.3 29.2 %collective-permute-done.11.refs_4_.refs_1_ = bf16[64,32,128]{2,1,0:T(8,128)(2,1)S(1)} collective-permute-done((bf16[64,32,128]{2,1,0:T(8,128)(2,1)}, bf16[64,32,128]{2,1,0:T(8,128)(2,1)S(1)}, u32[]{:S(2)}, u32[]{:S(2)}) %collective-permute-start.11) | collective-permute-done | bytes 524320 | tf_op jit(solution)/shard_map/ppermute | solution.py:580
  144.6 1.6 copy-done.8
  146.2 1.6 copy-done.11
  148.8 1.3 merge.7
  150.4 1.5 collective-permute-start.15
  151.9 1.7 collective-permute-start.17
  153.6 2.9 settle.6
  157.2 1.9 sum_pieces.3
  159.0 4.4 %all-to-all-start.2 = ((f32[4,160,128]{2,1,0:T(8,128)}), f32[4,160,128]{2,1,0:T(8,128)}, u32[]{:S(2)}, u32[]{:S(2)}) async-start(f32[4,160,128]{2,1,0:T(8,128)} %bitcast.32), calls=%async_computation.2 | async-start | bytes 655360 | tf_op jit(solution)/shard_map/all_to_all | solution.py:606
  163.4 3.8 %collective-permute-start.14 = (bf16[64,16,128]{2,1,0:T(8,128)(2,1)S(1)}, bf16[64,16,128]{2,1,0:T(8,128)(2,1)S(1)}, u32[]{:S(2)}, u32[]{:S(2)}) collective-permute-start(bf16[64,16,128]{2,1,0:T(8,128)(2,1)S(1)} %get-tuple-element.63), channel_id=1, source_target_pairs={{0,3},{1,2},{2,1},{3,0},{4,7},{5,6},{6,5},{7,4},{8,11},{9,10},{10,... | collective-permute-start | bytes 786440 | tf_op jit(solution)/shard_map/ppermute | solution.py:580
  167.3 12.8 %collective-permute-done.14.refs_1_.refs_8_ = bf16[64,16,128]{2,1,0:T(8,128)(2,1)S(1)} collective-permute-done((bf16[64,16,128]{2,1,0:T(8,128)(2,1)S(1)}, bf16[64,16,128]{2,1,0:T(8,128)(2,1)S(1)}, u32[]{:S(2)}, u32[]{:S(2)}) %collective-permute-start.14) | collective-permute-done | bytes 262176 | tf_op jit(solution)/shard_map/ppermute | solution.py:580
  180.0 15.2 %collective-permute-done.13.refs_0_.refs_6_ = bf16[64,16,128]{2,1,0:T(8,128)(2,1)S(1)} collective-permute-done((bf16[64,16,128]{2,1,0:T(8,128)(2,1)}, bf16[64,16,128]{2,1,0:T(8,128)(2,1)S(1)}, u32[]{:S(2)}, u32[]{:S(2)}) %collective-permute-start.13) | collective-permute-done | bytes 262176 | tf_op jit(solution)/shard_map/ppermute | solution.py:580
  196.0 1.6 sum_pieces.4.refs_0_
  200.6 2.5 settle.7
  203.2 2.0 collective-permute-start.19
  205.2 2.4 collective-permute-start.20
  207.6 10.5 %all_gather.3 = f32[1280,128]{1,0:T(8,128)S(1)} all-gather(f32[160,128]{1,0:T(8,128)S(1)} %copy-done.45), channel_id=1, replica_groups=mesh['space'=8,'snap'=4] {'space'}, dimensions={0}, use_global_device_ids=true | all-gather | bytes 737280 | tf_op jit(solution)/shard_map/all_gather | solution.py:647
  218.1 4.9 %factor.4.refs_0_ = f32[4,8,128,128]{3,2,1,0:T(8,128)S(1)} custom-call(bf16[64,32,128]{2,1,0:T(8,128)(2,1)S(1)} %get-tuple-element.68.refs_0_.refs_4_, f32[10,128,128]{2,1,0:T(8,128)S(1)} %bitcast.26), custom_call_target="tpu_custom_call" | custom-call | flops 1 | bytes 1 | tf_op jit(solution)/shard_map/factor/pallas_call | solution.py:429
  223.1 4.8 %factor.5.refs_0_.refs_1_ = f32[4,8,128,128]{3,2,1,0:T(8,128)S(1)} custom-call(f32[4,8,128,128]{3,2,1,0:T(8,128)S(1)} %factor.4.refs_0_), custom_call_target="tpu_custom_call", output_to_operand_aliasing={{}: (0, {})} | custom-call | flops 1 | bytes 1 | tf_op jit(solution)/shard_map/factor/pallas_call | solution.py:429
  228.0 3.2 %cross_sum.1.refs_0_ = f32[512,512]{1,0:T(8,128)} custom-call(f32[4,8,128,128]{3,2,1,0:T(8,128)S(1)} %factor.5.refs_0_.refs_1_, bf16[64,32,128]{2,1,0:T(8,128)(2,1)S(1)} %get-tuple-element.56.refs_1_.refs_2_, bf16[64,32,128]{2,1,0:T(8,128)(2,1)S(1)} %collective-permute-done.10.refs_2_.refs_3_, bf16[4,64,32,128]{3,2,1,0:T(8,128)(2,1)S(1)} %copy-done.3, ...), custom_call_target="tpu_custom_call" | custom-call | flops 1 | bytes 1 | tf_op jit(solution)/shard_map/cross_sum/pallas_call | solution.py:293
  231.2 4.5 %all-to-all-start.3 = ((f32[8,64,512]{2,1,0:T(8,128)}), f32[8,64,512]{2,1,0:T(8,128)}, u32[]{:S(2)}, u32[]{:S(2)}) async-start(f32[8,64,512]{2,1,0:T(8,128)} %bitcast.17), calls=%async_computation.3 | async-start | bytes 2097152 | tf_op jit(solution)/shard_map/all_to_all | solution.py:606
  235.7 4.6 %factor.6.refs_0_.refs_1_ = f32[4,8,128,128]{3,2,1,0:T(8,128)S(1)} custom-call(f32[512,512]{1,0:T(8,128)} %cross_sum.1.refs_0_, f32[4,8,128,128]{3,2,1,0:T(8,128)S(1)} %factor.5.refs_0_.refs_1_), custom_call_target="tpu_custom_call", output_to_operand_aliasing={{}: (1, {})} | custom-call | flops 1 | bytes 1 | tf_op jit(solution)/shard_map/factor/pallas_call | solution.py:429
  240.3 1.3 copy-done
  241.6 9.3 %all-to-all-done.3 = f32[8,64,512]{2,1,0:T(8,128)} async-done(((f32[8,64,512]{2,1,0:T(8,128)}), f32[8,64,512]{2,1,0:T(8,128)}, u32[]{:S(2)}, u32[]{:S(2)}) %all-to-all-start.3) | async-done | bytes 1048608 | tf_op jit(solution)/shard_map/all_to_all | solution.py:606
  250.9 2.1 sum_pieces.5.refs_0_.refs_1_
  254.6 5.4 %factor.7 = (f32[512,512]{1,0:T(8,128)}, f32[512,512]{1,0:T(8,128)S(1)}, bf16[512,512]{1,0:T(8,128)(2,1)S(1)}, bf16[512,512]{1,0:T(8,128)(2,1)S(1)}, bf16[512,512]{1,0:T(8,128)(2,1)S(1)}) custom-call(f32[64,512]{1,0:T(8,128)S(1)} %copy-done.38, f32[4,8,128,128]{3,2,1,0:T(8,128)S(1)} %copy-done.1), custom_call_target="tpu_custom_call" | custom-call | flops 1 | bytes 1 | tf_op jit(solution)/shard_map/factor/pallas_call | solution.py:429
  264.0 1.7 add.2.refs_0_.refs_1_
  265.7 1.3 collective-permute-start.22
  267.0 1.6 copy-done.4
  272.6 3.5 %basis.2.refs_0_ = f32[64,32,512]{2,1,0:T(8,128)} custom-call(f32[64,512]{1,0:T(8,128)S(1)} %copy-done.37, bf16[64,32,128]{2,1,0:T(8,128)(2,1)S(1)} %get-tuple-element.56.refs_1_.refs_2_, bf16[64,32,128]{2,1,0:T(8,128)(2,1)S(1)} %collective-permute-done.10.refs_2_.refs_3_, bf16[4,64,32,128]{3,2,1,0:T(8,128)(2,1)S(1)} %copy-done.4, ...), custom_call_target="tpu_custom_call" | custom-call | flops 1 | bytes 1 | tf_op jit(solution)/shard_map/basis/pallas_call | solution.py:482
  276.8 1.6 add.3.refs_1_
  279.0 1.4 collective-permute-start.24
  280.4 1.5 collective-permute-start.23
  285.9 3.5 %basis.3.refs_0_ = f32[64,32,512]{2,1,0:T(8,128)} custom-call(f32[64,32,512]{2,1,0:T(8,128)} %basis.2.refs_0_, f32[64,512]{1,0:T(8,128)S(1)} %copy-done.36, bf16[64,32,128]{2,1,0:T(8,128)(2,1)S(1)} %get-tuple-element.56.refs_1_.refs_2_, bf16[64,32,128]{2,1,0:T(8,128)(2,1)S(1)} %collective-permute-done.10.refs_2_.refs_3_, ...), custom_call_target="tpu_custom_call", output_to_operand_aliasing={{}: (0, {})} | custom-call | flops 1 | bytes 1 | tf_op jit(solution)/shard_map/basis/pallas_call | solution.py:482
  290.8 1.9 join.1.refs_1_
  292.7 2.1 collective-permute-done.26.refs_2_
  295.9 2.9 project.1
  (146 shorter events, 31.6 us)
Async XLA Ops:
  0.6 2.2 copy-start.17
  3.5 5.9 %copy-start.18 = (bf16[128,128,128]{2,1,0:T(8,128)(2,1)S(1)}, bf16[128,128,128]{2,1,0:T(8,128)(2,1)}, u32[]{:S(2)}) copy-start(bf16[128,128,128]{2,1,0:T(8,128)(2,1)} %param.3) | copy-start | bytes 12582916
  6.5 1.3 copy-start.9
  7.8 35.3 %collective-permute-start.3 = (bf16[256,32,128]{2,1,0:T(8,128)(2,1)S(1)}, bf16[256,32,128]{2,1,0:T(8,128)(2,1)S(1)}, u32[]{:S(2)}, u32[]{:S(2)}) collective-permute-start(bf16[256,32,128]{2,1,0:T(8,128)(2,1)S(1)} %get-tuple-element.45), channel_id=1, source_target_pairs={{0,4},{4,0},{8,12},{12,8},{16,20},{20,16},{24,28},{28,24},{1,5},{5... | collective-permute-start | bytes 6291464 | tf_op jit(solution)/shard_map/ppermute | solution.py:580
  12.5 3.6 %collective-permute-start.5 = (bf16[132,32,128]{2,1,0:T(8,128)(2,1)S(1)}, bf16[132,32,128]{2,1,0:T(8,128)(2,1)S(1)}, u32[]{:S(2)}, u32[]{:S(2)}) collective-permute-start(bf16[132,32,128]{2,1,0:T(8,128)(2,1)S(1)} %get-tuple-element.49), channel_id=1, source_target_pairs={{0,4},{4,0},{8,12},{12,8},{16,20},{20,16},{24,28},{28,24},{1,5},{5... | collective-permute-start | bytes 3244040 | tf_op jit(solution)/shard_map/ppermute | solution.py:580
  13.8 6.0 %collective-permute-start = (bf16[128,32,128]{2,1,0:T(8,128)(2,1)S(1)}, bf16[128,32,128]{2,1,0:T(8,128)(2,1)S(1)}, u32[]{:S(2)}, u32[]{:S(2)}) collective-permute-start(bf16[128,32,128]{2,1,0:T(8,128)(2,1)S(1)} %get-tuple-element.41), channel_id=1, source_target_pairs={{0,4},{4,0},{8,12},{12,8},{16,20},{20,16},{24,28},{28,24},{1,5},{5... | collective-permute-start | bytes 3145736 | tf_op jit(solution)/shard_map/ppermute | solution.py:580
  16.2 15.2 %collective-permute-start.6 = (bf16[66,32,128]{2,1,0:T(8,128)(2,1)S(1)}, bf16[66,32,128]{2,1,0:T(8,128)(2,1)S(1)}, u32[]{:S(2)}, u32[]{:S(2)}) collective-permute-start(bf16[66,32,128]{2,1,0:T(8,128)(2,1)S(1)} %get-tuple-element.51), channel_id=1, source_target_pairs={{0,8},{4,12},{8,0},{12,4},{16,24},{20,28},{24,16},{28,20},{1,9},{5... | collective-permute-start | bytes 1622024 | tf_op jit(solution)/shard_map/ppermute | solution.py:580
  17.5 25.6 %collective-permute-start.7 = (bf16[66,32,128]{2,1,0:T(8,128)(2,1)S(1)}, bf16[66,32,128]{2,1,0:T(8,128)(2,1)S(1)}, u32[]{:S(2)}, u32[]{:S(2)}) collective-permute-start(bf16[66,32,128]{2,1,0:T(8,128)(2,1)S(1)} %get-tuple-element.52), channel_id=1, source_target_pairs={{0,16},{4,20},{8,24},{12,28},{16,0},{20,4},{24,8},{28,12},{1,17},{... | collective-permute-start | bytes 1622024 | tf_op jit(solution)/shard_map/ppermute | solution.py:580
  18.6 24.5 %collective-permute-start.8 = (bf16[66,32,128]{2,1,0:T(8,128)(2,1)S(1)}, bf16[66,32,128]{2,1,0:T(8,128)(2,1)S(1)}, u32[]{:S(2)}, u32[]{:S(2)}) collective-permute-start(bf16[66,32,128]{2,1,0:T(8,128)(2,1)S(1)} %get-tuple-element.53), channel_id=1, source_target_pairs={{0,24},{4,28},{8,16},{12,20},{16,8},{20,12},{24,0},{28,4},{1,25},{... | collective-permute-start | bytes 1622024 | tf_op jit(solution)/shard_map/ppermute | solution.py:580
  19.9 26.0 %copy-start.29 = (bf16[64,32,128]{2,1,0:T(8,128)(2,1)}, bf16[64,32,128]{2,1,0:T(8,128)(2,1)S(1)}, u32[]{:S(2)}) copy-start(bf16[64,32,128]{2,1,0:T(8,128)(2,1)S(1)} %get-tuple-element.47.refs_1_) | copy-start | bytes 1572868
  20.0 26.0 %copy-start.51 = (bf16[64,32,128]{2,1,0:T(8,128)(2,1)}, bf16[64,32,128]{2,1,0:T(8,128)(2,1)S(1)}, u32[]{:S(2)}) copy-start(bf16[64,32,128]{2,1,0:T(8,128)(2,1)S(1)} %get-tuple-element.55) | copy-start | bytes 1572868
  20.0 26.0 %copy-start.53 = (bf16[64,32,128]{2,1,0:T(8,128)(2,1)}, bf16[64,32,128]{2,1,0:T(8,128)(2,1)S(1)}, u32[]{:S(2)}) copy-start(bf16[64,32,128]{2,1,0:T(8,128)(2,1)S(1)} %get-tuple-element.43) | copy-start | bytes 1572868
  20.0 26.0 %copy-start.54 = (bf16[64,32,128]{2,1,0:T(8,128)(2,1)}, bf16[64,32,128]{2,1,0:T(8,128)(2,1)S(1)}, u32[]{:S(2)}) copy-start(bf16[64,32,128]{2,1,0:T(8,128)(2,1)S(1)} %get-tuple-element.42) | copy-start | bytes 1572868
  43.1 2.9 copy-start.6
  46.0 1.3 copy-start.28
  47.4 7.2 %copy-start.52 = (bf16[64,32,128]{2,1,0:T(8,128)(2,1)S(1)}, bf16[64,32,128]{2,1,0:T(8,128)(2,1)}, u32[]{:S(2)}) copy-start(bf16[64,32,128]{2,1,0:T(8,128)(2,1)} %copy-done.51) | copy-start | bytes 1572868
  47.4 30.6 %copy-start.30 = (bf16[64,32,128]{2,1,0:T(8,128)(2,1)S(1)}, bf16[64,32,128]{2,1,0:T(8,128)(2,1)}, u32[]{:S(2)}) copy-start(bf16[64,32,128]{2,1,0:T(8,128)(2,1)} %copy-done.29) | copy-start | bytes 1572868
  47.4 55.9 %all-to-all-start = ((bf16[4,64,32,128]{3,2,1,0:T(8,128)(2,1)}), bf16[4,64,32,128]{3,2,1,0:T(8,128)(2,1)S(1)}, u32[]{:S(2)}, u32[]{:S(2)}) async-start(bf16[4,64,32,128]{3,2,1,0:T(8,128)(2,1)} %copy-done.28), calls=%async_computation | async-start | bytes 4194304 | tf_op jit(solution)/shard_map/all_to_all | solution.py:606
  52.6 29.2 %copy-start.7 = (bf16[256,32,128]{2,1,0:T(8,128)(2,1)S(1)}, bf16[256,32,128]{2,1,0:T(8,128)(2,1)}, u32[]{:S(2)}) copy-start(bf16[256,32,128]{2,1,0:T(8,128)(2,1)} %copy-done.6) | copy-start | bytes 6291460
  52.6 15.1 %collective-permute-start.1 = (bf16[64,32,128]{2,1,0:T(8,128)(2,1)}, bf16[64,32,128]{2,1,0:T(8,128)(2,1)S(1)}, u32[]{:S(2)}, u32[]{:S(2)}) collective-permute-start(bf16[64,32,128]{2,1,0:T(8,128)(2,1)} %copy-done.54), channel_id=1, source_target_pairs={{0,8},{4,12},{8,0},{12,4},{16,24},{20,28},{24,16},{28,20},{1,9},{5... | collective-permute-start | bytes 1572872 | tf_op jit(solution)/shard_map/ppermute | solution.py:580
  54.2 21.9 %collective-permute-start.2 = (bf16[64,32,128]{2,1,0:T(8,128)(2,1)}, bf16[64,32,128]{2,1,0:T(8,128)(2,1)S(1)}, u32[]{:S(2)}, u32[]{:S(2)}) collective-permute-start(bf16[64,32,128]{2,1,0:T(8,128)(2,1)} %copy-done.53), channel_id=1, source_target_pairs={{0,16},{4,20},{8,24},{12,28},{16,0},{20,4},{24,8},{28,12},{1,17},{... | collective-permute-start | bytes 1572872 | tf_op jit(solution)/shard_map/ppermute | solution.py:580
  54.5 23.4 %collective-permute-start.9 = (bf16[64,32,128]{2,1,0:T(8,128)(2,1)S(1)}, bf16[64,32,128]{2,1,0:T(8,128)(2,1)S(1)}, u32[]{:S(2)}, u32[]{:S(2)}) collective-permute-start(bf16[64,32,128]{2,1,0:T(8,128)(2,1)S(1)} %copy-done.52), channel_id=1, source_target_pairs={{0,24},{4,28},{8,16},{12,20},{16,8},{20,12},{24,0},{28,4},{1,25},{... | collective-permute-start | bytes 1572872 | tf_op jit(solution)/shard_map/ppermute | solution.py:580
  80.0 22.4 %collective-permute-start.10 = (bf16[64,32,128]{2,1,0:T(8,128)(2,1)S(1)}, bf16[64,32,128]{2,1,0:T(8,128)(2,1)S(1)}, u32[]{:S(2)}, u32[]{:S(2)}) collective-permute-start(bf16[64,32,128]{2,1,0:T(8,128)(2,1)S(1)} %get-tuple-element.57), channel_id=1, source_target_pairs={{0,1},{1,0},{2,3},{3,2},{4,5},{5,4},{6,7},{7,6},{8,9},{9,8},{10,11... | collective-permute-start | bytes 1572872 | tf_op jit(solution)/shard_map/ppermute | solution.py:580
  81.8 1.6 copy-start.10
  86.0 16.5 %collective-permute-start.4 = (bf16[64,32,128]{2,1,0:T(8,128)(2,1)S(1)}, bf16[64,32,128]{2,1,0:T(8,128)(2,1)S(1)}, u32[]{:S(2)}, u32[]{:S(2)}) collective-permute-start(bf16[64,32,128]{2,1,0:T(8,128)(2,1)S(1)} %bitcast.31), channel_id=1, source_target_pairs={{0,8},{4,12},{8,0},{12,4},{16,24},{20,28},{24,16},{28,20},{1,9},{5... | collective-permute-start | bytes 1572872 | tf_op jit(solution)/shard_map/ppermute | solution.py:580
  103.2 3.7 %copy-start.2 = (bf16[4,64,32,128]{3,2,1,0:T(8,128)(2,1)}, bf16[4,64,32,128]{3,2,1,0:T(8,128)(2,1)S(1)}, u32[]{:S(2)}) copy-start(bf16[4,64,32,128]{3,2,1,0:T(8,128)(2,1)S(1)} %all-to-all-done.refs_3_.refs_4_) | copy-start | bytes 6291460
  103.2 1.4 copy-start.15
  107.8 49.4 %all-to-all-start.1 = ((f32[8,160,128]{2,1,0:T(8,128)}), f32[8,160,128]{2,1,0:T(8,128)}, u32[]{:S(2)}, u32[]{:S(2)}) async-start(f32[8,160,128]{2,1,0:T(8,128)} %bitcast.23), calls=%async_computation.1 | async-start | bytes 1310720 | tf_op jit(solution)/shard_map/all_to_all | solution.py:606
  112.0 32.6 %collective-permute-start.11 = (bf16[64,32,128]{2,1,0:T(8,128)(2,1)}, bf16[64,32,128]{2,1,0:T(8,128)(2,1)S(1)}, u32[]{:S(2)}, u32[]{:S(2)}) collective-permute-start(bf16[64,32,128]{2,1,0:T(8,128)(2,1)} %bitcast.30), channel_id=1, source_target_pairs={{0,16},{4,20},{8,24},{12,28},{16,0},{20,4},{24,8},{28,12},{1,17},{... | collective-permute-start | bytes 1572872 | tf_op jit(solution)/shard_map/ppermute | solution.py:580
  113.9 39.7 %collective-permute-start.12 = (bf16[64,32,128]{2,1,0:T(8,128)(2,1)}, bf16[64,32,128]{2,1,0:T(8,128)(2,1)S(1)}, u32[]{:S(2)}, u32[]{:S(2)}) collective-permute-start(bf16[64,32,128]{2,1,0:T(8,128)(2,1)} %bitcast.29), channel_id=1, source_target_pairs={{0,24},{4,28},{8,16},{12,20},{16,8},{20,12},{24,0},{28,4},{1,25},{... | collective-permute-start | bytes 1572872 | tf_op jit(solution)/shard_map/ppermute | solution.py:580
  144.6 1.6 copy-start.8
  146.2 1.6 copy-start.11
  148.8 4.8 %copy-start.13 = (f32[10,128,128]{2,1,0:T(8,128)S(1)}, f32[10,128,128]{2,1,0:T(8,128)}, u32[]{:S(2)}) copy-start(f32[10,128,128]{2,1,0:T(8,128)} %copy-done.12) | copy-start | bytes 1966084
  148.8 4.8 %copy-start.47 = (bf16[2,16,2,32,128]{4,3,2,1,0:T(8,128)(2,1)S(1)}, bf16[2,16,2,32,128]{4,3,2,1,0:T(8,128)(2,1)}, u32[]{:S(2)}) copy-start(bf16[2,16,2,32,128]{4,3,2,1,0:T(8,128)(2,1)} %copy-done.46) | copy-start | bytes 1572868
  150.1 17.2 %collective-permute-start.16 = (bf16[64,32,128]{2,1,0:T(8,128)(2,1)}, bf16[64,32,128]{2,1,0:T(8,128)(2,1)S(1)}, u32[]{:S(2)}, u32[]{:S(2)}) collective-permute-start(bf16[64,32,128]{2,1,0:T(8,128)(2,1)} %bitcast.9), channel_id=1, source_target_pairs={{0,16},{4,20},{8,24},{12,28},{16,0},{20,4},{24,8},{28,12},{1,17},{... | collective-permute-start | bytes 1572872 | tf_op jit(solution)/shard_map/ppermute | solution.py:580
  150.4 16.9 %collective-permute-start.15 = (bf16[64,32,128]{2,1,0:T(8,128)(2,1)}, bf16[64,32,128]{2,1,0:T(8,128)(2,1)S(1)}, u32[]{:S(2)}, u32[]{:S(2)}) collective-permute-start(bf16[64,32,128]{2,1,0:T(8,128)(2,1)} %bitcast.8), channel_id=1, source_target_pairs={{0,8},{4,12},{8,0},{12,4},{16,24},{20,28},{24,16},{28,20},{1,9},{5... | collective-permute-start | bytes 1572872 | tf_op jit(solution)/shard_map/ppermute | solution.py:580
  151.9 45.8 %collective-permute-start.17 = (bf16[64,32,128]{2,1,0:T(8,128)(2,1)}, bf16[64,32,128]{2,1,0:T(8,128)(2,1)}, u32[]{:S(2)}, u32[]{:S(2)}) collective-permute-start(bf16[64,32,128]{2,1,0:T(8,128)(2,1)} %bitcast.15), channel_id=1, source_target_pairs={{0,24},{4,28},{8,16},{12,20},{16,8},{20,12},{24,0},{28,4},{1,25},{... | collective-permute-start | bytes 1572872 | tf_op jit(solution)/shard_map/ppermute | solution.py:580
  159.0 36.3 %all-to-all-start.2 = ((f32[4,160,128]{2,1,0:T(8,128)}), f32[4,160,128]{2,1,0:T(8,128)}, u32[]{:S(2)}, u32[]{:S(2)}) async-start(f32[4,160,128]{2,1,0:T(8,128)} %bitcast.32), calls=%async_computation.2 | async-start | bytes 655360 | tf_op jit(solution)/shard_map/all_to_all | solution.py:606
  163.4 16.6 %collective-permute-start.14 = (bf16[64,16,128]{2,1,0:T(8,128)(2,1)S(1)}, bf16[64,16,128]{2,1,0:T(8,128)(2,1)S(1)}, u32[]{:S(2)}, u32[]{:S(2)}) collective-permute-start(bf16[64,16,128]{2,1,0:T(8,128)(2,1)S(1)} %get-tuple-element.63), channel_id=1, source_target_pairs={{0,3},{1,2},{2,1},{3,0},{4,7},{5,6},{6,5},{7,4},{8,11},{9,10},{10,... | collective-permute-start | bytes 786440 | tf_op jit(solution)/shard_map/ppermute | solution.py:580
  167.2 28.0 %collective-permute-start.13 = (bf16[64,16,128]{2,1,0:T(8,128)(2,1)}, bf16[64,16,128]{2,1,0:T(8,128)(2,1)S(1)}, u32[]{:S(2)}, u32[]{:S(2)}) collective-permute-start(bf16[64,16,128]{2,1,0:T(8,128)(2,1)} %copy-done.48), channel_id=1, source_target_pairs={{0,2},{1,3},{2,0},{3,1},{4,6},{5,7},{6,4},{7,5},{8,10},{9,11},{10,... | collective-permute-start | bytes 786440 | tf_op jit(solution)/shard_map/ppermute | solution.py:580
  167.3 28.0 %copy-start.32 = (bf16[64,32,128]{2,1,0:T(8,128)(2,1)}, bf16[64,32,128]{2,1,0:T(8,128)(2,1)S(1)}, u32[]{:S(2)}) copy-start(bf16[64,32,128]{2,1,0:T(8,128)(2,1)S(1)} %collective-permute-done.16.refs_3_.refs_4_) | copy-start | bytes 1572868
  167.3 28.0 %copy-start.34 = (bf16[64,32,128]{2,1,0:T(8,128)(2,1)}, bf16[64,32,128]{2,1,0:T(8,128)(2,1)S(1)}, u32[]{:S(2)}) copy-start(bf16[64,32,128]{2,1,0:T(8,128)(2,1)S(1)} %collective-permute-done.15.refs_2_.refs_3_) | copy-start | bytes 1572868
  180.0 15.3 %copy-start.41 = (bf16[64,16,128]{2,1,0:T(8,128)(2,1)}, bf16[64,16,128]{2,1,0:T(8,128)(2,1)S(1)}, u32[]{:S(2)}) copy-start(bf16[64,16,128]{2,1,0:T(8,128)(2,1)S(1)} %collective-permute-done.14.refs_1_.refs_8_) | copy-start | bytes 786436
  197.6 1.0 copy-start.33
  203.1 24.8 %collective-permute-start.18 = (bf16[64,32,128]{2,1,0:T(8,128)(2,1)S(1)}, bf16[64,32,128]{2,1,0:T(8,128)(2,1)S(1)}, u32[]{:S(2)}, u32[]{:S(2)}) collective-permute-start(bf16[64,32,128]{2,1,0:T(8,128)(2,1)S(1)} %get-tuple-element.69), channel_id=1, source_target_pairs={{0,1},{1,0},{2,3},{3,2},{4,5},{5,4},{6,7},{7,6},{8,9},{9,8},{10,11... | collective-permute-start | bytes 1572872 | tf_op jit(solution)/shard_map/ppermute | solution.py:580
  203.2 24.7 %collective-permute-start.19 = (bf16[64,16,128]{2,1,0:T(8,128)(2,1)}, bf16[64,16,128]{2,1,0:T(8,128)(2,1)S(1)}, u32[]{:S(2)}, u32[]{:S(2)}) collective-permute-start(bf16[64,16,128]{2,1,0:T(8,128)(2,1)} %get-tuple-element.70), channel_id=1, source_target_pairs={{0,2},{1,3},{2,0},{3,1},{4,6},{5,7},{6,4},{7,5},{8,10},{9,11},{10,... | collective-permute-start | bytes 786440 | tf_op jit(solution)/shard_map/ppermute | solution.py:580
  205.2 22.7 %collective-permute-start.20 = (bf16[64,16,128]{2,1,0:T(8,128)(2,1)}, bf16[64,16,128]{2,1,0:T(8,128)(2,1)S(1)}, u32[]{:S(2)}, u32[]{:S(2)}) collective-permute-start(bf16[64,16,128]{2,1,0:T(8,128)(2,1)} %get-tuple-element.71), channel_id=1, source_target_pairs={{0,3},{1,2},{2,1},{3,0},{4,7},{5,6},{6,5},{7,4},{8,11},{9,10},{10,... | collective-permute-start | bytes 786440 | tf_op jit(solution)/shard_map/ppermute | solution.py:580
  223.1 4.9 %copy-start.3 = (bf16[4,64,32,128]{3,2,1,0:T(8,128)(2,1)S(1)}, bf16[4,64,32,128]{3,2,1,0:T(8,128)(2,1)}, u32[]{:S(2)}) copy-start(bf16[4,64,32,128]{3,2,1,0:T(8,128)(2,1)} %copy-done.2) | copy-start | bytes 6291460
  223.1 4.9 %copy-start.42 = (bf16[64,16,128]{2,1,0:T(8,128)(2,1)S(1)}, bf16[64,16,128]{2,1,0:T(8,128)(2,1)}, u32[]{:S(2)}) copy-start(bf16[64,16,128]{2,1,0:T(8,128)(2,1)} %copy-done.41) | copy-start | bytes 786436
  223.1 4.9 %copy-start.44 = (bf16[64,16,128]{2,1,0:T(8,128)(2,1)S(1)}, bf16[64,16,128]{2,1,0:T(8,128)(2,1)}, u32[]{:S(2)}) copy-start(bf16[64,16,128]{2,1,0:T(8,128)(2,1)} %copy-done.43) | copy-start | bytes 786436
  231.2 19.7 %all-to-all-start.3 = ((f32[8,64,512]{2,1,0:T(8,128)}), f32[8,64,512]{2,1,0:T(8,128)}, u32[]{:S(2)}, u32[]{:S(2)}) async-start(f32[8,64,512]{2,1,0:T(8,128)} %bitcast.17), calls=%async_computation.3 | async-start | bytes 2097152 | tf_op jit(solution)/shard_map/all_to_all | solution.py:606
  240.3 1.3 copy-start
  250.9 2.8 copy-start.1
  253.0 10.4 %collective-permute-start.21 = (f32[64,512]{1,0:T(8,128)}, f32[64,512]{1,0:T(8,128)S(1)}, u32[]{:S(2)}, u32[]{:S(2)}) collective-permute-start(f32[64,512]{1,0:T(8,128)} %sum_pieces.5.refs_0_.refs_1_), channel_id=1, source_target_pairs={{0,1},{1,0},{2,3},{3,2},{4,5},{5,4},{6,7},{7,6},{8,9},{9,8},{10,11... | collective-permute-start | bytes 393224 | tf_op jit(solution)/shard_map/ppermute | solution.py:580
  265.7 10.4 %collective-permute-start.22 = (f32[64,512]{1,0:T(8,128)}, f32[64,512]{1,0:T(8,128)S(1)}, u32[]{:S(2)}, u32[]{:S(2)}) collective-permute-start(f32[64,512]{1,0:T(8,128)} %add.2.refs_0_.refs_1_), channel_id=1, source_target_pairs={{0,2},{1,3},{2,0},{3,1},{4,6},{5,7},{6,4},{7,5},{8,10},{9,11},{10,... | collective-permute-start | bytes 393224 | tf_op jit(solution)/shard_map/ppermute | solution.py:580
  267.0 1.6 copy-start.4
  276.1 5.8 %copy-start.5 = (bf16[4,64,32,128]{3,2,1,0:T(8,128)(2,1)S(1)}, bf16[4,64,32,128]{3,2,1,0:T(8,128)(2,1)}, u32[]{:S(2)}) copy-start(bf16[4,64,32,128]{3,2,1,0:T(8,128)(2,1)} %copy-done.2) | copy-start | bytes 6291460
  278.4 11.0 %collective-permute-start.25 = (f32[64,512]{1,0:T(8,128)}, f32[64,512]{1,0:T(8,128)S(1)}, u32[]{:S(2)}, u32[]{:S(2)}) collective-permute-start(f32[64,512]{1,0:T(8,128)} %add.3.refs_1_), channel_id=1, source_target_pairs={{0,24},{4,28},{8,16},{12,20},{16,8},{20,12},{24,0},{28,4},{1,25},{... | collective-permute-start | bytes 393224 | tf_op jit(solution)/shard_map/ppermute | solution.py:580
  279.0 10.4 %collective-permute-start.24 = (f32[64,512]{1,0:T(8,128)}, f32[64,512]{1,0:T(8,128)S(1)}, u32[]{:S(2)}, u32[]{:S(2)}) collective-permute-start(f32[64,512]{1,0:T(8,128)} %add.3.refs_1_), channel_id=1, source_target_pairs={{0,16},{4,20},{8,24},{12,28},{16,0},{20,4},{24,8},{28,12},{1,17},{... | collective-permute-start | bytes 393224 | tf_op jit(solution)/shard_map/ppermute | solution.py:580
  280.4 9.1 %collective-permute-start.23 = (f32[64,512]{1,0:T(8,128)}, f32[64,512]{1,0:T(8,128)S(1)}, u32[]{:S(2)}, u32[]{:S(2)}) collective-permute-start(f32[64,512]{1,0:T(8,128)} %add.3.refs_1_), channel_id=1, source_target_pairs={{0,8},{4,12},{8,0},{12,4},{16,24},{20,28},{24,16},{28,20},{1,9},{5... | collective-permute-start | bytes 393224 | tf_op jit(solution)/shard_map/ppermute | solution.py:580
  281.9 1.0 copy-start.21
  289.4 5.4 %copy-start.40 = (f32[512,512]{1,0:T(8,128)S(1)}, f32[512,512]{1,0:T(8,128)}, u32[]{:S(2)}) copy-start(f32[512,512]{1,0:T(8,128)} %copy-done.39) | copy-start | bytes 3145732
  292.7 2.1 collective-permute-start.26
  294.8 1.0 copy-start.31
  (28 other events, 23.7 us)

commit v11 on v10

--- a/solution.py
+++ b/solution.py
@@ -11,6 +11,7 @@
 GROUP = 8
 CORES = 2
 VMEM_BYTES = 32 * 1024 * 1024
+GRID_VMEM_BYTES = 56 * 1024 * 1024
 HIGHEST = lax.Precision.HIGHEST
 SMEM = pl.BlockSpec(memory_space=pltpu.SMEM)
 VMEM = pl.BlockSpec(memory_space=pltpu.VMEM)
@@ -244,7 +245,7 @@
         in_specs=[ANY] * len(after) + cell_specs(shares, blocks // steps, rows, width, 0),
         out_specs=pl.BlockSpec((pairs, TILE, TILE), lambda i: (0, 0, 0)),
         scratch_shapes=[pltpu.VMEM((full, full), jnp.float32)],
-        compiler_params=pltpu.CompilerParams(vmem_limit_bytes=VMEM_BYTES),
+        compiler_params=pltpu.CompilerParams(vmem_limit_bytes=GRID_VMEM_BYTES),
         cost_estimate=LIGHT,
         name="gram_blocks",
     )(*after, *cells)
@@ -297,7 +298,7 @@
         in_specs=[ANY] * len(after) + specs,
         out_specs=pl.BlockSpec((full, full), lambda i: (0, 0)),
         scratch_shapes=[pltpu.VMEM((full, full), jnp.float32)],
-        compiler_params=pltpu.CompilerParams(vmem_limit_bytes=VMEM_BYTES),
+        compiler_params=pltpu.CompilerParams(vmem_limit_bytes=GRID_VMEM_BYTES),
         cost_estimate=LIGHT,
         name="cross_sum",
     )(*after, *x_cells, *y_cells)
@@ -486,7 +487,7 @@
         in_specs=[ANY] * len(unread) + cell_specs(shares, size, rows, width, first) + [term] * 3,
         out_specs=pl.BlockSpec((size, rows, full), lambda i: (first + i, 0, 0)),
         input_output_aliases={} if filled is None else {0: 0},
-        compiler_params=pltpu.CompilerParams(vmem_limit_bytes=VMEM_BYTES),
+        compiler_params=pltpu.CompilerParams(vmem_limit_bytes=GRID_VMEM_BYTES),
         cost_estimate=LIGHT,
         name="basis",
     )(*unread, *cells, *terms)
@@ -637,7 +638,7 @@
     _, x_near = place(meta, near, 1, 1, [])
     x_cells = x_near + [x_far]
 
-    gram_local = gram_blocks(x_cells, y_far[1:2])
+    gram_local = gram_blocks(x_cells, y_far[1:])
     gram = to_pieces(gram_local.reshape(pairs * TILE, TILE))
     settled, y_far = place(meta, y_far, 0, 2, [gram_local])
     gram = sum_pieces(gram, slabs, settled[:1], shares)

time: 300 us -> 270 us (0.900)
  waiting for transfers between devices: 132 us -> 105 us
  local copies, waits for them, and re-layouts: 40.1 us -> 30.9 us
  Pallas kernels: 63.9 us -> 70.4 us
    ppermute x27, waiting for transfers between devices: 123 us -> 97 us  [swap(): lax.ppermute(value, axis, [(i, i ^ mask) for i in range(lax.axis_size(axi...]
    unnamed x122 -> x96, local copies, waits for them, and re-layouts: 40.1 us -> 30.9 us
    pallas_call x2, Pallas kernels: 6.95 us -> 10.8 us  [basis(): pl.pallas_call(lambda *refs: basis_kernel(*refs[len(unread):]), grid=(ste...]
  transfers between devices with their start and end apart: 31 -> 31, of which waited for: 12 -> 13; matrix products, arithmetic and copies ran while one was open for 0% -> 0% of each run, Pallas kernels for 13% -> 16%
where the time goes in v11:
time: 270 us; the launch traced here: 269 us
  waiting for transfers between devices  105 us (39%)
  Pallas kernels  70.4 us (26%)
  starting transfers between devices  50.7 us (19%)
  local copies, waits for them, and re-layouts  30.9 us (11%)
  blocking collectives  10.5 us (4%)
    ppermute x27, waiting for transfers between devices, swap(): lax.ppermute(value, axis, [(i, i ^ mask) for i in range(lax.axis_size(axi...  97 us
    ppermute x27, starting transfers between devices, swap(): lax.ppermute(value, axis, [(i, i ^ mask) for i in range(lax.axis_size(axi...  33.3 us
    unnamed x96, local copies, waits for them, and re-layouts  30.9 us
    pallas_call x4, Pallas kernels, factor_call(): pl.pallas_call(lambda *refs: kernel(*refs[len(after):]), out_shape=out_sh...  19.7 us
    all_to_all x4, starting transfers between devices, to_pieces(): return lax.all_to_all(value, axis, split_axis=0, concat_axis=0, tiled=True)  17.5 us
    pallas_call x2, Pallas kernels, basis(): pl.pallas_call(lambda *refs: basis_kernel(*refs[len(unread):]), grid=(ste...  10.8 us
    all_gather x1, blocking collectives, body(): gram = lax.all_gather(gram, 'space', axis=0, tiled=True)  10.5 us
    pallas_call x4, Pallas kernels, settle(): pl.pallas_call(lambda *refs: settle_kernel(chips, capacity, with_ids, far...  9.47 us
  transfers between devices with their start and end apart: 31, of which 13 were waited for; matrix products, arithmetic and copies ran while one was open for 0% of the time, Pallas kernels for 16%

profile of v11, /device:TPU:0, one launch (start us, length us, event | category | flops | bytes accessed | tf_op | source)
XLA Modules:
  0.0 268.5 jit_solution(6488310707521019694)
XLA Ops:
  0.6 2.2 copy-done.16
  3.5 2.6 pack.3
  6.1 1.3 copy-done.5
  7.5 1.9 collective-permute-start.3
  9.4 2.7 %pack.2 = (bf16[132,32,128]{2,1,0:T(8,128)(2,1)S(1)}, bf16[132,32,128]{2,1,0:T(8,128)(2,1)S(1)}, bf16[128,32,128]{2,1,0:T(8,128)(2,1)S(1)}, bf16[128,32,128]{2,1,0:T(8,128)(2,1)S(1)}) custom-call(s32[128]{0:T(128)S(1)} %copy-done.33, bf16[128,4,32,128]{3,2,1,0:T(8,128)(2,1)S(1)} %bitcast.26), custom_call_target="tpu_custom_call" | custom-call | flops 1 | bytes 1 | tf_op jit(solution)/shard_map/pack/pallas_call | solution.py:78
  12.1 1.6 collective-permute-start.7
  13.8 2.3 collective-permute-done.7.refs_1_
  17.1 1.2 collective-permute-start.9
  18.3 1.5 collective-permute-start.10
  21.5 9.9 %collective-permute-done.8.refs_3_ = bf16[66,32,128]{2,1,0:T(8,128)(2,1)S(1)} collective-permute-done((bf16[66,32,128]{2,1,0:T(8,128)(2,1)S(1)}, bf16[66,32,128]{2,1,0:T(8,128)(2,1)S(1)}, u32[]{:S(2)}, u32[]{:S(2)}) %collective-permute-start.8) | collective-permute-done | bytes 540704 | tf_op jit(solution)/shard_map/ppermute | solution.py:581
  31.9 11.0 %collective-permute-done.10.refs_5_ = bf16[66,32,128]{2,1,0:T(8,128)(2,1)S(1)} collective-permute-done((bf16[66,32,128]{2,1,0:T(8,128)(2,1)S(1)}, bf16[66,32,128]{2,1,0:T(8,128)(2,1)S(1)}, u32[]{:S(2)}, u32[]{:S(2)}) %collective-permute-start.10) | collective-permute-done | bytes 540704 | tf_op jit(solution)/shard_map/ppermute | solution.py:581
  43.0 2.8 %settle.4 = (bf16[4,64,32,128]{3,2,1,0:T(8,128)(2,1)S(1)}, s32[8,128]{1,0:T(8,128)S(1)}) custom-call(bf16[256,32,128]{2,1,0:T(8,128)(2,1)S(1)} %collective-permute-done.3.refs_0_, bf16[64,32,128]{2,1,0:T(8,128)(2,1)S(1)} %get-tuple-element.49.refs_1_, bf16[66,32,128]{2,1,0:T(8,128)(2,1)S(1)} %get-tuple-element.52.refs_2_, ...), custom_call_target="tpu_custom_call" | custom-call | flops 1 | bytes 1 | tf_op jit(solution)/shard_map/settle/pallas_call | solution.py:176
  45.8 1.3 copy-done.22
  47.2 5.2 %all-to-all-start = ((bf16[4,64,32,128]{3,2,1,0:T(8,128)(2,1)}), bf16[4,64,32,128]{3,2,1,0:T(8,128)(2,1)}, u32[]{:S(2)}, u32[]{:S(2)}) async-start(bf16[4,64,32,128]{3,2,1,0:T(8,128)(2,1)} %copy-done.22), calls=%async_computation | async-start | bytes 4194304 | tf_op jit(solution)/shard_map/all_to_all | solution.py:607
  52.4 1.7 collective-permute-start.1
  54.4 1.5 collective-permute-start.11
  55.9 11.6 %collective-permute-done.1.refs_0_.refs_2_ = bf16[64,32,128]{2,1,0:T(8,128)(2,1)S(1)} collective-permute-done((bf16[64,32,128]{2,1,0:T(8,128)(2,1)}, bf16[64,32,128]{2,1,0:T(8,128)(2,1)S(1)}, u32[]{:S(2)}, u32[]{:S(2)}) %collective-permute-start.1) | collective-permute-done | bytes 524320 | tf_op jit(solution)/shard_map/ppermute | solution.py:581
  67.5 10.5 %collective-permute-done.2.refs_1_.refs_3_ = bf16[64,32,128]{2,1,0:T(8,128)(2,1)S(1)} collective-permute-done((bf16[64,32,128]{2,1,0:T(8,128)(2,1)}, bf16[64,32,128]{2,1,0:T(8,128)(2,1)S(1)}, u32[]{:S(2)}, u32[]{:S(2)}) %collective-permute-start.2) | collective-permute-done | bytes 524320 | tf_op jit(solution)/shard_map/ppermute | solution.py:581
  78.0 2.1 settle.5
  80.9 1.7 collective-permute-start.12
  84.2 1.5 collective-permute-start.4
  85.7 1.4 collective-permute-start.6
  87.1 16.0 %collective-permute-done.12.refs_4_.refs_2_.refs_3_ = bf16[64,32,128]{2,1,0:T(8,128)(2,1)S(1)} collective-permute-done((bf16[64,32,128]{2,1,0:T(8,128)(2,1)S(1)}, bf16[64,32,128]{2,1,0:T(8,128)(2,1)S(1)}, u32[]{:S(2)}, u32[]{:S(2)}) %collective-permute-start.12) | collective-permute-done | bytes 524320 | tf_op jit(solution)/shard_map/ppermute | solution.py:581
  103.9 3.7 %collective-permute-done.6.refs_2_.refs_5_ = bf16[64,32,128]{2,1,0:T(8,128)(2,1)} collective-permute-done((bf16[64,32,128]{2,1,0:T(8,128)(2,1)S(1)}, bf16[64,32,128]{2,1,0:T(8,128)(2,1)}, u32[]{:S(2)}, u32[]{:S(2)}) %collective-permute-start.6) | collective-permute-done | bytes 524320 | tf_op jit(solution)/shard_map/ppermute | solution.py:581
  107.5 4.8 %gram_blocks.1.refs_0_ = f32[10,128,128]{2,1,0:T(8,128)} custom-call(bf16[64,32,128]{2,1,0:T(8,128)(2,1)} %copy-done.13, bf16[64,32,128]{2,1,0:T(8,128)(2,1)} %copy-done.10, bf16[64,32,128]{2,1,0:T(8,128)(2,1)} %collective-permute-done.6.refs_2_.refs_5_, bf16[64,32,128]{2,1,0:T(8,128)(2,1)} %copy-done.8, bf16[64,32,128]{2,1,0:T(8,128)(2,1)} %copy-done.37, ...), custom_call_target="tpu_custom_call" | custom-call | flops 1 | bytes 1 | tf_op jit(solution)/shard_map/gram_blocks/pallas_call | solution.py:241
  112.4 4.2 %all-to-all-start.1 = ((f32[8,160,128]{2,1,0:T(8,128)}), f32[8,160,128]{2,1,0:T(8,128)}, u32[]{:S(2)}, u32[]{:S(2)}) async-start(f32[8,160,128]{2,1,0:T(8,128)} %bitcast.24), calls=%async_computation.1 | async-start | bytes 1310720 | tf_op jit(solution)/shard_map/all_to_all | solution.py:607
  116.6 1.6 copy-done.7
  120.3 1.1 merge.7
  121.4 1.9 collective-permute-start.16
  123.3 1.5 collective-permute-start.15
  124.9 2.5 settle.6
  128.9 1.9 sum_pieces.3
  130.7 4.1 %all-to-all-start.2 = ((f32[4,160,128]{2,1,0:T(8,128)}), f32[4,160,128]{2,1,0:T(8,128)}, u32[]{:S(2)}, u32[]{:S(2)}) async-start(f32[4,160,128]{2,1,0:T(8,128)} %bitcast.35), calls=%async_computation.2 | async-start | bytes 655360 | tf_op jit(solution)/shard_map/all_to_all | solution.py:607
  134.8 3.8 %collective-permute-start.14 = (bf16[64,16,128]{2,1,0:T(8,128)(2,1)S(1)}, bf16[64,16,128]{2,1,0:T(8,128)(2,1)S(1)}, u32[]{:S(2)}, u32[]{:S(2)}) collective-permute-start(bf16[64,16,128]{2,1,0:T(8,128)(2,1)S(1)} %get-tuple-element.63), channel_id=1, source_target_pairs={{0,3},{1,2},{2,1},{3,0},{4,7},{5,6},{6,5},{7,4},{8,11},{9,10},{10,... | collective-permute-start | bytes 786440 | tf_op jit(solution)/shard_map/ppermute | solution.py:581
  138.6 12.8 %collective-permute-done.14.refs_1_.refs_8_ = bf16[64,16,128]{2,1,0:T(8,128)(2,1)S(1)} collective-permute-done((bf16[64,16,128]{2,1,0:T(8,128)(2,1)S(1)}, bf16[64,16,128]{2,1,0:T(8,128)(2,1)S(1)}, u32[]{:S(2)}, u32[]{:S(2)}) %collective-permute-start.14) | collective-permute-done | bytes 262176 | tf_op jit(solution)/shard_map/ppermute | solution.py:581
  151.4 16.3 %collective-permute-done.13.refs_0_.refs_6_ = bf16[64,16,128]{2,1,0:T(8,128)(2,1)} collective-permute-done((bf16[64,16,128]{2,1,0:T(8,128)(2,1)}, bf16[64,16,128]{2,1,0:T(8,128)(2,1)}, u32[]{:S(2)}, u32[]{:S(2)}) %collective-permute-start.13) | collective-permute-done | bytes 262176 | tf_op jit(solution)/shard_map/ppermute | solution.py:581
  167.7 1.6 sum_pieces.4.refs_0_
  169.3 1.0 copy-done.25
  172.3 2.1 settle.7
  174.4 2.0 collective-permute-start.19
  176.4 2.4 collective-permute-start.20
  178.8 10.5 %all_gather.3 = f32[1280,128]{1,0:T(8,128)S(1)} all-gather(f32[160,128]{1,0:T(8,128)S(1)} %copy-done.29), channel_id=1, replica_groups=mesh['space'=8,'snap'=4] {'space'}, dimensions={0}, use_global_device_ids=true | all-gather | bytes 737280 | tf_op jit(solution)/shard_map/all_gather | solution.py:648
  189.3 4.9 %factor.4.refs_0_ = f32[4,8,128,128]{3,2,1,0:T(8,128)S(1)} custom-call(bf16[64,32,128]{2,1,0:T(8,128)(2,1)S(1)} %get-tuple-element.68.refs_0_.refs_4_, f32[10,128,128]{2,1,0:T(8,128)S(1)} %bitcast.27), custom_call_target="tpu_custom_call" | custom-call | flops 1 | bytes 1 | tf_op jit(solution)/shard_map/factor/pallas_call | solution.py:430
  194.2 4.8 %factor.5.refs_0_.refs_1_ = f32[4,8,128,128]{3,2,1,0:T(8,128)S(1)} custom-call(f32[4,8,128,128]{3,2,1,0:T(8,128)S(1)} %factor.4.refs_0_), custom_call_target="tpu_custom_call", output_to_operand_aliasing={{}: (0, {})} | custom-call | flops 1 | bytes 1 | tf_op jit(solution)/shard_map/factor/pallas_call | solution.py:430
  199.1 1.3 copy-done
  202.0 5.2 %cross_sum.1.refs_0_ = f32[512,512]{1,0:T(8,128)} custom-call(f32[4,8,128,128]{3,2,1,0:T(8,128)} %copy-done, bf16[64,32,128]{2,1,0:T(8,128)(2,1)} %copy-done.8, bf16[64,32,128]{2,1,0:T(8,128)(2,1)} %copy-done.37, bf16[4,64,32,128]{3,2,1,0:T(8,128)(2,1)} %all-to-all-done.refs_5_.refs_3_.refs_4_, bf16[64,32,128]{2,1,0:T(8,128)(2,1)} %copy-done.18, ...), custom_call_target="tpu_custom_call" | custom-call | flops 1 | bytes 1 | tf_op jit(solution)/shard_map/cross_sum/pallas_call | solution.py:294
  207.2 3.9 %all-to-all-start.3 = ((f32[8,64,512]{2,1,0:T(8,128)}), f32[8,64,512]{2,1,0:T(8,128)S(1)}, u32[]{:S(2)}, u32[]{:S(2)}) async-start(f32[8,64,512]{2,1,0:T(8,128)} %bitcast.21), calls=%async_computation.3 | async-start | bytes 2097152 | tf_op jit(solution)/shard_map/all_to_all | solution.py:607
  211.1 1.3 copy-done.4
  212.4 4.6 %factor.6.refs_0_.refs_1_ = f32[4,8,128,128]{3,2,1,0:T(8,128)S(1)} custom-call(f32[512,512]{1,0:T(8,128)S(1)} %copy-done.4, f32[4,8,128,128]{3,2,1,0:T(8,128)S(1)} %copy-done.1), custom_call_target="tpu_custom_call", output_to_operand_aliasing={{}: (1, {})} | custom-call | flops 1 | bytes 1 | tf_op jit(solution)/shard_map/factor/pallas_call | solution.py:430
  217.0 1.3 copy-done.2
  218.3 8.0 %all-to-all-done.3 = f32[8,64,512]{2,1,0:T(8,128)S(1)} async-done(((f32[8,64,512]{2,1,0:T(8,128)}), f32[8,64,512]{2,1,0:T(8,128)S(1)}, u32[]{:S(2)}, u32[]{:S(2)}) %all-to-all-start.3) | async-done | bytes 1048608 | tf_op jit(solution)/shard_map/all_to_all | solution.py:607
  227.2 2.0 sum_pieces.5.refs_0_.refs_1_
  230.3 5.4 %factor.7 = (f32[512,512]{1,0:T(8,128)}, f32[512,512]{1,0:T(8,128)S(1)}, bf16[512,512]{1,0:T(8,128)(2,1)S(1)}, bf16[512,512]{1,0:T(8,128)(2,1)S(1)}, bf16[512,512]{1,0:T(8,128)(2,1)S(1)}) custom-call(f32[64,512]{1,0:T(8,128)S(1)} %copy-done.28, f32[4,8,128,128]{3,2,1,0:T(8,128)S(1)} %copy-done.3), custom_call_target="tpu_custom_call" | custom-call | flops 1 | bytes 1 | tf_op jit(solution)/shard_map/factor/pallas_call | solution.py:430
  238.8 1.6 add.2.refs_0_.refs_1_
  240.4 1.8 collective-permute-start.22
  242.2 5.4 %basis.2.refs_0_ = f32[64,32,512]{2,1,0:T(8,128)} custom-call(f32[64,512]{1,0:T(8,128)} %add.2.refs_0_.refs_1_, bf16[64,32,128]{2,1,0:T(8,128)(2,1)} %copy-done.8, bf16[64,32,128]{2,1,0:T(8,128)(2,1)} %copy-done.37, bf16[4,64,32,128]{3,2,1,0:T(8,128)(2,1)} %all-to-all-done.refs_5_.refs_3_.refs_4_, bf16[512,512]{1,0:T(8,128)(2,1)} %copy-done.19, ...), custom_call_target="tpu_custom_call" | custom-call | flops 1 | bytes 1 | tf_op jit(solution)/shard_map/basis/pallas_call | solution.py:483
  248.5 1.6 add.3.refs_1_
  250.2 2.0 collective-permute-start.25
  252.2 1.6 collective-permute-start.24
  253.8 5.4 %basis.3.refs_0_ = f32[64,32,512]{2,1,0:T(8,128)} custom-call(f32[64,32,512]{2,1,0:T(8,128)} %basis.2.refs_0_, f32[64,512]{1,0:T(8,128)} %add.3.refs_1_, bf16[64,32,128]{2,1,0:T(8,128)(2,1)} %copy-done.8, bf16[64,32,128]{2,1,0:T(8,128)(2,1)} %copy-done.37, ...), custom_call_target="tpu_custom_call", output_to_operand_aliasing={{}: (0, {})} | custom-call | flops 1 | bytes 1 | tf_op jit(solution)/shard_map/basis/pallas_call | solution.py:483
  260.6 1.9 join.1.refs_1_
  262.5 2.1 collective-permute-done.26.refs_2_
  264.6 1.0 copy-done.23
  265.7 2.9 %project.1 = f32[512,512]{1,0:T(8,128)} custom-call(f32[512,512]{1,0:T(8,128)S(1)} %get-tuple-element.76.refs_0_, f32[256,512]{1,0:T(8,128)S(1)} %copy-done.23, f32[256,512]{1,0:T(8,128)S(1)} %collective-permute-done.26.refs_2_), custom_call_target="tpu_custom_call" | custom-call | tf_op jit(solution)/shard_map/project/pallas_call | solution.py:569
  (120 shorter events, 22.2 us)
Async XLA Ops:
  0.6 2.2 copy-start.16
  3.5 5.9 %copy-start.17 = (bf16[128,128,128]{2,1,0:T(8,128)(2,1)S(1)}, bf16[128,128,128]{2,1,0:T(8,128)(2,1)}, u32[]{:S(2)}) copy-start(bf16[128,128,128]{2,1,0:T(8,128)(2,1)} %param.3) | copy-start | bytes 12582916
  6.1 1.3 copy-start.5
  7.5 35.5 %collective-permute-start.3 = (bf16[256,32,128]{2,1,0:T(8,128)(2,1)S(1)}, bf16[256,32,128]{2,1,0:T(8,128)(2,1)S(1)}, u32[]{:S(2)}, u32[]{:S(2)}) collective-permute-start(bf16[256,32,128]{2,1,0:T(8,128)(2,1)S(1)} %get-tuple-element.45), channel_id=1, source_target_pairs={{0,4},{4,0},{8,12},{12,8},{16,20},{20,16},{24,28},{28,24},{1,5},{5... | collective-permute-start | bytes 6291464 | tf_op jit(solution)/shard_map/ppermute | solution.py:581
  12.1 4.0 %collective-permute-start.7 = (bf16[132,32,128]{2,1,0:T(8,128)(2,1)S(1)}, bf16[132,32,128]{2,1,0:T(8,128)(2,1)S(1)}, u32[]{:S(2)}, u32[]{:S(2)}) collective-permute-start(bf16[132,32,128]{2,1,0:T(8,128)(2,1)S(1)} %get-tuple-element.51), channel_id=1, source_target_pairs={{0,4},{4,0},{8,12},{12,8},{16,20},{20,16},{24,28},{28,24},{1,5},{5... | collective-permute-start | bytes 3244040 | tf_op jit(solution)/shard_map/ppermute | solution.py:581
  13.8 6.0 %collective-permute-start = (bf16[128,32,128]{2,1,0:T(8,128)(2,1)S(1)}, bf16[128,32,128]{2,1,0:T(8,128)(2,1)S(1)}, u32[]{:S(2)}, u32[]{:S(2)}) collective-permute-start(bf16[128,32,128]{2,1,0:T(8,128)(2,1)S(1)} %get-tuple-element.41), channel_id=1, source_target_pairs={{0,4},{4,0},{8,12},{12,8},{16,20},{20,16},{24,28},{28,24},{1,5},{5... | collective-permute-start | bytes 3145736 | tf_op jit(solution)/shard_map/ppermute | solution.py:581
  16.2 15.2 %collective-permute-start.8 = (bf16[66,32,128]{2,1,0:T(8,128)(2,1)S(1)}, bf16[66,32,128]{2,1,0:T(8,128)(2,1)S(1)}, u32[]{:S(2)}, u32[]{:S(2)}) collective-permute-start(bf16[66,32,128]{2,1,0:T(8,128)(2,1)S(1)} %get-tuple-element.53), channel_id=1, source_target_pairs={{0,8},{4,12},{8,0},{12,4},{16,24},{20,28},{24,16},{28,20},{1,9},{5... | collective-permute-start | bytes 1622024 | tf_op jit(solution)/shard_map/ppermute | solution.py:581
  17.1 14.8 %collective-permute-start.9 = (bf16[66,32,128]{2,1,0:T(8,128)(2,1)S(1)}, bf16[66,32,128]{2,1,0:T(8,128)(2,1)S(1)}, u32[]{:S(2)}, u32[]{:S(2)}) collective-permute-start(bf16[66,32,128]{2,1,0:T(8,128)(2,1)S(1)} %get-tuple-element.54), channel_id=1, source_target_pairs={{0,16},{4,20},{8,24},{12,28},{16,0},{20,4},{24,8},{28,12},{1,17},{... | collective-permute-start | bytes 1622024 | tf_op jit(solution)/shard_map/ppermute | solution.py:581
  18.3 24.7 %collective-permute-start.10 = (bf16[66,32,128]{2,1,0:T(8,128)(2,1)S(1)}, bf16[66,32,128]{2,1,0:T(8,128)(2,1)S(1)}, u32[]{:S(2)}, u32[]{:S(2)}) collective-permute-start(bf16[66,32,128]{2,1,0:T(8,128)(2,1)S(1)} %get-tuple-element.55), channel_id=1, source_target_pairs={{0,24},{4,28},{8,16},{12,20},{16,8},{20,12},{24,0},{28,4},{1,25},{... | collective-permute-start | bytes 1622024 | tf_op jit(solution)/shard_map/ppermute | solution.py:581
  45.8 1.4 copy-start.22
  47.2 60.4 %all-to-all-start = ((bf16[4,64,32,128]{3,2,1,0:T(8,128)(2,1)}), bf16[4,64,32,128]{3,2,1,0:T(8,128)(2,1)}, u32[]{:S(2)}, u32[]{:S(2)}) async-start(bf16[4,64,32,128]{3,2,1,0:T(8,128)(2,1)} %copy-done.22), calls=%async_computation | async-start | bytes 4194304 | tf_op jit(solution)/shard_map/all_to_all | solution.py:607
  52.4 30.2 %copy-start.6 = (bf16[256,32,128]{2,1,0:T(8,128)(2,1)S(1)}, bf16[256,32,128]{2,1,0:T(8,128)(2,1)}, u32[]{:S(2)}) copy-start(bf16[256,32,128]{2,1,0:T(8,128)(2,1)} %copy-done.5) | copy-start | bytes 6291460
  52.4 15.1 %collective-permute-start.1 = (bf16[64,32,128]{2,1,0:T(8,128)(2,1)}, bf16[64,32,128]{2,1,0:T(8,128)(2,1)S(1)}, u32[]{:S(2)}, u32[]{:S(2)}) collective-permute-start(bf16[64,32,128]{2,1,0:T(8,128)(2,1)} %copy-done.35), channel_id=1, source_target_pairs={{0,8},{4,12},{8,0},{12,4},{16,24},{20,28},{24,16},{28,20},{1,9},{5... | collective-permute-start | bytes 1572872 | tf_op jit(solution)/shard_map/ppermute | solution.py:581
  54.1 24.0 %collective-permute-start.2 = (bf16[64,32,128]{2,1,0:T(8,128)(2,1)}, bf16[64,32,128]{2,1,0:T(8,128)(2,1)S(1)}, u32[]{:S(2)}, u32[]{:S(2)}) collective-permute-start(bf16[64,32,128]{2,1,0:T(8,128)(2,1)} %copy-done.34), channel_id=1, source_target_pairs={{0,16},{4,20},{8,24},{12,28},{16,0},{20,4},{24,8},{28,12},{1,17},{... | collective-permute-start | bytes 1572872 | tf_op jit(solution)/shard_map/ppermute | solution.py:581
  54.4 23.7 %collective-permute-start.11 = (bf16[64,32,128]{2,1,0:T(8,128)(2,1)S(1)}, bf16[64,32,128]{2,1,0:T(8,128)(2,1)S(1)}, u32[]{:S(2)}, u32[]{:S(2)}) collective-permute-start(bf16[64,32,128]{2,1,0:T(8,128)(2,1)S(1)} %get-tuple-element.57), channel_id=1, source_target_pairs={{0,24},{4,28},{8,16},{12,20},{16,8},{20,12},{24,0},{28,4},{1,25},{... | collective-permute-start | bytes 1572872 | tf_op jit(solution)/shard_map/ppermute | solution.py:581
  80.1 0.8 copy-start.8
  80.9 22.2 %collective-permute-start.12 = (bf16[64,32,128]{2,1,0:T(8,128)(2,1)S(1)}, bf16[64,32,128]{2,1,0:T(8,128)(2,1)S(1)}, u32[]{:S(2)}, u32[]{:S(2)}) collective-permute-start(bf16[64,32,128]{2,1,0:T(8,128)(2,1)S(1)} %get-tuple-element.59), channel_id=1, source_target_pairs={{0,1},{1,0},{2,3},{3,2},{4,5},{5,4},{6,7},{7,6},{8,9},{9,8},{10,11... | collective-permute-start | bytes 1572872 | tf_op jit(solution)/shard_map/ppermute | solution.py:581
  83.6 19.5 %collective-permute-start.5 = (bf16[64,32,128]{2,1,0:T(8,128)(2,1)S(1)}, bf16[64,32,128]{2,1,0:T(8,128)(2,1)S(1)}, u32[]{:S(2)}, u32[]{:S(2)}) collective-permute-start(bf16[64,32,128]{2,1,0:T(8,128)(2,1)S(1)} %bitcast.33), channel_id=1, source_target_pairs={{0,16},{4,20},{8,24},{12,28},{16,0},{20,4},{24,8},{28,12},{1,17},{... | collective-permute-start | bytes 1572872 | tf_op jit(solution)/shard_map/ppermute | solution.py:581
  84.2 18.9 %collective-permute-start.4 = (bf16[64,32,128]{2,1,0:T(8,128)(2,1)S(1)}, bf16[64,32,128]{2,1,0:T(8,128)(2,1)S(1)}, u32[]{:S(2)}, u32[]{:S(2)}) collective-permute-start(bf16[64,32,128]{2,1,0:T(8,128)(2,1)S(1)} %bitcast.32), channel_id=1, source_target_pairs={{0,8},{4,12},{8,0},{12,4},{16,24},{20,28},{24,16},{28,20},{1,9},{5... | collective-permute-start | bytes 1572872 | tf_op jit(solution)/shard_map/ppermute | solution.py:581
  85.7 21.9 %collective-permute-start.6 = (bf16[64,32,128]{2,1,0:T(8,128)(2,1)S(1)}, bf16[64,32,128]{2,1,0:T(8,128)(2,1)}, u32[]{:S(2)}, u32[]{:S(2)}) collective-permute-start(bf16[64,32,128]{2,1,0:T(8,128)(2,1)S(1)} %bitcast.31), channel_id=1, source_target_pairs={{0,24},{4,28},{8,16},{12,20},{16,8},{20,12},{24,0},{28,4},{1,25},{... | collective-permute-start | bytes 1572872 | tf_op jit(solution)/shard_map/ppermute | solution.py:581
  103.1 0.8 copy-start.37
  103.1 4.5 %copy-start.10 = (bf16[64,32,128]{2,1,0:T(8,128)(2,1)}, bf16[64,32,128]{2,1,0:T(8,128)(2,1)S(1)}, u32[]{:S(2)}) copy-start(bf16[64,32,128]{2,1,0:T(8,128)(2,1)S(1)} %collective-permute-done.5.refs_1_.refs_4_) | copy-start | bytes 1572868
  103.9 3.7 %copy-start.13 = (bf16[64,32,128]{2,1,0:T(8,128)(2,1)}, bf16[64,32,128]{2,1,0:T(8,128)(2,1)S(1)}, u32[]{:S(2)}) copy-start(bf16[64,32,128]{2,1,0:T(8,128)(2,1)S(1)} %collective-permute-done.4.refs_0_.refs_3_) | copy-start | bytes 1572868
  112.4 16.5 %all-to-all-start.1 = ((f32[8,160,128]{2,1,0:T(8,128)}), f32[8,160,128]{2,1,0:T(8,128)}, u32[]{:S(2)}, u32[]{:S(2)}) async-start(f32[8,160,128]{2,1,0:T(8,128)} %bitcast.24), calls=%async_computation.1 | async-start | bytes 1310720 | tf_op jit(solution)/shard_map/all_to_all | solution.py:607
  116.6 1.6 copy-start.7
  118.2 1.0 copy-start.11
  119.2 1.0 copy-start.14
  120.3 4.6 %copy-start.9 = (f32[10,128,128]{2,1,0:T(8,128)S(1)}, f32[10,128,128]{2,1,0:T(8,128)}, u32[]{:S(2)}) copy-start(f32[10,128,128]{2,1,0:T(8,128)} %gram_blocks.1.refs_0_) | copy-start | bytes 1966084
  120.3 4.6 %copy-start.12 = (bf16[64,32,128]{2,1,0:T(8,128)(2,1)S(1)}, bf16[64,32,128]{2,1,0:T(8,128)(2,1)}, u32[]{:S(2)}) copy-start(bf16[64,32,128]{2,1,0:T(8,128)(2,1)} %copy-done.10) | copy-start | bytes 1572868
  120.3 4.6 %copy-start.15 = (bf16[64,32,128]{2,1,0:T(8,128)(2,1)S(1)}, bf16[64,32,128]{2,1,0:T(8,128)(2,1)}, u32[]{:S(2)}) copy-start(bf16[64,32,128]{2,1,0:T(8,128)(2,1)} %copy-done.13) | copy-start | bytes 1572868
  120.3 4.6 %copy-start.31 = (bf16[2,16,2,32,128]{4,3,2,1,0:T(8,128)(2,1)S(1)}, bf16[2,16,2,32,128]{4,3,2,1,0:T(8,128)(2,1)}, u32[]{:S(2)}) copy-start(bf16[2,16,2,32,128]{4,3,2,1,0:T(8,128)(2,1)} %copy-done.30) | copy-start | bytes 1572868
  121.4 17.2 %collective-permute-start.16 = (bf16[64,32,128]{2,1,0:T(8,128)(2,1)}, bf16[64,32,128]{2,1,0:T(8,128)(2,1)S(1)}, u32[]{:S(2)}, u32[]{:S(2)}) collective-permute-start(bf16[64,32,128]{2,1,0:T(8,128)(2,1)} %bitcast.9), channel_id=1, source_target_pairs={{0,16},{4,20},{8,24},{12,28},{16,0},{20,4},{24,8},{28,12},{1,17},{... | collective-permute-start | bytes 1572872 | tf_op jit(solution)/shard_map/ppermute | solution.py:581
  123.3 15.3 %collective-permute-start.15 = (bf16[64,32,128]{2,1,0:T(8,128)(2,1)}, bf16[64,32,128]{2,1,0:T(8,128)(2,1)S(1)}, u32[]{:S(2)}, u32[]{:S(2)}) collective-permute-start(bf16[64,32,128]{2,1,0:T(8,128)(2,1)} %bitcast.8), channel_id=1, source_target_pairs={{0,8},{4,12},{8,0},{12,4},{16,24},{20,28},{24,16},{28,20},{1,9},{5... | collective-permute-start | bytes 1572872 | tf_op jit(solution)/shard_map/ppermute | solution.py:581
  124.8 44.5 %collective-permute-start.17 = (bf16[64,32,128]{2,1,0:T(8,128)(2,1)S(1)}, bf16[64,32,128]{2,1,0:T(8,128)(2,1)S(1)}, u32[]{:S(2)}, u32[]{:S(2)}) collective-permute-start(bf16[64,32,128]{2,1,0:T(8,128)(2,1)S(1)} %bitcast.30), channel_id=1, source_target_pairs={{0,24},{4,28},{8,16},{12,20},{16,8},{20,12},{24,0},{28,4},{1,25},{... | collective-permute-start | bytes 1572872 | tf_op jit(solution)/shard_map/ppermute | solution.py:581
  130.7 36.9 %all-to-all-start.2 = ((f32[4,160,128]{2,1,0:T(8,128)}), f32[4,160,128]{2,1,0:T(8,128)}, u32[]{:S(2)}, u32[]{:S(2)}) async-start(f32[4,160,128]{2,1,0:T(8,128)} %bitcast.35), calls=%async_computation.2 | async-start | bytes 655360 | tf_op jit(solution)/shard_map/all_to_all | solution.py:607
  134.8 16.6 %collective-permute-start.14 = (bf16[64,16,128]{2,1,0:T(8,128)(2,1)S(1)}, bf16[64,16,128]{2,1,0:T(8,128)(2,1)S(1)}, u32[]{:S(2)}, u32[]{:S(2)}) collective-permute-start(bf16[64,16,128]{2,1,0:T(8,128)(2,1)S(1)} %get-tuple-element.63), channel_id=1, source_target_pairs={{0,3},{1,2},{2,1},{3,0},{4,7},{5,6},{6,5},{7,4},{8,11},{9,10},{10,... | collective-permute-start | bytes 786440 | tf_op jit(solution)/shard_map/ppermute | solution.py:581
  138.6 29.0 %collective-permute-start.13 = (bf16[64,16,128]{2,1,0:T(8,128)(2,1)}, bf16[64,16,128]{2,1,0:T(8,128)(2,1)}, u32[]{:S(2)}, u32[]{:S(2)}) collective-permute-start(bf16[64,16,128]{2,1,0:T(8,128)(2,1)} %copy-done.32), channel_id=1, source_target_pairs={{0,2},{1,3},{2,0},{3,1},{4,6},{5,7},{6,4},{7,5},{8,10},{9,11},{10,... | collective-permute-start | bytes 786440 | tf_op jit(solution)/shard_map/ppermute | solution.py:581
  138.6 29.0 %copy-start.24 = (bf16[64,32,128]{2,1,0:T(8,128)(2,1)}, bf16[64,32,128]{2,1,0:T(8,128)(2,1)S(1)}, u32[]{:S(2)}) copy-start(bf16[64,32,128]{2,1,0:T(8,128)(2,1)S(1)} %collective-permute-done.16.refs_3_.refs_4_) | copy-start | bytes 1572868
  138.6 29.0 %copy-start.26 = (bf16[64,32,128]{2,1,0:T(8,128)(2,1)}, bf16[64,32,128]{2,1,0:T(8,128)(2,1)S(1)}, u32[]{:S(2)}) copy-start(bf16[64,32,128]{2,1,0:T(8,128)(2,1)S(1)} %collective-permute-done.15.refs_2_.refs_3_) | copy-start | bytes 1572868
  151.4 16.3 %copy-start.39 = (bf16[64,16,128]{2,1,0:T(8,128)(2,1)}, bf16[64,16,128]{2,1,0:T(8,128)(2,1)S(1)}, u32[]{:S(2)}) copy-start(bf16[64,16,128]{2,1,0:T(8,128)(2,1)S(1)} %collective-permute-done.14.refs_1_.refs_8_) | copy-start | bytes 786436
  169.3 1.0 copy-start.25
  170.3 1.0 copy-start.27
  171.4 0.9 copy-start.29
  174.3 24.7 %copy-start.18 = (bf16[64,32,128]{2,1,0:T(8,128)(2,1)}, bf16[64,32,128]{2,1,0:T(8,128)(2,1)S(1)}, u32[]{:S(2)}) copy-start(bf16[64,32,128]{2,1,0:T(8,128)(2,1)S(1)} %get-tuple-element.68.refs_0_.refs_4_) | copy-start | bytes 1572868
  174.4 26.1 %collective-permute-start.18 = (bf16[64,32,128]{2,1,0:T(8,128)(2,1)S(1)}, bf16[64,32,128]{2,1,0:T(8,128)(2,1)S(1)}, u32[]{:S(2)}, u32[]{:S(2)}) collective-permute-start(bf16[64,32,128]{2,1,0:T(8,128)(2,1)S(1)} %get-tuple-element.69), channel_id=1, source_target_pairs={{0,1},{1,0},{2,3},{3,2},{4,5},{5,4},{6,7},{7,6},{8,9},{9,8},{10,11... | collective-permute-start | bytes 1572872 | tf_op jit(solution)/shard_map/ppermute | solution.py:581
  174.4 26.0 %collective-permute-start.19 = (bf16[64,16,128]{2,1,0:T(8,128)(2,1)}, bf16[64,16,128]{2,1,0:T(8,128)(2,1)S(1)}, u32[]{:S(2)}, u32[]{:S(2)}) collective-permute-start(bf16[64,16,128]{2,1,0:T(8,128)(2,1)} %copy-done.36), channel_id=1, source_target_pairs={{0,2},{1,3},{2,0},{3,1},{4,6},{5,7},{6,4},{7,5},{8,10},{9,11},{10,... | collective-permute-start | bytes 786440 | tf_op jit(solution)/shard_map/ppermute | solution.py:581
  176.4 24.0 %collective-permute-start.20 = (bf16[64,16,128]{2,1,0:T(8,128)(2,1)S(1)}, bf16[64,16,128]{2,1,0:T(8,128)(2,1)S(1)}, u32[]{:S(2)}, u32[]{:S(2)}) collective-permute-start(bf16[64,16,128]{2,1,0:T(8,128)(2,1)S(1)} %get-tuple-element.71), channel_id=1, source_target_pairs={{0,3},{1,2},{2,1},{3,0},{4,7},{5,6},{6,5},{7,4},{8,11},{9,10},{10,... | collective-permute-start | bytes 786440 | tf_op jit(solution)/shard_map/ppermute | solution.py:581
  199.1 1.3 copy-start
  201.2 0.8 copy-start.40
  207.2 3.9 %copy-start.1 = (f32[4,8,128,128]{3,2,1,0:T(8,128)S(1)}, f32[4,8,128,128]{3,2,1,0:T(8,128)}, u32[]{:S(2)}) copy-start(f32[4,8,128,128]{3,2,1,0:T(8,128)} %copy-done) | copy-start | bytes 6291460
  207.2 19.0 %all-to-all-start.3 = ((f32[8,64,512]{2,1,0:T(8,128)}), f32[8,64,512]{2,1,0:T(8,128)S(1)}, u32[]{:S(2)}, u32[]{:S(2)}) async-start(f32[8,64,512]{2,1,0:T(8,128)} %bitcast.21), calls=%async_computation.3 | async-start | bytes 2097152 | tf_op jit(solution)/shard_map/all_to_all | solution.py:607
  211.1 1.3 copy-start.4
  217.0 1.3 copy-start.2
  226.2 1.0 copy-start.38
  226.2 3.2 %copy-start.3 = (f32[4,8,128,128]{3,2,1,0:T(8,128)S(1)}, f32[4,8,128,128]{3,2,1,0:T(8,128)}, u32[]{:S(2)}) copy-start(f32[4,8,128,128]{3,2,1,0:T(8,128)} %copy-done.2) | copy-start | bytes 6291460
  229.2 9.0 %collective-permute-start.21 = (f32[64,512]{1,0:T(8,128)}, f32[64,512]{1,0:T(8,128)S(1)}, u32[]{:S(2)}, u32[]{:S(2)}) collective-permute-start(f32[64,512]{1,0:T(8,128)} %sum_pieces.5.refs_0_.refs_1_), channel_id=1, source_target_pairs={{0,1},{1,0},{2,3},{3,2},{4,5},{5,4},{6,7},{7,6},{8,9},{9,8},{10,11... | collective-permute-start | bytes 393224 | tf_op jit(solution)/shard_map/ppermute | solution.py:581
  229.4 0.9 copy-start.28
  236.5 0.8 copy-start.20
  240.4 7.5 %collective-permute-start.22 = (f32[64,512]{1,0:T(8,128)}, f32[64,512]{1,0:T(8,128)S(1)}, u32[]{:S(2)}, u32[]{:S(2)}) collective-permute-start(f32[64,512]{1,0:T(8,128)} %add.2.refs_0_.refs_1_), channel_id=1, source_target_pairs={{0,2},{1,3},{2,0},{3,1},{4,6},{5,7},{6,4},{7,5},{8,10},{9,11},{10,... | collective-permute-start | bytes 393224 | tf_op jit(solution)/shard_map/ppermute | solution.py:581
  250.2 9.0 %collective-permute-start.25 = (f32[64,512]{1,0:T(8,128)}, f32[64,512]{1,0:T(8,128)S(1)}, u32[]{:S(2)}, u32[]{:S(2)}) collective-permute-start(f32[64,512]{1,0:T(8,128)} %add.3.refs_1_), channel_id=1, source_target_pairs={{0,24},{4,28},{8,16},{12,20},{16,8},{20,12},{24,0},{28,4},{1,25},{... | collective-permute-start | bytes 393224 | tf_op jit(solution)/shard_map/ppermute | solution.py:581
  252.2 7.0 %collective-permute-start.24 = (f32[64,512]{1,0:T(8,128)}, f32[64,512]{1,0:T(8,128)S(1)}, u32[]{:S(2)}, u32[]{:S(2)}) collective-permute-start(f32[64,512]{1,0:T(8,128)} %add.3.refs_1_), channel_id=1, source_target_pairs={{0,16},{4,20},{8,24},{12,28},{16,0},{20,4},{24,8},{28,12},{1,17},{... | collective-permute-start | bytes 393224 | tf_op jit(solution)/shard_map/ppermute | solution.py:581
  253.8 5.4 %collective-permute-start.23 = (f32[64,512]{1,0:T(8,128)}, f32[64,512]{1,0:T(8,128)S(1)}, u32[]{:S(2)}, u32[]{:S(2)}) collective-permute-start(f32[64,512]{1,0:T(8,128)} %add.3.refs_1_), channel_id=1, source_target_pairs={{0,8},{4,12},{8,0},{12,4},{16,24},{20,28},{24,16},{28,20},{1,9},{5... | collective-permute-start | bytes 393224 | tf_op jit(solution)/shard_map/ppermute | solution.py:581
  262.5 2.1 collective-permute-start.26
  264.6 1.0 copy-start.23
  (15 other events, 10.8 us)

commit v12 on v11

--- a/solution.py
+++ b/solution.py
@@ -163,7 +163,7 @@
         lax.fori_loop(0, capacity, place, 0, unroll=4)
 
 
-def settle(meta, moved, capacity, per_slab, shares, far, cuts, after):
+def settle(meta, moved, capacity, per_slab, shares, far, count, cuts, after):
     with_ids = meta is None
     chips = len(moved)
     rows, width = moved[0].shape[1:]
@@ -171,7 +171,7 @@
         pieces = (jax.ShapeDtypeStruct((shares, per_slab, rows, width), moved[0].dtype),)
     else:
         piece = jax.ShapeDtypeStruct((per_slab, rows // cuts, width), moved[0].dtype)
-        pieces = (piece,) * (shares // 2 * cuts)
+        pieces = (piece,) * (count * cuts)
     ids = jax.ShapeDtypeStruct((chips * CORES, TILE), jnp.int32)
     outs = pl.pallas_call(
         lambda *refs: settle_kernel(chips, capacity, with_ids, far, cuts, *refs[len(after) :]),
@@ -189,13 +189,13 @@
 def by_distance(refs):
     near = len(refs) - 1
     mine = lax.axis_index("snap")
-    return list(refs[:near]) + [refs[near].at[mine ^ share] for share in range(near, 2 * near)]
+    return list(refs[:near]) + [refs[near].at[mine ^ share] for share in range(near, refs[near].shape[0])]
 
 
 def cell_specs(shares, size, rows, width, first):
     near = pl.BlockSpec((size, rows, width), lambda i: (first + i, 0, 0))
     far = pl.BlockSpec((shares, size, rows, width), lambda i: (0, first + i, 0, 0))
-    return [near] * (shares // 2) + [far]
+    return [near, far]
 
 
 def whole_rows(refs):
@@ -259,7 +259,7 @@
     def _():
         acc_ref[...] = jnp.zeros_like(acc_ref)
 
-    count = shares // 2 + 1
+    count = 2
     rows = refs[0].shape[1]
     y_refs, y_shares = refs[count:-2], []
     while y_refs:
@@ -590,8 +590,8 @@
     full = shares * width
     tiles = full // TILE
     pairs = tiles * (tiles + 1) // 2
-    half = shares // 2
-    shares_of = (tuple(range(half, shares)), tuple(range(half)))
+    shares_of = (tuple(range(1, shares)), (0,))
+    away = len(shares_of[0])
 
     def packed(owned, groups, with_ids, after):
         cells = owned.reshape(slots, shares, patch // shares, width)
@@ -608,12 +608,13 @@
 
     def place_far(meta, moved, after):
         pieces, meta = settle(
-            meta, moved, slots // slabs, per_slab, shares, shares_of[0], 1, after
+            meta, moved, slots // slabs, per_slab, shares, shares_of[0], 0, 1, after
         )
-        return to_pieces(pieces[0], "snap"), meta
+        return pieces, to_pieces(pieces[0], "snap"), meta
 
     def place(meta, moved, group, cuts, after):
-        pieces, _ = settle(meta, moved, slots // slabs, per_slab, shares, (), cuts, after)
+        count = len(shares_of[group])
+        pieces, _ = settle(meta, moved, slots // slabs, per_slab, shares, (), count, cuts, after)
         return pieces, [
             swap(piece, "snap", shares_of[group][k // cuts]) if shares_of[group][k // cuts] else piece
             for k, piece in enumerate(pieces)
@@ -629,25 +630,25 @@
     sent_x = packed(owned_x, shares_of, True, [])
     ((same_y, other_y),) = packed(owned_y, (shares_of[0] + shares_of[1],), False, [])
     other_y = swap(other_y, "space", 1)
-    joined_near = merged(sent_x[1], [])
     far = to_chips(merged(sent_x[0], []))
-    x_far, meta = place_far(None, far, [other_y, joined_near[0]])
-    near = to_chips(joined_near)
-    y_far = to_chips(merge(same_y, other_y, chips, near[1:3], slice(0, half), shares))
-    y_near = to_chips(merge(same_y, other_y, chips, y_far[1:3], slice(half, shares), shares))
+    near = to_chips(merged(sent_x[1], far[1:3]))
+    settled, x_far, meta = place_far(None, far, [other_y])
+    after = settled + near[1:2]
+    y_far = to_chips(merge(same_y, other_y, chips, after, slice(0, away), shares))
+    y_near = to_chips(merge(same_y, other_y, chips, y_far[1:3], slice(away, shares), shares))
     _, x_near = place(meta, near, 1, 1, [])
     x_cells = x_near + [x_far]
 
-    gram_local = gram_blocks(x_cells, y_far[1:])
+    settled, y_far = place(meta, y_far, 0, 2, x_near)
+    gram_local = gram_blocks(x_cells, settled[:1])
     gram = to_pieces(gram_local.reshape(pairs * TILE, TILE))
-    settled, y_far = place(meta, y_far, 0, 2, [gram_local])
-    gram = sum_pieces(gram, slabs, settled[:1], shares)
-    gram = sum_pieces(to_pieces(gram, "snap"), shares, [y_far[0], y_far[2]] + y_near[1:3])
+    gram = sum_pieces(gram, slabs, [y_far[2], y_far[4]] + y_near[1:], shares)
+    gram = sum_pieces(to_pieces(gram, "snap"), shares, [])
     settled, y_near = place(meta, y_near, 1, 1, [gram])
     y_cells = y_near + y_far
     gram = lax.all_gather(gram, "space", axis=0, tiled=True)
 
-    steps = factor_steps(gram.reshape(pairs, TILE, TILE), tiles, rows_total, settled[:1])
+    steps = factor_steps(gram.reshape(pairs, TILE, TILE), tiles, rows_total, [])
     state = next(steps)
     for _ in range(tiles - 3):
         state = steps.send([])

time: 270 us -> 288 us (1.067)
  waiting for transfers between devices: 105 us -> 119 us
    ppermute x27, waiting for transfers between devices: 97 us -> 105 us  [swap(): lax.ppermute(value, axis, [(i, i ^ mask) for i in range(lax.axis_size(axi...]
    all_to_all x4, waiting for transfers between devices: 7.96 us -> 14 us  [to_pieces(): return lax.all_to_all(value, axis, split_axis=0, concat_axis=0, tiled=True)]
    all_to_all x4, starting transfers between devices: 17.5 us -> 21.4 us  [to_pieces(): return lax.all_to_all(value, axis, split_axis=0, concat_axis=0, tiled=True)]
    pallas_call x2, Pallas kernels: 5.37 us -> 8.28 us  [pack(): pl.pallas_call(lambda *refs: pack_kernel(slabs, capacity, per_slab, share...]
    unnamed x96 -> x102, local copies, waits for them, and re-layouts: 30.9 us -> 30.4 us
  transfers between devices with their start and end apart: 31 -> 31, of which waited for: 13 -> 13; matrix products, arithmetic and copies ran while one was open for 0% -> 0% of each run, Pallas kernels for 16% -> 15%
where the time goes in v12:
time: 288 us; the launch traced here: 287 us
  waiting for transfers between devices  119 us (41%)
  Pallas kernels  72.4 us (25%)
  starting transfers between devices  53.3 us (19%)
  local copies, waits for them, and re-layouts  30.4 us (11%)
  blocking collectives  10.8 us (4%)
    ppermute x27, waiting for transfers between devices, swap(): lax.ppermute(value, axis, [(i, i ^ mask) for i in range(lax.axis_size(axi...  105 us
    ppermute x27, starting transfers between devices, swap(): lax.ppermute(value, axis, [(i, i ^ mask) for i in range(lax.axis_size(axi...  31.9 us
    unnamed x102, local copies, waits for them, and re-layouts  30.4 us
    all_to_all x4, starting transfers between devices, to_pieces(): return lax.all_to_all(value, axis, split_axis=0, concat_axis=0, tiled=True)  21.4 us
    pallas_call x4, Pallas kernels, factor_call(): pl.pallas_call(lambda *refs: kernel(*refs[len(after):]), out_shape=out_sh...  19.7 us
    all_to_all x4, waiting for transfers between devices, to_pieces(): return lax.all_to_all(value, axis, split_axis=0, concat_axis=0, tiled=True)  14 us
    all_gather x1, blocking collectives, body(): gram = lax.all_gather(gram, 'space', axis=0, tiled=True)  10.8 us
    pallas_call x2, Pallas kernels, basis(): pl.pallas_call(lambda *refs: basis_kernel(*refs[len(unread):]), grid=(ste...  10.6 us
  transfers between devices with their start and end apart: 31, of which 13 were waited for; matrix products, arithmetic and copies ran while one was open for 0% of the time, Pallas kernels for 15%

profile of v12, /device:TPU:0, one launch (start us, length us, event | category | flops | bytes accessed | tf_op | source)
XLA Modules:
  0.0 286.5 jit_solution(10018356441360048583)
XLA Ops:
  0.6 2.2 copy-done.11
  3.5 4.2 %pack.3 = (bf16[196,32,128]{2,1,0:T(8,128)(2,1)S(1)}, bf16[196,32,128]{2,1,0:T(8,128)(2,1)S(1)}, bf16[64,32,128]{2,1,0:T(8,128)(2,1)S(1)}, bf16[64,32,128]{2,1,0:T(8,128)(2,1)S(1)}) custom-call(s32[128]{0:T(128)S(1)} %copy-done.32, bf16[128,4,32,128]{3,2,1,0:T(8,128)(2,1)S(1)} %bitcast.24), custom_call_target="tpu_custom_call" | custom-call | flops 1 | bytes 1 | tf_op jit(solution)/shard_map/pack/pallas_call | solution.py:78
  8.9 4.1 %pack.2 = (bf16[256,32,128]{2,1,0:T(8,128)(2,1)S(1)}, bf16[256,32,128]{2,1,0:T(8,128)(2,1)S(1)}) custom-call(s32[128]{0:T(128)S(1)} %copy-done.33, bf16[128,4,32,128]{3,2,1,0:T(8,128)(2,1)S(1)} %bitcast.25), custom_call_target="tpu_custom_call" | custom-call | flops 1 | bytes 1 | tf_op jit(solution)/shard_map/pack/pallas_call | solution.py:78
  13.0 1.3 copy-done.8
  14.7 1.9 collective-permute-start.3
  16.6 1.6 collective-permute-start.4
  18.5 16.9 %collective-permute-done.2.refs_2_.refs_0_ = bf16[98,32,128]{2,1,0:T(8,128)(2,1)S(1)} collective-permute-done((bf16[98,32,128]{2,1,0:T(8,128)(2,1)S(1)}, bf16[98,32,128]{2,1,0:T(8,128)(2,1)S(1)}, u32[]{:S(2)}, u32[]{:S(2)}) %collective-permute-start.2) | collective-permute-done | bytes 802848 | tf_op jit(solution)/shard_map/ppermute | solution.py:581
  35.4 17.8 %collective-permute-done.4.refs_4_ = bf16[98,32,128]{2,1,0:T(8,128)(2,1)S(1)} collective-permute-done((bf16[98,32,128]{2,1,0:T(8,128)(2,1)S(1)}, bf16[98,32,128]{2,1,0:T(8,128)(2,1)S(1)}, u32[]{:S(2)}, u32[]{:S(2)}) %collective-permute-start.4) | collective-permute-done | bytes 802848 | tf_op jit(solution)/shard_map/ppermute | solution.py:581
  53.1 2.9 %settle.4 = (bf16[4,64,32,128]{3,2,1,0:T(8,128)(2,1)S(1)}, s32[8,128]{1,0:T(8,128)S(1)}) custom-call(bf16[256,32,128]{2,1,0:T(8,128)(2,1)S(1)} %collective-permute-done.refs_0_, bf16[98,32,128]{2,1,0:T(8,128)(2,1)S(1)} %get-tuple-element.41.refs_1_, bf16[98,32,128]{2,1,0:T(8,128)(2,1)S(1)} %collective-permute-done.2.refs_2_.refs_0_, ...), custom_call_target="tpu_custom_call" | custom-call | flops 1 | bytes 1 | tf_op jit(solution)/shard_map/settle/pallas_call | solution.py:176
  56.1 1.3 copy-done.6
  57.4 5.0 %all-to-all-start = ((bf16[4,64,32,128]{3,2,1,0:T(8,128)(2,1)}), bf16[4,64,32,128]{3,2,1,0:T(8,128)(2,1)}, u32[]{:S(2)}, u32[]{:S(2)}) async-start(bf16[4,64,32,128]{3,2,1,0:T(8,128)(2,1)} %copy-done.6), calls=%async_computation | async-start | bytes 4194304 | tf_op jit(solution)/shard_map/all_to_all | solution.py:607
  62.4 2.1 collective-permute-done.5.refs_3_
  64.5 1.1 copy-done.14
  65.7 1.7 collective-permute-start.6
  67.5 6.7 %collective-permute-done.6.refs_2_.refs_1_ = bf16[32,32,128]{2,1,0:T(8,128)(2,1)S(1)} collective-permute-done((bf16[32,32,128]{2,1,0:T(8,128)(2,1)S(1)}, bf16[32,32,128]{2,1,0:T(8,128)(2,1)S(1)}, u32[]{:S(2)}, u32[]{:S(2)}) %collective-permute-start.6) | collective-permute-done | bytes 262176 | tf_op jit(solution)/shard_map/ppermute | solution.py:581
  74.2 1.6 copy-done.9
  75.9 1.7 collective-permute-start.9
  78.2 1.3 collective-permute-start.11
  79.5 1.4 collective-permute-start.7
  80.9 1.8 collective-permute-start.8
  82.6 41.7 %collective-permute-done.7.refs_3_ = bf16[32,32,128]{2,1,0:T(8,128)(2,1)S(1)} collective-permute-done((bf16[32,32,128]{2,1,0:T(8,128)(2,1)S(1)}, bf16[32,32,128]{2,1,0:T(8,128)(2,1)S(1)}, u32[]{:S(2)}, u32[]{:S(2)}) %collective-permute-start.7) | collective-permute-done | bytes 262176 | tf_op jit(solution)/shard_map/ppermute | solution.py:581
  124.4 2.0 settle.5.refs_0_.refs_1_.refs_2_
  126.4 2.9 %settle.6 = (bf16[64,16,128]{2,1,0:T(8,128)(2,1)S(1)}, bf16[64,16,128]{2,1,0:T(8,128)(2,1)}, bf16[64,16,128]{2,1,0:T(8,128)(2,1)S(1)}, bf16[64,16,128]{2,1,0:T(8...) custom-call(bf16[64,32,128]{2,1,0:T(8,128)(2,1)S(1)} %settle.5.refs_0_.refs_1_.refs_2_, ...), custom_call_target="tpu_custom_call" | custom-call | flops 1 | bytes 1 | tf_op jit(solution)/shard_map/settle/pallas_call | solution.py:176
  133.1 4.7 %gram_blocks.1 = f32[10,128,128]{2,1,0:T(8,128)} custom-call(bf16[64,16,128]{2,1,0:T(8,128)(2,1)} %copy-done.30, bf16[64,32,128]{2,1,0:T(8,128)(2,1)} %copy-done.4, bf16[4,64,32,128]{3,2,1,0:T(8,128)(2,1)} %all-to-all-done.refs_2_.refs_3_), custom_call_target="tpu_custom_call" | custom-call | flops 1 | bytes 1 | tf_op jit(solution)/shard_map/gram_blocks/pallas_call | solution.py:241
  137.8 4.2 %all-to-all-start.1 = ((f32[8,160,128]{2,1,0:T(8,128)}), f32[8,160,128]{2,1,0:T(8,128)}, u32[]{:S(2)}, u32[]{:S(2)}) async-start(f32[8,160,128]{2,1,0:T(8,128)} %bitcast.36), calls=%async_computation.1 | async-start | bytes 1310720 | tf_op jit(solution)/shard_map/all_to_all | solution.py:607
  142.0 1.6 copy-done.10
  143.6 1.1 copy-done.16
  144.9 2.0 collective-permute-start.15
  146.8 1.5 collective-permute-start.14
  148.4 2.9 %collective-permute-start.12 = (bf16[64,16,128]{2,1,0:T(8,128)(2,1)S(1)}, bf16[64,16,128]{2,1,0:T(8,128)(2,1)S(1)}, u32[]{:S(2)}, u32[]{:S(2)}) collective-permute-start(bf16[64,16,128]{2,1,0:T(8,128)(2,1)S(1)} %copy-done.40), channel_id=1, source_target_pairs={{0,2},{1,3},{2,0},{3,1},{4,6},{5,7},{6,4},{7,5},{8,10},{9,11},{10,... | collective-permute-start | bytes 786440 | tf_op jit(solution)/shard_map/ppermute | solution.py:581
  151.4 1.4 collective-permute-start.13
  152.8 5.0 %collective-permute-done.15.refs_3_.refs_4_ = bf16[32,32,128]{2,1,0:T(8,128)(2,1)S(1)} collective-permute-done((bf16[32,32,128]{2,1,0:T(8,128)(2,1)S(1)}, bf16[32,32,128]{2,1,0:T(8,128)(2,1)S(1)}, u32[]{:S(2)}, u32[]{:S(2)}) %collective-permute-start.15) | collective-permute-done | bytes 262176 | tf_op jit(solution)/shard_map/ppermute | solution.py:581
  158.2 6.1 %collective-permute-done.16.refs_4_.refs_5_ = bf16[32,32,128]{2,1,0:T(8,128)(2,1)S(1)} collective-permute-done((bf16[32,32,128]{2,1,0:T(8,128)(2,1)S(1)}, bf16[32,32,128]{2,1,0:T(8,128)(2,1)S(1)}, u32[]{:S(2)}, u32[]{:S(2)}) %collective-permute-start.16) | collective-permute-done | bytes 262176 | tf_op jit(solution)/shard_map/ppermute | solution.py:581
  164.3 5.5 %collective-permute-done.12.refs_0_.refs_6_ = bf16[64,16,128]{2,1,0:T(8,128)(2,1)S(1)} collective-permute-done((bf16[64,16,128]{2,1,0:T(8,128)(2,1)S(1)}, bf16[64,16,128]{2,1,0:T(8,128)(2,1)S(1)}, u32[]{:S(2)}, u32[]{:S(2)}) %collective-permute-start.12) | collective-permute-done | bytes 262176 | tf_op jit(solution)/shard_map/ppermute | solution.py:581
  170.6 1.8 sum_pieces.3
  172.4 8.3 %all-to-all-start.2 = ((f32[4,160,128]{2,1,0:T(8,128)}), f32[4,160,128]{2,1,0:T(8,128)S(1)}, u32[]{:S(2)}, u32[]{:S(2)}) async-start(f32[4,160,128]{2,1,0:T(8,128)} %bitcast.37), calls=%async_computation.2 | async-start | bytes 655360 | tf_op jit(solution)/shard_map/all_to_all | solution.py:607
  180.7 2.0 collective-permute-start.18
  182.7 2.4 collective-permute-start.19
  185.1 1.1 collective-permute-start.17
  186.2 6.1 %all-to-all-done.2 = f32[4,160,128]{2,1,0:T(8,128)S(1)} async-done(((f32[4,160,128]{2,1,0:T(8,128)}), f32[4,160,128]{2,1,0:T(8,128)S(1)}, u32[]{:S(2)}, u32[]{:S(2)}) %all-to-all-start.2) | async-done | bytes 327712 | tf_op jit(solution)/shard_map/all_to_all | solution.py:607
  193.0 1.6 sum_pieces.4.refs_0_
  194.7 10.8 %all_gather.3 = f32[1280,128]{1,0:T(8,128)S(1)} all-gather(f32[160,128]{1,0:T(8,128)} %sum_pieces.4.refs_0_), channel_id=1, replica_groups=mesh['space'=8,'snap'=4] {'space'}, dimensions={0}, use_global_device_ids=true | all-gather | bytes 737280 | tf_op jit(solution)/shard_map/all_gather | solution.py:649
  205.4 4.9 %factor.4.refs_0_ = f32[4,8,128,128]{3,2,1,0:T(8,128)S(1)} custom-call(f32[10,128,128]{2,1,0:T(8,128)S(1)} %bitcast.26), custom_call_target="tpu_custom_call" | custom-call | flops 1 | bytes 1 | tf_op jit(solution)/shard_map/factor/pallas_call | solution.py:430
  210.4 4.8 %factor.5.refs_0_.refs_1_ = f32[4,8,128,128]{3,2,1,0:T(8,128)S(1)} custom-call(f32[4,8,128,128]{3,2,1,0:T(8,128)S(1)} %factor.4.refs_0_), custom_call_target="tpu_custom_call", output_to_operand_aliasing={{}: (0, {})} | custom-call | flops 1 | bytes 1 | tf_op jit(solution)/shard_map/factor/pallas_call | solution.py:430
  215.3 1.3 copy-done
  216.6 2.0 settle.7.refs_3_
  220.1 5.1 %cross_sum.1.refs_0_ = f32[512,512]{1,0:T(8,128)} custom-call(f32[4,8,128,128]{3,2,1,0:T(8,128)} %copy-done, bf16[64,32,128]{2,1,0:T(8,128)(2,1)} %copy-done.4, bf16[4,64,32,128]{3,2,1,0:T(8,128)(2,1)} %all-to-all-done.refs_2_.refs_3_, bf16[64,32,128]{2,1,0:T(8,128)(2,1)} %copy-done.21, bf16[64,16,128]{2,1,0:T(8,128)(2,1)} %collective-permute-done.17.refs_4_, ...), custom_call_target="tpu_custom_call" | custom-call | flops 1 | bytes 1 | tf_op jit(solution)/shard_map/cross_sum/pallas_call | solution.py:294
  225.2 3.9 %all-to-all-start.3 = ((f32[8,64,512]{2,1,0:T(8,128)}), f32[8,64,512]{2,1,0:T(8,128)S(1)}, u32[]{:S(2)}, u32[]{:S(2)}) async-start(f32[8,64,512]{2,1,0:T(8,128)} %bitcast.21), calls=%async_computation.3 | async-start | bytes 2097152 | tf_op jit(solution)/shard_map/all_to_all | solution.py:607
  229.1 1.3 copy-done.5
  230.4 4.6 %factor.6.refs_0_.refs_1_ = f32[4,8,128,128]{3,2,1,0:T(8,128)S(1)} custom-call(f32[512,512]{1,0:T(8,128)S(1)} %copy-done.5, f32[4,8,128,128]{3,2,1,0:T(8,128)S(1)} %copy-done.1), custom_call_target="tpu_custom_call", output_to_operand_aliasing={{}: (1, {})} | custom-call | flops 1 | bytes 1 | tf_op jit(solution)/shard_map/factor/pallas_call | solution.py:430
  235.0 1.3 copy-done.2
  236.3 8.0 %all-to-all-done.3 = f32[8,64,512]{2,1,0:T(8,128)S(1)} async-done(((f32[8,64,512]{2,1,0:T(8,128)}), f32[8,64,512]{2,1,0:T(8,128)S(1)}, u32[]{:S(2)}, u32[]{:S(2)}) %all-to-all-start.3) | async-done | bytes 1048608 | tf_op jit(solution)/shard_map/all_to_all | solution.py:607
  245.2 2.0 sum_pieces.5.refs_0_.refs_1_
  248.1 5.4 %factor.7 = (f32[512,512]{1,0:T(8,128)}, f32[512,512]{1,0:T(8,128)S(1)}, bf16[512,512]{1,0:T(8,128)(2,1)S(1)}, bf16[512,512]{1,0:T(8,128)(2,1)S(1)}, bf16[512,512]{1,0:T(8,128)(2,1)S(1)}) custom-call(f32[64,512]{1,0:T(8,128)S(1)} %copy-done.22, f32[4,8,128,128]{3,2,1,0:T(8,128)S(1)} %copy-done.3), custom_call_target="tpu_custom_call" | custom-call | flops 1 | bytes 1 | tf_op jit(solution)/shard_map/factor/pallas_call | solution.py:430
  256.6 1.6 add.2.refs_0_.refs_1_
  258.2 1.9 collective-permute-start.22
  260.1 5.3 %basis.2.refs_0_ = f32[64,32,512]{2,1,0:T(8,128)} custom-call(f32[64,512]{1,0:T(8,128)} %add.2.refs_0_.refs_1_, bf16[64,32,128]{2,1,0:T(8,128)(2,1)} %copy-done.4, bf16[4,64,32,128]{3,2,1,0:T(8,128)(2,1)} %all-to-all-done.refs_2_.refs_3_, bf16[512,512]{1,0:T(8,128)(2,1)} %copy-done.17, bf16[512,512]{1,0:T(8,128)(2,1)} %copy-done.18, bf16[512,512]{1,0:T(8,128)(2,1)} %copy-done.19), custom_call_target="tpu_custom_call" | custom-call | flops 1 | bytes 1 | tf_op jit(solution)/shard_map/basis/pallas_call | solution.py:483
  266.1 1.6 add.3.refs_1_
  267.7 2.6 collective-permute-start.25
  270.3 1.6 collective-permute-start.24
  271.9 5.3 %basis.3.refs_0_ = f32[64,32,512]{2,1,0:T(8,128)} custom-call(f32[64,32,512]{2,1,0:T(8,128)} %basis.2.refs_0_, f32[64,512]{1,0:T(8,128)} %add.3.refs_1_, bf16[64,32,128]{2,1,0:T(8,128)(2,1)} %copy-done.4, bf16[4,64,32,128]{3,2,1,0:T(8,128)(2,1)} %all-to-all-done.refs_2_.refs_3_, bf16[512,512]{1,0:T(8,128)(2,1)} %copy-done.17, ...), custom_call_target="tpu_custom_call", output_to_operand_aliasing={{}: (0, {})} | custom-call | flops 1 | bytes 1 | tf_op jit(solution)/shard_map/basis/pallas_call | solution.py:483
  278.6 1.9 join.1.refs_1_
  280.5 2.1 collective-permute-done.26.refs_2_
  283.7 2.9 %project.1 = f32[512,512]{1,0:T(8,128)} custom-call(f32[512,512]{1,0:T(8,128)S(1)} %get-tuple-element.72.refs_0_, f32[256,512]{1,0:T(8,128)S(1)} %copy-done.20, f32[256,512]{1,0:T(8,128)S(1)} %collective-permute-done.26.refs_2_), custom_call_target="tpu_custom_call" | custom-call | tf_op jit(solution)/shard_map/project/pallas_call | solution.py:569
  (126 shorter events, 18.8 us)
Async XLA Ops:
  0.6 2.2 copy-start.11
  3.5 5.4 %copy-start.12 = (bf16[128,128,128]{2,1,0:T(8,128)(2,1)S(1)}, bf16[128,128,128]{2,1,0:T(8,128)(2,1)}, u32[]{:S(2)}) copy-start(bf16[128,128,128]{2,1,0:T(8,128)(2,1)} %param.4) | copy-start | bytes 12582916
  3.5 5.4 %copy-start.33 = (s32[128]{0:T(128)S(1)}, s32[128]{0:T(128)}, u32[]{:S(2)}) copy-start(s32[128]{0:T(128)} %refs_0_.3) | copy-start | bytes 1540
  8.5 5.9 %collective-permute-start.1 = (bf16[196,32,128]{2,1,0:T(8,128)(2,1)S(1)}, bf16[196,32,128]{2,1,0:T(8,128)(2,1)S(1)}, u32[]{:S(2)}, u32[]{:S(2)}) collective-permute-start(bf16[196,32,128]{2,1,0:T(8,128)(2,1)S(1)} %get-tuple-element.40), channel_id=1, source_target_pairs={{0,4},{4,0},{8,12},{12,8},{16,20},{20,16},{24,28},{28,24},{1,5},{5... | collective-permute-start | bytes 4816904 | tf_op jit(solution)/shard_map/ppermute | solution.py:581
  13.0 1.4 copy-start.8
  14.3 4.2 %collective-permute-start = (bf16[256,32,128]{2,1,0:T(8,128)(2,1)S(1)}, bf16[256,32,128]{2,1,0:T(8,128)(2,1)S(1)}, u32[]{:S(2)}, u32[]{:S(2)}) collective-permute-start(bf16[256,32,128]{2,1,0:T(8,128)(2,1)S(1)} %get-tuple-element.38), channel_id=1, source_target_pairs={{0,4},{4,0},{8,12},{12,8},{16,20},{20,16},{24,28},{28,24},{1,5},{5... | collective-permute-start | bytes 6291464 | tf_op jit(solution)/shard_map/ppermute | solution.py:581
  14.6 20.8 %collective-permute-start.2 = (bf16[98,32,128]{2,1,0:T(8,128)(2,1)S(1)}, bf16[98,32,128]{2,1,0:T(8,128)(2,1)S(1)}, u32[]{:S(2)}, u32[]{:S(2)}) collective-permute-start(bf16[98,32,128]{2,1,0:T(8,128)(2,1)S(1)} %get-tuple-element.42), channel_id=1, source_target_pairs={{0,8},{4,12},{8,0},{12,4},{16,24},{20,28},{24,16},{28,20},{1,9},{5... | collective-permute-start | bytes 2408456 | tf_op jit(solution)/shard_map/ppermute | solution.py:581
  14.7 20.7 %collective-permute-start.3 = (bf16[98,32,128]{2,1,0:T(8,128)(2,1)S(1)}, bf16[98,32,128]{2,1,0:T(8,128)(2,1)S(1)}, u32[]{:S(2)}, u32[]{:S(2)}) collective-permute-start(bf16[98,32,128]{2,1,0:T(8,128)(2,1)S(1)} %get-tuple-element.43), channel_id=1, source_target_pairs={{0,16},{4,20},{8,24},{12,28},{16,0},{20,4},{24,8},{28,12},{1,17},{... | collective-permute-start | bytes 2408456 | tf_op jit(solution)/shard_map/ppermute | solution.py:581
  16.6 36.6 %collective-permute-start.4 = (bf16[98,32,128]{2,1,0:T(8,128)(2,1)S(1)}, bf16[98,32,128]{2,1,0:T(8,128)(2,1)S(1)}, u32[]{:S(2)}, u32[]{:S(2)}) collective-permute-start(bf16[98,32,128]{2,1,0:T(8,128)(2,1)S(1)} %get-tuple-element.44), channel_id=1, source_target_pairs={{0,24},{4,28},{8,16},{12,20},{16,8},{20,12},{24,0},{28,4},{1,25},{... | collective-permute-start | bytes 2408456 | tf_op jit(solution)/shard_map/ppermute | solution.py:581
  35.4 20.7 %copy-start.13 = (bf16[98,32,128]{2,1,0:T(8,128)(2,1)}, bf16[98,32,128]{2,1,0:T(8,128)(2,1)S(1)}, u32[]{:S(2)}) copy-start(bf16[98,32,128]{2,1,0:T(8,128)(2,1)S(1)} %collective-permute-done.3.refs_3_.refs_1_) | copy-start | bytes 2408452
  56.1 1.3 copy-start.6
  57.4 75.7 %all-to-all-start = ((bf16[4,64,32,128]{3,2,1,0:T(8,128)(2,1)}), bf16[4,64,32,128]{3,2,1,0:T(8,128)(2,1)}, u32[]{:S(2)}, u32[]{:S(2)}) async-start(bf16[4,64,32,128]{3,2,1,0:T(8,128)(2,1)} %copy-done.6), calls=%async_computation | async-start | bytes 4194304 | tf_op jit(solution)/shard_map/all_to_all | solution.py:607
  62.4 11.8 %copy-start.7 = (bf16[4,64,32,128]{3,2,1,0:T(8,128)(2,1)S(1)}, bf16[4,64,32,128]{3,2,1,0:T(8,128)(2,1)}, u32[]{:S(2)}) copy-start(bf16[4,64,32,128]{3,2,1,0:T(8,128)(2,1)} %copy-done.6) | copy-start | bytes 6291460
  62.4 2.1 collective-permute-start.5
  64.5 1.1 copy-start.14
  65.7 8.4 %collective-permute-start.6 = (bf16[32,32,128]{2,1,0:T(8,128)(2,1)S(1)}, bf16[32,32,128]{2,1,0:T(8,128)(2,1)S(1)}, u32[]{:S(2)}, u32[]{:S(2)}) collective-permute-start(bf16[32,32,128]{2,1,0:T(8,128)(2,1)S(1)} %get-tuple-element.49), channel_id=1, source_target_pairs={{0,8},{4,12},{8,0},{12,4},{16,24},{20,28},{24,16},{28,20},{1,9},{5... | collective-permute-start | bytes 786440 | tf_op jit(solution)/shard_map/ppermute | solution.py:581
  74.1 1.6 copy-start.9
  75.9 50.5 %collective-permute-start.9 = (bf16[96,32,128]{2,1,0:T(8,128)(2,1)S(1)}, bf16[96,32,128]{2,1,0:T(8,128)(2,1)S(1)}, u32[]{:S(2)}, u32[]{:S(2)}) collective-permute-start(bf16[96,32,128]{2,1,0:T(8,128)(2,1)S(1)} %bitcast.31), channel_id=1, source_target_pairs={{0,8},{4,12},{8,0},{12,4},{16,24},{20,28},{24,16},{28,20},{1,9},{5... | collective-permute-start | bytes 2359304 | tf_op jit(solution)/shard_map/ppermute | solution.py:581
  77.7 48.7 %collective-permute-start.10 = (bf16[96,32,128]{2,1,0:T(8,128)(2,1)S(1)}, bf16[96,32,128]{2,1,0:T(8,128)(2,1)S(1)}, u32[]{:S(2)}, u32[]{:S(2)}) collective-permute-start(bf16[96,32,128]{2,1,0:T(8,128)(2,1)S(1)} %bitcast.30), channel_id=1, source_target_pairs={{0,16},{4,20},{8,24},{12,28},{16,0},{20,4},{24,8},{28,12},{1,17},{... | collective-permute-start | bytes 2359304 | tf_op jit(solution)/shard_map/ppermute | solution.py:581
  78.2 48.2 %collective-permute-start.11 = (bf16[96,32,128]{2,1,0:T(8,128)(2,1)S(1)}, bf16[96,32,128]{2,1,0:T(8,128)(2,1)S(1)}, u32[]{:S(2)}, u32[]{:S(2)}) collective-permute-start(bf16[96,32,128]{2,1,0:T(8,128)(2,1)S(1)} %bitcast.29), channel_id=1, source_target_pairs={{0,24},{4,28},{8,16},{12,20},{16,8},{20,12},{24,0},{28,4},{1,25},{... | collective-permute-start | bytes 2359304 | tf_op jit(solution)/shard_map/ppermute | solution.py:581
  79.5 44.8 %collective-permute-start.7 = (bf16[32,32,128]{2,1,0:T(8,128)(2,1)S(1)}, bf16[32,32,128]{2,1,0:T(8,128)(2,1)S(1)}, u32[]{:S(2)}, u32[]{:S(2)}) collective-permute-start(bf16[32,32,128]{2,1,0:T(8,128)(2,1)S(1)} %get-tuple-element.50), channel_id=1, source_target_pairs={{0,16},{4,20},{8,24},{12,28},{16,0},{20,4},{24,8},{28,12},{1,17},{... | collective-permute-start | bytes 786440 | tf_op jit(solution)/shard_map/ppermute | solution.py:581
  80.9 43.5 %collective-permute-start.8 = (bf16[32,32,128]{2,1,0:T(8,128)(2,1)S(1)}, bf16[32,32,128]{2,1,0:T(8,128)(2,1)S(1)}, u32[]{:S(2)}, u32[]{:S(2)}) collective-permute-start(bf16[32,32,128]{2,1,0:T(8,128)(2,1)S(1)} %get-tuple-element.51), channel_id=1, source_target_pairs={{0,24},{4,28},{8,16},{12,20},{16,8},{20,12},{24,0},{28,4},{1,25},{... | collective-permute-start | bytes 786440 | tf_op jit(solution)/shard_map/ppermute | solution.py:581
  126.4 6.7 %copy-start.4 = (bf16[64,32,128]{2,1,0:T(8,128)(2,1)}, bf16[64,32,128]{2,1,0:T(8,128)(2,1)S(1)}, u32[]{:S(2)}) copy-start(bf16[64,32,128]{2,1,0:T(8,128)(2,1)S(1)} %settle.5.refs_0_.refs_1_.refs_2_) | copy-start | bytes 1572868
  129.4 0.9 copy-start.15
  137.8 32.0 %all-to-all-start.1 = ((f32[8,160,128]{2,1,0:T(8,128)}), f32[8,160,128]{2,1,0:T(8,128)}, u32[]{:S(2)}, u32[]{:S(2)}) async-start(f32[8,160,128]{2,1,0:T(8,128)} %bitcast.36), calls=%async_computation.1 | async-start | bytes 1310720 | tf_op jit(solution)/shard_map/all_to_all | solution.py:607
  142.0 1.6 copy-start.10
  143.6 1.1 copy-start.16
  144.7 3.7 %copy-start.40 = (bf16[64,16,128]{2,1,0:T(8,128)(2,1)S(1)}, bf16[64,16,128]{2,1,0:T(8,128)(2,1)}, u32[]{:S(2)}) copy-start(bf16[64,16,128]{2,1,0:T(8,128)(2,1)} %copy-done.39) | copy-start | bytes 786436
  144.7 6.6 %copy-start.38 = (bf16[64,16,128]{2,1,0:T(8,128)(2,1)S(1)}, bf16[64,16,128]{2,1,0:T(8,128)(2,1)}, u32[]{:S(2)}) copy-start(bf16[64,16,128]{2,1,0:T(8,128)(2,1)} %copy-done.37) | copy-start | bytes 786436
  144.8 40.3 %copy-start.36 = (bf16[64,16,128]{2,1,0:T(8,128)(2,1)S(1)}, bf16[64,16,128]{2,1,0:T(8,128)(2,1)}, u32[]{:S(2)}) copy-start(bf16[64,16,128]{2,1,0:T(8,128)(2,1)} %copy-done.35) | copy-start | bytes 786436
  144.8 40.3 %copy-start.31 = (bf16[64,16,128]{2,1,0:T(8,128)(2,1)S(1)}, bf16[64,16,128]{2,1,0:T(8,128)(2,1)}, u32[]{:S(2)}) copy-start(bf16[64,16,128]{2,1,0:T(8,128)(2,1)} %copy-done.30) | copy-start | bytes 786436
  144.9 12.9 %collective-permute-start.15 = (bf16[32,32,128]{2,1,0:T(8,128)(2,1)S(1)}, bf16[32,32,128]{2,1,0:T(8,128)(2,1)S(1)}, u32[]{:S(2)}, u32[]{:S(2)}) collective-permute-start(bf16[32,32,128]{2,1,0:T(8,128)(2,1)S(1)} %bitcast.34), channel_id=1, source_target_pairs={{0,16},{4,20},{8,24},{12,28},{16,0},{20,4},{24,8},{28,12},{1,17},{... | collective-permute-start | bytes 786440 | tf_op jit(solution)/shard_map/ppermute | solution.py:581
  146.8 11.4 %collective-permute-start.14 = (bf16[32,32,128]{2,1,0:T(8,128)(2,1)S(1)}, bf16[32,32,128]{2,1,0:T(8,128)(2,1)S(1)}, u32[]{:S(2)}, u32[]{:S(2)}) collective-permute-start(bf16[32,32,128]{2,1,0:T(8,128)(2,1)S(1)} %bitcast.33), channel_id=1, source_target_pairs={{0,8},{4,12},{8,0},{12,4},{16,24},{20,28},{24,16},{28,20},{1,9},{5... | collective-permute-start | bytes 786440 | tf_op jit(solution)/shard_map/ppermute | solution.py:581
  148.3 16.0 %collective-permute-start.16 = (bf16[32,32,128]{2,1,0:T(8,128)(2,1)S(1)}, bf16[32,32,128]{2,1,0:T(8,128)(2,1)S(1)}, u32[]{:S(2)}, u32[]{:S(2)}) collective-permute-start(bf16[32,32,128]{2,1,0:T(8,128)(2,1)S(1)} %bitcast.32), channel_id=1, source_target_pairs={{0,24},{4,28},{8,16},{12,20},{16,8},{20,12},{24,0},{28,4},{1,25},{... | collective-permute-start | bytes 786440 | tf_op jit(solution)/shard_map/ppermute | solution.py:581
  148.4 21.3 %collective-permute-start.12 = (bf16[64,16,128]{2,1,0:T(8,128)(2,1)S(1)}, bf16[64,16,128]{2,1,0:T(8,128)(2,1)S(1)}, u32[]{:S(2)}, u32[]{:S(2)}) collective-permute-start(bf16[64,16,128]{2,1,0:T(8,128)(2,1)S(1)} %copy-done.40), channel_id=1, source_target_pairs={{0,2},{1,3},{2,0},{3,1},{4,6},{5,7},{6,4},{7,5},{8,10},{9,11},{10,... | collective-permute-start | bytes 786440 | tf_op jit(solution)/shard_map/ppermute | solution.py:581
  151.4 18.4 %collective-permute-start.13 = (bf16[64,16,128]{2,1,0:T(8,128)(2,1)S(1)}, bf16[64,16,128]{2,1,0:T(8,128)(2,1)S(1)}, u32[]{:S(2)}, u32[]{:S(2)}) collective-permute-start(bf16[64,16,128]{2,1,0:T(8,128)(2,1)S(1)} %copy-done.38), channel_id=1, source_target_pairs={{0,3},{1,2},{2,1},{3,0},{4,7},{5,6},{6,5},{7,4},{8,11},{9,10},{10,... | collective-permute-start | bytes 786440 | tf_op jit(solution)/shard_map/ppermute | solution.py:581
  157.8 12.0 %copy-start.23 = (bf16[32,32,128]{2,1,0:T(8,128)(2,1)}, bf16[32,32,128]{2,1,0:T(8,128)(2,1)S(1)}, u32[]{:S(2)}) copy-start(bf16[32,32,128]{2,1,0:T(8,128)(2,1)S(1)} %collective-permute-done.15.refs_3_.refs_4_) | copy-start | bytes 786436
  158.2 11.6 %copy-start.25 = (bf16[32,32,128]{2,1,0:T(8,128)(2,1)}, bf16[32,32,128]{2,1,0:T(8,128)(2,1)S(1)}, u32[]{:S(2)}) copy-start(bf16[32,32,128]{2,1,0:T(8,128)(2,1)S(1)} %collective-permute-done.14.refs_2_.refs_3_) | copy-start | bytes 786436
  164.3 5.5 %copy-start.27 = (bf16[32,32,128]{2,1,0:T(8,128)(2,1)}, bf16[32,32,128]{2,1,0:T(8,128)(2,1)S(1)}, u32[]{:S(2)}) copy-start(bf16[32,32,128]{2,1,0:T(8,128)(2,1)S(1)} %collective-permute-done.16.refs_4_.refs_5_) | copy-start | bytes 786436
  172.4 19.9 %all-to-all-start.2 = ((f32[4,160,128]{2,1,0:T(8,128)}), f32[4,160,128]{2,1,0:T(8,128)S(1)}, u32[]{:S(2)}, u32[]{:S(2)}) async-start(f32[4,160,128]{2,1,0:T(8,128)} %bitcast.37), calls=%async_computation.2 | async-start | bytes 655360 | tf_op jit(solution)/shard_map/all_to_all | solution.py:607
  180.7 38.7 %collective-permute-start.18 = (bf16[64,16,128]{2,1,0:T(8,128)(2,1)}, bf16[64,16,128]{2,1,0:T(8,128)(2,1)S(1)}, u32[]{:S(2)}, u32[]{:S(2)}) collective-permute-start(bf16[64,16,128]{2,1,0:T(8,128)(2,1)} %get-tuple-element.65), channel_id=1, source_target_pairs={{0,1},{1,0},{2,3},{3,2},{4,5},{5,4},{6,7},{7,6},{8,9},{9,8},{10,11... | collective-permute-start | bytes 786440 | tf_op jit(solution)/shard_map/ppermute | solution.py:581
  182.7 36.7 %collective-permute-start.19 = (bf16[64,16,128]{2,1,0:T(8,128)(2,1)}, bf16[64,16,128]{2,1,0:T(8,128)(2,1)}, u32[]{:S(2)}, u32[]{:S(2)}) collective-permute-start(bf16[64,16,128]{2,1,0:T(8,128)(2,1)} %get-tuple-element.66), channel_id=1, source_target_pairs={{0,2},{1,3},{2,0},{3,1},{4,6},{5,7},{6,4},{7,5},{8,10},{9,11},{10,... | collective-permute-start | bytes 786440 | tf_op jit(solution)/shard_map/ppermute | solution.py:581
  185.1 34.3 %collective-permute-start.20 = (bf16[64,16,128]{2,1,0:T(8,128)(2,1)S(1)}, bf16[64,16,128]{2,1,0:T(8,128)(2,1)}, u32[]{:S(2)}, u32[]{:S(2)}) collective-permute-start(bf16[64,16,128]{2,1,0:T(8,128)(2,1)S(1)} %copy-done.36), channel_id=1, source_target_pairs={{0,3},{1,2},{2,1},{3,0},{4,7},{5,6},{6,5},{7,4},{8,11},{9,10},{10,... | collective-permute-start | bytes 786440 | tf_op jit(solution)/shard_map/ppermute | solution.py:581
  185.1 34.3 %collective-permute-start.17 = (bf16[64,16,128]{2,1,0:T(8,128)(2,1)S(1)}, bf16[64,16,128]{2,1,0:T(8,128)(2,1)}, u32[]{:S(2)}, u32[]{:S(2)}) collective-permute-start(bf16[64,16,128]{2,1,0:T(8,128)(2,1)S(1)} %copy-done.31), channel_id=1, source_target_pairs={{0,1},{1,0},{2,3},{3,2},{4,5},{5,4},{6,7},{7,6},{8,9},{9,8},{10,11... | collective-permute-start | bytes 786440 | tf_op jit(solution)/shard_map/ppermute | solution.py:581
  210.4 6.2 %copy-start.24 = (bf16[32,32,128]{2,1,0:T(8,128)(2,1)S(1)}, bf16[32,32,128]{2,1,0:T(8,128)(2,1)}, u32[]{:S(2)}) copy-start(bf16[32,32,128]{2,1,0:T(8,128)(2,1)} %copy-done.23) | copy-start | bytes 786436
  210.4 6.2 %copy-start.26 = (bf16[32,32,128]{2,1,0:T(8,128)(2,1)S(1)}, bf16[32,32,128]{2,1,0:T(8,128)(2,1)}, u32[]{:S(2)}) copy-start(bf16[32,32,128]{2,1,0:T(8,128)(2,1)} %copy-done.25) | copy-start | bytes 786436
  210.4 6.2 %copy-start.28 = (bf16[32,32,128]{2,1,0:T(8,128)(2,1)S(1)}, bf16[32,32,128]{2,1,0:T(8,128)(2,1)}, u32[]{:S(2)}) copy-start(bf16[32,32,128]{2,1,0:T(8,128)(2,1)} %copy-done.27) | copy-start | bytes 786436
  210.4 6.2 %copy-start.29 = (f32[160,128]{1,0:T(8,128)S(1)}, f32[160,128]{1,0:T(8,128)}, u32[]{:S(2)}) copy-start(f32[160,128]{1,0:T(8,128)} %sum_pieces.4.refs_0_) | copy-start | bytes 245764
  215.2 1.3 copy-start
  225.2 3.9 %copy-start.1 = (f32[4,8,128,128]{3,2,1,0:T(8,128)S(1)}, f32[4,8,128,128]{3,2,1,0:T(8,128)}, u32[]{:S(2)}) copy-start(f32[4,8,128,128]{3,2,1,0:T(8,128)} %copy-done) | copy-start | bytes 6291460
  225.2 19.0 %all-to-all-start.3 = ((f32[8,64,512]{2,1,0:T(8,128)}), f32[8,64,512]{2,1,0:T(8,128)S(1)}, u32[]{:S(2)}, u32[]{:S(2)}) async-start(f32[8,64,512]{2,1,0:T(8,128)} %bitcast.21), calls=%async_computation.3 | async-start | bytes 2097152 | tf_op jit(solution)/shard_map/all_to_all | solution.py:607
  229.1 1.3 copy-start.5
  235.0 1.3 copy-start.2
  244.2 1.0 copy-start.41
  244.2 3.0 %copy-start.3 = (f32[4,8,128,128]{3,2,1,0:T(8,128)S(1)}, f32[4,8,128,128]{3,2,1,0:T(8,128)}, u32[]{:S(2)}) copy-start(f32[4,8,128,128]{3,2,1,0:T(8,128)} %copy-done.2) | copy-start | bytes 6291460
  247.2 8.8 %collective-permute-start.21 = (f32[64,512]{1,0:T(8,128)}, f32[64,512]{1,0:T(8,128)S(1)}, u32[]{:S(2)}, u32[]{:S(2)}) collective-permute-start(f32[64,512]{1,0:T(8,128)} %sum_pieces.5.refs_0_.refs_1_), channel_id=1, source_target_pairs={{0,1},{1,0},{2,3},{3,2},{4,5},{5,4},{6,7},{7,6},{8,9},{9,8},{10,11... | collective-permute-start | bytes 393224 | tf_op jit(solution)/shard_map/ppermute | solution.py:581
  247.2 0.9 copy-start.22
  254.3 0.8 copy-start.18
  258.2 7.2 %collective-permute-start.22 = (f32[64,512]{1,0:T(8,128)}, f32[64,512]{1,0:T(8,128)S(1)}, u32[]{:S(2)}, u32[]{:S(2)}) collective-permute-start(f32[64,512]{1,0:T(8,128)} %add.2.refs_0_.refs_1_), channel_id=1, source_target_pairs={{0,2},{1,3},{2,0},{3,1},{4,6},{5,7},{6,4},{7,5},{8,10},{9,11},{10,... | collective-permute-start | bytes 393224 | tf_op jit(solution)/shard_map/ppermute | solution.py:581
  267.7 9.5 %collective-permute-start.25 = (f32[64,512]{1,0:T(8,128)}, f32[64,512]{1,0:T(8,128)S(1)}, u32[]{:S(2)}, u32[]{:S(2)}) collective-permute-start(f32[64,512]{1,0:T(8,128)} %add.3.refs_1_), channel_id=1, source_target_pairs={{0,24},{4,28},{8,16},{12,20},{16,8},{20,12},{24,0},{28,4},{1,25},{... | collective-permute-start | bytes 393224 | tf_op jit(solution)/shard_map/ppermute | solution.py:581
  270.3 6.9 %collective-permute-start.24 = (f32[64,512]{1,0:T(8,128)}, f32[64,512]{1,0:T(8,128)S(1)}, u32[]{:S(2)}, u32[]{:S(2)}) collective-permute-start(f32[64,512]{1,0:T(8,128)} %add.3.refs_1_), channel_id=1, source_target_pairs={{0,16},{4,20},{8,24},{12,28},{16,0},{20,4},{24,8},{28,12},{1,17},{... | collective-permute-start | bytes 393224 | tf_op jit(solution)/shard_map/ppermute | solution.py:581
  271.9 5.3 %collective-permute-start.23 = (f32[64,512]{1,0:T(8,128)}, f32[64,512]{1,0:T(8,128)S(1)}, u32[]{:S(2)}, u32[]{:S(2)}) collective-permute-start(f32[64,512]{1,0:T(8,128)} %add.3.refs_1_), channel_id=1, source_target_pairs={{0,8},{4,12},{8,0},{12,4},{16,24},{20,28},{24,16},{28,20},{1,9},{5... | collective-permute-start | bytes 393224 | tf_op jit(solution)/shard_map/ppermute | solution.py:581
  280.5 2.1 collective-permute-start.26
  282.6 1.0 copy-start.20
  (18 other events, 12.9 us)

commit v13 on v12

--- a/solution.py
+++ b/solution.py
@@ -98,32 +98,18 @@
         out_ref[span:] = other_ref[chip * span : (chip + 1) * span]
 
 
-def pick_kernel(picked, same_ref, other_ref, *out_refs):
-    for chip, out_ref in enumerate(out_refs):
-        for owner, ref in enumerate((same_ref, other_ref)):
-            out_ref[owner] = ref[chip, :, picked]
-
-
-def merge(same, other, chips, after, picked=None, of=1):
+def merge(same, other, chips, after):
     tiles, rows, width = same.shape
-    if picked is None:
-        kernel = merge_kernel
-        shape = (CORES * tiles // chips, rows, width)
-    else:
-        kernel = lambda *refs: pick_kernel(picked, *refs)
-        ranks = tiles // chips // of
-        shape = (CORES, ranks, picked.stop - picked.start, rows, width)
-        same, other = (value.reshape(chips, ranks, of, rows, width) for value in (same, other))
-    outs = pl.pallas_call(
-        lambda *refs: kernel(*refs[len(after) :]),
-        out_shape=(jax.ShapeDtypeStruct(shape, same.dtype),) * chips,
+    out = jax.ShapeDtypeStruct((CORES * tiles // chips, rows, width), same.dtype)
+    return pl.pallas_call(
+        lambda *refs: merge_kernel(*refs[len(after) :]),
+        out_shape=(out,) * chips,
         in_specs=[ANY] * len(after) + [VMEM, VMEM],
         out_specs=(VMEM,) * chips,
         compiler_params=pltpu.CompilerParams(vmem_limit_bytes=VMEM_BYTES),
         cost_estimate=LIGHT,
         name="merge",
     )(*after, same, other)
-    return [out.reshape(-1, rows, width) for out in outs]
 
 
 def settle_kernel(chips, capacity, with_ids, far, cuts, *refs):
@@ -259,16 +245,10 @@
     def _():
         acc_ref[...] = jnp.zeros_like(acc_ref)
 
-    count = 2
-    rows = refs[0].shape[1]
-    y_refs, y_shares = refs[count:-2], []
-    while y_refs:
-        cuts = rows // y_refs[0].shape[1]
-        y_shares.append(jnp.concatenate([ref[...] for ref in y_refs[:cuts]], axis=1))
-        y_refs = y_refs[cuts:]
+    y_ref = refs[2]
     acc_ref[...] += lax.dot_general(
-        whole_rows(by_distance(refs[:count])),
-        whole_rows(y_shares),
+        whole_rows(by_distance(refs[:2])),
+        whole_rows([y_ref.at[share] for share in range(shares)]),
         ROWS_BY_ROWS,
         preferred_element_type=jnp.float32,
     )
@@ -278,30 +258,24 @@
         mine = lax.axis_index("snap")
         for a in range(shares):
             rows = pl.ds(pl.multiple_of((mine ^ a) * TILE, TILE), TILE)
-            for b in range(shares):
-                lanes = pl.ds(pl.multiple_of((mine ^ b) * TILE, TILE), TILE)
-                out_ref[rows, lanes] = acc_ref[
-                    a * TILE : (a + 1) * TILE, b * TILE : (b + 1) * TILE
-                ]
+            out_ref[rows, :] = acc_ref[a * TILE : (a + 1) * TILE, :]
 
 
 def cross_sum(x_cells, y_cells, after, steps=4):
     shares, blocks, rows, width = x_cells[-1].shape
     full = shares * width
     specs = cell_specs(shares, blocks // steps, rows, width, 0)
-    for piece in y_cells:
-        specs.append(pl.BlockSpec((blocks // steps, piece.shape[1], width), lambda i: (i, 0, 0)))
     return pl.pallas_call(
         lambda *refs: cross_kernel(shares, *refs[len(after) :]),
         grid=(steps,),
         out_shape=jax.ShapeDtypeStruct((full, full), jnp.float32),
-        in_specs=[ANY] * len(after) + specs,
+        in_specs=[ANY] * len(after) + specs + specs[-1:],
         out_specs=pl.BlockSpec((full, full), lambda i: (0, 0)),
         scratch_shapes=[pltpu.VMEM((full, full), jnp.float32)],
         compiler_params=pltpu.CompilerParams(vmem_limit_bytes=GRID_VMEM_BYTES),
         cost_estimate=LIGHT,
         name="cross_sum",
-    )(*after, *x_cells, *y_cells)
+    )(*after, *x_cells, y_cells)
 
 
 def three_terms(value):
@@ -591,7 +565,6 @@
     tiles = full // TILE
     pairs = tiles * (tiles + 1) // 2
     shares_of = (tuple(range(1, shares)), (0,))
-    away = len(shares_of[0])
 
     def packed(owned, groups, with_ids, after):
         cells = owned.reshape(slots, shares, patch // shares, width)
@@ -606,19 +579,15 @@
     def to_pieces(value, axis="space"):
         return lax.all_to_all(value, axis, split_axis=0, concat_axis=0, tiled=True)
 
-    def place_far(meta, moved, after):
+    def place_far(meta, moved, group, after):
         pieces, meta = settle(
-            meta, moved, slots // slabs, per_slab, shares, shares_of[0], 0, 1, after
+            meta, moved, slots // slabs, per_slab, shares, group, 0, 1, after
         )
         return pieces, to_pieces(pieces[0], "snap"), meta
 
-    def place(meta, moved, group, cuts, after):
-        count = len(shares_of[group])
-        pieces, _ = settle(meta, moved, slots // slabs, per_slab, shares, (), count, cuts, after)
-        return pieces, [
-            swap(piece, "snap", shares_of[group][k // cuts]) if shares_of[group][k // cuts] else piece
-            for k, piece in enumerate(pieces)
-        ]
+    def place_own(meta, moved):
+        (piece,), _ = settle(meta, moved, slots // slabs, per_slab, shares, (), 1, 1, [])
+        return piece
 
     def hops():
         hop = 1
@@ -626,44 +595,33 @@
             yield hop
             hop *= 2
 
-    chips = slabs // CORES
     sent_x = packed(owned_x, shares_of, True, [])
-    ((same_y, other_y),) = packed(owned_y, (shares_of[0] + shares_of[1],), False, [])
-    other_y = swap(other_y, "space", 1)
+    (sent_y,) = packed(owned_y, (tuple(range(shares)),), False, [])
     far = to_chips(merged(sent_x[0], []))
     near = to_chips(merged(sent_x[1], far[1:3]))
-    settled, x_far, meta = place_far(None, far, [other_y])
-    after = settled + near[1:2]
-    y_far = to_chips(merge(same_y, other_y, chips, after, slice(0, away), shares))
-    y_near = to_chips(merge(same_y, other_y, chips, y_far[1:3], slice(away, shares), shares))
-    _, x_near = place(meta, near, 1, 1, [])
-    x_cells = x_near + [x_far]
-
-    settled, y_far = place(meta, y_far, 0, 2, x_near)
-    gram_local = gram_blocks(x_cells, settled[:1])
+    settled, x_far, meta = place_far(None, far, shares_of[0], [])
+    moved_y = to_chips(merged(sent_y, settled + near[1:]))
+    x_cells = [place_own(meta, near), x_far]
+
+    gram_local = gram_blocks(x_cells, moved_y[1:2])
     gram = to_pieces(gram_local.reshape(pairs * TILE, TILE))
-    gram = sum_pieces(gram, slabs, [y_far[2], y_far[4]] + y_near[1:], shares)
-    gram = sum_pieces(to_pieces(gram, "snap"), shares, [])
-    settled, y_near = place(meta, y_near, 1, 1, [gram])
-    y_cells = y_near + y_far
+    gram = to_pieces(sum_pieces(gram, slabs, [], shares), "snap")
+    settled, y_cells, _ = place_far(meta, moved_y, tuple(range(shares)), [gram])
+    gram = sum_pieces(gram, shares, settled)
     gram = lax.all_gather(gram, "space", axis=0, tiled=True)
 
     steps = factor_steps(gram.reshape(pairs, TILE, TILE), tiles, rows_total, [])
     state = next(steps)
-    for _ in range(tiles - 3):
+    for _ in range(1, tiles):
         state = steps.send([])
-    cross_local = cross_sum(x_cells, y_cells, [state])
-    state = steps.send([cross_local])
-    cross = sum_pieces(to_pieces(cross_local), slabs, [state])
-    r_factor, inverse, *terms = steps.send([cross])
-    tied = [r_factor]
+    r_factor, inverse, *terms = state
+    q_basis = basis(x_cells, terms, 0, 1, None, [], 8)
+
+    cross_local = cross_sum(x_cells, y_cells, [q_basis])
+    cross = sum_pieces(to_pieces(cross_local), slabs, [])
     for hop in hops():
-        cross = add(cross, swap(cross, "snap", hop), tied)
-        if hop == 1:
-            q_basis = basis(x_cells, terms, 0, 2, None, [cross])
-            tied = [q_basis]
-    q_basis = basis(x_cells, terms, 1, 2, q_basis, [cross])
-    same = join([cross] + [swap(cross, "space", m) for m in range(CORES, slabs, CORES)], [q_basis])
+        cross = add(cross, swap(cross, "snap", hop), [])
+    same = join([cross] + [swap(cross, "space", m) for m in range(CORES, slabs, CORES)], [])
     projection = project(inverse, same, swap(same, "space", 1), slabs, math.sqrt(rows_total))
     return q_basis, r_factor, projection
 

time: 288 us -> 292 us (1.014)
  waiting for transfers between devices: 119 us -> 140 us
  starting transfers between devices: 53.3 us -> 33.8 us
  blocking collectives: 10.8 us -> 29.8 us
  local copies, waits for them, and re-layouts: 30.4 us -> 13.1 us
    all_to_all x0 -> x1, blocking collectives: none -> 19.6 us  [to_pieces(): return lax.all_to_all(value, axis, split_axis=0, concat_axis=0, tiled=True)]
    ppermute x27 -> x18, waiting for transfers between devices: 105 us -> 122 us  [swap(): lax.ppermute(value, axis, [(i, i ^ mask) for i in range(lax.axis_size(axi...]
    unnamed x102 -> x42, local copies, waits for them, and re-layouts: 30.4 us -> 13.1 us
    ppermute x27 -> x18, starting transfers between devices: 31.9 us -> 17.6 us  [swap(): lax.ppermute(value, axis, [(i, i ^ mask) for i in range(lax.axis_size(axi...]
    all_to_all x4, starting transfers between devices: 21.4 us -> 16.3 us  [to_pieces(): return lax.all_to_all(value, axis, split_axis=0, concat_axis=0, tiled=True)]
    all_to_all x4, waiting for transfers between devices: 14 us -> 17.5 us  [to_pieces(): return lax.all_to_all(value, axis, split_axis=0, concat_axis=0, tiled=True)]
    pallas_call x2 -> x1, Pallas kernels: 10.6 us -> 8.95 us  [basis(): pl.pallas_call(lambda *refs: basis_kernel(*refs[len(unread):]), grid=(ste...]
    pallas_call x4 -> x3, Pallas kernels: 9.92 us -> 10.1 us  [settle(): pl.pallas_call(lambda *refs: settle_kernel(chips, capacity, with_ids, far...]
  transfers between devices with their start and end apart: 31 -> 22, of which waited for: 13 -> 19; matrix products, arithmetic and copies ran while one was open for 0% -> 0% of each run, Pallas kernels for 15% -> 15%
where the time goes in v13:
time: 292 us; the launch traced here: 291 us
  waiting for transfers between devices  140 us (48%)
  Pallas kernels  73 us (25%)
  starting transfers between devices  33.8 us (12%)
  blocking collectives  29.8 us (10%)
  local copies, waits for them, and re-layouts  13.1 us (4%)
    ppermute x18, waiting for transfers between devices, swap(): lax.ppermute(value, axis, [(i, i ^ mask) for i in range(lax.axis_size(axi...  122 us
    pallas_call x4, Pallas kernels, factor_call(): pl.pallas_call(lambda *refs: kernel(*refs[len(after):]), out_shape=out_sh...  19.9 us
    all_to_all x1, blocking collectives, to_pieces(): return lax.all_to_all(value, axis, split_axis=0, concat_axis=0, tiled=True)  19.6 us
    ppermute x18, starting transfers between devices, swap(): lax.ppermute(value, axis, [(i, i ^ mask) for i in range(lax.axis_size(axi...  17.6 us
    all_to_all x4, waiting for transfers between devices, to_pieces(): return lax.all_to_all(value, axis, split_axis=0, concat_axis=0, tiled=True)  17.5 us
    all_to_all x4, starting transfers between devices, to_pieces(): return lax.all_to_all(value, axis, split_axis=0, concat_axis=0, tiled=True)  16.3 us
    unnamed x42, local copies, waits for them, and re-layouts  13.1 us
    all_gather x1, blocking collectives, body(): gram = lax.all_gather(gram, 'space', axis=0, tiled=True)  10.2 us
  transfers between devices with their start and end apart: 22, of which 19 were waited for; matrix products, arithmetic and copies ran while one was open for 0% of the time, Pallas kernels for 15%

profile of v13, /device:TPU:0, one launch (start us, length us, event | category | flops | bytes accessed | tf_op | source)
XLA Modules:
  0.0 290.6 jit_solution(12639250973764942071)
XLA Ops:
  0.6 2.2 copy-done.1
  3.5 3.6 %pack.2 = (bf16[196,32,128]{2,1,0:T(8,128)(2,1)S(1)}, bf16[196,32,128]{2,1,0:T(8,128)(2,1)S(1)}, bf16[64,32,128]{2,1,0:T(8,128)(2,1)S(1)}, bf16[64,32,128]{2,1,0:T(8,128)(2,1)S(1)}) custom-call(s32[128]{0:T(128)S(1)} %copy-done.12, bf16[128,4,32,128]{3,2,1,0:T(8,128)(2,1)S(1)} %bitcast.9), custom_call_target="tpu_custom_call" | custom-call | flops 1 | bytes 1 | tf_op jit(solution)/shard_map/pack/pallas_call | solution.py:78
  7.1 0.8 collective-permute-start
  7.9 3.1 %collective-permute-done.refs_1_ = bf16[196,32,128]{2,1,0:T(8,128)(2,1)S(1)} collective-permute-done((bf16[196,32,128]{2,1,0:T(8,128)(2,1)S(1)}, bf16[196,32,128]{2,1,0:T(8,128)(2,1)S(1)}, u32[]{:S(2)}, u32[]{:S(2)}) %collective-permute-start) | collective-permute-done | bytes 1605664 | tf_op jit(solution)/shard_map/ppermute | solution.py:555
  11.2 1.4 collective-permute-start.1
  12.6 2.5 collective-permute-start.2
  15.1 0.8 collective-permute-start.3
  15.9 4.9 %pack.3 = (bf16[256,32,128]{2,1,0:T(8,128)(2,1)S(1)}, bf16[256,32,128]{2,1,0:T(8,128)(2,1)}) custom-call(s32[128]{0:T(128)S(1)} %copy-done.12, bf16[128,4,32,128]{3,2,1,0:T(8,128)(2,1)S(1)} %bitcast.10), custom_call_target="tpu_custom_call" | custom-call | flops 1 | bytes 1 | tf_op jit(solution)/shard_map/pack/pallas_call | solution.py:78
  20.8 1.4 copy-done.6
  22.2 9.8 %collective-permute-done.1.refs_1_.refs_0_ = bf16[98,32,128]{2,1,0:T(8,128)(2,1)S(1)} collective-permute-done((bf16[98,32,128]{2,1,0:T(8,128)(2,1)S(1)}, bf16[98,32,128]{2,1,0:T(8,128)(2,1)S(1)}, u32[]{:S(2)}, u32[]{:S(2)}) %collective-permute-start.1) | collective-permute-done | bytes 802848 | tf_op jit(solution)/shard_map/ppermute | solution.py:555
  32.0 17.5 %collective-permute-done.2.refs_2_.refs_1_ = bf16[98,32,128]{2,1,0:T(8,128)(2,1)S(1)} collective-permute-done((bf16[98,32,128]{2,1,0:T(8,128)(2,1)S(1)}, bf16[98,32,128]{2,1,0:T(8,128)(2,1)S(1)}, u32[]{:S(2)}, u32[]{:S(2)}) %collective-permute-start.2) | collective-permute-done | bytes 802848 | tf_op jit(solution)/shard_map/ppermute | solution.py:555
  49.5 1.6 collective-permute-done.3.refs_3_
  51.1 3.6 %settle.3 = (bf16[4,64,32,128]{3,2,1,0:T(8,128)(2,1)}, s32[8,128]{1,0:T(8,128)S(1)}) custom-call(bf16[98,32,128]{2,1,0:T(8,128)(2,1)S(1)} %get-tuple-element.30.refs_0_, bf16[98,32,128]{2,1,0:T(8,128)(2,1)S(1)} %collective-permute-done.1.refs_1_.refs_0_, bf16[98,32,128]{2,1,0:T(8,128)(2,1)S(1)} %collective-permute-done.2.refs_2_.refs_1_, ...), custom_call_target="tpu_custom_call" | custom-call | flops 1 | bytes 1 | tf_op jit(solution)/shard_map/settle/pallas_call | solution.py:162
  54.7 4.9 %all-to-all-start = ((bf16[4,64,32,128]{3,2,1,0:T(8,128)(2,1)}), bf16[4,64,32,128]{3,2,1,0:T(8,128)(2,1)}, u32[]{:S(2)}, u32[]{:S(2)}) async-start(bf16[4,64,32,128]{3,2,1,0:T(8,128)(2,1)} %get-tuple-element.41.refs_0_), calls=%async_computation | async-start | bytes 4194304 | tf_op jit(solution)/shard_map/all_to_all | solution.py:580
  59.5 1.9 collective-permute-done.4.refs_3_
  62.2 1.7 collective-permute-start.6
  63.9 1.2 collective-permute-start.7
  65.1 5.7 %collective-permute-done.5.refs_2_.refs_1_ = bf16[32,32,128]{2,1,0:T(8,128)(2,1)S(1)} collective-permute-done((bf16[32,32,128]{2,1,0:T(8,128)(2,1)S(1)}, bf16[32,32,128]{2,1,0:T(8,128)(2,1)S(1)}, u32[]{:S(2)}, u32[]{:S(2)}) %collective-permute-start.5) | collective-permute-done | bytes 262176 | tf_op jit(solution)/shard_map/ppermute | solution.py:555
  70.7 4.4 %collective-permute-done.6.refs_3_.refs_2_ = bf16[32,32,128]{2,1,0:T(8,128)(2,1)S(1)} collective-permute-done((bf16[32,32,128]{2,1,0:T(8,128)(2,1)S(1)}, bf16[32,32,128]{2,1,0:T(8,128)(2,1)S(1)}, u32[]{:S(2)}, u32[]{:S(2)}) %collective-permute-start.6) | collective-permute-done | bytes 262176 | tf_op jit(solution)/shard_map/ppermute | solution.py:555
  75.1 0.8 collective-permute-done.7.refs_4_.refs_3_
  75.9 1.9 merge.5
  77.8 1.0 copy-done.14
  78.8 1.4 collective-permute-start.9
  80.2 2.0 settle.4.refs_1_.refs_0_
  82.2 0.8 copy-done
  83.0 20.2 %collective-permute-done.9.refs_0_.refs_3_ = bf16[128,32,128]{2,1,0:T(8,128)(2,1)S(1)} collective-permute-done((bf16[128,32,128]{2,1,0:T(8,128)(2,1)S(1)}, bf16[128,32,128]{2,1,0:T(8,128)(2,1)S(1)}, u32[]{:S(2)}, u32[]{:S(2)}) %collective-permute-start.9) | collective-permute-done | bytes 1048608 | tf_op jit(solution)/shard_map/ppermute | solution.py:555
  103.2 4.1 %all-to-all-done.refs_2_.refs_1_ = bf16[4,64,32,128]{3,2,1,0:T(8,128)(2,1)} async-done(((bf16[4,64,32,128]{3,2,1,0:T(8,128)(2,1)}), bf16[4,64,32,128]{3,2,1,0:T(8,128)(2,1)}, u32[]{:S(2)}, u32[]{:S(2)}) %all-to-all-start) | async-done | bytes 2097184 | tf_op jit(solution)/shard_map/all_to_all | solution.py:580
  107.3 4.7 %gram_blocks.1 = f32[10,128,128]{2,1,0:T(8,128)} custom-call(bf16[128,32,128]{2,1,0:T(8,128)(2,1)} %copy-done.3, bf16[64,32,128]{2,1,0:T(8,128)(2,1)} %copy-done, bf16[4,64,32,128]{3,2,1,0:T(8,128)(2,1)} %all-to-all-done.refs_2_.refs_1_), custom_call_target="tpu_custom_call" | custom-call | flops 1 | bytes 1 | tf_op jit(solution)/shard_map/gram_blocks/pallas_call | solution.py:227
  112.0 4.3 %all-to-all-start.1 = ((f32[8,160,128]{2,1,0:T(8,128)}), f32[8,160,128]{2,1,0:T(8,128)}, u32[]{:S(2)}, u32[]{:S(2)}) async-start(f32[8,160,128]{2,1,0:T(8,128)} %bitcast.16), calls=%async_computation.1 | async-start | bytes 1310720 | tf_op jit(solution)/shard_map/all_to_all | solution.py:580
  116.4 1.9 collective-permute-start.10
  118.3 1.4 collective-permute-start.11
  119.8 8.4 %all-to-all-done.1 = f32[8,160,128]{2,1,0:T(8,128)} async-done(((f32[8,160,128]{2,1,0:T(8,128)}), f32[8,160,128]{2,1,0:T(8,128)}, u32[]{:S(2)}, u32[]{:S(2)}) %all-to-all-start.1) | async-done | bytes 655392 | tf_op jit(solution)/shard_map/all_to_all | solution.py:580
  128.1 1.8 sum_pieces.3
  130.0 3.5 %all-to-all-start.2 = ((f32[4,160,128]{2,1,0:T(8,128)}), f32[4,160,128]{2,1,0:T(8,128)S(1)}, u32[]{:S(2)}, u32[]{:S(2)}) async-start(f32[4,160,128]{2,1,0:T(8,128)} %bitcast.17), calls=%async_computation.2 | async-start | bytes 655360 | tf_op jit(solution)/shard_map/all_to_all | solution.py:580
  133.4 38.0 %collective-permute-done.10.refs_4_ = bf16[128,32,128]{2,1,0:T(8,128)(2,1)S(1)} collective-permute-done((bf16[128,32,128]{2,1,0:T(8,128)(2,1)}, bf16[128,32,128]{2,1,0:T(8,128)(2,1)S(1)}, u32[]{:S(2)}, u32[]{:S(2)}) %collective-permute-start.10) | collective-permute-done | bytes 1048608 | tf_op jit(solution)/shard_map/ppermute | solution.py:555
  171.5 4.5 %settle.5.refs_0_ = bf16[4,64,32,128]{3,2,1,0:T(8,128)(2,1)} custom-call(f32[640,128]{1,0:T(8,128)S(1)} %bitcast.11, s32[8,128]{1,0:T(8,128)S(1)} %get-tuple-element.34.refs_0_.refs_1_, bf16[128,32,128]{2,1,0:T(8,128)(2,1)S(1)} %get-tuple-element.45.refs_2_, bf16[128,32,128]{2,1,0:T(8,128)(2,1)S(1)} %copy-done.4, ...), custom_call_target="tpu_custom_call" | custom-call | flops 1 | bytes 1 | tf_op jit(solution)/shard_map/settle/pallas_call | solution.py:162
  176.0 3.6 %all-to-all-start.3 = ((bf16[4,64,32,128]{3,2,1,0:T(8,128)(2,1)}), bf16[4,64,32,128]{3,2,1,0:T(8,128)(2,1)S(1)}, u32[]{:S(2)}, u32[]{:S(2)}) async-start(bf16[4,64,32,128]{3,2,1,0:T(8,128)(2,1)} %settle.5.refs_0_), calls=%async_computation.3 | async-start | bytes 4194304 | tf_op jit(solution)/shard_map/all_to_all | solution.py:580
  179.6 1.6 sum_pieces.4
  181.2 10.2 %all_gather.3 = f32[1280,128]{1,0:T(8,128)S(1)} all-gather(f32[160,128]{1,0:T(8,128)} %sum_pieces.4), channel_id=1, replica_groups=mesh['space'=8,'snap'=4] {'space'}, dimensions={0}, use_global_device_ids=true | all-gather | bytes 737280 | tf_op jit(solution)/shard_map/all_gather | solution.py:611
  191.5 4.9 %factor.4.refs_0_ = f32[4,8,128,128]{3,2,1,0:T(8,128)S(1)} custom-call(f32[10,128,128]{2,1,0:T(8,128)S(1)} %bitcast.13), custom_call_target="tpu_custom_call" | custom-call | flops 1 | bytes 1 | tf_op jit(solution)/shard_map/factor/pallas_call | solution.py:404
  196.4 4.8 %factor.5.refs_0_ = f32[4,8,128,128]{3,2,1,0:T(8,128)S(1)} custom-call(f32[4,8,128,128]{3,2,1,0:T(8,128)S(1)} %factor.4.refs_0_), custom_call_target="tpu_custom_call", output_to_operand_aliasing={{}: (0, {})} | custom-call | flops 1 | bytes 1 | tf_op jit(solution)/shard_map/factor/pallas_call | solution.py:404
  201.2 4.6 %factor.6.refs_0_ = f32[4,8,128,128]{3,2,1,0:T(8,128)S(1)} custom-call(f32[4,8,128,128]{3,2,1,0:T(8,128)S(1)} %factor.5.refs_0_), custom_call_target="tpu_custom_call", output_to_operand_aliasing={{}: (0, {})} | custom-call | flops 1 | bytes 1 | tf_op jit(solution)/shard_map/factor/pallas_call | solution.py:404
  205.8 5.6 %factor.7 = (f32[512,512]{1,0:T(8,128)}, f32[512,512]{1,0:T(8,128)S(1)}, bf16[512,512]{1,0:T(8,128)(2,1)S(1)}, bf16[512,512]{1,0:T(8,128)(2,1)S(1)}, bf16[512,512]{1,0:T(8,128)(2,1)S(1)}) custom-call(f32[4,8,128,128]{3,2,1,0:T(8,128)S(1)} %factor.6.refs_0_), custom_call_target="tpu_custom_call" | custom-call | flops 1 | bytes 1 | tf_op jit(solution)/shard_map/factor/pallas_call | solution.py:404
  211.4 0.8 copy-done.9
  212.2 0.8 copy-done.10
  213.0 0.8 copy-done.11
  213.8 9.0 %basis.1.refs_0_ = f32[64,32,512]{2,1,0:T(8,128)} custom-call(bf16[64,32,128]{2,1,0:T(8,128)(2,1)} %copy-done, bf16[4,64,32,128]{3,2,1,0:T(8,128)(2,1)} %all-to-all-done.refs_2_.refs_1_, bf16[512,512]{1,0:T(8,128)(2,1)} %copy-done.9, bf16[512,512]{1,0:T(8,128)(2,1)} %copy-done.10, bf16[512,512]{1,0:T(8,128)(2,1)} %copy-done.11), custom_call_target="tpu_custom_call" | custom-call | flops 1 | bytes 1 | tf_op jit(solution)/shard_map/basis/pallas_call | solution.py:457
  222.8 5.1 %all-to-all-done.3.refs_3_ = bf16[4,64,32,128]{3,2,1,0:T(8,128)(2,1)S(1)} async-done(((bf16[4,64,32,128]{3,2,1,0:T(8,128)(2,1)}), bf16[4,64,32,128]{3,2,1,0:T(8,128)(2,1)S(1)}, u32[]{:S(2)}, u32[]{:S(2)}) %all-to-all-start.3) | async-done | bytes 2097184 | tf_op jit(solution)/shard_map/all_to_all | solution.py:580
  227.8 1.3 copy-done.15
  229.2 5.2 %cross_sum.1 = f32[512,512]{1,0:T(8,128)} custom-call(f32[64,32,512]{2,1,0:T(8,128)} %basis.1.refs_0_, bf16[64,32,128]{2,1,0:T(8,128)(2,1)} %copy-done, bf16[4,64,32,128]{3,2,1,0:T(8,128)(2,1)} %all-to-all-done.refs_2_.refs_1_, bf16[4,64,32,128]{3,2,1,0:T(8,128)(2,1)} %copy-done.15), custom_call_target="tpu_custom_call" | custom-call | flops 1 | bytes 1 | tf_op jit(solution)/shard_map/cross_sum/pallas_call | solution.py:268
  234.4 19.6 %all_to_all.43 = f32[8,64,512]{2,1,0:T(8,128)} all-to-all(f32[8,64,512]{2,1,0:T(8,128)} %bitcast.14), channel_id=1, replica_groups=mesh['space'=8,'snap'=4] {'space'}, dimensions={0} | all-to-all | bytes 2097152 | tf_op jit(solution)/shard_map/all_to_all | solution.py:580
  253.9 1.9 sum_pieces.5.refs_0_
  255.9 5.2 %collective-permute-done.12.refs_1_ = f32[64,512]{1,0:T(8,128)S(1)} collective-permute-done((f32[64,512]{1,0:T(8,128)}, f32[64,512]{1,0:T(8,128)S(1)}, u32[]{:S(2)}, u32[]{:S(2)}) %collective-permute-start.12) | collective-permute-done | bytes 131104 | tf_op jit(solution)/shard_map/ppermute | solution.py:555
  261.7 1.6 add.2.refs_0_
  263.4 7.1 %collective-permute-done.13.refs_1_ = f32[64,512]{1,0:T(8,128)S(1)} collective-permute-done((f32[64,512]{1,0:T(8,128)}, f32[64,512]{1,0:T(8,128)S(1)}, u32[]{:S(2)}, u32[]{:S(2)}) %collective-permute-start.13) | collective-permute-done | bytes 131104 | tf_op jit(solution)/shard_map/ppermute | solution.py:555
  271.1 1.6 add.3.refs_0_
  272.7 1.9 collective-permute-start.16
  274.6 1.8 collective-permute-start.15
  276.4 2.9 %collective-permute-done.16.refs_3_ = f32[64,512]{1,0:T(8,128)S(1)} collective-permute-done((f32[64,512]{1,0:T(8,128)}, f32[64,512]{1,0:T(8,128)S(1)}, u32[]{:S(2)}, u32[]{:S(2)}) %collective-permute-start.16) | collective-permute-done | bytes 131104 | tf_op jit(solution)/shard_map/ppermute | solution.py:555
  279.4 2.0 collective-permute-done.15.refs_2_
  282.6 1.9 join.1.refs_1_
  284.5 2.1 collective-permute-done.17.refs_2_
  286.7 1.0 copy-done.8
  287.7 2.9 project.1
  (46 shorter events, 4.3 us)
Async XLA Ops:
  0.6 2.2 copy-start.1
  2.8 0.7 copy-start.12
  3.5 12.5 %copy-start.2 = (bf16[128,128,128]{2,1,0:T(8,128)(2,1)S(1)}, bf16[128,128,128]{2,1,0:T(8,128)(2,1)}, u32[]{:S(2)}) copy-start(bf16[128,128,128]{2,1,0:T(8,128)(2,1)} %param.4) | copy-start | bytes 12582916
  7.1 3.9 %collective-permute-start = (bf16[196,32,128]{2,1,0:T(8,128)(2,1)S(1)}, bf16[196,32,128]{2,1,0:T(8,128)(2,1)S(1)}, u32[]{:S(2)}, u32[]{:S(2)}) collective-permute-start(bf16[196,32,128]{2,1,0:T(8,128)(2,1)S(1)} %get-tuple-element.29), channel_id=1, source_target_pairs={{0,4},{4,0},{8,12},{12,8},{16,20},{20,16},{24,28},{28,24},{1,5},{5... | collective-permute-start | bytes 4816904 | tf_op jit(solution)/shard_map/ppermute | solution.py:555
  11.2 20.8 %collective-permute-start.1 = (bf16[98,32,128]{2,1,0:T(8,128)(2,1)S(1)}, bf16[98,32,128]{2,1,0:T(8,128)(2,1)S(1)}, u32[]{:S(2)}, u32[]{:S(2)}) collective-permute-start(bf16[98,32,128]{2,1,0:T(8,128)(2,1)S(1)} %get-tuple-element.31), channel_id=1, source_target_pairs={{0,8},{4,12},{8,0},{12,4},{16,24},{20,28},{24,16},{28,20},{1,9},{5... | collective-permute-start | bytes 2408456 | tf_op jit(solution)/shard_map/ppermute | solution.py:555
  12.6 36.9 %collective-permute-start.2 = (bf16[98,32,128]{2,1,0:T(8,128)(2,1)S(1)}, bf16[98,32,128]{2,1,0:T(8,128)(2,1)S(1)}, u32[]{:S(2)}, u32[]{:S(2)}) collective-permute-start(bf16[98,32,128]{2,1,0:T(8,128)(2,1)S(1)} %get-tuple-element.32), channel_id=1, source_target_pairs={{0,16},{4,20},{8,24},{12,28},{16,0},{20,4},{24,8},{28,12},{1,17},{... | collective-permute-start | bytes 2408456 | tf_op jit(solution)/shard_map/ppermute | solution.py:555
  15.1 35.9 %collective-permute-start.3 = (bf16[98,32,128]{2,1,0:T(8,128)(2,1)S(1)}, bf16[98,32,128]{2,1,0:T(8,128)(2,1)S(1)}, u32[]{:S(2)}, u32[]{:S(2)}) collective-permute-start(bf16[98,32,128]{2,1,0:T(8,128)(2,1)S(1)} %get-tuple-element.33), channel_id=1, source_target_pairs={{0,24},{4,28},{8,16},{12,20},{16,8},{20,12},{24,0},{28,4},{1,25},{... | collective-permute-start | bytes 2408456 | tf_op jit(solution)/shard_map/ppermute | solution.py:555
  20.8 1.4 copy-start.6
  22.2 42.9 %collective-permute-start.8 = (bf16[256,32,128]{2,1,0:T(8,128)(2,1)}, bf16[256,32,128]{2,1,0:T(8,128)(2,1)}, u32[]{:S(2)}, u32[]{:S(2)}) collective-permute-start(bf16[256,32,128]{2,1,0:T(8,128)(2,1)} %get-tuple-element.43), channel_id=1, source_target_pairs={{0,4},{4,0},{8,12},{12,8},{16,20},{20,16},{24,28},{28,24},{1,5},{5... | collective-permute-start | bytes 6291464 | tf_op jit(solution)/shard_map/ppermute | solution.py:555
  54.7 52.7 %all-to-all-start = ((bf16[4,64,32,128]{3,2,1,0:T(8,128)(2,1)}), bf16[4,64,32,128]{3,2,1,0:T(8,128)(2,1)}, u32[]{:S(2)}, u32[]{:S(2)}) async-start(bf16[4,64,32,128]{3,2,1,0:T(8,128)(2,1)} %get-tuple-element.41.refs_0_), calls=%async_computation | async-start | bytes 4194304 | tf_op jit(solution)/shard_map/all_to_all | solution.py:580
  59.5 16.4 %copy-start.7 = (bf16[256,32,128]{2,1,0:T(8,128)(2,1)S(1)}, bf16[256,32,128]{2,1,0:T(8,128)(2,1)}, u32[]{:S(2)}) copy-start(bf16[256,32,128]{2,1,0:T(8,128)(2,1)} %copy-done.6) | copy-start | bytes 6291460
  59.5 1.9 collective-permute-start.4
  61.5 9.2 %collective-permute-start.5 = (bf16[32,32,128]{2,1,0:T(8,128)(2,1)S(1)}, bf16[32,32,128]{2,1,0:T(8,128)(2,1)S(1)}, u32[]{:S(2)}, u32[]{:S(2)}) collective-permute-start(bf16[32,32,128]{2,1,0:T(8,128)(2,1)S(1)} %get-tuple-element.38), channel_id=1, source_target_pairs={{0,8},{4,12},{8,0},{12,4},{16,24},{20,28},{24,16},{28,20},{1,9},{5... | collective-permute-start | bytes 786440 | tf_op jit(solution)/shard_map/ppermute | solution.py:555
  62.2 12.9 %collective-permute-start.6 = (bf16[32,32,128]{2,1,0:T(8,128)(2,1)S(1)}, bf16[32,32,128]{2,1,0:T(8,128)(2,1)S(1)}, u32[]{:S(2)}, u32[]{:S(2)}) collective-permute-start(bf16[32,32,128]{2,1,0:T(8,128)(2,1)S(1)} %get-tuple-element.39), channel_id=1, source_target_pairs={{0,16},{4,20},{8,24},{12,28},{16,0},{20,4},{24,8},{28,12},{1,17},{... | collective-permute-start | bytes 786440 | tf_op jit(solution)/shard_map/ppermute | solution.py:555
  63.9 12.0 %collective-permute-start.7 = (bf16[32,32,128]{2,1,0:T(8,128)(2,1)S(1)}, bf16[32,32,128]{2,1,0:T(8,128)(2,1)S(1)}, u32[]{:S(2)}, u32[]{:S(2)}) collective-permute-start(bf16[32,32,128]{2,1,0:T(8,128)(2,1)S(1)} %get-tuple-element.40), channel_id=1, source_target_pairs={{0,24},{4,28},{8,16},{12,20},{16,8},{20,12},{24,0},{28,4},{1,25},{... | collective-permute-start | bytes 786440 | tf_op jit(solution)/shard_map/ppermute | solution.py:555
  77.8 1.0 copy-start.14
  78.8 3.4 %copy-start.13 = (bf16[128,32,128]{2,1,0:T(8,128)(2,1)}, bf16[128,32,128]{2,1,0:T(8,128)(2,1)S(1)}, u32[]{:S(2)}) copy-start(bf16[128,32,128]{2,1,0:T(8,128)(2,1)S(1)} %get-tuple-element.47) | copy-start | bytes 3145732
  78.8 24.5 %collective-permute-start.9 = (bf16[128,32,128]{2,1,0:T(8,128)(2,1)S(1)}, bf16[128,32,128]{2,1,0:T(8,128)(2,1)S(1)}, u32[]{:S(2)}, u32[]{:S(2)}) collective-permute-start(bf16[128,32,128]{2,1,0:T(8,128)(2,1)S(1)} %get-tuple-element.44), channel_id=1, source_target_pairs={{0,8},{4,12},{8,0},{12,4},{16,24},{20,28},{24,16},{28,20},{1,9},{5... | collective-permute-start | bytes 3145736 | tf_op jit(solution)/shard_map/ppermute | solution.py:555
  82.2 0.8 copy-start
  103.2 4.1 %copy-start.3 = (bf16[128,32,128]{2,1,0:T(8,128)(2,1)}, bf16[128,32,128]{2,1,0:T(8,128)(2,1)S(1)}, u32[]{:S(2)}) copy-start(bf16[128,32,128]{2,1,0:T(8,128)(2,1)S(1)} %collective-permute-done.9.refs_0_.refs_3_) | copy-start | bytes 3145732
  112.0 59.5 %copy-start.4 = (bf16[128,32,128]{2,1,0:T(8,128)(2,1)S(1)}, bf16[128,32,128]{2,1,0:T(8,128)(2,1)}, u32[]{:S(2)}) copy-start(bf16[128,32,128]{2,1,0:T(8,128)(2,1)} %copy-done.3) | copy-start | bytes 3145732
  112.0 16.1 %all-to-all-start.1 = ((f32[8,160,128]{2,1,0:T(8,128)}), f32[8,160,128]{2,1,0:T(8,128)}, u32[]{:S(2)}, u32[]{:S(2)}) async-start(f32[8,160,128]{2,1,0:T(8,128)} %bitcast.16), calls=%async_computation.1 | async-start | bytes 1310720 | tf_op jit(solution)/shard_map/all_to_all | solution.py:580
  116.4 55.1 %collective-permute-start.10 = (bf16[128,32,128]{2,1,0:T(8,128)(2,1)}, bf16[128,32,128]{2,1,0:T(8,128)(2,1)S(1)}, u32[]{:S(2)}, u32[]{:S(2)}) collective-permute-start(bf16[128,32,128]{2,1,0:T(8,128)(2,1)} %copy-done.14), channel_id=1, source_target_pairs={{0,16},{4,20},{8,24},{12,28},{16,0},{20,4},{24,8},{28,12},{1,17},{... | collective-permute-start | bytes 3145736 | tf_op jit(solution)/shard_map/ppermute | solution.py:555
  118.3 53.2 %collective-permute-start.11 = (bf16[128,32,128]{2,1,0:T(8,128)(2,1)}, bf16[128,32,128]{2,1,0:T(8,128)(2,1)}, u32[]{:S(2)}, u32[]{:S(2)}) collective-permute-start(bf16[128,32,128]{2,1,0:T(8,128)(2,1)} %copy-done.13), channel_id=1, source_target_pairs={{0,24},{4,28},{8,16},{12,20},{16,8},{20,12},{24,0},{28,4},{1,25},{... | collective-permute-start | bytes 3145736 | tf_op jit(solution)/shard_map/ppermute | solution.py:555
  130.0 41.5 %all-to-all-start.2 = ((f32[4,160,128]{2,1,0:T(8,128)}), f32[4,160,128]{2,1,0:T(8,128)S(1)}, u32[]{:S(2)}, u32[]{:S(2)}) async-start(f32[4,160,128]{2,1,0:T(8,128)} %bitcast.17), calls=%async_computation.2 | async-start | bytes 655360 | tf_op jit(solution)/shard_map/all_to_all | solution.py:580
  171.5 4.5 %copy-start.5 = (f32[4,160,128]{2,1,0:T(8,128)}, f32[4,160,128]{2,1,0:T(8,128)S(1)}, u32[]{:S(2)}) copy-start(f32[4,160,128]{2,1,0:T(8,128)S(1)} %all-to-all-done.2) | copy-start | bytes 983044
  176.0 51.9 %all-to-all-start.3 = ((bf16[4,64,32,128]{3,2,1,0:T(8,128)(2,1)}), bf16[4,64,32,128]{3,2,1,0:T(8,128)(2,1)S(1)}, u32[]{:S(2)}, u32[]{:S(2)}) async-start(bf16[4,64,32,128]{3,2,1,0:T(8,128)(2,1)} %settle.5.refs_0_), calls=%async_computation.3 | async-start | bytes 4194304 | tf_op jit(solution)/shard_map/all_to_all | solution.py:580
  211.4 0.8 copy-start.9
  212.2 0.8 copy-start.10
  213.0 0.8 copy-start.11
  227.8 1.3 copy-start.15
  255.9 5.2 %collective-permute-start.12 = (f32[64,512]{1,0:T(8,128)}, f32[64,512]{1,0:T(8,128)S(1)}, u32[]{:S(2)}, u32[]{:S(2)}) collective-permute-start(f32[64,512]{1,0:T(8,128)} %sum_pieces.5.refs_0_), channel_id=1, source_target_pairs={{0,1},{1,0},{2,3},{3,2},{4,5},{5,4},{6,7},{7,6},{8,9},{9,8},{10,11... | collective-permute-start | bytes 393224 | tf_op jit(solution)/shard_map/ppermute | solution.py:555
  261.1 0.7 copy-start.16
  263.4 7.1 %collective-permute-start.13 = (f32[64,512]{1,0:T(8,128)}, f32[64,512]{1,0:T(8,128)S(1)}, u32[]{:S(2)}, u32[]{:S(2)}) collective-permute-start(f32[64,512]{1,0:T(8,128)} %add.2.refs_0_), channel_id=1, source_target_pairs={{0,2},{1,3},{2,0},{3,1},{4,6},{5,7},{6,4},{7,5},{8,10},{9,11},{10,... | collective-permute-start | bytes 393224 | tf_op jit(solution)/shard_map/ppermute | solution.py:555
  270.4 0.7 copy-start.17
  272.7 6.6 %collective-permute-start.16 = (f32[64,512]{1,0:T(8,128)}, f32[64,512]{1,0:T(8,128)S(1)}, u32[]{:S(2)}, u32[]{:S(2)}) collective-permute-start(f32[64,512]{1,0:T(8,128)} %add.3.refs_0_), channel_id=1, source_target_pairs={{0,24},{4,28},{8,16},{12,20},{16,8},{20,12},{24,0},{28,4},{1,25},{... | collective-permute-start | bytes 393224 | tf_op jit(solution)/shard_map/ppermute | solution.py:555
  274.6 6.7 %collective-permute-start.15 = (f32[64,512]{1,0:T(8,128)}, f32[64,512]{1,0:T(8,128)S(1)}, u32[]{:S(2)}, u32[]{:S(2)}) collective-permute-start(f32[64,512]{1,0:T(8,128)} %add.3.refs_0_), channel_id=1, source_target_pairs={{0,16},{4,20},{8,24},{12,28},{16,0},{20,4},{24,8},{28,12},{1,17},{... | collective-permute-start | bytes 393224 | tf_op jit(solution)/shard_map/ppermute | solution.py:555
  276.4 5.2 %collective-permute-start.14 = (f32[64,512]{1,0:T(8,128)}, f32[64,512]{1,0:T(8,128)S(1)}, u32[]{:S(2)}, u32[]{:S(2)}) collective-permute-start(f32[64,512]{1,0:T(8,128)} %add.3.refs_0_), channel_id=1, source_target_pairs={{0,8},{4,12},{8,0},{12,4},{16,24},{20,28},{24,16},{28,20},{1,9},{5... | collective-permute-start | bytes 393224 | tf_op jit(solution)/shard_map/ppermute | solution.py:555
  279.4 2.2 copy-start.18
  281.3 0.6 copy-start.19
  282.0 0.7 copy-start.20
  284.5 2.1 collective-permute-start.17
  286.7 1.0 copy-start.8

commit v14 on v8

--- a/solution.py
+++ b/solution.py
@@ -111,8 +111,7 @@
     )(*after, same, other)
 
 
-def settle_kernel(chips, capacity, parts, part, *refs):
-    first = part is None
+def settle_kernel(chips, capacity, parts, first, *refs):
     if first:
         moved_refs, (out_ref, meta_ref, ids_ref) = refs[:chips], refs[chips:]
         span = moved_refs[0].shape[0] // CORES
@@ -125,7 +124,7 @@
     else:
         meta_ref, moved_refs, out_refs = refs[0], refs[1 : 1 + chips], refs[1 + chips :]
         span = moved_refs[0].shape[0] // CORES
-        shares = len(out_refs)
+        shares = len(out_refs) // parts
     tiles = shares * parts
     rows = moved_refs[0].shape[1]
     mine = lax.axis_index("snap")
@@ -144,16 +143,17 @@
                             cells = slice(k * rows, (k + 1) * rows)
                             out_ref[share, block, cells] = moved_ref[at + share * parts + k]
                     else:
-                        cells = moved_ref[at + (mine ^ share) * parts + part]
-                        out_refs[share][block] = cells
+                        for k in range(parts):
+                            cells = moved_ref[at + (mine ^ share) * parts + k]
+                            out_refs[k * shares + share][block] = cells
 
             return 0
 
         lax.fori_loop(0, capacity, place, 0, unroll=4)
 
 
-def settle(meta, moved, capacity, per_slab, shares, parts, part, after):
-    first = part is None
+def settle(meta, moved, capacity, per_slab, shares, parts, after):
+    first = meta is None
     chips = len(moved)
     rows, width = moved[0].shape[1:]
     if first:
@@ -162,12 +162,12 @@
             jax.ShapeDtypeStruct((chips * CORES, TILE), jnp.int32),
         )
     else:
-        pieces = (jax.ShapeDtypeStruct((per_slab, rows, width), moved[0].dtype),) * shares
-    return pl.pallas_call(
-        lambda *refs: settle_kernel(chips, capacity, parts, part, *refs[len(after) :]),
+        pieces = (jax.ShapeDtypeStruct((per_slab, rows, width), moved[0].dtype),) * (shares * parts)
+    return pl.pallas_call(
+        lambda *refs: settle_kernel(chips, capacity, parts, first, *refs[len(after) :]),
         out_shape=pieces,
         in_specs=[ANY] * len(after) + ([] if first else [SMEM]) + [VMEM] * chips,
-        out_specs=(VMEM, SMEM) if first else (VMEM,) * shares,
+        out_specs=(VMEM, SMEM) if first else (VMEM,) * len(pieces),
         scratch_shapes=[pltpu.VMEM((chips * CORES, TILE), jnp.int32)] if first else [],
         compiler_params=pltpu.CompilerParams(vmem_limit_bytes=VMEM_BYTES),
         cost_estimate=cost(
@@ -512,15 +512,15 @@
         refs[-1][i * rows : (i + 1) * rows] = ref[...]
 
 
-def join(values):
+def join(values, after):
     rows, lanes = values[0].shape
     return pl.pallas_call(
-        join_kernel,
+        lambda *refs: join_kernel(*refs[len(after) :]),
         out_shape=jax.ShapeDtypeStruct((len(values) * rows, lanes), values[0].dtype),
-        in_specs=[VMEM] * len(values),
+        in_specs=[ANY] * len(after) + [VMEM] * len(values),
         out_specs=VMEM,
         name="join",
-    )(*values)
+    )(*after, *values)
 
 
 def projection_kernel(slabs, divisor, inverse_ref, same_ref, other_ref, out_ref, cross_ref):
@@ -581,8 +581,8 @@
     def to_rows(pieces):
         return [pieces[0]] + [swap(pieces[r], "snap", r) for r in range(1, shares)]
 
-    def place(meta, moved, part, after):
-        return settle(meta, moved, slots // slabs, per_slab, shares, parts, part, after)
+    def place(meta, moved, after):
+        return settle(meta, moved, slots // slabs, per_slab, shares, parts, after)
 
     def to_pieces(value):
         return lax.all_to_all(value, "space", split_axis=0, concat_axis=0, tiled=True)
@@ -594,36 +594,36 @@
             hop *= 2
 
     moved_x = to_chips(merged(packed(owned_x, True), []))
-    moved_y = to_chips(merged(packed(owned_y, False), moved_x[1:3]))
-    pieces, meta = place(None, moved_x, None, [])
+    joined_y = merged(packed(owned_y, False), moved_x[1:3])
+    moved_y = to_chips(joined_y)
+    pieces, meta = place(None, moved_x, joined_y[:1])
     x_cells = lax.all_to_all(pieces, "snap", split_axis=0, concat_axis=0, tiled=True)
 
     gram_local = gram_blocks(x_cells, moved_y[1:2])
     gram = to_pieces(gram_local.reshape(pairs * TILE, TILE))
-    pieces = place(meta, moved_y, 0, [gram_local])
-    y_cells = [to_rows(pieces)]
-    gram = sum_pieces(gram, slabs, pieces[:1])
+    pieces = place(meta, moved_y, [gram_local])
+    y_cells = [to_rows(pieces[part * shares : (part + 1) * shares]) for part in range(parts)]
+    gram = sum_pieces(gram, slabs, y_cells[0][2:])
     for hop in hops():
-        gram = add(gram, swap(gram, "snap", hop), y_cells[0][hop : hop + 1])
+        gram = add(gram, swap(gram, "snap", hop), [] if hop == 1 else y_cells[1][2:3])
     gram = lax.all_gather(gram, "space", axis=0, tiled=True)
-    for part in range(1, parts):
-        pieces = place(meta, moved_y, part, y_cells[-1][1:3])
-        y_cells.append(to_rows(pieces))
-
-    steps = factor_steps(gram.reshape(pairs, TILE, TILE), tiles, rows_total, pieces[:1])
+
+    steps = factor_steps(gram.reshape(pairs, TILE, TILE), tiles, rows_total, [])
     state = next(steps)
-    for _ in range(tiles - 2):
+    for _ in range(tiles - 3):
         state = steps.send([])
     cross_local = cross_sum(x_cells, y_cells, [state])
-    cross = to_pieces(cross_local)
-    r_factor, inverse, *terms = steps.send([cross_local])
-
-    q_basis = basis(x_cells, terms, 0, 2, None, [])
-    cross = sum_pieces(cross, slabs, [q_basis])
+    state = steps.send([cross_local])
+    cross = sum_pieces(to_pieces(cross_local), slabs, [state])
+    r_factor, inverse, *terms = steps.send([cross])
+    tied = [r_factor]
+    for hop in hops():
+        cross = add(cross, swap(cross, "snap", hop), tied)
+        if hop == 1:
+            q_basis = basis(x_cells, terms, 0, 2, None, [cross])
+            tied = [q_basis]
     q_basis = basis(x_cells, terms, 1, 2, q_basis, [cross])
-    for hop in hops():
-        cross = add(cross, swap(cross, "snap", hop), [q_basis] if hop == 1 else [])
-    same = join([cross] + [swap(cross, "space", m) for m in range(CORES, slabs, CORES)])
+    same = join([cross] + [swap(cross, "space", m) for m in range(CORES, slabs, CORES)], [q_basis])
     projection = project(inverse, same, swap(same, "space", 1), slabs, math.sqrt(rows_total))
     return q_basis, r_factor, projection
 

time: 258 us -> 274 us (1.062)
  waiting for transfers between devices: 107 us -> 128 us
  Pallas kernels: 67.8 us -> 58.9 us
  starting transfers between devices: 40.4 us -> 43.3 us
    ppermute x22, waiting for transfers between devices: 90.3 us -> 101 us  [swap(): lax.ppermute(value, axis, [(i, i ^ mask) for i in range(lax.axis_size(axi...]
    all_to_all x1, waiting for transfers between devices: 13.2 us -> 19.7 us  [body(): lax.all_to_all(pieces, 'snap', split_axis=0, concat_axis=0, tiled=True)]
    pallas_call x4 -> x3, Pallas kernels: 13.1 us -> 8.87 us  [the longest x2 6.91 us: settle(): pl.pallas_call(lambda *refs: settle_kernel(chips, capacity, parts, first,...]
    all_to_all x2, waiting for transfers between devices: 3.91 us -> 7.64 us  [to_pieces(): lax.all_to_all(value, 'space', split_axis=0, concat_axis=0, tiled=True)]
    ppermute x22, starting transfers between devices: 27 us -> 30.5 us  [swap(): lax.ppermute(value, axis, [(i, i ^ mask) for i in range(lax.axis_size(axi...]
    unnamed x82 -> x90, local copies, waits for them, and re-layouts: 29.5 us -> 30.2 us
  transfers between devices with their start and end apart: 25 -> 25, of which waited for: 14 -> 10; matrix products, arithmetic and copies ran while one was open for 0% -> 0% of each run, Pallas kernels for 20% -> 15%
where the time goes in v14:
time: 274 us; the launch traced here: 272 us
  waiting for transfers between devices  128 us (47%)
  Pallas kernels  58.9 us (21%)
  starting transfers between devices  43.3 us (16%)
  local copies, waits for them, and re-layouts  30.2 us (11%)
  blocking collectives  10.8 us (4%)
    ppermute x22, waiting for transfers between devices, swap(): lax.ppermute(value, axis, [(i, i ^ mask) for i in range(lax.axis_size(axi...  101 us
    ppermute x22, starting transfers between devices, swap(): lax.ppermute(value, axis, [(i, i ^ mask) for i in range(lax.axis_size(axi...  30.5 us
    unnamed x90, local copies, waits for them, and re-layouts  30.2 us
    pallas_call x4, Pallas kernels, factor_call(): pl.pallas_call(lambda *refs: kernel(*refs[len(after):]), out_shape=out_sh...  19.7 us
    all_to_all x1, waiting for transfers between devices, body(): lax.all_to_all(pieces, 'snap', split_axis=0, concat_axis=0, tiled=True)  19.7 us
    all_gather x1, blocking collectives, body(): gram = lax.all_gather(gram, 'space', axis=0, tiled=True)  10.8 us
    all_to_all x2, starting transfers between devices, to_pieces(): lax.all_to_all(value, 'space', split_axis=0, concat_axis=0, tiled=True)  7.98 us
    all_to_all x2, waiting for transfers between devices, to_pieces(): lax.all_to_all(value, 'space', split_axis=0, concat_axis=0, tiled=True)  7.64 us
  transfers between devices with their start and end apart: 25, of which 10 were waited for; matrix products, arithmetic and copies ran while one was open for 0% of the time, Pallas kernels for 15%

profile of v14, /device:TPU:0, one launch (start us, length us, event | category | flops | bytes accessed | tf_op | source)
XLA Modules:
  0.0 272.4 jit_solution(16582488265985173422)
XLA Ops:
  0.6 2.2 copy-done.4
  3.5 2.4 pack.2
  6.2 2.4 pack.3
  8.7 1.4 collective-permute-done.refs_1_
  10.4 4.3 %collective-permute-start.1 = (bf16[258,16,128]{2,1,0:T(8,128)(2,1)S(1)}, bf16[258,16,128]{2,1,0:T(8,128)(2,1)S(1)}, u32[]{:S(2)}, u32[]{:S(2)}) collective-permute-start(bf16[258,16,128]{2,1,0:T(8,128)(2,1)S(1)} %get-tuple-element.32), channel_id=1, source_target_pairs={{0,8},{4,12},{8,0},{12,4},{16,24},{20,28},{24,16},{28,20},{1,9},{5... | collective-permute-start | bytes 3170312 | tf_op jit(solution)/shard_map/ppermute | solution.py:557
  14.7 1.3 collective-permute-start.2
  16.2 22.6 %collective-permute-done.1.refs_0_.refs_2_ = bf16[258,16,128]{2,1,0:T(8,128)(2,1)S(1)} collective-permute-done((bf16[258,16,128]{2,1,0:T(8,128)(2,1)S(1)}, bf16[258,16,128]{2,1,0:T(8,128)(2,1)S(1)}, u32[]{:S(2)}, u32[]{:S(2)}) %collective-permute-start.1) | collective-permute-done | bytes 1056800 | tf_op jit(solution)/shard_map/ppermute | solution.py:557
  38.8 23.6 %collective-permute-done.2.refs_1_.refs_3_ = bf16[258,16,128]{2,1,0:T(8,128)(2,1)S(1)} collective-permute-done((bf16[258,16,128]{2,1,0:T(8,128)(2,1)S(1)}, bf16[258,16,128]{2,1,0:T(8,128)(2,1)S(1)}, u32[]{:S(2)}, u32[]{:S(2)}) %collective-permute-start.2) | collective-permute-done | bytes 1056800 | tf_op jit(solution)/shard_map/ppermute | solution.py:557
  62.7 2.8 %settle.2 = (bf16[4,64,32,128]{3,2,1,0:T(8,128)(2,1)S(1)}, s32[8,128]{1,0:T(8,128)S(1)}) custom-call(bf16[256,16,128]{2,1,0:T(8,128)(2,1)S(1)} %get-tuple-element.37.refs_0_.refs_2_, bf16[258,16,128]{2,1,0:T(8,128)(2,1)S(1)} %get-tuple-element.38.refs_1_, bf16[258,16,128]{2,1,0:T(8,128)(2,1)S(1)} %collective-permute-done.1.refs_0_.refs_2_, ...), custom_call_target="tpu_custom_call" | custom-call | bytes 4227072 | tf_op jit(solution)/shard_map/settle/pallas_call | solution.py:166
  65.6 1.3 copy-done.8
  66.9 4.9 %all-to-all-start = ((bf16[4,64,32,128]{3,2,1,0:T(8,128)(2,1)}), bf16[4,64,32,128]{3,2,1,0:T(8,128)(2,1)S(1)}, u32[]{:S(2)}, u32[]{:S(2)}) async-start(bf16[4,64,32,128]{3,2,1,0:T(8,128)(2,1)} %copy-done.8), calls=%async_computation | async-start | bytes 4194304 | tf_op jit(solution)/shard_map/all_to_all | solution.py:600
  72.5 1.2 collective-permute-start.6
  73.6 1.6 collective-permute-start.7
  75.2 22.8 %collective-permute-done.4.refs_0_.refs_3_ = bf16[256,16,128]{2,1,0:T(8,128)(2,1)S(1)} collective-permute-done((bf16[256,16,128]{2,1,0:T(8,128)(2,1)}, bf16[256,16,128]{2,1,0:T(8,128)(2,1)S(1)}, u32[]{:S(2)}, u32[]{:S(2)}) %collective-permute-start.4) | collective-permute-done | bytes 1048608 | tf_op jit(solution)/shard_map/ppermute | solution.py:557
  98.1 1.0 copy-done.23
  99.0 19.7 %all-to-all-done.refs_1_.refs_2_ = bf16[4,64,32,128]{3,2,1,0:T(8,128)(2,1)S(1)} async-done(((bf16[4,64,32,128]{3,2,1,0:T(8,128)(2,1)}), bf16[4,64,32,128]{3,2,1,0:T(8,128)(2,1)S(1)}, u32[]{:S(2)}, u32[]{:S(2)}) %all-to-all-start) | async-done | bytes 2097184 | tf_op jit(solution)/shard_map/all_to_all | solution.py:600
  118.7 1.2 copy-done.24
  119.9 1.9 gram_blocks.1.refs_0_
  122.7 4.2 %all-to-all-start.1 = ((f32[8,160,128]{2,1,0:T(8,128)}), f32[8,160,128]{2,1,0:T(8,128)}, u32[]{:S(2)}, u32[]{:S(2)}) async-start(f32[8,160,128]{2,1,0:T(8,128)} %bitcast.9), calls=%async_computation.1 | async-start | bytes 1310720 | tf_op jit(solution)/shard_map/all_to_all | solution.py:588
  126.9 1.1 copy-done.7
  128.0 1.2 copy-done.25
  129.2 4.1 %settle.3 = (bf16[64,16,128]{2,1,0:T(8,128)(2,1)S(1)}, bf16[64,16,128]{2,1,0:T(8,128)(2,1)S(1)}, bf16[64,16,128]{2,1,0:T(8,128)(2,1)S(1)}, bf16[64,16,128]{2,1,0...) custom-call(f32[10,128,128]{2,1,0:T(8,128)S(1)} %copy-done.7, ...), custom_call_target="tpu_custom_call" | custom-call | bytes 4194304 | tf_op jit(solution)/shard_map/settle/pallas_call | solution.py:166
  136.2 1.5 collective-permute-start.10
  137.7 2.0 collective-permute-start.8
  139.7 21.7 %collective-permute-done.9.refs_0_.refs_4_ = bf16[64,16,128]{2,1,0:T(8,128)(2,1)S(1)} collective-permute-done((bf16[64,16,128]{2,1,0:T(8,128)(2,1)S(1)}, bf16[64,16,128]{2,1,0:T(8,128)(2,1)S(1)}, u32[]{:S(2)}, u32[]{:S(2)}) %collective-permute-start.9) | collective-permute-done | bytes 262176 | tf_op jit(solution)/shard_map/ppermute | solution.py:557
  162.2 1.8 sum_pieces.2.refs_0_
  164.0 6.1 %collective-permute-start.11 = (f32[160,128]{1,0:T(8,128)}, f32[160,128]{1,0:T(8,128)S(1)}, u32[]{:S(2)}, u32[]{:S(2)}) collective-permute-start(f32[160,128]{1,0:T(8,128)} %sum_pieces.2.refs_0_), channel_id=1, source_target_pairs={{0,1},{1,0},{2,3},{3,2},{4,5},{5,4},{6,7},{7,6},{8,9},{9,8},{10,11... | collective-permute-start | bytes 245768 | tf_op jit(solution)/shard_map/ppermute | solution.py:557
  170.1 4.3 %collective-permute-done.11.refs_1_ = f32[160,128]{1,0:T(8,128)S(1)} collective-permute-done((f32[160,128]{1,0:T(8,128)}, f32[160,128]{1,0:T(8,128)S(1)}, u32[]{:S(2)}, u32[]{:S(2)}) %collective-permute-start.11) | collective-permute-done | bytes 81952 | tf_op jit(solution)/shard_map/ppermute | solution.py:557
  175.0 1.6 add.4.refs_1_
  176.5 1.3 collective-permute-start.12
  177.8 1.7 collective-permute-start.13
  179.8 1.5 collective-permute-start.15
  181.3 2.3 collective-permute-done.12.refs_2_
  184.3 1.6 add.5
  185.8 10.8 %all_gather.3 = f32[1280,128]{1,0:T(8,128)S(1)} all-gather(f32[160,128]{1,0:T(8,128)} %add.5), channel_id=1, replica_groups=mesh['space'=8,'snap'=4] {'space'}, dimensions={0}, use_global_device_ids=true | all-gather | bytes 737280 | tf_op jit(solution)/shard_map/all_gather | solution.py:609
  196.6 4.9 %factor.4.refs_0_ = f32[4,8,128,128]{3,2,1,0:T(8,128)S(1)} custom-call(f32[10,128,128]{2,1,0:T(8,128)S(1)} %bitcast.10), custom_call_target="tpu_custom_call" | custom-call | flops 7000000000 | bytes 655360 | tf_op jit(solution)/shard_map/factor/pallas_call | solution.py:401
  201.6 4.8 %factor.5.refs_0_.refs_1_ = f32[4,8,128,128]{3,2,1,0:T(8,128)S(1)} custom-call(f32[4,8,128,128]{3,2,1,0:T(8,128)S(1)} %factor.4.refs_0_), custom_call_target="tpu_custom_call", output_to_operand_aliasing={{}: (0, {})} | custom-call | flops 7000000000 | bytes 2097152 | tf_op jit(solution)/shard_map/factor/pallas_call | solution.py:401
  206.5 3.3 %cross_sum.1.refs_0_ = f32[512,512]{1,0:T(8,128)} custom-call(f32[4,8,128,128]{3,2,1,0:T(8,128)S(1)} %factor.5.refs_0_.refs_1_, bf16[4,64,32,128]{3,2,1,0:T(8,128)(2,1)S(1)} %all-to-all-done.refs_1_.refs_2_, bf16[64,16,128]{2,1,0:T(8,128)(2,1)S(1)} %get-tuple-element.47.refs_2_, bf16[64,16,128]{2,1,0:T(8,128)(2,1)S(1)} %collective-permute-done.13.refs_3_, ...), custom_call_target="tpu_custom_call" | custom-call | flops 1073741824 | bytes 4194304 | tf_op jit(solution)/shard_map/cross_sum/pallas_call | solution.py:263
  209.8 3.8 %all-to-all-start.2 = ((f32[8,64,512]{2,1,0:T(8,128)}), f32[8,64,512]{2,1,0:T(8,128)S(1)}, u32[]{:S(2)}, u32[]{:S(2)}) async-start(f32[8,64,512]{2,1,0:T(8,128)} %bitcast.5), calls=%async_computation.2 | async-start | bytes 2097152 | tf_op jit(solution)/shard_map/all_to_all | solution.py:588
  213.6 1.6 copy-done.1
  215.2 4.6 %factor.6.refs_0_.refs_1_ = f32[4,8,128,128]{3,2,1,0:T(8,128)S(1)} custom-call(f32[512,512]{1,0:T(8,128)} %cross_sum.1.refs_0_, f32[4,8,128,128]{3,2,1,0:T(8,128)S(1)} %copy-done.1), custom_call_target="tpu_custom_call", output_to_operand_aliasing={{}: (1, {})} | custom-call | flops 7000000000 | bytes 2097152 | tf_op jit(solution)/shard_map/factor/pallas_call | solution.py:401
  219.8 1.3 copy-done.2
  221.1 7.6 %all-to-all-done.2 = f32[8,64,512]{2,1,0:T(8,128)S(1)} async-done(((f32[8,64,512]{2,1,0:T(8,128)}), f32[8,64,512]{2,1,0:T(8,128)S(1)}, u32[]{:S(2)}, u32[]{:S(2)}) %all-to-all-start.2) | async-done | bytes 1048608 | tf_op jit(solution)/shard_map/all_to_all | solution.py:588
  228.7 1.0 copy-done.37
  229.7 1.9 sum_pieces.3.refs_0_.refs_1_
  231.6 1.6 copy-done.3
  233.2 0.9 copy-done.26
  234.1 5.4 %factor.7 = (f32[512,512]{1,0:T(8,128)}, f32[512,512]{1,0:T(8,128)S(1)}, bf16[512,512]{1,0:T(8,128)(2,1)S(1)}, bf16[512,512]{1,0:T(8,128)(2,1)S(1)}, bf16[512,512]{1,0:T(8,128)(2,1)S(1)}) custom-call(f32[64,512]{1,0:T(8,128)S(1)} %copy-done.26, f32[4,8,128,128]{3,2,1,0:T(8,128)S(1)} %copy-done.3), custom_call_target="tpu_custom_call" | custom-call | flops 7000000000 | bytes 2097152 | tf_op jit(solution)/shard_map/factor/pallas_call | solution.py:401
  240.3 1.0 copy-done.15
  242.0 1.6 add.6.refs_0_.refs_1_
  243.6 2.9 %collective-permute-start.17 = (f32[64,512]{1,0:T(8,128)}, f32[64,512]{1,0:T(8,128)S(1)}, u32[]{:S(2)}, u32[]{:S(2)}) collective-permute-start(f32[64,512]{1,0:T(8,128)} %add.6.refs_0_.refs_1_), channel_id=1, source_target_pairs={{0,2},{1,3},{2,0},{3,1},{4,6},{5,7},{6,4},{7,5},{8,10},{9,11},{10,... | collective-permute-start | bytes 393224 | tf_op jit(solution)/shard_map/ppermute | solution.py:557
  246.5 1.0 copy-done.11
  247.5 0.9 copy-done.14
  248.4 3.5 %basis.2.refs_0_ = f32[64,32,512]{2,1,0:T(8,128)} custom-call(f32[64,512]{1,0:T(8,128)S(1)} %copy-done.14, bf16[4,64,32,128]{3,2,1,0:T(8,128)(2,1)S(1)} %all-to-all-done.refs_1_.refs_2_, bf16[512,512]{1,0:T(8,128)(2,1)S(1)} %get-tuple-element.53.refs_2_.refs_3_, bf16[512,512]{1,0:T(8,128)(2,1)S(1)} %get-tuple-element.54.refs_3_.refs_4_, ...), custom_call_target="tpu_custom_call" | custom-call | flops 1610612736 | bytes 3145728 | tf_op jit(solution)/shard_map/basis/pallas_call | solution.py:457
  252.5 1.6 add.7.refs_1_
  254.2 1.5 collective-permute-start.20
  255.6 1.6 collective-permute-start.19
  257.7 1.0 copy-done.12
  258.7 0.9 copy-done.13
  259.6 3.5 %basis.3.refs_0_ = f32[64,32,512]{2,1,0:T(8,128)} custom-call(f32[64,32,512]{2,1,0:T(8,128)} %basis.2.refs_0_, f32[64,512]{1,0:T(8,128)S(1)} %copy-done.13, bf16[4,64,32,128]{3,2,1,0:T(8,128)(2,1)S(1)} %all-to-all-done.refs_1_.refs_2_, bf16[512,512]{1,0:T(8,128)(2,1)S(1)} %get-tuple-element.53.refs_2_.refs_3_, ...), custom_call_target="tpu_custom_call", output_to_operand_aliasing={{}: (0, {})} | custom-call | flops 1610612736 | bytes 3145728 | tf_op jit(solution)/shard_map/basis/pallas_call | solution.py:457
  264.4 2.0 join.1.refs_1_
  266.4 2.1 collective-permute-done.21.refs_2_
  268.5 1.0 copy-done.9
  269.6 2.9 %project.1 = f32[512,512]{1,0:T(8,128)} custom-call(f32[512,512]{1,0:T(8,128)S(1)} %copy-done.16, f32[256,512]{1,0:T(8,128)S(1)} %copy-done.9, f32[256,512]{1,0:T(8,128)S(1)} %collective-permute-done.21.refs_2_), custom_call_target="tpu_custom_call" | custom-call | tf_op jit(solution)/shard_map/project/pallas_call | solution.py:545
  (99 shorter events, 12.7 us)
Async XLA Ops:
  0.6 2.2 copy-start.4
  3.5 2.7 %copy-start.5 = (bf16[128,128,128]{2,1,0:T(8,128)(2,1)S(1)}, bf16[128,128,128]{2,1,0:T(8,128)(2,1)}, u32[]{:S(2)}) copy-start(bf16[128,128,128]{2,1,0:T(8,128)(2,1)} %param.4) | copy-start | bytes 12582916
  3.5 2.7 %copy-start.30 = (s32[128]{0:T(128)S(1)}, s32[128]{0:T(128)}, u32[]{:S(2)}) copy-start(s32[128]{0:T(128)} %refs_0_.3) | copy-start | bytes 1540
  5.9 4.2 %collective-permute-start = (bf16[516,16,128]{2,1,0:T(8,128)(2,1)S(1)}, bf16[516,16,128]{2,1,0:T(8,128)(2,1)S(1)}, u32[]{:S(2)}, u32[]{:S(2)}) collective-permute-start(bf16[516,16,128]{2,1,0:T(8,128)(2,1)S(1)} %get-tuple-element.31), channel_id=1, source_target_pairs={{0,4},{4,0},{8,12},{12,8},{16,20},{20,16},{24,28},{28,24},{1,5},{5... | collective-permute-start | bytes 6340616 | tf_op jit(solution)/shard_map/ppermute | solution.py:557
  8.6 7.6 %collective-permute-start.3 = (bf16[512,16,128]{2,1,0:T(8,128)(2,1)S(1)}, bf16[512,16,128]{2,1,0:T(8,128)(2,1)S(1)}, u32[]{:S(2)}, u32[]{:S(2)}) collective-permute-start(bf16[512,16,128]{2,1,0:T(8,128)(2,1)S(1)} %get-tuple-element.35), channel_id=1, source_target_pairs={{0,4},{4,0},{8,12},{12,8},{16,20},{20,16},{24,28},{28,24},{1,5},{5... | collective-permute-start | bytes 6291464 | tf_op jit(solution)/shard_map/ppermute | solution.py:557
  10.4 28.4 %collective-permute-start.1 = (bf16[258,16,128]{2,1,0:T(8,128)(2,1)S(1)}, bf16[258,16,128]{2,1,0:T(8,128)(2,1)S(1)}, u32[]{:S(2)}, u32[]{:S(2)}) collective-permute-start(bf16[258,16,128]{2,1,0:T(8,128)(2,1)S(1)} %get-tuple-element.32), channel_id=1, source_target_pairs={{0,8},{4,12},{8,0},{12,4},{16,24},{20,28},{24,16},{28,20},{1,9},{5... | collective-permute-start | bytes 3170312 | tf_op jit(solution)/shard_map/ppermute | solution.py:557
  14.7 47.7 %collective-permute-start.2 = (bf16[258,16,128]{2,1,0:T(8,128)(2,1)S(1)}, bf16[258,16,128]{2,1,0:T(8,128)(2,1)S(1)}, u32[]{:S(2)}, u32[]{:S(2)}) collective-permute-start(bf16[258,16,128]{2,1,0:T(8,128)(2,1)S(1)} %get-tuple-element.33), channel_id=1, source_target_pairs={{0,16},{4,20},{8,24},{12,28},{16,0},{20,4},{24,8},{28,12},{1,17},{... | collective-permute-start | bytes 3170312 | tf_op jit(solution)/shard_map/ppermute | solution.py:557
  16.0 46.7 %collective-permute-start.5 = (bf16[258,16,128]{2,1,0:T(8,128)(2,1)S(1)}, bf16[258,16,128]{2,1,0:T(8,128)(2,1)S(1)}, u32[]{:S(2)}, u32[]{:S(2)}) collective-permute-start(bf16[258,16,128]{2,1,0:T(8,128)(2,1)S(1)} %get-tuple-element.39), channel_id=1, source_target_pairs={{0,24},{4,28},{8,16},{12,20},{16,8},{20,12},{24,0},{28,4},{1,25},{... | collective-permute-start | bytes 3170312 | tf_op jit(solution)/shard_map/ppermute | solution.py:557
  62.7 2.8 %copy-start.31 = (bf16[256,16,128]{2,1,0:T(8,128)(2,1)}, bf16[256,16,128]{2,1,0:T(8,128)(2,1)S(1)}, u32[]{:S(2)}) copy-start(bf16[256,16,128]{2,1,0:T(8,128)(2,1)S(1)} %get-tuple-element.43) | copy-start | bytes 3145732
  62.7 2.8 %copy-start.32 = (bf16[256,16,128]{2,1,0:T(8,128)(2,1)}, bf16[256,16,128]{2,1,0:T(8,128)(2,1)S(1)}, u32[]{:S(2)}) copy-start(bf16[256,16,128]{2,1,0:T(8,128)(2,1)S(1)} %get-tuple-element.42) | copy-start | bytes 3145732
  62.7 2.8 %copy-start.33 = (bf16[256,16,128]{2,1,0:T(8,128)(2,1)}, bf16[256,16,128]{2,1,0:T(8,128)(2,1)S(1)}, u32[]{:S(2)}) copy-start(bf16[256,16,128]{2,1,0:T(8,128)(2,1)S(1)} %get-tuple-element.36) | copy-start | bytes 3145732
  65.6 1.3 copy-start.8
  66.9 51.8 %all-to-all-start = ((bf16[4,64,32,128]{3,2,1,0:T(8,128)(2,1)}), bf16[4,64,32,128]{3,2,1,0:T(8,128)(2,1)S(1)}, u32[]{:S(2)}, u32[]{:S(2)}) async-start(bf16[4,64,32,128]{3,2,1,0:T(8,128)(2,1)} %copy-done.8), calls=%async_computation | async-start | bytes 4194304 | tf_op jit(solution)/shard_map/all_to_all | solution.py:600
  71.7 26.3 %collective-permute-start.4 = (bf16[256,16,128]{2,1,0:T(8,128)(2,1)}, bf16[256,16,128]{2,1,0:T(8,128)(2,1)S(1)}, u32[]{:S(2)}, u32[]{:S(2)}) collective-permute-start(bf16[256,16,128]{2,1,0:T(8,128)(2,1)} %copy-done.33), channel_id=1, source_target_pairs={{0,8},{4,12},{8,0},{12,4},{16,24},{20,28},{24,16},{28,20},{1,9},{5... | collective-permute-start | bytes 3145736 | tf_op jit(solution)/shard_map/ppermute | solution.py:557
  72.5 54.4 %collective-permute-start.6 = (bf16[256,16,128]{2,1,0:T(8,128)(2,1)}, bf16[256,16,128]{2,1,0:T(8,128)(2,1)}, u32[]{:S(2)}, u32[]{:S(2)}) collective-permute-start(bf16[256,16,128]{2,1,0:T(8,128)(2,1)} %copy-done.32), channel_id=1, source_target_pairs={{0,16},{4,20},{8,24},{12,28},{16,0},{20,4},{24,8},{28,12},{1,17},{... | collective-permute-start | bytes 3145736 | tf_op jit(solution)/shard_map/ppermute | solution.py:557
  73.6 53.3 %collective-permute-start.7 = (bf16[256,16,128]{2,1,0:T(8,128)(2,1)}, bf16[256,16,128]{2,1,0:T(8,128)(2,1)}, u32[]{:S(2)}, u32[]{:S(2)}) collective-permute-start(bf16[256,16,128]{2,1,0:T(8,128)(2,1)} %copy-done.31), channel_id=1, source_target_pairs={{0,24},{4,28},{8,16},{12,20},{16,8},{20,12},{24,0},{28,4},{1,25},{... | collective-permute-start | bytes 3145736 | tf_op jit(solution)/shard_map/ppermute | solution.py:557
  98.1 1.0 copy-start.23
  118.7 1.2 copy-start.24
  121.8 0.8 copy-start.6
  122.7 38.7 %all-to-all-start.1 = ((f32[8,160,128]{2,1,0:T(8,128)}), f32[8,160,128]{2,1,0:T(8,128)}, u32[]{:S(2)}, u32[]{:S(2)}) async-start(f32[8,160,128]{2,1,0:T(8,128)} %bitcast.9), calls=%async_computation.1 | async-start | bytes 1310720 | tf_op jit(solution)/shard_map/all_to_all | solution.py:588
  126.9 1.1 copy-start.7
  128.0 1.2 copy-start.25
  133.4 0.7 copy-start.27
  134.1 0.7 copy-start.34
  134.8 0.7 copy-start.35
  135.5 0.7 copy-start.36
  136.2 25.2 %collective-permute-start.9 = (bf16[64,16,128]{2,1,0:T(8,128)(2,1)S(1)}, bf16[64,16,128]{2,1,0:T(8,128)(2,1)S(1)}, u32[]{:S(2)}, u32[]{:S(2)}) collective-permute-start(bf16[64,16,128]{2,1,0:T(8,128)(2,1)S(1)} %get-tuple-element.45), channel_id=1, source_target_pairs={{0,2},{1,3},{2,0},{3,1},{4,6},{5,7},{6,4},{7,5},{8,10},{9,11},{10,... | collective-permute-start | bytes 786440 | tf_op jit(solution)/shard_map/ppermute | solution.py:557
  136.2 25.2 %collective-permute-start.10 = (bf16[64,16,128]{2,1,0:T(8,128)(2,1)S(1)}, bf16[64,16,128]{2,1,0:T(8,128)(2,1)S(1)}, u32[]{:S(2)}, u32[]{:S(2)}) collective-permute-start(bf16[64,16,128]{2,1,0:T(8,128)(2,1)S(1)} %get-tuple-element.46), channel_id=1, source_target_pairs={{0,3},{1,2},{2,1},{3,0},{4,7},{5,6},{6,5},{7,4},{8,11},{9,10},{10,... | collective-permute-start | bytes 786440 | tf_op jit(solution)/shard_map/ppermute | solution.py:557
  137.7 43.6 %collective-permute-start.8 = (bf16[64,16,128]{2,1,0:T(8,128)(2,1)}, bf16[64,16,128]{2,1,0:T(8,128)(2,1)S(1)}, u32[]{:S(2)}, u32[]{:S(2)}) collective-permute-start(bf16[64,16,128]{2,1,0:T(8,128)(2,1)} %get-tuple-element.44), channel_id=1, source_target_pairs={{0,2},{1,3},{2,0},{3,1},{4,6},{5,7},{6,4},{7,5},{8,10},{9,11},{10,... | collective-permute-start | bytes 786440 | tf_op jit(solution)/shard_map/ppermute | solution.py:557
  161.4 0.7 copy-start.17
  161.4 0.8 copy-start.19
  164.0 10.4 %collective-permute-start.11 = (f32[160,128]{1,0:T(8,128)}, f32[160,128]{1,0:T(8,128)S(1)}, u32[]{:S(2)}, u32[]{:S(2)}) collective-permute-start(f32[160,128]{1,0:T(8,128)} %sum_pieces.2.refs_0_), channel_id=1, source_target_pairs={{0,1},{1,0},{2,3},{3,2},{4,5},{5,4},{6,7},{7,6},{8,9},{9,8},{10,11... | collective-permute-start | bytes 245768 | tf_op jit(solution)/shard_map/ppermute | solution.py:557
  176.5 7.1 %collective-permute-start.12 = (f32[160,128]{1,0:T(8,128)}, f32[160,128]{1,0:T(8,128)S(1)}, u32[]{:S(2)}, u32[]{:S(2)}) collective-permute-start(f32[160,128]{1,0:T(8,128)} %add.4.refs_1_), channel_id=1, source_target_pairs={{0,2},{1,3},{2,0},{3,1},{4,6},{5,7},{6,4},{7,5},{8,10},{9,11},{10,... | collective-permute-start | bytes 245768 | tf_op jit(solution)/shard_map/ppermute | solution.py:557
  177.8 28.7 %collective-permute-start.13 = (bf16[64,16,128]{2,1,0:T(8,128)(2,1)}, bf16[64,16,128]{2,1,0:T(8,128)(2,1)S(1)}, u32[]{:S(2)}, u32[]{:S(2)}) collective-permute-start(bf16[64,16,128]{2,1,0:T(8,128)(2,1)} %copy-done.36), channel_id=1, source_target_pairs={{0,1},{1,0},{2,3},{3,2},{4,5},{5,4},{6,7},{7,6},{8,9},{9,8},{10,11... | collective-permute-start | bytes 786440 | tf_op jit(solution)/shard_map/ppermute | solution.py:557
  179.5 27.0 %collective-permute-start.14 = (bf16[64,16,128]{2,1,0:T(8,128)(2,1)}, bf16[64,16,128]{2,1,0:T(8,128)(2,1)S(1)}, u32[]{:S(2)}, u32[]{:S(2)}) collective-permute-start(bf16[64,16,128]{2,1,0:T(8,128)(2,1)} %copy-done.35), channel_id=1, source_target_pairs={{0,1},{1,0},{2,3},{3,2},{4,5},{5,4},{6,7},{7,6},{8,9},{9,8},{10,11... | collective-permute-start | bytes 786440 | tf_op jit(solution)/shard_map/ppermute | solution.py:557
  179.8 26.7 %collective-permute-start.15 = (bf16[64,16,128]{2,1,0:T(8,128)(2,1)}, bf16[64,16,128]{2,1,0:T(8,128)(2,1)S(1)}, u32[]{:S(2)}, u32[]{:S(2)}) collective-permute-start(bf16[64,16,128]{2,1,0:T(8,128)(2,1)} %copy-done.34), channel_id=1, source_target_pairs={{0,3},{1,2},{2,1},{3,0},{4,7},{5,6},{6,5},{7,4},{8,11},{9,10},{10,... | collective-permute-start | bytes 786440 | tf_op jit(solution)/shard_map/ppermute | solution.py:557
  181.3 2.4 copy-start.21
  201.6 4.9 %copy-start.18 = (bf16[64,16,128]{2,1,0:T(8,128)(2,1)S(1)}, bf16[64,16,128]{2,1,0:T(8,128)(2,1)}, u32[]{:S(2)}) copy-start(bf16[64,16,128]{2,1,0:T(8,128)(2,1)} %copy-done.17) | copy-start | bytes 786436
  201.6 4.9 %copy-start.20 = (bf16[64,16,128]{2,1,0:T(8,128)(2,1)S(1)}, bf16[64,16,128]{2,1,0:T(8,128)(2,1)}, u32[]{:S(2)}) copy-start(bf16[64,16,128]{2,1,0:T(8,128)(2,1)} %copy-done.19) | copy-start | bytes 786436
  201.6 4.9 %copy-start.22 = (bf16[64,16,128]{2,1,0:T(8,128)(2,1)S(1)}, bf16[64,16,128]{2,1,0:T(8,128)(2,1)}, u32[]{:S(2)}) copy-start(bf16[64,16,128]{2,1,0:T(8,128)(2,1)} %copy-done.21) | copy-start | bytes 786436
  201.6 4.9 %copy-start.28 = (bf16[64,16,128]{2,1,0:T(8,128)(2,1)S(1)}, bf16[64,16,128]{2,1,0:T(8,128)(2,1)}, u32[]{:S(2)}) copy-start(bf16[64,16,128]{2,1,0:T(8,128)(2,1)} %copy-done.27) | copy-start | bytes 786436
  206.5 3.4 %copy-start = (f32[4,8,128,128]{3,2,1,0:T(8,128)}, f32[4,8,128,128]{3,2,1,0:T(8,128)S(1)}, u32[]{:S(2)}) copy-start(f32[4,8,128,128]{3,2,1,0:T(8,128)S(1)} %factor.5.refs_0_.refs_1_) | copy-start | bytes 6291460
  209.8 18.9 %all-to-all-start.2 = ((f32[8,64,512]{2,1,0:T(8,128)}), f32[8,64,512]{2,1,0:T(8,128)S(1)}, u32[]{:S(2)}, u32[]{:S(2)}) async-start(f32[8,64,512]{2,1,0:T(8,128)} %bitcast.5), calls=%async_computation.2 | async-start | bytes 2097152 | tf_op jit(solution)/shard_map/all_to_all | solution.py:588
  213.6 1.6 copy-start.1
  219.8 1.3 copy-start.2
  228.7 1.0 copy-start.37
  231.6 9.7 %collective-permute-start.16 = (f32[64,512]{1,0:T(8,128)}, f32[64,512]{1,0:T(8,128)S(1)}, u32[]{:S(2)}, u32[]{:S(2)}) collective-permute-start(f32[64,512]{1,0:T(8,128)} %sum_pieces.3.refs_0_.refs_1_), channel_id=1, source_target_pairs={{0,1},{1,0},{2,3},{3,2},{4,5},{5,4},{6,7},{7,6},{8,9},{9,8},{10,11... | collective-permute-start | bytes 393224 | tf_op jit(solution)/shard_map/ppermute | solution.py:557
  231.6 1.6 copy-start.3
  233.2 0.9 copy-start.26
  239.5 0.8 copy-start.10
  240.3 1.0 copy-start.15
  241.3 0.7 copy-start.42
  243.6 8.3 %collective-permute-start.17 = (f32[64,512]{1,0:T(8,128)}, f32[64,512]{1,0:T(8,128)S(1)}, u32[]{:S(2)}, u32[]{:S(2)}) collective-permute-start(f32[64,512]{1,0:T(8,128)} %add.6.refs_0_.refs_1_), channel_id=1, source_target_pairs={{0,2},{1,3},{2,0},{3,1},{4,6},{5,7},{6,4},{7,5},{8,10},{9,11},{10,... | collective-permute-start | bytes 393224 | tf_op jit(solution)/shard_map/ppermute | solution.py:557
  246.5 1.0 copy-start.11
  247.5 0.9 copy-start.14
  254.2 8.9 %collective-permute-start.20 = (f32[64,512]{1,0:T(8,128)}, f32[64,512]{1,0:T(8,128)S(1)}, u32[]{:S(2)}, u32[]{:S(2)}) collective-permute-start(f32[64,512]{1,0:T(8,128)} %add.7.refs_1_), channel_id=1, source_target_pairs={{0,24},{4,28},{8,16},{12,20},{16,8},{20,12},{24,0},{28,4},{1,25},{... | collective-permute-start | bytes 393224 | tf_op jit(solution)/shard_map/ppermute | solution.py:557
  255.6 7.5 %collective-permute-start.19 = (f32[64,512]{1,0:T(8,128)}, f32[64,512]{1,0:T(8,128)S(1)}, u32[]{:S(2)}, u32[]{:S(2)}) collective-permute-start(f32[64,512]{1,0:T(8,128)} %add.7.refs_1_), channel_id=1, source_target_pairs={{0,16},{4,20},{8,24},{12,28},{16,0},{20,4},{24,8},{28,12},{1,17},{... | collective-permute-start | bytes 393224 | tf_op jit(solution)/shard_map/ppermute | solution.py:557
  257.2 5.9 %collective-permute-start.18 = (f32[64,512]{1,0:T(8,128)}, f32[64,512]{1,0:T(8,128)S(1)}, u32[]{:S(2)}, u32[]{:S(2)}) collective-permute-start(f32[64,512]{1,0:T(8,128)} %add.7.refs_1_), channel_id=1, source_target_pairs={{0,8},{4,12},{8,0},{12,4},{16,24},{20,28},{24,16},{28,20},{1,9},{5... | collective-permute-start | bytes 393224 | tf_op jit(solution)/shard_map/ppermute | solution.py:557
  257.7 1.0 copy-start.12
  258.7 0.9 copy-start.13
  263.1 5.4 %copy-start.16 = (f32[512,512]{1,0:T(8,128)S(1)}, f32[512,512]{1,0:T(8,128)}, u32[]{:S(2)}) copy-start(f32[512,512]{1,0:T(8,128)} %copy-done.15) | copy-start | bytes 3145732
  263.1 0.7 copy-start.39
  266.4 2.1 collective-permute-start.21
  268.5 1.0 copy-start.9
  (6 other events, 3.9 us)

commit v15 on v14

--- a/solution.py
+++ b/solution.py
@@ -603,27 +603,25 @@
     gram = to_pieces(gram_local.reshape(pairs * TILE, TILE))
     pieces = place(meta, moved_y, [gram_local])
     y_cells = [to_rows(pieces[part * shares : (part + 1) * shares]) for part in range(parts)]
-    gram = sum_pieces(gram, slabs, y_cells[0][2:])
+    gram = sum_pieces(gram, slabs, pieces[:1])
     for hop in hops():
-        gram = add(gram, swap(gram, "snap", hop), [] if hop == 1 else y_cells[1][2:3])
+        gram = add(gram, swap(gram, "snap", hop), y_cells[0][hop : hop + 1])
     gram = lax.all_gather(gram, "space", axis=0, tiled=True)
 
     steps = factor_steps(gram.reshape(pairs, TILE, TILE), tiles, rows_total, [])
     state = next(steps)
-    for _ in range(tiles - 3):
+    for _ in range(tiles - 2):
         state = steps.send([])
     cross_local = cross_sum(x_cells, y_cells, [state])
-    state = steps.send([cross_local])
-    cross = sum_pieces(to_pieces(cross_local), slabs, [state])
-    r_factor, inverse, *terms = steps.send([cross])
-    tied = [r_factor]
+    cross = to_pieces(cross_local)
+    r_factor, inverse, *terms = steps.send([cross_local])
+
+    q_basis = basis(x_cells, terms, 0, 2, None, [])
+    cross = sum_pieces(cross, slabs, [q_basis])
+    q_basis = basis(x_cells, terms, 1, 2, q_basis, [cross])
     for hop in hops():
-        cross = add(cross, swap(cross, "snap", hop), tied)
-        if hop == 1:
-            q_basis = basis(x_cells, terms, 0, 2, None, [cross])
-            tied = [q_basis]
-    q_basis = basis(x_cells, terms, 1, 2, q_basis, [cross])
-    same = join([cross] + [swap(cross, "space", m) for m in range(CORES, slabs, CORES)], [q_basis])
+        cross = add(cross, swap(cross, "snap", hop), [q_basis] if hop == 1 else [])
+    same = join([cross] + [swap(cross, "space", m) for m in range(CORES, slabs, CORES)], [])
     projection = project(inverse, same, swap(same, "space", 1), slabs, math.sqrt(rows_total))
     return q_basis, r_factor, projection
 

time: 274 us -> 259 us (0.945)
  local copies, waits for them, and re-layouts: 30.2 us -> 22.7 us
  starting transfers between devices: 43.3 us -> 37.5 us
  waiting for transfers between devices: 128 us -> 124 us
    unnamed x90 -> x76, local copies, waits for them, and re-layouts: 30.2 us -> 22.7 us
    ppermute x22, starting transfers between devices: 30.5 us -> 24.2 us  [swap(): lax.ppermute(value, axis, [(i, i ^ mask) for i in range(lax.axis_size(axi...]
    all_to_all x2, waiting for transfers between devices: 7.64 us -> 3.14 us  [to_pieces(): lax.all_to_all(value, 'space', split_axis=0, concat_axis=0, tiled=True)]
  transfers between devices with their start and end apart: 25 -> 25, of which waited for: 10 -> 14; matrix products, arithmetic and copies ran while one was open for 0% -> 0% of each run, Pallas kernels for 15% -> 16%
where the time goes in v15:
time: 259 us; the launch traced here: 257 us
  waiting for transfers between devices  124 us (48%)
  Pallas kernels  60.8 us (23%)
  starting transfers between devices  37.5 us (14%)
  local copies, waits for them, and re-layouts  22.7 us (9%)
  blocking collectives  10.7 us (4%)
    ppermute x22, waiting for transfers between devices, swap(): lax.ppermute(value, axis, [(i, i ^ mask) for i in range(lax.axis_size(axi...  101 us
    ppermute x22, starting transfers between devices, swap(): lax.ppermute(value, axis, [(i, i ^ mask) for i in range(lax.axis_size(axi...  24.2 us
    unnamed x76, local copies, waits for them, and re-layouts  22.7 us
    all_to_all x1, waiting for transfers between devices, body(): lax.all_to_all(pieces, 'snap', split_axis=0, concat_axis=0, tiled=True)  19.9 us
    pallas_call x4, Pallas kernels, factor_call(): pl.pallas_call(lambda *refs: kernel(*refs[len(after):]), out_shape=out_sh...  19.7 us
    all_gather x1, blocking collectives, body(): gram = lax.all_gather(gram, 'space', axis=0, tiled=True)  10.7 us
    all_to_all x2, starting transfers between devices, to_pieces(): lax.all_to_all(value, 'space', split_axis=0, concat_axis=0, tiled=True)  8.43 us
    pallas_call x2, Pallas kernels, settle(): pl.pallas_call(lambda *refs: settle_kernel(chips, capacity, parts, first,...  7 us
  transfers between devices with their start and end apart: 25, of which 14 were waited for; matrix products, arithmetic and copies ran while one was open for 0% of the time, Pallas kernels for 16%

profile of v15, /device:TPU:0, one launch (start us, length us, event | category | flops | bytes accessed | tf_op | source)
XLA Modules:
  0.0 257.4 jit_solution(5663602328426752973)
XLA Ops:
  0.6 2.2 copy-done
  3.5 2.7 %pack.2 = (bf16[516,16,128]{2,1,0:T(8,128)(2,1)S(1)}, bf16[516,16,128]{2,1,0:T(8,128)(2,1)S(1)}) custom-call(s32[128]{0:T(128)S(1)} %copy-done.22, bf16[128,8,16,128]{3,2,1,0:T(8,128)(2,1)S(1)} %bitcast.7), custom_call_target="tpu_custom_call" | custom-call | bytes 8388608 | tf_op jit(solution)/shard_map/pack/pallas_call | solution.py:78
  6.2 0.9 collective-permute-start
  7.0 2.6 %pack.3 = (bf16[512,16,128]{2,1,0:T(8,128)(2,1)S(1)}, bf16[512,16,128]{2,1,0:T(8,128)(2,1)S(1)}) custom-call(s32[128]{0:T(128)S(1)} %copy-done.23, bf16[128,8,16,128]{3,2,1,0:T(8,128)(2,1)S(1)} %bitcast.8), custom_call_target="tpu_custom_call" | custom-call | bytes 8388608 | tf_op jit(solution)/shard_map/pack/pallas_call | solution.py:78
  10.1 0.7 collective-permute-done.refs_1_
  11.1 3.0 %collective-permute-start.1 = (bf16[258,16,128]{2,1,0:T(8,128)(2,1)S(1)}, bf16[258,16,128]{2,1,0:T(8,128)(2,1)S(1)}, u32[]{:S(2)}, u32[]{:S(2)}) collective-permute-start(bf16[258,16,128]{2,1,0:T(8,128)(2,1)S(1)} %get-tuple-element.32), channel_id=1, source_target_pairs={{0,8},{4,12},{8,0},{12,4},{16,24},{20,28},{24,16},{28,20},{1,9},{5... | collective-permute-start | bytes 3170312 | tf_op jit(solution)/shard_map/ppermute | solution.py:557
  14.1 1.3 collective-permute-start.2
  15.7 22.6 %collective-permute-done.1.refs_0_.refs_2_ = bf16[258,16,128]{2,1,0:T(8,128)(2,1)S(1)} collective-permute-done((bf16[258,16,128]{2,1,0:T(8,128)(2,1)S(1)}, bf16[258,16,128]{2,1,0:T(8,128)(2,1)S(1)}, u32[]{:S(2)}, u32[]{:S(2)}) %collective-permute-start.1) | collective-permute-done | bytes 1056800 | tf_op jit(solution)/shard_map/ppermute | solution.py:557
  38.3 23.8 %collective-permute-done.2.refs_1_.refs_3_ = bf16[258,16,128]{2,1,0:T(8,128)(2,1)S(1)} collective-permute-done((bf16[258,16,128]{2,1,0:T(8,128)(2,1)S(1)}, bf16[258,16,128]{2,1,0:T(8,128)(2,1)S(1)}, u32[]{:S(2)}, u32[]{:S(2)}) %collective-permute-start.2) | collective-permute-done | bytes 1056800 | tf_op jit(solution)/shard_map/ppermute | solution.py:557
  62.4 2.8 %settle.2 = (bf16[4,64,32,128]{3,2,1,0:T(8,128)(2,1)S(1)}, s32[8,128]{1,0:T(8,128)S(1)}) custom-call(bf16[256,16,128]{2,1,0:T(8,128)(2,1)S(1)} %get-tuple-element.36.refs_0_.refs_2_, bf16[258,16,128]{2,1,0:T(8,128)(2,1)S(1)} %get-tuple-element.37.refs_1_, bf16[258,16,128]{2,1,0:T(8,128)(2,1)S(1)} %collective-permute-done.1.refs_0_.refs_2_, ...), custom_call_target="tpu_custom_call" | custom-call | bytes 4227072 | tf_op jit(solution)/shard_map/settle/pallas_call | solution.py:166
  65.3 1.3 copy-done.6
  66.6 4.9 %all-to-all-start = ((bf16[4,64,32,128]{3,2,1,0:T(8,128)(2,1)}), bf16[4,64,32,128]{3,2,1,0:T(8,128)(2,1)S(1)}, u32[]{:S(2)}, u32[]{:S(2)}) async-start(bf16[4,64,32,128]{3,2,1,0:T(8,128)(2,1)} %copy-done.6), calls=%async_computation | async-start | bytes 4194304 | tf_op jit(solution)/shard_map/all_to_all | solution.py:600
  71.4 0.7 collective-permute-start.5
  72.9 2.1 collective-permute-start.7
  74.9 22.8 %collective-permute-done.5.refs_0_.refs_3_ = bf16[256,16,128]{2,1,0:T(8,128)(2,1)S(1)} collective-permute-done((bf16[256,16,128]{2,1,0:T(8,128)(2,1)}, bf16[256,16,128]{2,1,0:T(8,128)(2,1)S(1)}, u32[]{:S(2)}, u32[]{:S(2)}) %collective-permute-start.5) | collective-permute-done | bytes 1048608 | tf_op jit(solution)/shard_map/ppermute | solution.py:557
  97.8 1.0 copy-done.19
  98.7 19.9 %all-to-all-done.refs_1_.refs_0_.refs_2_ = bf16[4,64,32,128]{3,2,1,0:T(8,128)(2,1)S(1)} async-done(((bf16[4,64,32,128]{3,2,1,0:T(8,128)(2,1)}), bf16[4,64,32,128]{3,2,1,0:T(8,128)(2,1)S(1)}, u32[]{:S(2)}, u32[]{:S(2)}) %all-to-all-start) | async-done | bytes 2097184 | tf_op jit(solution)/shard_map/all_to_all | solution.py:600
  118.6 1.2 copy-done.20
  119.9 1.9 gram_blocks.1.refs_0_
  121.8 0.8 copy-done.2
  122.6 4.2 %all-to-all-start.1 = ((f32[8,160,128]{2,1,0:T(8,128)}), f32[8,160,128]{2,1,0:T(8,128)}, u32[]{:S(2)}, u32[]{:S(2)}) async-start(f32[8,160,128]{2,1,0:T(8,128)} %bitcast.9), calls=%async_computation.1 | async-start | bytes 1310720 | tf_op jit(solution)/shard_map/all_to_all | solution.py:588
  126.8 1.1 copy-done.3
  127.9 1.2 copy-done.21
  129.1 4.2 %settle.3 = (bf16[64,16,128]{2,1,0:T(8,128)(2,1)S(1)}, bf16[64,16,128]{2,1,0:T(8,128)(2,1)}, bf16[64,16,128]{2,1,0:T(8,128)(2,1)}, bf16[64,16,128]{2,1,0:T(8,128...) custom-call(f32[10,128,128]{2,1,0:T(8,128)S(1)} %copy-done.3, ...), custom_call_target="tpu_custom_call" | custom-call | bytes 4194304 | tf_op jit(solution)/shard_map/settle/pallas_call | solution.py:166
  136.9 2.0 collective-permute-start.8
  138.9 1.8 sum_pieces.2.refs_1_
  140.7 10.0 %collective-permute-done.9.refs_0_.refs_3_ = bf16[64,16,128]{2,1,0:T(8,128)(2,1)S(1)} collective-permute-done((bf16[64,16,128]{2,1,0:T(8,128)(2,1)}, bf16[64,16,128]{2,1,0:T(8,128)(2,1)S(1)}, u32[]{:S(2)}, u32[]{:S(2)}) %collective-permute-start.9) | collective-permute-done | bytes 262176 | tf_op jit(solution)/shard_map/ppermute | solution.py:557
  150.7 2.3 collective-permute-done.10.refs_2_
  153.7 1.6 add.4.refs_1_
  155.6 2.4 collective-permute-start.12
  157.9 0.8 collective-permute-start.13
  158.7 1.2 collective-permute-start.14
  160.0 2.4 collective-permute-start.15
  162.3 5.7 %collective-permute-done.11.refs_2_ = f32[160,128]{1,0:T(8,128)S(1)} collective-permute-done((f32[160,128]{1,0:T(8,128)}, f32[160,128]{1,0:T(8,128)S(1)}, u32[]{:S(2)}, u32[]{:S(2)}) %collective-permute-start.11) | collective-permute-done | bytes 81952 | tf_op jit(solution)/shard_map/ppermute | solution.py:557
  168.6 1.6 add.5
  170.2 10.7 %all_gather.3 = f32[1280,128]{1,0:T(8,128)S(1)} all-gather(f32[160,128]{1,0:T(8,128)} %add.5), channel_id=1, replica_groups=mesh['space'=8,'snap'=4] {'space'}, dimensions={0}, use_global_device_ids=true | all-gather | bytes 737280 | tf_op jit(solution)/shard_map/all_gather | solution.py:609
  180.9 4.9 %factor.4.refs_0_ = f32[4,8,128,128]{3,2,1,0:T(8,128)S(1)} custom-call(f32[10,128,128]{2,1,0:T(8,128)S(1)} %bitcast.10), custom_call_target="tpu_custom_call" | custom-call | flops 7000000000 | bytes 655360 | tf_op jit(solution)/shard_map/factor/pallas_call | solution.py:401
  185.8 4.8 %factor.5.refs_0_ = f32[4,8,128,128]{3,2,1,0:T(8,128)S(1)} custom-call(f32[4,8,128,128]{3,2,1,0:T(8,128)S(1)} %factor.4.refs_0_), custom_call_target="tpu_custom_call", output_to_operand_aliasing={{}: (0, {})} | custom-call | flops 7000000000 | bytes 2097152 | tf_op jit(solution)/shard_map/factor/pallas_call | solution.py:401
  190.7 4.6 %factor.6.refs_0_.refs_1_ = f32[4,8,128,128]{3,2,1,0:T(8,128)S(1)} custom-call(f32[4,8,128,128]{3,2,1,0:T(8,128)S(1)} %factor.5.refs_0_), custom_call_target="tpu_custom_call", output_to_operand_aliasing={{}: (0, {})} | custom-call | flops 7000000000 | bytes 2097152 | tf_op jit(solution)/shard_map/factor/pallas_call | solution.py:401
  195.6 4.5 %cross_sum.1.refs_0_ = f32[512,512]{1,0:T(8,128)} custom-call(f32[4,8,128,128]{3,2,1,0:T(8,128)S(1)} %factor.6.refs_0_.refs_1_, bf16[4,64,32,128]{3,2,1,0:T(8,128)(2,1)S(1)} %all-to-all-done.refs_1_.refs_0_.refs_2_, bf16[64,16,128]{2,1,0:T(8,128)(2,1)S(1)} %copy-done.18, bf16[64,16,128]{2,1,0:T(8,128)(2,1)S(1)} %copy-done.14, ...), custom_call_target="tpu_custom_call" | custom-call | flops 1073741824 | bytes 4194304 | tf_op jit(solution)/shard_map/cross_sum/pallas_call | solution.py:263
  200.1 4.2 %all-to-all-start.2 = ((f32[8,64,512]{2,1,0:T(8,128)}), f32[8,64,512]{2,1,0:T(8,128)}, u32[]{:S(2)}, u32[]{:S(2)}) async-start(f32[8,64,512]{2,1,0:T(8,128)} %bitcast.5), calls=%async_computation.2 | async-start | bytes 2097152 | tf_op jit(solution)/shard_map/all_to_all | solution.py:588
  204.3 1.6 copy-done.5
  205.9 5.4 %factor.7 = (f32[512,512]{1,0:T(8,128)}, f32[512,512]{1,0:T(8,128)S(1)}, bf16[512,512]{1,0:T(8,128)(2,1)S(1)}, bf16[512,512]{1,0:T(8,128)(2,1)S(1)}, bf16[512,512]{1,0:T(8,128)(2,1)S(1)}) custom-call(f32[512,512]{1,0:T(8,128)} %cross_sum.1.refs_0_, f32[4,8,128,128]{3,2,1,0:T(8,128)S(1)} %copy-done.5), custom_call_target="tpu_custom_call" | custom-call | flops 7000000000 | bytes 2097152 | tf_op jit(solution)/shard_map/factor/pallas_call | solution.py:401
  211.3 1.0 copy-done.11
  212.3 3.5 %basis.2.refs_0_ = f32[64,32,512]{2,1,0:T(8,128)} custom-call(bf16[4,64,32,128]{3,2,1,0:T(8,128)(2,1)S(1)} %all-to-all-done.refs_1_.refs_0_.refs_2_, bf16[512,512]{1,0:T(8,128)(2,1)S(1)} %get-tuple-element.52.refs_1_.refs_3_, bf16[512,512]{1,0:T(8,128)(2,1)S(1)} %get-tuple-element.53.refs_2_.refs_4_, bf16[512,512]{1,0:T(8,128)(2,1)S(1)} %get-tuple-element.54.refs_3_.refs_5_), custom_call_target="tpu_custom_call" | custom-call | flops 1610612736 | bytes 3145728 | tf_op jit(solution)/shard_map/basis/pallas_call | solution.py:457
  215.8 0.8 copy-done.8
  216.6 3.1 %all-to-all-done.2 = f32[8,64,512]{2,1,0:T(8,128)} async-done(((f32[8,64,512]{2,1,0:T(8,128)}), f32[8,64,512]{2,1,0:T(8,128)}, u32[]{:S(2)}, u32[]{:S(2)}) %all-to-all-start.2) | async-done | bytes 1048608 | tf_op jit(solution)/shard_map/all_to_all | solution.py:588
  219.7 1.9 sum_pieces.3.refs_1_
  221.7 0.8 collective-permute-start.16
  222.5 1.0 copy-done.9
  223.5 0.9 copy-done.10
  224.4 3.5 %basis.3.refs_0_ = f32[64,32,512]{2,1,0:T(8,128)} custom-call(f32[64,32,512]{2,1,0:T(8,128)} %basis.2.refs_0_, f32[64,512]{1,0:T(8,128)S(1)} %copy-done.10, bf16[4,64,32,128]{3,2,1,0:T(8,128)(2,1)S(1)} %all-to-all-done.refs_1_.refs_0_.refs_2_, bf16[512,512]{1,0:T(8,128)(2,1)S(1)} %get-tuple-element.52.refs_1_.refs_3_, ...), custom_call_target="tpu_custom_call", output_to_operand_aliasing={{}: (0, {})} | custom-call | flops 1610612736 | bytes 3145728 | tf_op jit(solution)/shard_map/basis/pallas_call | solution.py:457
  228.6 1.6 add.6.refs_0_
  230.2 1.3 collective-permute-start.17
  231.5 6.2 %collective-permute-done.17.refs_1_ = f32[64,512]{1,0:T(8,128)S(1)} collective-permute-done((f32[64,512]{1,0:T(8,128)}, f32[64,512]{1,0:T(8,128)S(1)}, u32[]{:S(2)}, u32[]{:S(2)}) %collective-permute-start.17) | collective-permute-done | bytes 131104 | tf_op jit(solution)/shard_map/ppermute | solution.py:557
  238.3 1.6 add.7.refs_0_
  240.0 1.9 collective-permute-start.20
  241.9 1.7 collective-permute-start.19
  243.6 3.6 %collective-permute-done.20.refs_3_ = f32[64,512]{1,0:T(8,128)S(1)} collective-permute-done((f32[64,512]{1,0:T(8,128)}, f32[64,512]{1,0:T(8,128)S(1)}, u32[]{:S(2)}, u32[]{:S(2)}) %collective-permute-start.20) | collective-permute-done | bytes 131104 | tf_op jit(solution)/shard_map/ppermute | solution.py:557
  247.9 0.8 collective-permute-done.18.refs_1_
  249.4 1.9 join.1.refs_1_
  251.3 2.1 collective-permute-done.21.refs_2_
  253.5 1.0 copy-done.7
  254.5 2.9 %project.1 = f32[512,512]{1,0:T(8,128)} custom-call(f32[512,512]{1,0:T(8,128)S(1)} %copy-done.12, f32[256,512]{1,0:T(8,128)S(1)} %copy-done.7, f32[256,512]{1,0:T(8,128)S(1)} %collective-permute-done.21.refs_2_), custom_call_target="tpu_custom_call" | custom-call | tf_op jit(solution)/shard_map/project/pallas_call | solution.py:545
  (85 shorter events, 10.5 us)
Async XLA Ops:
  0.6 2.2 copy-start
  2.8 0.7 copy-start.22
  3.5 3.6 %copy-start.1 = (bf16[128,128,128]{2,1,0:T(8,128)(2,1)S(1)}, bf16[128,128,128]{2,1,0:T(8,128)(2,1)}, u32[]{:S(2)}) copy-start(bf16[128,128,128]{2,1,0:T(8,128)(2,1)} %param.4) | copy-start | bytes 12582916
  3.5 3.6 %copy-start.23 = (s32[128]{0:T(128)S(1)}, s32[128]{0:T(128)}, u32[]{:S(2)}) copy-start(s32[128]{0:T(128)} %refs_0_.3) | copy-start | bytes 1540
  6.2 4.7 %collective-permute-start = (bf16[516,16,128]{2,1,0:T(8,128)(2,1)S(1)}, bf16[516,16,128]{2,1,0:T(8,128)(2,1)S(1)}, u32[]{:S(2)}, u32[]{:S(2)}) collective-permute-start(bf16[516,16,128]{2,1,0:T(8,128)(2,1)S(1)} %get-tuple-element.31), channel_id=1, source_target_pairs={{0,4},{4,0},{8,12},{12,8},{16,20},{20,16},{24,28},{28,24},{1,5},{5... | collective-permute-start | bytes 6340616 | tf_op jit(solution)/shard_map/ppermute | solution.py:557
  9.7 6.0 %collective-permute-start.3 = (bf16[512,16,128]{2,1,0:T(8,128)(2,1)S(1)}, bf16[512,16,128]{2,1,0:T(8,128)(2,1)S(1)}, u32[]{:S(2)}, u32[]{:S(2)}) collective-permute-start(bf16[512,16,128]{2,1,0:T(8,128)(2,1)S(1)} %get-tuple-element.35), channel_id=1, source_target_pairs={{0,4},{4,0},{8,12},{12,8},{16,20},{20,16},{24,28},{28,24},{1,5},{5... | collective-permute-start | bytes 6291464 | tf_op jit(solution)/shard_map/ppermute | solution.py:557
  11.1 27.2 %collective-permute-start.1 = (bf16[258,16,128]{2,1,0:T(8,128)(2,1)S(1)}, bf16[258,16,128]{2,1,0:T(8,128)(2,1)S(1)}, u32[]{:S(2)}, u32[]{:S(2)}) collective-permute-start(bf16[258,16,128]{2,1,0:T(8,128)(2,1)S(1)} %get-tuple-element.32), channel_id=1, source_target_pairs={{0,8},{4,12},{8,0},{12,4},{16,24},{20,28},{24,16},{28,20},{1,9},{5... | collective-permute-start | bytes 3170312 | tf_op jit(solution)/shard_map/ppermute | solution.py:557
  14.1 48.0 %collective-permute-start.2 = (bf16[258,16,128]{2,1,0:T(8,128)(2,1)S(1)}, bf16[258,16,128]{2,1,0:T(8,128)(2,1)S(1)}, u32[]{:S(2)}, u32[]{:S(2)}) collective-permute-start(bf16[258,16,128]{2,1,0:T(8,128)(2,1)S(1)} %get-tuple-element.33), channel_id=1, source_target_pairs={{0,16},{4,20},{8,24},{12,28},{16,0},{20,4},{24,8},{28,12},{1,17},{... | collective-permute-start | bytes 3170312 | tf_op jit(solution)/shard_map/ppermute | solution.py:557
  15.5 46.9 %collective-permute-start.4 = (bf16[258,16,128]{2,1,0:T(8,128)(2,1)S(1)}, bf16[258,16,128]{2,1,0:T(8,128)(2,1)S(1)}, u32[]{:S(2)}, u32[]{:S(2)}) collective-permute-start(bf16[258,16,128]{2,1,0:T(8,128)(2,1)S(1)} %get-tuple-element.38), channel_id=1, source_target_pairs={{0,24},{4,28},{8,16},{12,20},{16,8},{20,12},{24,0},{28,4},{1,25},{... | collective-permute-start | bytes 3170312 | tf_op jit(solution)/shard_map/ppermute | solution.py:557
  62.4 2.8 %copy-start.24 = (bf16[256,16,128]{2,1,0:T(8,128)(2,1)}, bf16[256,16,128]{2,1,0:T(8,128)(2,1)S(1)}, u32[]{:S(2)}) copy-start(bf16[256,16,128]{2,1,0:T(8,128)(2,1)S(1)} %get-tuple-element.43) | copy-start | bytes 3145732
  62.4 2.8 %copy-start.25 = (bf16[256,16,128]{2,1,0:T(8,128)(2,1)}, bf16[256,16,128]{2,1,0:T(8,128)(2,1)S(1)}, u32[]{:S(2)}) copy-start(bf16[256,16,128]{2,1,0:T(8,128)(2,1)S(1)} %get-tuple-element.42) | copy-start | bytes 3145732
  62.4 2.8 %copy-start.26 = (bf16[256,16,128]{2,1,0:T(8,128)(2,1)}, bf16[256,16,128]{2,1,0:T(8,128)(2,1)S(1)}, u32[]{:S(2)}) copy-start(bf16[256,16,128]{2,1,0:T(8,128)(2,1)S(1)} %get-tuple-element.40) | copy-start | bytes 3145732
  65.3 1.3 copy-start.6
  66.6 52.1 %all-to-all-start = ((bf16[4,64,32,128]{3,2,1,0:T(8,128)(2,1)}), bf16[4,64,32,128]{3,2,1,0:T(8,128)(2,1)S(1)}, u32[]{:S(2)}, u32[]{:S(2)}) async-start(bf16[4,64,32,128]{3,2,1,0:T(8,128)(2,1)} %copy-done.6), calls=%async_computation | async-start | bytes 4194304 | tf_op jit(solution)/shard_map/all_to_all | solution.py:600
  71.4 26.3 %collective-permute-start.5 = (bf16[256,16,128]{2,1,0:T(8,128)(2,1)}, bf16[256,16,128]{2,1,0:T(8,128)(2,1)S(1)}, u32[]{:S(2)}, u32[]{:S(2)}) collective-permute-start(bf16[256,16,128]{2,1,0:T(8,128)(2,1)} %copy-done.26), channel_id=1, source_target_pairs={{0,8},{4,12},{8,0},{12,4},{16,24},{20,28},{24,16},{28,20},{1,9},{5... | collective-permute-start | bytes 3145736 | tf_op jit(solution)/shard_map/ppermute | solution.py:557
  72.2 54.6 %collective-permute-start.6 = (bf16[256,16,128]{2,1,0:T(8,128)(2,1)}, bf16[256,16,128]{2,1,0:T(8,128)(2,1)}, u32[]{:S(2)}, u32[]{:S(2)}) collective-permute-start(bf16[256,16,128]{2,1,0:T(8,128)(2,1)} %copy-done.25), channel_id=1, source_target_pairs={{0,16},{4,20},{8,24},{12,28},{16,0},{20,4},{24,8},{28,12},{1,17},{... | collective-permute-start | bytes 3145736 | tf_op jit(solution)/shard_map/ppermute | solution.py:557
  72.9 53.9 %collective-permute-start.7 = (bf16[256,16,128]{2,1,0:T(8,128)(2,1)}, bf16[256,16,128]{2,1,0:T(8,128)(2,1)}, u32[]{:S(2)}, u32[]{:S(2)}) collective-permute-start(bf16[256,16,128]{2,1,0:T(8,128)(2,1)} %copy-done.24), channel_id=1, source_target_pairs={{0,24},{4,28},{8,16},{12,20},{16,8},{20,12},{24,0},{28,4},{1,25},{... | collective-permute-start | bytes 3145736 | tf_op jit(solution)/shard_map/ppermute | solution.py:557
  97.8 1.0 copy-start.19
  118.6 1.2 copy-start.20
  121.8 0.8 copy-start.2
  122.6 16.3 %all-to-all-start.1 = ((f32[8,160,128]{2,1,0:T(8,128)}), f32[8,160,128]{2,1,0:T(8,128)}, u32[]{:S(2)}, u32[]{:S(2)}) async-start(f32[8,160,128]{2,1,0:T(8,128)} %bitcast.9), calls=%async_computation.1 | async-start | bytes 1310720 | tf_op jit(solution)/shard_map/all_to_all | solution.py:588
  126.8 1.1 copy-start.3
  127.9 1.2 copy-start.21
  133.4 0.7 copy-start.17
  134.1 0.7 copy-start.27
  134.8 0.7 copy-start.28
  135.5 0.7 copy-start.29
  136.2 0.7 copy-start.30
  136.9 13.8 %collective-permute-start.9 = (bf16[64,16,128]{2,1,0:T(8,128)(2,1)}, bf16[64,16,128]{2,1,0:T(8,128)(2,1)S(1)}, u32[]{:S(2)}, u32[]{:S(2)}) collective-permute-start(bf16[64,16,128]{2,1,0:T(8,128)(2,1)} %get-tuple-element.45), channel_id=1, source_target_pairs={{0,1},{1,0},{2,3},{3,2},{4,5},{5,4},{6,7},{7,6},{8,9},{9,8},{10,11... | collective-permute-start | bytes 786440 | tf_op jit(solution)/shard_map/ppermute | solution.py:557
  136.9 23.1 %collective-permute-start.8 = (bf16[64,16,128]{2,1,0:T(8,128)(2,1)}, bf16[64,16,128]{2,1,0:T(8,128)(2,1)S(1)}, u32[]{:S(2)}, u32[]{:S(2)}) collective-permute-start(bf16[64,16,128]{2,1,0:T(8,128)(2,1)} %get-tuple-element.44), channel_id=1, source_target_pairs={{0,2},{1,3},{2,0},{3,1},{4,6},{5,7},{6,4},{7,5},{8,10},{9,11},{10,... | collective-permute-start | bytes 786440 | tf_op jit(solution)/shard_map/ppermute | solution.py:557
  140.7 12.4 %collective-permute-start.10 = (f32[160,128]{1,0:T(8,128)}, f32[160,128]{1,0:T(8,128)S(1)}, u32[]{:S(2)}, u32[]{:S(2)}) collective-permute-start(f32[160,128]{1,0:T(8,128)} %sum_pieces.2.refs_1_), channel_id=1, source_target_pairs={{0,1},{1,0},{2,3},{3,2},{4,5},{5,4},{6,7},{7,6},{8,9},{9,8},{10,11... | collective-permute-start | bytes 245768 | tf_op jit(solution)/shard_map/ppermute | solution.py:557
  150.7 2.3 copy-start.13
  153.0 0.6 copy-start.37
  155.3 12.7 %collective-permute-start.11 = (f32[160,128]{1,0:T(8,128)}, f32[160,128]{1,0:T(8,128)S(1)}, u32[]{:S(2)}, u32[]{:S(2)}) collective-permute-start(f32[160,128]{1,0:T(8,128)} %add.4.refs_1_), channel_id=1, source_target_pairs={{0,2},{1,3},{2,0},{3,1},{4,6},{5,7},{6,4},{7,5},{8,10},{9,11},{10,... | collective-permute-start | bytes 245768 | tf_op jit(solution)/shard_map/ppermute | solution.py:557
  155.6 39.7 %collective-permute-start.12 = (bf16[64,16,128]{2,1,0:T(8,128)(2,1)}, bf16[64,16,128]{2,1,0:T(8,128)(2,1)S(1)}, u32[]{:S(2)}, u32[]{:S(2)}) collective-permute-start(bf16[64,16,128]{2,1,0:T(8,128)(2,1)} %copy-done.30), channel_id=1, source_target_pairs={{0,3},{1,2},{2,1},{3,0},{4,7},{5,6},{6,5},{7,4},{8,11},{9,10},{10,... | collective-permute-start | bytes 786440 | tf_op jit(solution)/shard_map/ppermute | solution.py:557
  157.9 37.3 %collective-permute-start.13 = (bf16[64,16,128]{2,1,0:T(8,128)(2,1)}, bf16[64,16,128]{2,1,0:T(8,128)(2,1)S(1)}, u32[]{:S(2)}, u32[]{:S(2)}) collective-permute-start(bf16[64,16,128]{2,1,0:T(8,128)(2,1)} %copy-done.29), channel_id=1, source_target_pairs={{0,1},{1,0},{2,3},{3,2},{4,5},{5,4},{6,7},{7,6},{8,9},{9,8},{10,11... | collective-permute-start | bytes 786440 | tf_op jit(solution)/shard_map/ppermute | solution.py:557
  158.7 36.5 %collective-permute-start.14 = (bf16[64,16,128]{2,1,0:T(8,128)(2,1)}, bf16[64,16,128]{2,1,0:T(8,128)(2,1)S(1)}, u32[]{:S(2)}, u32[]{:S(2)}) collective-permute-start(bf16[64,16,128]{2,1,0:T(8,128)(2,1)} %copy-done.28), channel_id=1, source_target_pairs={{0,2},{1,3},{2,0},{3,1},{4,6},{5,7},{6,4},{7,5},{8,10},{9,11},{10,... | collective-permute-start | bytes 786440 | tf_op jit(solution)/shard_map/ppermute | solution.py:557
  160.0 8.0 %copy-start.15 = (bf16[64,16,128]{2,1,0:T(8,128)(2,1)}, bf16[64,16,128]{2,1,0:T(8,128)(2,1)S(1)}, u32[]{:S(2)}) copy-start(bf16[64,16,128]{2,1,0:T(8,128)(2,1)S(1)} %collective-permute-done.8.refs_0_.refs_4_) | copy-start | bytes 786436
  160.0 35.3 %collective-permute-start.15 = (bf16[64,16,128]{2,1,0:T(8,128)(2,1)}, bf16[64,16,128]{2,1,0:T(8,128)(2,1)}, u32[]{:S(2)}, u32[]{:S(2)}) collective-permute-start(bf16[64,16,128]{2,1,0:T(8,128)(2,1)} %copy-done.27), channel_id=1, source_target_pairs={{0,3},{1,2},{2,1},{3,0},{4,7},{5,6},{6,5},{7,4},{8,11},{9,10},{10,... | collective-permute-start | bytes 786440 | tf_op jit(solution)/shard_map/ppermute | solution.py:557
  168.0 0.6 copy-start.36
  190.6 4.7 %copy-start.14 = (bf16[64,16,128]{2,1,0:T(8,128)(2,1)S(1)}, bf16[64,16,128]{2,1,0:T(8,128)(2,1)}, u32[]{:S(2)}) copy-start(bf16[64,16,128]{2,1,0:T(8,128)(2,1)} %copy-done.13) | copy-start | bytes 786436
  190.7 4.7 %copy-start.16 = (bf16[64,16,128]{2,1,0:T(8,128)(2,1)S(1)}, bf16[64,16,128]{2,1,0:T(8,128)(2,1)}, u32[]{:S(2)}) copy-start(bf16[64,16,128]{2,1,0:T(8,128)(2,1)} %copy-done.15) | copy-start | bytes 786436
  190.7 4.9 %copy-start.18 = (bf16[64,16,128]{2,1,0:T(8,128)(2,1)S(1)}, bf16[64,16,128]{2,1,0:T(8,128)(2,1)}, u32[]{:S(2)}) copy-start(bf16[64,16,128]{2,1,0:T(8,128)(2,1)} %copy-done.17) | copy-start | bytes 786436
  195.2 4.8 %copy-start.4 = (f32[4,8,128,128]{3,2,1,0:T(8,128)}, f32[4,8,128,128]{3,2,1,0:T(8,128)S(1)}, u32[]{:S(2)}) copy-start(f32[4,8,128,128]{3,2,1,0:T(8,128)S(1)} %factor.6.refs_0_.refs_1_) | copy-start | bytes 6291460
  200.1 19.7 %all-to-all-start.2 = ((f32[8,64,512]{2,1,0:T(8,128)}), f32[8,64,512]{2,1,0:T(8,128)}, u32[]{:S(2)}, u32[]{:S(2)}) async-start(f32[8,64,512]{2,1,0:T(8,128)} %bitcast.5), calls=%async_computation.2 | async-start | bytes 2097152 | tf_op jit(solution)/shard_map/all_to_all | solution.py:588
  204.3 1.6 copy-start.5
  211.3 1.0 copy-start.11
  215.8 0.8 copy-start.8
  221.7 6.3 %collective-permute-start.16 = (f32[64,512]{1,0:T(8,128)}, f32[64,512]{1,0:T(8,128)S(1)}, u32[]{:S(2)}, u32[]{:S(2)}) collective-permute-start(f32[64,512]{1,0:T(8,128)} %sum_pieces.3.refs_1_), channel_id=1, source_target_pairs={{0,1},{1,0},{2,3},{3,2},{4,5},{5,4},{6,7},{7,6},{8,9},{9,8},{10,11... | collective-permute-start | bytes 393224 | tf_op jit(solution)/shard_map/ppermute | solution.py:557
  222.5 1.0 copy-start.9
  223.5 0.9 copy-start.10
  227.9 25.5 %copy-start.12 = (f32[512,512]{1,0:T(8,128)S(1)}, f32[512,512]{1,0:T(8,128)}, u32[]{:S(2)}) copy-start(f32[512,512]{1,0:T(8,128)} %copy-done.11) | copy-start | bytes 3145732
  227.9 0.7 copy-start.31
  230.2 7.5 %collective-permute-start.17 = (f32[64,512]{1,0:T(8,128)}, f32[64,512]{1,0:T(8,128)S(1)}, u32[]{:S(2)}, u32[]{:S(2)}) collective-permute-start(f32[64,512]{1,0:T(8,128)} %add.6.refs_0_), channel_id=1, source_target_pairs={{0,2},{1,3},{2,0},{3,1},{4,6},{5,7},{6,4},{7,5},{8,10},{9,11},{10,... | collective-permute-start | bytes 393224 | tf_op jit(solution)/shard_map/ppermute | solution.py:557
  237.7 0.7 copy-start.32
  240.0 7.2 %collective-permute-start.20 = (f32[64,512]{1,0:T(8,128)}, f32[64,512]{1,0:T(8,128)S(1)}, u32[]{:S(2)}, u32[]{:S(2)}) collective-permute-start(f32[64,512]{1,0:T(8,128)} %add.7.refs_0_), channel_id=1, source_target_pairs={{0,24},{4,28},{8,16},{12,20},{16,8},{20,12},{24,0},{28,4},{1,25},{... | collective-permute-start | bytes 393224 | tf_op jit(solution)/shard_map/ppermute | solution.py:557
  241.9 6.0 %collective-permute-start.19 = (f32[64,512]{1,0:T(8,128)}, f32[64,512]{1,0:T(8,128)S(1)}, u32[]{:S(2)}, u32[]{:S(2)}) collective-permute-start(f32[64,512]{1,0:T(8,128)} %add.7.refs_0_), channel_id=1, source_target_pairs={{0,16},{4,20},{8,24},{12,28},{16,0},{20,4},{24,8},{28,12},{1,17},{... | collective-permute-start | bytes 393224 | tf_op jit(solution)/shard_map/ppermute | solution.py:557
  243.6 5.2 %collective-permute-start.18 = (f32[64,512]{1,0:T(8,128)}, f32[64,512]{1,0:T(8,128)S(1)}, u32[]{:S(2)}, u32[]{:S(2)}) collective-permute-start(f32[64,512]{1,0:T(8,128)} %add.7.refs_0_), channel_id=1, source_target_pairs={{0,8},{4,12},{8,0},{12,4},{16,24},{20,28},{24,16},{28,20},{1,9},{5... | collective-permute-start | bytes 393224 | tf_op jit(solution)/shard_map/ppermute | solution.py:557
  247.2 1.5 copy-start.33
  247.9 0.8 copy-start.34
  248.8 0.7 copy-start.35
  251.3 2.1 collective-permute-start.21
  253.4 1.0 copy-start.7

commit v16 on v15

--- a/solution.py
+++ b/solution.py
@@ -605,22 +605,23 @@
     y_cells = [to_rows(pieces[part * shares : (part + 1) * shares]) for part in range(parts)]
     gram = sum_pieces(gram, slabs, pieces[:1])
     for hop in hops():
-        gram = add(gram, swap(gram, "snap", hop), y_cells[0][hop : hop + 1])
+        gram = add(gram, swap(gram, "snap", hop), [] if hop == 1 else y_cells[0][1:3])
     gram = lax.all_gather(gram, "space", axis=0, tiled=True)
 
     steps = factor_steps(gram.reshape(pairs, TILE, TILE), tiles, rows_total, [])
     state = next(steps)
-    for _ in range(tiles - 2):
+    for _ in range(tiles - 3):
         state = steps.send([])
     cross_local = cross_sum(x_cells, y_cells, [state])
     cross = to_pieces(cross_local)
-    r_factor, inverse, *terms = steps.send([cross_local])
-
-    q_basis = basis(x_cells, terms, 0, 2, None, [])
-    cross = sum_pieces(cross, slabs, [q_basis])
-    q_basis = basis(x_cells, terms, 1, 2, q_basis, [cross])
-    for hop in hops():
-        cross = add(cross, swap(cross, "snap", hop), [q_basis] if hop == 1 else [])
+    state = steps.send([cross_local])
+    r_factor, inverse, *terms = steps.send([])
+
+    cross = sum_pieces(cross, slabs, [r_factor])
+    q_basis = None
+    for call, hop in enumerate(hops()):
+        q_basis = basis(x_cells, terms, call, 2, q_basis, [cross])
+        cross = add(cross, swap(cross, "snap", hop), [q_basis])
     same = join([cross] + [swap(cross, "space", m) for m in range(CORES, slabs, CORES)], [])
     projection = project(inverse, same, swap(same, "space", 1), slabs, math.sqrt(rows_total))
     return q_basis, r_factor, projection

time: 259 us -> 260 us (level)
  waiting for transfers between devices: 124 us -> 119 us
  starting transfers between devices: 37.5 us -> 40.3 us
    ppermute x22, waiting for transfers between devices: 101 us -> 96.8 us  [swap(): lax.ppermute(value, axis, [(i, i ^ mask) for i in range(lax.axis_size(axi...]
    unnamed x76 -> x80, local copies, waits for them, and re-layouts: 22.7 us -> 25.1 us
where the time goes in v16:
time: 260 us; the launch traced here: 258 us
  waiting for transfers between devices  119 us (46%)
  Pallas kernels  62.4 us (24%)
  starting transfers between devices  40.3 us (15%)
  local copies, waits for them, and re-layouts  25.1 us (10%)
  blocking collectives  10.7 us (4%)
    ppermute x22, waiting for transfers between devices, swap(): lax.ppermute(value, axis, [(i, i ^ mask) for i in range(lax.axis_size(axi...  96.8 us
    ppermute x22, starting transfers between devices, swap(): lax.ppermute(value, axis, [(i, i ^ mask) for i in range(lax.axis_size(axi...  26.7 us
    unnamed x80, local copies, waits for them, and re-layouts  25.1 us
    all_to_all x1, waiting for transfers between devices, body(): lax.all_to_all(pieces, 'snap', split_axis=0, concat_axis=0, tiled=True)  20.4 us
    pallas_call x4, Pallas kernels, factor_call(): pl.pallas_call(lambda *refs: kernel(*refs[len(after):]), out_shape=out_sh...  19.7 us
    all_gather x1, blocking collectives, body(): gram = lax.all_gather(gram, 'space', axis=0, tiled=True)  10.7 us
    all_to_all x2, starting transfers between devices, to_pieces(): lax.all_to_all(value, 'space', split_axis=0, concat_axis=0, tiled=True)  8.66 us
    pallas_call x2, Pallas kernels, settle(): pl.pallas_call(lambda *refs: settle_kernel(chips, capacity, parts, first,...  6.99 us
  transfers between devices with their start and end apart: 25, of which 14 were waited for; matrix products, arithmetic and copies ran while one was open for 0% of the time, Pallas kernels for 16%

profile of v16, /device:TPU:0, one launch (start us, length us, event | category | flops | bytes accessed | tf_op | source)
XLA Modules:
  0.0 258.4 jit_solution(14581426745110032140)
XLA Ops:
  0.6 2.2 copy-done
  3.5 3.4 %pack.2 = (bf16[516,16,128]{2,1,0:T(8,128)(2,1)S(1)}, bf16[516,16,128]{2,1,0:T(8,128)(2,1)S(1)}) custom-call(s32[128]{0:T(128)S(1)} %copy-done.24, bf16[128,8,16,128]{3,2,1,0:T(8,128)(2,1)S(1)} %bitcast.7), custom_call_target="tpu_custom_call" | custom-call | bytes 8388608 | tf_op jit(solution)/shard_map/pack/pallas_call | solution.py:78
  7.0 3.4 %pack.3 = (bf16[512,16,128]{2,1,0:T(8,128)(2,1)S(1)}, bf16[512,16,128]{2,1,0:T(8,128)(2,1)S(1)}) custom-call(s32[128]{0:T(128)S(1)} %copy-done.25, bf16[128,8,16,128]{3,2,1,0:T(8,128)(2,1)S(1)} %bitcast.8), custom_call_target="tpu_custom_call" | custom-call | bytes 8388608 | tf_op jit(solution)/shard_map/pack/pallas_call | solution.py:78
  11.4 2.4 collective-permute-start.1
  13.9 2.2 collective-permute-start.2
  16.2 21.9 %collective-permute-done.1.refs_0_.refs_2_ = bf16[258,16,128]{2,1,0:T(8,128)(2,1)S(1)} collective-permute-done((bf16[258,16,128]{2,1,0:T(8,128)(2,1)S(1)}, bf16[258,16,128]{2,1,0:T(8,128)(2,1)S(1)}, u32[]{:S(2)}, u32[]{:S(2)}) %collective-permute-start.1) | collective-permute-done | bytes 1056800 | tf_op jit(solution)/shard_map/ppermute | solution.py:557
  38.0 23.3 %collective-permute-done.2.refs_1_.refs_3_ = bf16[258,16,128]{2,1,0:T(8,128)(2,1)S(1)} collective-permute-done((bf16[258,16,128]{2,1,0:T(8,128)(2,1)S(1)}, bf16[258,16,128]{2,1,0:T(8,128)(2,1)S(1)}, u32[]{:S(2)}, u32[]{:S(2)}) %collective-permute-start.2) | collective-permute-done | bytes 1056800 | tf_op jit(solution)/shard_map/ppermute | solution.py:557
  62.2 2.8 %settle.2 = (bf16[4,64,32,128]{3,2,1,0:T(8,128)(2,1)S(1)}, s32[8,128]{1,0:T(8,128)S(1)}) custom-call(bf16[256,16,128]{2,1,0:T(8,128)(2,1)S(1)} %get-tuple-element.37.refs_0_.refs_2_, bf16[258,16,128]{2,1,0:T(8,128)(2,1)S(1)} %get-tuple-element.38.refs_1_, bf16[258,16,128]{2,1,0:T(8,128)(2,1)S(1)} %collective-permute-done.1.refs_0_.refs_2_, ...), custom_call_target="tpu_custom_call" | custom-call | bytes 4227072 | tf_op jit(solution)/shard_map/settle/pallas_call | solution.py:166
  65.0 1.3 copy-done.6
  66.3 4.9 %all-to-all-start = ((bf16[4,64,32,128]{3,2,1,0:T(8,128)(2,1)}), bf16[4,64,32,128]{3,2,1,0:T(8,128)(2,1)S(1)}, u32[]{:S(2)}, u32[]{:S(2)}) async-start(bf16[4,64,32,128]{3,2,1,0:T(8,128)(2,1)} %copy-done.6), calls=%async_computation | async-start | bytes 4194304 | tf_op jit(solution)/shard_map/all_to_all | solution.py:600
  71.2 1.4 collective-permute-start.4
  72.6 1.2 collective-permute-start.6
  73.8 0.9 collective-permute-start.7
  74.7 22.8 %collective-permute-done.4.refs_0_.refs_3_ = bf16[256,16,128]{2,1,0:T(8,128)(2,1)S(1)} collective-permute-done((bf16[256,16,128]{2,1,0:T(8,128)(2,1)}, bf16[256,16,128]{2,1,0:T(8,128)(2,1)S(1)}, u32[]{:S(2)}, u32[]{:S(2)}) %collective-permute-start.4) | collective-permute-done | bytes 1048608 | tf_op jit(solution)/shard_map/ppermute | solution.py:557
  97.5 1.0 copy-done.21
  98.4 20.4 %all-to-all-done.refs_1_.refs_2_ = bf16[4,64,32,128]{3,2,1,0:T(8,128)(2,1)S(1)} async-done(((bf16[4,64,32,128]{3,2,1,0:T(8,128)(2,1)}), bf16[4,64,32,128]{3,2,1,0:T(8,128)(2,1)S(1)}, u32[]{:S(2)}, u32[]{:S(2)}) %all-to-all-start) | async-done | bytes 2097184 | tf_op jit(solution)/shard_map/all_to_all | solution.py:600
  118.8 1.2 copy-done.22
  120.1 1.9 gram_blocks.1.refs_0_
  122.0 0.8 copy-done.2
  122.8 4.2 %all-to-all-start.1 = ((f32[8,160,128]{2,1,0:T(8,128)}), f32[8,160,128]{2,1,0:T(8,128)}, u32[]{:S(2)}, u32[]{:S(2)}) async-start(f32[8,160,128]{2,1,0:T(8,128)} %bitcast.9), calls=%async_computation.1 | async-start | bytes 1310720 | tf_op jit(solution)/shard_map/all_to_all | solution.py:588
  127.0 1.1 copy-done.3
  128.1 1.2 copy-done.23
  129.3 4.2 %settle.3 = (bf16[64,16,128]{2,1,0:T(8,128)(2,1)S(1)}, bf16[64,16,128]{2,1,0:T(8,128)(2,1)}, bf16[64,16,128]{2,1,0:T(8,128)(2,1)}, bf16[64,16,128]{2,1,0:T(8,128...) custom-call(f32[10,128,128]{2,1,0:T(8,128)S(1)} %copy-done.3, ...), custom_call_target="tpu_custom_call" | custom-call | bytes 4194304 | tf_op jit(solution)/shard_map/settle/pallas_call | solution.py:166
  135.7 0.7 copy-done.31
  137.1 2.0 collective-permute-start.9
  139.1 1.8 sum_pieces.2.refs_0_
  140.9 12.4 %collective-permute-done.10.refs_1_ = f32[160,128]{1,0:T(8,128)S(1)} collective-permute-done((f32[160,128]{1,0:T(8,128)}, f32[160,128]{1,0:T(8,128)S(1)}, u32[]{:S(2)}, u32[]{:S(2)}) %collective-permute-start.10) | collective-permute-done | bytes 81952 | tf_op jit(solution)/shard_map/ppermute | solution.py:557
  153.9 1.6 add.4.refs_2_
  155.8 2.4 collective-permute-start.12
  158.2 0.8 collective-permute-start.13
  159.0 1.2 collective-permute-start.14
  160.2 2.4 collective-permute-start.15
  162.6 5.6 %collective-permute-done.11.refs_3_ = f32[160,128]{1,0:T(8,128)S(1)} collective-permute-done((f32[160,128]{1,0:T(8,128)}, f32[160,128]{1,0:T(8,128)S(1)}, u32[]{:S(2)}, u32[]{:S(2)}) %collective-permute-start.11) | collective-permute-done | bytes 81952 | tf_op jit(solution)/shard_map/ppermute | solution.py:557
  168.8 1.6 add.5
  170.4 10.7 %all_gather.3 = f32[1280,128]{1,0:T(8,128)S(1)} all-gather(f32[160,128]{1,0:T(8,128)} %add.5), channel_id=1, replica_groups=mesh['space'=8,'snap'=4] {'space'}, dimensions={0}, use_global_device_ids=true | all-gather | bytes 737280 | tf_op jit(solution)/shard_map/all_gather | solution.py:609
  181.1 4.9 %factor.4.refs_0_ = f32[4,8,128,128]{3,2,1,0:T(8,128)S(1)} custom-call(f32[10,128,128]{2,1,0:T(8,128)S(1)} %bitcast.10), custom_call_target="tpu_custom_call" | custom-call | flops 7000000000 | bytes 655360 | tf_op jit(solution)/shard_map/factor/pallas_call | solution.py:401
  186.1 4.8 %factor.5.refs_0_.refs_1_ = f32[4,8,128,128]{3,2,1,0:T(8,128)S(1)} custom-call(f32[4,8,128,128]{3,2,1,0:T(8,128)S(1)} %factor.4.refs_0_), custom_call_target="tpu_custom_call", output_to_operand_aliasing={{}: (0, {})} | custom-call | flops 7000000000 | bytes 2097152 | tf_op jit(solution)/shard_map/factor/pallas_call | solution.py:401
  191.0 4.7 %cross_sum.1.refs_0_ = f32[512,512]{1,0:T(8,128)} custom-call(f32[4,8,128,128]{3,2,1,0:T(8,128)S(1)} %factor.5.refs_0_.refs_1_, bf16[4,64,32,128]{3,2,1,0:T(8,128)(2,1)S(1)} %all-to-all-done.refs_1_.refs_2_, bf16[64,16,128]{2,1,0:T(8,128)(2,1)S(1)} %copy-done.20, bf16[64,16,128]{2,1,0:T(8,128)(2,1)S(1)} %copy-done.16, bf16[64,16,128]{2,1,0:T(8,128)(2,1)S(1)} %copy-done.18, ...), custom_call_target="tpu_custom_call" | custom-call | flops 1073741824 | bytes 4194304 | tf_op jit(solution)/shard_map/cross_sum/pallas_call | solution.py:263
  195.7 4.5 %all-to-all-start.2 = ((f32[8,64,512]{2,1,0:T(8,128)}), f32[8,64,512]{2,1,0:T(8,128)}, u32[]{:S(2)}, u32[]{:S(2)}) async-start(f32[8,64,512]{2,1,0:T(8,128)} %bitcast.5), calls=%async_computation.2 | async-start | bytes 2097152 | tf_op jit(solution)/shard_map/all_to_all | solution.py:588
  200.1 1.6 copy-done.5
  201.7 4.6 %factor.6.refs_0_ = f32[4,8,128,128]{3,2,1,0:T(8,128)S(1)} custom-call(f32[512,512]{1,0:T(8,128)} %cross_sum.1.refs_0_, f32[4,8,128,128]{3,2,1,0:T(8,128)S(1)} %copy-done.5), custom_call_target="tpu_custom_call", output_to_operand_aliasing={{}: (1, {})} | custom-call | flops 7000000000 | bytes 2097152 | tf_op jit(solution)/shard_map/factor/pallas_call | solution.py:401
  206.3 5.4 %factor.7 = (f32[512,512]{1,0:T(8,128)}, f32[512,512]{1,0:T(8,128)S(1)}, bf16[512,512]{1,0:T(8,128)(2,1)S(1)}, bf16[512,512]{1,0:T(8,128)(2,1)S(1)}, bf16[512,512]{1,0:T(8,128)(2,1)S(1)}) custom-call(f32[4,8,128,128]{3,2,1,0:T(8,128)S(1)} %factor.6.refs_0_), custom_call_target="tpu_custom_call" | custom-call | flops 7000000000 | bytes 2097152 | tf_op jit(solution)/shard_map/factor/pallas_call | solution.py:401
  211.7 0.8 copy-done.8
  212.5 1.0 copy-done.13
  213.5 1.8 all-to-all-done.2
  215.3 1.9 sum_pieces.3.refs_0_.refs_1_
  217.3 5.5 %collective-permute-start.16 = (f32[64,512]{1,0:T(8,128)}, f32[64,512]{1,0:T(8,128)S(1)}, u32[]{:S(2)}, u32[]{:S(2)}) collective-permute-start(f32[64,512]{1,0:T(8,128)} %sum_pieces.3.refs_0_.refs_1_), channel_id=1, source_target_pairs={{0,1},{1,0},{2,3},{3,2},{4,5},{5,4},{6,7},{7,6},{8,9},{9,8},{10,11... | collective-permute-start | bytes 393224 | tf_op jit(solution)/shard_map/ppermute | solution.py:557
  222.8 1.0 copy-done.9
  223.8 0.9 copy-done.12
  224.7 3.5 %basis.2.refs_0_ = f32[64,32,512]{2,1,0:T(8,128)} custom-call(f32[64,512]{1,0:T(8,128)S(1)} %copy-done.12, bf16[4,64,32,128]{3,2,1,0:T(8,128)(2,1)S(1)} %all-to-all-done.refs_1_.refs_2_, bf16[512,512]{1,0:T(8,128)(2,1)S(1)} %get-tuple-element.53.refs_2_.refs_3_, bf16[512,512]{1,0:T(8,128)(2,1)S(1)} %get-tuple-element.54.refs_3_.refs_4_, ...), custom_call_target="tpu_custom_call" | custom-call | flops 1610612736 | bytes 3145728 | tf_op jit(solution)/shard_map/basis/pallas_call | solution.py:457
  228.9 1.6 add.6.refs_1_
  230.5 1.0 copy-done.10
  231.6 0.9 copy-done.11
  232.5 3.5 %basis.3.refs_0_ = f32[64,32,512]{2,1,0:T(8,128)} custom-call(f32[64,32,512]{2,1,0:T(8,128)} %basis.2.refs_0_, f32[64,512]{1,0:T(8,128)S(1)} %copy-done.11, bf16[4,64,32,128]{3,2,1,0:T(8,128)(2,1)S(1)} %all-to-all-done.refs_1_.refs_2_, bf16[512,512]{1,0:T(8,128)(2,1)S(1)} %get-tuple-element.53.refs_2_.refs_3_, ...), custom_call_target="tpu_custom_call", output_to_operand_aliasing={{}: (0, {})} | custom-call | flops 1610612736 | bytes 3145728 | tf_op jit(solution)/shard_map/basis/pallas_call | solution.py:457
  235.9 1.7 collective-permute-done.17.refs_2_
  238.2 1.6 add.7.refs_0_
  239.9 2.6 %collective-permute-start.20 = (f32[64,512]{1,0:T(8,128)}, f32[64,512]{1,0:T(8,128)S(1)}, u32[]{:S(2)}, u32[]{:S(2)}) collective-permute-start(f32[64,512]{1,0:T(8,128)} %add.7.refs_0_), channel_id=1, source_target_pairs={{0,24},{4,28},{8,16},{12,20},{16,8},{20,12},{24,0},{28,4},{1,25},{... | collective-permute-start | bytes 393224 | tf_op jit(solution)/shard_map/ppermute | solution.py:557
  242.5 1.1 collective-permute-start.19
  243.6 3.1 %collective-permute-done.20.refs_3_ = f32[64,512]{1,0:T(8,128)S(1)} collective-permute-done((f32[64,512]{1,0:T(8,128)}, f32[64,512]{1,0:T(8,128)S(1)}, u32[]{:S(2)}, u32[]{:S(2)}) %collective-permute-start.20) | collective-permute-done | bytes 131104 | tf_op jit(solution)/shard_map/ppermute | solution.py:557
  246.7 2.5 collective-permute-done.19.refs_2_
  250.5 1.9 join.1.refs_1_
  252.4 2.1 collective-permute-done.21.refs_2_
  254.5 1.0 copy-done.7
  255.6 2.9 %project.1 = f32[512,512]{1,0:T(8,128)} custom-call(f32[512,512]{1,0:T(8,128)S(1)} %copy-done.14, f32[256,512]{1,0:T(8,128)S(1)} %copy-done.7, f32[256,512]{1,0:T(8,128)S(1)} %collective-permute-done.21.refs_2_), custom_call_target="tpu_custom_call" | custom-call | tf_op jit(solution)/shard_map/project/pallas_call | solution.py:545
  (89 shorter events, 9.8 us)
Async XLA Ops:
  0.6 2.2 copy-start
  2.8 0.7 copy-start.24
  3.5 3.5 %copy-start.1 = (bf16[128,128,128]{2,1,0:T(8,128)(2,1)S(1)}, bf16[128,128,128]{2,1,0:T(8,128)(2,1)}, u32[]{:S(2)}) copy-start(bf16[128,128,128]{2,1,0:T(8,128)(2,1)} %param.4) | copy-start | bytes 12582916
  3.5 3.5 %copy-start.25 = (s32[128]{0:T(128)S(1)}, s32[128]{0:T(128)}, u32[]{:S(2)}) copy-start(s32[128]{0:T(128)} %refs_0_.3) | copy-start | bytes 1540
  6.9 4.2 %collective-permute-start = (bf16[516,16,128]{2,1,0:T(8,128)(2,1)S(1)}, bf16[516,16,128]{2,1,0:T(8,128)(2,1)S(1)}, u32[]{:S(2)}, u32[]{:S(2)}) collective-permute-start(bf16[516,16,128]{2,1,0:T(8,128)(2,1)S(1)} %get-tuple-element.31), channel_id=1, source_target_pairs={{0,4},{4,0},{8,12},{12,8},{16,20},{20,16},{24,28},{28,24},{1,5},{5... | collective-permute-start | bytes 6340616 | tf_op jit(solution)/shard_map/ppermute | solution.py:557
  10.4 5.8 %collective-permute-start.3 = (bf16[512,16,128]{2,1,0:T(8,128)(2,1)S(1)}, bf16[512,16,128]{2,1,0:T(8,128)(2,1)S(1)}, u32[]{:S(2)}, u32[]{:S(2)}) collective-permute-start(bf16[512,16,128]{2,1,0:T(8,128)(2,1)S(1)} %get-tuple-element.35), channel_id=1, source_target_pairs={{0,4},{4,0},{8,12},{12,8},{16,20},{20,16},{24,28},{28,24},{1,5},{5... | collective-permute-start | bytes 6291464 | tf_op jit(solution)/shard_map/ppermute | solution.py:557
  11.4 26.6 %collective-permute-start.1 = (bf16[258,16,128]{2,1,0:T(8,128)(2,1)S(1)}, bf16[258,16,128]{2,1,0:T(8,128)(2,1)S(1)}, u32[]{:S(2)}, u32[]{:S(2)}) collective-permute-start(bf16[258,16,128]{2,1,0:T(8,128)(2,1)S(1)} %get-tuple-element.32), channel_id=1, source_target_pairs={{0,8},{4,12},{8,0},{12,4},{16,24},{20,28},{24,16},{28,20},{1,9},{5... | collective-permute-start | bytes 3170312 | tf_op jit(solution)/shard_map/ppermute | solution.py:557
  13.9 47.5 %collective-permute-start.2 = (bf16[258,16,128]{2,1,0:T(8,128)(2,1)S(1)}, bf16[258,16,128]{2,1,0:T(8,128)(2,1)S(1)}, u32[]{:S(2)}, u32[]{:S(2)}) collective-permute-start(bf16[258,16,128]{2,1,0:T(8,128)(2,1)S(1)} %get-tuple-element.33), channel_id=1, source_target_pairs={{0,16},{4,20},{8,24},{12,28},{16,0},{20,4},{24,8},{28,12},{1,17},{... | collective-permute-start | bytes 3170312 | tf_op jit(solution)/shard_map/ppermute | solution.py:557
  16.1 46.1 %collective-permute-start.5 = (bf16[258,16,128]{2,1,0:T(8,128)(2,1)S(1)}, bf16[258,16,128]{2,1,0:T(8,128)(2,1)S(1)}, u32[]{:S(2)}, u32[]{:S(2)}) collective-permute-start(bf16[258,16,128]{2,1,0:T(8,128)(2,1)S(1)} %get-tuple-element.39), channel_id=1, source_target_pairs={{0,24},{4,28},{8,16},{12,20},{16,8},{20,12},{24,0},{28,4},{1,25},{... | collective-permute-start | bytes 3170312 | tf_op jit(solution)/shard_map/ppermute | solution.py:557
  61.6 3.3 %copy-start.26 = (bf16[256,16,128]{2,1,0:T(8,128)(2,1)}, bf16[256,16,128]{2,1,0:T(8,128)(2,1)S(1)}, u32[]{:S(2)}) copy-start(bf16[256,16,128]{2,1,0:T(8,128)(2,1)S(1)} %get-tuple-element.43) | copy-start | bytes 3145732
  61.6 3.3 %copy-start.27 = (bf16[256,16,128]{2,1,0:T(8,128)(2,1)}, bf16[256,16,128]{2,1,0:T(8,128)(2,1)S(1)}, u32[]{:S(2)}) copy-start(bf16[256,16,128]{2,1,0:T(8,128)(2,1)S(1)} %get-tuple-element.42) | copy-start | bytes 3145732
  61.6 3.3 %copy-start.28 = (bf16[256,16,128]{2,1,0:T(8,128)(2,1)}, bf16[256,16,128]{2,1,0:T(8,128)(2,1)S(1)}, u32[]{:S(2)}) copy-start(bf16[256,16,128]{2,1,0:T(8,128)(2,1)S(1)} %get-tuple-element.36) | copy-start | bytes 3145732
  65.0 1.3 copy-start.6
  66.3 52.5 %all-to-all-start = ((bf16[4,64,32,128]{3,2,1,0:T(8,128)(2,1)}), bf16[4,64,32,128]{3,2,1,0:T(8,128)(2,1)S(1)}, u32[]{:S(2)}, u32[]{:S(2)}) async-start(bf16[4,64,32,128]{3,2,1,0:T(8,128)(2,1)} %copy-done.6), calls=%async_computation | async-start | bytes 4194304 | tf_op jit(solution)/shard_map/all_to_all | solution.py:600
  71.2 26.3 %collective-permute-start.4 = (bf16[256,16,128]{2,1,0:T(8,128)(2,1)}, bf16[256,16,128]{2,1,0:T(8,128)(2,1)S(1)}, u32[]{:S(2)}, u32[]{:S(2)}) collective-permute-start(bf16[256,16,128]{2,1,0:T(8,128)(2,1)} %copy-done.28), channel_id=1, source_target_pairs={{0,8},{4,12},{8,0},{12,4},{16,24},{20,28},{24,16},{28,20},{1,9},{5... | collective-permute-start | bytes 3145736 | tf_op jit(solution)/shard_map/ppermute | solution.py:557
  72.6 54.4 %collective-permute-start.6 = (bf16[256,16,128]{2,1,0:T(8,128)(2,1)}, bf16[256,16,128]{2,1,0:T(8,128)(2,1)}, u32[]{:S(2)}, u32[]{:S(2)}) collective-permute-start(bf16[256,16,128]{2,1,0:T(8,128)(2,1)} %copy-done.27), channel_id=1, source_target_pairs={{0,16},{4,20},{8,24},{12,28},{16,0},{20,4},{24,8},{28,12},{1,17},{... | collective-permute-start | bytes 3145736 | tf_op jit(solution)/shard_map/ppermute | solution.py:557
  73.8 53.2 %collective-permute-start.7 = (bf16[256,16,128]{2,1,0:T(8,128)(2,1)}, bf16[256,16,128]{2,1,0:T(8,128)(2,1)}, u32[]{:S(2)}, u32[]{:S(2)}) collective-permute-start(bf16[256,16,128]{2,1,0:T(8,128)(2,1)} %copy-done.26), channel_id=1, source_target_pairs={{0,24},{4,28},{8,16},{12,20},{16,8},{20,12},{24,0},{28,4},{1,25},{... | collective-permute-start | bytes 3145736 | tf_op jit(solution)/shard_map/ppermute | solution.py:557
  97.5 1.0 copy-start.21
  118.8 1.2 copy-start.22
  122.0 0.8 copy-start.2
  122.8 16.3 %all-to-all-start.1 = ((f32[8,160,128]{2,1,0:T(8,128)}), f32[8,160,128]{2,1,0:T(8,128)}, u32[]{:S(2)}, u32[]{:S(2)}) async-start(f32[8,160,128]{2,1,0:T(8,128)} %bitcast.9), calls=%async_computation.1 | async-start | bytes 1310720 | tf_op jit(solution)/shard_map/all_to_all | solution.py:588
  127.0 1.1 copy-start.3
  128.1 1.2 copy-start.23
  133.6 0.7 copy-start.19
  134.3 0.7 copy-start.29
  135.0 0.7 copy-start.30
  135.7 0.7 copy-start.31
  136.4 0.7 copy-start.32
  137.1 21.9 %collective-permute-start.8 = (bf16[64,16,128]{2,1,0:T(8,128)(2,1)}, bf16[64,16,128]{2,1,0:T(8,128)(2,1)S(1)}, u32[]{:S(2)}, u32[]{:S(2)}) collective-permute-start(bf16[64,16,128]{2,1,0:T(8,128)(2,1)} %get-tuple-element.44), channel_id=1, source_target_pairs={{0,1},{1,0},{2,3},{3,2},{4,5},{5,4},{6,7},{7,6},{8,9},{9,8},{10,11... | collective-permute-start | bytes 786440 | tf_op jit(solution)/shard_map/ppermute | solution.py:557
  137.1 23.1 %collective-permute-start.9 = (bf16[64,16,128]{2,1,0:T(8,128)(2,1)}, bf16[64,16,128]{2,1,0:T(8,128)(2,1)S(1)}, u32[]{:S(2)}, u32[]{:S(2)}) collective-permute-start(bf16[64,16,128]{2,1,0:T(8,128)(2,1)} %get-tuple-element.45), channel_id=1, source_target_pairs={{0,2},{1,3},{2,0},{3,1},{4,6},{5,7},{6,4},{7,5},{8,10},{9,11},{10,... | collective-permute-start | bytes 786440 | tf_op jit(solution)/shard_map/ppermute | solution.py:557
  140.9 12.4 %collective-permute-start.10 = (f32[160,128]{1,0:T(8,128)}, f32[160,128]{1,0:T(8,128)S(1)}, u32[]{:S(2)}, u32[]{:S(2)}) collective-permute-start(f32[160,128]{1,0:T(8,128)} %sum_pieces.2.refs_0_), channel_id=1, source_target_pairs={{0,1},{1,0},{2,3},{3,2},{4,5},{5,4},{6,7},{7,6},{8,9},{9,8},{10,11... | collective-permute-start | bytes 245768 | tf_op jit(solution)/shard_map/ppermute | solution.py:557
  155.5 12.7 %collective-permute-start.11 = (f32[160,128]{1,0:T(8,128)}, f32[160,128]{1,0:T(8,128)S(1)}, u32[]{:S(2)}, u32[]{:S(2)}) collective-permute-start(f32[160,128]{1,0:T(8,128)} %add.4.refs_2_), channel_id=1, source_target_pairs={{0,2},{1,3},{2,0},{3,1},{4,6},{5,7},{6,4},{7,5},{8,10},{9,11},{10,... | collective-permute-start | bytes 245768 | tf_op jit(solution)/shard_map/ppermute | solution.py:557
  155.8 35.1 %collective-permute-start.12 = (bf16[64,16,128]{2,1,0:T(8,128)(2,1)}, bf16[64,16,128]{2,1,0:T(8,128)(2,1)S(1)}, u32[]{:S(2)}, u32[]{:S(2)}) collective-permute-start(bf16[64,16,128]{2,1,0:T(8,128)(2,1)} %copy-done.32), channel_id=1, source_target_pairs={{0,3},{1,2},{2,1},{3,0},{4,7},{5,6},{6,5},{7,4},{8,11},{9,10},{10,... | collective-permute-start | bytes 786440 | tf_op jit(solution)/shard_map/ppermute | solution.py:557
  158.2 32.8 %collective-permute-start.13 = (bf16[64,16,128]{2,1,0:T(8,128)(2,1)}, bf16[64,16,128]{2,1,0:T(8,128)(2,1)S(1)}, u32[]{:S(2)}, u32[]{:S(2)}) collective-permute-start(bf16[64,16,128]{2,1,0:T(8,128)(2,1)} %copy-done.31), channel_id=1, source_target_pairs={{0,1},{1,0},{2,3},{3,2},{4,5},{5,4},{6,7},{7,6},{8,9},{9,8},{10,11... | collective-permute-start | bytes 786440 | tf_op jit(solution)/shard_map/ppermute | solution.py:557
  159.0 9.2 %copy-start.15 = (bf16[64,16,128]{2,1,0:T(8,128)(2,1)}, bf16[64,16,128]{2,1,0:T(8,128)(2,1)S(1)}, u32[]{:S(2)}) copy-start(bf16[64,16,128]{2,1,0:T(8,128)(2,1)S(1)} %collective-permute-done.8.refs_0_.refs_3_) | copy-start | bytes 786436
  159.0 32.0 %collective-permute-start.14 = (bf16[64,16,128]{2,1,0:T(8,128)(2,1)}, bf16[64,16,128]{2,1,0:T(8,128)(2,1)}, u32[]{:S(2)}, u32[]{:S(2)}) collective-permute-start(bf16[64,16,128]{2,1,0:T(8,128)(2,1)} %copy-done.30), channel_id=1, source_target_pairs={{0,2},{1,3},{2,0},{3,1},{4,6},{5,7},{6,4},{7,5},{8,10},{9,11},{10,... | collective-permute-start | bytes 786440 | tf_op jit(solution)/shard_map/ppermute | solution.py:557
  160.2 8.0 %copy-start.17 = (bf16[64,16,128]{2,1,0:T(8,128)(2,1)}, bf16[64,16,128]{2,1,0:T(8,128)(2,1)S(1)}, u32[]{:S(2)}) copy-start(bf16[64,16,128]{2,1,0:T(8,128)(2,1)S(1)} %collective-permute-done.9.refs_1_.refs_4_) | copy-start | bytes 786436
  160.2 30.7 %collective-permute-start.15 = (bf16[64,16,128]{2,1,0:T(8,128)(2,1)}, bf16[64,16,128]{2,1,0:T(8,128)(2,1)}, u32[]{:S(2)}, u32[]{:S(2)}) collective-permute-start(bf16[64,16,128]{2,1,0:T(8,128)(2,1)} %copy-done.29), channel_id=1, source_target_pairs={{0,3},{1,2},{2,1},{3,0},{4,7},{5,6},{6,5},{7,4},{8,11},{9,10},{10,... | collective-permute-start | bytes 786440 | tf_op jit(solution)/shard_map/ppermute | solution.py:557
  168.2 0.6 copy-start.38
  186.0 4.9 %copy-start.16 = (bf16[64,16,128]{2,1,0:T(8,128)(2,1)S(1)}, bf16[64,16,128]{2,1,0:T(8,128)(2,1)}, u32[]{:S(2)}) copy-start(bf16[64,16,128]{2,1,0:T(8,128)(2,1)} %copy-done.15) | copy-start | bytes 786436
  186.1 4.9 %copy-start.18 = (bf16[64,16,128]{2,1,0:T(8,128)(2,1)S(1)}, bf16[64,16,128]{2,1,0:T(8,128)(2,1)}, u32[]{:S(2)}) copy-start(bf16[64,16,128]{2,1,0:T(8,128)(2,1)} %copy-done.17) | copy-start | bytes 786436
  186.1 4.9 %copy-start.20 = (bf16[64,16,128]{2,1,0:T(8,128)(2,1)S(1)}, bf16[64,16,128]{2,1,0:T(8,128)(2,1)}, u32[]{:S(2)}) copy-start(bf16[64,16,128]{2,1,0:T(8,128)(2,1)} %copy-done.19) | copy-start | bytes 786436
  190.9 4.8 %copy-start.4 = (f32[4,8,128,128]{3,2,1,0:T(8,128)}, f32[4,8,128,128]{3,2,1,0:T(8,128)S(1)}, u32[]{:S(2)}) copy-start(f32[4,8,128,128]{3,2,1,0:T(8,128)S(1)} %factor.5.refs_0_.refs_1_) | copy-start | bytes 6291460
  195.7 19.7 %all-to-all-start.2 = ((f32[8,64,512]{2,1,0:T(8,128)}), f32[8,64,512]{2,1,0:T(8,128)}, u32[]{:S(2)}, u32[]{:S(2)}) async-start(f32[8,64,512]{2,1,0:T(8,128)} %bitcast.5), calls=%async_computation.2 | async-start | bytes 2097152 | tf_op jit(solution)/shard_map/all_to_all | solution.py:588
  200.1 1.6 copy-start.5
  211.7 0.8 copy-start.8
  212.5 1.0 copy-start.13
  217.3 11.0 %collective-permute-start.16 = (f32[64,512]{1,0:T(8,128)}, f32[64,512]{1,0:T(8,128)S(1)}, u32[]{:S(2)}, u32[]{:S(2)}) collective-permute-start(f32[64,512]{1,0:T(8,128)} %sum_pieces.3.refs_0_.refs_1_), channel_id=1, source_target_pairs={{0,1},{1,0},{2,3},{3,2},{4,5},{5,4},{6,7},{7,6},{8,9},{9,8},{10,11... | collective-permute-start | bytes 393224 | tf_op jit(solution)/shard_map/ppermute | solution.py:557
  222.8 1.0 copy-start.9
  223.8 0.9 copy-start.12
  228.2 0.7 copy-start.34
  230.5 7.1 %collective-permute-start.17 = (f32[64,512]{1,0:T(8,128)}, f32[64,512]{1,0:T(8,128)S(1)}, u32[]{:S(2)}, u32[]{:S(2)}) collective-permute-start(f32[64,512]{1,0:T(8,128)} %add.6.refs_1_), channel_id=1, source_target_pairs={{0,2},{1,3},{2,0},{3,1},{4,6},{5,7},{6,4},{7,5},{8,10},{9,11},{10,... | collective-permute-start | bytes 393224 | tf_op jit(solution)/shard_map/ppermute | solution.py:557
  230.5 1.0 copy-start.10
  231.6 0.9 copy-start.11
  235.9 18.6 %copy-start.14 = (f32[512,512]{1,0:T(8,128)S(1)}, f32[512,512]{1,0:T(8,128)}, u32[]{:S(2)}) copy-start(f32[512,512]{1,0:T(8,128)} %copy-done.13) | copy-start | bytes 3145732
  237.6 0.7 copy-start.33
  239.9 6.8 %collective-permute-start.20 = (f32[64,512]{1,0:T(8,128)}, f32[64,512]{1,0:T(8,128)S(1)}, u32[]{:S(2)}, u32[]{:S(2)}) collective-permute-start(f32[64,512]{1,0:T(8,128)} %add.7.refs_0_), channel_id=1, source_target_pairs={{0,24},{4,28},{8,16},{12,20},{16,8},{20,12},{24,0},{28,4},{1,25},{... | collective-permute-start | bytes 393224 | tf_op jit(solution)/shard_map/ppermute | solution.py:557
  242.5 6.7 %collective-permute-start.19 = (f32[64,512]{1,0:T(8,128)}, f32[64,512]{1,0:T(8,128)S(1)}, u32[]{:S(2)}, u32[]{:S(2)}) collective-permute-start(f32[64,512]{1,0:T(8,128)} %add.7.refs_0_), channel_id=1, source_target_pairs={{0,16},{4,20},{8,24},{12,28},{16,0},{20,4},{24,8},{28,12},{1,17},{... | collective-permute-start | bytes 393224 | tf_op jit(solution)/shard_map/ppermute | solution.py:557
  243.6 5.9 %collective-permute-start.18 = (f32[64,512]{1,0:T(8,128)}, f32[64,512]{1,0:T(8,128)S(1)}, u32[]{:S(2)}, u32[]{:S(2)}) collective-permute-start(f32[64,512]{1,0:T(8,128)} %add.7.refs_0_), channel_id=1, source_target_pairs={{0,8},{4,12},{8,0},{12,4},{16,24},{20,28},{24,16},{28,20},{1,9},{5... | collective-permute-start | bytes 393224 | tf_op jit(solution)/shard_map/ppermute | solution.py:557
  246.7 2.7 %copy-start.35 = (f32[64,512]{1,0:T(8,128)}, f32[64,512]{1,0:T(8,128)S(1)}, u32[]{:S(2)}) copy-start(f32[64,512]{1,0:T(8,128)S(1)} %collective-permute-done.20.refs_3_) | copy-start | bytes 393220
  249.2 0.7 copy-start.36
  249.8 0.7 copy-start.37
  252.4 2.1 collective-permute-start.21
  254.5 1.0 copy-start.7
  (1 other events, 0.6 us)
